TPU v7x, 32 devices: a whole 2x2x4 slice. The times are simulated.
32 devices in a mesh: groups: 2 (over y), ctx: 4 (over z), dp: 4 (over x, core).
Axes of the slice: x: 2, y: 2, z: 4, core: 2. Of those that a mesh axis runs over, the one named last changes fastest.
Arguments:
- queries: bfloat16 [8, 512, 1024], P(('groups', 'dp'), 'ctx'), parts along dimension 0, may hold values from -6 to 6
- key_rows: bfloat16 [8, 512, 1024], P(('groups', 'dp'), 'ctx'), parts along dimension 0, may hold values from -6 to 6
- value_rows: bfloat16 [8, 512, 1024], P(('groups', 'dp'), 'ctx'), parts along dimension 0, may hold values from -6 to 6
- update_gate: bfloat16 [8, 512, 1024], P(('groups', 'dp'), 'ctx'), parts along dimension 0, may hold values from -6 to 6
- out_grad: bfloat16 [8, 512, 1024], P(('groups', 'dp'), 'ctx'), parts along dimension 0, may hold values from -6 to 6
- user_lengths: int32 [8, 4], P(('groups', 'dp')), parts along dimension 0, may hold values from 1 to 256, 512 in all within a row
- rel_bias: float32 [8, 8], replicated, may hold values from -1 to 1
- norm_gain: float32 [1024], replicated, may hold values from 0.5 to 1.5
Outputs:
- query_grad: bfloat16 [8, 512, 1024], P(('groups', 'dp'), 'ctx'), parts along dimension 0
- key_grad: bfloat16 [8, 512, 1024], P(('groups', 'dp'), 'ctx'), parts along dimension 0
- value_grad: bfloat16 [8, 512, 1024], P(('groups', 'dp'), 'ctx'), parts along dimension 0
- gate_grad: bfloat16 [8, 512, 1024], P(('groups', 'dp'), 'ctx'), parts along dimension 0
- bias_grad: float32 [16, 8], P('groups'), parts along dimension 0
- gain_grad: float32 [2048], P('groups'), parts along dimension 0
There are 2 independent parts, one for each index of `groups`. A program takes and returns all parts, laid end to end along the dimension named above; an argument that names none is the same for every part. Nothing has to cross between parts.
Inputs may be any that keep to these rules, and one draw needn't show every extreme that they name: `user_lengths`: each row lists the event counts of the 4 users packed one after another into a sequence; a row sums to 512 and its largest entry is exactly 256.
All inputs are finite; a program needn't handle non-finite values.
Results may differ from a plain program's by a relative error of at most 0.0058.
Values may be sent and summed in bfloat16 or wider, within the bound.
No kernel may reach another device: no remote copies, remote signals or barrier semaphores. Data moves between devices by JAX's collectives and lax.ppermute only.
A program may use at most 64 MiB of HBM per device.

v0:
```python
from functools import partial

import jax
import jax.numpy as jnp
from jax import lax
from jax.sharding import PartitionSpec as P

EPSILON = 1e-05


def passed_along(array, axis, by):
    size = lax.axis_size(axis)
    pairs = [(i, i + by) for i in range(size) if 0 <= i + by < size]
    return lax.ppermute(array, axis, pairs)


def segment_of(positions, user_ends):
    return jnp.sum((positions[:, None] >= user_ends[None, :]).astype(jnp.int32), axis=1)


def pair_mask(query_pos, key_pos, user_ends, seq_total, level_count):
    distance = query_pos[:, None] - key_pos[None, :]
    same_user = segment_of(query_pos, user_ends)[:, None] == segment_of(key_pos, user_ends)[None, :]
    inside = (key_pos[None, :] >= 0) & (query_pos[:, None] < seq_total)
    visible = (distance >= 0) & same_user & inside
    bucket = jnp.zeros(distance.shape, jnp.int32)
    for level in range(level_count - 1):
        bucket = bucket + (distance >= 2**level).astype(jnp.int32)
    return (visible, bucket)


def bias_values(bucket, rel_bias):
    total = jnp.zeros((rel_bias.shape[1],) + bucket.shape, jnp.float32)
    for level in range(rel_bias.shape[0]):
        total = jnp.where(bucket[None] == level, rel_bias[level][:, None, None], total)
    return total


def bias_sums(bucket, grads, level_count):
    return jnp.stack(
        [
            jnp.sum(jnp.where(bucket[None] == level, grads, 0.0), axis=(1, 2))
            for level in range(level_count)
        ]
    )


def silu_slope(logits):
    sigma = jax.nn.sigmoid(logits)
    return sigma * (1.0 + logits * (1.0 - sigma))


def forward_pair(query_blk, key_blk, value_blk, visible, bucket, rel_bias, scaling):
    logits = jnp.einsum(
        "qhd,khd->hqk", query_blk, key_blk, preferred_element_type=jnp.float32
    ) * scaling + bias_values(bucket, rel_bias)
    weights = jnp.where(visible[None], jax.nn.silu(logits), 0.0).astype(jnp.bfloat16)
    return jnp.einsum("hqk,khd->qhd", weights, value_blk, preferred_element_type=jnp.float32)


def backward_pair(
    query_blk, grad_blk, key_blk, value_blk, visible, bucket, rel_bias, scaling, for_query, for_key
):
    logits = jnp.einsum(
        "qhd,khd->hqk", query_blk, key_blk, preferred_element_type=jnp.float32
    ) * scaling + bias_values(bucket, rel_bias)
    weight_grad = jnp.einsum(
        "qhd,khd->hqk", grad_blk, value_blk, preferred_element_type=jnp.float32
    )
    logit_grad = jnp.where(visible[None], weight_grad * silu_slope(logits), 0.0)
    rounded_grad = logit_grad.astype(jnp.bfloat16)
    pieces = ()
    query_part = jnp.einsum(
        "hqk,khd->qhd", rounded_grad, key_blk, preferred_element_type=jnp.float32
    )
    pieces = pieces + (query_part, bias_sums(bucket, logit_grad, rel_bias.shape[0]))
    weights = jnp.where(visible[None], jax.nn.silu(logits), 0.0).astype(jnp.bfloat16)
    key_part = jnp.einsum(
        "hqk,qhd->khd", rounded_grad, query_blk, preferred_element_type=jnp.float32
    )
    value_part = jnp.einsum("hqk,qhd->khd", weights, grad_blk, preferred_element_type=jnp.float32)
    pieces = pieces + (key_part, value_part)
    return pieces


def local(queries, key_rows, value_rows, update_gate, out_grad, user_lengths, rel_bias, norm_gain):
    row_count = queries.shape[1]
    feature_count = queries.shape[2]
    head_count = rel_bias.shape[1]
    level_count = rel_bias.shape[0]
    shape3 = (row_count, head_count, feature_count // head_count)
    scaling = (feature_count // head_count) ** (-0.5)
    query3 = queries[0].reshape(shape3)
    key3 = key_rows[0].reshape(shape3)
    value3 = value_rows[0].reshape(shape3)
    ctx_count = lax.axis_size("ctx")
    reach = min(3, ctx_count // 2)
    seq_total = row_count * ctx_count
    first_row = lax.axis_index("ctx") * row_count
    row_index = jnp.arange(row_count, dtype=jnp.int32)
    own_pos = first_row + row_index
    user_ends = jnp.cumsum(user_lengths[0])
    zero_rows = jnp.zeros(shape3, jnp.float32)
    zero_bias = jnp.zeros((level_count, head_count), jnp.float32)
    held = [(key3, value3)]
    current = (key3, value3)
    for hop_num in range(1, reach + 1):
        current = passed_along((current[0], current[1]), "ctx", 1)
        held.append(current)
    masks = []
    attention = zero_rows
    for hop_num in range(reach + 1):
        key_pos = first_row - hop_num * row_count + row_index
        visible, bucket = pair_mask(own_pos, key_pos, user_ends, seq_total, level_count)
        masks.append((visible, bucket))
        compute = partial(
            forward_pair,
            query3,
            held[hop_num][0],
            held[hop_num][1],
            visible,
            bucket,
            rel_bias,
            scaling,
        )
        attention = attention + compute()
    attention = attention.reshape(row_count, feature_count)
    center = attention - jnp.mean(attention, axis=1, keepdims=True)
    inverse = lax.rsqrt(jnp.mean(center * center, axis=1, keepdims=True) + EPSILON)
    normed = center * inverse
    grad_f = out_grad[0].astype(jnp.float32)
    gate_f = update_gate[0].astype(jnp.float32)
    gate_grad = (grad_f * normed * norm_gain).astype(jnp.bfloat16)
    gain_part = jnp.sum(grad_f * gate_f * normed, axis=0)
    pushed = grad_f * gate_f * norm_gain
    attn_grad = inverse * (
        pushed
        - jnp.mean(pushed, axis=1, keepdims=True)
        - normed * jnp.mean(pushed * normed, axis=1, keepdims=True)
    )
    grad3 = attn_grad.astype(jnp.bfloat16).reshape(shape3)
    query_total = zero_rows
    bias_total = zero_bias
    key_parts = []
    value_parts = []
    for hop_num in range(reach + 1):
        visible, bucket = masks[hop_num]
        compute = partial(
            backward_pair,
            query3,
            grad3,
            held[hop_num][0],
            held[hop_num][1],
            visible,
            bucket,
            rel_bias,
            scaling,
            True,
            True,
        )
        pieces = compute()
        query_total = query_total + pieces[0]
        bias_total = bias_total + pieces[1]
        key_parts.append(pieces[2])
        value_parts.append(pieces[3])
    carried = (key_parts[reach], value_parts[reach])
    for hop_num in range(reach - 1, -1, -1):
        moved = passed_along((carried[0], carried[1]), "ctx", -1)
        carried = (moved[0] + key_parts[hop_num], moved[1] + value_parts[hop_num])
    key_total, value_total = carried
    query_grad = (query_total.reshape(row_count, feature_count) * scaling).astype(jnp.bfloat16)
    key_grad = (key_total.reshape(row_count, feature_count) * scaling).astype(jnp.bfloat16)
    value_grad = value_total.reshape(row_count, feature_count).astype(jnp.bfloat16)
    summed = lax.psum((bias_total, gain_part), ("ctx", "dp"))
    return (
        query_grad[None],
        key_grad[None],
        value_grad[None],
        gate_grad[None],
        summed[0],
        summed[1],
    )


def solution(mesh):
    in_specs = (
        P(("groups", "dp"), "ctx", None),
        P(("groups", "dp"), "ctx", None),
        P(("groups", "dp"), "ctx", None),
        P(("groups", "dp"), "ctx", None),
        P(("groups", "dp"), "ctx", None),
        P(("groups", "dp"), None),
        P(),
        P(),
    )
    out_specs = (
        P(("groups", "dp"), "ctx", None),
        P(("groups", "dp"), "ctx", None),
        P(("groups", "dp"), "ctx", None),
        P(("groups", "dp"), "ctx", None),
        P("groups", None),
        P("groups"),
    )
    return jax.shard_map(local, mesh=mesh, in_specs=in_specs, out_specs=out_specs, check_vma=False)
```

profile of v0, /device:TPU:0, one launch (start us, length us, event | category | flops | bytes accessed | tf_op | source)
XLA Modules:
  0.0 117.5 jit_solution(2227867411048834364)
XLA Ops:
  0.6 1.2 copy.75
  1.8 4.9 %collective-permute-start.1 = (bf16[128,8,128]{0,2,1:T(8,128)(2,1)S(1)}, bf16[128,8,128]{0,2,1:T(8,128)(2,1)S(1)}, u32[]{:S(2)}, u32[]{:S(2)}) collective-permute-start(bf16[128,8,128]{0,2,1:T(8,128)(2,1)S(1)} %bitcast.132), channel_id=1, source_target_pairs={{0,4},{4,8},{8,12},{1,5},{5,9},{9,13},{2,6},{6,10},{10,14},{3,7},{... | collective-permute-start | bytes 786440 | tf_op jit(solution)/shard_map/ppermute | solution.py:14
  7.1 3.5 %collective-permute-start = (bf16[128,8,128]{2,0,1:T(8,128)(2,1)S(1)}, bf16[128,8,128]{2,0,1:T(8,128)(2,1)S(1)}, u32[]{:S(2)}, u32[]{:S(2)}) collective-permute-start(bf16[128,8,128]{2,0,1:T(8,128)(2,1)S(1)} %copy.76), channel_id=1, source_target_pairs={{0,4},{4,8},{8,12},{1,5},{5,9},{9,13},{2,6},{6,10},{10,14},{3,7},{... | collective-permute-start | bytes 786440 | tf_op jit(solution)/shard_map/ppermute | solution.py:14
  10.7 0.6 copy-done.46
  11.6 0.6 copy-done.75
  12.5 0.5 fusion.27
  13.2 0.4 fusion.8
  13.7 0.3 fusion.28
  14.0 0.5 copy-done.81
  14.5 3.5 %collective-permute-start.3 = (bf16[128,8,128]{0,2,1:T(8,128)(2,1)S(1)}, bf16[128,8,128]{0,2,1:T(8,128)(2,1)S(1)}, u32[]{:S(2)}, u32[]{:S(2)}) collective-permute-start(bf16[128,8,128]{0,2,1:T(8,128)(2,1)S(1)} %collective-permute-done.1), channel_id=1, source_target_pairs={{0,4},{4,8},{8,12},{1,5},{5,9},{9,13},{2,6},{6,10},{10,14},{3,7},{... | collective-permute-start | bytes 786440 | tf_op jit(solution)/shard_map/ppermute | solution.py:14
  18.0 0.4 collective-permute-done
  18.4 4.4 %collective-permute-start.2 = (bf16[128,8,128]{2,0,1:T(8,128)(2,1)S(1)}, bf16[128,8,128]{2,0,1:T(8,128)(2,1)S(1)}, u32[]{:S(2)}, u32[]{:S(2)}) collective-permute-start(bf16[128,8,128]{2,0,1:T(8,128)(2,1)S(1)} %collective-permute-done), channel_id=1, source_target_pairs={{0,4},{4,8},{8,12},{1,5},{5,9},{9,13},{2,6},{6,10},{10,14},{3,7},{... | collective-permute-start | bytes 786440 | tf_op jit(solution)/shard_map/ppermute | solution.py:14
  22.8 0.5 fusion.7
  23.3 0.3 convolution_add_fusion.3
  23.6 0.5 copy-done.76
  24.1 5.0 %collective-permute-done.2 = bf16[128,8,128]{2,0,1:T(8,128)(2,1)S(1)} collective-permute-done((bf16[128,8,128]{2,0,1:T(8,128)(2,1)S(1)}, bf16[128,8,128]{2,0,1:T(8,128)(2,1)S(1)}, u32[]{:S(2)}, u32[]{:S(2)}) %collective-permute-start.2) | collective-permute-done | bytes 262176 | tf_op jit(solution)/shard_map/ppermute | solution.py:14
  29.2 0.5 fusion.6
  29.7 0.3 fusion.29
  30.0 0.4 copy-done.79
  30.9 0.7 copy-done
  31.7 0.8 fusion.13
  32.7 0.9 fusion.12
  34.1 0.4 copy-done.30
  34.7 0.3 copy-done.82
  35.0 1.5 %select_reduce_fusion.16 = (f32[8]{0:T(128)}, f32[8]{0:T(128)}, f32[8]{0:T(128)}, f32[8]{0:T(128)}, f32[8]{0:T(128)}, /*index=5*/f32[8]{0:T(128)}, f32[8]{0:T(128)}, f32[8]{0:T(128)}, bf16[8,128,128]{2,1,0:T(8,128)(2,1)S(1)}) fusion(pred[128,128]{1,0:T(8,128)(4,1)S(1)} %copy-done.44, pred[128,128]{1,0:T(8,128)(4,1)S(1)} %copy-done.30, ...), kind=kOutput, calls=%fused_computation.51 | convolution fusion | flops 36962240 | bytes 1458432 | tf_op jit(solution)/shard_map/qhd,khd->hqk/dot_general | solution.py:67
  36.6 1.1 convolution_bitcast_fusion.2
  37.7 0.3 fusion.20
  38.0 0.4 copy-done.14
  38.8 1.5 %select_reduce_fusion = (f32[8]{0:T(128)}, f32[8]{0:T(128)}, f32[8]{0:T(128)}, f32[8]{0:T(128)}, f32[8]{0:T(128)}, /*index=5*/f32[8]{0:T(128)}, f32[8]{0:T(128)}, f32[8]{0:T(128)}, bf16[8,128,128]{2,1,0:T(8,128)(2,1)S(1)}) fusion(pred[128,128]{1,0:T(8,128)(4,1)S(1)} %copy-done.26, pred[128,128]{1,0:T(8,128)(4,1)S(1)} %copy-done.28, ...), kind=kOutput, calls=%fused_computation.35 | convolution fusion | flops 36962240 | bytes 1458432 | tf_op jit(solution)/shard_map/qhd,khd->hqk/dot_general | solution.py:67
  40.3 0.3 convolution_bitcast_fusion.5
  40.6 1.4 %collective-permute-start.4 = (f32[128,8,128]{2,0,1:T(8,128)S(1)}, f32[128,8,128]{2,0,1:T(8,128)S(1)}, u32[]{:S(2)}, u32[]{:S(2)}) collective-permute-start(f32[128,8,128]{2,0,1:T(8,128)S(1)} %convolution_bitcast_fusion.5), channel_id=1, source_target_pairs={{4,0},{8,4},{12,8},{5,1},{9,5},{13,9},{6,2},{10,6},{14,10},{7,3},{... | collective-permute-start | bytes 1572872 | tf_op jit(solution)/shard_map/ppermute | solution.py:14
  42.1 1.3 %collective-permute-start.6 = (f32[128,8,128]{0,2,1:T(8,128)}, f32[128,8,128]{0,2,1:T(8,128)}, u32[]{:S(2)}, u32[]{:S(2)}) collective-permute-start(f32[128,8,128]{0,2,1:T(8,128)} %convolution_bitcast_fusion.2), channel_id=1, source_target_pairs={{4,0},{8,4},{12,8},{5,1},{9,5},{13,9},{6,2},{10,6},{14,10},{7,3},{... | collective-permute-start | bytes 1572872 | tf_op jit(solution)/shard_map/ppermute | solution.py:14
  43.4 1.5 %select_reduce_fusion.8 = (f32[8]{0:T(128)}, f32[8]{0:T(128)}, f32[8]{0:T(128)}, f32[8]{0:T(128)}, f32[8]{0:T(128)}, /*index=5*/f32[8]{0:T(128)}, f32[8]{0:T(128)}, f32[8]{0:T(128)}, bf16[8,128,128]{2,1,0:T(8,128)(2,1)S(1)}) fusion(pred[128,128]{1,0:T(8,128)(4,1)S(1)} %copy-done.10, pred[128,128]{1,0:T(8,128)(4,1)S(1)} %get-tuple-element.69, ...), kind=kOutput, calls=%fused_computation.43 | convolution fusion | flops 36962240 | bytes 1458432 | tf_op jit(solution)/shard_map/qhd,khd->hqk/dot_general | solution.py:67
  45.2 0.3 convolution_bitcast_fusion.3
  45.9 0.4 copy-done.47
  46.4 0.6 copy-done.66
  47.1 0.5 copy-done.55
  48.0 10.0 %collective-permute-done.4 = f32[128,8,128]{2,0,1:T(8,128)S(1)} collective-permute-done((f32[128,8,128]{2,0,1:T(8,128)S(1)}, f32[128,8,128]{2,0,1:T(8,128)S(1)}, u32[]{:S(2)}, u32[]{:S(2)}) %collective-permute-start.4) | collective-permute-done | bytes 524320 | tf_op jit(solution)/shard_map/ppermute | solution.py:14
  58.0 0.3 fusion
  58.3 1.3 %collective-permute-start.5 = (f32[128,8,128]{2,0,1:T(8,128)S(1)}, f32[128,8,128]{2,0,1:T(8,128)S(1)}, u32[]{:S(2)}, u32[]{:S(2)}) collective-permute-start(f32[128,8,128]{2,0,1:T(8,128)S(1)} %fusion), channel_id=1, source_target_pairs={{4,0},{8,4},{12,8},{5,1},{9,5},{13,9},{6,2},{10,6},{14,10},{7,3},{... | collective-permute-start | bytes 1572872 | tf_op jit(solution)/shard_map/ppermute | solution.py:14
  59.6 9.7 %collective-permute-done.6 = f32[128,8,128]{0,2,1:T(8,128)} collective-permute-done((f32[128,8,128]{0,2,1:T(8,128)}, f32[128,8,128]{0,2,1:T(8,128)}, u32[]{:S(2)}, u32[]{:S(2)}) %collective-permute-start.6) | collective-permute-done | bytes 524320 | tf_op jit(solution)/shard_map/ppermute | solution.py:14
  69.3 2.1 %fusion.1 = f32[128,8,128]{0,2,1:T(8,128)} fusion(f32[128,8,128]{0,2,1:T(8,128)} %collective-permute-done.6, bf16[128,8,128]{0,2,1:T(8,128)(2,1)S(1)} %copy-done.3, f32[8,128,128]{2,1,0:T(8,128)S(1)} %copy-done.78, pred[128,128]{1,0:T(8,128)(4,1)S(1)} %get-tuple-element.68), kind=kOutput, calls=%fused_computation.7 | convolution fusion | flops 34471936 | bytes 1851392 | tf_op jit(solution)/shard_map/hqk,qhd->khd/dot_general | solution.py:81
  71.5 1.3 %collective-permute-start.7 = (f32[128,8,128]{0,2,1:T(8,128)}, f32[128,8,128]{0,2,1:T(8,128)S(1)}, u32[]{:S(2)}, u32[]{:S(2)}) collective-permute-start(f32[128,8,128]{0,2,1:T(8,128)} %fusion.1), channel_id=1, source_target_pairs={{4,0},{8,4},{12,8},{5,1},{9,5},{13,9},{6,2},{10,6},{14,10},{7,3},{... | collective-permute-start | bytes 1572872 | tf_op jit(solution)/shard_map/ppermute | solution.py:14
  73.0 0.9 copy.101
  73.8 40.2 %all-reduce = (f32[8,8]{1,0:T(8,128)}, f32[1024]{0:T(1024)}) all-reduce(f32[8,8]{1,0:T(8,128)S(1)} %add_add_fusion, f32[1024]{0:T(1024)S(1)} %copy-done.45), channel_id=1, replica_groups=mesh['groups'=2,'ctx'=4,'dp'=4] {'ctx','dp'}, use_global_device_ids=true, to_apply=%region_32.33 | all-reduce | flops 1088 | bytes 8704 | tf_op jit(solution)/shard_map/psum | solution.py:174
  114.1 1.3 %convolution_bitcast_fusion = f32[128,8,128]{0,2,1:T(8,128)S(1)} fusion(bf16[128,8,128]{0,2,1:T(8,128)(2,1)S(1)} %copy-done.3, f32[8,128,128]{2,1,0:T(8,128)} %copy-done.81, pred[128,128]{1,0:T(8,128)(4,1)S(1)} %get-tuple-element.67), kind=kOutput, calls=%fused_computation | convolution fusion | flops 34340864 | bytes 1327104 | tf_op jit(solution)/shard_map/hqk,qhd->khd/dot_general | solution.py:81
  115.7 0.9 copy.102
  116.6 0.9 copy.103
  (187 shorter events, 4.1 us)
Async XLA Ops:
  0.6 6.1 %copy-start.4 = (bf16[1,128,1024]{2,1,0:T(8,128)(2,1)S(1)}, bf16[1,128,1024]{2,1,0:T(8,128)(2,1)}, u32[]{:S(2)}) copy-start(bf16[1,128,1024]{2,1,0:T(8,128)(2,1)} %param.9) | copy-start | bytes 786436
  1.8 12.7 %collective-permute-start.1 = (bf16[128,8,128]{0,2,1:T(8,128)(2,1)S(1)}, bf16[128,8,128]{0,2,1:T(8,128)(2,1)S(1)}, u32[]{:S(2)}, u32[]{:S(2)}) collective-permute-start(bf16[128,8,128]{0,2,1:T(8,128)(2,1)S(1)} %bitcast.132), channel_id=1, source_target_pairs={{0,4},{4,8},{8,12},{1,5},{5,9},{9,13},{2,6},{6,10},{10,14},{3,7},{... | collective-permute-start | bytes 786440 | tf_op jit(solution)/shard_map/ppermute | solution.py:14
  6.9 4.4 %copy-start.5 = (bf16[1,128,1024]{2,1,0:T(8,128)(2,1)S(1)}, bf16[1,128,1024]{2,1,0:T(8,128)(2,1)}, u32[]{:S(2)}) copy-start(bf16[1,128,1024]{2,1,0:T(8,128)(2,1)} %param.8) | copy-start | bytes 786436
  7.1 11.3 %collective-permute-start = (bf16[128,8,128]{2,0,1:T(8,128)(2,1)S(1)}, bf16[128,8,128]{2,0,1:T(8,128)(2,1)S(1)}, u32[]{:S(2)}, u32[]{:S(2)}) collective-permute-start(bf16[128,8,128]{2,0,1:T(8,128)(2,1)S(1)} %copy.76), channel_id=1, source_target_pairs={{0,4},{4,8},{8,12},{1,5},{5,9},{9,13},{2,6},{6,10},{10,14},{3,7},{... | collective-permute-start | bytes 786440 | tf_op jit(solution)/shard_map/ppermute | solution.py:14
  13.1 9.8 %copy-start.9 = (pred[128,128]{1,0:T(8,128)(4,1)}, pred[128,128]{1,0:T(8,128)(4,1)S(1)}, u32[]{:S(2)}) copy-start(pred[128,128]{1,0:T(8,128)(4,1)S(1)} %get-tuple-element.76) | copy-start | bytes 49156
  13.1 16.1 %copy-start.13 = (pred[128,128]{1,0:T(8,128)(4,1)}, pred[128,128]{1,0:T(8,128)(4,1)S(1)}, u32[]{:S(2)}) copy-start(pred[128,128]{1,0:T(8,128)(4,1)S(1)} %get-tuple-element.77) | copy-start | bytes 49156
  13.1 16.1 %copy-start.15 = (pred[128,128]{1,0:T(8,128)(4,1)}, pred[128,128]{1,0:T(8,128)(4,1)S(1)}, u32[]{:S(2)}) copy-start(pred[128,128]{1,0:T(8,128)(4,1)S(1)} %get-tuple-element.78) | copy-start | bytes 49156
  13.1 16.1 %copy-start.17 = (pred[128,128]{1,0:T(8,128)(4,1)}, pred[128,128]{1,0:T(8,128)(4,1)S(1)}, u32[]{:S(2)}) copy-start(pred[128,128]{1,0:T(8,128)(4,1)S(1)} %get-tuple-element.79) | copy-start | bytes 49156
  13.1 16.0 %copy-start.19 = (pred[128,128]{1,0:T(8,128)(4,1)}, pred[128,128]{1,0:T(8,128)(4,1)S(1)}, u32[]{:S(2)}) copy-start(pred[128,128]{1,0:T(8,128)(4,1)S(1)} %get-tuple-element.80) | copy-start | bytes 49156
  13.1 16.0 %copy-start.21 = (pred[128,128]{1,0:T(8,128)(4,1)}, pred[128,128]{1,0:T(8,128)(4,1)S(1)}, u32[]{:S(2)}) copy-start(pred[128,128]{1,0:T(8,128)(4,1)S(1)} %get-tuple-element.81) | copy-start | bytes 49156
  13.1 16.0 %copy-start.23 = (pred[128,128]{1,0:T(8,128)(4,1)}, pred[128,128]{1,0:T(8,128)(4,1)S(1)}, u32[]{:S(2)}) copy-start(pred[128,128]{1,0:T(8,128)(4,1)S(1)} %get-tuple-element.82) | copy-start | bytes 49156
  13.1 16.0 %copy-start.25 = (pred[128,128]{1,0:T(8,128)(4,1)}, pred[128,128]{1,0:T(8,128)(4,1)S(1)}, u32[]{:S(2)}) copy-start(pred[128,128]{1,0:T(8,128)(4,1)S(1)} %get-tuple-element.83) | copy-start | bytes 49156
  13.1 16.0 %copy-start.27 = (pred[128,128]{1,0:T(8,128)(4,1)}, pred[128,128]{1,0:T(8,128)(4,1)S(1)}, u32[]{:S(2)}) copy-start(pred[128,128]{1,0:T(8,128)(4,1)S(1)} %get-tuple-element.84) | copy-start | bytes 49156
  13.2 16.5 %copy-start.11 = (pred[128,128]{1,0:T(8,128)(4,1)}, pred[128,128]{1,0:T(8,128)(4,1)S(1)}, u32[]{:S(2)}) copy-start(pred[128,128]{1,0:T(8,128)(4,1)S(1)} %get-tuple-element.66) | copy-start | bytes 49156
  13.7 0.8 copy-start.81
  14.5 8.8 %copy-start.71 = (bf16[128,8,128]{0,2,1:T(8,128)(2,1)}, bf16[128,8,128]{0,2,1:T(8,128)(2,1)S(1)}, u32[]{:S(2)}) copy-start(bf16[128,8,128]{0,2,1:T(8,128)(2,1)S(1)} %collective-permute-done.1) | copy-start | bytes 786436
  14.5 15.2 %collective-permute-start.3 = (bf16[128,8,128]{0,2,1:T(8,128)(2,1)S(1)}, bf16[128,8,128]{0,2,1:T(8,128)(2,1)S(1)}, u32[]{:S(2)}, u32[]{:S(2)}) collective-permute-start(bf16[128,8,128]{0,2,1:T(8,128)(2,1)S(1)} %collective-permute-done.1), channel_id=1, source_target_pairs={{0,4},{4,8},{8,12},{1,5},{5,9},{9,13},{2,6},{6,10},{10,14},{3,7},{... | collective-permute-start | bytes 786440 | tf_op jit(solution)/shard_map/ppermute | solution.py:14
  18.4 4.9 %copy-start.6 = (bf16[128,8,128]{2,0,1:T(8,128)(2,1)}, bf16[128,8,128]{2,0,1:T(8,128)(2,1)S(1)}, u32[]{:S(2)}) copy-start(bf16[128,8,128]{2,0,1:T(8,128)(2,1)S(1)} %collective-permute-done) | copy-start | bytes 786436
  18.4 10.7 %collective-permute-start.2 = (bf16[128,8,128]{2,0,1:T(8,128)(2,1)S(1)}, bf16[128,8,128]{2,0,1:T(8,128)(2,1)S(1)}, u32[]{:S(2)}, u32[]{:S(2)}) collective-permute-start(bf16[128,8,128]{2,0,1:T(8,128)(2,1)S(1)} %collective-permute-done), channel_id=1, source_target_pairs={{0,4},{4,8},{8,12},{1,5},{5,9},{9,13},{2,6},{6,10},{10,14},{3,7},{... | collective-permute-start | bytes 786440 | tf_op jit(solution)/shard_map/ppermute | solution.py:14
  23.3 0.8 copy-start.76
  29.7 0.8 copy-start.79
  29.7 0.9 copy-start.73
  30.7 1.0 copy-start
  30.7 1.0 copy-start.1
  30.7 1.0 copy-start.8
  33.9 1.1 copy-start.82
  35.0 8.3 %copy-start.2 = (bf16[128,8,128]{0,2,1:T(8,128)(2,1)}, bf16[128,8,128]{0,2,1:T(8,128)(2,1)S(1)}, u32[]{:S(2)}) copy-start(bf16[128,8,128]{0,2,1:T(8,128)(2,1)S(1)} %multiply_convert_fusion.1) | copy-start | bytes 786436
  35.0 1.5 %copy-start.12 = (pred[128,128]{1,0:T(8,128)(4,1)S(1)}, pred[128,128]{1,0:T(8,128)(4,1)}, u32[]{:S(2)}) copy-start(pred[128,128]{1,0:T(8,128)(4,1)} %copy-done.11) | copy-start | bytes 49156
  35.0 1.5 %copy-start.80 = (f32[8,128,128]{2,1,0:T(8,128)S(1)}, f32[8,128,128]{2,1,0:T(8,128)}, u32[]{:S(2)}) copy-start(f32[8,128,128]{2,1,0:T(8,128)} %copy-done.79) | copy-start | bytes 1572868
  37.7 0.8 copy-start.26
  37.7 0.8 copy-start.28
  37.7 1.0 copy-start.74
  40.3 3.1 %copy-start.10 = (pred[128,128]{1,0:T(8,128)(4,1)S(1)}, pred[128,128]{1,0:T(8,128)(4,1)}, u32[]{:S(2)}) copy-start(pred[128,128]{1,0:T(8,128)(4,1)} %copy-done.9) | copy-start | bytes 49156
  40.3 3.1 %copy-start.72 = (bf16[128,8,128]{0,2,1:T(8,128)(2,1)S(1)}, bf16[128,8,128]{0,2,1:T(8,128)(2,1)}, u32[]{:S(2)}) copy-start(bf16[128,8,128]{0,2,1:T(8,128)(2,1)} %copy-done.71) | copy-start | bytes 786436
  40.3 3.1 %copy-start.77 = (f32[8,128,128]{2,1,0:T(8,128)S(1)}, f32[8,128,128]{2,1,0:T(8,128)}, u32[]{:S(2)}) copy-start(f32[8,128,128]{2,1,0:T(8,128)} %copy-done.76) | copy-start | bytes 1572868
  40.6 4.3 %copy-start.7 = (bf16[128,8,128]{2,0,1:T(8,128)(2,1)S(1)}, bf16[128,8,128]{2,0,1:T(8,128)(2,1)}, u32[]{:S(2)}) copy-start(bf16[128,8,128]{2,0,1:T(8,128)(2,1)} %copy-done.6) | copy-start | bytes 786436
  40.6 17.4 %collective-permute-start.4 = (f32[128,8,128]{2,0,1:T(8,128)S(1)}, f32[128,8,128]{2,0,1:T(8,128)S(1)}, u32[]{:S(2)}, u32[]{:S(2)}) collective-permute-start(f32[128,8,128]{2,0,1:T(8,128)S(1)} %convolution_bitcast_fusion.5), channel_id=1, source_target_pairs={{4,0},{8,4},{12,8},{5,1},{9,5},{13,9},{6,2},{10,6},{14,10},{7,3},{... | collective-permute-start | bytes 1572872 | tf_op jit(solution)/shard_map/ppermute | solution.py:14
  42.1 27.3 %collective-permute-start.6 = (f32[128,8,128]{0,2,1:T(8,128)}, f32[128,8,128]{0,2,1:T(8,128)}, u32[]{:S(2)}, u32[]{:S(2)}) collective-permute-start(f32[128,8,128]{0,2,1:T(8,128)} %convolution_bitcast_fusion.2), channel_id=1, source_target_pairs={{4,0},{8,4},{12,8},{5,1},{9,5},{13,9},{6,2},{10,6},{14,10},{7,3},{... | collective-permute-start | bytes 1572872 | tf_op jit(solution)/shard_map/ppermute | solution.py:14
  45.5 1.5 %copy-start.58 = (f32[8]{0:T(128)S(1)}, f32[8]{0:T(128)}, u32[]{:S(2)}) copy-start(f32[8]{0:T(128)} %get-tuple-element.46) | copy-start | bytes 100
  45.6 1.6 %copy-start.59 = (f32[8]{0:T(128)S(1)}, f32[8]{0:T(128)}, u32[]{:S(2)}) copy-start(f32[8]{0:T(128)} %get-tuple-element.47) | copy-start | bytes 100
  45.6 1.6 %copy-start.60 = (f32[8]{0:T(128)S(1)}, f32[8]{0:T(128)}, u32[]{:S(2)}) copy-start(f32[8]{0:T(128)} %get-tuple-element.48) | copy-start | bytes 100
  45.6 1.6 %copy-start.61 = (f32[8]{0:T(128)S(1)}, f32[8]{0:T(128)}, u32[]{:S(2)}) copy-start(f32[8]{0:T(128)} %get-tuple-element.49) | copy-start | bytes 100
  45.6 1.6 %copy-start.62 = (f32[8]{0:T(128)S(1)}, f32[8]{0:T(128)}, u32[]{:S(2)}) copy-start(f32[8]{0:T(128)} %get-tuple-element.50) | copy-start | bytes 100
  48.0 21.4 %copy-start.3 = (bf16[128,8,128]{0,2,1:T(8,128)(2,1)S(1)}, bf16[128,8,128]{0,2,1:T(8,128)(2,1)}, u32[]{:S(2)}) copy-start(bf16[128,8,128]{0,2,1:T(8,128)(2,1)} %copy-done.2) | copy-start | bytes 786436
  48.0 21.4 %copy-start.78 = (f32[8,128,128]{2,1,0:T(8,128)S(1)}, f32[8,128,128]{2,1,0:T(8,128)}, u32[]{:S(2)}) copy-start(f32[8,128,128]{2,1,0:T(8,128)} %copy-done.76) | copy-start | bytes 1572868
  58.3 57.1 %collective-permute-start.5 = (f32[128,8,128]{2,0,1:T(8,128)S(1)}, f32[128,8,128]{2,0,1:T(8,128)S(1)}, u32[]{:S(2)}, u32[]{:S(2)}) collective-permute-start(f32[128,8,128]{2,0,1:T(8,128)S(1)} %fusion), channel_id=1, source_target_pairs={{4,0},{8,4},{12,8},{5,1},{9,5},{13,9},{6,2},{10,6},{14,10},{7,3},{... | collective-permute-start | bytes 1572872 | tf_op jit(solution)/shard_map/ppermute | solution.py:14
  71.5 45.1 %collective-permute-start.7 = (f32[128,8,128]{0,2,1:T(8,128)}, f32[128,8,128]{0,2,1:T(8,128)S(1)}, u32[]{:S(2)}, u32[]{:S(2)}) collective-permute-start(f32[128,8,128]{0,2,1:T(8,128)} %fusion.1), channel_id=1, source_target_pairs={{4,0},{8,4},{12,8},{5,1},{9,5},{13,9},{6,2},{10,6},{14,10},{7,3},{... | collective-permute-start | bytes 1572872 | tf_op jit(solution)/shard_map/ppermute | solution.py:14
  73.0 0.9 copy-start.45
  (43 other events, 29.5 us)
where the time goes:
time: 118 us; the launch traced here: 117 us
  blocking collectives  40.2 us (34%)
  waiting for transfers between devices  25.2 us (21%)
  starting transfers between devices  21.6 us (18%)
  matrix products  13.3 us (11%)
  local copies, waits for them, and re-layouts  12.5 us (11%)
  other arithmetic  3.01 us (3%)
  between operations  1.71 us (1%)
    psum x1, blocking collectives, local(): summed = lax.psum((bias_total, gain_part), ('ctx', 'dp'))  40.2 us
    ppermute x8, waiting for transfers between devices, passed_along(): return lax.ppermute(array, axis, pairs)  25.2 us
    ppermute x8, starting transfers between devices, passed_along(): return lax.ppermute(array, axis, pairs)  21.6 us
    unnamed x171, local copies, waits for them, and re-layouts  11.1 us
    dot_general x3, matrix products, backward_pair(): jnp.einsum('qhd,khd->hqk', grad_blk, value_blk, preferred_element_type=jn...  4.6 us
    dot_general x3, matrix products, backward_pair(): jnp.einsum('hqk,qhd->khd', weights, grad_blk, preferred_element_type=jnp....  4.6 us
  transfers between devices with their start and end apart: 8, of which 4 were waited for; matrix products, arithmetic and copies ran while one was open for 10% of the time, Pallas kernels for 0%

commit v1 on v0

v1 whole, which is shorter than its diff:
```python
from functools import partial

import jax
import jax.numpy as jnp
from jax import lax
from jax.experimental import pallas as pl
from jax.experimental.pallas import tpu as pltpu
from jax.sharding import PartitionSpec as P

EPSILON = 1e-05
VMEM_LIMIT = 24 * 1024 * 1024
F32 = jnp.float32
BF16 = jnp.bfloat16


def passed_along(array, axis, by):
    size = lax.axis_size(axis)
    pairs = [(i, i + by) for i in range(size) if 0 <= i + by < size]
    return lax.ppermute(array, axis, pairs)


def contract(left, right, left_dim, right_dim):
    return lax.dot_general(
        left, right, (((left_dim,), (right_dim,)), ((), ())), preferred_element_type=F32
    )


class Pair:
    def __init__(self, lengths, bias, query_block, hops, rows, flipped):
        self.bias = bias
        self.levels, self.heads = bias.shape
        shape = (rows, rows)
        query_dim, key_dim = (1, 0) if flipped else (0, 1)
        first = (lax.axis_index("ctx") + query_block) * rows
        line = (1, rows) if flipped else (rows, 1)
        query_pos = first + lax.broadcasted_iota(jnp.int32, line, query_dim)
        end = jnp.int32(0)
        start = jnp.zeros(line, jnp.int32)
        for user in range(lengths.shape[1]):
            end = end + lengths[0, user]
            start = jnp.where(query_pos >= end, end, start)
        key_pos = first - hops * rows + lax.broadcasted_iota(jnp.int32, shape, key_dim)
        seen = key_pos >= start
        if hops == 0:
            seen = seen & (key_pos <= query_pos)
        self.mask = jnp.where(seen, 1.0, 0.0).astype(F32)
        self.far = (hops - 1) * rows + 1 >= 2 ** (self.levels - 2)
        self.distance = None if self.far else query_pos - key_pos

    def half_bias(self, head):
        value = 0.5 * self.bias[self.levels - 1, head]
        if self.far:
            return value
        for level in range(self.levels - 2, -1, -1):
            value = jnp.where(self.distance < 2**level, 0.5 * self.bias[level, head], value)
        return value

    def half_logits(self, scores, head, scaling):
        return scores * (0.5 * scaling) + self.half_bias(head)

    def bias_rows(self, grads):
        sub = lax.broadcasted_iota(jnp.int32, (self.levels, grads.shape[1]), 0)
        if self.far:
            row = jnp.sum(grads, axis=0, keepdims=True)
            return jnp.where(sub == self.levels - 1, row, 0.0)
        total = jnp.zeros(sub.shape, F32)
        for level in range(self.levels):
            inside = None
            if level > 0:
                inside = self.distance >= 2 ** (level - 1)
            if level < self.levels - 1:
                below = self.distance < 2**level
                inside = below if inside is None else inside & below
            row = jnp.sum(jnp.where(inside, grads, 0.0), axis=0, keepdims=True)
            total = jnp.where(sub == level, row, total)
        return total


def weights_of(half, mask):
    return ((half + half * jnp.tanh(half)) * mask).astype(BF16)


def slope_of(half, tanh):
    return (0.5 + 0.5 * tanh) * (1.0 + half * (1.0 - tanh))


def columns(head, width):
    return slice(head * width, (head + 1) * width)


def forward_kernel(hop_list, query_block, scaling, lengths, bias, *refs):
    count = len(hop_list)
    query, keys, values = refs[0], refs[1 : 1 + count], refs[1 + count : 1 + 2 * count]
    total = refs[1 + 2 * count] if len(refs) > 2 + 2 * count else None
    out = refs[-1]
    rows = query.shape[0]
    heads = bias.shape[1]
    width = query.shape[1] // heads
    pairs = [Pair(lengths, bias, query_block, hops, rows, False) for hops in hop_list]
    for head in range(heads):
        cols = columns(head, width)
        part = None if total is None else total[:, cols]
        for pair, key, value in zip(pairs, keys, values):
            half = pair.half_logits(contract(query[:, cols], key[:, cols], 1, 1), head, scaling)
            added = contract(weights_of(half, pair.mask), value[:, cols], 1, 0)
            part = added if part is None else part + added
        out[:, cols] = part.astype(out.dtype)


def norm_kernel(total, far_part, out_grad, update_gate, gain, attn_grad, gate_grad, gain_grad):
    rows, features = total.shape
    step = 16
    gain_row = gain[...]
    gain_sum = jnp.zeros((8, features), F32)
    for low in range(0, rows, step):
        span = slice(low, low + step)
        attention = total[span, :] + far_part[span, :].astype(F32)
        center = attention - jnp.mean(attention, axis=1, keepdims=True)
        inverse = lax.rsqrt(jnp.mean(center * center, axis=1, keepdims=True) + EPSILON)
        normed = center * inverse
        grad_f = out_grad[span, :].astype(F32)
        gate_grad[span, :] = (grad_f * normed * gain_row).astype(BF16)
        gated = grad_f * update_gate[span, :].astype(F32)
        product = gated * normed
        for part in range(0, step, 8):
            gain_sum = gain_sum + product[part : part + 8, :]
        pushed = gated * gain_row
        attn_grad[span, :] = (
            inverse
            * (
                pushed
                - jnp.mean(pushed, axis=1, keepdims=True)
                - normed * jnp.mean(pushed * normed, axis=1, keepdims=True)
            )
        ).astype(BF16)
    gain_grad[...] = jnp.sum(gain_sum, axis=0, keepdims=True)


def backward_own_kernel(hop_list, scaling, lengths, bias, *refs):
    count = len(hop_list)
    query, grad = refs[:2]
    keys, values = refs[2 : 2 + count], refs[2 + count : 2 + 2 * count]
    query_out, key_out, value_out, bias_out = refs[2 + 2 * count :]
    rows = query.shape[0]
    heads = bias.shape[1]
    width = query.shape[1] // heads
    pairs = [Pair(lengths, bias, 0, hops, rows, hops == 0) for hops in hop_list]
    lane = lax.broadcasted_iota(jnp.int32, bias_out.shape, 1)
    bias_total = jnp.zeros(bias_out.shape, F32)
    for head in range(heads):
        cols = columns(head, width)
        query_h, grad_h = query[:, cols], grad[:, cols]
        query_part = None
        bias_part = None
        for pair, hops, key, value in zip(pairs, hop_list, keys, values):
            key_h, value_h = key[:, cols], value[:, cols]
            if hops == 0:
                half = pair.half_logits(contract(key_h, query_h, 1, 1), head, scaling)
                weight_grad = contract(value_h, grad_h, 1, 1)
            else:
                half = pair.half_logits(contract(query_h, key_h, 1, 1), head, scaling)
                weight_grad = contract(grad_h, value_h, 1, 1)
            tanh = jnp.tanh(half)
            logit_grad = weight_grad * (slope_of(half, tanh) * pair.mask)
            rounded = logit_grad.astype(BF16)
            if hops == 0:
                weights = ((half + half * tanh) * pair.mask).astype(BF16)
                key_out[:, cols] = contract(rounded, query_h, 1, 0)
                value_out[:, cols] = contract(weights, grad_h, 1, 0)
                added = contract(rounded, key_h, 0, 0)
            else:
                added = contract(rounded, key_h, 1, 0)
            query_part = added if query_part is None else query_part + added
            sums = pair.bias_rows(logit_grad)
            bias_part = sums if bias_part is None else bias_part + sums
        query_out[:, cols] = query_part
        bias_total = jnp.where(lane == head, jnp.sum(bias_part, axis=1, keepdims=True), bias_total)
    bias_out[...] = bias_total


def backward_far_kernel(hops, scaling, lengths, bias, *refs):
    query, grad, key, value, bias_in, gain_in, query_out, small_out = refs
    rows = query.shape[0]
    levels, heads = bias.shape
    width = query.shape[1] // heads
    pair = Pair(lengths, bias, 1, hops, rows, False)
    lane = lax.broadcasted_iota(jnp.int32, bias_in.shape, 1)
    bias_total = bias_in[...]
    for head in range(heads):
        cols = columns(head, width)
        key_h = key[:, cols]
        half = pair.half_logits(contract(query[:, cols], key_h, 1, 1), head, scaling)
        weight_grad = contract(grad[:, cols], value[:, cols], 1, 1)
        logit_grad = weight_grad * (slope_of(half, jnp.tanh(half)) * pair.mask)
        query_out[:, cols] = contract(logit_grad.astype(BF16), key_h, 1, 0).astype(BF16)
        sums = jnp.sum(pair.bias_rows(logit_grad), axis=1, keepdims=True)
        bias_total = bias_total + jnp.where(lane == head, sums, 0.0)
    lanes = small_out.shape[1]
    lines = gain_in.shape[1] // lanes
    for line in range(lines):
        small_out[line : line + 1, :] = gain_in[:, line * lanes : (line + 1) * lanes]
    small_out[lines:, :] = bias_total


def backward_key_kernel(hops, scaling, lengths, bias, *refs):
    query, grad, key, value, key_in, value_in, key_out, value_out = refs
    last = key_out.dtype == BF16
    rows = query.shape[0]
    heads = bias.shape[1]
    width = query.shape[1] // heads
    pair = Pair(lengths, bias, hops, hops, rows, True)
    for head in range(heads):
        cols = columns(head, width)
        query_h, grad_h = query[:, cols], grad[:, cols]
        half = pair.half_logits(contract(key[:, cols], query_h, 1, 1), head, scaling)
        weight_grad = contract(value[:, cols], grad_h, 1, 1)
        tanh = jnp.tanh(half)
        rounded = (weight_grad * (slope_of(half, tanh) * pair.mask)).astype(BF16)
        weights = ((half + half * tanh) * pair.mask).astype(BF16)
        key_part = key_in[:, cols] + contract(rounded, query_h, 1, 0)
        value_part = value_in[:, cols] + contract(weights, grad_h, 1, 0)
        if last:
            key_part = key_part * scaling
        key_out[:, cols] = key_part.astype(key_out.dtype)
        value_out[:, cols] = value_part.astype(value_out.dtype)


def on_device(kernel, outs, smem, vmem, flops):
    moved = sum(array.size * array.dtype.itemsize for array in (*vmem, *outs))
    return pl.pallas_call(
        kernel,
        out_shape=outs,
        in_specs=[pl.BlockSpec(memory_space=pltpu.SMEM)] * len(smem)
        + [pl.BlockSpec(memory_space=pltpu.VMEM)] * len(vmem),
        out_specs=[pl.BlockSpec(memory_space=pltpu.VMEM)] * len(outs),
        compiler_params=pltpu.CompilerParams(vmem_limit_bytes=VMEM_LIMIT),
        cost_estimate=pl.CostEstimate(flops=flops, bytes_accessed=moved, transcendentals=0),
    )(*smem, *vmem)


def summed_over(array, axes):
    for axis in axes:
        size = lax.axis_size(axis)
        step = 1
        while step < size:
            array = array + lax.ppermute(array, axis, [(i, i ^ step) for i in range(size)])
            step = 2 * step
    return array


def local(queries, key_rows, value_rows, update_gate, out_grad, user_lengths, rel_bias, norm_gain):
    rows, features = queries.shape[1:]
    levels, heads = rel_bias.shape
    scaling = (features // heads) ** (-0.5)
    query, key, value = queries[0], key_rows[0], value_rows[0]
    reach = min(3, lax.axis_size("ctx") // 2)
    smem = (user_lengths, rel_bias)
    unit = 2 * rows * rows * features
    wide = jax.ShapeDtypeStruct((rows, features), F32)
    narrow = jax.ShapeDtypeStruct((rows, features), BF16)

    keys, values = [key], [value]
    for _ in range(reach - 1):
        keys.append(passed_along(keys[-1], "ctx", 1))
        values.append(passed_along(values[-1], "ctx", 1))
    later_queries = [query] + [passed_along(query, "ctx", -hops) for hops in range(1, reach + 1)]

    (attention,) = on_device(
        partial(forward_kernel, (0,), 0, scaling), [wide], smem, (query, key, value), 2 * unit
    )
    (far_part,) = on_device(
        partial(forward_kernel, (reach,), 1, scaling),
        [narrow],
        smem,
        (later_queries[1], keys[reach - 1], values[reach - 1]),
        2 * unit,
    )
    far_part = passed_along(far_part, "ctx", 1)
    near = tuple(range(1, reach))
    if near:
        (attention,) = on_device(
            partial(forward_kernel, near, 0, scaling),
            [wide],
            smem,
            (query, *keys[1:], *values[1:], attention),
            2 * len(near) * unit,
        )
    attn_grad, gate_grad, gain_part = on_device(
        norm_kernel,
        [narrow, narrow, jax.ShapeDtypeStruct((1, features), F32)],
        (),
        (attention, far_part, out_grad[0], update_gate[0], norm_gain[None]),
        20 * rows * features,
    )
    later_grads = [attn_grad]
    for _ in range(reach):
        later_grads.append(passed_along(later_grads[-1], "ctx", -1))

    lanes = features // 8
    small = jax.ShapeDtypeStruct((levels, lanes), F32)
    query_total, key_total, value_total, bias_part = on_device(
        partial(backward_own_kernel, (0, *near), scaling),
        [wide, wide, wide, small],
        smem,
        (query, attn_grad, *keys, *values),
        (5 + 3 * len(near)) * unit,
    )
    query_part, sums = on_device(
        partial(backward_far_kernel, reach, scaling),
        [narrow, jax.ShapeDtypeStruct((8 + levels, lanes), F32)],
        smem,
        (later_queries[1], later_grads[1], keys[-1], values[-1], bias_part, gain_part),
        3 * unit,
    )
    query_part = passed_along(query_part, "ctx", 1)
    sums = summed_over(sums, ("dp", "ctx"))
    for hops in range(1, reach + 1):
        key_total, value_total = on_device(
            partial(backward_key_kernel, hops, scaling),
            [narrow if hops == reach else wide] * 2,
            smem,
            (later_queries[hops], later_grads[hops], key, value, key_total, value_total),
            4 * unit,
        )
    query_grad = ((query_total + query_part.astype(F32)) * scaling).astype(BF16)
    return (
        query_grad[None],
        key_total[None],
        value_total[None],
        gate_grad[None],
        sums[8:, :heads],
        sums[:8].reshape(features),
    )


def solution(mesh):
    in_specs = (
        P(("groups", "dp"), "ctx", None),
        P(("groups", "dp"), "ctx", None),
        P(("groups", "dp"), "ctx", None),
        P(("groups", "dp"), "ctx", None),
        P(("groups", "dp"), "ctx", None),
        P(("groups", "dp"), None),
        P(),
        P(),
    )
    out_specs = (
        P(("groups", "dp"), "ctx", None),
        P(("groups", "dp"), "ctx", None),
        P(("groups", "dp"), "ctx", None),
        P(("groups", "dp"), "ctx", None),
        P("groups", None),
        P("groups"),
    )
    return jax.shard_map(local, mesh=mesh, in_specs=in_specs, out_specs=out_specs, check_vma=False)
```

time: 118 us -> 77.2 us (0.65)
  blocking collectives: 40.2 us -> 0 us
  Pallas kernels: 0 us -> 18.2 us
  matrix products: 13.3 us -> 0 us
  local copies, waits for them, and re-layouts: 12.5 us -> 1.88 us
  starting transfers between devices: 21.6 us -> 27.8 us
  other arithmetic: 3.01 us -> 0.79 us
  waiting for transfers between devices: 25.2 us -> 27.3 us
    psum x1 -> x0, blocking collectives: 40.2 us -> none  [local(): summed = lax.psum((bias_total, gain_part), ('ctx', 'dp'))]
    pallas_call x0 -> x8, Pallas kernels: none -> 18.2 us  [on_device(): pl.pallas_call(kernel, out_shape=outs, in_specs=[pl.BlockSpec(memory_spac...]
    ppermute x0 -> x4, waiting for transfers between devices: none -> 15.9 us  [summed_over(): lax.ppermute(array, axis, [(i, i ^ step) for i in range(size)])]
    ppermute x8, waiting for transfers between devices: 25.2 us -> 11.4 us  [passed_along(): return lax.ppermute(array, axis, pairs)]
    dot_general x18 -> x0, matrix products: 13.3 us -> none  [the longest x3 4.6 us: backward_pair(): jnp.einsum('qhd,khd->hqk', grad_blk, value_blk, preferred_element_type=jn...]
    unnamed x171 -> x16, local copies, waits for them, and re-layouts: 11.1 us -> 0.69 us
    ppermute x0 -> x4, starting transfers between devices: none -> 7.02 us  [summed_over(): lax.ppermute(array, axis, [(i, i ^ step) for i in range(size)])]
    convert_element_type x4 -> x0, other arithmetic: 1.23 us -> none  [the longest x1 0.89 us: local(): gate_grad = (grad_f * normed * norm_gain).astype(jnp.bfloat16)]
  transfers between devices with their start and end apart: 8 -> 12, of which waited for: 4 -> 7; matrix products, arithmetic and copies ran while one was open for 10% -> 3% of each run, Pallas kernels for 0% -> 13%
where the time goes in v1:
time: 77.2 us; the launch traced here: 76.8 us
  starting transfers between devices  27.8 us (36%)
  waiting for transfers between devices  27.3 us (35%)
  Pallas kernels  18.2 us (24%)
  local copies, waits for them, and re-layouts  1.88 us (2%)
  between operations  0.87 us (1%)
  other arithmetic  0.79 us (1%)
    ppermute x8, starting transfers between devices, passed_along(): return lax.ppermute(array, axis, pairs)  20.8 us
    pallas_call x8, Pallas kernels, on_device(): pl.pallas_call(kernel, out_shape=outs, in_specs=[pl.BlockSpec(memory_spac...  18.2 us
    ppermute x4, waiting for transfers between devices, summed_over(): lax.ppermute(array, axis, [(i, i ^ step) for i in range(size)])  15.9 us
    ppermute x8, waiting for transfers between devices, passed_along(): return lax.ppermute(array, axis, pairs)  11.4 us
    ppermute x4, starting transfers between devices, summed_over(): lax.ppermute(array, axis, [(i, i ^ step) for i in range(size)])  7.02 us
  transfers between devices with their start and end apart: 12, of which 7 were waited for; matrix products, arithmetic and copies ran while one was open for 3% of the time, Pallas kernels for 13%

profile of v1, /device:TPU:0, one launch (start us, length us, event | category | flops | bytes accessed | tf_op | source)
XLA Modules:
  0.0 76.8 jit_solution(8443168625559780619)
XLA Ops:
  0.6 0.0 copy-start.5
  0.6 4.9 %collective-permute-start = (bf16[128,1024]{1,0:T(8,128)(2,1)}, bf16[128,1024]{1,0:T(8,128)(2,1)S(1)}, u32[]{:S(2)}, u32[]{:S(2)}) collective-permute-start(bf16[128,1024]{1,0:T(8,128)(2,1)} %bitcast.13), channel_id=1, source_target_pairs={{0,4},{4,8},{8,12},{1,5},{5,9},{9,13},{2,6},{6,10},{10,14},{3,7},{... | collective-permute-start | bytes 786440 | tf_op jit(solution)/shard_map/ppermute | solution.py:19
  5.6 0.0 copy-start.6
  5.6 3.5 %collective-permute-start.1 = (bf16[128,1024]{1,0:T(8,128)(2,1)}, bf16[128,1024]{1,0:T(8,128)(2,1)S(1)}, u32[]{:S(2)}, u32[]{:S(2)}) collective-permute-start(bf16[128,1024]{1,0:T(8,128)(2,1)} %bitcast.18), channel_id=1, source_target_pairs={{0,4},{4,8},{8,12},{1,5},{5,9},{9,13},{2,6},{6,10},{10,14},{3,7},{... | collective-permute-start | bytes 786440 | tf_op jit(solution)/shard_map/ppermute | solution.py:19
  9.1 0.0 copy-start
  9.1 0.0 copy-start.1
  9.1 0.0 copy-start.2
  9.1 1.4 %collective-permute-start.2 = (bf16[128,1024]{1,0:T(8,128)(2,1)}, bf16[128,1024]{1,0:T(8,128)(2,1)S(1)}, u32[]{:S(2)}, u32[]{:S(2)}) collective-permute-start(bf16[128,1024]{1,0:T(8,128)(2,1)} %bitcast.23), channel_id=1, source_target_pairs={{4,0},{8,4},{12,8},{5,1},{9,5},{13,9},{6,2},{10,6},{14,10},{7,3},{... | collective-permute-start | bytes 786440 | tf_op jit(solution)/shard_map/ppermute | solution.py:19
  10.6 2.0 %collective-permute-done.refs_1_.refs_3_.refs_2_ = bf16[128,1024]{1,0:T(8,128)(2,1)S(1)} collective-permute-done((bf16[128,1024]{1,0:T(8,128)(2,1)}, bf16[128,1024]{1,0:T(8,128)(2,1)S(1)}, u32[]{:S(2)}, u32[]{:S(2)}) %collective-permute-start) | collective-permute-done | bytes 262176 | tf_op jit(solution)/shard_map/ppermute | solution.py:19
  12.6 4.5 %collective-permute-done.1.refs_2_.refs_5_.refs_3_ = bf16[128,1024]{1,0:T(8,128)(2,1)S(1)} collective-permute-done((bf16[128,1024]{1,0:T(8,128)(2,1)}, bf16[128,1024]{1,0:T(8,128)(2,1)S(1)}, u32[]{:S(2)}, u32[]{:S(2)}) %collective-permute-start.1) | collective-permute-done | bytes 262176 | tf_op jit(solution)/shard_map/ppermute | solution.py:19
  17.1 1.8 %collective-permute-done.2.refs_0_ = bf16[128,1024]{1,0:T(8,128)(2,1)S(1)} collective-permute-done((bf16[128,1024]{1,0:T(8,128)(2,1)}, bf16[128,1024]{1,0:T(8,128)(2,1)S(1)}, u32[]{:S(2)}, u32[]{:S(2)}) %collective-permute-start.2) | collective-permute-done | bytes 262176 | tf_op jit(solution)/shard_map/ppermute | solution.py:19
  18.8 0.0 copy-done.5
  18.9 0.0 copy-done.6
  18.9 2.0 %shard_map.129 = bf16[128,1024]{1,0:T(8,128)(2,1)S(1)} custom-call(s32[1,4]{1,0:T(1,128)S(1)} %copy-done.6, f32[8,8]{1,0:T(8,128)S(1)} %copy-done.5, bf16[128,1024]{1,0:T(8,128)(2,1)S(1)} %collective-permute-done.2.refs_0_, bf16[128,1024]{1,0:T(8,128)(2,1)S(1)} %collective-permute-done.refs_1_.refs_3_.refs_2_, ...), custom_call_target="tpu_custom_call" | custom-call | flops 67108864 | bytes 1048576 | tf_op jit(solution)/shard_map/pallas_call | solution.py:230
  20.9 3.5 %collective-permute-start.3 = (bf16[128,1024]{1,0:T(8,128)(2,1)S(1)}, bf16[128,1024]{1,0:T(8,128)(2,1)S(1)}, u32[]{:S(2)}, u32[]{:S(2)}) collective-permute-start(bf16[128,1024]{1,0:T(8,128)(2,1)S(1)} %shard_map.129), channel_id=1, source_target_pairs={{0,4},{4,8},{8,12},{1,5},{5,9},{9,13},{2,6},{6,10},{10,14},{3,7},{... | collective-permute-start | bytes 786440 | tf_op jit(solution)/shard_map/ppermute | solution.py:19
  24.4 2.1 %shard_map.127.refs_3_ = f32[128,1024]{1,0:T(8,128)S(1)} custom-call(s32[1,4]{1,0:T(1,128)S(1)} %copy-done.6, f32[8,8]{1,0:T(8,128)S(1)} %copy-done.5, bf16[128,1024]{1,0:T(8,128)(2,1)S(1)} %bitcast.24, bf16[128,1024]{1,0:T(8,128)(2,1)S(1)} %bitcast.14, bf16[128,1024]{1,0:T(8,128)(2,1)S(1)} %bitcast.19), custom_call_target="tpu_custom_call" | custom-call | flops 67108864 | bytes 1310720 | tf_op jit(solution)/shard_map/pallas_call | solution.py:230
  26.5 0.0 copy-start.3
  26.5 0.0 copy-start.4
  26.5 2.1 %shard_map.128.total = f32[128,1024]{1,0:T(8,128)S(1)} custom-call(s32[1,4]{1,0:T(1,128)S(1)} %copy-done.6, f32[8,8]{1,0:T(8,128)S(1)} %copy-done.5, bf16[128,1024]{1,0:T(8,128)(2,1)S(1)} %bitcast.25, bf16[128,1024]{1,0:T(8,128)(2,1)S(1)} %collective-permute-done.refs_1_.refs_3_.refs_2_, ...), custom_call_target="tpu_custom_call" | custom-call | flops 67108864 | bytes 1835008 | tf_op jit(solution)/shard_map/pallas_call | solution.py:230
  28.6 0.0 copy-start.7
  28.6 0.0 collective-permute-done.3.far_part
  28.6 0.0 copy-done.3
  28.6 0.0 copy-done.4
  28.6 0.6 copy-done.7
  29.3 1.1 %shard_map.130 = (bf16[128,1024]{1,0:T(8,128)(2,1)S(1)}, bf16[128,1024]{1,0:T(8,128)(2,1)}, f32[1,1024]{1,0:T(1,128)S(1)}) custom-call(f32[128,1024]{1,0:T(8,128)S(1)} %shard_map.128.total, bf16[128,1024]{1,0:T(8,128)(2,1)S(1)} %collective-permute-done.3.far_part, bf16[128,1024]{1,0:T(8,128)(2,1)S(1)} %bitcast.28, bf16[128,1024]{1,0:T(8,128)(2,1)S(1)} %bitcast.29, ...), custom_call_target="tpu_custom_call" | custom-call | flops 2621440 | bytes 1843200 | tf_op jit(solution)/shard_map/pallas_call | solution.py:230
  30.4 1.3 %collective-permute-start.4 = (bf16[128,1024]{1,0:T(8,128)(2,1)S(1)}, bf16[128,1024]{1,0:T(8,128)(2,1)S(1)}, u32[]{:S(2)}, u32[]{:S(2)}) collective-permute-start(bf16[128,1024]{1,0:T(8,128)(2,1)S(1)} %get-tuple-element.19.refs_1_), channel_id=1, source_target_pairs={{4,0},{8,4},{12,8},{5,1},{9,5},{13,9},{6,2},{10,6},{14,10},{7,3},{... | collective-permute-start | bytes 786440 | tf_op jit(solution)/shard_map/ppermute | solution.py:19
  31.6 3.9 %shard_map.131 = (f32[128,1024]{1,0:T(8,128)S(1)}, f32[128,1024]{1,0:T(8,128)S(1)}, f32[128,1024]{1,0:T(8,128)S(1)}, f32[8,128]{1,0:T(8,128)S(1)}) custom-call(s32[1,4]{1,0:T(1,128)S(1)} %copy-done.6, f32[8,8]{1,0:T(8,128)S(1)} %copy-done.5, bf16[128,1024]{1,0:T(8,128)(2,1)S(1)} %bitcast.26, bf16[128,1024]{1,0:T(8,128)(2,1)S(1)} %get-tuple-element.19.refs_1_, ...), custom_call_target="tpu_custom_call" | custom-call | flops 268435456 | bytes 3149824 | tf_op jit(solution)/shard_map/pallas_call | solution.py:230
  35.5 3.1 %collective-permute-done.4.refs_1_ = bf16[128,1024]{1,0:T(8,128)(2,1)S(1)} collective-permute-done((bf16[128,1024]{1,0:T(8,128)(2,1)S(1)}, bf16[128,1024]{1,0:T(8,128)(2,1)S(1)}, u32[]{:S(2)}, u32[]{:S(2)}) %collective-permute-start.4) | collective-permute-done | bytes 262176 | tf_op jit(solution)/shard_map/ppermute | solution.py:19
  38.6 2.0 %shard_map.132 = (bf16[128,1024]{1,0:T(8,128)(2,1)S(1)}, f32[16,128]{1,0:T(8,128)S(1)}) custom-call(s32[1,4]{1,0:T(1,128)S(1)} %copy-done.6, f32[8,8]{1,0:T(8,128)S(1)} %copy-done.5, bf16[128,1024]{1,0:T(8,128)(2,1)S(1)} %collective-permute-done.2.refs_0_, bf16[128,1024]{1,0:T(8,128)(2,1)S(1)} %collective-permute-done.4.refs_1_, ...), custom_call_target="tpu_custom_call" | custom-call | flops 100663296 | bytes 1327104 | tf_op jit(solution)/shard_map/pallas_call | solution.py:230
  40.6 3.6 %collective-permute-start.5 = (bf16[128,1024]{1,0:T(8,128)(2,1)S(1)}, bf16[128,1024]{1,0:T(8,128)(2,1)S(1)}, u32[]{:S(2)}, u32[]{:S(2)}) collective-permute-start(bf16[128,1024]{1,0:T(8,128)(2,1)S(1)} %get-tuple-element.23), channel_id=1, source_target_pairs={{0,4},{4,8},{8,12},{1,5},{5,9},{9,13},{2,6},{6,10},{10,14},{3,7},{... | collective-permute-start | bytes 786440 | tf_op jit(solution)/shard_map/ppermute | solution.py:19
  44.2 0.1 collective-permute-start.8
  44.3 1.2 %collective-permute-done.8 = f32[16,128]{1,0:T(8,128)S(1)} collective-permute-done((f32[16,128]{1,0:T(8,128)S(1)}, f32[16,128]{1,0:T(8,128)S(1)}, u32[]{:S(2)}, u32[]{:S(2)}) %collective-permute-start.8) | collective-permute-done | bytes 8224 | tf_op jit(solution)/shard_map/ppermute | solution.py:246
  45.4 1.5 %collective-permute-start.9 = (f32[16,128]{1,0:T(8,128)S(1)}, f32[16,128]{1,0:T(8,128)S(1)}, u32[]{:S(2)}, u32[]{:S(2)}) collective-permute-start(f32[16,128]{1,0:T(8,128)S(1)} %add.16), channel_id=1, source_target_pairs={{0,2},{1,3},{2,0},{3,1},{4,6},{5,7},{6,4},{7,5},{8,10},{9,11},{10,... | collective-permute-start | bytes 24584 | tf_op jit(solution)/shard_map/ppermute | solution.py:246
  46.9 2.2 %collective-permute-done.9 = f32[16,128]{1,0:T(8,128)S(1)} collective-permute-done((f32[16,128]{1,0:T(8,128)S(1)}, f32[16,128]{1,0:T(8,128)S(1)}, u32[]{:S(2)}, u32[]{:S(2)}) %collective-permute-start.9) | collective-permute-done | bytes 8224 | tf_op jit(solution)/shard_map/ppermute | solution.py:246
  49.1 1.2 %collective-permute-start.10 = (f32[16,128]{1,0:T(8,128)S(1)}, f32[16,128]{1,0:T(8,128)S(1)}, u32[]{:S(2)}, u32[]{:S(2)}) collective-permute-start(f32[16,128]{1,0:T(8,128)S(1)} %add.17), channel_id=1, source_target_pairs={{0,4},{4,0},{8,12},{12,8},{1,5},{5,1},{9,13},{13,9},{2,6},{6,2},{1... | collective-permute-start | bytes 24584 | tf_op jit(solution)/shard_map/ppermute | solution.py:246
  50.3 1.3 %collective-permute-start.6 = (bf16[128,1024]{1,0:T(8,128)(2,1)S(1)}, bf16[128,1024]{1,0:T(8,128)(2,1)S(1)}, u32[]{:S(2)}, u32[]{:S(2)}) collective-permute-start(bf16[128,1024]{1,0:T(8,128)(2,1)S(1)} %bitcast.27), channel_id=1, source_target_pairs={{8,0},{12,4},{9,1},{13,5},{10,2},{14,6},{11,3},{15,7},{24,16},{28,... | collective-permute-start | bytes 786440 | tf_op jit(solution)/shard_map/ppermute | solution.py:19
  51.6 1.3 %collective-permute-start.7 = (bf16[128,1024]{1,0:T(8,128)(2,1)S(1)}, bf16[128,1024]{1,0:T(8,128)(2,1)S(1)}, u32[]{:S(2)}, u32[]{:S(2)}) collective-permute-start(bf16[128,1024]{1,0:T(8,128)(2,1)S(1)} %collective-permute-done.4.refs_1_), channel_id=1, source_target_pairs={{4,0},{8,4},{12,8},{5,1},{9,5},{13,9},{6,2},{10,6},{14,10},{7,3},{... | collective-permute-start | bytes 786440 | tf_op jit(solution)/shard_map/ppermute | solution.py:19
  52.9 0.0 collective-permute-done.10
  52.9 4.2 %collective-permute-start.11 = (f32[16,128]{1,0:T(8,128)S(1)}, f32[16,128]{1,0:T(8,128)S(1)}, u32[]{:S(2)}, u32[]{:S(2)}) collective-permute-start(f32[16,128]{1,0:T(8,128)S(1)} %add.18), channel_id=1, source_target_pairs={{0,8},{4,12},{8,0},{12,4},{1,9},{5,13},{9,1},{13,5},{2,10},{6,14},... | collective-permute-start | bytes 24584 | tf_op jit(solution)/shard_map/ppermute | solution.py:246
  57.2 2.2 %shard_map.133 = (f32[128,1024]{1,0:T(8,128)S(1)}, f32[128,1024]{1,0:T(8,128)S(1)}) custom-call(s32[1,4]{1,0:T(1,128)S(1)} %copy-done.6, f32[8,8]{1,0:T(8,128)S(1)} %copy-done.5, bf16[128,1024]{1,0:T(8,128)(2,1)S(1)} %collective-permute-done.2.refs_0_, bf16[128,1024]{1,0:T(8,128)(2,1)S(1)} %collective-permute-done.4.refs_1_, bf16[128,1024]{1,0:T(8,128)(2,1)S(1)} %bitcast.16, ...), custom_call_target="tpu_custom_call" | custom-call | flops 134217728 | bytes 3145728 | tf_op jit(solution)/shard_map/pallas_call | solution.py:230
  59.3 12.6 %collective-permute-done.11 = f32[16,128]{1,0:T(8,128)S(1)} collective-permute-done((f32[16,128]{1,0:T(8,128)S(1)}, f32[16,128]{1,0:T(8,128)S(1)}, u32[]{:S(2)}, u32[]{:S(2)}) %collective-permute-start.11) | collective-permute-done | bytes 8224 | tf_op jit(solution)/shard_map/ppermute | solution.py:246
  71.9 0.6 slice_bitcast_fusion
  72.5 0.6 slice.8
  73.1 0.0 collective-permute-done.5
  73.1 0.8 %fusion = bf16[1,128,1024]{2,1,0:T(8,128)(2,1)} fusion(f32[128,1024]{1,0:T(8,128)S(1)} %get-tuple-element.20, bf16[128,1024]{1,0:T(8,128)(2,1)S(1)} %collective-permute-done.5), kind=kLoop, calls=%fused_computation.1 | loop fusion | flops 524288 | bytes 1048576 | tf_op jit(solution)/shard_map/broadcast_in_dim | solution.py:327
  73.9 0.0 collective-permute-done.6.refs_0_
  73.9 0.0 collective-permute-done.7.refs_1_
  73.9 2.9 %shard_map.134 = (bf16[128,1024]{1,0:T(8,128)(2,1)}, bf16[128,1024]{1,0:T(8,128)(2,1)}) custom-call(s32[1,4]{1,0:T(1,128)S(1)} %copy-done.6, f32[8,8]{1,0:T(8,128)S(1)} %copy-done.5, bf16[128,1024]{1,0:T(8,128)(2,1)S(1)} %collective-permute-done.6.refs_0_, bf16[128,1024]{1,0:T(8,128)(2,1)S(1)} %collective-permute-done.7.refs_1_, ...), custom_call_target="tpu_custom_call" | custom-call | flops 134217728 | bytes 2621440 | tf_op jit(solution)/shard_map/pallas_call | solution.py:230
  (7 shorter events, 0.0 us)
Async XLA Ops:
  0.6 18.2 %copy-start.5 = (f32[8,8]{1,0:T(8,128)S(1)}, f32[8,8]{1,0:T(8,128)}, u32[]{:S(2)}) copy-start(f32[8,8]{1,0:T(8,128)} %bias.13) | copy-start | bytes 772
  0.6 11.9 %collective-permute-start = (bf16[128,1024]{1,0:T(8,128)(2,1)}, bf16[128,1024]{1,0:T(8,128)(2,1)S(1)}, u32[]{:S(2)}, u32[]{:S(2)}) collective-permute-start(bf16[128,1024]{1,0:T(8,128)(2,1)} %bitcast.13), channel_id=1, source_target_pairs={{0,4},{4,8},{8,12},{1,5},{5,9},{9,13},{2,6},{6,10},{10,14},{3,7},{... | collective-permute-start | bytes 786440 | tf_op jit(solution)/shard_map/ppermute | solution.py:19
  5.6 13.3 %copy-start.6 = (s32[1,4]{1,0:T(1,128)S(1)}, s32[1,4]{1,0:T(1,128)}, u32[]{:S(2)}) copy-start(s32[1,4]{1,0:T(1,128)} %lengths.13) | copy-start | bytes 52
  5.6 11.5 %collective-permute-start.1 = (bf16[128,1024]{1,0:T(8,128)(2,1)}, bf16[128,1024]{1,0:T(8,128)(2,1)S(1)}, u32[]{:S(2)}, u32[]{:S(2)}) collective-permute-start(bf16[128,1024]{1,0:T(8,128)(2,1)} %bitcast.18), channel_id=1, source_target_pairs={{0,4},{4,8},{8,12},{1,5},{5,9},{9,13},{2,6},{6,10},{10,14},{3,7},{... | collective-permute-start | bytes 786440 | tf_op jit(solution)/shard_map/ppermute | solution.py:19
  9.1 15.3 %copy-start = (bf16[1,128,1024]{2,1,0:T(8,128)(2,1)S(1)}, bf16[1,128,1024]{2,1,0:T(8,128)(2,1)}, u32[]{:S(2)}) copy-start(bf16[1,128,1024]{2,1,0:T(8,128)(2,1)} %param.9) | copy-start | bytes 786436
  9.1 15.3 %copy-start.1 = (bf16[1,128,1024]{2,1,0:T(8,128)(2,1)S(1)}, bf16[1,128,1024]{2,1,0:T(8,128)(2,1)}, u32[]{:S(2)}) copy-start(bf16[1,128,1024]{2,1,0:T(8,128)(2,1)} %param.10) | copy-start | bytes 786436
  9.1 15.3 %copy-start.2 = (bf16[1,128,1024]{2,1,0:T(8,128)(2,1)S(1)}, bf16[1,128,1024]{2,1,0:T(8,128)(2,1)}, u32[]{:S(2)}) copy-start(bf16[1,128,1024]{2,1,0:T(8,128)(2,1)} %param.8) | copy-start | bytes 786436
  9.1 9.7 %collective-permute-start.2 = (bf16[128,1024]{1,0:T(8,128)(2,1)}, bf16[128,1024]{1,0:T(8,128)(2,1)S(1)}, u32[]{:S(2)}, u32[]{:S(2)}) collective-permute-start(bf16[128,1024]{1,0:T(8,128)(2,1)} %bitcast.23), channel_id=1, source_target_pairs={{4,0},{8,4},{12,8},{5,1},{9,5},{13,9},{6,2},{10,6},{14,10},{7,3},{... | collective-permute-start | bytes 786440 | tf_op jit(solution)/shard_map/ppermute | solution.py:19
  20.9 7.7 %collective-permute-start.3 = (bf16[128,1024]{1,0:T(8,128)(2,1)S(1)}, bf16[128,1024]{1,0:T(8,128)(2,1)S(1)}, u32[]{:S(2)}, u32[]{:S(2)}) collective-permute-start(bf16[128,1024]{1,0:T(8,128)(2,1)S(1)} %shard_map.129), channel_id=1, source_target_pairs={{0,4},{4,8},{8,12},{1,5},{5,9},{9,13},{2,6},{6,10},{10,14},{3,7},{... | collective-permute-start | bytes 786440 | tf_op jit(solution)/shard_map/ppermute | solution.py:19
  26.5 2.1 %copy-start.3 = (bf16[1,128,1024]{2,1,0:T(8,128)(2,1)S(1)}, bf16[1,128,1024]{2,1,0:T(8,128)(2,1)}, u32[]{:S(2)}) copy-start(bf16[1,128,1024]{2,1,0:T(8,128)(2,1)} %param.12) | copy-start | bytes 786436
  26.5 2.1 %copy-start.4 = (bf16[1,128,1024]{2,1,0:T(8,128)(2,1)S(1)}, bf16[1,128,1024]{2,1,0:T(8,128)(2,1)}, u32[]{:S(2)}) copy-start(bf16[1,128,1024]{2,1,0:T(8,128)(2,1)} %param.11) | copy-start | bytes 786436
  28.6 0.7 copy-start.7
  30.4 8.3 %collective-permute-start.4 = (bf16[128,1024]{1,0:T(8,128)(2,1)S(1)}, bf16[128,1024]{1,0:T(8,128)(2,1)S(1)}, u32[]{:S(2)}, u32[]{:S(2)}) collective-permute-start(bf16[128,1024]{1,0:T(8,128)(2,1)S(1)} %get-tuple-element.19.refs_1_), channel_id=1, source_target_pairs={{4,0},{8,4},{12,8},{5,1},{9,5},{13,9},{6,2},{10,6},{14,10},{7,3},{... | collective-permute-start | bytes 786440 | tf_op jit(solution)/shard_map/ppermute | solution.py:19
  40.6 32.5 %collective-permute-start.5 = (bf16[128,1024]{1,0:T(8,128)(2,1)S(1)}, bf16[128,1024]{1,0:T(8,128)(2,1)S(1)}, u32[]{:S(2)}, u32[]{:S(2)}) collective-permute-start(bf16[128,1024]{1,0:T(8,128)(2,1)S(1)} %get-tuple-element.23), channel_id=1, source_target_pairs={{0,4},{4,8},{8,12},{1,5},{5,9},{9,13},{2,6},{6,10},{10,14},{3,7},{... | collective-permute-start | bytes 786440 | tf_op jit(solution)/shard_map/ppermute | solution.py:19
  44.2 1.2 %collective-permute-start.8 = (f32[16,128]{1,0:T(8,128)S(1)}, f32[16,128]{1,0:T(8,128)S(1)}, u32[]{:S(2)}, u32[]{:S(2)}) collective-permute-start(f32[16,128]{1,0:T(8,128)S(1)} %get-tuple-element.31), channel_id=1, source_target_pairs={{0,1},{1,0},{2,3},{3,2},{4,5},{5,4},{6,7},{7,6},{8,9},{9,8},{10,11... | collective-permute-start | bytes 24584 | tf_op jit(solution)/shard_map/ppermute | solution.py:246
  45.4 3.7 %collective-permute-start.9 = (f32[16,128]{1,0:T(8,128)S(1)}, f32[16,128]{1,0:T(8,128)S(1)}, u32[]{:S(2)}, u32[]{:S(2)}) collective-permute-start(f32[16,128]{1,0:T(8,128)S(1)} %add.16), channel_id=1, source_target_pairs={{0,2},{1,3},{2,0},{3,1},{4,6},{5,7},{6,4},{7,5},{8,10},{9,11},{10,... | collective-permute-start | bytes 24584 | tf_op jit(solution)/shard_map/ppermute | solution.py:246
  49.1 3.8 %collective-permute-start.10 = (f32[16,128]{1,0:T(8,128)S(1)}, f32[16,128]{1,0:T(8,128)S(1)}, u32[]{:S(2)}, u32[]{:S(2)}) collective-permute-start(f32[16,128]{1,0:T(8,128)S(1)} %add.17), channel_id=1, source_target_pairs={{0,4},{4,0},{8,12},{12,8},{1,5},{5,1},{9,13},{13,9},{2,6},{6,2},{1... | collective-permute-start | bytes 24584 | tf_op jit(solution)/shard_map/ppermute | solution.py:246
  50.3 23.6 %collective-permute-start.6 = (bf16[128,1024]{1,0:T(8,128)(2,1)S(1)}, bf16[128,1024]{1,0:T(8,128)(2,1)S(1)}, u32[]{:S(2)}, u32[]{:S(2)}) collective-permute-start(bf16[128,1024]{1,0:T(8,128)(2,1)S(1)} %bitcast.27), channel_id=1, source_target_pairs={{8,0},{12,4},{9,1},{13,5},{10,2},{14,6},{11,3},{15,7},{24,16},{28,... | collective-permute-start | bytes 786440 | tf_op jit(solution)/shard_map/ppermute | solution.py:19
  51.6 22.3 %collective-permute-start.7 = (bf16[128,1024]{1,0:T(8,128)(2,1)S(1)}, bf16[128,1024]{1,0:T(8,128)(2,1)S(1)}, u32[]{:S(2)}, u32[]{:S(2)}) collective-permute-start(bf16[128,1024]{1,0:T(8,128)(2,1)S(1)} %collective-permute-done.4.refs_1_), channel_id=1, source_target_pairs={{4,0},{8,4},{12,8},{5,1},{9,5},{13,9},{6,2},{10,6},{14,10},{7,3},{... | collective-permute-start | bytes 786440 | tf_op jit(solution)/shard_map/ppermute | solution.py:19
  52.9 19.0 %collective-permute-start.11 = (f32[16,128]{1,0:T(8,128)S(1)}, f32[16,128]{1,0:T(8,128)S(1)}, u32[]{:S(2)}, u32[]{:S(2)}) collective-permute-start(f32[16,128]{1,0:T(8,128)S(1)} %add.18), channel_id=1, source_target_pairs={{0,8},{4,12},{8,0},{12,4},{1,9},{5,13},{9,1},{13,5},{2,10},{6,14},... | collective-permute-start | bytes 24584 | tf_op jit(solution)/shard_map/ppermute | solution.py:246

commit v2 on v1

v2 whole, which is shorter than its diff:
```python
from functools import partial

import jax
import jax.numpy as jnp
from jax import lax
from jax.experimental import pallas as pl
from jax.experimental.pallas import tpu as pltpu
from jax.sharding import PartitionSpec as P

EPSILON = 1e-05
VMEM_LIMIT = 24 * 1024 * 1024
F32 = jnp.float32
BF16 = jnp.bfloat16


def passed_along(array, axis, by):
    size = lax.axis_size(axis)
    pairs = [(i, i + by) for i in range(size) if 0 <= i + by < size]
    return lax.ppermute(array, axis, pairs)


def contract(left, right, left_dim, right_dim):
    return lax.dot_general(
        left, right, (((left_dim,), (right_dim,)), ((), ())), preferred_element_type=F32
    )


def user_starts(lengths, query_pos):
    end = jnp.int32(0)
    start = jnp.zeros(query_pos.shape, jnp.int32)
    for user in range(lengths.shape[1]):
        end = end + lengths[0, user]
        start = jnp.where(query_pos >= end, end, start)
    return start


class Pair:
    def __init__(self, mask, table, heads, hops, flipped=False):
        rows = mask.shape[0]
        self.table, self.heads, self.levels = table, heads, table.shape[0] // heads
        self.mask = mask[...]
        self.far = (hops - 1) * rows + 1 >= 2 ** (self.levels - 2)
        if not self.far:
            query_dim, key_dim = (1, 0) if flipped else (0, 1)
            query_row = lax.broadcasted_iota(jnp.int32, mask.shape, query_dim)
            key_row = lax.broadcasted_iota(jnp.int32, mask.shape, key_dim)
            self.distance = query_row - key_row + hops * rows

    def half_logits(self, scores, head, scaling):
        def level_row(level):
            at = level * self.heads + head
            return self.table[at : at + 1, :]

        value = level_row(self.levels - 1)
        if not self.far:
            for level in range(self.levels - 2, -1, -1):
                value = jnp.where(self.distance < 2**level, level_row(level), value)
        return scores * (0.5 * scaling) + value

    def bias_rows(self, grads):
        sub = lax.broadcasted_iota(jnp.int32, (self.levels, grads.shape[1]), 0)
        if self.far:
            row = jnp.sum(grads, axis=0, keepdims=True)
            return jnp.where(sub == self.levels - 1, row, 0.0)
        total = jnp.zeros(sub.shape, F32)
        for level in range(self.levels):
            inside = None
            if level > 0:
                inside = self.distance >= 2 ** (level - 1)
            if level < self.levels - 1:
                below = self.distance < 2**level
                inside = below if inside is None else inside & below
            row = jnp.sum(jnp.where(inside, grads, 0.0), axis=0, keepdims=True)
            total = jnp.where(sub == level, row, total)
        return total


def slope_of(half, tanh):
    return (0.5 + 0.5 * tanh) * (1.0 + half * (1.0 - tanh))


def columns(head, width):
    return slice(head * width, (head + 1) * width)


def in_stages(count, first, second, ahead=3):
    held = [first(i) for i in range(min(ahead, count))]
    for i in range(count):
        if i + ahead < count:
            held.append(first(i + ahead))
        second(i, held.pop(0))


def mask_kernel(plan, lengths, bias, table, *masks):
    levels, heads = bias.shape
    for level in range(levels):
        for head in range(heads):
            at = level * heads + head
            table[at : at + 1, :] = jnp.full((1, table.shape[1]), 0.5 * bias[level, head], F32)
    for (block, hops, flipped), mask in zip(plan, masks):
        rows = mask.shape[0]
        query_dim, key_dim = (1, 0) if flipped else (0, 1)
        line = (1, rows) if flipped else (rows, 1)
        first = (lax.axis_index("ctx") + block) * rows
        query_pos = first + lax.broadcasted_iota(jnp.int32, line, query_dim)
        key_pos = first - hops * rows + lax.broadcasted_iota(jnp.int32, mask.shape, key_dim)
        seen = (key_pos >= user_starts(lengths, query_pos)) & (key_pos <= query_pos)
        mask[...] = jnp.where(seen, 1.0, 0.0).astype(F32)


def forward_kernel(hop_list, heads, scaling, *refs):
    count = len(hop_list)
    table, masks, query = refs[0], refs[1 : 1 + count], refs[1 + count]
    keys, values = refs[2 + count : 2 + 2 * count], refs[2 + 2 * count : 2 + 3 * count]
    total = refs[2 + 3 * count] if len(refs) > 3 + 3 * count else None
    out = refs[-1]
    width = query.shape[1] // heads
    pairs = [Pair(mask, table, heads, hops) for mask, hops in zip(masks, hop_list)]

    def scores(head):
        cols = columns(head, width)
        return [contract(query[:, cols], key[:, cols], 1, 1) for key in keys]

    def attend(head, found):
        cols = columns(head, width)
        part = None if total is None else total[:, cols]
        for pair, score, value in zip(pairs, found, values):
            half = pair.half_logits(score, head, scaling)
            weights = ((half + half * jnp.tanh(half)) * pair.mask).astype(BF16)
            added = contract(weights, value[:, cols], 1, 0)
            part = added if part is None else part + added
        out[:, cols] = part.astype(out.dtype)

    in_stages(heads, scores, attend)


def norm_kernel(total, far_part, out_grad, update_gate, gain, attn_grad, gate_grad, gain_grad):
    rows, features = total.shape
    step = 16
    gain_row = gain[...]
    gain_sum = jnp.zeros((8, features), F32)
    for low in range(0, rows, step):
        span = slice(low, low + step)
        attention = total[span, :] + far_part[span, :].astype(F32)
        center = attention - jnp.mean(attention, axis=1, keepdims=True)
        inverse = lax.rsqrt(jnp.mean(center * center, axis=1, keepdims=True) + EPSILON)
        normed = center * inverse
        grad_f = out_grad[span, :].astype(F32)
        gate_grad[span, :] = (grad_f * normed * gain_row).astype(BF16)
        gated = grad_f * update_gate[span, :].astype(F32)
        product = gated * normed
        for part in range(0, step, 8):
            gain_sum = gain_sum + product[part : part + 8, :]
        pushed = gated * gain_row
        attn_grad[span, :] = (
            inverse
            * (
                pushed
                - jnp.mean(pushed, axis=1, keepdims=True)
                - normed * jnp.mean(pushed * normed, axis=1, keepdims=True)
            )
        ).astype(BF16)
    gain_grad[...] = jnp.sum(gain_sum, axis=0, keepdims=True)


def backward_own_kernel(hop_list, heads, scaling, *refs):
    count = len(hop_list)
    table, masks = refs[0], refs[1 : 1 + count]
    query, grad = refs[1 + count : 3 + count]
    keys, values = refs[3 + count : 3 + 2 * count], refs[3 + 2 * count : 3 + 3 * count]
    query_out, key_out, value_out, bias_out = refs[3 + 3 * count :]
    width = query.shape[1] // heads
    pairs = [
        Pair(mask, table, heads, hops, hops == 0) for mask, hops in zip(masks, hop_list)
    ]
    lane = lax.broadcasted_iota(jnp.int32, bias_out.shape, 1)
    bias_total = [jnp.zeros(bias_out.shape, F32)]

    def scores(head):
        cols = columns(head, width)
        query_h, grad_h = query[:, cols], grad[:, cols]
        found = []
        for hops, key, value in zip(hop_list, keys, values):
            key_h, value_h = key[:, cols], value[:, cols]
            if hops == 0:
                found.append((contract(key_h, query_h, 1, 1), contract(value_h, grad_h, 1, 1)))
            else:
                found.append((contract(query_h, key_h, 1, 1), contract(grad_h, value_h, 1, 1)))
        return found

    def differentiate(head, found):
        cols = columns(head, width)
        query_part, bias_part = None, None
        for pair, hops, key, (score, weight_grad) in zip(pairs, hop_list, keys, found):
            half = pair.half_logits(score, head, scaling)
            tanh = jnp.tanh(half)
            logit_grad = weight_grad * (slope_of(half, tanh) * pair.mask)
            rounded = logit_grad.astype(BF16)
            if hops == 0:
                weights = ((half + half * tanh) * pair.mask).astype(BF16)
                key_out[:, cols] = contract(rounded, query[:, cols], 1, 0)
                value_out[:, cols] = contract(weights, grad[:, cols], 1, 0)
                added = contract(rounded, key[:, cols], 0, 0)
            else:
                added = contract(rounded, key[:, cols], 1, 0)
            query_part = added if query_part is None else query_part + added
            sums = pair.bias_rows(logit_grad)
            bias_part = sums if bias_part is None else bias_part + sums
        query_out[:, cols] = query_part
        sums = jnp.sum(bias_part, axis=1, keepdims=True)
        bias_total[0] = jnp.where(lane == head, sums, bias_total[0])

    in_stages(heads, scores, differentiate, 1)
    bias_out[...] = bias_total[0]


def backward_far_kernel(hops, heads, scaling, *refs):
    table, mask, query, grad, key, value, bias_in, gain_in, query_out, small_out = refs
    width = query.shape[1] // heads
    pair = Pair(mask, table, heads, hops)
    lane = lax.broadcasted_iota(jnp.int32, bias_in.shape, 1)
    bias_total = [bias_in[...]]

    def scores(head):
        cols = columns(head, width)
        score = contract(query[:, cols], key[:, cols], 1, 1)
        return score, contract(grad[:, cols], value[:, cols], 1, 1)

    def differentiate(head, found):
        cols = columns(head, width)
        half = pair.half_logits(found[0], head, scaling)
        logit_grad = found[1] * (slope_of(half, jnp.tanh(half)) * pair.mask)
        query_out[:, cols] = contract(logit_grad.astype(BF16), key[:, cols], 1, 0).astype(BF16)
        sums = jnp.sum(pair.bias_rows(logit_grad), axis=1, keepdims=True)
        bias_total[0] = bias_total[0] + jnp.where(lane == head, sums, 0.0)

    in_stages(heads, scores, differentiate)
    lanes = small_out.shape[1]
    lines = gain_in.shape[1] // lanes
    for line in range(lines):
        small_out[line : line + 1, :] = gain_in[:, line * lanes : (line + 1) * lanes]
    small_out[lines:, :] = bias_total[0]


def backward_key_kernel(hops, heads, scaling, *refs):
    table, mask, query, grad, key, value, key_in, value_in, key_out, value_out = refs
    last = key_out.dtype == BF16
    width = query.shape[1] // heads
    pair = Pair(mask, table, heads, hops, True)

    def scores(head):
        cols = columns(head, width)
        score = contract(key[:, cols], query[:, cols], 1, 1)
        return score, contract(value[:, cols], grad[:, cols], 1, 1)

    def differentiate(head, found):
        cols = columns(head, width)
        half = pair.half_logits(found[0], head, scaling)
        tanh = jnp.tanh(half)
        rounded = (found[1] * (slope_of(half, tanh) * pair.mask)).astype(BF16)
        weights = ((half + half * tanh) * pair.mask).astype(BF16)
        key_part = key_in[:, cols] + contract(rounded, query[:, cols], 1, 0)
        value_part = value_in[:, cols] + contract(weights, grad[:, cols], 1, 0)
        if last:
            key_part = key_part * scaling
        key_out[:, cols] = key_part.astype(key_out.dtype)
        value_out[:, cols] = value_part.astype(value_out.dtype)

    in_stages(heads, scores, differentiate)


def query_kernel(scaling, total, part, out):
    out[...] = ((total[...] + part[...].astype(F32)) * scaling).astype(BF16)


def on_device(kernel, outs, args, smem=(), ahead=()):
    count = len(args)

    def body(*refs):
        kernel(*refs[: len(smem) + count], *refs[len(smem) + count + len(ahead) :])

    return pl.pallas_call(
        body,
        out_shape=outs,
        in_specs=[pl.BlockSpec(memory_space=pltpu.SMEM)] * len(smem)
        + [pl.BlockSpec(memory_space=pltpu.VMEM)] * count
        + [pl.BlockSpec(memory_space=pl.ANY)] * len(ahead),
        out_specs=[pl.BlockSpec(memory_space=pltpu.VMEM)] * len(outs),
        compiler_params=pltpu.CompilerParams(vmem_limit_bytes=VMEM_LIMIT),
        cost_estimate=pl.CostEstimate(flops=1000000, bytes_accessed=100000, transcendentals=0),
    )(*smem, *args, *ahead)


def summed_over(array, axes):
    return jnp.sum(lax.all_gather(array, axes), axis=0)


def local(queries, key_rows, value_rows, update_gate, out_grad, user_lengths, rel_bias, norm_gain):
    rows, features = queries.shape[1:]
    levels, heads = rel_bias.shape
    scaling = (features // heads) ** (-0.5)
    query, key, value = queries[0], key_rows[0], value_rows[0]
    reach = min(3, lax.axis_size("ctx") // 2)
    wide = jax.ShapeDtypeStruct((rows, features), F32)
    narrow = jax.ShapeDtypeStruct((rows, features), BF16)

    keys, values = [key], [value]
    for _ in range(reach - 1):
        keys.append(passed_along(keys[-1], "ctx", 1))
        values.append(passed_along(values[-1], "ctx", 1))
    later_queries = [query] + [passed_along(query, "ctx", -hops) for hops in range(1, reach + 1)]

    near = tuple(range(1, reach))
    plan = [(0, 0, False), (0, 0, True), (1, reach, False)]
    plan += [(0, hops, False) for hops in near]
    plan += [(hops, hops, True) for hops in range(1, reach + 1)]
    outs = [jax.ShapeDtypeStruct((levels * heads, rows), F32)]
    outs += [jax.ShapeDtypeStruct((rows, rows), F32)] * len(plan)
    table, *masks = on_device(partial(mask_kernel, plan), outs, (), (user_lengths, rel_bias))
    mask_of = dict(zip(plan, masks))
    near_masks = [mask_of[0, hops, False] for hops in near]
    (attention,) = on_device(
        partial(forward_kernel, (0,), heads, scaling),
        [wide],
        (table, mask_of[0, 0, False], query, key, value),
    )
    far = (table, mask_of[1, reach, False], later_queries[1])
    (far_part,) = on_device(
        partial(forward_kernel, (reach,), heads, scaling), [narrow], (*far, keys[-1], values[-1])
    )
    far_part = passed_along(far_part, "ctx", 1)
    if near:
        (attention,) = on_device(
            partial(forward_kernel, near, heads, scaling),
            [wide],
            (table, *near_masks, query, *keys[1:], *values[1:], attention),
        )
    attn_grad, gate_grad, gain_part = on_device(
        norm_kernel,
        [narrow, narrow, jax.ShapeDtypeStruct((1, features), F32)],
        (attention, far_part, out_grad[0], update_gate[0], norm_gain[None]),
        ahead=later_queries[2:],
    )
    later_grads = [attn_grad]
    for _ in range(reach):
        later_grads.append(passed_along(later_grads[-1], "ctx", -1))

    lanes = features // 8
    query_total, key_total, value_total, bias_part = on_device(
        partial(backward_own_kernel, (0, *near), heads, scaling),
        [wide, wide, wide, jax.ShapeDtypeStruct((levels, lanes), F32)],
        (table, mask_of[0, 0, True], *near_masks, query, attn_grad, *keys, *values),
    )
    query_part, sums = on_device(
        partial(backward_far_kernel, reach, heads, scaling),
        [narrow, jax.ShapeDtypeStruct((8 + levels, lanes), F32)],
        (*far, later_grads[1], keys[-1], values[-1], bias_part, gain_part),
    )
    query_part = passed_along(query_part, "ctx", 1)
    sums = summed_over(sums, ("ctx", "dp"))
    for hops in range(1, reach + 1):
        key_total, value_total = on_device(
            partial(backward_key_kernel, hops, heads, scaling),
            [narrow if hops == reach else wide] * 2,
            (
                table,
                mask_of[hops, hops, True],
                later_queries[hops],
                later_grads[hops],
                key,
                value,
                key_total,
                value_total,
            ),
        )
    (query_grad,) = on_device(partial(query_kernel, scaling), [narrow], (query_total, query_part))
    return (
        query_grad[None],
        key_total[None],
        value_total[None],
        gate_grad[None],
        sums[8:, :heads],
        sums[:8].reshape(features),
    )


def solution(mesh):
    in_specs = (
        P(("groups", "dp"), "ctx", None),
        P(("groups", "dp"), "ctx", None),
        P(("groups", "dp"), "ctx", None),
        P(("groups", "dp"), "ctx", None),
        P(("groups", "dp"), "ctx", None),
        P(("groups", "dp"), None),
        P(),
        P(),
    )
    out_specs = (
        P(("groups", "dp"), "ctx", None),
        P(("groups", "dp"), "ctx", None),
        P(("groups", "dp"), "ctx", None),
        P(("groups", "dp"), "ctx", None),
        P("groups", None),
        P("groups"),
    )
    return jax.shard_map(local, mesh=mesh, in_specs=in_specs, out_specs=out_specs, check_vma=False)
```

time: 77.2 us -> 78.5 us (1.017)
  blocking collectives: 0 us -> 21 us
  waiting for transfers between devices: 27.3 us -> 14.7 us
  Pallas kernels: 18.2 us -> 9.88 us
  starting transfers between devices: 27.8 us -> 28.7 us
    all_gather x0 -> x1, blocking collectives: none -> 21 us  [summed_over(): return jnp.sum(lax.all_gather(array, axes), axis=0)]
    ppermute x4 -> x0, waiting for transfers between devices: 15.9 us -> none  [summed_over(): lax.ppermute(array, axis, [(i, i ^ step) for i in range(size)])]
    pallas_call x8 -> x10, Pallas kernels: 18.2 us -> 9.88 us  [on_device(): pl.pallas_call(body, out_shape=outs, in_specs=[pl.BlockSpec(memory_space=...]
    ppermute x8, starting transfers between devices: 20.8 us -> 28.7 us  [passed_along(): return lax.ppermute(array, axis, pairs)]
    ppermute x4 -> x0, starting transfers between devices: 7.02 us -> none  [summed_over(): lax.ppermute(array, axis, [(i, i ^ step) for i in range(size)])]
    ppermute x8, waiting for transfers between devices: 11.4 us -> 14.7 us  [passed_along(): return lax.ppermute(array, axis, pairs)]
    reduce_sum x0 -> x1, other arithmetic: none -> 0.92 us  [summed_over(): return jnp.sum(lax.all_gather(array, axes), axis=0)]
  transfers between devices with their start and end apart: 12 -> 8, of which waited for: 7 -> 5; matrix products, arithmetic and copies ran while one was open for 3% -> 3% of each run, Pallas kernels for 13% -> 7%
where the time goes in v2:
time: 78.5 us; the launch traced here: 78.1 us
  starting transfers between devices  28.7 us (37%)
  blocking collectives  21 us (27%)
  waiting for transfers between devices  14.7 us (19%)
  Pallas kernels  9.88 us (13%)
  local copies, waits for them, and re-layouts  2.07 us (3%)
  other arithmetic  0.92 us (1%)
  between operations  0.84 us (1%)
    ppermute x8, starting transfers between devices, passed_along(): return lax.ppermute(array, axis, pairs)  28.7 us
    all_gather x1, blocking collectives, summed_over(): return jnp.sum(lax.all_gather(array, axes), axis=0)  21 us
    ppermute x8, waiting for transfers between devices, passed_along(): return lax.ppermute(array, axis, pairs)  14.7 us
    pallas_call x10, Pallas kernels, on_device(): pl.pallas_call(body, out_shape=outs, in_specs=[pl.BlockSpec(memory_space=...  9.88 us
  transfers between devices with their start and end apart: 8, of which 5 were waited for; matrix products, arithmetic and copies ran while one was open for 3% of the time, Pallas kernels for 7%

profile of v2, /device:TPU:0, one launch (start us, length us, event | category | flops | bytes accessed | tf_op | source)
XLA Modules:
  0.0 78.1 jit_solution(10763037923824256394)
XLA Ops:
  0.6 0.0 copy-start.8
  0.6 4.9 %collective-permute-start = (bf16[128,1024]{1,0:T(8,128)(2,1)}, bf16[128,1024]{1,0:T(8,128)(2,1)S(1)}, u32[]{:S(2)}, u32[]{:S(2)}) collective-permute-start(bf16[128,1024]{1,0:T(8,128)(2,1)} %bitcast.13), channel_id=1, source_target_pairs={{0,4},{4,8},{8,12},{1,5},{5,9},{9,13},{2,6},{6,10},{10,14},{3,7},{... | collective-permute-start | bytes 786440 | tf_op jit(solution)/shard_map/ppermute | solution.py:19
  5.6 0.0 copy-start.9
  5.6 3.5 %collective-permute-start.1 = (bf16[128,1024]{1,0:T(8,128)(2,1)}, bf16[128,1024]{1,0:T(8,128)(2,1)S(1)}, u32[]{:S(2)}, u32[]{:S(2)}) collective-permute-start(bf16[128,1024]{1,0:T(8,128)(2,1)} %bitcast.18), channel_id=1, source_target_pairs={{0,4},{4,8},{8,12},{1,5},{5,9},{9,13},{2,6},{6,10},{10,14},{3,7},{... | collective-permute-start | bytes 786440 | tf_op jit(solution)/shard_map/ppermute | solution.py:19
  9.1 1.3 %collective-permute-start.2 = (bf16[128,1024]{1,0:T(8,128)(2,1)}, bf16[128,1024]{1,0:T(8,128)(2,1)S(1)}, u32[]{:S(2)}, u32[]{:S(2)}) collective-permute-start(bf16[128,1024]{1,0:T(8,128)(2,1)} %bitcast.23), channel_id=1, source_target_pairs={{4,0},{8,4},{12,8},{5,1},{9,5},{13,9},{6,2},{10,6},{14,10},{7,3},{... | collective-permute-start | bytes 786440 | tf_op jit(solution)/shard_map/ppermute | solution.py:19
  10.4 1.3 %collective-permute-start.4 = (bf16[128,1024]{1,0:T(8,128)(2,1)}, bf16[128,1024]{1,0:T(8,128)(2,1)S(1)}, u32[]{:S(2)}, u32[]{:S(2)}) collective-permute-start(bf16[128,1024]{1,0:T(8,128)(2,1)} %bitcast.24), channel_id=1, source_target_pairs={{8,0},{12,4},{9,1},{13,5},{10,2},{14,6},{11,3},{15,7},{24,16},{28,... | collective-permute-start | bytes 786440 | tf_op jit(solution)/shard_map/ppermute | solution.py:19
  11.7 0.0 copy-done.8
  11.7 0.0 copy-done.9
  11.7 0.8 shard_map.127
  12.5 0.0 copy-start.5
  12.5 0.1 collective-permute-done.refs_3_.refs_6_.refs_4_
  12.6 4.5 %collective-permute-done.1.refs_4_.refs_8_.refs_5_ = bf16[128,1024]{1,0:T(8,128)(2,1)S(1)} collective-permute-done((bf16[128,1024]{1,0:T(8,128)(2,1)}, bf16[128,1024]{1,0:T(8,128)(2,1)S(1)}, u32[]{:S(2)}, u32[]{:S(2)}) %collective-permute-start.1) | collective-permute-done | bytes 262176 | tf_op jit(solution)/shard_map/ppermute | solution.py:19
  17.1 1.9 %collective-permute-done.2.refs_2_ = bf16[128,1024]{1,0:T(8,128)(2,1)S(1)} collective-permute-done((bf16[128,1024]{1,0:T(8,128)(2,1)}, bf16[128,1024]{1,0:T(8,128)(2,1)S(1)}, u32[]{:S(2)}, u32[]{:S(2)}) %collective-permute-start.2) | collective-permute-done | bytes 262176 | tf_op jit(solution)/shard_map/ppermute | solution.py:19
  19.0 0.0 copy-start
  19.0 0.0 copy-start.1
  19.0 0.5 shard_map.130
  19.5 0.0 copy-done.5
  19.5 10.6 %collective-permute-start.3 = (bf16[128,1024]{1,0:T(8,128)(2,1)S(1)}, bf16[128,1024]{1,0:T(8,128)(2,1)S(1)}, u32[]{:S(2)}, u32[]{:S(2)}) collective-permute-start(bf16[128,1024]{1,0:T(8,128)(2,1)S(1)} %shard_map.130), channel_id=1, source_target_pairs={{0,4},{4,8},{8,12},{1,5},{5,9},{9,13},{2,6},{6,10},{10,14},{3,7},{... | collective-permute-start | bytes 786440 | tf_op jit(solution)/shard_map/ppermute | solution.py:19
  30.1 0.0 copy-done
  30.1 0.0 copy-done.1
  30.2 0.0 copy-done.2
  30.2 0.6 shard_map.128.refs_5_
  30.8 0.0 copy-start.3
  30.8 0.0 copy-start.4
  30.8 0.5 shard_map.129.refs_0_
  31.3 0.0 copy-start.7
  31.4 0.0 collective-permute-done.4.refs_5_.refs_2_
  31.4 2.6 %collective-permute-done.3.refs_1_ = bf16[128,1024]{1,0:T(8,128)(2,1)S(1)} collective-permute-done((bf16[128,1024]{1,0:T(8,128)(2,1)S(1)}, bf16[128,1024]{1,0:T(8,128)(2,1)S(1)}, u32[]{:S(2)}, u32[]{:S(2)}) %collective-permute-start.3) | collective-permute-done | bytes 262176 | tf_op jit(solution)/shard_map/ppermute | solution.py:19
  34.0 0.0 copy-done.3
  34.0 0.0 copy-done.4
  34.0 0.0 copy-done.7
  34.0 1.1 %shard_map.131 = (bf16[128,1024]{1,0:T(8,128)(2,1)S(1)}, bf16[128,1024]{1,0:T(8,128)(2,1)}, f32[1,1024]{1,0:T(1,128)S(1)}) custom-call(f32[128,1024]{1,0:T(8,128)S(1)} %shard_map.129.refs_0_, bf16[128,1024]{1,0:T(8,128)(2,1)S(1)} %collective-permute-done.3.refs_1_, bf16[128,1024]{1,0:T(8,128)(2,1)S(1)} %bitcast.28, bf16[128,1024]{1,0:T(8,128)(2,1)S(1)} %bitcast.29, ...), custom_call_target="tpu_custom_call" | custom-call | flops 1000000 | bytes 100000 | tf_op jit(solution)/shard_map/pallas_call | solution.py:282
  35.1 1.3 %collective-permute-start.5 = (bf16[128,1024]{1,0:T(8,128)(2,1)S(1)}, bf16[128,1024]{1,0:T(8,128)(2,1)S(1)}, u32[]{:S(2)}, u32[]{:S(2)}) collective-permute-start(bf16[128,1024]{1,0:T(8,128)(2,1)S(1)} %get-tuple-element.31.refs_4_), channel_id=1, source_target_pairs={{4,0},{8,4},{12,8},{5,1},{9,5},{13,9},{6,2},{10,6},{14,10},{7,3},{... | collective-permute-start | bytes 786440 | tf_op jit(solution)/shard_map/ppermute | solution.py:19
  36.4 1.8 %shard_map.132 = (f32[128,1024]{1,0:T(8,128)S(1)}, f32[128,1024]{1,0:T(8,128)S(1)}, f32[128,1024]{1,0:T(8,128)S(1)}, f32[8,128]{1,0:T(8,128)S(1)}) custom-call(f32[64,128]{1,0:T(8,128)S(1)} %get-tuple-element.26.refs_0_, f32[128,128]{1,0:T(8,128)S(1)} %get-tuple-element.27.refs_1_, f32[128,128]{1,0:T(8,128)S(1)} %get-tuple-element.28.refs_1_.refs_2_, ...), custom_call_target="tpu_custom_call" | custom-call | flops 1000000 | bytes 100000 | tf_op jit(solution)/shard_map/pallas_call | solution.py:282
  38.2 5.6 %collective-permute-done.5.refs_3_ = bf16[128,1024]{1,0:T(8,128)(2,1)S(1)} collective-permute-done((bf16[128,1024]{1,0:T(8,128)(2,1)S(1)}, bf16[128,1024]{1,0:T(8,128)(2,1)S(1)}, u32[]{:S(2)}, u32[]{:S(2)}) %collective-permute-start.5) | collective-permute-done | bytes 262176 | tf_op jit(solution)/shard_map/ppermute | solution.py:19
  43.8 1.4 %shard_map.133 = (bf16[128,1024]{1,0:T(8,128)(2,1)}, f32[16,128]{1,0:T(8,128)S(1)}) custom-call(f32[64,128]{1,0:T(8,128)S(1)} %get-tuple-element.26.refs_0_, f32[128,128]{1,0:T(8,128)S(1)} %get-tuple-element.30.refs_1_, bf16[128,1024]{1,0:T(8,128)(2,1)S(1)} %collective-permute-done.2.refs_2_, bf16[128,1024]{1,0:T(8,128)(2,1)S(1)} %collective-permute-done.5.refs_3_, ...), custom_call_target="tpu_custom_call" | custom-call | flops 1000000 | bytes 100000 | tf_op jit(solution)/shard_map/pallas_call | solution.py:282
  45.2 4.5 %collective-permute-start.6 = (bf16[128,1024]{1,0:T(8,128)(2,1)}, bf16[128,1024]{1,0:T(8,128)(2,1)S(1)}, u32[]{:S(2)}, u32[]{:S(2)}) collective-permute-start(bf16[128,1024]{1,0:T(8,128)(2,1)} %get-tuple-element.35), channel_id=1, source_target_pairs={{0,4},{4,8},{8,12},{1,5},{5,9},{9,13},{2,6},{6,10},{10,14},{3,7},{... | collective-permute-start | bytes 786440 | tf_op jit(solution)/shard_map/ppermute | solution.py:19
  49.7 1.3 %collective-permute-start.7 = (bf16[128,1024]{1,0:T(8,128)(2,1)S(1)}, bf16[128,1024]{1,0:T(8,128)(2,1)S(1)}, u32[]{:S(2)}, u32[]{:S(2)}) collective-permute-start(bf16[128,1024]{1,0:T(8,128)(2,1)S(1)} %collective-permute-done.5.refs_3_), channel_id=1, source_target_pairs={{4,0},{8,4},{12,8},{5,1},{9,5},{13,9},{6,2},{10,6},{14,10},{7,3},{... | collective-permute-start | bytes 786440 | tf_op jit(solution)/shard_map/ppermute | solution.py:19
  51.0 21.0 %all-gather = f32[256,128]{1,0:T(8,128)} all-gather(f32[16,128]{1,0:T(8,128)S(1)} %get-tuple-element.45), channel_id=2, replica_groups=mesh['groups'=2,'ctx'=4,'dp'=4] {'ctx','dp'}, dimensions={0}, use_global_device_ids=true | all-gather | bytes 139264 | tf_op jit(solution)/shard_map/all_gather | solution.py:295
  72.0 0.9 %reduce_sum.9 = f32[16,128]{1,0:T(8,128)S(1)} reduce(f32[16,16,128]{2,1,0:T(8,128)} %bitcast.31, f32[]{:T(128)} %constant.0.clone.1), dimensions={0}, to_apply=%region_0.0 | reduce | flops 30720 | bytes 139268 | tf_op jit(solution)/shard_map/reduce_sum | solution.py:295
  72.9 0.6 slice.8
  73.5 0.8 %copy-done.6 = f32[128,128]{1,0:T(8,128)S(1)} copy-done((f32[128,128]{1,0:T(8,128)S(1)}, f32[128,128]{1,0:T(8,128)}, u32[]{:S(2)}) %copy-start.6) | copy-done | bytes 65560
  74.4 0.8 %shard_map.135 = (f32[128,1024]{1,0:T(8,128)S(1)}, f32[128,1024]{1,0:T(8,128)S(1)}) custom-call(f32[64,128]{1,0:T(8,128)S(1)} %get-tuple-element.26.refs_0_, f32[128,128]{1,0:T(8,128)S(1)} %copy-done.6, bf16[128,1024]{1,0:T(8,128)(2,1)S(1)} %collective-permute-done.2.refs_2_, bf16[128,1024]{1,0:T(8,128)(2,1)S(1)} %collective-permute-done.5.refs_3_, ...), custom_call_target="tpu_custom_call" | custom-call | flops 1000000 | bytes 100000 | tf_op jit(solution)/shard_map/pallas_call | solution.py:282
  75.2 0.6 slice_bitcast_fusion
  75.7 0.0 collective-permute-done.6.refs_1_
  75.8 0.8 shard_map.134
  76.5 0.0 collective-permute-done.7.refs_3_
  76.5 1.6 %shard_map.136 = (bf16[128,1024]{1,0:T(8,128)(2,1)}, bf16[128,1024]{1,0:T(8,128)(2,1)}) custom-call(f32[64,128]{1,0:T(8,128)S(1)} %get-tuple-element.26.refs_0_, f32[128,128]{1,0:T(8,128)S(1)} %get-tuple-element.36.refs_1_, bf16[128,1024]{1,0:T(8,128)(2,1)S(1)} %collective-permute-done.4.refs_5_.refs_2_, ...), custom_call_target="tpu_custom_call" | custom-call | flops 1000000 | bytes 100000 | tf_op jit(solution)/shard_map/pallas_call | solution.py:282
  (2 shorter events, 0.0 us)
Async XLA Ops:
  0.6 11.1 %copy-start.8 = (f32[8,8]{1,0:T(8,128)S(1)}, f32[8,8]{1,0:T(8,128)}, u32[]{:S(2)}) copy-start(f32[8,8]{1,0:T(8,128)} %refs_1_.1) | copy-start | bytes 772
  0.6 11.9 %collective-permute-start = (bf16[128,1024]{1,0:T(8,128)(2,1)}, bf16[128,1024]{1,0:T(8,128)(2,1)S(1)}, u32[]{:S(2)}, u32[]{:S(2)}) collective-permute-start(bf16[128,1024]{1,0:T(8,128)(2,1)} %bitcast.13), channel_id=1, source_target_pairs={{0,4},{4,8},{8,12},{1,5},{5,9},{9,13},{2,6},{6,10},{10,14},{3,7},{... | collective-permute-start | bytes 786440 | tf_op jit(solution)/shard_map/ppermute | solution.py:19
  5.6 6.1 %copy-start.9 = (s32[1,4]{1,0:T(1,128)S(1)}, s32[1,4]{1,0:T(1,128)}, u32[]{:S(2)}) copy-start(s32[1,4]{1,0:T(1,128)} %refs_0_.1) | copy-start | bytes 52
  5.6 11.5 %collective-permute-start.1 = (bf16[128,1024]{1,0:T(8,128)(2,1)}, bf16[128,1024]{1,0:T(8,128)(2,1)S(1)}, u32[]{:S(2)}, u32[]{:S(2)}) collective-permute-start(bf16[128,1024]{1,0:T(8,128)(2,1)} %bitcast.18), channel_id=1, source_target_pairs={{0,4},{4,8},{8,12},{1,5},{5,9},{9,13},{2,6},{6,10},{10,14},{3,7},{... | collective-permute-start | bytes 786440 | tf_op jit(solution)/shard_map/ppermute | solution.py:19
  9.1 9.9 %collective-permute-start.2 = (bf16[128,1024]{1,0:T(8,128)(2,1)}, bf16[128,1024]{1,0:T(8,128)(2,1)S(1)}, u32[]{:S(2)}, u32[]{:S(2)}) collective-permute-start(bf16[128,1024]{1,0:T(8,128)(2,1)} %bitcast.23), channel_id=1, source_target_pairs={{4,0},{8,4},{12,8},{5,1},{9,5},{13,9},{6,2},{10,6},{14,10},{7,3},{... | collective-permute-start | bytes 786440 | tf_op jit(solution)/shard_map/ppermute | solution.py:19
  10.4 21.0 %collective-permute-start.4 = (bf16[128,1024]{1,0:T(8,128)(2,1)}, bf16[128,1024]{1,0:T(8,128)(2,1)S(1)}, u32[]{:S(2)}, u32[]{:S(2)}) collective-permute-start(bf16[128,1024]{1,0:T(8,128)(2,1)} %bitcast.24), channel_id=1, source_target_pairs={{8,0},{12,4},{9,1},{13,5},{10,2},{14,6},{11,3},{15,7},{24,16},{28,... | collective-permute-start | bytes 786440 | tf_op jit(solution)/shard_map/ppermute | solution.py:19
  12.5 7.0 %copy-start.5 = (f32[128,128]{1,0:T(8,128)}, f32[128,128]{1,0:T(8,128)S(1)}, u32[]{:S(2)}) copy-start(f32[128,128]{1,0:T(8,128)S(1)} %get-tuple-element.37.refs_1_) | copy-start | bytes 196612
  19.0 11.2 %copy-start = (bf16[1,128,1024]{2,1,0:T(8,128)(2,1)S(1)}, bf16[1,128,1024]{2,1,0:T(8,128)(2,1)}, u32[]{:S(2)}) copy-start(bf16[1,128,1024]{2,1,0:T(8,128)(2,1)} %param.9) | copy-start | bytes 786436
  19.0 11.2 %copy-start.1 = (bf16[1,128,1024]{2,1,0:T(8,128)(2,1)S(1)}, bf16[1,128,1024]{2,1,0:T(8,128)(2,1)}, u32[]{:S(2)}) copy-start(bf16[1,128,1024]{2,1,0:T(8,128)(2,1)} %param.10) | copy-start | bytes 786436
  19.0 11.2 %copy-start.2 = (bf16[1,128,1024]{2,1,0:T(8,128)(2,1)S(1)}, bf16[1,128,1024]{2,1,0:T(8,128)(2,1)}, u32[]{:S(2)}) copy-start(bf16[1,128,1024]{2,1,0:T(8,128)(2,1)} %param.8) | copy-start | bytes 786436
  19.5 14.5 %collective-permute-start.3 = (bf16[128,1024]{1,0:T(8,128)(2,1)S(1)}, bf16[128,1024]{1,0:T(8,128)(2,1)S(1)}, u32[]{:S(2)}, u32[]{:S(2)}) collective-permute-start(bf16[128,1024]{1,0:T(8,128)(2,1)S(1)} %shard_map.130), channel_id=1, source_target_pairs={{0,4},{4,8},{8,12},{1,5},{5,9},{9,13},{2,6},{6,10},{10,14},{3,7},{... | collective-permute-start | bytes 786440 | tf_op jit(solution)/shard_map/ppermute | solution.py:19
  30.8 3.2 %copy-start.3 = (bf16[1,128,1024]{2,1,0:T(8,128)(2,1)S(1)}, bf16[1,128,1024]{2,1,0:T(8,128)(2,1)}, u32[]{:S(2)}) copy-start(bf16[1,128,1024]{2,1,0:T(8,128)(2,1)} %param.12) | copy-start | bytes 786436
  30.8 3.2 %copy-start.4 = (bf16[1,128,1024]{2,1,0:T(8,128)(2,1)S(1)}, bf16[1,128,1024]{2,1,0:T(8,128)(2,1)}, u32[]{:S(2)}) copy-start(bf16[1,128,1024]{2,1,0:T(8,128)(2,1)} %param.11) | copy-start | bytes 786436
  31.3 2.7 %copy-start.7 = (f32[1024]{0:T(1024)S(1)}, f32[1024]{0:T(1024)}, u32[]{:S(2)}) copy-start(f32[1024]{0:T(1024)} %param.15) | copy-start | bytes 12292
  35.1 8.7 %collective-permute-start.5 = (bf16[128,1024]{1,0:T(8,128)(2,1)S(1)}, bf16[128,1024]{1,0:T(8,128)(2,1)S(1)}, u32[]{:S(2)}, u32[]{:S(2)}) collective-permute-start(bf16[128,1024]{1,0:T(8,128)(2,1)S(1)} %get-tuple-element.31.refs_4_), channel_id=1, source_target_pairs={{4,0},{8,4},{12,8},{5,1},{9,5},{13,9},{6,2},{10,6},{14,10},{7,3},{... | collective-permute-start | bytes 786440 | tf_op jit(solution)/shard_map/ppermute | solution.py:19
  45.2 30.6 %collective-permute-start.6 = (bf16[128,1024]{1,0:T(8,128)(2,1)}, bf16[128,1024]{1,0:T(8,128)(2,1)S(1)}, u32[]{:S(2)}, u32[]{:S(2)}) collective-permute-start(bf16[128,1024]{1,0:T(8,128)(2,1)} %get-tuple-element.35), channel_id=1, source_target_pairs={{0,4},{4,8},{8,12},{1,5},{5,9},{9,13},{2,6},{6,10},{10,14},{3,7},{... | collective-permute-start | bytes 786440 | tf_op jit(solution)/shard_map/ppermute | solution.py:19
  49.7 26.8 %collective-permute-start.7 = (bf16[128,1024]{1,0:T(8,128)(2,1)S(1)}, bf16[128,1024]{1,0:T(8,128)(2,1)S(1)}, u32[]{:S(2)}, u32[]{:S(2)}) collective-permute-start(bf16[128,1024]{1,0:T(8,128)(2,1)S(1)} %collective-permute-done.5.refs_3_), channel_id=1, source_target_pairs={{4,0},{8,4},{12,8},{5,1},{9,5},{13,9},{6,2},{10,6},{14,10},{7,3},{... | collective-permute-start | bytes 786440 | tf_op jit(solution)/shard_map/ppermute | solution.py:19
  73.5 0.8 %copy-start.6 = (f32[128,128]{1,0:T(8,128)S(1)}, f32[128,128]{1,0:T(8,128)}, u32[]{:S(2)}) copy-start(f32[128,128]{1,0:T(8,128)} %copy-done.5) | copy-start | bytes 196612

commit v3 on v2

--- a/solution.py
+++ b/solution.py
@@ -134,14 +134,14 @@
     in_stages(heads, scores, attend)
 
 
-def norm_kernel(total, far_part, out_grad, update_gate, gain, attn_grad, gate_grad, gain_grad):
+def norm_kernel(total, out_grad, update_gate, gain, attn_grad, gate_grad, gain_grad):
     rows, features = total.shape
     step = 16
     gain_row = gain[...]
     gain_sum = jnp.zeros((8, features), F32)
     for low in range(0, rows, step):
         span = slice(low, low + step)
-        attention = total[span, :] + far_part[span, :].astype(F32)
+        attention = total[span, :]
         center = attention - jnp.mean(attention, axis=1, keepdims=True)
         inverse = lax.rsqrt(jnp.mean(center * center, axis=1, keepdims=True) + EPSILON)
         normed = center * inverse
@@ -168,13 +168,16 @@
     table, masks = refs[0], refs[1 : 1 + count]
     query, grad = refs[1 + count : 3 + count]
     keys, values = refs[3 + count : 3 + 2 * count], refs[3 + 2 * count : 3 + 3 * count]
-    query_out, key_out, value_out, bias_out = refs[3 + 3 * count :]
+    gain_in, query_out, key_out, value_out, small_out = refs[3 + 3 * count :]
     width = query.shape[1] // heads
     pairs = [
         Pair(mask, table, heads, hops, hops == 0) for mask, hops in zip(masks, hop_list)
     ]
-    lane = lax.broadcasted_iota(jnp.int32, bias_out.shape, 1)
-    bias_total = [jnp.zeros(bias_out.shape, F32)]
+    lanes = small_out.shape[1]
+    lines = gain_in.shape[1] // lanes
+    levels = small_out.shape[0] - lines
+    lane = lax.broadcasted_iota(jnp.int32, (levels, lanes), 1)
+    bias_total = [jnp.zeros((levels, lanes), F32)]
 
     def scores(head):
         cols = columns(head, width)
@@ -206,37 +209,11 @@
             query_part = added if query_part is None else query_part + added
             sums = pair.bias_rows(logit_grad)
             bias_part = sums if bias_part is None else bias_part + sums
-        query_out[:, cols] = query_part
+        query_out[:, cols] = (query_part * scaling).astype(BF16)
         sums = jnp.sum(bias_part, axis=1, keepdims=True)
         bias_total[0] = jnp.where(lane == head, sums, bias_total[0])
 
     in_stages(heads, scores, differentiate, 1)
-    bias_out[...] = bias_total[0]
-
-
-def backward_far_kernel(hops, heads, scaling, *refs):
-    table, mask, query, grad, key, value, bias_in, gain_in, query_out, small_out = refs
-    width = query.shape[1] // heads
-    pair = Pair(mask, table, heads, hops)
-    lane = lax.broadcasted_iota(jnp.int32, bias_in.shape, 1)
-    bias_total = [bias_in[...]]
-
-    def scores(head):
-        cols = columns(head, width)
-        score = contract(query[:, cols], key[:, cols], 1, 1)
-        return score, contract(grad[:, cols], value[:, cols], 1, 1)
-
-    def differentiate(head, found):
-        cols = columns(head, width)
-        half = pair.half_logits(found[0], head, scaling)
-        logit_grad = found[1] * (slope_of(half, jnp.tanh(half)) * pair.mask)
-        query_out[:, cols] = contract(logit_grad.astype(BF16), key[:, cols], 1, 0).astype(BF16)
-        sums = jnp.sum(pair.bias_rows(logit_grad), axis=1, keepdims=True)
-        bias_total[0] = bias_total[0] + jnp.where(lane == head, sums, 0.0)
-
-    in_stages(heads, scores, differentiate)
-    lanes = small_out.shape[1]
-    lines = gain_in.shape[1] // lanes
     for line in range(lines):
         small_out[line : line + 1, :] = gain_in[:, line * lanes : (line + 1) * lanes]
     small_out[lines:, :] = bias_total[0]
@@ -269,10 +246,6 @@
     in_stages(heads, scores, differentiate)
 
 
-def query_kernel(scaling, total, part, out):
-    out[...] = ((total[...] + part[...].astype(F32)) * scaling).astype(BF16)
-
-
 def on_device(kernel, outs, args, smem=(), ahead=()):
     count = len(args)
 
@@ -291,8 +264,15 @@
     )(*smem, *args, *ahead)
 
 
-def summed_over(array, axes):
-    return jnp.sum(lax.all_gather(array, axes), axis=0)
+def partners_of(axes):
+    rounds = []
+    for axis in axes:
+        size = lax.axis_size(axis)
+        step = 1
+        while step < size:
+            rounds.append((axis, [(i, i ^ step) for i in range(size)]))
+            step = 2 * step
+    return rounds
 
 
 def local(queries, key_rows, value_rows, update_gate, out_grad, user_lengths, rel_bias, norm_gain):
@@ -304,67 +284,52 @@
     wide = jax.ShapeDtypeStruct((rows, features), F32)
     narrow = jax.ShapeDtypeStruct((rows, features), BF16)
 
-    keys, values = [key], [value]
-    for _ in range(reach - 1):
+    keys, values, later_queries = [key], [value], [query]
+    for _ in range(reach):
         keys.append(passed_along(keys[-1], "ctx", 1))
         values.append(passed_along(values[-1], "ctx", 1))
-    later_queries = [query] + [passed_along(query, "ctx", -hops) for hops in range(1, reach + 1)]
-
-    near = tuple(range(1, reach))
-    plan = [(0, 0, False), (0, 0, True), (1, reach, False)]
-    plan += [(0, hops, False) for hops in near]
-    plan += [(hops, hops, True) for hops in range(1, reach + 1)]
+        later_queries.append(passed_along(later_queries[-1], "ctx", -1))
+
+    hop_list = tuple(range(reach + 1))
+    plan = [(0, hops, False) for hops in hop_list] + [(hops, hops, True) for hops in hop_list]
     outs = [jax.ShapeDtypeStruct((levels * heads, rows), F32)]
     outs += [jax.ShapeDtypeStruct((rows, rows), F32)] * len(plan)
     table, *masks = on_device(partial(mask_kernel, plan), outs, (), (user_lengths, rel_bias))
-    mask_of = dict(zip(plan, masks))
-    near_masks = [mask_of[0, hops, False] for hops in near]
-    (attention,) = on_device(
-        partial(forward_kernel, (0,), heads, scaling),
-        [wide],
-        (table, mask_of[0, 0, False], query, key, value),
-    )
-    far = (table, mask_of[1, reach, False], later_queries[1])
-    (far_part,) = on_device(
-        partial(forward_kernel, (reach,), heads, scaling), [narrow], (*far, keys[-1], values[-1])
-    )
-    far_part = passed_along(far_part, "ctx", 1)
-    if near:
-        (attention,) = on_device(
-            partial(forward_kernel, near, heads, scaling),
+    masks, flipped = masks[: reach + 1], masks[reach + 1 :]
+    attention = ()
+    for hops in hop_list:
+        attention = on_device(
+            partial(forward_kernel, (hops,), heads, scaling),
             [wide],
-            (table, *near_masks, query, *keys[1:], *values[1:], attention),
+            (table, masks[hops], query, keys[hops], values[hops], *attention),
+            ahead=later_queries[hops : hops + 1] if 0 < hops < reach else (),
         )
     attn_grad, gate_grad, gain_part = on_device(
         norm_kernel,
         [narrow, narrow, jax.ShapeDtypeStruct((1, features), F32)],
-        (attention, far_part, out_grad[0], update_gate[0], norm_gain[None]),
-        ahead=later_queries[2:],
-    )
-    later_grads = [attn_grad]
-    for _ in range(reach):
-        later_grads.append(passed_along(later_grads[-1], "ctx", -1))
-
+        (*attention, out_grad[0], update_gate[0], norm_gain[None]),
+        ahead=later_queries[reach:],
+    )
     lanes = features // 8
-    query_total, key_total, value_total, bias_part = on_device(
-        partial(backward_own_kernel, (0, *near), heads, scaling),
-        [wide, wide, wide, jax.ShapeDtypeStruct((levels, lanes), F32)],
-        (table, mask_of[0, 0, True], *near_masks, query, attn_grad, *keys, *values),
-    )
-    query_part, sums = on_device(
-        partial(backward_far_kernel, reach, heads, scaling),
-        [narrow, jax.ShapeDtypeStruct((8 + levels, lanes), F32)],
-        (*far, later_grads[1], keys[-1], values[-1], bias_part, gain_part),
-    )
-    query_part = passed_along(query_part, "ctx", 1)
-    sums = summed_over(sums, ("ctx", "dp"))
+    query_grad, key_total, value_total, sums = on_device(
+        partial(backward_own_kernel, hop_list, heads, scaling),
+        [narrow, wide, wide, jax.ShapeDtypeStruct((8 + levels, lanes), F32)],
+        (table, flipped[0], *masks[1:], query, attn_grad, *keys, *values, gain_part),
+    )
+    rounds = partners_of(("dp", "ctx"))
+    later_grads = [attn_grad, passed_along(attn_grad, "ctx", -1)]
+    for number, (axis, pairs) in enumerate(rounds, 1):
+        sums = sums + lax.ppermute(sums, axis, pairs)
+        if number < reach:
+            arrived, sums = lax.optimization_barrier((later_grads[-1], sums))
+            later_grads.append(passed_along(arrived, "ctx", -1))
     for hops in range(1, reach + 1):
         key_total, value_total = on_device(
             partial(backward_key_kernel, hops, heads, scaling),
             [narrow if hops == reach else wide] * 2,
             (
                 table,
-                mask_of[hops, hops, True],
+                flipped[hops],
                 later_queries[hops],
                 later_grads[hops],
                 key,
@@ -373,7 +338,6 @@
                 value_total,
             ),
         )
-    (query_grad,) = on_device(partial(query_kernel, scaling), [narrow], (query_total, query_part))
     return (
         query_grad[None],
         key_total[None],

time: 78.5 us -> 57.7 us (0.74)
  blocking collectives: 21 us -> 0 us
  local copies, waits for them, and re-layouts: 2.07 us -> 4.08 us
  other arithmetic: 0.92 us -> 0.01 us
  Pallas kernels: 9.88 us -> 8.98 us
  waiting for transfers between devices: 14.7 us -> 13.8 us
  starting transfers between devices: 28.7 us -> 29.5 us
    all_gather x1 -> x0, blocking collectives: 21 us -> none  [summed_over(): return jnp.sum(lax.all_gather(array, axes), axis=0)]
    ppermute x0 -> x4, starting transfers between devices: none -> 7.39 us  [local(): sums = sums + lax.ppermute(sums, axis, pairs)]
    ppermute x8, waiting for transfers between devices: 14.7 us -> 8.03 us  [passed_along(): return lax.ppermute(array, axis, pairs)]
    ppermute x8, starting transfers between devices: 28.7 us -> 22.1 us  [passed_along(): return lax.ppermute(array, axis, pairs)]
    ppermute x0 -> x4, waiting for transfers between devices: none -> 5.76 us  [local(): sums = sums + lax.ppermute(sums, axis, pairs)]
    unnamed x20 -> x22, local copies, waits for them, and re-layouts: 0.88 us -> 2.89 us
    reduce_sum x1 -> x0, other arithmetic: 0.92 us -> none  [summed_over(): return jnp.sum(lax.all_gather(array, axes), axis=0)]
    pallas_call x10 -> x8, Pallas kernels: 9.88 us -> 8.98 us  [on_device(): pl.pallas_call(body, out_shape=outs, in_specs=[pl.BlockSpec(memory_space=...]
  transfers between devices with their start and end apart: 8 -> 12, of which waited for: 5 -> 8; matrix products, arithmetic and copies ran while one was open for 3% -> 2% of each run, Pallas kernels for 7% -> 11%
where the time goes in v3:
time: 57.7 us; the launch traced here: 57.3 us
  starting transfers between devices  29.5 us (51%)
  waiting for transfers between devices  13.8 us (24%)
  Pallas kernels  8.98 us (16%)
  local copies, waits for them, and re-layouts  4.08 us (7%)
  between operations  0.87 us (2%)
    ppermute x8, starting transfers between devices, passed_along(): return lax.ppermute(array, axis, pairs)  22.1 us
    pallas_call x8, Pallas kernels, on_device(): pl.pallas_call(body, out_shape=outs, in_specs=[pl.BlockSpec(memory_space=...  8.98 us
    ppermute x8, waiting for transfers between devices, passed_along(): return lax.ppermute(array, axis, pairs)  8.03 us
    ppermute x4, starting transfers between devices, local(): sums = sums + lax.ppermute(sums, axis, pairs)  7.39 us
    ppermute x4, waiting for transfers between devices, local(): sums = sums + lax.ppermute(sums, axis, pairs)  5.76 us
    unnamed x22, local copies, waits for them, and re-layouts  2.89 us
  transfers between devices with their start and end apart: 12, of which 8 were waited for; matrix products, arithmetic and copies ran while one was open for 2% of the time, Pallas kernels for 11%

profile of v3, /device:TPU:0, one launch (start us, length us, event | category | flops | bytes accessed | tf_op | source)
XLA Modules:
  0.0 57.3 jit_solution(4014039206679335553)
XLA Ops:
  0.6 0.0 copy-start.9
  0.6 4.9 %collective-permute-start = (bf16[128,1024]{1,0:T(8,128)(2,1)}, bf16[128,1024]{1,0:T(8,128)(2,1)S(1)}, u32[]{:S(2)}, u32[]{:S(2)}) collective-permute-start(bf16[128,1024]{1,0:T(8,128)(2,1)} %bitcast.12), channel_id=1, source_target_pairs={{0,4},{4,8},{8,12},{1,5},{5,9},{9,13},{2,6},{6,10},{10,14},{3,7},{... | collective-permute-start | bytes 786440 | tf_op jit(solution)/shard_map/ppermute | solution.py:19
  5.6 0.0 copy-start.10
  5.6 3.5 %collective-permute-start.2 = (bf16[128,1024]{1,0:T(8,128)(2,1)}, bf16[128,1024]{1,0:T(8,128)(2,1)S(1)}, u32[]{:S(2)}, u32[]{:S(2)}) collective-permute-start(bf16[128,1024]{1,0:T(8,128)(2,1)} %bitcast.17), channel_id=1, source_target_pairs={{0,4},{4,8},{8,12},{1,5},{5,9},{9,13},{2,6},{6,10},{10,14},{3,7},{... | collective-permute-start | bytes 786440 | tf_op jit(solution)/shard_map/ppermute | solution.py:19
  9.1 1.3 %collective-permute-start.4 = (bf16[128,1024]{1,0:T(8,128)(2,1)}, bf16[128,1024]{1,0:T(8,128)(2,1)S(1)}, u32[]{:S(2)}, u32[]{:S(2)}) collective-permute-start(bf16[128,1024]{1,0:T(8,128)(2,1)} %bitcast.22), channel_id=1, source_target_pairs={{4,0},{8,4},{12,8},{5,1},{9,5},{13,9},{6,2},{10,6},{14,10},{7,3},{... | collective-permute-start | bytes 786440 | tf_op jit(solution)/shard_map/ppermute | solution.py:19
  10.4 2.2 %collective-permute-done.refs_3_.refs_7_ = bf16[128,1024]{1,0:T(8,128)(2,1)S(1)} collective-permute-done((bf16[128,1024]{1,0:T(8,128)(2,1)}, bf16[128,1024]{1,0:T(8,128)(2,1)S(1)}, u32[]{:S(2)}, u32[]{:S(2)}) %collective-permute-start) | collective-permute-done | bytes 262176 | tf_op jit(solution)/shard_map/ppermute | solution.py:19
  12.6 4.3 %collective-permute-start.1 = (bf16[128,1024]{1,0:T(8,128)(2,1)S(1)}, bf16[128,1024]{1,0:T(8,128)(2,1)S(1)}, u32[]{:S(2)}, u32[]{:S(2)}) collective-permute-start(bf16[128,1024]{1,0:T(8,128)(2,1)S(1)} %collective-permute-done.refs_3_.refs_7_), channel_id=1, source_target_pairs={{0,4},{4,8},{8,12},{1,5},{5,9},{9,13},{2,6},{6,10},{10,14},{3,7},{... | collective-permute-start | bytes 786440 | tf_op jit(solution)/shard_map/ppermute | solution.py:19
  16.9 1.3 %collective-permute-done.2.refs_4_.refs_10_ = bf16[128,1024]{1,0:T(8,128)(2,1)S(1)} collective-permute-done((bf16[128,1024]{1,0:T(8,128)(2,1)}, bf16[128,1024]{1,0:T(8,128)(2,1)S(1)}, u32[]{:S(2)}, u32[]{:S(2)}) %collective-permute-start.2) | collective-permute-done | bytes 262176 | tf_op jit(solution)/shard_map/ppermute | solution.py:19
  18.2 4.3 %collective-permute-start.3 = (bf16[128,1024]{1,0:T(8,128)(2,1)S(1)}, bf16[128,1024]{1,0:T(8,128)(2,1)S(1)}, u32[]{:S(2)}, u32[]{:S(2)}) collective-permute-start(bf16[128,1024]{1,0:T(8,128)(2,1)S(1)} %collective-permute-done.2.refs_4_.refs_10_), channel_id=1, source_target_pairs={{0,4},{4,8},{8,12},{1,5},{5,9},{9,13},{2,6},{6,10},{10,14},{3,7},{... | collective-permute-start | bytes 786440 | tf_op jit(solution)/shard_map/ppermute | solution.py:19
  22.5 0.0 collective-permute-done.4.refs_6_.refs_2_
  22.5 1.3 %collective-permute-start.5 = (bf16[128,1024]{1,0:T(8,128)(2,1)S(1)}, bf16[128,1024]{1,0:T(8,128)(2,1)S(1)}, u32[]{:S(2)}, u32[]{:S(2)}) collective-permute-start(bf16[128,1024]{1,0:T(8,128)(2,1)S(1)} %collective-permute-done.4.refs_6_.refs_2_), channel_id=1, source_target_pairs={{4,0},{8,4},{12,8},{5,1},{9,5},{13,9},{6,2},{10,6},{14,10},{7,3},{... | collective-permute-start | bytes 786440 | tf_op jit(solution)/shard_map/ppermute | solution.py:19
  23.8 0.0 copy-done.9
  23.8 0.0 copy-done.10
  23.8 0.7 %shard_map.127 = (f32[64,128]{1,0:T(8,128)S(1)}, f32[128,128]{1,0:T(8,128)S(1)}, f32[128,128]{1,0:T(8,128)S(1)}, f32[128,128]{1,0:T(8,128)S(1)}, f32[128,128]{1,...) custom-call(s32[1,4]{1,0:T(1,128)S(1)} %copy-done.10, f32[8,8]{1,0:T(8,128)S(1)} %copy-done.9), custom_call_target="tpu_custom_call" | custom-call | flops 1000000 | bytes 100000 | tf_op jit(solution)/shard_map/pallas_call | solution.py:255
  24.6 0.0 copy-start
  24.6 0.9 %copy-done = bf16[1,128,1024]{2,1,0:T(8,128)(2,1)S(1)} copy-done((bf16[1,128,1024]{2,1,0:T(8,128)(2,1)S(1)}, bf16[1,128,1024]{2,1,0:T(8,128)(2,1)}, u32[]{:S(2)}) %copy-start) | copy-done | bytes 262168
  25.5 0.9 %copy-done.2 = bf16[1,128,1024]{2,1,0:T(8,128)(2,1)S(1)} copy-done((bf16[1,128,1024]{2,1,0:T(8,128)(2,1)S(1)}, bf16[1,128,1024]{2,1,0:T(8,128)(2,1)}, u32[]{:S(2)}) %copy-start.2) | copy-done | bytes 262168
  26.5 0.9 %copy-done.4 = bf16[1,128,1024]{2,1,0:T(8,128)(2,1)S(1)} copy-done((bf16[1,128,1024]{2,1,0:T(8,128)(2,1)S(1)}, bf16[1,128,1024]{2,1,0:T(8,128)(2,1)}, u32[]{:S(2)}) %copy-start.4) | copy-done | bytes 262168
  27.4 0.6 %shard_map.128.refs_5_ = f32[128,1024]{1,0:T(8,128)S(1)} custom-call(f32[64,128]{1,0:T(8,128)S(1)} %get-tuple-element.26.refs_0_, f32[128,128]{1,0:T(8,128)S(1)} %get-tuple-element.30.refs_1_, bf16[128,1024]{1,0:T(8,128)(2,1)S(1)} %bitcast.23, bf16[128,1024]{1,0:T(8,128)(2,1)S(1)} %bitcast.13, bf16[128,1024]{1,0:T(8,128)(2,1)S(1)} %bitcast.18), custom_call_target="tpu_custom_call" | custom-call | flops 1000000 | bytes 100000 | tf_op jit(solution)/shard_map/pallas_call | solution.py:255
  28.0 0.6 shard_map.129.refs_5_
  28.6 0.0 collective-permute-done.1.refs_3_.refs_8_
  28.6 0.0 collective-permute-done.3.refs_4_.refs_11_
  28.6 0.0 copy-start.6
  28.6 0.0 copy-start.7
  28.6 0.6 shard_map.130.refs_0_
  29.2 0.0 copy-start.8
  29.2 1.6 %collective-permute-done.5.refs_4_.refs_2_ = bf16[128,1024]{1,0:T(8,128)(2,1)S(1)} collective-permute-done((bf16[128,1024]{1,0:T(8,128)(2,1)S(1)}, bf16[128,1024]{1,0:T(8,128)(2,1)S(1)}, u32[]{:S(2)}, u32[]{:S(2)}) %collective-permute-start.5) | collective-permute-done | bytes 262176 | tf_op jit(solution)/shard_map/ppermute | solution.py:19
  30.8 0.0 copy-start.1
  30.8 0.0 copy-start.3
  30.8 0.0 copy-start.5
  30.8 1.1 %shard_map.131 = (bf16[128,1024]{1,0:T(8,128)(2,1)S(1)}, bf16[128,1024]{1,0:T(8,128)(2,1)}, f32[1,1024]{1,0:T(1,128)S(1)}) custom-call(f32[128,1024]{1,0:T(8,128)S(1)} %shard_map.130.refs_0_, bf16[128,1024]{1,0:T(8,128)(2,1)S(1)} %bitcast.27, bf16[128,1024]{1,0:T(8,128)(2,1)S(1)} %bitcast.28, f32[1,1024]{1,0:T(1,128)S(1)} %bitcast.29, ...), custom_call_target="tpu_custom_call" | custom-call | flops 1000000 | bytes 100000 | tf_op jit(solution)/shard_map/pallas_call | solution.py:255
  31.9 1.3 %collective-permute-start.6 = (bf16[128,1024]{1,0:T(8,128)(2,1)S(1)}, bf16[128,1024]{1,0:T(8,128)(2,1)S(1)}, u32[]{:S(2)}, u32[]{:S(2)}) collective-permute-start(bf16[128,1024]{1,0:T(8,128)(2,1)S(1)} %get-tuple-element.31.refs_5_), channel_id=1, source_target_pairs={{4,0},{8,4},{12,8},{5,1},{9,5},{13,9},{6,2},{10,6},{14,10},{7,3},{... | collective-permute-start | bytes 786440 | tf_op jit(solution)/shard_map/ppermute | solution.py:19
  33.2 3.0 %shard_map.132 = (bf16[128,1024]{1,0:T(8,128)(2,1)}, f32[128,1024]{1,0:T(8,128)S(1)}, f32[128,1024]{1,0:T(8,128)S(1)}, f32[16,128]{1,0:T(8,128)S(1)}) custom-call(f32[64,128]{1,0:T(8,128)S(1)} %get-tuple-element.26.refs_0_, f32[128,128]{1,0:T(8,128)S(1)} %get-tuple-element.27.refs_1_, f32[128,128]{1,0:T(8,128)S(1)} %get-tuple-element.28.refs_1_.refs_2_, ...), custom_call_target="tpu_custom_call" | custom-call | flops 1000000 | bytes 100000 | tf_op jit(solution)/shard_map/pallas_call | solution.py:255
  36.3 0.0 collective-permute-start.7
  36.3 1.2 %collective-permute-done.7 = f32[16,128]{1,0:T(8,128)S(1)} collective-permute-done((f32[16,128]{1,0:T(8,128)S(1)}, f32[16,128]{1,0:T(8,128)S(1)}, u32[]{:S(2)}, u32[]{:S(2)}) %collective-permute-start.7) | collective-permute-done | bytes 8224 | tf_op jit(solution)/shard_map/ppermute | solution.py:322
  37.4 2.9 %collective-permute-done.6.refs_3_ = bf16[128,1024]{1,0:T(8,128)(2,1)S(1)} collective-permute-done((bf16[128,1024]{1,0:T(8,128)(2,1)S(1)}, bf16[128,1024]{1,0:T(8,128)(2,1)S(1)}, u32[]{:S(2)}, u32[]{:S(2)}) %collective-permute-start.6) | collective-permute-done | bytes 262176 | tf_op jit(solution)/shard_map/ppermute | solution.py:19
  40.4 1.3 %collective-permute-start.8 = (bf16[128,1024]{1,0:T(8,128)(2,1)S(1)}, bf16[128,1024]{1,0:T(8,128)(2,1)S(1)}, u32[]{:S(2)}, u32[]{:S(2)}) collective-permute-start(bf16[128,1024]{1,0:T(8,128)(2,1)S(1)} %collective-permute-done.6.refs_3_), channel_id=1, source_target_pairs={{4,0},{8,4},{12,8},{5,1},{9,5},{13,9},{6,2},{10,6},{14,10},{7,3},{... | collective-permute-start | bytes 786440 | tf_op jit(solution)/shard_map/ppermute | solution.py:19
  41.7 1.6 %collective-permute-start.9 = (f32[16,128]{1,0:T(8,128)S(1)}, f32[16,128]{1,0:T(8,128)S(1)}, u32[]{:S(2)}, u32[]{:S(2)}) collective-permute-start(f32[16,128]{1,0:T(8,128)S(1)} %add.12), channel_id=1, source_target_pairs={{0,2},{1,3},{2,0},{3,1},{4,6},{5,7},{6,4},{7,5},{8,10},{9,11},{10,... | collective-permute-start | bytes 24584 | tf_op jit(solution)/shard_map/ppermute | solution.py:322
  43.2 2.2 %collective-permute-done.9 = f32[16,128]{1,0:T(8,128)S(1)} collective-permute-done((f32[16,128]{1,0:T(8,128)S(1)}, f32[16,128]{1,0:T(8,128)S(1)}, u32[]{:S(2)}, u32[]{:S(2)}) %collective-permute-start.9) | collective-permute-done | bytes 8224 | tf_op jit(solution)/shard_map/ppermute | solution.py:322
  45.4 2.6 %collective-permute-start.10 = (f32[16,128]{1,0:T(8,128)S(1)}, f32[16,128]{1,0:T(8,128)S(1)}, u32[]{:S(2)}, u32[]{:S(2)}) collective-permute-start(f32[16,128]{1,0:T(8,128)S(1)} %add.13), channel_id=1, source_target_pairs={{0,4},{4,0},{8,12},{12,8},{1,5},{5,1},{9,13},{13,9},{2,6},{6,2},{1... | collective-permute-start | bytes 24584 | tf_op jit(solution)/shard_map/ppermute | solution.py:322
  48.0 1.6 %collective-permute-done.10 = f32[16,128]{1,0:T(8,128)S(1)} collective-permute-done((f32[16,128]{1,0:T(8,128)S(1)}, f32[16,128]{1,0:T(8,128)S(1)}, u32[]{:S(2)}, u32[]{:S(2)}) %collective-permute-start.10) | collective-permute-done | bytes 8224 | tf_op jit(solution)/shard_map/ppermute | solution.py:322
  49.7 3.2 %collective-permute-start.11 = (f32[16,128]{1,0:T(8,128)S(1)}, f32[16,128]{1,0:T(8,128)S(1)}, u32[]{:S(2)}, u32[]{:S(2)}) collective-permute-start(f32[16,128]{1,0:T(8,128)S(1)} %add.14), channel_id=1, source_target_pairs={{0,8},{4,12},{8,0},{12,4},{1,9},{5,13},{9,1},{13,5},{2,10},{6,14},... | collective-permute-start | bytes 24584 | tf_op jit(solution)/shard_map/ppermute | solution.py:322
  52.9 0.8 %shard_map.133 = (f32[128,1024]{1,0:T(8,128)S(1)}, f32[128,1024]{1,0:T(8,128)S(1)}) custom-call(f32[64,128]{1,0:T(8,128)S(1)} %get-tuple-element.26.refs_0_, f32[128,128]{1,0:T(8,128)S(1)} %get-tuple-element.37.refs_1_, bf16[128,1024]{1,0:T(8,128)(2,1)S(1)} %collective-permute-done.4.refs_6_.refs_2_, bf16[128,1024]{1,0:T(8,128)(2,1)S(1)} %collective-permute-done.6.refs_3_, ...), custom_call_target="tpu_custom_call" | custom-call | flops 1000000 | bytes 100000 | tf_op jit(solution)/shard_map/pallas_call | solution.py:255
  53.7 0.8 %collective-permute-done.11 = f32[16,128]{1,0:T(8,128)S(1)} collective-permute-done((f32[16,128]{1,0:T(8,128)S(1)}, f32[16,128]{1,0:T(8,128)S(1)}, u32[]{:S(2)}, u32[]{:S(2)}) %collective-permute-start.11) | collective-permute-done | bytes 8224 | tf_op jit(solution)/shard_map/ppermute | solution.py:322
  54.5 0.6 %slice.8 = f32[8,8]{1,0:T(8,128)} slice(f32[16,128]{1,0:T(8,128)S(1)} %add.15), slice={[8:16], [0:8]} | slice | bytes 512 | tf_op jit(solution)/shard_map/slice | solution.py:346
  55.1 0.6 %slice_bitcast_fusion = f32[1024]{0:T(1024)} fusion(f32[16,128]{1,0:T(8,128)S(1)} %add.15), kind=kLoop, calls=%fused_computation | loop fusion | bytes 8192 | tf_op jit(solution)/shard_map/reshape | solution.py:347
  55.7 0.0 collective-permute-done.8.refs_3_
  55.7 1.6 %shard_map.134 = (bf16[128,1024]{1,0:T(8,128)(2,1)}, bf16[128,1024]{1,0:T(8,128)(2,1)}) custom-call(f32[64,128]{1,0:T(8,128)S(1)} %get-tuple-element.26.refs_0_, f32[128,128]{1,0:T(8,128)S(1)} %get-tuple-element.34.refs_1_, bf16[128,1024]{1,0:T(8,128)(2,1)S(1)} %collective-permute-done.5.refs_4_.refs_2_, ...), custom_call_target="tpu_custom_call" | custom-call | flops 1000000 | bytes 100000 | tf_op jit(solution)/shard_map/pallas_call | solution.py:255
  (12 shorter events, 0.0 us)
Async XLA Ops:
  0.6 23.2 %copy-start.9 = (f32[8,8]{1,0:T(8,128)S(1)}, f32[8,8]{1,0:T(8,128)}, u32[]{:S(2)}) copy-start(f32[8,8]{1,0:T(8,128)} %refs_1_.1) | copy-start | bytes 772
  0.6 11.9 %collective-permute-start = (bf16[128,1024]{1,0:T(8,128)(2,1)}, bf16[128,1024]{1,0:T(8,128)(2,1)S(1)}, u32[]{:S(2)}, u32[]{:S(2)}) collective-permute-start(bf16[128,1024]{1,0:T(8,128)(2,1)} %bitcast.12), channel_id=1, source_target_pairs={{0,4},{4,8},{8,12},{1,5},{5,9},{9,13},{2,6},{6,10},{10,14},{3,7},{... | collective-permute-start | bytes 786440 | tf_op jit(solution)/shard_map/ppermute | solution.py:19
  5.6 18.2 %copy-start.10 = (s32[1,4]{1,0:T(1,128)S(1)}, s32[1,4]{1,0:T(1,128)}, u32[]{:S(2)}) copy-start(s32[1,4]{1,0:T(1,128)} %refs_0_.1) | copy-start | bytes 52
  5.6 12.6 %collective-permute-start.2 = (bf16[128,1024]{1,0:T(8,128)(2,1)}, bf16[128,1024]{1,0:T(8,128)(2,1)S(1)}, u32[]{:S(2)}, u32[]{:S(2)}) collective-permute-start(bf16[128,1024]{1,0:T(8,128)(2,1)} %bitcast.17), channel_id=1, source_target_pairs={{0,4},{4,8},{8,12},{1,5},{5,9},{9,13},{2,6},{6,10},{10,14},{3,7},{... | collective-permute-start | bytes 786440 | tf_op jit(solution)/shard_map/ppermute | solution.py:19
  9.1 13.4 %collective-permute-start.4 = (bf16[128,1024]{1,0:T(8,128)(2,1)}, bf16[128,1024]{1,0:T(8,128)(2,1)S(1)}, u32[]{:S(2)}, u32[]{:S(2)}) collective-permute-start(bf16[128,1024]{1,0:T(8,128)(2,1)} %bitcast.22), channel_id=1, source_target_pairs={{4,0},{8,4},{12,8},{5,1},{9,5},{13,9},{6,2},{10,6},{14,10},{7,3},{... | collective-permute-start | bytes 786440 | tf_op jit(solution)/shard_map/ppermute | solution.py:19
  12.6 16.0 %collective-permute-start.1 = (bf16[128,1024]{1,0:T(8,128)(2,1)S(1)}, bf16[128,1024]{1,0:T(8,128)(2,1)S(1)}, u32[]{:S(2)}, u32[]{:S(2)}) collective-permute-start(bf16[128,1024]{1,0:T(8,128)(2,1)S(1)} %collective-permute-done.refs_3_.refs_7_), channel_id=1, source_target_pairs={{0,4},{4,8},{8,12},{1,5},{5,9},{9,13},{2,6},{6,10},{10,14},{3,7},{... | collective-permute-start | bytes 786440 | tf_op jit(solution)/shard_map/ppermute | solution.py:19
  18.2 10.4 %collective-permute-start.3 = (bf16[128,1024]{1,0:T(8,128)(2,1)S(1)}, bf16[128,1024]{1,0:T(8,128)(2,1)S(1)}, u32[]{:S(2)}, u32[]{:S(2)}) collective-permute-start(bf16[128,1024]{1,0:T(8,128)(2,1)S(1)} %collective-permute-done.2.refs_4_.refs_10_), channel_id=1, source_target_pairs={{0,4},{4,8},{8,12},{1,5},{5,9},{9,13},{2,6},{6,10},{10,14},{3,7},{... | collective-permute-start | bytes 786440 | tf_op jit(solution)/shard_map/ppermute | solution.py:19
  22.5 8.3 %collective-permute-start.5 = (bf16[128,1024]{1,0:T(8,128)(2,1)S(1)}, bf16[128,1024]{1,0:T(8,128)(2,1)S(1)}, u32[]{:S(2)}, u32[]{:S(2)}) collective-permute-start(bf16[128,1024]{1,0:T(8,128)(2,1)S(1)} %collective-permute-done.4.refs_6_.refs_2_), channel_id=1, source_target_pairs={{4,0},{8,4},{12,8},{5,1},{9,5},{13,9},{6,2},{10,6},{14,10},{7,3},{... | collective-permute-start | bytes 786440 | tf_op jit(solution)/shard_map/ppermute | solution.py:19
  24.6 1.0 %copy-start = (bf16[1,128,1024]{2,1,0:T(8,128)(2,1)S(1)}, bf16[1,128,1024]{2,1,0:T(8,128)(2,1)}, u32[]{:S(2)}) copy-start(bf16[1,128,1024]{2,1,0:T(8,128)(2,1)} %param.9) | copy-start | bytes 786436
  25.5 0.9 %copy-start.2 = (bf16[1,128,1024]{2,1,0:T(8,128)(2,1)S(1)}, bf16[1,128,1024]{2,1,0:T(8,128)(2,1)}, u32[]{:S(2)}) copy-start(bf16[1,128,1024]{2,1,0:T(8,128)(2,1)} %param.10) | copy-start | bytes 786436
  26.5 0.9 %copy-start.4 = (bf16[1,128,1024]{2,1,0:T(8,128)(2,1)S(1)}, bf16[1,128,1024]{2,1,0:T(8,128)(2,1)}, u32[]{:S(2)}) copy-start(bf16[1,128,1024]{2,1,0:T(8,128)(2,1)} %param.8) | copy-start | bytes 786436
  28.6 2.2 %copy-start.6 = (bf16[1,128,1024]{2,1,0:T(8,128)(2,1)S(1)}, bf16[1,128,1024]{2,1,0:T(8,128)(2,1)}, u32[]{:S(2)}) copy-start(bf16[1,128,1024]{2,1,0:T(8,128)(2,1)} %param.12) | copy-start | bytes 786436
  28.6 2.2 %copy-start.7 = (bf16[1,128,1024]{2,1,0:T(8,128)(2,1)S(1)}, bf16[1,128,1024]{2,1,0:T(8,128)(2,1)}, u32[]{:S(2)}) copy-start(bf16[1,128,1024]{2,1,0:T(8,128)(2,1)} %param.11) | copy-start | bytes 786436
  29.2 1.6 %copy-start.8 = (f32[1024]{0:T(1024)S(1)}, f32[1024]{0:T(1024)}, u32[]{:S(2)}) copy-start(f32[1024]{0:T(1024)} %param.15) | copy-start | bytes 12292
  30.8 2.4 %copy-start.1 = (bf16[1,128,1024]{2,1,0:T(8,128)(2,1)S(1)}, bf16[1,128,1024]{2,1,0:T(8,128)(2,1)}, u32[]{:S(2)}) copy-start(bf16[1,128,1024]{2,1,0:T(8,128)(2,1)} %param.9) | copy-start | bytes 786436
  30.8 2.4 %copy-start.3 = (bf16[1,128,1024]{2,1,0:T(8,128)(2,1)S(1)}, bf16[1,128,1024]{2,1,0:T(8,128)(2,1)}, u32[]{:S(2)}) copy-start(bf16[1,128,1024]{2,1,0:T(8,128)(2,1)} %param.10) | copy-start | bytes 786436
  30.8 2.4 %copy-start.5 = (bf16[1,128,1024]{2,1,0:T(8,128)(2,1)S(1)}, bf16[1,128,1024]{2,1,0:T(8,128)(2,1)}, u32[]{:S(2)}) copy-start(bf16[1,128,1024]{2,1,0:T(8,128)(2,1)} %param.8) | copy-start | bytes 786436
  31.9 8.5 %collective-permute-start.6 = (bf16[128,1024]{1,0:T(8,128)(2,1)S(1)}, bf16[128,1024]{1,0:T(8,128)(2,1)S(1)}, u32[]{:S(2)}, u32[]{:S(2)}) collective-permute-start(bf16[128,1024]{1,0:T(8,128)(2,1)S(1)} %get-tuple-element.31.refs_5_), channel_id=1, source_target_pairs={{4,0},{8,4},{12,8},{5,1},{9,5},{13,9},{6,2},{10,6},{14,10},{7,3},{... | collective-permute-start | bytes 786440 | tf_op jit(solution)/shard_map/ppermute | solution.py:19
  36.3 1.2 %collective-permute-start.7 = (f32[16,128]{1,0:T(8,128)S(1)}, f32[16,128]{1,0:T(8,128)S(1)}, u32[]{:S(2)}, u32[]{:S(2)}) collective-permute-start(f32[16,128]{1,0:T(8,128)S(1)} %get-tuple-element.35), channel_id=1, source_target_pairs={{0,1},{1,0},{2,3},{3,2},{4,5},{5,4},{6,7},{7,6},{8,9},{9,8},{10,11... | collective-permute-start | bytes 24584 | tf_op jit(solution)/shard_map/ppermute | solution.py:322
  40.4 15.3 %collective-permute-start.8 = (bf16[128,1024]{1,0:T(8,128)(2,1)S(1)}, bf16[128,1024]{1,0:T(8,128)(2,1)S(1)}, u32[]{:S(2)}, u32[]{:S(2)}) collective-permute-start(bf16[128,1024]{1,0:T(8,128)(2,1)S(1)} %collective-permute-done.6.refs_3_), channel_id=1, source_target_pairs={{4,0},{8,4},{12,8},{5,1},{9,5},{13,9},{6,2},{10,6},{14,10},{7,3},{... | collective-permute-start | bytes 786440 | tf_op jit(solution)/shard_map/ppermute | solution.py:19
  41.7 3.7 %collective-permute-start.9 = (f32[16,128]{1,0:T(8,128)S(1)}, f32[16,128]{1,0:T(8,128)S(1)}, u32[]{:S(2)}, u32[]{:S(2)}) collective-permute-start(f32[16,128]{1,0:T(8,128)S(1)} %add.12), channel_id=1, source_target_pairs={{0,2},{1,3},{2,0},{3,1},{4,6},{5,7},{6,4},{7,5},{8,10},{9,11},{10,... | collective-permute-start | bytes 24584 | tf_op jit(solution)/shard_map/ppermute | solution.py:322
  45.4 4.3 %collective-permute-start.10 = (f32[16,128]{1,0:T(8,128)S(1)}, f32[16,128]{1,0:T(8,128)S(1)}, u32[]{:S(2)}, u32[]{:S(2)}) collective-permute-start(f32[16,128]{1,0:T(8,128)S(1)} %add.13), channel_id=1, source_target_pairs={{0,4},{4,0},{8,12},{12,8},{1,5},{5,1},{9,13},{13,9},{2,6},{6,2},{1... | collective-permute-start | bytes 24584 | tf_op jit(solution)/shard_map/ppermute | solution.py:322
  49.7 4.8 %collective-permute-start.11 = (f32[16,128]{1,0:T(8,128)S(1)}, f32[16,128]{1,0:T(8,128)S(1)}, u32[]{:S(2)}, u32[]{:S(2)}) collective-permute-start(f32[16,128]{1,0:T(8,128)S(1)} %add.14), channel_id=1, source_target_pairs={{0,8},{4,12},{8,0},{12,4},{1,9},{5,13},{9,1},{13,5},{2,10},{6,14},... | collective-permute-start | bytes 24584 | tf_op jit(solution)/shard_map/ppermute | solution.py:322

commit v4 on v3

v4 whole, which is shorter than its diff:
```python
from functools import partial

import jax
import jax.numpy as jnp
from jax import lax
from jax.experimental import pallas as pl
from jax.experimental.pallas import tpu as pltpu
from jax.sharding import PartitionSpec as P

EPSILON = 1e-05
VMEM_LIMIT = 24 * 1024 * 1024
F32 = jnp.float32
BF16 = jnp.bfloat16


def passed_along(array, axis, by):
    size = lax.axis_size(axis)
    pairs = [(i, i + by) for i in range(size) if 0 <= i + by < size]
    return lax.ppermute(array, axis, pairs)


def contract(left, right, left_dim, right_dim):
    return lax.dot_general(
        left, right, (((left_dim,), (right_dim,)), ((), ())), preferred_element_type=F32
    )


def user_starts(lengths, query_pos):
    end = jnp.int32(0)
    start = jnp.zeros(query_pos.shape, jnp.int32)
    for user in range(lengths.shape[1]):
        end = end + lengths[0, user]
        start = jnp.where(query_pos >= end, end, start)
    return start


class Pair:
    def __init__(self, mask, table, heads, hops, flipped=False):
        rows = mask.shape[0]
        self.table, self.heads, self.levels = table, heads, table.shape[0] // heads
        self.mask = mask[...]
        self.far = (hops - 1) * rows + 1 >= 2 ** (self.levels - 2)
        if not self.far:
            query_dim, key_dim = (1, 0) if flipped else (0, 1)
            query_row = lax.broadcasted_iota(jnp.int32, mask.shape, query_dim)
            key_row = lax.broadcasted_iota(jnp.int32, mask.shape, key_dim)
            self.distance = query_row - key_row + hops * rows

    def half_logits(self, scores, head, scaling):
        def level_row(level):
            at = level * self.heads + head
            return self.table[at : at + 1, :]

        value = level_row(self.levels - 1)
        if not self.far:
            for level in range(self.levels - 2, -1, -1):
                value = jnp.where(self.distance < 2**level, level_row(level), value)
        return scores * (0.5 * scaling) + value

    def bias_rows(self, grads):
        sub = lax.broadcasted_iota(jnp.int32, (self.levels, grads.shape[1]), 0)
        if self.far:
            row = jnp.sum(grads, axis=0, keepdims=True)
            return jnp.where(sub == self.levels - 1, row, 0.0)
        total = jnp.zeros(sub.shape, F32)
        for level in range(self.levels):
            inside = None
            if level > 0:
                inside = self.distance >= 2 ** (level - 1)
            if level < self.levels - 1:
                below = self.distance < 2**level
                inside = below if inside is None else inside & below
            row = jnp.sum(jnp.where(inside, grads, 0.0), axis=0, keepdims=True)
            total = jnp.where(sub == level, row, total)
        return total


def slope_of(half, tanh):
    return (0.5 + 0.5 * tanh) * (1.0 + half * (1.0 - tanh))


def columns(head, width):
    return slice(head * width, (head + 1) * width)


def in_stages(count, first, second, ahead=3):
    held = [first(i) for i in range(min(ahead, count))]
    for i in range(count):
        if i + ahead < count:
            held.append(first(i + ahead))
        second(i, held.pop(0))


def attend(pairs, heads, scaling, query, keys, values, total, out):
    width = query.shape[1] // heads

    def scores(head):
        cols = columns(head, width)
        return [contract(query[:, cols], key[:, cols], 1, 1) for key in keys]

    def weigh(head, found):
        cols = columns(head, width)
        part = None if total is None else total[:, cols]
        for pair, score, value in zip(pairs, found, values):
            half = pair.half_logits(score, head, scaling)
            weights = ((half + half * jnp.tanh(half)) * pair.mask).astype(BF16)
            added = contract(weights, value[:, cols], 1, 0)
            part = added if part is None else part + added
        out[:, cols] = part.astype(out.dtype)

    in_stages(heads, scores, weigh)


def first_kernel(plan, heads, scaling, lengths, bias, *refs):
    inputs, refs = refs[:5], refs[5:]
    table, masks, refs = refs[0], refs[1 : 1 + len(plan)], refs[1 + len(plan) :]
    held, out, arrived = refs[:5], refs[5], refs[6]
    copies = [
        pltpu.make_async_copy(source, target, arrived.at[at])
        for at, (source, target) in enumerate(zip(inputs, held))
    ]
    for copy in copies:
        copy.start()
    levels = bias.shape[0]
    for level in range(levels):
        for head in range(heads):
            at = level * heads + head
            table[at : at + 1, :] = jnp.full((1, table.shape[1]), 0.5 * bias[level, head], F32)
    for (block, hops, flipped), mask in zip(plan, masks):
        rows = mask.shape[0]
        query_dim, key_dim = (1, 0) if flipped else (0, 1)
        line = (1, rows) if flipped else (rows, 1)
        first = (lax.axis_index("ctx") + block) * rows
        query_pos = first + lax.broadcasted_iota(jnp.int32, line, query_dim)
        key_pos = first - hops * rows + lax.broadcasted_iota(jnp.int32, mask.shape, key_dim)
        seen = (key_pos >= user_starts(lengths, query_pos)) & (key_pos <= query_pos)
        mask[...] = jnp.where(seen, 1.0, 0.0).astype(F32)
    for copy in copies:
        copy.wait()
    query, key, value = held[:3]
    pair = Pair(masks[0], table, heads, 0)
    attend([pair], heads, scaling, query, [key], [value], None, out)


def forward_kernel(hops, heads, scaling, table, mask, query, key, value, total, out):
    pair = Pair(mask, table, heads, hops)
    attend([pair], heads, scaling, query, [key], [value], total, out)


def normed_rows(attention):
    center = attention - jnp.mean(attention, axis=1, keepdims=True)
    inverse = lax.rsqrt(jnp.mean(center * center, axis=1, keepdims=True) + EPSILON)
    return center * inverse, inverse


def norm_kernel(hops, heads, scaling, *refs):
    table, mask, query, key, value, total, out_grad, update_gate, gain = refs[:9]
    attention, attn_grad, gain_grad = refs[9:]
    forward_kernel(hops, heads, scaling, table, mask, query, key, value, total, attention)
    rows, features = attention.shape
    step = 16
    gain_row = gain[...]
    gain_sum = jnp.zeros((8, features), F32)
    for low in range(0, rows, step):
        span = slice(low, low + step)
        normed, inverse = normed_rows(attention[span, :])
        gated = out_grad[span, :].astype(F32) * update_gate[span, :].astype(F32)
        product = gated * normed
        for part in range(0, step, 8):
            gain_sum = gain_sum + product[part : part + 8, :]
        pushed = gated * gain_row
        attn_grad[span, :] = (
            inverse
            * (
                pushed
                - jnp.mean(pushed, axis=1, keepdims=True)
                - normed * jnp.mean(pushed * normed, axis=1, keepdims=True)
            )
        ).astype(BF16)
    gain_grad[...] = jnp.sum(gain_sum, axis=0, keepdims=True)


def gate_kernel(attention, out_grad, gain, gate_grad):
    step = 16
    gain_row = gain[...]
    for low in range(0, attention.shape[0], step):
        span = slice(low, low + step)
        normed, _ = normed_rows(attention[span, :])
        gate_grad[span, :] = (out_grad[span, :].astype(F32) * normed * gain_row).astype(BF16)


def backward_query_kernel(hop_list, heads, scaling, *refs):
    count = len(hop_list)
    table, masks = refs[0], refs[1 : 1 + count]
    query, grad = refs[1 + count : 3 + count]
    keys, values = refs[3 + count : 3 + 2 * count], refs[3 + 2 * count : 3 + 3 * count]
    gain_in, query_out, small_out = refs[3 + 3 * count :]
    width = query.shape[1] // heads
    pairs = [Pair(mask, table, heads, hops) for mask, hops in zip(masks, hop_list)]
    lanes = small_out.shape[1]
    lines = gain_in.shape[1] // lanes
    levels = small_out.shape[0] - lines
    lane = lax.broadcasted_iota(jnp.int32, (levels, lanes), 1)
    bias_total = [jnp.zeros((levels, lanes), F32)]

    def scores(head):
        cols = columns(head, width)
        query_h, grad_h = query[:, cols], grad[:, cols]
        return [
            (contract(query_h, key[:, cols], 1, 1), contract(grad_h, value[:, cols], 1, 1))
            for key, value in zip(keys, values)
        ]

    def differentiate(head, found):
        cols = columns(head, width)
        query_part, bias_part = None, None
        for pair, key, (score, weight_grad) in zip(pairs, keys, found):
            half = pair.half_logits(score, head, scaling)
            logit_grad = weight_grad * (slope_of(half, jnp.tanh(half)) * pair.mask)
            added = contract(logit_grad.astype(BF16), key[:, cols], 1, 0)
            query_part = added if query_part is None else query_part + added
            sums = pair.bias_rows(logit_grad)
            bias_part = sums if bias_part is None else bias_part + sums
        query_out[:, cols] = (query_part * scaling).astype(BF16)
        sums = jnp.sum(bias_part, axis=1, keepdims=True)
        bias_total[0] = jnp.where(lane == head, sums, bias_total[0])

    in_stages(heads, scores, differentiate, 1)
    for line in range(lines):
        small_out[line : line + 1, :] = gain_in[:, line * lanes : (line + 1) * lanes]
    small_out[lines:, :] = bias_total[0]


def add_key_grads(hops, heads, scaling, table, mask, query, grad, key, value, sums, store):
    width = query.shape[1] // heads
    pair = Pair(mask, table, heads, hops, True)

    def scores(head):
        cols = columns(head, width)
        score = contract(key[:, cols], query[:, cols], 1, 1)
        return score, contract(value[:, cols], grad[:, cols], 1, 1)

    def differentiate(head, found):
        cols = columns(head, width)
        half = pair.half_logits(found[0], head, scaling)
        tanh = jnp.tanh(half)
        rounded = (found[1] * (slope_of(half, tanh) * pair.mask)).astype(BF16)
        weights = ((half + half * tanh) * pair.mask).astype(BF16)
        parts = [contract(rounded, query[:, cols], 1, 0), contract(weights, grad[:, cols], 1, 0)]
        store(head, cols, *[part + held[:, cols] for part, held in zip(parts, sums)] or parts)

    in_stages(heads, scores, differentiate)


def backward_key_kernel(hops, heads, scaling, *refs):
    key_out, value_out = refs[-2:]

    def store(head, cols, key_part, value_part):
        key_out[:, cols] = key_part
        value_out[:, cols] = value_part

    add_key_grads(hops, heads, scaling, *refs[:6], refs[6:-2], store)


def last_kernel(hops, heads, scaling, *refs):
    pieces = refs[8:-7]
    key_out, value_out, gain_out, bias_out, key_held, value_held, written = refs[-7:]
    copies = []
    group = 2

    def store(head, cols, key_part, value_part):
        key_held[:, cols] = (key_part * scaling).astype(BF16)
        value_held[:, cols] = value_part.astype(BF16)
        if (head + 1) % group == 0:
            done = slice(cols.stop - group * (cols.stop - cols.start), cols.stop)
            for held, out in ((key_held, key_out), (value_held, value_out)):
                at = written.at[len(copies)]
                copies.append(pltpu.make_async_copy(held.at[:, done], out.at[:, done], at))
                copies[-1].start()

    total = added_up([piece[...] for piece in pieces])
    lines = gain_out.shape[0]
    gain_out[...] = total[:lines]
    bias_out[...] = total[lines:, :heads]
    add_key_grads(hops, heads, scaling, *refs[:6], refs[6:8], store)
    for copy in copies:
        copy.wait()


def on_device(kernel, outs, args, smem=(), ahead=(), far=(), far_outs=0, scratch=()):
    count = len(smem) + len(far) + len(args)
    far = [pltpu.with_memory_space_constraint(array, pltpu.HBM) for array in far]

    def body(*refs):
        kernel(*refs[:count], *refs[count + len(ahead) :])

    vmem, anywhere = pl.BlockSpec(memory_space=pltpu.VMEM), pl.BlockSpec(memory_space=pl.ANY)
    return pl.pallas_call(
        body,
        out_shape=outs,
        in_specs=[pl.BlockSpec(memory_space=pltpu.SMEM)] * len(smem)
        + [pl.BlockSpec(memory_space=pltpu.HBM)] * len(far)
        + [vmem] * len(args)
        + [anywhere] * len(ahead),
        out_specs=[anywhere] * far_outs + [vmem] * (len(outs) - far_outs),
        scratch_shapes=scratch,
        compiler_params=pltpu.CompilerParams(vmem_limit_bytes=VMEM_LIMIT),
        cost_estimate=pl.CostEstimate(flops=1000000, bytes_accessed=100000, transcendentals=0),
    )(*smem, *far, *args, *ahead)


def rounds_of(axes):
    rounds = []
    for axis in axes:
        size = lax.axis_size(axis)
        step = 1
        while step < size:
            radix = 4 if size // step >= 4 else 2
            rounds.append((axis, [step * at for at in range(1, radix)]))
            step = radix * step
    return rounds


def exchanged(array, axis, distances):
    size = lax.axis_size(axis)
    return [array] + [
        lax.ppermute(array, axis, [(i, i ^ distance) for i in range(size)])
        for distance in distances
    ]


def added_up(pieces):
    while len(pieces) > 1:
        pieces = [left + right for left, right in zip(pieces[::2], pieces[1::2])]
    return pieces[0]


def local(queries, key_rows, value_rows, update_gate, out_grad, user_lengths, rel_bias, norm_gain):
    rows, features = queries.shape[1:]
    levels, heads = rel_bias.shape
    scaling = (features // heads) ** (-0.5)
    reach = min(3, lax.axis_size("ctx") // 2)
    wide = jax.ShapeDtypeStruct((rows, features), F32)
    narrow = jax.ShapeDtypeStruct((rows, features), BF16)
    inputs = (queries[0], key_rows[0], value_rows[0], update_gate[0], out_grad[0])
    gain = norm_gain[None]

    hop_list = tuple(range(reach + 1))
    plan = [(0, hops, False) for hops in hop_list] + [(hops, hops, True) for hops in hop_list]
    outs = [jax.ShapeDtypeStruct((levels * heads, rows), F32)]
    outs += [jax.ShapeDtypeStruct((rows, rows), F32)] * len(plan)
    outs += [narrow] * len(inputs) + [wide]
    table, *found = on_device(
        partial(first_kernel, plan, heads, scaling),
        outs,
        (),
        (user_lengths, rel_bias),
        far=inputs,
        scratch=[pltpu.SemaphoreType.DMA((len(inputs),))],
    )
    masks, flipped = found[: reach + 1], found[reach + 1 : 2 * reach + 2]
    query, key, value, gate, grad, attention = found[2 * reach + 2 :]

    later_queries = [query, passed_along(inputs[0], "ctx", -1)]
    keys = [key, passed_along(inputs[1], "ctx", 1)]
    values = [value, passed_along(inputs[2], "ctx", 1)]
    for hops in range(1, reach):
        keys.append(passed_along(keys[-1], "ctx", 1))
        if hops == 1:
            values[1], attention = lax.optimization_barrier((values[1], attention))
        values.append(passed_along(values[-1], "ctx", 1))
        later_queries.append(passed_along(later_queries[-1], "ctx", -1))
    for hops in range(1, reach):
        (attention,) = on_device(
            partial(forward_kernel, hops, heads, scaling),
            [wide],
            (table, masks[hops], query, keys[hops], values[hops], attention),
            ahead=later_queries[hops : hops + 1],
        )
    attention, attn_grad, gain_part = on_device(
        partial(norm_kernel, reach, heads, scaling),
        [wide, narrow, jax.ShapeDtypeStruct((1, features), F32)],
        (table, masks[-1], query, keys[-1], values[-1], attention, grad, gate, gain),
        ahead=later_queries[reach:],
    )

    lanes = features // 8
    query_grad, sums = on_device(
        partial(backward_query_kernel, hop_list, heads, scaling),
        [narrow, jax.ShapeDtypeStruct((8 + levels, lanes), F32)],
        (table, *masks, query, attn_grad, *keys, *values, gain_part),
    )
    later_grads = [attn_grad, passed_along(attn_grad, "ctx", -1)]
    pieces = [sums]
    first_pieces = None
    for number, (axis, distances) in enumerate(rounds_of(("dp", "ctx")), 1):
        pieces = exchanged(added_up(pieces), axis, distances)
        if number < reach:
            arrived, *pieces = lax.optimization_barrier((later_grads[-1], *pieces))
            later_grads.append(passed_along(arrived, "ctx", -1))
        first_pieces = first_pieces or pieces[1:2]
    key_grads = ()
    for hops in range(reach):
        key_grads = on_device(
            partial(backward_key_kernel, hops, heads, scaling),
            [wide] * 2,
            (table, flipped[hops], later_queries[hops], later_grads[hops], key, value, *key_grads),
            ahead=first_pieces,
        )
    (gate_grad,) = on_device(gate_kernel, [narrow], (attention, grad, gain), ahead=key_grads[:1])
    key_grad, value_grad, gain_grad, bias_grad = on_device(
        partial(last_kernel, reach, heads, scaling),
        [
            narrow,
            narrow,
            jax.ShapeDtypeStruct((8, lanes), F32),
            jax.ShapeDtypeStruct((levels, heads), F32),
        ],
        (
            table,
            flipped[reach],
            later_queries[reach],
            later_grads[reach],
            key,
            value,
            *key_grads,
            *pieces,
        ),
        far_outs=2,
        scratch=[pltpu.VMEM((rows, features), BF16)] * 2 + [pltpu.SemaphoreType.DMA((heads,))],
    )
    return (
        query_grad[None],
        key_grad[None],
        value_grad[None],
        gate_grad[None],
        bias_grad,
        gain_grad.reshape(features),
    )


def solution(mesh):
    in_specs = (
        P(("groups", "dp"), "ctx", None),
        P(("groups", "dp"), "ctx", None),
        P(("groups", "dp"), "ctx", None),
        P(("groups", "dp"), "ctx", None),
        P(("groups", "dp"), "ctx", None),
        P(("groups", "dp"), None),
        P(),
        P(),
    )
    out_specs = (
        P(("groups", "dp"), "ctx", None),
        P(("groups", "dp"), "ctx", None),
        P(("groups", "dp"), "ctx", None),
        P(("groups", "dp"), "ctx", None),
        P("groups", None),
        P("groups"),
    )
    return jax.shard_map(local, mesh=mesh, in_specs=in_specs, out_specs=out_specs, check_vma=False)
```

time: 57.7 us -> 56.2 us (0.974)
  local copies, waits for them, and re-layouts: 4.08 us -> 0.65 us
  Pallas kernels: 8.98 us -> 11.6 us
  waiting for transfers between devices: 13.8 us -> 13 us
    pallas_call x8, Pallas kernels: 8.98 us -> 11.6 us  [on_device(): pl.pallas_call(body, out_shape=outs, in_specs=[pl.BlockSpec(memory_space=...]
    unnamed x22 -> x6, local copies, waits for them, and re-layouts: 2.89 us -> 0.65 us
    ppermute x8, waiting for transfers between devices: 8.03 us -> 6.68 us  [passed_along(): return lax.ppermute(array, axis, pairs)]
    ppermute x4 -> x6, starting transfers between devices: 7.39 us -> 8.2 us  [exchanged(): lax.ppermute(array, axis, [(i, i ^ distance) for i in range(size)])]
    slice x1 -> x0, local copies, waits for them, and re-layouts: 0.6 us -> none  [local(): sums[8:, :heads]]
    reshape x1 -> x0, local copies, waits for them, and re-layouts: 0.59 us -> none  [local(): sums[:8].reshape(features)]
    ppermute x4 -> x6, waiting for transfers between devices: 5.76 us -> 6.28 us  [exchanged(): lax.ppermute(array, axis, [(i, i ^ distance) for i in range(size)])]
  transfers between devices with their start and end apart: 12 -> 14, of which waited for: 8 -> 8; matrix products, arithmetic and copies ran while one was open for 2% -> 0% of each run, Pallas kernels for 11% -> 15%
where the time goes in v4:
time: 56.2 us; the launch traced here: 55.9 us
  starting transfers between devices  29.8 us (53%)
  waiting for transfers between devices  13 us (23%)
  Pallas kernels  11.6 us (21%)
  between operations  0.8 us (1%)
  local copies, waits for them, and re-layouts  0.65 us (1%)
    ppermute x8, starting transfers between devices, passed_along(): return lax.ppermute(array, axis, pairs)  21.6 us
    pallas_call x8, Pallas kernels, on_device(): pl.pallas_call(body, out_shape=outs, in_specs=[pl.BlockSpec(memory_space=...  11.6 us
    ppermute x6, starting transfers between devices, exchanged(): lax.ppermute(array, axis, [(i, i ^ distance) for i in range(size)])  8.2 us
    ppermute x8, waiting for transfers between devices, passed_along(): return lax.ppermute(array, axis, pairs)  6.68 us
    ppermute x6, waiting for transfers between devices, exchanged(): lax.ppermute(array, axis, [(i, i ^ distance) for i in range(size)])  6.28 us
  transfers between devices with their start and end apart: 14, of which 8 were waited for; matrix products, arithmetic and copies ran while one was open for 0% of the time, Pallas kernels for 15%

profile of v4, /device:TPU:0, one launch (start us, length us, event | category | flops | bytes accessed | tf_op | source)
XLA Modules:
  0.0 55.9 jit_solution(11267961194500985114)
XLA Ops:
  0.6 0.0 copy-start.1
  0.6 4.9 %collective-permute-start.2 = (bf16[128,1024]{1,0:T(8,128)(2,1)}, bf16[128,1024]{1,0:T(8,128)(2,1)S(1)}, u32[]{:S(2)}, u32[]{:S(2)}) collective-permute-start(bf16[128,1024]{1,0:T(8,128)(2,1)} %bitcast.15), channel_id=1, source_target_pairs={{0,4},{4,8},{8,12},{1,5},{5,9},{9,13},{2,6},{6,10},{10,14},{3,7},{... | collective-permute-start | bytes 786440 | tf_op jit(solution)/shard_map/ppermute | solution.py:19
  5.6 3.5 %collective-permute-start = (bf16[128,1024]{1,0:T(8,128)(2,1)}, bf16[128,1024]{1,0:T(8,128)(2,1)S(1)}, u32[]{:S(2)}, u32[]{:S(2)}) collective-permute-start(bf16[128,1024]{1,0:T(8,128)(2,1)} %bitcast.17), channel_id=1, source_target_pairs={{0,4},{4,8},{8,12},{1,5},{5,9},{9,13},{2,6},{6,10},{10,14},{3,7},{... | collective-permute-start | bytes 786440 | tf_op jit(solution)/shard_map/ppermute | solution.py:19
  9.1 1.3 %collective-permute-start.4 = (bf16[128,1024]{1,0:T(8,128)(2,1)}, bf16[128,1024]{1,0:T(8,128)(2,1)S(1)}, u32[]{:S(2)}, u32[]{:S(2)}) collective-permute-start(bf16[128,1024]{1,0:T(8,128)(2,1)} %bitcast.19), channel_id=1, source_target_pairs={{4,0},{8,4},{12,8},{5,1},{9,5},{13,9},{6,2},{10,6},{14,10},{7,3},{... | collective-permute-start | bytes 786440 | tf_op jit(solution)/shard_map/ppermute | solution.py:19
  10.4 0.0 copy-start.2
  10.4 0.0 copy-done.1
  10.4 0.6 %copy-done.2 = s32[1,4]{1,0:T(1,128)S(1)} copy-done((s32[1,4]{1,0:T(1,128)S(1)}, s32[1,4]{1,0:T(1,128)}, u32[]{:S(2)}) %copy-start.2) | copy-done | bytes 40
  11.0 2.5 %shard_map.127 = (f32[64,128]{1,0:T(8,128)S(1)}, f32[128,128]{1,0:T(8,128)S(1)}, f32[128,128]{1,0:T(8,128)S(1)}, f32[128,128]{1,0:T(8,128)S(1)}, f32[128,128]{1,...) custom-call(s32[1,4]{1,0:T(1,128)S(1)} %copy-done.2, ...), custom_call_target="tpu_custom_call" | custom-call | flops 1000000 | bytes 100000 | tf_op jit(solution)/shard_map/pallas_call | solution.py:298
  13.6 0.0 collective-permute-done.2.refs_4_.refs_10_
  13.6 4.6 %collective-permute-start.3 = (bf16[128,1024]{1,0:T(8,128)(2,1)S(1)}, bf16[128,1024]{1,0:T(8,128)(2,1)S(1)}, u32[]{:S(2)}, u32[]{:S(2)}) collective-permute-start(bf16[128,1024]{1,0:T(8,128)(2,1)S(1)} %collective-permute-done.2.refs_4_.refs_10_), channel_id=1, source_target_pairs={{0,4},{4,8},{8,12},{1,5},{5,9},{9,13},{2,6},{6,10},{10,14},{3,7},{... | collective-permute-start | bytes 786440 | tf_op jit(solution)/shard_map/ppermute | solution.py:19
  18.1 0.0 collective-permute-done.refs_3_.refs_7_
  18.1 3.5 %collective-permute-start.1 = (bf16[128,1024]{1,0:T(8,128)(2,1)S(1)}, bf16[128,1024]{1,0:T(8,128)(2,1)S(1)}, u32[]{:S(2)}, u32[]{:S(2)}) collective-permute-start(bf16[128,1024]{1,0:T(8,128)(2,1)S(1)} %collective-permute-done.refs_3_.refs_7_), channel_id=1, source_target_pairs={{0,4},{4,8},{8,12},{1,5},{5,9},{9,13},{2,6},{6,10},{10,14},{3,7},{... | collective-permute-start | bytes 786440 | tf_op jit(solution)/shard_map/ppermute | solution.py:19
  21.6 0.0 collective-permute-done.4.refs_6_.refs_2_
  21.6 1.3 %collective-permute-start.5 = (bf16[128,1024]{1,0:T(8,128)(2,1)S(1)}, bf16[128,1024]{1,0:T(8,128)(2,1)S(1)}, u32[]{:S(2)}, u32[]{:S(2)}) collective-permute-start(bf16[128,1024]{1,0:T(8,128)(2,1)S(1)} %collective-permute-done.4.refs_6_.refs_2_), channel_id=1, source_target_pairs={{4,0},{8,4},{12,8},{5,1},{9,5},{13,9},{6,2},{10,6},{14,10},{7,3},{... | collective-permute-start | bytes 786440 | tf_op jit(solution)/shard_map/ppermute | solution.py:19
  22.9 0.6 shard_map.128.refs_5_
  23.5 0.0 copy-start
  23.5 1.4 %collective-permute-done.3.refs_4_.refs_11_ = bf16[128,1024]{1,0:T(8,128)(2,1)S(1)} collective-permute-done((bf16[128,1024]{1,0:T(8,128)(2,1)S(1)}, bf16[128,1024]{1,0:T(8,128)(2,1)S(1)}, u32[]{:S(2)}, u32[]{:S(2)}) %collective-permute-start.3) | collective-permute-done | bytes 262176 | tf_op jit(solution)/shard_map/ppermute | solution.py:19
  24.9 3.6 %collective-permute-done.1.refs_3_.refs_8_ = bf16[128,1024]{1,0:T(8,128)(2,1)S(1)} collective-permute-done((bf16[128,1024]{1,0:T(8,128)(2,1)S(1)}, bf16[128,1024]{1,0:T(8,128)(2,1)S(1)}, u32[]{:S(2)}, u32[]{:S(2)}) %collective-permute-start.1) | collective-permute-done | bytes 262176 | tf_op jit(solution)/shard_map/ppermute | solution.py:19
  28.4 1.7 %collective-permute-done.5.refs_9_.refs_2_ = bf16[128,1024]{1,0:T(8,128)(2,1)S(1)} collective-permute-done((bf16[128,1024]{1,0:T(8,128)(2,1)S(1)}, bf16[128,1024]{1,0:T(8,128)(2,1)S(1)}, u32[]{:S(2)}, u32[]{:S(2)}) %collective-permute-start.5) | collective-permute-done | bytes 262176 | tf_op jit(solution)/shard_map/ppermute | solution.py:19
  30.2 0.0 copy-done
  30.2 1.0 %shard_map.129 = (f32[128,1024]{1,0:T(8,128)S(1)}, bf16[128,1024]{1,0:T(8,128)(2,1)S(1)}, f32[1,1024]{1,0:T(1,128)S(1)}) custom-call(f32[64,128]{1,0:T(8,128)S(1)} %get-tuple-element.39.refs_0_, f32[128,128]{1,0:T(8,128)S(1)} %get-tuple-element.42.refs_1_.refs_3_, bf16[128,1024]{1,0:T(8,128)(2,1)S(1)} %get-tuple-element.43.refs_2_.refs_4_, ...), custom_call_target="tpu_custom_call" | custom-call | flops 1000000 | bytes 100000 | tf_op jit(solution)/shard_map/pallas_call | solution.py:298
  31.2 1.3 %collective-permute-start.6 = (bf16[128,1024]{1,0:T(8,128)(2,1)S(1)}, bf16[128,1024]{1,0:T(8,128)(2,1)S(1)}, u32[]{:S(2)}, u32[]{:S(2)}) collective-permute-start(bf16[128,1024]{1,0:T(8,128)(2,1)S(1)} %get-tuple-element.49.refs_5_.refs_3_), channel_id=1, source_target_pairs={{4,0},{8,4},{12,8},{5,1},{9,5},{13,9},{6,2},{10,6},{14,10},{7,3},{... | collective-permute-start | bytes 786440 | tf_op jit(solution)/shard_map/ppermute | solution.py:19
  32.5 2.8 %shard_map.130 = (bf16[128,1024]{1,0:T(8,128)(2,1)}, f32[16,128]{1,0:T(8,128)S(1)}) custom-call(f32[64,128]{1,0:T(8,128)S(1)} %get-tuple-element.39.refs_0_, f32[128,128]{1,0:T(8,128)S(1)} %get-tuple-element.40.refs_1_, f32[128,128]{1,0:T(8,128)S(1)} %get-tuple-element.41.refs_1_.refs_2_, f32[128,128]{1,0:T(8,128)S(1)} %get-tuple-element.42.refs_1_.refs_3_, ...), custom_call_target="tpu_custom_call" | custom-call | flops 1000000 | bytes 100000 | tf_op jit(solution)/shard_map/pallas_call | solution.py:298
  35.2 0.0 collective-permute-start.7
  35.2 1.5 %collective-permute-start.8 = (f32[16,128]{1,0:T(8,128)S(1)}, f32[16,128]{1,0:T(8,128)S(1)}, u32[]{:S(2)}, u32[]{:S(2)}) collective-permute-start(f32[16,128]{1,0:T(8,128)S(1)} %get-tuple-element.64), channel_id=1, source_target_pairs={{0,2},{1,3},{2,0},{3,1},{4,6},{5,7},{6,4},{7,5},{8,10},{9,11},{10,... | collective-permute-start | bytes 24584 | tf_op jit(solution)/shard_map/ppermute | solution.py:327
  36.7 0.4 collective-permute-start.9
  37.1 0.0 collective-permute-done.7.refs_6_.refs_8_
  37.1 1.8 %collective-permute-done.8 = f32[16,128]{1,0:T(8,128)S(1)} collective-permute-done((f32[16,128]{1,0:T(8,128)S(1)}, f32[16,128]{1,0:T(8,128)S(1)}, u32[]{:S(2)}, u32[]{:S(2)}) %collective-permute-start.8) | collective-permute-done | bytes 8224 | tf_op jit(solution)/shard_map/ppermute | solution.py:327
  38.9 0.9 %collective-permute-done.9 = f32[16,128]{1,0:T(8,128)S(1)} collective-permute-done((f32[16,128]{1,0:T(8,128)S(1)}, f32[16,128]{1,0:T(8,128)S(1)}, u32[]{:S(2)}, u32[]{:S(2)}) %collective-permute-start.9) | collective-permute-done | bytes 8224 | tf_op jit(solution)/shard_map/ppermute | solution.py:327
  39.8 0.0 collective-permute-done.6.refs_3_
  39.8 1.3 %collective-permute-start.10 = (bf16[128,1024]{1,0:T(8,128)(2,1)S(1)}, bf16[128,1024]{1,0:T(8,128)(2,1)S(1)}, u32[]{:S(2)}, u32[]{:S(2)}) collective-permute-start(bf16[128,1024]{1,0:T(8,128)(2,1)S(1)} %collective-permute-done.6.refs_3_), channel_id=1, source_target_pairs={{4,0},{8,4},{12,8},{5,1},{9,5},{13,9},{6,2},{10,6},{14,10},{7,3},{... | collective-permute-start | bytes 786440 | tf_op jit(solution)/shard_map/ppermute | solution.py:19
  41.1 3.3 %collective-permute-start.11 = (f32[16,128]{1,0:T(8,128)S(1)}, f32[16,128]{1,0:T(8,128)S(1)}, u32[]{:S(2)}, u32[]{:S(2)}) collective-permute-start(f32[16,128]{1,0:T(8,128)S(1)} %add_add_fusion.refs_8_), channel_id=1, source_target_pairs={{0,4},{4,0},{8,12},{12,8},{1,5},{5,1},{9,13},{13,9},{2,6},{6,2},{1... | collective-permute-start | bytes 24584 | tf_op jit(solution)/shard_map/ppermute | solution.py:327
  44.5 3.0 %collective-permute-start.12 = (f32[16,128]{1,0:T(8,128)S(1)}, f32[16,128]{1,0:T(8,128)S(1)}, u32[]{:S(2)}, u32[]{:S(2)}) collective-permute-start(f32[16,128]{1,0:T(8,128)S(1)} %add_add_fusion.refs_8_), channel_id=1, source_target_pairs={{0,8},{4,12},{8,0},{12,4},{1,9},{5,13},{9,1},{13,5},{2,10},{6,14},... | collective-permute-start | bytes 24584 | tf_op jit(solution)/shard_map/ppermute | solution.py:327
  47.5 0.0 collective-permute-start.13
  47.5 0.9 %shard_map.131 = (f32[128,1024]{1,0:T(8,128)S(1)}, f32[128,1024]{1,0:T(8,128)S(1)}) custom-call(f32[64,128]{1,0:T(8,128)S(1)} %get-tuple-element.39.refs_0_, f32[128,128]{1,0:T(8,128)S(1)} %get-tuple-element.58.refs_1_, bf16[128,1024]{1,0:T(8,128)(2,1)S(1)} %get-tuple-element.43.refs_2_.refs_4_, bf16[128,1024]{1,0:T(8,128)(2,1)S(1)} %get-tuple-element.49.refs_5_.refs_3_, ...), custom_call_target="tpu_custom_call" | custom-call | flops 1000000 | bytes 100000 | tf_op jit(solution)/shard_map/pallas_call | solution.py:298
  48.3 0.8 %shard_map.132 = (f32[128,1024]{1,0:T(8,128)S(1)}, f32[128,1024]{1,0:T(8,128)S(1)}) custom-call(f32[64,128]{1,0:T(8,128)S(1)} %get-tuple-element.39.refs_0_, f32[128,128]{1,0:T(8,128)S(1)} %get-tuple-element.57.refs_1_, bf16[128,1024]{1,0:T(8,128)(2,1)S(1)} %collective-permute-done.4.refs_6_.refs_2_, bf16[128,1024]{1,0:T(8,128)(2,1)S(1)} %collective-permute-done.6.refs_3_, ...), custom_call_target="tpu_custom_call" | custom-call | flops 1000000 | bytes 100000 | tf_op jit(solution)/shard_map/pallas_call | solution.py:298
  49.2 1.0 %shard_map.134 = bf16[128,1024]{1,0:T(8,128)(2,1)} custom-call(f32[128,1024]{1,0:T(8,128)S(1)} %get-tuple-element.69.refs_0_, bf16[128,1024]{1,0:T(8,128)(2,1)S(1)} %get-tuple-element.47.refs_6_.refs_1_, f32[1,1024]{1,0:T(1,128)S(1)} %bitcast.12, f32[128,1024]{1,0:T(8,128)S(1)} %get-tuple-element.62.refs_6_.refs_3_), custom_call_target="tpu_custom_call" | custom-call | flops 1000000 | bytes 100000 | tf_op jit(solution)/shard_map/pallas_call | solution.py:298
  50.2 1.1 %collective-permute-done.11.refs_9_ = f32[16,128]{1,0:T(8,128)S(1)} collective-permute-done((f32[16,128]{1,0:T(8,128)S(1)}, f32[16,128]{1,0:T(8,128)S(1)}, u32[]{:S(2)}, u32[]{:S(2)}) %collective-permute-start.11) | collective-permute-done | bytes 8224 | tf_op jit(solution)/shard_map/ppermute | solution.py:327
  51.2 1.3 %collective-permute-done.12.refs_10_ = f32[16,128]{1,0:T(8,128)S(1)} collective-permute-done((f32[16,128]{1,0:T(8,128)S(1)}, f32[16,128]{1,0:T(8,128)S(1)}, u32[]{:S(2)}, u32[]{:S(2)}) %collective-permute-start.12) | collective-permute-done | bytes 8224 | tf_op jit(solution)/shard_map/ppermute | solution.py:327
  52.5 1.2 %collective-permute-done.13.refs_11_ = f32[16,128]{1,0:T(8,128)S(1)} collective-permute-done((f32[16,128]{1,0:T(8,128)S(1)}, f32[16,128]{1,0:T(8,128)S(1)}, u32[]{:S(2)}, u32[]{:S(2)}) %collective-permute-start.13) | collective-permute-done | bytes 8224 | tf_op jit(solution)/shard_map/ppermute | solution.py:327
  53.7 0.0 collective-permute-done.10.refs_3_
  53.7 2.1 %shard_map.133 = (bf16[128,1024]{1,0:T(8,128)(2,1)}, bf16[128,1024]{1,0:T(8,128)(2,1)}, f32[8,128]{1,0:T(8,128)}, f32[8,8]{1,0:T(8,128)}) custom-call(f32[64,128]{1,0:T(8,128)S(1)} %get-tuple-element.39.refs_0_, f32[128,128]{1,0:T(8,128)S(1)} %get-tuple-element.54.refs_1_, bf16[128,1024]{1,0:T(8,128)(2,1)S(1)} %collective-permute-done.5.refs_9_.refs_2_, ...), custom_call_target="tpu_custom_call" | custom-call | flops 1000000 | bytes 100000 | tf_op jit(solution)/shard_map/pallas_call | solution.py:298
  (1 shorter events, 0.0 us)
Async XLA Ops:
  0.6 9.8 %copy-start.1 = (f32[8,8]{1,0:T(8,128)S(1)}, f32[8,8]{1,0:T(8,128)}, u32[]{:S(2)}) copy-start(f32[8,8]{1,0:T(8,128)} %refs_1_.1) | copy-start | bytes 772
  0.6 12.9 %collective-permute-start.2 = (bf16[128,1024]{1,0:T(8,128)(2,1)}, bf16[128,1024]{1,0:T(8,128)(2,1)S(1)}, u32[]{:S(2)}, u32[]{:S(2)}) collective-permute-start(bf16[128,1024]{1,0:T(8,128)(2,1)} %bitcast.15), channel_id=1, source_target_pairs={{0,4},{4,8},{8,12},{1,5},{5,9},{9,13},{2,6},{6,10},{10,14},{3,7},{... | collective-permute-start | bytes 786440 | tf_op jit(solution)/shard_map/ppermute | solution.py:19
  5.6 12.5 %collective-permute-start = (bf16[128,1024]{1,0:T(8,128)(2,1)}, bf16[128,1024]{1,0:T(8,128)(2,1)S(1)}, u32[]{:S(2)}, u32[]{:S(2)}) collective-permute-start(bf16[128,1024]{1,0:T(8,128)(2,1)} %bitcast.17), channel_id=1, source_target_pairs={{0,4},{4,8},{8,12},{1,5},{5,9},{9,13},{2,6},{6,10},{10,14},{3,7},{... | collective-permute-start | bytes 786440 | tf_op jit(solution)/shard_map/ppermute | solution.py:19
  9.1 12.5 %collective-permute-start.4 = (bf16[128,1024]{1,0:T(8,128)(2,1)}, bf16[128,1024]{1,0:T(8,128)(2,1)S(1)}, u32[]{:S(2)}, u32[]{:S(2)}) collective-permute-start(bf16[128,1024]{1,0:T(8,128)(2,1)} %bitcast.19), channel_id=1, source_target_pairs={{4,0},{8,4},{12,8},{5,1},{9,5},{13,9},{6,2},{10,6},{14,10},{7,3},{... | collective-permute-start | bytes 786440 | tf_op jit(solution)/shard_map/ppermute | solution.py:19
  10.4 0.7 %copy-start.2 = (s32[1,4]{1,0:T(1,128)S(1)}, s32[1,4]{1,0:T(1,128)}, u32[]{:S(2)}) copy-start(s32[1,4]{1,0:T(1,128)} %refs_0_.1) | copy-start | bytes 52
  13.6 11.3 %collective-permute-start.3 = (bf16[128,1024]{1,0:T(8,128)(2,1)S(1)}, bf16[128,1024]{1,0:T(8,128)(2,1)S(1)}, u32[]{:S(2)}, u32[]{:S(2)}) collective-permute-start(bf16[128,1024]{1,0:T(8,128)(2,1)S(1)} %collective-permute-done.2.refs_4_.refs_10_), channel_id=1, source_target_pairs={{0,4},{4,8},{8,12},{1,5},{5,9},{9,13},{2,6},{6,10},{10,14},{3,7},{... | collective-permute-start | bytes 786440 | tf_op jit(solution)/shard_map/ppermute | solution.py:19
  18.1 10.3 %collective-permute-start.1 = (bf16[128,1024]{1,0:T(8,128)(2,1)S(1)}, bf16[128,1024]{1,0:T(8,128)(2,1)S(1)}, u32[]{:S(2)}, u32[]{:S(2)}) collective-permute-start(bf16[128,1024]{1,0:T(8,128)(2,1)S(1)} %collective-permute-done.refs_3_.refs_7_), channel_id=1, source_target_pairs={{0,4},{4,8},{8,12},{1,5},{5,9},{9,13},{2,6},{6,10},{10,14},{3,7},{... | collective-permute-start | bytes 786440 | tf_op jit(solution)/shard_map/ppermute | solution.py:19
  21.6 8.5 %collective-permute-start.5 = (bf16[128,1024]{1,0:T(8,128)(2,1)S(1)}, bf16[128,1024]{1,0:T(8,128)(2,1)S(1)}, u32[]{:S(2)}, u32[]{:S(2)}) collective-permute-start(bf16[128,1024]{1,0:T(8,128)(2,1)S(1)} %collective-permute-done.4.refs_6_.refs_2_), channel_id=1, source_target_pairs={{4,0},{8,4},{12,8},{5,1},{9,5},{13,9},{6,2},{10,6},{14,10},{7,3},{... | collective-permute-start | bytes 786440 | tf_op jit(solution)/shard_map/ppermute | solution.py:19
  23.5 6.7 %copy-start = (f32[1024]{0:T(1024)S(1)}, f32[1024]{0:T(1024)}, u32[]{:S(2)}) copy-start(f32[1024]{0:T(1024)} %param.15) | copy-start | bytes 12292
  31.2 8.7 %collective-permute-start.6 = (bf16[128,1024]{1,0:T(8,128)(2,1)S(1)}, bf16[128,1024]{1,0:T(8,128)(2,1)S(1)}, u32[]{:S(2)}, u32[]{:S(2)}) collective-permute-start(bf16[128,1024]{1,0:T(8,128)(2,1)S(1)} %get-tuple-element.49.refs_5_.refs_3_), channel_id=1, source_target_pairs={{4,0},{8,4},{12,8},{5,1},{9,5},{13,9},{6,2},{10,6},{14,10},{7,3},{... | collective-permute-start | bytes 786440 | tf_op jit(solution)/shard_map/ppermute | solution.py:19
  35.2 1.9 %collective-permute-start.7 = (f32[16,128]{1,0:T(8,128)S(1)}, f32[16,128]{1,0:T(8,128)S(1)}, u32[]{:S(2)}, u32[]{:S(2)}) collective-permute-start(f32[16,128]{1,0:T(8,128)S(1)} %get-tuple-element.64), channel_id=1, source_target_pairs={{0,1},{1,0},{2,3},{3,2},{4,5},{5,4},{6,7},{7,6},{8,9},{9,8},{10,11... | collective-permute-start | bytes 24584 | tf_op jit(solution)/shard_map/ppermute | solution.py:327
  35.2 3.7 %collective-permute-start.8 = (f32[16,128]{1,0:T(8,128)S(1)}, f32[16,128]{1,0:T(8,128)S(1)}, u32[]{:S(2)}, u32[]{:S(2)}) collective-permute-start(f32[16,128]{1,0:T(8,128)S(1)} %get-tuple-element.64), channel_id=1, source_target_pairs={{0,2},{1,3},{2,0},{3,1},{4,6},{5,7},{6,4},{7,5},{8,10},{9,11},{10,... | collective-permute-start | bytes 24584 | tf_op jit(solution)/shard_map/ppermute | solution.py:327
  36.7 3.1 %collective-permute-start.9 = (f32[16,128]{1,0:T(8,128)S(1)}, f32[16,128]{1,0:T(8,128)S(1)}, u32[]{:S(2)}, u32[]{:S(2)}) collective-permute-start(f32[16,128]{1,0:T(8,128)S(1)} %get-tuple-element.64), channel_id=1, source_target_pairs={{0,3},{1,2},{2,1},{3,0},{4,7},{5,6},{6,5},{7,4},{8,11},{9,10},{10,... | collective-permute-start | bytes 24584 | tf_op jit(solution)/shard_map/ppermute | solution.py:327
  39.8 13.9 %collective-permute-start.10 = (bf16[128,1024]{1,0:T(8,128)(2,1)S(1)}, bf16[128,1024]{1,0:T(8,128)(2,1)S(1)}, u32[]{:S(2)}, u32[]{:S(2)}) collective-permute-start(bf16[128,1024]{1,0:T(8,128)(2,1)S(1)} %collective-permute-done.6.refs_3_), channel_id=1, source_target_pairs={{4,0},{8,4},{12,8},{5,1},{9,5},{13,9},{6,2},{10,6},{14,10},{7,3},{... | collective-permute-start | bytes 786440 | tf_op jit(solution)/shard_map/ppermute | solution.py:19
  41.1 10.1 %collective-permute-start.11 = (f32[16,128]{1,0:T(8,128)S(1)}, f32[16,128]{1,0:T(8,128)S(1)}, u32[]{:S(2)}, u32[]{:S(2)}) collective-permute-start(f32[16,128]{1,0:T(8,128)S(1)} %add_add_fusion.refs_8_), channel_id=1, source_target_pairs={{0,4},{4,0},{8,12},{12,8},{1,5},{5,1},{9,13},{13,9},{2,6},{6,2},{1... | collective-permute-start | bytes 24584 | tf_op jit(solution)/shard_map/ppermute | solution.py:327
  44.5 8.0 %collective-permute-start.12 = (f32[16,128]{1,0:T(8,128)S(1)}, f32[16,128]{1,0:T(8,128)S(1)}, u32[]{:S(2)}, u32[]{:S(2)}) collective-permute-start(f32[16,128]{1,0:T(8,128)S(1)} %add_add_fusion.refs_8_), channel_id=1, source_target_pairs={{0,8},{4,12},{8,0},{12,4},{1,9},{5,13},{9,1},{13,5},{2,10},{6,14},... | collective-permute-start | bytes 24584 | tf_op jit(solution)/shard_map/ppermute | solution.py:327
  47.5 6.3 %collective-permute-start.13 = (f32[16,128]{1,0:T(8,128)S(1)}, f32[16,128]{1,0:T(8,128)S(1)}, u32[]{:S(2)}, u32[]{:S(2)}) collective-permute-start(f32[16,128]{1,0:T(8,128)S(1)} %add_add_fusion.refs_8_), channel_id=1, source_target_pairs={{0,12},{4,8},{8,4},{12,0},{1,13},{5,9},{9,5},{13,1},{2,14},{6,10},... | collective-permute-start | bytes 24584 | tf_op jit(solution)/shard_map/ppermute | solution.py:327

commit v5 on v4

--- a/solution.py
+++ b/solution.py
@@ -35,10 +35,10 @@
 
 
 class Pair:
-    def __init__(self, mask, table, heads, hops, flipped=False):
+    def __init__(self, mask, table, heads, hops, flipped=False, near=None):
         rows = mask.shape[0]
         self.table, self.heads, self.levels = table, heads, table.shape[0] // heads
-        self.mask = mask[...]
+        self.mask, self.hops, self.near = mask[...], hops, near
         self.far = (hops - 1) * rows + 1 >= 2 ** (self.levels - 2)
         if not self.far:
             query_dim, key_dim = (1, 0) if flipped else (0, 1)
@@ -46,33 +46,24 @@
             key_row = lax.broadcasted_iota(jnp.int32, mask.shape, key_dim)
             self.distance = query_row - key_row + hops * rows
 
-    def half_logits(self, scores, head, scaling):
+    def half_bias(self, head):
         def level_row(level):
             at = level * self.heads + head
             return self.table[at : at + 1, :]
 
         value = level_row(self.levels - 1)
-        if not self.far:
-            for level in range(self.levels - 2, -1, -1):
-                value = jnp.where(self.distance < 2**level, level_row(level), value)
-        return scores * (0.5 * scaling) + value
-
-    def bias_rows(self, grads):
-        sub = lax.broadcasted_iota(jnp.int32, (self.levels, grads.shape[1]), 0)
         if self.far:
-            row = jnp.sum(grads, axis=0, keepdims=True)
-            return jnp.where(sub == self.levels - 1, row, 0.0)
-        total = jnp.zeros(sub.shape, F32)
-        for level in range(self.levels):
-            inside = None
-            if level > 0:
-                inside = self.distance >= 2 ** (level - 1)
-            if level < self.levels - 1:
-                below = self.distance < 2**level
-                inside = below if inside is None else inside & below
-            row = jnp.sum(jnp.where(inside, grads, 0.0), axis=0, keepdims=True)
-            total = jnp.where(sub == level, row, total)
-        return total
+            return value
+        if self.near is not None:
+            rows = self.mask.shape[0]
+            close = self.near[head * rows : (head + 1) * rows, :]
+            return close if self.hops == 0 else jnp.where(self.distance < rows, close, value)
+        for level in range(self.levels - 2, -1, -1):
+            value = jnp.where(self.distance < 2**level, level_row(level), value)
+        return value
+
+    def half_logits(self, scores, head, scaling):
+        return scores * (0.5 * scaling) + self.half_bias(head)
 
 
 def slope_of(half, tanh):
@@ -113,7 +104,7 @@
 
 def first_kernel(plan, heads, scaling, lengths, bias, *refs):
     inputs, refs = refs[:5], refs[5:]
-    table, masks, refs = refs[0], refs[1 : 1 + len(plan)], refs[1 + len(plan) :]
+    table, near, masks, refs = refs[0], refs[1], refs[2 : 2 + len(plan)], refs[2 + len(plan) :]
     held, out, arrived = refs[:5], refs[5], refs[6]
     copies = [
         pltpu.make_async_copy(source, target, arrived.at[at])
@@ -126,8 +117,16 @@
         for head in range(heads):
             at = level * heads + head
             table[at : at + 1, :] = jnp.full((1, table.shape[1]), 0.5 * bias[level, head], F32)
+    rows = masks[0].shape[0]
+    apart = lax.broadcasted_iota(jnp.int32, (rows, rows), 0)
+    apart = (apart - lax.broadcasted_iota(jnp.int32, (rows, rows), 1)) & (rows - 1)
+    for head in range(heads):
+        value = table[(levels - 1) * heads + head : (levels - 1) * heads + head + 1, :]
+        for level in range(levels - 2, -1, -1):
+            at = level * heads + head
+            value = jnp.where(apart < 2**level, table[at : at + 1, :], value)
+        near[head * rows : (head + 1) * rows, :] = value
     for (block, hops, flipped), mask in zip(plan, masks):
-        rows = mask.shape[0]
         query_dim, key_dim = (1, 0) if flipped else (0, 1)
         line = (1, rows) if flipped else (rows, 1)
         first = (lax.axis_index("ctx") + block) * rows
@@ -138,12 +137,12 @@
     for copy in copies:
         copy.wait()
     query, key, value = held[:3]
-    pair = Pair(masks[0], table, heads, 0)
+    pair = Pair(masks[0], table, heads, 0, near=near)
     attend([pair], heads, scaling, query, [key], [value], None, out)
 
 
-def forward_kernel(hops, heads, scaling, table, mask, query, key, value, total, out):
-    pair = Pair(mask, table, heads, hops)
+def forward_kernel(hops, heads, scaling, table, near, mask, query, key, value, total, out):
+    pair = Pair(mask, table, heads, hops, near=near)
     attend([pair], heads, scaling, query, [key], [value], total, out)
 
 
@@ -154,9 +153,8 @@
 
 
 def norm_kernel(hops, heads, scaling, *refs):
-    table, mask, query, key, value, total, out_grad, update_gate, gain = refs[:9]
-    attention, attn_grad, gain_grad = refs[9:]
-    forward_kernel(hops, heads, scaling, table, mask, query, key, value, total, attention)
+    out_grad, update_gate, gain, attention, attn_grad, gain_grad = refs[-6:]
+    forward_kernel(hops, heads, scaling, *refs[:-6], attention)
     rows, features = attention.shape
     step = 16
     gain_row = gain[...]
@@ -191,17 +189,35 @@
 
 def backward_query_kernel(hop_list, heads, scaling, *refs):
     count = len(hop_list)
-    table, masks = refs[0], refs[1 : 1 + count]
-    query, grad = refs[1 + count : 3 + count]
-    keys, values = refs[3 + count : 3 + 2 * count], refs[3 + 2 * count : 3 + 3 * count]
-    gain_in, query_out, small_out = refs[3 + 3 * count :]
-    width = query.shape[1] // heads
-    pairs = [Pair(mask, table, heads, hops) for mask, hops in zip(masks, hop_list)]
+    table, near, masks, refs = refs[0], refs[1], refs[2 : 2 + count], refs[2 + count :]
+    query, grad, keys, values = refs[0], refs[1], refs[2 : 2 + count], refs[2 + count : 2 + 2 * count]
+    gain_in, query_out, small_out = refs[2 + 2 * count :]
+    rows, width = query.shape[0], query.shape[1] // heads
+    pairs = [Pair(mask, table, heads, hops, near=near) for mask, hops in zip(masks, hop_list)]
     lanes = small_out.shape[1]
     lines = gain_in.shape[1] // lanes
     levels = small_out.shape[0] - lines
     lane = lax.broadcasted_iota(jnp.int32, (levels, lanes), 1)
+    level_row = lax.broadcasted_iota(jnp.int32, (levels, lanes), 0)
+    group = lax.broadcasted_iota(jnp.int32, (8, rows), 0)
+    distance = (group - lax.broadcasted_iota(jnp.int32, (8, rows), 1)) & (rows - 1)
+    bucket = sum((distance >= 2**level).astype(jnp.int32) for level in range(levels - 1))
+    own = pairs[0].distance >= 0
     bias_total = [jnp.zeros((levels, lanes), F32)]
+
+    def bias_sums(grads):
+        close = jnp.where(own, grads[0], grads[1])
+        rest = sum(grads[2:], jnp.where(own, grads[1], 0.0))
+        by_place, far = jnp.zeros((8, rows), F32), jnp.zeros((8, rows), F32)
+        for low in range(0, rows, 8):
+            part = close[low : low + 8, :]
+            by_place = by_place + (pltpu.roll(part, rows - low, 1) if low else part)
+            far = far + rest[low : low + 8, :]
+        sums = jnp.where(level_row == levels - 1, jnp.sum(far, axis=0, keepdims=True), 0.0)
+        for level in range(levels):
+            row = jnp.sum(jnp.where(bucket == level, by_place, 0.0), axis=0, keepdims=True)
+            sums = sums + jnp.where(level_row == level, row, 0.0)
+        return sums
 
     def scores(head):
         cols = columns(head, width)
@@ -213,16 +229,14 @@
 
     def differentiate(head, found):
         cols = columns(head, width)
-        query_part, bias_part = None, None
+        query_part, grads = None, []
         for pair, key, (score, weight_grad) in zip(pairs, keys, found):
             half = pair.half_logits(score, head, scaling)
-            logit_grad = weight_grad * (slope_of(half, jnp.tanh(half)) * pair.mask)
-            added = contract(logit_grad.astype(BF16), key[:, cols], 1, 0)
+            grads.append(weight_grad * (slope_of(half, jnp.tanh(half)) * pair.mask))
+            added = contract(grads[-1].astype(BF16), key[:, cols], 1, 0)
             query_part = added if query_part is None else query_part + added
-            sums = pair.bias_rows(logit_grad)
-            bias_part = sums if bias_part is None else bias_part + sums
         query_out[:, cols] = (query_part * scaling).astype(BF16)
-        sums = jnp.sum(bias_part, axis=1, keepdims=True)
+        sums = jnp.sum(bias_sums(grads), axis=1, keepdims=True)
         bias_total[0] = jnp.where(lane == head, sums, bias_total[0])
 
     in_stages(heads, scores, differentiate, 1)
@@ -263,25 +277,30 @@
 
 
 def last_kernel(hops, heads, scaling, *refs):
-    pieces = refs[8:-7]
-    key_out, value_out, gain_out, bias_out, key_held, value_held, written = refs[-7:]
+    pieces, outs, held = refs[8:-9], refs[-9:-5], refs[-5:-1]
+    written = refs[-1]
     copies = []
     group = 2
 
+    def write(at, cols):
+        source, target = held[at].at[:, cols], outs[at].at[:, cols]
+        copies.append(pltpu.make_async_copy(source, target, written.at[len(copies)]))
+        copies[-1].start()
+
     def store(head, cols, key_part, value_part):
-        key_held[:, cols] = (key_part * scaling).astype(BF16)
-        value_held[:, cols] = value_part.astype(BF16)
+        held[0][:, cols] = (key_part * scaling).astype(BF16)
+        held[1][:, cols] = value_part.astype(BF16)
         if (head + 1) % group == 0:
             done = slice(cols.stop - group * (cols.stop - cols.start), cols.stop)
-            for held, out in ((key_held, key_out), (value_held, value_out)):
-                at = written.at[len(copies)]
-                copies.append(pltpu.make_async_copy(held.at[:, done], out.at[:, done], at))
-                copies[-1].start()
+            write(0, done)
+            write(1, done)
 
     total = added_up([piece[...] for piece in pieces])
-    lines = gain_out.shape[0]
-    gain_out[...] = total[:lines]
-    bias_out[...] = total[lines:, :heads]
+    lines = held[2].shape[0]
+    held[2][...] = total[:lines]
+    held[3][...] = total[lines:, :heads]
+    for at in (2, 3):
+        write(at, slice(0, held[at].shape[1]))
     add_key_grads(hops, heads, scaling, *refs[:6], refs[6:8], store)
     for copy in copies:
         copy.wait()
@@ -345,42 +364,42 @@
     inputs = (queries[0], key_rows[0], value_rows[0], update_gate[0], out_grad[0])
     gain = norm_gain[None]
 
+    arrived = [passed_along(inputs[at], "ctx", by) for at, by in ((1, 1), (2, 1), (0, -1))]
+
     hop_list = tuple(range(reach + 1))
     plan = [(0, hops, False) for hops in hop_list] + [(hops, hops, True) for hops in hop_list]
-    outs = [jax.ShapeDtypeStruct((levels * heads, rows), F32)]
+    outs = [jax.ShapeDtypeStruct((count * heads, rows), F32) for count in (levels, rows)]
     outs += [jax.ShapeDtypeStruct((rows, rows), F32)] * len(plan)
     outs += [narrow] * len(inputs) + [wide]
-    table, *found = on_device(
+    table, near, *found = on_device(
         partial(first_kernel, plan, heads, scaling),
         outs,
         (),
         (user_lengths, rel_bias),
         far=inputs,
+        ahead=arrived,
         scratch=[pltpu.SemaphoreType.DMA((len(inputs),))],
     )
     masks, flipped = found[: reach + 1], found[reach + 1 : 2 * reach + 2]
     query, key, value, gate, grad, attention = found[2 * reach + 2 :]
 
-    later_queries = [query, passed_along(inputs[0], "ctx", -1)]
-    keys = [key, passed_along(inputs[1], "ctx", 1)]
-    values = [value, passed_along(inputs[2], "ctx", 1)]
+    later_queries = [query, *arrived[2:]]
+    keys, values = [key, *arrived[:1]], [value, *arrived[1:2]]
     for hops in range(1, reach):
         keys.append(passed_along(keys[-1], "ctx", 1))
-        if hops == 1:
-            values[1], attention = lax.optimization_barrier((values[1], attention))
         values.append(passed_along(values[-1], "ctx", 1))
         later_queries.append(passed_along(later_queries[-1], "ctx", -1))
     for hops in range(1, reach):
         (attention,) = on_device(
             partial(forward_kernel, hops, heads, scaling),
             [wide],
-            (table, masks[hops], query, keys[hops], values[hops], attention),
+            (table, near, masks[hops], query, keys[hops], values[hops], attention),
             ahead=later_queries[hops : hops + 1],
         )
     attention, attn_grad, gain_part = on_device(
         partial(norm_kernel, reach, heads, scaling),
         [wide, narrow, jax.ShapeDtypeStruct((1, features), F32)],
-        (table, masks[-1], query, keys[-1], values[-1], attention, grad, gate, gain),
+        (table, near, masks[-1], query, keys[-1], values[-1], attention, grad, gate, gain),
         ahead=later_queries[reach:],
     )
 
@@ -388,12 +407,12 @@
     query_grad, sums = on_device(
         partial(backward_query_kernel, hop_list, heads, scaling),
         [narrow, jax.ShapeDtypeStruct((8 + levels, lanes), F32)],
-        (table, *masks, query, attn_grad, *keys, *values, gain_part),
+        (table, near, *masks, query, attn_grad, *keys, *values, gain_part),
     )
     later_grads = [attn_grad, passed_along(attn_grad, "ctx", -1)]
     pieces = [sums]
     first_pieces = None
-    for number, (axis, distances) in enumerate(rounds_of(("dp", "ctx")), 1):
+    for number, (axis, distances) in enumerate(rounds_of(("ctx", "dp")), 1):
         pieces = exchanged(added_up(pieces), axis, distances)
         if number < reach:
             arrived, *pieces = lax.optimization_barrier((later_grads[-1], *pieces))
@@ -426,8 +445,10 @@
             *key_grads,
             *pieces,
         ),
-        far_outs=2,
-        scratch=[pltpu.VMEM((rows, features), BF16)] * 2 + [pltpu.SemaphoreType.DMA((heads,))],
+        far_outs=4,
+        scratch=[pltpu.VMEM((rows, features), BF16)] * 2
+        + [pltpu.VMEM((8, lanes), F32), pltpu.VMEM((levels, heads), F32)]
+        + [pltpu.SemaphoreType.DMA((heads + 2,))],
     )
     return (
         query_grad[None],

time: 56.2 us -> 55.2 us (0.982)
  waiting for transfers between devices: 13 us -> 11.4 us
  starting transfers between devices: 29.8 us -> 31.4 us
  Pallas kernels: 11.6 us -> 10.6 us
    ppermute x6, waiting for transfers between devices: 6.28 us -> 3.99 us  [exchanged(): lax.ppermute(array, axis, [(i, i ^ distance) for i in range(size)])]
    ppermute x8, starting transfers between devices: 21.6 us -> 23.2 us  [passed_along(): return lax.ppermute(array, axis, pairs)]
    pallas_call x8, Pallas kernels: 11.6 us -> 10.6 us  [on_device(): pl.pallas_call(body, out_shape=outs, in_specs=[pl.BlockSpec(memory_space=...]
    ppermute x8, waiting for transfers between devices: 6.68 us -> 7.39 us  [passed_along(): return lax.ppermute(array, axis, pairs)]
  transfers between devices with their start and end apart: 14 -> 14, of which waited for: 8 -> 7; matrix products, arithmetic and copies ran while one was open for 0% -> 0% of each run, Pallas kernels for 15% -> 15%
where the time goes in v5:
time: 55.2 us; the launch traced here: 54.9 us
  starting transfers between devices  31.4 us (57%)
  waiting for transfers between devices  11.4 us (21%)
  Pallas kernels  10.6 us (19%)
  between operations  0.8 us (1%)
  local copies, waits for them, and re-layouts  0.65 us (1%)
    ppermute x8, starting transfers between devices, passed_along(): return lax.ppermute(array, axis, pairs)  23.2 us
    pallas_call x8, Pallas kernels, on_device(): pl.pallas_call(body, out_shape=outs, in_specs=[pl.BlockSpec(memory_space=...  10.6 us
    ppermute x6, starting transfers between devices, exchanged(): lax.ppermute(array, axis, [(i, i ^ distance) for i in range(size)])  8.23 us
    ppermute x8, waiting for transfers between devices, passed_along(): return lax.ppermute(array, axis, pairs)  7.39 us
    ppermute x6, waiting for transfers between devices, exchanged(): lax.ppermute(array, axis, [(i, i ^ distance) for i in range(size)])  3.99 us
  transfers between devices with their start and end apart: 14, of which 7 were waited for; matrix products, arithmetic and copies ran while one was open for 0% of the time, Pallas kernels for 15%

profile of v5, /device:TPU:0, one launch (start us, length us, event | category | flops | bytes accessed | tf_op | source)
XLA Modules:
  0.0 54.9 jit_solution(5745222622366620383)
XLA Ops:
  0.6 0.0 copy-start.1
  0.6 1.3 %collective-permute-start.2 = (bf16[128,1024]{1,0:T(8,128)(2,1)}, bf16[128,1024]{1,0:T(8,128)(2,1)S(1)}, u32[]{:S(2)}, u32[]{:S(2)}) collective-permute-start(bf16[128,1024]{1,0:T(8,128)(2,1)} %bitcast.13), channel_id=1, source_target_pairs={{4,0},{8,4},{12,8},{5,1},{9,5},{13,9},{6,2},{10,6},{14,10},{7,3},{... | collective-permute-start | bytes 786440 | tf_op jit(solution)/shard_map/ppermute | solution.py:19
  1.9 5.6 %collective-permute-start = (bf16[128,1024]{1,0:T(8,128)(2,1)}, bf16[128,1024]{1,0:T(8,128)(2,1)S(1)}, u32[]{:S(2)}, u32[]{:S(2)}) collective-permute-start(bf16[128,1024]{1,0:T(8,128)(2,1)} %bitcast.15), channel_id=1, source_target_pairs={{0,4},{4,8},{8,12},{1,5},{5,9},{9,13},{2,6},{6,10},{10,14},{3,7},{... | collective-permute-start | bytes 786440 | tf_op jit(solution)/shard_map/ppermute | solution.py:19
  7.5 3.9 %collective-permute-start.1 = (bf16[128,1024]{1,0:T(8,128)(2,1)}, bf16[128,1024]{1,0:T(8,128)(2,1)S(1)}, u32[]{:S(2)}, u32[]{:S(2)}) collective-permute-start(bf16[128,1024]{1,0:T(8,128)(2,1)} %bitcast.17), channel_id=1, source_target_pairs={{0,4},{4,8},{8,12},{1,5},{5,9},{9,13},{2,6},{6,10},{10,14},{3,7},{... | collective-permute-start | bytes 786440 | tf_op jit(solution)/shard_map/ppermute | solution.py:19
  11.5 0.6 %collective-permute-done.2.refs_9_.refs_7_.refs_2_ = bf16[128,1024]{1,0:T(8,128)(2,1)S(1)} collective-permute-done((bf16[128,1024]{1,0:T(8,128)(2,1)}, bf16[128,1024]{1,0:T(8,128)(2,1)S(1)}, u32[]{:S(2)}, u32[]{:S(2)}) %collective-permute-start.2) | collective-permute-done | bytes 262176 | tf_op jit(solution)/shard_map/ppermute | solution.py:19
  12.1 1.3 %collective-permute-start.5 = (bf16[128,1024]{1,0:T(8,128)(2,1)S(1)}, bf16[128,1024]{1,0:T(8,128)(2,1)S(1)}, u32[]{:S(2)}, u32[]{:S(2)}) collective-permute-start(bf16[128,1024]{1,0:T(8,128)(2,1)S(1)} %collective-permute-done.2.refs_9_.refs_7_.refs_2_), channel_id=1, source_target_pairs={{4,0},{8,4},{12,8},{5,1},{9,5},{13,9},{6,2},{10,6},{14,10},{7,3},{... | collective-permute-start | bytes 786440 | tf_op jit(solution)/shard_map/ppermute | solution.py:19
  13.4 1.1 %collective-permute-done.refs_7_.refs_4_.refs_8_ = bf16[128,1024]{1,0:T(8,128)(2,1)S(1)} collective-permute-done((bf16[128,1024]{1,0:T(8,128)(2,1)}, bf16[128,1024]{1,0:T(8,128)(2,1)S(1)}, u32[]{:S(2)}, u32[]{:S(2)}) %collective-permute-start) | collective-permute-done | bytes 262176 | tf_op jit(solution)/shard_map/ppermute | solution.py:19
  14.5 4.3 %collective-permute-start.3 = (bf16[128,1024]{1,0:T(8,128)(2,1)S(1)}, bf16[128,1024]{1,0:T(8,128)(2,1)S(1)}, u32[]{:S(2)}, u32[]{:S(2)}) collective-permute-start(bf16[128,1024]{1,0:T(8,128)(2,1)S(1)} %collective-permute-done.refs_7_.refs_4_.refs_8_), channel_id=1, source_target_pairs={{0,4},{4,8},{8,12},{1,5},{5,9},{9,13},{2,6},{6,10},{10,14},{3,7},{... | collective-permute-start | bytes 786440 | tf_op jit(solution)/shard_map/ppermute | solution.py:19
  18.8 1.3 %collective-permute-done.1.refs_8_.refs_5_.refs_11_ = bf16[128,1024]{1,0:T(8,128)(2,1)S(1)} collective-permute-done((bf16[128,1024]{1,0:T(8,128)(2,1)}, bf16[128,1024]{1,0:T(8,128)(2,1)S(1)}, u32[]{:S(2)}, u32[]{:S(2)}) %collective-permute-start.1) | collective-permute-done | bytes 262176 | tf_op jit(solution)/shard_map/ppermute | solution.py:19
  20.1 4.3 %collective-permute-start.4 = (bf16[128,1024]{1,0:T(8,128)(2,1)S(1)}, bf16[128,1024]{1,0:T(8,128)(2,1)S(1)}, u32[]{:S(2)}, u32[]{:S(2)}) collective-permute-start(bf16[128,1024]{1,0:T(8,128)(2,1)S(1)} %collective-permute-done.1.refs_8_.refs_5_.refs_11_), channel_id=1, source_target_pairs={{0,4},{4,8},{8,12},{1,5},{5,9},{9,13},{2,6},{6,10},{10,14},{3,7},{... | collective-permute-start | bytes 786440 | tf_op jit(solution)/shard_map/ppermute | solution.py:19
  24.4 0.0 copy-start.2
  24.4 0.0 copy-done.1
  24.4 0.6 %copy-done.2 = s32[1,4]{1,0:T(1,128)S(1)} copy-done((s32[1,4]{1,0:T(1,128)S(1)}, s32[1,4]{1,0:T(1,128)}, u32[]{:S(2)}) %copy-start.2) | copy-done | bytes 40
  25.1 2.5 %shard_map.127 = (f32[64,128]{1,0:T(8,128)S(1)}, f32[1024,128]{1,0:T(8,128)S(1)}, f32[128,128]{1,0:T(8,128)S(1)}, f32[128,128]{1,0:T(8,128)S(1)}, f32[128,128]{1...) custom-call(s32[1,4]{1,0:T(1,128)S(1)} %copy-done.2, ...), custom_call_target="tpu_custom_call" | custom-call | flops 1000000 | bytes 100000 | tf_op jit(solution)/shard_map/pallas_call | solution.py:317
  27.6 0.6 %shard_map.128.refs_6_ = f32[128,1024]{1,0:T(8,128)S(1)} custom-call(f32[64,128]{1,0:T(8,128)S(1)} %get-tuple-element.38.refs_0_, f32[1024,128]{1,0:T(8,128)S(1)} %get-tuple-element.39.refs_1_, f32[128,128]{1,0:T(8,128)S(1)} %get-tuple-element.41.refs_2_.refs_3_, bf16[128,1024]{1,0:T(8,128)(2,1)S(1)} %get-tuple-element.43.refs_3_.refs_5_.refs_2_, ...), custom_call_target="tpu_custom_call" | custom-call | flops 1000000 | bytes 100000 | tf_op jit(solution)/shard_map/pallas_call | solution.py:317
  28.1 0.0 copy-start
  28.1 0.0 collective-permute-done.5.refs_10_.refs_2_
  28.1 0.0 collective-permute-done.3.refs_4_.refs_9_
  28.1 2.0 %collective-permute-done.4.refs_5_.refs_12_ = bf16[128,1024]{1,0:T(8,128)(2,1)S(1)} collective-permute-done((bf16[128,1024]{1,0:T(8,128)(2,1)S(1)}, bf16[128,1024]{1,0:T(8,128)(2,1)S(1)}, u32[]{:S(2)}, u32[]{:S(2)}) %collective-permute-start.4) | collective-permute-done | bytes 262176 | tf_op jit(solution)/shard_map/ppermute | solution.py:19
  30.1 0.0 copy-done
  30.1 1.0 %shard_map.129 = (f32[128,1024]{1,0:T(8,128)S(1)}, bf16[128,1024]{1,0:T(8,128)(2,1)S(1)}, f32[1,1024]{1,0:T(1,128)S(1)}) custom-call(f32[64,128]{1,0:T(8,128)S(1)} %get-tuple-element.38.refs_0_, f32[1024,128]{1,0:T(8,128)S(1)} %get-tuple-element.39.refs_1_, f32[128,128]{1,0:T(8,128)S(1)} %get-tuple-element.42.refs_2_.refs_4_, ...), custom_call_target="tpu_custom_call" | custom-call | flops 1000000 | bytes 100000 | tf_op jit(solution)/shard_map/pallas_call | solution.py:317
  31.1 1.3 %collective-permute-start.6 = (bf16[128,1024]{1,0:T(8,128)(2,1)S(1)}, bf16[128,1024]{1,0:T(8,128)(2,1)S(1)}, u32[]{:S(2)}, u32[]{:S(2)}) collective-permute-start(bf16[128,1024]{1,0:T(8,128)(2,1)S(1)} %get-tuple-element.47.refs_6_.refs_3_), channel_id=1, source_target_pairs={{4,0},{8,4},{12,8},{5,1},{9,5},{13,9},{6,2},{10,6},{14,10},{7,3},{... | collective-permute-start | bytes 786440 | tf_op jit(solution)/shard_map/ppermute | solution.py:19
  32.4 2.4 %shard_map.130 = (bf16[128,1024]{1,0:T(8,128)(2,1)}, f32[16,128]{1,0:T(8,128)S(1)}) custom-call(f32[64,128]{1,0:T(8,128)S(1)} %get-tuple-element.38.refs_0_, f32[1024,128]{1,0:T(8,128)S(1)} %get-tuple-element.39.refs_1_, f32[128,128]{1,0:T(8,128)S(1)} %get-tuple-element.40.refs_2_, f32[128,128]{1,0:T(8,128)S(1)} %get-tuple-element.41.refs_2_.refs_3_, ...), custom_call_target="tpu_custom_call" | custom-call | flops 1000000 | bytes 100000 | tf_op jit(solution)/shard_map/pallas_call | solution.py:317
  34.7 5.7 %collective-permute-start.9 = (f32[16,128]{1,0:T(8,128)S(1)}, f32[16,128]{1,0:T(8,128)S(1)}, u32[]{:S(2)}, u32[]{:S(2)}) collective-permute-start(f32[16,128]{1,0:T(8,128)S(1)} %get-tuple-element.62), channel_id=1, source_target_pairs={{0,12},{4,8},{8,4},{12,0},{1,13},{5,9},{9,5},{13,1},{2,14},{6,10},... | collective-permute-start | bytes 24584 | tf_op jit(solution)/shard_map/ppermute | solution.py:346
  40.5 0.0 collective-permute-start.8
  40.5 0.6 %collective-permute-start.7 = (f32[16,128]{1,0:T(8,128)S(1)}, f32[16,128]{1,0:T(8,128)S(1)}, u32[]{:S(2)}, u32[]{:S(2)}) collective-permute-start(f32[16,128]{1,0:T(8,128)S(1)} %get-tuple-element.62), channel_id=1, source_target_pairs={{0,4},{4,0},{8,12},{12,8},{1,5},{5,1},{9,13},{13,9},{2,6},{6,2},{1... | collective-permute-start | bytes 24584 | tf_op jit(solution)/shard_map/ppermute | solution.py:346
  41.1 2.1 %collective-permute-done.9 = f32[16,128]{1,0:T(8,128)S(1)} collective-permute-done((f32[16,128]{1,0:T(8,128)S(1)}, f32[16,128]{1,0:T(8,128)S(1)}, u32[]{:S(2)}, u32[]{:S(2)}) %collective-permute-start.9) | collective-permute-done | bytes 8224 | tf_op jit(solution)/shard_map/ppermute | solution.py:346
  43.2 1.8 %collective-permute-done.8 = f32[16,128]{1,0:T(8,128)S(1)} collective-permute-done((f32[16,128]{1,0:T(8,128)S(1)}, f32[16,128]{1,0:T(8,128)S(1)}, u32[]{:S(2)}, u32[]{:S(2)}) %collective-permute-start.8) | collective-permute-done | bytes 8224 | tf_op jit(solution)/shard_map/ppermute | solution.py:346
  45.0 0.0 collective-permute-done.7.refs_6_.refs_8_
  45.0 0.0 collective-permute-done.6.refs_3_
  45.0 1.3 %collective-permute-start.10 = (bf16[128,1024]{1,0:T(8,128)(2,1)S(1)}, bf16[128,1024]{1,0:T(8,128)(2,1)S(1)}, u32[]{:S(2)}, u32[]{:S(2)}) collective-permute-start(bf16[128,1024]{1,0:T(8,128)(2,1)S(1)} %collective-permute-done.6.refs_3_), channel_id=1, source_target_pairs={{4,0},{8,4},{12,8},{5,1},{9,5},{13,9},{6,2},{10,6},{14,10},{7,3},{... | collective-permute-start | bytes 786440 | tf_op jit(solution)/shard_map/ppermute | solution.py:19
  46.4 0.1 collective-permute-start.13
  46.4 1.6 %collective-permute-start.12 = (f32[16,128]{1,0:T(8,128)S(1)}, f32[16,128]{1,0:T(8,128)S(1)}, u32[]{:S(2)}, u32[]{:S(2)}) collective-permute-start(f32[16,128]{1,0:T(8,128)S(1)} %add_add_fusion.refs_8_), channel_id=1, source_target_pairs={{0,2},{1,3},{2,0},{3,1},{4,6},{5,7},{6,4},{7,5},{8,10},{9,11},{10,... | collective-permute-start | bytes 24584 | tf_op jit(solution)/shard_map/ppermute | solution.py:346
  48.0 0.3 collective-permute-start.11
  48.3 0.9 %shard_map.131 = (f32[128,1024]{1,0:T(8,128)S(1)}, f32[128,1024]{1,0:T(8,128)S(1)}) custom-call(f32[64,128]{1,0:T(8,128)S(1)} %get-tuple-element.38.refs_0_, f32[128,128]{1,0:T(8,128)S(1)} %get-tuple-element.56.refs_1_, bf16[128,1024]{1,0:T(8,128)(2,1)S(1)} %get-tuple-element.43.refs_3_.refs_5_.refs_2_, ...), custom_call_target="tpu_custom_call" | custom-call | flops 1000000 | bytes 100000 | tf_op jit(solution)/shard_map/pallas_call | solution.py:317
  49.2 0.8 %shard_map.132 = (f32[128,1024]{1,0:T(8,128)S(1)}, f32[128,1024]{1,0:T(8,128)S(1)}) custom-call(f32[64,128]{1,0:T(8,128)S(1)} %get-tuple-element.38.refs_0_, f32[128,128]{1,0:T(8,128)S(1)} %get-tuple-element.55.refs_1_, bf16[128,1024]{1,0:T(8,128)(2,1)S(1)} %collective-permute-done.2.refs_9_.refs_7_.refs_2_, ...), custom_call_target="tpu_custom_call" | custom-call | flops 1000000 | bytes 100000 | tf_op jit(solution)/shard_map/pallas_call | solution.py:317
  50.0 1.0 %shard_map.134 = bf16[128,1024]{1,0:T(8,128)(2,1)} custom-call(f32[128,1024]{1,0:T(8,128)S(1)} %get-tuple-element.67.refs_0_, bf16[128,1024]{1,0:T(8,128)(2,1)S(1)} %get-tuple-element.45.refs_7_.refs_1_, f32[1,1024]{1,0:T(1,128)S(1)} %bitcast.12, f32[128,1024]{1,0:T(8,128)S(1)} %get-tuple-element.60.refs_6_.refs_3_), custom_call_target="tpu_custom_call" | custom-call | flops 1000000 | bytes 100000 | tf_op jit(solution)/shard_map/pallas_call | solution.py:317
  51.0 0.0 collective-permute-done.13.refs_11_
  51.0 0.0 collective-permute-done.12.refs_10_
  51.0 0.0 collective-permute-done.11.refs_9_
  51.0 2.3 %collective-permute-done.10.refs_3_ = bf16[128,1024]{1,0:T(8,128)(2,1)S(1)} collective-permute-done((bf16[128,1024]{1,0:T(8,128)(2,1)S(1)}, bf16[128,1024]{1,0:T(8,128)(2,1)S(1)}, u32[]{:S(2)}, u32[]{:S(2)}) %collective-permute-start.10) | collective-permute-done | bytes 262176 | tf_op jit(solution)/shard_map/ppermute | solution.py:19
  53.3 1.6 %shard_map.133 = (bf16[128,1024]{1,0:T(8,128)(2,1)}, bf16[128,1024]{1,0:T(8,128)(2,1)}, f32[8,128]{1,0:T(8,128)}, f32[8,8]{1,0:T(8,128)}) custom-call(f32[64,128]{1,0:T(8,128)S(1)} %get-tuple-element.38.refs_0_, f32[128,128]{1,0:T(8,128)S(1)} %get-tuple-element.52.refs_1_, bf16[128,1024]{1,0:T(8,128)(2,1)S(1)} %collective-permute-done.5.refs_10_.refs_2_, ...), custom_call_target="tpu_custom_call" | custom-call | flops 1000000 | bytes 100000 | tf_op jit(solution)/shard_map/pallas_call | solution.py:317
  (1 shorter events, 0.0 us)
Async XLA Ops:
  0.6 23.8 %copy-start.1 = (f32[8,8]{1,0:T(8,128)S(1)}, f32[8,8]{1,0:T(8,128)}, u32[]{:S(2)}) copy-start(f32[8,8]{1,0:T(8,128)} %refs_1_.1) | copy-start | bytes 772
  0.6 11.4 %collective-permute-start.2 = (bf16[128,1024]{1,0:T(8,128)(2,1)}, bf16[128,1024]{1,0:T(8,128)(2,1)S(1)}, u32[]{:S(2)}, u32[]{:S(2)}) collective-permute-start(bf16[128,1024]{1,0:T(8,128)(2,1)} %bitcast.13), channel_id=1, source_target_pairs={{4,0},{8,4},{12,8},{5,1},{9,5},{13,9},{6,2},{10,6},{14,10},{7,3},{... | collective-permute-start | bytes 786440 | tf_op jit(solution)/shard_map/ppermute | solution.py:19
  1.9 12.6 %collective-permute-start = (bf16[128,1024]{1,0:T(8,128)(2,1)}, bf16[128,1024]{1,0:T(8,128)(2,1)S(1)}, u32[]{:S(2)}, u32[]{:S(2)}) collective-permute-start(bf16[128,1024]{1,0:T(8,128)(2,1)} %bitcast.15), channel_id=1, source_target_pairs={{0,4},{4,8},{8,12},{1,5},{5,9},{9,13},{2,6},{6,10},{10,14},{3,7},{... | collective-permute-start | bytes 786440 | tf_op jit(solution)/shard_map/ppermute | solution.py:19
  7.5 12.6 %collective-permute-start.1 = (bf16[128,1024]{1,0:T(8,128)(2,1)}, bf16[128,1024]{1,0:T(8,128)(2,1)S(1)}, u32[]{:S(2)}, u32[]{:S(2)}) collective-permute-start(bf16[128,1024]{1,0:T(8,128)(2,1)} %bitcast.17), channel_id=1, source_target_pairs={{0,4},{4,8},{8,12},{1,5},{5,9},{9,13},{2,6},{6,10},{10,14},{3,7},{... | collective-permute-start | bytes 786440 | tf_op jit(solution)/shard_map/ppermute | solution.py:19
  12.1 16.0 %collective-permute-start.5 = (bf16[128,1024]{1,0:T(8,128)(2,1)S(1)}, bf16[128,1024]{1,0:T(8,128)(2,1)S(1)}, u32[]{:S(2)}, u32[]{:S(2)}) collective-permute-start(bf16[128,1024]{1,0:T(8,128)(2,1)S(1)} %collective-permute-done.2.refs_9_.refs_7_.refs_2_), channel_id=1, source_target_pairs={{4,0},{8,4},{12,8},{5,1},{9,5},{13,9},{6,2},{10,6},{14,10},{7,3},{... | collective-permute-start | bytes 786440 | tf_op jit(solution)/shard_map/ppermute | solution.py:19
  14.5 13.6 %collective-permute-start.3 = (bf16[128,1024]{1,0:T(8,128)(2,1)S(1)}, bf16[128,1024]{1,0:T(8,128)(2,1)S(1)}, u32[]{:S(2)}, u32[]{:S(2)}) collective-permute-start(bf16[128,1024]{1,0:T(8,128)(2,1)S(1)} %collective-permute-done.refs_7_.refs_4_.refs_8_), channel_id=1, source_target_pairs={{0,4},{4,8},{8,12},{1,5},{5,9},{9,13},{2,6},{6,10},{10,14},{3,7},{... | collective-permute-start | bytes 786440 | tf_op jit(solution)/shard_map/ppermute | solution.py:19
  20.1 10.0 %collective-permute-start.4 = (bf16[128,1024]{1,0:T(8,128)(2,1)S(1)}, bf16[128,1024]{1,0:T(8,128)(2,1)S(1)}, u32[]{:S(2)}, u32[]{:S(2)}) collective-permute-start(bf16[128,1024]{1,0:T(8,128)(2,1)S(1)} %collective-permute-done.1.refs_8_.refs_5_.refs_11_), channel_id=1, source_target_pairs={{0,4},{4,8},{8,12},{1,5},{5,9},{9,13},{2,6},{6,10},{10,14},{3,7},{... | collective-permute-start | bytes 786440 | tf_op jit(solution)/shard_map/ppermute | solution.py:19
  24.4 0.7 %copy-start.2 = (s32[1,4]{1,0:T(1,128)S(1)}, s32[1,4]{1,0:T(1,128)}, u32[]{:S(2)}) copy-start(s32[1,4]{1,0:T(1,128)} %refs_0_.1) | copy-start | bytes 52
  28.1 2.0 %copy-start = (f32[1024]{0:T(1024)S(1)}, f32[1024]{0:T(1024)}, u32[]{:S(2)}) copy-start(f32[1024]{0:T(1024)} %param.15) | copy-start | bytes 12292
  31.1 14.0 %collective-permute-start.6 = (bf16[128,1024]{1,0:T(8,128)(2,1)S(1)}, bf16[128,1024]{1,0:T(8,128)(2,1)S(1)}, u32[]{:S(2)}, u32[]{:S(2)}) collective-permute-start(bf16[128,1024]{1,0:T(8,128)(2,1)S(1)} %get-tuple-element.47.refs_6_.refs_3_), channel_id=1, source_target_pairs={{4,0},{8,4},{12,8},{5,1},{9,5},{13,9},{6,2},{10,6},{14,10},{7,3},{... | collective-permute-start | bytes 786440 | tf_op jit(solution)/shard_map/ppermute | solution.py:19
  34.7 8.4 %collective-permute-start.9 = (f32[16,128]{1,0:T(8,128)S(1)}, f32[16,128]{1,0:T(8,128)S(1)}, u32[]{:S(2)}, u32[]{:S(2)}) collective-permute-start(f32[16,128]{1,0:T(8,128)S(1)} %get-tuple-element.62), channel_id=1, source_target_pairs={{0,12},{4,8},{8,4},{12,0},{1,13},{5,9},{9,5},{13,1},{2,14},{6,10},... | collective-permute-start | bytes 24584 | tf_op jit(solution)/shard_map/ppermute | solution.py:346
  40.5 4.5 %collective-permute-start.8 = (f32[16,128]{1,0:T(8,128)S(1)}, f32[16,128]{1,0:T(8,128)S(1)}, u32[]{:S(2)}, u32[]{:S(2)}) collective-permute-start(f32[16,128]{1,0:T(8,128)S(1)} %get-tuple-element.62), channel_id=1, source_target_pairs={{0,8},{4,12},{8,0},{12,4},{1,9},{5,13},{9,1},{13,5},{2,10},{6,14},... | collective-permute-start | bytes 24584 | tf_op jit(solution)/shard_map/ppermute | solution.py:346
  40.5 4.5 %collective-permute-start.7 = (f32[16,128]{1,0:T(8,128)S(1)}, f32[16,128]{1,0:T(8,128)S(1)}, u32[]{:S(2)}, u32[]{:S(2)}) collective-permute-start(f32[16,128]{1,0:T(8,128)S(1)} %get-tuple-element.62), channel_id=1, source_target_pairs={{0,4},{4,0},{8,12},{12,8},{1,5},{5,1},{9,13},{13,9},{2,6},{6,2},{1... | collective-permute-start | bytes 24584 | tf_op jit(solution)/shard_map/ppermute | solution.py:346
  45.0 8.3 %collective-permute-start.10 = (bf16[128,1024]{1,0:T(8,128)(2,1)S(1)}, bf16[128,1024]{1,0:T(8,128)(2,1)S(1)}, u32[]{:S(2)}, u32[]{:S(2)}) collective-permute-start(bf16[128,1024]{1,0:T(8,128)(2,1)S(1)} %collective-permute-done.6.refs_3_), channel_id=1, source_target_pairs={{4,0},{8,4},{12,8},{5,1},{9,5},{13,9},{6,2},{10,6},{14,10},{7,3},{... | collective-permute-start | bytes 786440 | tf_op jit(solution)/shard_map/ppermute | solution.py:19
  46.4 4.6 %collective-permute-start.13 = (f32[16,128]{1,0:T(8,128)S(1)}, f32[16,128]{1,0:T(8,128)S(1)}, u32[]{:S(2)}, u32[]{:S(2)}) collective-permute-start(f32[16,128]{1,0:T(8,128)S(1)} %add_add_fusion.refs_8_), channel_id=1, source_target_pairs={{0,3},{1,2},{2,1},{3,0},{4,7},{5,6},{6,5},{7,4},{8,11},{9,10},{10,... | collective-permute-start | bytes 24584 | tf_op jit(solution)/shard_map/ppermute | solution.py:346
  46.4 4.6 %collective-permute-start.12 = (f32[16,128]{1,0:T(8,128)S(1)}, f32[16,128]{1,0:T(8,128)S(1)}, u32[]{:S(2)}, u32[]{:S(2)}) collective-permute-start(f32[16,128]{1,0:T(8,128)S(1)} %add_add_fusion.refs_8_), channel_id=1, source_target_pairs={{0,2},{1,3},{2,0},{3,1},{4,6},{5,7},{6,4},{7,5},{8,10},{9,11},{10,... | collective-permute-start | bytes 24584 | tf_op jit(solution)/shard_map/ppermute | solution.py:346
  48.0 3.0 %collective-permute-start.11 = (f32[16,128]{1,0:T(8,128)S(1)}, f32[16,128]{1,0:T(8,128)S(1)}, u32[]{:S(2)}, u32[]{:S(2)}) collective-permute-start(f32[16,128]{1,0:T(8,128)S(1)} %add_add_fusion.refs_8_), channel_id=1, source_target_pairs={{0,1},{1,0},{2,3},{3,2},{4,5},{5,4},{6,7},{7,6},{8,9},{9,8},{10,11... | collective-permute-start | bytes 24584 | tf_op jit(solution)/shard_map/ppermute | solution.py:346

commit v6 on v5

--- a/solution.py
+++ b/solution.py
@@ -277,33 +277,31 @@
 
 
 def last_kernel(hops, heads, scaling, *refs):
-    pieces, outs, held = refs[8:-9], refs[-9:-5], refs[-5:-1]
-    written = refs[-1]
+    outs, held, written = refs[-5:-3], refs[-3:-1], refs[-1]
     copies = []
     group = 2
-
-    def write(at, cols):
-        source, target = held[at].at[:, cols], outs[at].at[:, cols]
-        copies.append(pltpu.make_async_copy(source, target, written.at[len(copies)]))
-        copies[-1].start()
 
     def store(head, cols, key_part, value_part):
         held[0][:, cols] = (key_part * scaling).astype(BF16)
         held[1][:, cols] = value_part.astype(BF16)
         if (head + 1) % group == 0:
             done = slice(cols.stop - group * (cols.stop - cols.start), cols.stop)
-            write(0, done)
-            write(1, done)
-
-    total = added_up([piece[...] for piece in pieces])
-    lines = held[2].shape[0]
-    held[2][...] = total[:lines]
-    held[3][...] = total[lines:, :heads]
-    for at in (2, 3):
-        write(at, slice(0, held[at].shape[1]))
-    add_key_grads(hops, heads, scaling, *refs[:6], refs[6:8], store)
+            for source, target in zip(held, outs):
+                at = written.at[len(copies)]
+                copies.append(pltpu.make_async_copy(source.at[:, done], target.at[:, done], at))
+                copies[-1].start()
+
+    add_key_grads(hops, heads, scaling, *refs[:6], refs[6:-5], store)
     for copy in copies:
         copy.wait()
+
+
+def sum_kernel(*refs):
+    gain_out, bias_out = refs[-2:]
+    total = added_up([piece[...] for piece in refs[:-2]])
+    lines = gain_out.shape[0]
+    gain_out[...] = total[:lines]
+    bias_out[...] = total[lines:, : bias_out.shape[1]]
 
 
 def on_device(kernel, outs, args, smem=(), ahead=(), far=(), far_outs=0, scratch=()):
@@ -377,14 +375,13 @@
         (),
         (user_lengths, rel_bias),
         far=inputs,
-        ahead=arrived,
         scratch=[pltpu.SemaphoreType.DMA((len(inputs),))],
     )
     masks, flipped = found[: reach + 1], found[reach + 1 : 2 * reach + 2]
     query, key, value, gate, grad, attention = found[2 * reach + 2 :]
 
-    later_queries = [query, *arrived[2:]]
-    keys, values = [key, *arrived[:1]], [value, *arrived[1:2]]
+    later_queries = [query, arrived[2]]
+    keys, values = [key, arrived[0]], [value, arrived[1]]
     for hops in range(1, reach):
         keys.append(passed_along(keys[-1], "ctx", 1))
         values.append(passed_along(values[-1], "ctx", 1))
@@ -400,7 +397,6 @@
         partial(norm_kernel, reach, heads, scaling),
         [wide, narrow, jax.ShapeDtypeStruct((1, features), F32)],
         (table, near, masks[-1], query, keys[-1], values[-1], attention, grad, gate, gain),
-        ahead=later_queries[reach:],
     )
 
     lanes = features // 8
@@ -408,16 +404,16 @@
         partial(backward_query_kernel, hop_list, heads, scaling),
         [narrow, jax.ShapeDtypeStruct((8 + levels, lanes), F32)],
         (table, near, *masks, query, attn_grad, *keys, *values, gain_part),
+        ahead=later_queries[reach:],
     )
     later_grads = [attn_grad, passed_along(attn_grad, "ctx", -1)]
     pieces = [sums]
-    first_pieces = None
-    for number, (axis, distances) in enumerate(rounds_of(("ctx", "dp")), 1):
+    for axis, distances in rounds_of(("dp",)):
         pieces = exchanged(added_up(pieces), axis, distances)
-        if number < reach:
-            arrived, *pieces = lax.optimization_barrier((later_grads[-1], *pieces))
-            later_grads.append(passed_along(arrived, "ctx", -1))
-        first_pieces = first_pieces or pieces[1:2]
+    first_pieces = pieces[1:2]
+    for hops in range(1, reach):
+        arrived, *pieces = lax.optimization_barrier((later_grads[-1], *pieces))
+        later_grads.append(passed_along(arrived, "ctx", -1))
     key_grads = ()
     for hops in range(reach):
         key_grads = on_device(
@@ -427,14 +423,14 @@
             ahead=first_pieces,
         )
     (gate_grad,) = on_device(gate_kernel, [narrow], (attention, grad, gain), ahead=key_grads[:1])
-    key_grad, value_grad, gain_grad, bias_grad = on_device(
+    (later_grads[-1], gate_grad, key_grads), *pieces = lax.optimization_barrier(
+        ((later_grads[-1], gate_grad, key_grads), *pieces)
+    )
+    for axis, distances in rounds_of(("ctx",)):
+        pieces = exchanged(added_up(pieces), axis, distances)
+    key_grad, value_grad = on_device(
         partial(last_kernel, reach, heads, scaling),
-        [
-            narrow,
-            narrow,
-            jax.ShapeDtypeStruct((8, lanes), F32),
-            jax.ShapeDtypeStruct((levels, heads), F32),
-        ],
+        [narrow, narrow],
         (
             table,
             flipped[reach],
@@ -443,12 +439,14 @@
             key,
             value,
             *key_grads,
-            *pieces,
         ),
-        far_outs=4,
-        scratch=[pltpu.VMEM((rows, features), BF16)] * 2
-        + [pltpu.VMEM((8, lanes), F32), pltpu.VMEM((levels, heads), F32)]
-        + [pltpu.SemaphoreType.DMA((heads + 2,))],
+        far_outs=2,
+        scratch=[pltpu.VMEM((rows, features), BF16)] * 2 + [pltpu.SemaphoreType.DMA((heads,))],
+    )
+    gain_grad, bias_grad = on_device(
+        sum_kernel,
+        [jax.ShapeDtypeStruct((8, lanes), F32), jax.ShapeDtypeStruct((levels, heads), F32)],
+        pieces,
     )
     return (
         query_grad[None],

time: 55.2 us -> 59 us (1.069)
  waiting for transfers between devices: 11.4 us -> 17.3 us
  starting transfers between devices: 31.4 us -> 28.7 us
  Pallas kernels: 10.6 us -> 11.2 us
    ppermute x8, waiting for transfers between devices: 7.39 us -> 12.1 us  [passed_along(): return lax.ppermute(array, axis, pairs)]
    ppermute x6, starting transfers between devices: 8.23 us -> 6.51 us  [exchanged(): lax.ppermute(array, axis, [(i, i ^ distance) for i in range(size)])]
    ppermute x6, waiting for transfers between devices: 3.99 us -> 5.21 us  [exchanged(): lax.ppermute(array, axis, [(i, i ^ distance) for i in range(size)])]
    ppermute x8, starting transfers between devices: 23.2 us -> 22.2 us  [passed_along(): return lax.ppermute(array, axis, pairs)]
    pallas_call x8 -> x9, Pallas kernels: 10.6 us -> 11.2 us  [on_device(): pl.pallas_call(body, out_shape=outs, in_specs=[pl.BlockSpec(memory_space=...]
  transfers between devices with their start and end apart: 14 -> 14, of which waited for: 7 -> 10; matrix products, arithmetic and copies ran while one was open for 0% -> 0% of each run, Pallas kernels for 15% -> 18%
where the time goes in v6:
time: 59 us; the launch traced here: 58.6 us
  starting transfers between devices  28.7 us (49%)
  waiting for transfers between devices  17.3 us (29%)
  Pallas kernels  11.2 us (19%)
  between operations  0.8 us (1%)
  local copies, waits for them, and re-layouts  0.65 us (1%)
    ppermute x8, starting transfers between devices, passed_along(): return lax.ppermute(array, axis, pairs)  22.2 us
    ppermute x8, waiting for transfers between devices, passed_along(): return lax.ppermute(array, axis, pairs)  12.1 us
    pallas_call x9, Pallas kernels, on_device(): pl.pallas_call(body, out_shape=outs, in_specs=[pl.BlockSpec(memory_space=...  11.2 us
    ppermute x6, starting transfers between devices, exchanged(): lax.ppermute(array, axis, [(i, i ^ distance) for i in range(size)])  6.51 us
    ppermute x6, waiting for transfers between devices, exchanged(): lax.ppermute(array, axis, [(i, i ^ distance) for i in range(size)])  5.21 us
  transfers between devices with their start and end apart: 14, of which 10 were waited for; matrix products, arithmetic and copies ran while one was open for 0% of the time, Pallas kernels for 18%

profile of v6, /device:TPU:0, one launch (start us, length us, event | category | flops | bytes accessed | tf_op | source)
XLA Modules:
  0.0 58.6 jit_solution(3145435773709111140)
XLA Ops:
  0.6 0.0 copy-start.1
  0.6 4.9 %collective-permute-start = (bf16[128,1024]{1,0:T(8,128)(2,1)}, bf16[128,1024]{1,0:T(8,128)(2,1)S(1)}, u32[]{:S(2)}, u32[]{:S(2)}) collective-permute-start(bf16[128,1024]{1,0:T(8,128)(2,1)} %bitcast.15), channel_id=1, source_target_pairs={{0,4},{4,8},{8,12},{1,5},{5,9},{9,13},{2,6},{6,10},{10,14},{3,7},{... | collective-permute-start | bytes 786440 | tf_op jit(solution)/shard_map/ppermute | solution.py:19
  5.6 3.5 %collective-permute-start.2 = (bf16[128,1024]{1,0:T(8,128)(2,1)}, bf16[128,1024]{1,0:T(8,128)(2,1)S(1)}, u32[]{:S(2)}, u32[]{:S(2)}) collective-permute-start(bf16[128,1024]{1,0:T(8,128)(2,1)} %bitcast.17), channel_id=1, source_target_pairs={{0,4},{4,8},{8,12},{1,5},{5,9},{9,13},{2,6},{6,10},{10,14},{3,7},{... | collective-permute-start | bytes 786440 | tf_op jit(solution)/shard_map/ppermute | solution.py:19
  9.1 1.3 %collective-permute-start.4 = (bf16[128,1024]{1,0:T(8,128)(2,1)}, bf16[128,1024]{1,0:T(8,128)(2,1)S(1)}, u32[]{:S(2)}, u32[]{:S(2)}) collective-permute-start(bf16[128,1024]{1,0:T(8,128)(2,1)} %bitcast.13), channel_id=1, source_target_pairs={{4,0},{8,4},{12,8},{5,1},{9,5},{13,9},{6,2},{10,6},{14,10},{7,3},{... | collective-permute-start | bytes 786440 | tf_op jit(solution)/shard_map/ppermute | solution.py:19
  10.4 2.2 %collective-permute-done.refs_4_.refs_8_ = bf16[128,1024]{1,0:T(8,128)(2,1)S(1)} collective-permute-done((bf16[128,1024]{1,0:T(8,128)(2,1)}, bf16[128,1024]{1,0:T(8,128)(2,1)S(1)}, u32[]{:S(2)}, u32[]{:S(2)}) %collective-permute-start) | collective-permute-done | bytes 262176 | tf_op jit(solution)/shard_map/ppermute | solution.py:19
  12.6 4.3 %collective-permute-start.1 = (bf16[128,1024]{1,0:T(8,128)(2,1)S(1)}, bf16[128,1024]{1,0:T(8,128)(2,1)S(1)}, u32[]{:S(2)}, u32[]{:S(2)}) collective-permute-start(bf16[128,1024]{1,0:T(8,128)(2,1)S(1)} %collective-permute-done.refs_4_.refs_8_), channel_id=1, source_target_pairs={{0,4},{4,8},{8,12},{1,5},{5,9},{9,13},{2,6},{6,10},{10,14},{3,7},{... | collective-permute-start | bytes 786440 | tf_op jit(solution)/shard_map/ppermute | solution.py:19
  16.9 1.3 %collective-permute-done.2.refs_5_.refs_11_ = bf16[128,1024]{1,0:T(8,128)(2,1)S(1)} collective-permute-done((bf16[128,1024]{1,0:T(8,128)(2,1)}, bf16[128,1024]{1,0:T(8,128)(2,1)S(1)}, u32[]{:S(2)}, u32[]{:S(2)}) %collective-permute-start.2) | collective-permute-done | bytes 262176 | tf_op jit(solution)/shard_map/ppermute | solution.py:19
  18.2 4.3 %collective-permute-start.3 = (bf16[128,1024]{1,0:T(8,128)(2,1)S(1)}, bf16[128,1024]{1,0:T(8,128)(2,1)S(1)}, u32[]{:S(2)}, u32[]{:S(2)}) collective-permute-start(bf16[128,1024]{1,0:T(8,128)(2,1)S(1)} %collective-permute-done.2.refs_5_.refs_11_), channel_id=1, source_target_pairs={{0,4},{4,8},{8,12},{1,5},{5,9},{9,13},{2,6},{6,10},{10,14},{3,7},{... | collective-permute-start | bytes 786440 | tf_op jit(solution)/shard_map/ppermute | solution.py:19
  22.5 0.0 collective-permute-done.4.refs_7_.refs_2_
  22.5 1.3 %collective-permute-start.5 = (bf16[128,1024]{1,0:T(8,128)(2,1)S(1)}, bf16[128,1024]{1,0:T(8,128)(2,1)S(1)}, u32[]{:S(2)}, u32[]{:S(2)}) collective-permute-start(bf16[128,1024]{1,0:T(8,128)(2,1)S(1)} %collective-permute-done.4.refs_7_.refs_2_), channel_id=1, source_target_pairs={{4,0},{8,4},{12,8},{5,1},{9,5},{13,9},{6,2},{10,6},{14,10},{7,3},{... | collective-permute-start | bytes 786440 | tf_op jit(solution)/shard_map/ppermute | solution.py:19
  23.8 0.0 copy-start.2
  23.8 0.0 copy-done.1
  23.8 0.6 %copy-done.2 = s32[1,4]{1,0:T(1,128)S(1)} copy-done((s32[1,4]{1,0:T(1,128)S(1)}, s32[1,4]{1,0:T(1,128)}, u32[]{:S(2)}) %copy-start.2) | copy-done | bytes 40
  24.5 2.5 %shard_map.127 = (f32[64,128]{1,0:T(8,128)S(1)}, f32[1024,128]{1,0:T(8,128)S(1)}, f32[128,128]{1,0:T(8,128)S(1)}, f32[128,128]{1,0:T(8,128)S(1)}, f32[128,128]{1...) custom-call(s32[1,4]{1,0:T(1,128)S(1)} %copy-done.2, ...), custom_call_target="tpu_custom_call" | custom-call | flops 1000000 | bytes 100000 | tf_op jit(solution)/shard_map/pallas_call | solution.py:315
  26.9 0.6 shard_map.128.refs_6_
  27.5 0.0 copy-start
  27.5 0.0 collective-permute-done.1.refs_4_.refs_9_
  27.5 0.7 %collective-permute-done.3.refs_5_.refs_12_ = bf16[128,1024]{1,0:T(8,128)(2,1)S(1)} collective-permute-done((bf16[128,1024]{1,0:T(8,128)(2,1)S(1)}, bf16[128,1024]{1,0:T(8,128)(2,1)S(1)}, u32[]{:S(2)}, u32[]{:S(2)}) %collective-permute-start.3) | collective-permute-done | bytes 262176 | tf_op jit(solution)/shard_map/ppermute | solution.py:19
  28.2 0.0 copy-done
  28.2 1.0 %shard_map.129 = (f32[128,1024]{1,0:T(8,128)S(1)}, bf16[128,1024]{1,0:T(8,128)(2,1)S(1)}, f32[1,1024]{1,0:T(1,128)S(1)}) custom-call(f32[64,128]{1,0:T(8,128)S(1)} %get-tuple-element.46.refs_0_, f32[1024,128]{1,0:T(8,128)S(1)} %get-tuple-element.47.refs_1_, f32[128,128]{1,0:T(8,128)S(1)} %get-tuple-element.50.refs_2_.refs_4_, ...), custom_call_target="tpu_custom_call" | custom-call | flops 1000000 | bytes 100000 | tf_op jit(solution)/shard_map/pallas_call | solution.py:315
  29.2 1.3 %collective-permute-start.6 = (bf16[128,1024]{1,0:T(8,128)(2,1)S(1)}, bf16[128,1024]{1,0:T(8,128)(2,1)S(1)}, u32[]{:S(2)}, u32[]{:S(2)}) collective-permute-start(bf16[128,1024]{1,0:T(8,128)(2,1)S(1)} %get-tuple-element.55.refs_6_.refs_3_), channel_id=1, source_target_pairs={{4,0},{8,4},{12,8},{5,1},{9,5},{13,9},{6,2},{10,6},{14,10},{7,3},{... | collective-permute-start | bytes 786440 | tf_op jit(solution)/shard_map/ppermute | solution.py:19
  30.5 0.3 collective-permute-done.5.refs_14_.refs_2_
  30.8 2.4 %shard_map.130 = (bf16[128,1024]{1,0:T(8,128)(2,1)}, f32[16,128]{1,0:T(8,128)S(1)}) custom-call(f32[64,128]{1,0:T(8,128)S(1)} %get-tuple-element.46.refs_0_, f32[1024,128]{1,0:T(8,128)S(1)} %get-tuple-element.47.refs_1_, f32[128,128]{1,0:T(8,128)S(1)} %get-tuple-element.48.refs_2_, f32[128,128]{1,0:T(8,128)S(1)} %get-tuple-element.49.refs_2_.refs_3_, ...), custom_call_target="tpu_custom_call" | custom-call | flops 1000000 | bytes 100000 | tf_op jit(solution)/shard_map/pallas_call | solution.py:315
  33.1 0.0 collective-permute-start.7
  33.1 1.5 %collective-permute-start.8 = (f32[16,128]{1,0:T(8,128)S(1)}, f32[16,128]{1,0:T(8,128)S(1)}, u32[]{:S(2)}, u32[]{:S(2)}) collective-permute-start(f32[16,128]{1,0:T(8,128)S(1)} %get-tuple-element.80), channel_id=1, source_target_pairs={{0,2},{1,3},{2,0},{3,1},{4,6},{5,7},{6,4},{7,5},{8,10},{9,11},{10,... | collective-permute-start | bytes 24584 | tf_op jit(solution)/shard_map/ppermute | solution.py:344
  34.6 0.4 collective-permute-start.9
  35.0 0.0 collective-permute-done.7.refs_6_.refs_8_
  35.0 1.8 %collective-permute-done.8 = f32[16,128]{1,0:T(8,128)S(1)} collective-permute-done((f32[16,128]{1,0:T(8,128)S(1)}, f32[16,128]{1,0:T(8,128)S(1)}, u32[]{:S(2)}, u32[]{:S(2)}) %collective-permute-start.8) | collective-permute-done | bytes 8224 | tf_op jit(solution)/shard_map/ppermute | solution.py:344
  36.8 0.9 %collective-permute-done.9 = f32[16,128]{1,0:T(8,128)S(1)} collective-permute-done((f32[16,128]{1,0:T(8,128)S(1)}, f32[16,128]{1,0:T(8,128)S(1)}, u32[]{:S(2)}, u32[]{:S(2)}) %collective-permute-start.9) | collective-permute-done | bytes 8224 | tf_op jit(solution)/shard_map/ppermute | solution.py:344
  37.7 1.3 %collective-permute-done.6.refs_3_ = bf16[128,1024]{1,0:T(8,128)(2,1)S(1)} collective-permute-done((bf16[128,1024]{1,0:T(8,128)(2,1)S(1)}, bf16[128,1024]{1,0:T(8,128)(2,1)S(1)}, u32[]{:S(2)}, u32[]{:S(2)}) %collective-permute-start.6) | collective-permute-done | bytes 262176 | tf_op jit(solution)/shard_map/ppermute | solution.py:19
  39.0 1.3 %collective-permute-start.10 = (bf16[128,1024]{1,0:T(8,128)(2,1)S(1)}, bf16[128,1024]{1,0:T(8,128)(2,1)S(1)}, u32[]{:S(2)}, u32[]{:S(2)}) collective-permute-start(bf16[128,1024]{1,0:T(8,128)(2,1)S(1)} %collective-permute-done.6.refs_3_), channel_id=1, source_target_pairs={{4,0},{8,4},{12,8},{5,1},{9,5},{13,9},{6,2},{10,6},{14,10},{7,3},{... | collective-permute-start | bytes 786440 | tf_op jit(solution)/shard_map/ppermute | solution.py:19
  40.3 0.9 %shard_map.131 = (f32[128,1024]{1,0:T(8,128)S(1)}, f32[128,1024]{1,0:T(8,128)S(1)}) custom-call(f32[64,128]{1,0:T(8,128)S(1)} %get-tuple-element.46.refs_0_, f32[128,128]{1,0:T(8,128)S(1)} %get-tuple-element.65.refs_1_, bf16[128,1024]{1,0:T(8,128)(2,1)S(1)} %get-tuple-element.51.refs_3_.refs_5_.refs_2_, ...), custom_call_target="tpu_custom_call" | custom-call | flops 1000000 | bytes 100000 | tf_op jit(solution)/shard_map/pallas_call | solution.py:315
  41.2 0.8 %shard_map.132 = (f32[128,1024]{1,0:T(8,128)S(1)}, f32[128,1024]{1,0:T(8,128)S(1)}) custom-call(f32[64,128]{1,0:T(8,128)S(1)} %get-tuple-element.46.refs_0_, f32[128,128]{1,0:T(8,128)S(1)} %get-tuple-element.64.refs_1_, bf16[128,1024]{1,0:T(8,128)(2,1)S(1)} %collective-permute-done.4.refs_7_.refs_2_, bf16[128,1024]{1,0:T(8,128)(2,1)S(1)} %collective-permute-done.6.refs_3_, ...), custom_call_target="tpu_custom_call" | custom-call | flops 1000000 | bytes 100000 | tf_op jit(solution)/shard_map/pallas_call | solution.py:315
  42.0 1.0 %shard_map.133 = bf16[128,1024]{1,0:T(8,128)(2,1)} custom-call(f32[128,1024]{1,0:T(8,128)S(1)} %get-tuple-element.63.refs_0_, bf16[128,1024]{1,0:T(8,128)(2,1)S(1)} %get-tuple-element.53.refs_7_.refs_1_, f32[1,1024]{1,0:T(1,128)S(1)} %bitcast.12, f32[128,1024]{1,0:T(8,128)S(1)} %get-tuple-element.75.refs_3_.refs_6_), custom_call_target="tpu_custom_call" | custom-call | flops 1000000 | bytes 100000 | tf_op jit(solution)/shard_map/pallas_call | solution.py:315
  43.0 6.3 %collective-permute-done.10.refs_3_ = bf16[128,1024]{1,0:T(8,128)(2,1)S(1)} collective-permute-done((bf16[128,1024]{1,0:T(8,128)(2,1)S(1)}, bf16[128,1024]{1,0:T(8,128)(2,1)S(1)}, u32[]{:S(2)}, u32[]{:S(2)}) %collective-permute-start.10) | collective-permute-done | bytes 262176 | tf_op jit(solution)/shard_map/ppermute | solution.py:19
  49.3 2.0 %collective-permute-start.11 = (f32[16,128]{1,0:T(8,128)S(1)}, f32[16,128]{1,0:T(8,128)S(1)}, u32[]{:S(2)}, u32[]{:S(2)}) collective-permute-start(f32[16,128]{1,0:T(8,128)S(1)} %add_add_fusion.refs_0_), channel_id=1, source_target_pairs={{0,4},{4,0},{8,12},{12,8},{1,5},{5,1},{9,13},{13,9},{2,6},{6,2},{1... | collective-permute-start | bytes 24584 | tf_op jit(solution)/shard_map/ppermute | solution.py:344
  51.3 1.2 %collective-permute-start.12 = (f32[16,128]{1,0:T(8,128)S(1)}, f32[16,128]{1,0:T(8,128)S(1)}, u32[]{:S(2)}, u32[]{:S(2)}) collective-permute-start(f32[16,128]{1,0:T(8,128)S(1)} %add_add_fusion.refs_0_), channel_id=1, source_target_pairs={{0,8},{4,12},{8,0},{12,4},{1,9},{5,13},{9,1},{13,5},{2,10},{6,14},... | collective-permute-start | bytes 24584 | tf_op jit(solution)/shard_map/ppermute | solution.py:344
  52.5 1.4 %collective-permute-start.13 = (f32[16,128]{1,0:T(8,128)S(1)}, f32[16,128]{1,0:T(8,128)S(1)}, u32[]{:S(2)}, u32[]{:S(2)}) collective-permute-start(f32[16,128]{1,0:T(8,128)S(1)} %add_add_fusion.refs_0_), channel_id=1, source_target_pairs={{0,12},{4,8},{8,4},{12,0},{1,13},{5,9},{9,5},{13,1},{2,14},{6,10},... | collective-permute-start | bytes 24584 | tf_op jit(solution)/shard_map/ppermute | solution.py:344
  53.9 1.5 %shard_map.134 = (bf16[128,1024]{1,0:T(8,128)(2,1)}, bf16[128,1024]{1,0:T(8,128)(2,1)}) custom-call(f32[64,128]{1,0:T(8,128)S(1)} %get-tuple-element.46.refs_0_, f32[128,128]{1,0:T(8,128)S(1)} %get-tuple-element.60.refs_1_, bf16[128,1024]{1,0:T(8,128)(2,1)S(1)} %collective-permute-done.5.refs_14_.refs_2_, ...), custom_call_target="tpu_custom_call" | custom-call | flops 1000000 | bytes 100000 | tf_op jit(solution)/shard_map/pallas_call | solution.py:315
  55.5 0.0 collective-permute-done.11.refs_1_
  55.5 0.4 collective-permute-done.12.refs_2_
  55.8 2.1 %collective-permute-done.13.refs_3_ = f32[16,128]{1,0:T(8,128)S(1)} collective-permute-done((f32[16,128]{1,0:T(8,128)S(1)}, f32[16,128]{1,0:T(8,128)S(1)}, u32[]{:S(2)}, u32[]{:S(2)}) %collective-permute-start.13) | collective-permute-done | bytes 8224 | tf_op jit(solution)/shard_map/ppermute | solution.py:344
  58.0 0.6 %shard_map.135 = (f32[8,128]{1,0:T(8,128)}, f32[8,8]{1,0:T(8,128)}) custom-call(f32[16,128]{1,0:T(8,128)S(1)} %add_add_fusion.refs_0_, f32[16,128]{1,0:T(8,128)S(1)} %collective-permute-done.11.refs_1_, f32[16,128]{1,0:T(8,128)S(1)} %collective-permute-done.12.refs_2_, f32[16,128]{1,0:T(8,128)S(1)} %collective-permute-done.13.refs_3_), custom_call_target="tpu_custom_call" | custom-call | flops 1000000 | bytes 100000 | tf_op jit(solution)/shard_map/pallas_call | solution.py:315
  (1 shorter events, 0.0 us)
Async XLA Ops:
  0.6 23.2 %copy-start.1 = (f32[8,8]{1,0:T(8,128)S(1)}, f32[8,8]{1,0:T(8,128)}, u32[]{:S(2)}) copy-start(f32[8,8]{1,0:T(8,128)} %refs_1_.1) | copy-start | bytes 772
  0.6 11.9 %collective-permute-start = (bf16[128,1024]{1,0:T(8,128)(2,1)}, bf16[128,1024]{1,0:T(8,128)(2,1)S(1)}, u32[]{:S(2)}, u32[]{:S(2)}) collective-permute-start(bf16[128,1024]{1,0:T(8,128)(2,1)} %bitcast.15), channel_id=1, source_target_pairs={{0,4},{4,8},{8,12},{1,5},{5,9},{9,13},{2,6},{6,10},{10,14},{3,7},{... | collective-permute-start | bytes 786440 | tf_op jit(solution)/shard_map/ppermute | solution.py:19
  5.6 12.6 %collective-permute-start.2 = (bf16[128,1024]{1,0:T(8,128)(2,1)}, bf16[128,1024]{1,0:T(8,128)(2,1)S(1)}, u32[]{:S(2)}, u32[]{:S(2)}) collective-permute-start(bf16[128,1024]{1,0:T(8,128)(2,1)} %bitcast.17), channel_id=1, source_target_pairs={{0,4},{4,8},{8,12},{1,5},{5,9},{9,13},{2,6},{6,10},{10,14},{3,7},{... | collective-permute-start | bytes 786440 | tf_op jit(solution)/shard_map/ppermute | solution.py:19
  9.1 13.4 %collective-permute-start.4 = (bf16[128,1024]{1,0:T(8,128)(2,1)}, bf16[128,1024]{1,0:T(8,128)(2,1)S(1)}, u32[]{:S(2)}, u32[]{:S(2)}) collective-permute-start(bf16[128,1024]{1,0:T(8,128)(2,1)} %bitcast.13), channel_id=1, source_target_pairs={{4,0},{8,4},{12,8},{5,1},{9,5},{13,9},{6,2},{10,6},{14,10},{7,3},{... | collective-permute-start | bytes 786440 | tf_op jit(solution)/shard_map/ppermute | solution.py:19
  12.6 14.9 %collective-permute-start.1 = (bf16[128,1024]{1,0:T(8,128)(2,1)S(1)}, bf16[128,1024]{1,0:T(8,128)(2,1)S(1)}, u32[]{:S(2)}, u32[]{:S(2)}) collective-permute-start(bf16[128,1024]{1,0:T(8,128)(2,1)S(1)} %collective-permute-done.refs_4_.refs_8_), channel_id=1, source_target_pairs={{0,4},{4,8},{8,12},{1,5},{5,9},{9,13},{2,6},{6,10},{10,14},{3,7},{... | collective-permute-start | bytes 786440 | tf_op jit(solution)/shard_map/ppermute | solution.py:19
  18.2 10.0 %collective-permute-start.3 = (bf16[128,1024]{1,0:T(8,128)(2,1)S(1)}, bf16[128,1024]{1,0:T(8,128)(2,1)S(1)}, u32[]{:S(2)}, u32[]{:S(2)}) collective-permute-start(bf16[128,1024]{1,0:T(8,128)(2,1)S(1)} %collective-permute-done.2.refs_5_.refs_11_), channel_id=1, source_target_pairs={{0,4},{4,8},{8,12},{1,5},{5,9},{9,13},{2,6},{6,10},{10,14},{3,7},{... | collective-permute-start | bytes 786440 | tf_op jit(solution)/shard_map/ppermute | solution.py:19
  22.5 8.3 %collective-permute-start.5 = (bf16[128,1024]{1,0:T(8,128)(2,1)S(1)}, bf16[128,1024]{1,0:T(8,128)(2,1)S(1)}, u32[]{:S(2)}, u32[]{:S(2)}) collective-permute-start(bf16[128,1024]{1,0:T(8,128)(2,1)S(1)} %collective-permute-done.4.refs_7_.refs_2_), channel_id=1, source_target_pairs={{4,0},{8,4},{12,8},{5,1},{9,5},{13,9},{6,2},{10,6},{14,10},{7,3},{... | collective-permute-start | bytes 786440 | tf_op jit(solution)/shard_map/ppermute | solution.py:19
  23.8 0.7 %copy-start.2 = (s32[1,4]{1,0:T(1,128)S(1)}, s32[1,4]{1,0:T(1,128)}, u32[]{:S(2)}) copy-start(s32[1,4]{1,0:T(1,128)} %refs_0_.1) | copy-start | bytes 52
  27.5 0.7 %copy-start = (f32[1024]{0:T(1024)S(1)}, f32[1024]{0:T(1024)}, u32[]{:S(2)}) copy-start(f32[1024]{0:T(1024)} %param.15) | copy-start | bytes 12292
  29.2 9.8 %collective-permute-start.6 = (bf16[128,1024]{1,0:T(8,128)(2,1)S(1)}, bf16[128,1024]{1,0:T(8,128)(2,1)S(1)}, u32[]{:S(2)}, u32[]{:S(2)}) collective-permute-start(bf16[128,1024]{1,0:T(8,128)(2,1)S(1)} %get-tuple-element.55.refs_6_.refs_3_), channel_id=1, source_target_pairs={{4,0},{8,4},{12,8},{5,1},{9,5},{13,9},{6,2},{10,6},{14,10},{7,3},{... | collective-permute-start | bytes 786440 | tf_op jit(solution)/shard_map/ppermute | solution.py:19
  33.1 1.9 %collective-permute-start.7 = (f32[16,128]{1,0:T(8,128)S(1)}, f32[16,128]{1,0:T(8,128)S(1)}, u32[]{:S(2)}, u32[]{:S(2)}) collective-permute-start(f32[16,128]{1,0:T(8,128)S(1)} %get-tuple-element.80), channel_id=1, source_target_pairs={{0,1},{1,0},{2,3},{3,2},{4,5},{5,4},{6,7},{7,6},{8,9},{9,8},{10,11... | collective-permute-start | bytes 24584 | tf_op jit(solution)/shard_map/ppermute | solution.py:344
  33.1 3.7 %collective-permute-start.8 = (f32[16,128]{1,0:T(8,128)S(1)}, f32[16,128]{1,0:T(8,128)S(1)}, u32[]{:S(2)}, u32[]{:S(2)}) collective-permute-start(f32[16,128]{1,0:T(8,128)S(1)} %get-tuple-element.80), channel_id=1, source_target_pairs={{0,2},{1,3},{2,0},{3,1},{4,6},{5,7},{6,4},{7,5},{8,10},{9,11},{10,... | collective-permute-start | bytes 24584 | tf_op jit(solution)/shard_map/ppermute | solution.py:344
  34.6 3.1 %collective-permute-start.9 = (f32[16,128]{1,0:T(8,128)S(1)}, f32[16,128]{1,0:T(8,128)S(1)}, u32[]{:S(2)}, u32[]{:S(2)}) collective-permute-start(f32[16,128]{1,0:T(8,128)S(1)} %get-tuple-element.80), channel_id=1, source_target_pairs={{0,3},{1,2},{2,1},{3,0},{4,7},{5,6},{6,5},{7,4},{8,11},{9,10},{10,... | collective-permute-start | bytes 24584 | tf_op jit(solution)/shard_map/ppermute | solution.py:344
  39.0 10.3 %collective-permute-start.10 = (bf16[128,1024]{1,0:T(8,128)(2,1)S(1)}, bf16[128,1024]{1,0:T(8,128)(2,1)S(1)}, u32[]{:S(2)}, u32[]{:S(2)}) collective-permute-start(bf16[128,1024]{1,0:T(8,128)(2,1)S(1)} %collective-permute-done.6.refs_3_), channel_id=1, source_target_pairs={{4,0},{8,4},{12,8},{5,1},{9,5},{13,9},{6,2},{10,6},{14,10},{7,3},{... | collective-permute-start | bytes 786440 | tf_op jit(solution)/shard_map/ppermute | solution.py:19
  49.3 6.2 %collective-permute-start.11 = (f32[16,128]{1,0:T(8,128)S(1)}, f32[16,128]{1,0:T(8,128)S(1)}, u32[]{:S(2)}, u32[]{:S(2)}) collective-permute-start(f32[16,128]{1,0:T(8,128)S(1)} %add_add_fusion.refs_0_), channel_id=1, source_target_pairs={{0,4},{4,0},{8,12},{12,8},{1,5},{5,1},{9,13},{13,9},{2,6},{6,2},{1... | collective-permute-start | bytes 24584 | tf_op jit(solution)/shard_map/ppermute | solution.py:344
  51.3 4.5 %collective-permute-start.12 = (f32[16,128]{1,0:T(8,128)S(1)}, f32[16,128]{1,0:T(8,128)S(1)}, u32[]{:S(2)}, u32[]{:S(2)}) collective-permute-start(f32[16,128]{1,0:T(8,128)S(1)} %add_add_fusion.refs_0_), channel_id=1, source_target_pairs={{0,8},{4,12},{8,0},{12,4},{1,9},{5,13},{9,1},{13,5},{2,10},{6,14},... | collective-permute-start | bytes 24584 | tf_op jit(solution)/shard_map/ppermute | solution.py:344
  52.5 5.4 %collective-permute-start.13 = (f32[16,128]{1,0:T(8,128)S(1)}, f32[16,128]{1,0:T(8,128)S(1)}, u32[]{:S(2)}, u32[]{:S(2)}) collective-permute-start(f32[16,128]{1,0:T(8,128)S(1)} %add_add_fusion.refs_0_), channel_id=1, source_target_pairs={{0,12},{4,8},{8,4},{12,0},{1,13},{5,9},{9,5},{13,1},{2,14},{6,10},... | collective-permute-start | bytes 24584 | tf_op jit(solution)/shard_map/ppermute | solution.py:344

commit v7 on v6

--- a/solution.py
+++ b/solution.py
@@ -296,9 +296,8 @@
         copy.wait()
 
 
-def sum_kernel(*refs):
-    gain_out, bias_out = refs[-2:]
-    total = added_up([piece[...] for piece in refs[:-2]])
+def sum_kernel(pieces, gain_out, bias_out):
+    total = jnp.sum(pieces[...], axis=0)
     lines = gain_out.shape[0]
     gain_out[...] = total[:lines]
     bias_out[...] = total[lines:, : bias_out.shape[1]]
@@ -324,32 +323,6 @@
         compiler_params=pltpu.CompilerParams(vmem_limit_bytes=VMEM_LIMIT),
         cost_estimate=pl.CostEstimate(flops=1000000, bytes_accessed=100000, transcendentals=0),
     )(*smem, *far, *args, *ahead)
-
-
-def rounds_of(axes):
-    rounds = []
-    for axis in axes:
-        size = lax.axis_size(axis)
-        step = 1
-        while step < size:
-            radix = 4 if size // step >= 4 else 2
-            rounds.append((axis, [step * at for at in range(1, radix)]))
-            step = radix * step
-    return rounds
-
-
-def exchanged(array, axis, distances):
-    size = lax.axis_size(axis)
-    return [array] + [
-        lax.ppermute(array, axis, [(i, i ^ distance) for i in range(size)])
-        for distance in distances
-    ]
-
-
-def added_up(pieces):
-    while len(pieces) > 1:
-        pieces = [left + right for left, right in zip(pieces[::2], pieces[1::2])]
-    return pieces[0]
 
 
 def local(queries, key_rows, value_rows, update_gate, out_grad, user_lengths, rel_bias, norm_gain):
@@ -407,12 +380,8 @@
         ahead=later_queries[reach:],
     )
     later_grads = [attn_grad, passed_along(attn_grad, "ctx", -1)]
-    pieces = [sums]
-    for axis, distances in rounds_of(("dp",)):
-        pieces = exchanged(added_up(pieces), axis, distances)
-    first_pieces = pieces[1:2]
     for hops in range(1, reach):
-        arrived, *pieces = lax.optimization_barrier((later_grads[-1], *pieces))
+        arrived, sums = lax.optimization_barrier((later_grads[-1], sums))
         later_grads.append(passed_along(arrived, "ctx", -1))
     key_grads = ()
     for hops in range(reach):
@@ -420,14 +389,13 @@
             partial(backward_key_kernel, hops, heads, scaling),
             [wide] * 2,
             (table, flipped[hops], later_queries[hops], later_grads[hops], key, value, *key_grads),
-            ahead=first_pieces,
         )
     (gate_grad,) = on_device(gate_kernel, [narrow], (attention, grad, gain), ahead=key_grads[:1])
-    (later_grads[-1], gate_grad, key_grads), *pieces = lax.optimization_barrier(
-        ((later_grads[-1], gate_grad, key_grads), *pieces)
-    )
-    for axis, distances in rounds_of(("ctx",)):
-        pieces = exchanged(added_up(pieces), axis, distances)
+    sums, key_grads, gate_grad = lax.optimization_barrier((sums, key_grads, gate_grad))
+    for axes in [("ctx", "dp")] if lax.axis_size(("ctx", "dp")) <= 16 else ["ctx", "dp"]:
+        size = lax.axis_size(axes)
+        pieces = lax.all_to_all(jnp.broadcast_to(sums, (size, *sums.shape)), axes, 0, 0)
+        sums = jnp.sum(pieces, axis=0)
     key_grad, value_grad = on_device(
         partial(last_kernel, reach, heads, scaling),
         [narrow, narrow],
@@ -440,13 +408,14 @@
             value,
             *key_grads,
         ),
+        ahead=[pieces],
         far_outs=2,
         scratch=[pltpu.VMEM((rows, features), BF16)] * 2 + [pltpu.SemaphoreType.DMA((heads,))],
     )
     gain_grad, bias_grad = on_device(
         sum_kernel,
         [jax.ShapeDtypeStruct((8, lanes), F32), jax.ShapeDtypeStruct((levels, heads), F32)],
-        pieces,
+        [pieces],
     )
     return (
         query_grad[None],

time: 59 us -> 60.8 us (1.031)
  blocking collectives: 0 us -> 14.7 us
  starting transfers between devices: 28.7 us -> 22.2 us
  waiting for transfers between devices: 17.3 us -> 10.9 us
    all_to_all x0 -> x1, blocking collectives: none -> 14.7 us  [local(): lax.all_to_all(jnp.broadcast_to(sums, (size, *sums.shape)), axes, 0, 0)]
    ppermute x6 -> x0, starting transfers between devices: 6.51 us -> none  [exchanged(): lax.ppermute(array, axis, [(i, i ^ distance) for i in range(size)])]
    ppermute x6 -> x0, waiting for transfers between devices: 5.21 us -> none  [exchanged(): lax.ppermute(array, axis, [(i, i ^ distance) for i in range(size)])]
    ppermute x8, waiting for transfers between devices: 12.1 us -> 10.9 us  [passed_along(): return lax.ppermute(array, axis, pairs)]
  transfers between devices with their start and end apart: 14 -> 8, of which waited for: 10 -> 5; matrix products, arithmetic and copies ran while one was open for 0% -> 0% of each run, Pallas kernels for 18% -> 16%
where the time goes in v7:
time: 60.8 us; the launch traced here: 60.4 us
  starting transfers between devices  22.2 us (37%)
  blocking collectives  14.7 us (24%)
  Pallas kernels  11.2 us (18%)
  waiting for transfers between devices  10.9 us (18%)
  between operations  0.78 us (1%)
  local copies, waits for them, and re-layouts  0.66 us (1%)
    ppermute x8, starting transfers between devices, passed_along(): return lax.ppermute(array, axis, pairs)  22.2 us
    all_to_all x1, blocking collectives, local(): lax.all_to_all(jnp.broadcast_to(sums, (size, *sums.shape)), axes, 0, 0)  14.7 us
    pallas_call x9, Pallas kernels, on_device(): pl.pallas_call(body, out_shape=outs, in_specs=[pl.BlockSpec(memory_space=...  11.2 us
    ppermute x8, waiting for transfers between devices, passed_along(): return lax.ppermute(array, axis, pairs)  10.9 us
  transfers between devices with their start and end apart: 8, of which 5 were waited for; matrix products, arithmetic and copies ran while one was open for 0% of the time, Pallas kernels for 16%

profile of v7, /device:TPU:0, one launch (start us, length us, event | category | flops | bytes accessed | tf_op | source)
XLA Modules:
  0.0 60.4 jit_solution(15200764527520276323)
XLA Ops:
  0.6 0.0 copy-start.1
  0.6 4.9 %collective-permute-start = (bf16[128,1024]{1,0:T(8,128)(2,1)}, bf16[128,1024]{1,0:T(8,128)(2,1)S(1)}, u32[]{:S(2)}, u32[]{:S(2)}) collective-permute-start(bf16[128,1024]{1,0:T(8,128)(2,1)} %bitcast.13), channel_id=1, source_target_pairs={{0,4},{4,8},{8,12},{1,5},{5,9},{9,13},{2,6},{6,10},{10,14},{3,7},{... | collective-permute-start | bytes 786440 | tf_op jit(solution)/shard_map/ppermute | solution.py:19
  5.6 3.5 %collective-permute-start.2 = (bf16[128,1024]{1,0:T(8,128)(2,1)}, bf16[128,1024]{1,0:T(8,128)(2,1)S(1)}, u32[]{:S(2)}, u32[]{:S(2)}) collective-permute-start(bf16[128,1024]{1,0:T(8,128)(2,1)} %bitcast.15), channel_id=1, source_target_pairs={{0,4},{4,8},{8,12},{1,5},{5,9},{9,13},{2,6},{6,10},{10,14},{3,7},{... | collective-permute-start | bytes 786440 | tf_op jit(solution)/shard_map/ppermute | solution.py:19
  9.1 1.3 %collective-permute-start.4 = (bf16[128,1024]{1,0:T(8,128)(2,1)}, bf16[128,1024]{1,0:T(8,128)(2,1)S(1)}, u32[]{:S(2)}, u32[]{:S(2)}) collective-permute-start(bf16[128,1024]{1,0:T(8,128)(2,1)} %bitcast.19), channel_id=1, source_target_pairs={{4,0},{8,4},{12,8},{5,1},{9,5},{13,9},{6,2},{10,6},{14,10},{7,3},{... | collective-permute-start | bytes 786440 | tf_op jit(solution)/shard_map/ppermute | solution.py:19
  10.4 2.2 %collective-permute-done.refs_4_.refs_8_ = bf16[128,1024]{1,0:T(8,128)(2,1)S(1)} collective-permute-done((bf16[128,1024]{1,0:T(8,128)(2,1)}, bf16[128,1024]{1,0:T(8,128)(2,1)S(1)}, u32[]{:S(2)}, u32[]{:S(2)}) %collective-permute-start) | collective-permute-done | bytes 262176 | tf_op jit(solution)/shard_map/ppermute | solution.py:19
  12.6 4.3 %collective-permute-start.1 = (bf16[128,1024]{1,0:T(8,128)(2,1)S(1)}, bf16[128,1024]{1,0:T(8,128)(2,1)S(1)}, u32[]{:S(2)}, u32[]{:S(2)}) collective-permute-start(bf16[128,1024]{1,0:T(8,128)(2,1)S(1)} %collective-permute-done.refs_4_.refs_8_), channel_id=1, source_target_pairs={{0,4},{4,8},{8,12},{1,5},{5,9},{9,13},{2,6},{6,10},{10,14},{3,7},{... | collective-permute-start | bytes 786440 | tf_op jit(solution)/shard_map/ppermute | solution.py:19
  16.9 1.3 %collective-permute-done.2.refs_5_.refs_11_ = bf16[128,1024]{1,0:T(8,128)(2,1)S(1)} collective-permute-done((bf16[128,1024]{1,0:T(8,128)(2,1)}, bf16[128,1024]{1,0:T(8,128)(2,1)S(1)}, u32[]{:S(2)}, u32[]{:S(2)}) %collective-permute-start.2) | collective-permute-done | bytes 262176 | tf_op jit(solution)/shard_map/ppermute | solution.py:19
  18.2 4.3 %collective-permute-start.3 = (bf16[128,1024]{1,0:T(8,128)(2,1)S(1)}, bf16[128,1024]{1,0:T(8,128)(2,1)S(1)}, u32[]{:S(2)}, u32[]{:S(2)}) collective-permute-start(bf16[128,1024]{1,0:T(8,128)(2,1)S(1)} %collective-permute-done.2.refs_5_.refs_11_), channel_id=1, source_target_pairs={{0,4},{4,8},{8,12},{1,5},{5,9},{9,13},{2,6},{6,10},{10,14},{3,7},{... | collective-permute-start | bytes 786440 | tf_op jit(solution)/shard_map/ppermute | solution.py:19
  22.5 0.0 copy-start.2
  22.5 0.0 copy-done.1
  22.5 0.6 %copy-done.2 = s32[1,4]{1,0:T(1,128)S(1)} copy-done((s32[1,4]{1,0:T(1,128)S(1)}, s32[1,4]{1,0:T(1,128)}, u32[]{:S(2)}) %copy-start.2) | copy-done | bytes 40
  23.2 2.5 %shard_map.127 = (f32[64,128]{1,0:T(8,128)S(1)}, f32[1024,128]{1,0:T(8,128)S(1)}, f32[128,128]{1,0:T(8,128)S(1)}, f32[128,128]{1,0:T(8,128)S(1)}, f32[128,128]{1...) custom-call(s32[1,4]{1,0:T(1,128)S(1)} %copy-done.2, ...), custom_call_target="tpu_custom_call" | custom-call | flops 1000000 | bytes 100000 | tf_op jit(solution)/shard_map/pallas_call | solution.py:314
  25.6 0.0 collective-permute-done.4.refs_7_.refs_2_
  25.6 1.3 %collective-permute-start.5 = (bf16[128,1024]{1,0:T(8,128)(2,1)S(1)}, bf16[128,1024]{1,0:T(8,128)(2,1)S(1)}, u32[]{:S(2)}, u32[]{:S(2)}) collective-permute-start(bf16[128,1024]{1,0:T(8,128)(2,1)S(1)} %collective-permute-done.4.refs_7_.refs_2_), channel_id=1, source_target_pairs={{4,0},{8,4},{12,8},{5,1},{9,5},{13,9},{6,2},{10,6},{14,10},{7,3},{... | collective-permute-start | bytes 786440 | tf_op jit(solution)/shard_map/ppermute | solution.py:19
  26.9 0.6 shard_map.128.refs_6_
  27.5 0.0 copy-start
  27.5 0.0 collective-permute-done.1.refs_4_.refs_9_
  27.5 0.7 %collective-permute-done.3.refs_5_.refs_12_ = bf16[128,1024]{1,0:T(8,128)(2,1)S(1)} collective-permute-done((bf16[128,1024]{1,0:T(8,128)(2,1)S(1)}, bf16[128,1024]{1,0:T(8,128)(2,1)S(1)}, u32[]{:S(2)}, u32[]{:S(2)}) %collective-permute-start.3) | collective-permute-done | bytes 262176 | tf_op jit(solution)/shard_map/ppermute | solution.py:19
  28.2 0.0 copy-done
  28.2 1.0 %shard_map.129 = (f32[128,1024]{1,0:T(8,128)S(1)}, bf16[128,1024]{1,0:T(8,128)(2,1)S(1)}, f32[1,1024]{1,0:T(1,128)S(1)}) custom-call(f32[64,128]{1,0:T(8,128)S(1)} %get-tuple-element.39.refs_0_, f32[1024,128]{1,0:T(8,128)S(1)} %get-tuple-element.40.refs_1_, f32[128,128]{1,0:T(8,128)S(1)} %get-tuple-element.43.refs_2_.refs_4_, ...), custom_call_target="tpu_custom_call" | custom-call | flops 1000000 | bytes 100000 | tf_op jit(solution)/shard_map/pallas_call | solution.py:314
  29.2 1.3 %collective-permute-start.6 = (bf16[128,1024]{1,0:T(8,128)(2,1)S(1)}, bf16[128,1024]{1,0:T(8,128)(2,1)S(1)}, u32[]{:S(2)}, u32[]{:S(2)}) collective-permute-start(bf16[128,1024]{1,0:T(8,128)(2,1)S(1)} %get-tuple-element.48.refs_6_.refs_3_), channel_id=1, source_target_pairs={{4,0},{8,4},{12,8},{5,1},{9,5},{13,9},{6,2},{10,6},{14,10},{7,3},{... | collective-permute-start | bytes 786440 | tf_op jit(solution)/shard_map/ppermute | solution.py:19
  30.5 3.9 %collective-permute-done.5.refs_14_.refs_2_ = bf16[128,1024]{1,0:T(8,128)(2,1)S(1)} collective-permute-done((bf16[128,1024]{1,0:T(8,128)(2,1)S(1)}, bf16[128,1024]{1,0:T(8,128)(2,1)S(1)}, u32[]{:S(2)}, u32[]{:S(2)}) %collective-permute-start.5) | collective-permute-done | bytes 262176 | tf_op jit(solution)/shard_map/ppermute | solution.py:19
  34.4 2.3 %shard_map.130 = (bf16[128,1024]{1,0:T(8,128)(2,1)}, f32[16,128]{1,0:T(8,128)S(1)}) custom-call(f32[64,128]{1,0:T(8,128)S(1)} %get-tuple-element.39.refs_0_, f32[1024,128]{1,0:T(8,128)S(1)} %get-tuple-element.40.refs_1_, f32[128,128]{1,0:T(8,128)S(1)} %get-tuple-element.41.refs_2_, f32[128,128]{1,0:T(8,128)S(1)} %get-tuple-element.42.refs_2_.refs_3_, ...), custom_call_target="tpu_custom_call" | custom-call | flops 1000000 | bytes 100000 | tf_op jit(solution)/shard_map/pallas_call | solution.py:314
  36.7 2.8 %collective-permute-done.6.refs_3_ = bf16[128,1024]{1,0:T(8,128)(2,1)S(1)} collective-permute-done((bf16[128,1024]{1,0:T(8,128)(2,1)S(1)}, bf16[128,1024]{1,0:T(8,128)(2,1)S(1)}, u32[]{:S(2)}, u32[]{:S(2)}) %collective-permute-start.6) | collective-permute-done | bytes 262176 | tf_op jit(solution)/shard_map/ppermute | solution.py:19
  39.5 1.3 %collective-permute-start.7 = (bf16[128,1024]{1,0:T(8,128)(2,1)S(1)}, bf16[128,1024]{1,0:T(8,128)(2,1)S(1)}, u32[]{:S(2)}, u32[]{:S(2)}) collective-permute-start(bf16[128,1024]{1,0:T(8,128)(2,1)S(1)} %collective-permute-done.6.refs_3_), channel_id=1, source_target_pairs={{4,0},{8,4},{12,8},{5,1},{9,5},{13,9},{6,2},{10,6},{14,10},{7,3},{... | collective-permute-start | bytes 786440 | tf_op jit(solution)/shard_map/ppermute | solution.py:19
  40.8 0.9 %shard_map.131 = (f32[128,1024]{1,0:T(8,128)S(1)}, f32[128,1024]{1,0:T(8,128)S(1)}) custom-call(f32[64,128]{1,0:T(8,128)S(1)} %get-tuple-element.39.refs_0_, f32[128,128]{1,0:T(8,128)S(1)} %get-tuple-element.58.refs_1_, bf16[128,1024]{1,0:T(8,128)(2,1)S(1)} %get-tuple-element.44.refs_3_.refs_5_.refs_2_, ...), custom_call_target="tpu_custom_call" | custom-call | flops 1000000 | bytes 100000 | tf_op jit(solution)/shard_map/pallas_call | solution.py:314
  41.7 0.8 %shard_map.132 = (f32[128,1024]{1,0:T(8,128)S(1)}, f32[128,1024]{1,0:T(8,128)S(1)}) custom-call(f32[64,128]{1,0:T(8,128)S(1)} %get-tuple-element.39.refs_0_, f32[128,128]{1,0:T(8,128)S(1)} %get-tuple-element.57.refs_1_, bf16[128,1024]{1,0:T(8,128)(2,1)S(1)} %collective-permute-done.4.refs_7_.refs_2_, bf16[128,1024]{1,0:T(8,128)(2,1)S(1)} %collective-permute-done.6.refs_3_, ...), custom_call_target="tpu_custom_call" | custom-call | flops 1000000 | bytes 100000 | tf_op jit(solution)/shard_map/pallas_call | solution.py:314
  42.5 1.0 %shard_map.133 = bf16[128,1024]{1,0:T(8,128)(2,1)} custom-call(f32[128,1024]{1,0:T(8,128)S(1)} %get-tuple-element.63.refs_0_, bf16[128,1024]{1,0:T(8,128)(2,1)S(1)} %get-tuple-element.46.refs_7_.refs_1_, f32[1,1024]{1,0:T(1,128)S(1)} %bitcast.12, f32[128,1024]{1,0:T(8,128)S(1)} %get-tuple-element.64.refs_3_.refs_6_), custom_call_target="tpu_custom_call" | custom-call | flops 1000000 | bytes 100000 | tf_op jit(solution)/shard_map/pallas_call | solution.py:314
  43.5 14.7 %all_to_all.5.refs_8_.refs_0_ = f32[16,16,128]{2,1,0:T(8,128)S(1)} all-to-all(f32[16,16,128]{2,1,0:T(8,128)S(1)} %broadcast_in_dim.20), channel_id=1, replica_groups=mesh['groups'=2,'ctx'=4,'dp'=4] {'ctx','dp'}, dimensions={0} | all-to-all | bytes 262144 | tf_op jit(solution)/shard_map/all_to_all | solution.py:397
  58.2 0.6 %shard_map.135 = (f32[8,128]{1,0:T(8,128)}, f32[8,8]{1,0:T(8,128)}) custom-call(f32[16,16,128]{2,1,0:T(8,128)S(1)} %all_to_all.5.refs_8_.refs_0_), custom_call_target="tpu_custom_call" | custom-call | flops 1000000 | bytes 100000 | tf_op jit(solution)/shard_map/pallas_call | solution.py:314
  58.8 0.0 collective-permute-done.7.refs_3_
  58.8 1.5 %shard_map.134 = (bf16[128,1024]{1,0:T(8,128)(2,1)}, bf16[128,1024]{1,0:T(8,128)(2,1)}) custom-call(f32[64,128]{1,0:T(8,128)S(1)} %get-tuple-element.39.refs_0_, f32[128,128]{1,0:T(8,128)S(1)} %get-tuple-element.53.refs_1_, bf16[128,1024]{1,0:T(8,128)(2,1)S(1)} %collective-permute-done.5.refs_14_.refs_2_, ...), custom_call_target="tpu_custom_call" | custom-call | flops 1000000 | bytes 100000 | tf_op jit(solution)/shard_map/pallas_call | solution.py:314
  (1 shorter events, 0.0 us)
Async XLA Ops:
  0.6 21.9 %copy-start.1 = (f32[8,8]{1,0:T(8,128)S(1)}, f32[8,8]{1,0:T(8,128)}, u32[]{:S(2)}) copy-start(f32[8,8]{1,0:T(8,128)} %refs_1_.1) | copy-start | bytes 772
  0.6 11.9 %collective-permute-start = (bf16[128,1024]{1,0:T(8,128)(2,1)}, bf16[128,1024]{1,0:T(8,128)(2,1)S(1)}, u32[]{:S(2)}, u32[]{:S(2)}) collective-permute-start(bf16[128,1024]{1,0:T(8,128)(2,1)} %bitcast.13), channel_id=1, source_target_pairs={{0,4},{4,8},{8,12},{1,5},{5,9},{9,13},{2,6},{6,10},{10,14},{3,7},{... | collective-permute-start | bytes 786440 | tf_op jit(solution)/shard_map/ppermute | solution.py:19
  5.6 12.6 %collective-permute-start.2 = (bf16[128,1024]{1,0:T(8,128)(2,1)}, bf16[128,1024]{1,0:T(8,128)(2,1)S(1)}, u32[]{:S(2)}, u32[]{:S(2)}) collective-permute-start(bf16[128,1024]{1,0:T(8,128)(2,1)} %bitcast.15), channel_id=1, source_target_pairs={{0,4},{4,8},{8,12},{1,5},{5,9},{9,13},{2,6},{6,10},{10,14},{3,7},{... | collective-permute-start | bytes 786440 | tf_op jit(solution)/shard_map/ppermute | solution.py:19
  9.1 16.5 %collective-permute-start.4 = (bf16[128,1024]{1,0:T(8,128)(2,1)}, bf16[128,1024]{1,0:T(8,128)(2,1)S(1)}, u32[]{:S(2)}, u32[]{:S(2)}) collective-permute-start(bf16[128,1024]{1,0:T(8,128)(2,1)} %bitcast.19), channel_id=1, source_target_pairs={{4,0},{8,4},{12,8},{5,1},{9,5},{13,9},{6,2},{10,6},{14,10},{7,3},{... | collective-permute-start | bytes 786440 | tf_op jit(solution)/shard_map/ppermute | solution.py:19
  12.6 14.9 %collective-permute-start.1 = (bf16[128,1024]{1,0:T(8,128)(2,1)S(1)}, bf16[128,1024]{1,0:T(8,128)(2,1)S(1)}, u32[]{:S(2)}, u32[]{:S(2)}) collective-permute-start(bf16[128,1024]{1,0:T(8,128)(2,1)S(1)} %collective-permute-done.refs_4_.refs_8_), channel_id=1, source_target_pairs={{0,4},{4,8},{8,12},{1,5},{5,9},{9,13},{2,6},{6,10},{10,14},{3,7},{... | collective-permute-start | bytes 786440 | tf_op jit(solution)/shard_map/ppermute | solution.py:19
  18.2 10.0 %collective-permute-start.3 = (bf16[128,1024]{1,0:T(8,128)(2,1)S(1)}, bf16[128,1024]{1,0:T(8,128)(2,1)S(1)}, u32[]{:S(2)}, u32[]{:S(2)}) collective-permute-start(bf16[128,1024]{1,0:T(8,128)(2,1)S(1)} %collective-permute-done.2.refs_5_.refs_11_), channel_id=1, source_target_pairs={{0,4},{4,8},{8,12},{1,5},{5,9},{9,13},{2,6},{6,10},{10,14},{3,7},{... | collective-permute-start | bytes 786440 | tf_op jit(solution)/shard_map/ppermute | solution.py:19
  22.5 0.7 %copy-start.2 = (s32[1,4]{1,0:T(1,128)S(1)}, s32[1,4]{1,0:T(1,128)}, u32[]{:S(2)}) copy-start(s32[1,4]{1,0:T(1,128)} %refs_0_.1) | copy-start | bytes 52
  25.6 8.7 %collective-permute-start.5 = (bf16[128,1024]{1,0:T(8,128)(2,1)S(1)}, bf16[128,1024]{1,0:T(8,128)(2,1)S(1)}, u32[]{:S(2)}, u32[]{:S(2)}) collective-permute-start(bf16[128,1024]{1,0:T(8,128)(2,1)S(1)} %collective-permute-done.4.refs_7_.refs_2_), channel_id=1, source_target_pairs={{4,0},{8,4},{12,8},{5,1},{9,5},{13,9},{6,2},{10,6},{14,10},{7,3},{... | collective-permute-start | bytes 786440 | tf_op jit(solution)/shard_map/ppermute | solution.py:19
  27.5 0.7 %copy-start = (f32[1024]{0:T(1024)S(1)}, f32[1024]{0:T(1024)}, u32[]{:S(2)}) copy-start(f32[1024]{0:T(1024)} %param.15) | copy-start | bytes 12292
  29.2 10.3 %collective-permute-start.6 = (bf16[128,1024]{1,0:T(8,128)(2,1)S(1)}, bf16[128,1024]{1,0:T(8,128)(2,1)S(1)}, u32[]{:S(2)}, u32[]{:S(2)}) collective-permute-start(bf16[128,1024]{1,0:T(8,128)(2,1)S(1)} %get-tuple-element.48.refs_6_.refs_3_), channel_id=1, source_target_pairs={{4,0},{8,4},{12,8},{5,1},{9,5},{13,9},{6,2},{10,6},{14,10},{7,3},{... | collective-permute-start | bytes 786440 | tf_op jit(solution)/shard_map/ppermute | solution.py:19
  39.5 19.3 %collective-permute-start.7 = (bf16[128,1024]{1,0:T(8,128)(2,1)S(1)}, bf16[128,1024]{1,0:T(8,128)(2,1)S(1)}, u32[]{:S(2)}, u32[]{:S(2)}) collective-permute-start(bf16[128,1024]{1,0:T(8,128)(2,1)S(1)} %collective-permute-done.6.refs_3_), channel_id=1, source_target_pairs={{4,0},{8,4},{12,8},{5,1},{9,5},{13,9},{6,2},{10,6},{14,10},{7,3},{... | collective-permute-start | bytes 786440 | tf_op jit(solution)/shard_map/ppermute | solution.py:19

commit v8 on v7

--- a/solution.py
+++ b/solution.py
@@ -9,6 +9,7 @@
 
 EPSILON = 1e-05
 VMEM_LIMIT = 24 * 1024 * 1024
+LONG = 4 * 10**9
 F32 = jnp.float32
 BF16 = jnp.bfloat16
 
@@ -178,15 +179,6 @@
     gain_grad[...] = jnp.sum(gain_sum, axis=0, keepdims=True)
 
 
-def gate_kernel(attention, out_grad, gain, gate_grad):
-    step = 16
-    gain_row = gain[...]
-    for low in range(0, attention.shape[0], step):
-        span = slice(low, low + step)
-        normed, _ = normed_rows(attention[span, :])
-        gate_grad[span, :] = (out_grad[span, :].astype(F32) * normed * gain_row).astype(BF16)
-
-
 def backward_query_kernel(hop_list, heads, scaling, *refs):
     count = len(hop_list)
     table, near, masks, refs = refs[0], refs[1], refs[2 : 2 + count], refs[2 + count :]
@@ -266,14 +258,37 @@
     in_stages(heads, scores, differentiate)
 
 
-def backward_key_kernel(hops, heads, scaling, *refs):
-    key_out, value_out = refs[-2:]
-
+def into(key_out, value_out):
     def store(head, cols, key_part, value_part):
         key_out[:, cols] = key_part
         value_out[:, cols] = value_part
 
-    add_key_grads(hops, heads, scaling, *refs[:6], refs[6:-2], store)
+    return store
+
+
+def own_key_kernel(heads, scaling, *refs):
+    pieces, (key_out, value_out, shared) = refs[6:-3], refs[-3:]
+    shared[...] = added_up([piece[...] for piece in pieces])
+    add_key_grads(0, heads, scaling, *refs[:6], (), into(key_out, value_out))
+
+
+def next_key_kernel(hops, heads, scaling, *refs):
+    add_key_grads(hops, heads, scaling, *refs[:6], refs[6:8], into(*refs[8:]))
+
+
+def gate_and_key_kernel(hops, heads, scaling, *refs):
+    attention, out_grad, gain = refs[8:11]
+    gate_out, key_out, value_out, held, written = refs[11:]
+    step = 16
+    gain_row = gain[...]
+    for low in range(0, attention.shape[0], step):
+        span = slice(low, low + step)
+        normed, _ = normed_rows(attention[span, :])
+        held[span, :] = (out_grad[span, :].astype(F32) * normed * gain_row).astype(BF16)
+    copy = pltpu.make_async_copy(held, gate_out, written)
+    copy.start()
+    add_key_grads(hops, heads, scaling, *refs[:6], refs[6:8], into(key_out, value_out))
+    copy.wait()
 
 
 def last_kernel(hops, heads, scaling, *refs):
@@ -296,14 +311,15 @@
         copy.wait()
 
 
-def sum_kernel(pieces, gain_out, bias_out):
-    total = jnp.sum(pieces[...], axis=0)
+def sum_kernel(*refs):
+    gain_out, bias_out = refs[-2:]
+    total = added_up([piece[...] for piece in refs[:-2]])
     lines = gain_out.shape[0]
     gain_out[...] = total[:lines]
     bias_out[...] = total[lines:, : bias_out.shape[1]]
 
 
-def on_device(kernel, outs, args, smem=(), ahead=(), far=(), far_outs=0, scratch=()):
+def on_device(kernel, outs, args, smem=(), ahead=(), far=(), far_outs=0, scratch=(), flops=1000000):
     count = len(smem) + len(far) + len(args)
     far = [pltpu.with_memory_space_constraint(array, pltpu.HBM) for array in far]
 
@@ -321,8 +337,35 @@
         out_specs=[anywhere] * far_outs + [vmem] * (len(outs) - far_outs),
         scratch_shapes=scratch,
         compiler_params=pltpu.CompilerParams(vmem_limit_bytes=VMEM_LIMIT),
-        cost_estimate=pl.CostEstimate(flops=1000000, bytes_accessed=100000, transcendentals=0),
+        cost_estimate=pl.CostEstimate(flops=flops, bytes_accessed=100000, transcendentals=0),
     )(*smem, *far, *args, *ahead)
+
+
+def added_up(pieces):
+    while len(pieces) > 1:
+        pieces = [left + right for left, right in zip(pieces[::2], pieces[1::2])]
+    return pieces[0]
+
+
+def exchanged(array, axis):
+    size = lax.axis_size(axis)
+    return [array] + [
+        lax.ppermute(array, axis, [(i, i ^ distance) for i in range(size)])
+        for distance in range(1, size)
+    ]
+
+
+def spread(array, axis, helpers):
+    size, count = lax.axis_size(axis), lax.axis_size(helpers)
+    found = []
+    for low in range(0, size, count):
+        pairs = [
+            (i * count + m, (i ^ (low + m)) * count + m)
+            for i in range(size)
+            for m in range(min(count, size - low))
+        ]
+        found.append(lax.ppermute(array, (axis, helpers), pairs))
+    return found
 
 
 def local(queries, key_rows, value_rows, update_gate, out_grad, user_lengths, rel_bias, norm_gain):
@@ -380,42 +423,49 @@
         ahead=later_queries[reach:],
     )
     later_grads = [attn_grad, passed_along(attn_grad, "ctx", -1)]
+    sums = added_up(exchanged(sums, "dp"))
+
+    def key_operands(hops):
+        later = (later_queries[hops], later_grads[hops])
+        return (table, flipped[hops], *later, key, value)
+
+    *key_grads, shared = on_device(
+        partial(own_key_kernel, heads, scaling),
+        [wide, wide, jax.ShapeDtypeStruct(sums.shape, F32)],
+        (*key_operands(0), *spread(sums, "ctx", "dp")),
+        flops=LONG,
+    )
+    pieces = exchanged(shared, "dp")
     for hops in range(1, reach):
-        arrived, sums = lax.optimization_barrier((later_grads[-1], sums))
+        arrived, sums = lax.optimization_barrier((later_grads[hops], sums))
         later_grads.append(passed_along(arrived, "ctx", -1))
-    key_grads = ()
-    for hops in range(reach):
-        key_grads = on_device(
-            partial(backward_key_kernel, hops, heads, scaling),
-            [wide] * 2,
-            (table, flipped[hops], later_queries[hops], later_grads[hops], key, value, *key_grads),
-        )
-    (gate_grad,) = on_device(gate_kernel, [narrow], (attention, grad, gain), ahead=key_grads[:1])
-    sums, key_grads, gate_grad = lax.optimization_barrier((sums, key_grads, gate_grad))
-    for axes in [("ctx", "dp")] if lax.axis_size(("ctx", "dp")) <= 16 else ["ctx", "dp"]:
-        size = lax.axis_size(axes)
-        pieces = lax.all_to_all(jnp.broadcast_to(sums, (size, *sums.shape)), axes, 0, 0)
-        sums = jnp.sum(pieces, axis=0)
+        if hops == 1:
+            gate_grad, *key_grads = on_device(
+                partial(gate_and_key_kernel, hops, heads, scaling),
+                [narrow, wide, wide],
+                (*key_operands(hops), *key_grads, attention, grad, gain),
+                ahead=[shared],
+                far_outs=1,
+                scratch=[pltpu.VMEM((rows, features), BF16), pltpu.SemaphoreType.DMA(())],
+            )
+        else:
+            key_grads = on_device(
+                partial(next_key_kernel, hops, heads, scaling),
+                [wide] * 2,
+                (*key_operands(hops), *key_grads),
+            )
     key_grad, value_grad = on_device(
         partial(last_kernel, reach, heads, scaling),
         [narrow, narrow],
-        (
-            table,
-            flipped[reach],
-            later_queries[reach],
-            later_grads[reach],
-            key,
-            value,
-            *key_grads,
-        ),
-        ahead=[pieces],
+        (*key_operands(reach), *key_grads),
         far_outs=2,
         scratch=[pltpu.VMEM((rows, features), BF16)] * 2 + [pltpu.SemaphoreType.DMA((heads,))],
     )
     gain_grad, bias_grad = on_device(
         sum_kernel,
         [jax.ShapeDtypeStruct((8, lanes), F32), jax.ShapeDtypeStruct((levels, heads), F32)],
-        [pieces],
+        pieces,
+        ahead=key_grads[:1],
     )
     return (
         query_grad[None],

time: 60.8 us -> 54.9 us (0.903)
  the two profiles are of different devices: /device:TPU:0 before, /device:TPU:3 now
where the time goes in v8:
time: 54.9 us; the launch traced here: 54.5 us
  starting transfers between devices  32 us (58%)
  Pallas kernels  11.1 us (20%)
  waiting for transfers between devices  9.85 us (18%)
  between operations  0.85 us (2%)
  local copies, waits for them, and re-layouts  0.65 us (1%)
    ppermute x8, starting transfers between devices, passed_along(): return lax.ppermute(array, axis, pairs)  19.6 us
    pallas_call x8, Pallas kernels, on_device(): pl.pallas_call(body, out_shape=outs, in_specs=[pl.BlockSpec(memory_space=...  11.1 us
    ppermute x8, waiting for transfers between devices, passed_along(): return lax.ppermute(array, axis, pairs)  7.8 us
    ppermute x1, starting transfers between devices, spread(): found.append(lax.ppermute(array, (axis, helpers), pairs))  6.8 us
    ppermute x6, starting transfers between devices, exchanged(): lax.ppermute(array, axis, [(i, i ^ distance) for i in range(size)])  5.64 us
    ppermute x6, waiting for transfers between devices, exchanged(): lax.ppermute(array, axis, [(i, i ^ distance) for i in range(size)])  2.05 us
  transfers between devices with their start and end apart: 15, of which 7 were waited for; matrix products, arithmetic and copies ran while one was open for 0% of the time, Pallas kernels for 18%

profile of v8, /device:TPU:3, one launch (start us, length us, event | category | flops | bytes accessed | tf_op | source)
XLA Modules:
  0.0 54.5 jit_solution(12184710958184534783)
XLA Ops:
  0.6 0.0 copy-start.1
  0.6 3.2 %collective-permute-start = (bf16[128,1024]{1,0:T(8,128)(2,1)}, bf16[128,1024]{1,0:T(8,128)(2,1)S(1)}, u32[]{:S(2)}, u32[]{:S(2)}) collective-permute-start(bf16[128,1024]{1,0:T(8,128)(2,1)} %bitcast.15), channel_id=1, source_target_pairs={{0,4},{4,8},{8,12},{1,5},{5,9},{9,13},{2,6},{6,10},{10,14},{3,7},{... | collective-permute-start | bytes 786440 | tf_op jit(solution)/shard_map/ppermute | solution.py:20
  3.9 3.2 %collective-permute-start.2 = (bf16[128,1024]{1,0:T(8,128)(2,1)}, bf16[128,1024]{1,0:T(8,128)(2,1)S(1)}, u32[]{:S(2)}, u32[]{:S(2)}) collective-permute-start(bf16[128,1024]{1,0:T(8,128)(2,1)} %bitcast.17), channel_id=1, source_target_pairs={{0,4},{4,8},{8,12},{1,5},{5,9},{9,13},{2,6},{6,10},{10,14},{3,7},{... | collective-permute-start | bytes 786440 | tf_op jit(solution)/shard_map/ppermute | solution.py:20
  7.1 1.3 %collective-permute-start.4 = (bf16[128,1024]{1,0:T(8,128)(2,1)}, bf16[128,1024]{1,0:T(8,128)(2,1)S(1)}, u32[]{:S(2)}, u32[]{:S(2)}) collective-permute-start(bf16[128,1024]{1,0:T(8,128)(2,1)} %bitcast.13), channel_id=1, source_target_pairs={{4,0},{8,4},{12,8},{5,1},{9,5},{13,9},{6,2},{10,6},{14,10},{7,3},{... | collective-permute-start | bytes 786440 | tf_op jit(solution)/shard_map/ppermute | solution.py:20
  8.4 0.7 %collective-permute-done.refs_4_.refs_8_ = bf16[128,1024]{1,0:T(8,128)(2,1)S(1)} collective-permute-done((bf16[128,1024]{1,0:T(8,128)(2,1)}, bf16[128,1024]{1,0:T(8,128)(2,1)S(1)}, u32[]{:S(2)}, u32[]{:S(2)}) %collective-permute-start) | collective-permute-done | bytes 262176 | tf_op jit(solution)/shard_map/ppermute | solution.py:20
  9.1 4.0 %collective-permute-start.1 = (bf16[128,1024]{1,0:T(8,128)(2,1)S(1)}, bf16[128,1024]{1,0:T(8,128)(2,1)S(1)}, u32[]{:S(2)}, u32[]{:S(2)}) collective-permute-start(bf16[128,1024]{1,0:T(8,128)(2,1)S(1)} %collective-permute-done.refs_4_.refs_8_), channel_id=1, source_target_pairs={{0,4},{4,8},{8,12},{1,5},{5,9},{9,13},{2,6},{6,10},{10,14},{3,7},{... | collective-permute-start | bytes 786440 | tf_op jit(solution)/shard_map/ppermute | solution.py:20
  13.1 1.6 %collective-permute-done.2.refs_5_.refs_11_ = bf16[128,1024]{1,0:T(8,128)(2,1)S(1)} collective-permute-done((bf16[128,1024]{1,0:T(8,128)(2,1)}, bf16[128,1024]{1,0:T(8,128)(2,1)S(1)}, u32[]{:S(2)}, u32[]{:S(2)}) %collective-permute-start.2) | collective-permute-done | bytes 262176 | tf_op jit(solution)/shard_map/ppermute | solution.py:20
  14.7 4.0 %collective-permute-start.3 = (bf16[128,1024]{1,0:T(8,128)(2,1)S(1)}, bf16[128,1024]{1,0:T(8,128)(2,1)S(1)}, u32[]{:S(2)}, u32[]{:S(2)}) collective-permute-start(bf16[128,1024]{1,0:T(8,128)(2,1)S(1)} %collective-permute-done.2.refs_5_.refs_11_), channel_id=1, source_target_pairs={{0,4},{4,8},{8,12},{1,5},{5,9},{9,13},{2,6},{6,10},{10,14},{3,7},{... | collective-permute-start | bytes 786440 | tf_op jit(solution)/shard_map/ppermute | solution.py:20
  18.8 0.0 collective-permute-done.4.refs_7_.refs_2_
  18.8 1.3 %collective-permute-start.5 = (bf16[128,1024]{1,0:T(8,128)(2,1)S(1)}, bf16[128,1024]{1,0:T(8,128)(2,1)S(1)}, u32[]{:S(2)}, u32[]{:S(2)}) collective-permute-start(bf16[128,1024]{1,0:T(8,128)(2,1)S(1)} %collective-permute-done.4.refs_7_.refs_2_), channel_id=1, source_target_pairs={{4,0},{8,4},{12,8},{5,1},{9,5},{13,9},{6,2},{10,6},{14,10},{7,3},{... | collective-permute-start | bytes 786440 | tf_op jit(solution)/shard_map/ppermute | solution.py:20
  20.1 0.0 copy-start.2
  20.1 0.0 copy-done.1
  20.1 0.6 %copy-done.2 = s32[1,4]{1,0:T(1,128)S(1)} copy-done((s32[1,4]{1,0:T(1,128)S(1)}, s32[1,4]{1,0:T(1,128)}, u32[]{:S(2)}) %copy-start.2) | copy-done | bytes 40
  20.7 2.5 %shard_map.127 = (f32[64,128]{1,0:T(8,128)S(1)}, f32[1024,128]{1,0:T(8,128)S(1)}, f32[128,128]{1,0:T(8,128)S(1)}, f32[128,128]{1,0:T(8,128)S(1)}, f32[128,128]{1...) custom-call(s32[1,4]{1,0:T(1,128)S(1)} %copy-done.2, ...), custom_call_target="tpu_custom_call" | custom-call | flops 1000000 | bytes 100000 | tf_op jit(solution)/shard_map/pallas_call | solution.py:330
  23.2 0.6 %shard_map.128.refs_6_ = f32[128,1024]{1,0:T(8,128)S(1)} custom-call(f32[64,128]{1,0:T(8,128)S(1)} %get-tuple-element.36.refs_0_, f32[1024,128]{1,0:T(8,128)S(1)} %get-tuple-element.37.refs_1_, f32[128,128]{1,0:T(8,128)S(1)} %get-tuple-element.39.refs_2_.refs_3_, bf16[128,1024]{1,0:T(8,128)(2,1)S(1)} %get-tuple-element.41.refs_3_.refs_5_.refs_2_, ...), custom_call_target="tpu_custom_call" | custom-call | flops 1000000 | bytes 100000 | tf_op jit(solution)/shard_map/pallas_call | solution.py:330
  23.8 0.0 copy-start
  23.8 0.0 collective-permute-done.1.refs_4_.refs_9_
  23.8 2.1 %collective-permute-done.3.refs_5_.refs_12_ = bf16[128,1024]{1,0:T(8,128)(2,1)S(1)} collective-permute-done((bf16[128,1024]{1,0:T(8,128)(2,1)S(1)}, bf16[128,1024]{1,0:T(8,128)(2,1)S(1)}, u32[]{:S(2)}, u32[]{:S(2)}) %collective-permute-start.3) | collective-permute-done | bytes 262176 | tf_op jit(solution)/shard_map/ppermute | solution.py:20
  25.9 0.0 copy-done
  25.9 1.0 %shard_map.129 = (f32[128,1024]{1,0:T(8,128)S(1)}, bf16[128,1024]{1,0:T(8,128)(2,1)S(1)}, f32[1,1024]{1,0:T(1,128)S(1)}) custom-call(f32[64,128]{1,0:T(8,128)S(1)} %get-tuple-element.36.refs_0_, f32[1024,128]{1,0:T(8,128)S(1)} %get-tuple-element.37.refs_1_, f32[128,128]{1,0:T(8,128)S(1)} %get-tuple-element.40.refs_2_.refs_4_, ...), custom_call_target="tpu_custom_call" | custom-call | flops 1000000 | bytes 100000 | tf_op jit(solution)/shard_map/pallas_call | solution.py:330
  26.9 1.3 %collective-permute-start.6 = (bf16[128,1024]{1,0:T(8,128)(2,1)S(1)}, bf16[128,1024]{1,0:T(8,128)(2,1)S(1)}, u32[]{:S(2)}, u32[]{:S(2)}) collective-permute-start(bf16[128,1024]{1,0:T(8,128)(2,1)S(1)} %get-tuple-element.45.refs_6_.refs_3_), channel_id=1, source_target_pairs={{4,0},{8,4},{12,8},{5,1},{9,5},{13,9},{6,2},{10,6},{14,10},{7,3},{... | collective-permute-start | bytes 786440 | tf_op jit(solution)/shard_map/ppermute | solution.py:20
  28.2 0.0 collective-permute-done.5.refs_14_.refs_2_
  28.2 2.4 %shard_map.130 = (bf16[128,1024]{1,0:T(8,128)(2,1)}, f32[16,128]{1,0:T(8,128)S(1)}) custom-call(f32[64,128]{1,0:T(8,128)S(1)} %get-tuple-element.36.refs_0_, f32[1024,128]{1,0:T(8,128)S(1)} %get-tuple-element.37.refs_1_, f32[128,128]{1,0:T(8,128)S(1)} %get-tuple-element.38.refs_2_, f32[128,128]{1,0:T(8,128)S(1)} %get-tuple-element.39.refs_2_.refs_3_, ...), custom_call_target="tpu_custom_call" | custom-call | flops 1000000 | bytes 100000 | tf_op jit(solution)/shard_map/pallas_call | solution.py:330
  30.6 1.8 %collective-permute-start.7 = (f32[16,128]{1,0:T(8,128)S(1)}, f32[16,128]{1,0:T(8,128)S(1)}, u32[]{:S(2)}, u32[]{:S(2)}) collective-permute-start(f32[16,128]{1,0:T(8,128)S(1)} %get-tuple-element.51), channel_id=1, source_target_pairs={{0,1},{1,0},{2,3},{3,2},{4,5},{5,4},{6,7},{7,6},{8,9},{9,8},{10,11... | collective-permute-start | bytes 24584 | tf_op jit(solution)/shard_map/ppermute | solution.py:353
  32.4 0.3 collective-permute-start.8
  32.6 1.4 %collective-permute-start.9 = (f32[16,128]{1,0:T(8,128)S(1)}, f32[16,128]{1,0:T(8,128)S(1)}, u32[]{:S(2)}, u32[]{:S(2)}) collective-permute-start(f32[16,128]{1,0:T(8,128)S(1)} %get-tuple-element.51), channel_id=1, source_target_pairs={{0,3},{1,2},{2,1},{3,0},{4,7},{5,6},{6,5},{7,4},{8,11},{9,10},{10,... | collective-permute-start | bytes 24584 | tf_op jit(solution)/shard_map/ppermute | solution.py:353
  34.0 0.0 collective-permute-done.7
  34.0 1.2 %collective-permute-done.8 = f32[16,128]{1,0:T(8,128)S(1)} collective-permute-done((f32[16,128]{1,0:T(8,128)S(1)}, f32[16,128]{1,0:T(8,128)S(1)}, u32[]{:S(2)}, u32[]{:S(2)}) %collective-permute-start.8) | collective-permute-done | bytes 8224 | tf_op jit(solution)/shard_map/ppermute | solution.py:353
  35.2 0.8 %collective-permute-done.9 = f32[16,128]{1,0:T(8,128)S(1)} collective-permute-done((f32[16,128]{1,0:T(8,128)S(1)}, f32[16,128]{1,0:T(8,128)S(1)}, u32[]{:S(2)}, u32[]{:S(2)}) %collective-permute-start.9) | collective-permute-done | bytes 8224 | tf_op jit(solution)/shard_map/ppermute | solution.py:353
  36.0 6.8 %collective-permute-start.11 = (f32[16,128]{1,0:T(8,128)S(1)}, f32[16,128]{1,0:T(8,128)S(1)}, u32[]{:S(2)}, u32[]{:S(2)}) collective-permute-start(f32[16,128]{1,0:T(8,128)S(1)} %add_add_fusion), channel_id=1, source_target_pairs={{0,0},{1,5},{2,10},{3,15},{4,4},{5,1},{6,14},{7,11},{8,8},{9,13},{... | collective-permute-start | bytes 24584 | tf_op jit(solution)/shard_map/ppermute | solution.py:367
  42.8 0.0 collective-permute-done.6.refs_3_
  42.8 1.3 %collective-permute-start.10 = (bf16[128,1024]{1,0:T(8,128)(2,1)S(1)}, bf16[128,1024]{1,0:T(8,128)(2,1)S(1)}, u32[]{:S(2)}, u32[]{:S(2)}) collective-permute-start(bf16[128,1024]{1,0:T(8,128)(2,1)S(1)} %collective-permute-done.6.refs_3_), channel_id=1, source_target_pairs={{4,0},{8,4},{12,8},{5,1},{9,5},{13,9},{6,2},{10,6},{14,10},{7,3},{... | collective-permute-start | bytes 786440 | tf_op jit(solution)/shard_map/ppermute | solution.py:20
  44.1 0.0 collective-permute-done.11.refs_6_
  44.1 0.9 %shard_map.131 = (f32[128,1024]{1,0:T(8,128)S(1)}, f32[128,1024]{1,0:T(8,128)S(1)}, f32[16,128]{1,0:T(8,128)S(1)}) custom-call(f32[64,128]{1,0:T(8,128)S(1)} %get-tuple-element.36.refs_0_, f32[128,128]{1,0:T(8,128)S(1)} %get-tuple-element.54.refs_1_, bf16[128,1024]{1,0:T(8,128)(2,1)S(1)} %get-tuple-element.41.refs_3_.refs_5_.refs_2_, ...), custom_call_target="tpu_custom_call" | custom-call | flops 4000000000 | bytes 100000 | tf_op jit(solution)/shard_map/pallas_call | solution.py:330
  45.1 0.1 collective-permute-start.12
  45.1 0.1 collective-permute-start.13
  45.2 2.0 %collective-permute-start.14 = (f32[16,128]{1,0:T(8,128)S(1)}, f32[16,128]{1,0:T(8,128)S(1)}, u32[]{:S(2)}, u32[]{:S(2)}) collective-permute-start(f32[16,128]{1,0:T(8,128)S(1)} %get-tuple-element.58.refs_11_.refs_0_), channel_id=1, source_target_pairs={{0,3},{1,2},{2,1},{3,0},{4,7},{5,6},{6,5},{7,4},{8,11},{9,10},{10,... | collective-permute-start | bytes 24584 | tf_op jit(solution)/shard_map/ppermute | solution.py:353
  47.3 1.6 %shard_map.132 = (bf16[128,1024]{1,0:T(8,128)(2,1)}, f32[128,1024]{1,0:T(8,128)S(1)}, f32[128,1024]{1,0:T(8,128)S(1)}) custom-call(f32[64,128]{1,0:T(8,128)S(1)} %get-tuple-element.36.refs_0_, f32[128,128]{1,0:T(8,128)S(1)} %get-tuple-element.53.refs_1_, bf16[128,1024]{1,0:T(8,128)(2,1)S(1)} %collective-permute-done.4.refs_7_.refs_2_, ...), custom_call_target="tpu_custom_call" | custom-call | flops 1000000 | bytes 100000 | tf_op jit(solution)/shard_map/pallas_call | solution.py:330
  48.9 0.0 collective-permute-done.12.refs_1_
  48.9 0.0 collective-permute-done.13.refs_2_
  48.9 0.1 collective-permute-done.14.refs_3_
  49.0 0.6 %shard_map.134 = (f32[8,128]{1,0:T(8,128)}, f32[8,8]{1,0:T(8,128)}) custom-call(f32[16,128]{1,0:T(8,128)S(1)} %get-tuple-element.58.refs_11_.refs_0_, f32[16,128]{1,0:T(8,128)S(1)} %collective-permute-done.12.refs_1_, f32[16,128]{1,0:T(8,128)S(1)} %collective-permute-done.13.refs_2_, f32[16,128]{1,0:T(8,128)S(1)} %collective-permute-done.14.refs_3_, ...), custom_call_target="tpu_custom_call" | custom-call | flops 1000000 | bytes 100000 | tf_op jit(solution)/shard_map/pallas_call | solution.py:330
  49.6 3.4 %collective-permute-done.10.refs_3_ = bf16[128,1024]{1,0:T(8,128)(2,1)S(1)} collective-permute-done((bf16[128,1024]{1,0:T(8,128)(2,1)S(1)}, bf16[128,1024]{1,0:T(8,128)(2,1)S(1)}, u32[]{:S(2)}, u32[]{:S(2)}) %collective-permute-start.10) | collective-permute-done | bytes 262176 | tf_op jit(solution)/shard_map/ppermute | solution.py:20
  52.9 1.5 %shard_map.133 = (bf16[128,1024]{1,0:T(8,128)(2,1)}, bf16[128,1024]{1,0:T(8,128)(2,1)}) custom-call(f32[64,128]{1,0:T(8,128)S(1)} %get-tuple-element.36.refs_0_, f32[128,128]{1,0:T(8,128)S(1)} %get-tuple-element.50.refs_1_, bf16[128,1024]{1,0:T(8,128)(2,1)S(1)} %collective-permute-done.5.refs_14_.refs_2_, ...), custom_call_target="tpu_custom_call" | custom-call | flops 1000000 | bytes 100000 | tf_op jit(solution)/shard_map/pallas_call | solution.py:330
  (1 shorter events, 0.0 us)
Async XLA Ops:
  0.6 19.4 %copy-start.1 = (f32[8,8]{1,0:T(8,128)S(1)}, f32[8,8]{1,0:T(8,128)}, u32[]{:S(2)}) copy-start(f32[8,8]{1,0:T(8,128)} %refs_1_.1) | copy-start | bytes 772
  0.6 8.5 %collective-permute-start = (bf16[128,1024]{1,0:T(8,128)(2,1)}, bf16[128,1024]{1,0:T(8,128)(2,1)S(1)}, u32[]{:S(2)}, u32[]{:S(2)}) collective-permute-start(bf16[128,1024]{1,0:T(8,128)(2,1)} %bitcast.15), channel_id=1, source_target_pairs={{0,4},{4,8},{8,12},{1,5},{5,9},{9,13},{2,6},{6,10},{10,14},{3,7},{... | collective-permute-start | bytes 786440 | tf_op jit(solution)/shard_map/ppermute | solution.py:20
  3.9 10.9 %collective-permute-start.2 = (bf16[128,1024]{1,0:T(8,128)(2,1)}, bf16[128,1024]{1,0:T(8,128)(2,1)S(1)}, u32[]{:S(2)}, u32[]{:S(2)}) collective-permute-start(bf16[128,1024]{1,0:T(8,128)(2,1)} %bitcast.17), channel_id=1, source_target_pairs={{0,4},{4,8},{8,12},{1,5},{5,9},{9,13},{2,6},{6,10},{10,14},{3,7},{... | collective-permute-start | bytes 786440 | tf_op jit(solution)/shard_map/ppermute | solution.py:20
  7.1 11.7 %collective-permute-start.4 = (bf16[128,1024]{1,0:T(8,128)(2,1)}, bf16[128,1024]{1,0:T(8,128)(2,1)S(1)}, u32[]{:S(2)}, u32[]{:S(2)}) collective-permute-start(bf16[128,1024]{1,0:T(8,128)(2,1)} %bitcast.13), channel_id=1, source_target_pairs={{4,0},{8,4},{12,8},{5,1},{9,5},{13,9},{6,2},{10,6},{14,10},{7,3},{... | collective-permute-start | bytes 786440 | tf_op jit(solution)/shard_map/ppermute | solution.py:20
  9.1 14.7 %collective-permute-start.1 = (bf16[128,1024]{1,0:T(8,128)(2,1)S(1)}, bf16[128,1024]{1,0:T(8,128)(2,1)S(1)}, u32[]{:S(2)}, u32[]{:S(2)}) collective-permute-start(bf16[128,1024]{1,0:T(8,128)(2,1)S(1)} %collective-permute-done.refs_4_.refs_8_), channel_id=1, source_target_pairs={{0,4},{4,8},{8,12},{1,5},{5,9},{9,13},{2,6},{6,10},{10,14},{3,7},{... | collective-permute-start | bytes 786440 | tf_op jit(solution)/shard_map/ppermute | solution.py:20
  14.7 11.1 %collective-permute-start.3 = (bf16[128,1024]{1,0:T(8,128)(2,1)S(1)}, bf16[128,1024]{1,0:T(8,128)(2,1)S(1)}, u32[]{:S(2)}, u32[]{:S(2)}) collective-permute-start(bf16[128,1024]{1,0:T(8,128)(2,1)S(1)} %collective-permute-done.2.refs_5_.refs_11_), channel_id=1, source_target_pairs={{0,4},{4,8},{8,12},{1,5},{5,9},{9,13},{2,6},{6,10},{10,14},{3,7},{... | collective-permute-start | bytes 786440 | tf_op jit(solution)/shard_map/ppermute | solution.py:20
  18.8 9.4 %collective-permute-start.5 = (bf16[128,1024]{1,0:T(8,128)(2,1)S(1)}, bf16[128,1024]{1,0:T(8,128)(2,1)S(1)}, u32[]{:S(2)}, u32[]{:S(2)}) collective-permute-start(bf16[128,1024]{1,0:T(8,128)(2,1)S(1)} %collective-permute-done.4.refs_7_.refs_2_), channel_id=1, source_target_pairs={{4,0},{8,4},{12,8},{5,1},{9,5},{13,9},{6,2},{10,6},{14,10},{7,3},{... | collective-permute-start | bytes 786440 | tf_op jit(solution)/shard_map/ppermute | solution.py:20
  20.1 0.7 %copy-start.2 = (s32[1,4]{1,0:T(1,128)S(1)}, s32[1,4]{1,0:T(1,128)}, u32[]{:S(2)}) copy-start(s32[1,4]{1,0:T(1,128)} %refs_0_.1) | copy-start | bytes 52
  23.8 2.1 %copy-start = (f32[1024]{0:T(1024)S(1)}, f32[1024]{0:T(1024)}, u32[]{:S(2)}) copy-start(f32[1024]{0:T(1024)} %param.15) | copy-start | bytes 12292
  26.9 16.0 %collective-permute-start.6 = (bf16[128,1024]{1,0:T(8,128)(2,1)S(1)}, bf16[128,1024]{1,0:T(8,128)(2,1)S(1)}, u32[]{:S(2)}, u32[]{:S(2)}) collective-permute-start(bf16[128,1024]{1,0:T(8,128)(2,1)S(1)} %get-tuple-element.45.refs_6_.refs_3_), channel_id=1, source_target_pairs={{4,0},{8,4},{12,8},{5,1},{9,5},{13,9},{6,2},{10,6},{14,10},{7,3},{... | collective-permute-start | bytes 786440 | tf_op jit(solution)/shard_map/ppermute | solution.py:20
  30.6 3.5 %collective-permute-start.7 = (f32[16,128]{1,0:T(8,128)S(1)}, f32[16,128]{1,0:T(8,128)S(1)}, u32[]{:S(2)}, u32[]{:S(2)}) collective-permute-start(f32[16,128]{1,0:T(8,128)S(1)} %get-tuple-element.51), channel_id=1, source_target_pairs={{0,1},{1,0},{2,3},{3,2},{4,5},{5,4},{6,7},{7,6},{8,9},{9,8},{10,11... | collective-permute-start | bytes 24584 | tf_op jit(solution)/shard_map/ppermute | solution.py:353
  32.4 2.8 %collective-permute-start.8 = (f32[16,128]{1,0:T(8,128)S(1)}, f32[16,128]{1,0:T(8,128)S(1)}, u32[]{:S(2)}, u32[]{:S(2)}) collective-permute-start(f32[16,128]{1,0:T(8,128)S(1)} %get-tuple-element.51), channel_id=1, source_target_pairs={{0,2},{1,3},{2,0},{3,1},{4,6},{5,7},{6,4},{7,5},{8,10},{9,11},{10,... | collective-permute-start | bytes 24584 | tf_op jit(solution)/shard_map/ppermute | solution.py:353
  32.6 3.4 %collective-permute-start.9 = (f32[16,128]{1,0:T(8,128)S(1)}, f32[16,128]{1,0:T(8,128)S(1)}, u32[]{:S(2)}, u32[]{:S(2)}) collective-permute-start(f32[16,128]{1,0:T(8,128)S(1)} %get-tuple-element.51), channel_id=1, source_target_pairs={{0,3},{1,2},{2,1},{3,0},{4,7},{5,6},{6,5},{7,4},{8,11},{9,10},{10,... | collective-permute-start | bytes 24584 | tf_op jit(solution)/shard_map/ppermute | solution.py:353
  36.0 8.1 %collective-permute-start.11 = (f32[16,128]{1,0:T(8,128)S(1)}, f32[16,128]{1,0:T(8,128)S(1)}, u32[]{:S(2)}, u32[]{:S(2)}) collective-permute-start(f32[16,128]{1,0:T(8,128)S(1)} %add_add_fusion), channel_id=1, source_target_pairs={{0,0},{1,5},{2,10},{3,15},{4,4},{5,1},{6,14},{7,11},{8,8},{9,13},{... | collective-permute-start | bytes 24584 | tf_op jit(solution)/shard_map/ppermute | solution.py:367
  42.8 10.1 %collective-permute-start.10 = (bf16[128,1024]{1,0:T(8,128)(2,1)S(1)}, bf16[128,1024]{1,0:T(8,128)(2,1)S(1)}, u32[]{:S(2)}, u32[]{:S(2)}) collective-permute-start(bf16[128,1024]{1,0:T(8,128)(2,1)S(1)} %collective-permute-done.6.refs_3_), channel_id=1, source_target_pairs={{4,0},{8,4},{12,8},{5,1},{9,5},{13,9},{6,2},{10,6},{14,10},{7,3},{... | collective-permute-start | bytes 786440 | tf_op jit(solution)/shard_map/ppermute | solution.py:20
  45.1 3.8 %collective-permute-start.12 = (f32[16,128]{1,0:T(8,128)S(1)}, f32[16,128]{1,0:T(8,128)S(1)}, u32[]{:S(2)}, u32[]{:S(2)}) collective-permute-start(f32[16,128]{1,0:T(8,128)S(1)} %get-tuple-element.58.refs_11_.refs_0_), channel_id=1, source_target_pairs={{0,1},{1,0},{2,3},{3,2},{4,5},{5,4},{6,7},{7,6},{8,9},{9,8},{10,11... | collective-permute-start | bytes 24584 | tf_op jit(solution)/shard_map/ppermute | solution.py:353
  45.1 3.8 %collective-permute-start.13 = (f32[16,128]{1,0:T(8,128)S(1)}, f32[16,128]{1,0:T(8,128)S(1)}, u32[]{:S(2)}, u32[]{:S(2)}) collective-permute-start(f32[16,128]{1,0:T(8,128)S(1)} %get-tuple-element.58.refs_11_.refs_0_), channel_id=1, source_target_pairs={{0,2},{1,3},{2,0},{3,1},{4,6},{5,7},{6,4},{7,5},{8,10},{9,11},{10,... | collective-permute-start | bytes 24584 | tf_op jit(solution)/shard_map/ppermute | solution.py:353
  45.2 3.8 %collective-permute-start.14 = (f32[16,128]{1,0:T(8,128)S(1)}, f32[16,128]{1,0:T(8,128)S(1)}, u32[]{:S(2)}, u32[]{:S(2)}) collective-permute-start(f32[16,128]{1,0:T(8,128)S(1)} %get-tuple-element.58.refs_11_.refs_0_), channel_id=1, source_target_pairs={{0,3},{1,2},{2,1},{3,0},{4,7},{5,6},{6,5},{7,4},{8,11},{9,10},{10,... | collective-permute-start | bytes 24584 | tf_op jit(solution)/shard_map/ppermute | solution.py:353

commit v9 on v8

--- a/solution.py
+++ b/solution.py
@@ -9,7 +9,6 @@
 
 EPSILON = 1e-05
 VMEM_LIMIT = 24 * 1024 * 1024
-LONG = 4 * 10**9
 F32 = jnp.float32
 BF16 = jnp.bfloat16
 
@@ -266,14 +265,8 @@
     return store
 
 
-def own_key_kernel(heads, scaling, *refs):
-    pieces, (key_out, value_out, shared) = refs[6:-3], refs[-3:]
-    shared[...] = added_up([piece[...] for piece in pieces])
-    add_key_grads(0, heads, scaling, *refs[:6], (), into(key_out, value_out))
-
-
 def next_key_kernel(hops, heads, scaling, *refs):
-    add_key_grads(hops, heads, scaling, *refs[:6], refs[6:8], into(*refs[8:]))
+    add_key_grads(hops, heads, scaling, *refs[:6], refs[6:-2], into(*refs[-2:]))
 
 
 def gate_and_key_kernel(hops, heads, scaling, *refs):
@@ -319,7 +312,7 @@
     bias_out[...] = total[lines:, : bias_out.shape[1]]
 
 
-def on_device(kernel, outs, args, smem=(), ahead=(), far=(), far_outs=0, scratch=(), flops=1000000):
+def on_device(kernel, outs, args, smem=(), ahead=(), far=(), far_outs=0, scratch=()):
     count = len(smem) + len(far) + len(args)
     far = [pltpu.with_memory_space_constraint(array, pltpu.HBM) for array in far]
 
@@ -337,35 +330,34 @@
         out_specs=[anywhere] * far_outs + [vmem] * (len(outs) - far_outs),
         scratch_shapes=scratch,
         compiler_params=pltpu.CompilerParams(vmem_limit_bytes=VMEM_LIMIT),
-        cost_estimate=pl.CostEstimate(flops=flops, bytes_accessed=100000, transcendentals=0),
+        cost_estimate=pl.CostEstimate(flops=1000000, bytes_accessed=100000, transcendentals=0),
     )(*smem, *far, *args, *ahead)
+
+
+def rounds_of(axes):
+    rounds = []
+    for axis in axes:
+        size = lax.axis_size(axis)
+        step = 1
+        while step < size:
+            radix = 4 if size // step >= 4 else 2
+            rounds.append((axis, [step * at for at in range(1, radix)]))
+            step = radix * step
+    return rounds
+
+
+def exchanged(array, axis, distances):
+    size = lax.axis_size(axis)
+    return [array] + [
+        lax.ppermute(array, axis, [(i, i ^ distance) for i in range(size)])
+        for distance in distances
+    ]
 
 
 def added_up(pieces):
     while len(pieces) > 1:
         pieces = [left + right for left, right in zip(pieces[::2], pieces[1::2])]
     return pieces[0]
-
-
-def exchanged(array, axis):
-    size = lax.axis_size(axis)
-    return [array] + [
-        lax.ppermute(array, axis, [(i, i ^ distance) for i in range(size)])
-        for distance in range(1, size)
-    ]
-
-
-def spread(array, axis, helpers):
-    size, count = lax.axis_size(axis), lax.axis_size(helpers)
-    found = []
-    for low in range(0, size, count):
-        pairs = [
-            (i * count + m, (i ^ (low + m)) * count + m)
-            for i in range(size)
-            for m in range(min(count, size - low))
-        ]
-        found.append(lax.ppermute(array, (axis, helpers), pairs))
-    return found
 
 
 def local(queries, key_rows, value_rows, update_gate, out_grad, user_lengths, rel_bias, norm_gain):
@@ -423,28 +415,28 @@
         ahead=later_queries[reach:],
     )
     later_grads = [attn_grad, passed_along(attn_grad, "ctx", -1)]
-    sums = added_up(exchanged(sums, "dp"))
+    pieces = [sums]
+    for axis, distances in rounds_of(("dp",)):
+        pieces = exchanged(added_up(pieces), axis, distances)
 
     def key_operands(hops):
         later = (later_queries[hops], later_grads[hops])
         return (table, flipped[hops], *later, key, value)
 
-    *key_grads, shared = on_device(
-        partial(own_key_kernel, heads, scaling),
-        [wide, wide, jax.ShapeDtypeStruct(sums.shape, F32)],
-        (*key_operands(0), *spread(sums, "ctx", "dp")),
-        flops=LONG,
-    )
-    pieces = exchanged(shared, "dp")
+    key_grads = on_device(
+        partial(next_key_kernel, 0, heads, scaling),
+        [wide] * 2,
+        key_operands(0),
+        ahead=pieces[1:2],
+    )
     for hops in range(1, reach):
-        arrived, sums = lax.optimization_barrier((later_grads[hops], sums))
+        arrived, *pieces = lax.optimization_barrier((later_grads[hops], *pieces))
         later_grads.append(passed_along(arrived, "ctx", -1))
         if hops == 1:
             gate_grad, *key_grads = on_device(
                 partial(gate_and_key_kernel, hops, heads, scaling),
                 [narrow, wide, wide],
                 (*key_operands(hops), *key_grads, attention, grad, gain),
-                ahead=[shared],
                 far_outs=1,
                 scratch=[pltpu.VMEM((rows, features), BF16), pltpu.SemaphoreType.DMA(())],
             )
@@ -454,6 +446,9 @@
                 [wide] * 2,
                 (*key_operands(hops), *key_grads),
             )
+    key_grads, *pieces = lax.optimization_barrier((key_grads, *pieces))
+    for axis, distances in rounds_of(("ctx",)):
+        pieces = exchanged(added_up(pieces), axis, distances)
     key_grad, value_grad = on_device(
         partial(last_kernel, reach, heads, scaling),
         [narrow, narrow],
@@ -465,7 +460,7 @@
         sum_kernel,
         [jax.ShapeDtypeStruct((8, lanes), F32), jax.ShapeDtypeStruct((levels, heads), F32)],
         pieces,
-        ahead=key_grads[:1],
+        ahead=[key_grad],
     )
     return (
         query_grad[None],

time: 54.9 us -> 56.1 us (1.022)
  the two profiles are of different devices: /device:TPU:3 before, /device:TPU:0 now
where the time goes in v9:
time: 56.1 us; the launch traced here: 55.7 us
  starting transfers between devices  29.9 us (53%)
  waiting for transfers between devices  12.4 us (22%)
  Pallas kernels  11 us (20%)
  local copies, waits for them, and re-layouts  1.6 us (3%)
  between operations  0.81 us (1%)
    ppermute x8, starting transfers between devices, passed_along(): return lax.ppermute(array, axis, pairs)  22.2 us
    pallas_call x8, Pallas kernels, on_device(): pl.pallas_call(body, out_shape=outs, in_specs=[pl.BlockSpec(memory_space=...  11 us
    ppermute x6, starting transfers between devices, exchanged(): lax.ppermute(array, axis, [(i, i ^ distance) for i in range(size)])  7.74 us
    ppermute x8, waiting for transfers between devices, passed_along(): return lax.ppermute(array, axis, pairs)  6.42 us
    ppermute x6, waiting for transfers between devices, exchanged(): lax.ppermute(array, axis, [(i, i ^ distance) for i in range(size)])  5.95 us
    unnamed x8, local copies, waits for them, and re-layouts  1.6 us
  transfers between devices with their start and end apart: 14, of which 10 were waited for; matrix products, arithmetic and copies ran while one was open for 0% of the time, Pallas kernels for 19%

profile of v9, /device:TPU:0, one launch (start us, length us, event | category | flops | bytes accessed | tf_op | source)
XLA Modules:
  0.0 55.7 jit_solution(3181080038386569190)
XLA Ops:
  0.6 0.0 copy-start.2
  0.6 4.9 %collective-permute-start = (bf16[128,1024]{1,0:T(8,128)(2,1)}, bf16[128,1024]{1,0:T(8,128)(2,1)S(1)}, u32[]{:S(2)}, u32[]{:S(2)}) collective-permute-start(bf16[128,1024]{1,0:T(8,128)(2,1)} %bitcast.16), channel_id=1, source_target_pairs={{0,4},{4,8},{8,12},{1,5},{5,9},{9,13},{2,6},{6,10},{10,14},{3,7},{... | collective-permute-start | bytes 786440 | tf_op jit(solution)/shard_map/ppermute | solution.py:19
  5.6 3.5 %collective-permute-start.2 = (bf16[128,1024]{1,0:T(8,128)(2,1)}, bf16[128,1024]{1,0:T(8,128)(2,1)S(1)}, u32[]{:S(2)}, u32[]{:S(2)}) collective-permute-start(bf16[128,1024]{1,0:T(8,128)(2,1)} %bitcast.18), channel_id=1, source_target_pairs={{0,4},{4,8},{8,12},{1,5},{5,9},{9,13},{2,6},{6,10},{10,14},{3,7},{... | collective-permute-start | bytes 786440 | tf_op jit(solution)/shard_map/ppermute | solution.py:19
  9.1 1.3 %collective-permute-start.4 = (bf16[128,1024]{1,0:T(8,128)(2,1)}, bf16[128,1024]{1,0:T(8,128)(2,1)S(1)}, u32[]{:S(2)}, u32[]{:S(2)}) collective-permute-start(bf16[128,1024]{1,0:T(8,128)(2,1)} %bitcast.14), channel_id=1, source_target_pairs={{4,0},{8,4},{12,8},{5,1},{9,5},{13,9},{6,2},{10,6},{14,10},{7,3},{... | collective-permute-start | bytes 786440 | tf_op jit(solution)/shard_map/ppermute | solution.py:19
  10.4 2.2 %collective-permute-done.refs_4_.refs_8_ = bf16[128,1024]{1,0:T(8,128)(2,1)S(1)} collective-permute-done((bf16[128,1024]{1,0:T(8,128)(2,1)}, bf16[128,1024]{1,0:T(8,128)(2,1)S(1)}, u32[]{:S(2)}, u32[]{:S(2)}) %collective-permute-start) | collective-permute-done | bytes 262176 | tf_op jit(solution)/shard_map/ppermute | solution.py:19
  12.6 4.3 %collective-permute-start.1 = (bf16[128,1024]{1,0:T(8,128)(2,1)S(1)}, bf16[128,1024]{1,0:T(8,128)(2,1)S(1)}, u32[]{:S(2)}, u32[]{:S(2)}) collective-permute-start(bf16[128,1024]{1,0:T(8,128)(2,1)S(1)} %collective-permute-done.refs_4_.refs_8_), channel_id=1, source_target_pairs={{0,4},{4,8},{8,12},{1,5},{5,9},{9,13},{2,6},{6,10},{10,14},{3,7},{... | collective-permute-start | bytes 786440 | tf_op jit(solution)/shard_map/ppermute | solution.py:19
  16.9 1.3 %collective-permute-done.2.refs_5_.refs_11_ = bf16[128,1024]{1,0:T(8,128)(2,1)S(1)} collective-permute-done((bf16[128,1024]{1,0:T(8,128)(2,1)}, bf16[128,1024]{1,0:T(8,128)(2,1)S(1)}, u32[]{:S(2)}, u32[]{:S(2)}) %collective-permute-start.2) | collective-permute-done | bytes 262176 | tf_op jit(solution)/shard_map/ppermute | solution.py:19
  18.2 4.3 %collective-permute-start.3 = (bf16[128,1024]{1,0:T(8,128)(2,1)S(1)}, bf16[128,1024]{1,0:T(8,128)(2,1)S(1)}, u32[]{:S(2)}, u32[]{:S(2)}) collective-permute-start(bf16[128,1024]{1,0:T(8,128)(2,1)S(1)} %collective-permute-done.2.refs_5_.refs_11_), channel_id=1, source_target_pairs={{0,4},{4,8},{8,12},{1,5},{5,9},{9,13},{2,6},{6,10},{10,14},{3,7},{... | collective-permute-start | bytes 786440 | tf_op jit(solution)/shard_map/ppermute | solution.py:19
  22.5 0.0 collective-permute-done.4.refs_7_.refs_2_
  22.5 1.3 %collective-permute-start.5 = (bf16[128,1024]{1,0:T(8,128)(2,1)S(1)}, bf16[128,1024]{1,0:T(8,128)(2,1)S(1)}, u32[]{:S(2)}, u32[]{:S(2)}) collective-permute-start(bf16[128,1024]{1,0:T(8,128)(2,1)S(1)} %collective-permute-done.4.refs_7_.refs_2_), channel_id=1, source_target_pairs={{4,0},{8,4},{12,8},{5,1},{9,5},{13,9},{6,2},{10,6},{14,10},{7,3},{... | collective-permute-start | bytes 786440 | tf_op jit(solution)/shard_map/ppermute | solution.py:19
  23.8 0.0 copy-start.3
  23.8 0.0 copy-done.2
  23.8 0.6 %copy-done.3 = s32[1,4]{1,0:T(1,128)S(1)} copy-done((s32[1,4]{1,0:T(1,128)S(1)}, s32[1,4]{1,0:T(1,128)}, u32[]{:S(2)}) %copy-start.3) | copy-done | bytes 40
  24.5 2.5 %shard_map.127 = (f32[64,128]{1,0:T(8,128)S(1)}, f32[1024,128]{1,0:T(8,128)S(1)}, f32[128,128]{1,0:T(8,128)S(1)}, f32[128,128]{1,0:T(8,128)S(1)}, f32[128,128]{1...) custom-call(s32[1,4]{1,0:T(1,128)S(1)} %copy-done.3, ...), custom_call_target="tpu_custom_call" | custom-call | flops 1000000 | bytes 100000 | tf_op jit(solution)/shard_map/pallas_call | solution.py:323
  26.9 0.6 %shard_map.128.refs_6_ = f32[128,1024]{1,0:T(8,128)S(1)} custom-call(f32[64,128]{1,0:T(8,128)S(1)} %get-tuple-element.45.refs_0_, f32[1024,128]{1,0:T(8,128)S(1)} %get-tuple-element.46.refs_1_, f32[128,128]{1,0:T(8,128)S(1)} %get-tuple-element.48.refs_2_.refs_3_, bf16[128,1024]{1,0:T(8,128)(2,1)S(1)} %get-tuple-element.50.refs_3_.refs_5_.refs_2_, ...), custom_call_target="tpu_custom_call" | custom-call | flops 1000000 | bytes 100000 | tf_op jit(solution)/shard_map/pallas_call | solution.py:323
  27.5 0.0 copy-start.1
  27.5 0.0 collective-permute-done.1.refs_4_.refs_9_
  27.5 0.7 %collective-permute-done.3.refs_5_.refs_12_ = bf16[128,1024]{1,0:T(8,128)(2,1)S(1)} collective-permute-done((bf16[128,1024]{1,0:T(8,128)(2,1)S(1)}, bf16[128,1024]{1,0:T(8,128)(2,1)S(1)}, u32[]{:S(2)}, u32[]{:S(2)}) %collective-permute-start.3) | collective-permute-done | bytes 262176 | tf_op jit(solution)/shard_map/ppermute | solution.py:19
  28.2 0.0 copy-done.1
  28.2 1.0 %shard_map.129 = (f32[128,1024]{1,0:T(8,128)S(1)}, bf16[128,1024]{1,0:T(8,128)(2,1)S(1)}, f32[1,1024]{1,0:T(1,128)S(1)}) custom-call(f32[64,128]{1,0:T(8,128)S(1)} %get-tuple-element.45.refs_0_, f32[1024,128]{1,0:T(8,128)S(1)} %get-tuple-element.46.refs_1_, f32[128,128]{1,0:T(8,128)S(1)} %get-tuple-element.49.refs_2_.refs_4_, ...), custom_call_target="tpu_custom_call" | custom-call | flops 1000000 | bytes 100000 | tf_op jit(solution)/shard_map/pallas_call | solution.py:323
  29.2 1.3 %collective-permute-start.6 = (bf16[128,1024]{1,0:T(8,128)(2,1)S(1)}, bf16[128,1024]{1,0:T(8,128)(2,1)S(1)}, u32[]{:S(2)}, u32[]{:S(2)}) collective-permute-start(bf16[128,1024]{1,0:T(8,128)(2,1)S(1)} %get-tuple-element.54.refs_6_.refs_3_), channel_id=1, source_target_pairs={{4,0},{8,4},{12,8},{5,1},{9,5},{13,9},{6,2},{10,6},{14,10},{7,3},{... | collective-permute-start | bytes 786440 | tf_op jit(solution)/shard_map/ppermute | solution.py:19
  30.5 0.3 collective-permute-done.5.refs_14_.refs_2_
  30.8 2.4 %shard_map.130 = (bf16[128,1024]{1,0:T(8,128)(2,1)}, f32[16,128]{1,0:T(8,128)S(1)}) custom-call(f32[64,128]{1,0:T(8,128)S(1)} %get-tuple-element.45.refs_0_, f32[1024,128]{1,0:T(8,128)S(1)} %get-tuple-element.46.refs_1_, f32[128,128]{1,0:T(8,128)S(1)} %get-tuple-element.47.refs_2_, f32[128,128]{1,0:T(8,128)S(1)} %get-tuple-element.48.refs_2_.refs_3_, ...), custom_call_target="tpu_custom_call" | custom-call | flops 1000000 | bytes 100000 | tf_op jit(solution)/shard_map/pallas_call | solution.py:323
  33.1 0.0 collective-permute-start.7
  33.1 1.5 %collective-permute-start.8 = (f32[16,128]{1,0:T(8,128)S(1)}, f32[16,128]{1,0:T(8,128)S(1)}, u32[]{:S(2)}, u32[]{:S(2)}) collective-permute-start(f32[16,128]{1,0:T(8,128)S(1)} %get-tuple-element.78), channel_id=1, source_target_pairs={{0,2},{1,3},{2,0},{3,1},{4,6},{5,7},{6,4},{7,5},{8,10},{9,11},{10,... | collective-permute-start | bytes 24584 | tf_op jit(solution)/shard_map/ppermute | solution.py:352
  34.6 0.4 collective-permute-start.9
  35.0 0.0 collective-permute-done.7.refs_6_
  35.0 1.8 %collective-permute-done.8 = f32[16,128]{1,0:T(8,128)S(1)} collective-permute-done((f32[16,128]{1,0:T(8,128)S(1)}, f32[16,128]{1,0:T(8,128)S(1)}, u32[]{:S(2)}, u32[]{:S(2)}) %collective-permute-start.8) | collective-permute-done | bytes 8224 | tf_op jit(solution)/shard_map/ppermute | solution.py:352
  36.8 0.9 %collective-permute-done.9 = f32[16,128]{1,0:T(8,128)S(1)} collective-permute-done((f32[16,128]{1,0:T(8,128)S(1)}, f32[16,128]{1,0:T(8,128)S(1)}, u32[]{:S(2)}, u32[]{:S(2)}) %collective-permute-start.9) | collective-permute-done | bytes 8224 | tf_op jit(solution)/shard_map/ppermute | solution.py:352
  37.7 1.3 %collective-permute-done.6.refs_3_ = bf16[128,1024]{1,0:T(8,128)(2,1)S(1)} collective-permute-done((bf16[128,1024]{1,0:T(8,128)(2,1)S(1)}, bf16[128,1024]{1,0:T(8,128)(2,1)S(1)}, u32[]{:S(2)}, u32[]{:S(2)}) %collective-permute-start.6) | collective-permute-done | bytes 262176 | tf_op jit(solution)/shard_map/ppermute | solution.py:19
  39.0 1.3 %collective-permute-start.10 = (bf16[128,1024]{1,0:T(8,128)(2,1)S(1)}, bf16[128,1024]{1,0:T(8,128)(2,1)S(1)}, u32[]{:S(2)}, u32[]{:S(2)}) collective-permute-start(bf16[128,1024]{1,0:T(8,128)(2,1)S(1)} %collective-permute-done.6.refs_3_), channel_id=1, source_target_pairs={{4,0},{8,4},{12,8},{5,1},{9,5},{13,9},{6,2},{10,6},{14,10},{7,3},{... | collective-permute-start | bytes 786440 | tf_op jit(solution)/shard_map/ppermute | solution.py:19
  40.3 0.9 %shard_map.131 = (f32[128,1024]{1,0:T(8,128)S(1)}, f32[128,1024]{1,0:T(8,128)S(1)}) custom-call(f32[64,128]{1,0:T(8,128)S(1)} %get-tuple-element.45.refs_0_, f32[128,128]{1,0:T(8,128)S(1)} %get-tuple-element.63.refs_1_, bf16[128,1024]{1,0:T(8,128)(2,1)S(1)} %get-tuple-element.50.refs_3_.refs_5_.refs_2_, ...), custom_call_target="tpu_custom_call" | custom-call | flops 1000000 | bytes 100000 | tf_op jit(solution)/shard_map/pallas_call | solution.py:323
  41.2 1.6 %shard_map.132 = (bf16[128,1024]{1,0:T(8,128)(2,1)}, f32[128,1024]{1,0:T(8,128)S(1)}, f32[128,1024]{1,0:T(8,128)S(1)}) custom-call(f32[64,128]{1,0:T(8,128)S(1)} %get-tuple-element.45.refs_0_, f32[128,128]{1,0:T(8,128)S(1)} %get-tuple-element.62.refs_1_, bf16[128,1024]{1,0:T(8,128)(2,1)S(1)} %collective-permute-done.4.refs_7_.refs_2_, ...), custom_call_target="tpu_custom_call" | custom-call | flops 1000000 | bytes 100000 | tf_op jit(solution)/shard_map/pallas_call | solution.py:323
  42.8 2.7 %collective-permute-start.11 = (f32[16,128]{1,0:T(8,128)S(1)}, f32[16,128]{1,0:T(8,128)S(1)}, u32[]{:S(2)}, u32[]{:S(2)}) collective-permute-start(f32[16,128]{1,0:T(8,128)S(1)} %add_add_fusion.refs_0_), channel_id=1, source_target_pairs={{0,4},{4,0},{8,12},{12,8},{1,5},{5,1},{9,13},{13,9},{2,6},{6,2},{1... | collective-permute-start | bytes 24584 | tf_op jit(solution)/shard_map/ppermute | solution.py:352
  45.6 3.2 %collective-permute-start.12 = (f32[16,128]{1,0:T(8,128)S(1)}, f32[16,128]{1,0:T(8,128)S(1)}, u32[]{:S(2)}, u32[]{:S(2)}) collective-permute-start(f32[16,128]{1,0:T(8,128)S(1)} %add_add_fusion.refs_0_), channel_id=1, source_target_pairs={{0,8},{4,12},{8,0},{12,4},{1,9},{5,13},{9,1},{13,5},{2,10},{6,14},... | collective-permute-start | bytes 24584 | tf_op jit(solution)/shard_map/ppermute | solution.py:352
  48.7 0.0 collective-permute-start.13
  48.7 0.6 %collective-permute-done.10.refs_3_ = bf16[128,1024]{1,0:T(8,128)(2,1)S(1)} collective-permute-done((bf16[128,1024]{1,0:T(8,128)(2,1)S(1)}, bf16[128,1024]{1,0:T(8,128)(2,1)S(1)}, u32[]{:S(2)}, u32[]{:S(2)}) %collective-permute-start.10) | collective-permute-done | bytes 262176 | tf_op jit(solution)/shard_map/ppermute | solution.py:19
  49.4 1.5 %shard_map.133 = (bf16[128,1024]{1,0:T(8,128)(2,1)}, bf16[128,1024]{1,0:T(8,128)(2,1)}) custom-call(f32[64,128]{1,0:T(8,128)S(1)} %get-tuple-element.45.refs_0_, f32[128,128]{1,0:T(8,128)S(1)} %get-tuple-element.59.refs_1_, bf16[128,1024]{1,0:T(8,128)(2,1)S(1)} %collective-permute-done.5.refs_14_.refs_2_, ...), custom_call_target="tpu_custom_call" | custom-call | flops 1000000 | bytes 100000 | tf_op jit(solution)/shard_map/pallas_call | solution.py:323
  50.9 0.0 collective-permute-done.11.refs_1_
  50.9 0.1 collective-permute-done.12.refs_2_
  51.0 3.2 %collective-permute-done.13.refs_3_ = f32[16,128]{1,0:T(8,128)S(1)} collective-permute-done((f32[16,128]{1,0:T(8,128)S(1)}, f32[16,128]{1,0:T(8,128)S(1)}, u32[]{:S(2)}, u32[]{:S(2)}) %collective-permute-start.13) | collective-permute-done | bytes 8224 | tf_op jit(solution)/shard_map/ppermute | solution.py:352
  54.2 0.0 copy-start
  54.2 0.9 %copy-done = bf16[128,1024]{1,0:T(8,128)(2,1)S(1)} copy-done((bf16[128,1024]{1,0:T(8,128)(2,1)S(1)}, bf16[128,1024]{1,0:T(8,128)(2,1)}, u32[]{:S(2)}) %copy-start) | copy-done | bytes 262168
  55.1 0.6 %shard_map.134 = (f32[8,128]{1,0:T(8,128)}, f32[8,8]{1,0:T(8,128)}) custom-call(f32[16,128]{1,0:T(8,128)S(1)} %add_add_fusion.refs_0_, f32[16,128]{1,0:T(8,128)S(1)} %collective-permute-done.11.refs_1_, f32[16,128]{1,0:T(8,128)S(1)} %collective-permute-done.12.refs_2_, f32[16,128]{1,0:T(8,128)S(1)} %collective-permute-done.13.refs_3_, ...), custom_call_target="tpu_custom_call" | custom-call | flops 1000000 | bytes 100000 | tf_op jit(solution)/shard_map/pallas_call | solution.py:323
  (1 shorter events, 0.0 us)
Async XLA Ops:
  0.6 23.2 %copy-start.2 = (f32[8,8]{1,0:T(8,128)S(1)}, f32[8,8]{1,0:T(8,128)}, u32[]{:S(2)}) copy-start(f32[8,8]{1,0:T(8,128)} %refs_1_.1) | copy-start | bytes 772
  0.6 11.9 %collective-permute-start = (bf16[128,1024]{1,0:T(8,128)(2,1)}, bf16[128,1024]{1,0:T(8,128)(2,1)S(1)}, u32[]{:S(2)}, u32[]{:S(2)}) collective-permute-start(bf16[128,1024]{1,0:T(8,128)(2,1)} %bitcast.16), channel_id=1, source_target_pairs={{0,4},{4,8},{8,12},{1,5},{5,9},{9,13},{2,6},{6,10},{10,14},{3,7},{... | collective-permute-start | bytes 786440 | tf_op jit(solution)/shard_map/ppermute | solution.py:19
  5.6 12.6 %collective-permute-start.2 = (bf16[128,1024]{1,0:T(8,128)(2,1)}, bf16[128,1024]{1,0:T(8,128)(2,1)S(1)}, u32[]{:S(2)}, u32[]{:S(2)}) collective-permute-start(bf16[128,1024]{1,0:T(8,128)(2,1)} %bitcast.18), channel_id=1, source_target_pairs={{0,4},{4,8},{8,12},{1,5},{5,9},{9,13},{2,6},{6,10},{10,14},{3,7},{... | collective-permute-start | bytes 786440 | tf_op jit(solution)/shard_map/ppermute | solution.py:19
  9.1 13.4 %collective-permute-start.4 = (bf16[128,1024]{1,0:T(8,128)(2,1)}, bf16[128,1024]{1,0:T(8,128)(2,1)S(1)}, u32[]{:S(2)}, u32[]{:S(2)}) collective-permute-start(bf16[128,1024]{1,0:T(8,128)(2,1)} %bitcast.14), channel_id=1, source_target_pairs={{4,0},{8,4},{12,8},{5,1},{9,5},{13,9},{6,2},{10,6},{14,10},{7,3},{... | collective-permute-start | bytes 786440 | tf_op jit(solution)/shard_map/ppermute | solution.py:19
  12.6 14.9 %collective-permute-start.1 = (bf16[128,1024]{1,0:T(8,128)(2,1)S(1)}, bf16[128,1024]{1,0:T(8,128)(2,1)S(1)}, u32[]{:S(2)}, u32[]{:S(2)}) collective-permute-start(bf16[128,1024]{1,0:T(8,128)(2,1)S(1)} %collective-permute-done.refs_4_.refs_8_), channel_id=1, source_target_pairs={{0,4},{4,8},{8,12},{1,5},{5,9},{9,13},{2,6},{6,10},{10,14},{3,7},{... | collective-permute-start | bytes 786440 | tf_op jit(solution)/shard_map/ppermute | solution.py:19
  18.2 10.0 %collective-permute-start.3 = (bf16[128,1024]{1,0:T(8,128)(2,1)S(1)}, bf16[128,1024]{1,0:T(8,128)(2,1)S(1)}, u32[]{:S(2)}, u32[]{:S(2)}) collective-permute-start(bf16[128,1024]{1,0:T(8,128)(2,1)S(1)} %collective-permute-done.2.refs_5_.refs_11_), channel_id=1, source_target_pairs={{0,4},{4,8},{8,12},{1,5},{5,9},{9,13},{2,6},{6,10},{10,14},{3,7},{... | collective-permute-start | bytes 786440 | tf_op jit(solution)/shard_map/ppermute | solution.py:19
  22.5 8.3 %collective-permute-start.5 = (bf16[128,1024]{1,0:T(8,128)(2,1)S(1)}, bf16[128,1024]{1,0:T(8,128)(2,1)S(1)}, u32[]{:S(2)}, u32[]{:S(2)}) collective-permute-start(bf16[128,1024]{1,0:T(8,128)(2,1)S(1)} %collective-permute-done.4.refs_7_.refs_2_), channel_id=1, source_target_pairs={{4,0},{8,4},{12,8},{5,1},{9,5},{13,9},{6,2},{10,6},{14,10},{7,3},{... | collective-permute-start | bytes 786440 | tf_op jit(solution)/shard_map/ppermute | solution.py:19
  23.8 0.7 %copy-start.3 = (s32[1,4]{1,0:T(1,128)S(1)}, s32[1,4]{1,0:T(1,128)}, u32[]{:S(2)}) copy-start(s32[1,4]{1,0:T(1,128)} %refs_0_.1) | copy-start | bytes 52
  27.5 0.7 %copy-start.1 = (f32[1024]{0:T(1024)S(1)}, f32[1024]{0:T(1024)}, u32[]{:S(2)}) copy-start(f32[1024]{0:T(1024)} %param.15) | copy-start | bytes 12292
  29.2 9.8 %collective-permute-start.6 = (bf16[128,1024]{1,0:T(8,128)(2,1)S(1)}, bf16[128,1024]{1,0:T(8,128)(2,1)S(1)}, u32[]{:S(2)}, u32[]{:S(2)}) collective-permute-start(bf16[128,1024]{1,0:T(8,128)(2,1)S(1)} %get-tuple-element.54.refs_6_.refs_3_), channel_id=1, source_target_pairs={{4,0},{8,4},{12,8},{5,1},{9,5},{13,9},{6,2},{10,6},{14,10},{7,3},{... | collective-permute-start | bytes 786440 | tf_op jit(solution)/shard_map/ppermute | solution.py:19
  33.1 1.9 %collective-permute-start.7 = (f32[16,128]{1,0:T(8,128)S(1)}, f32[16,128]{1,0:T(8,128)S(1)}, u32[]{:S(2)}, u32[]{:S(2)}) collective-permute-start(f32[16,128]{1,0:T(8,128)S(1)} %get-tuple-element.78), channel_id=1, source_target_pairs={{0,1},{1,0},{2,3},{3,2},{4,5},{5,4},{6,7},{7,6},{8,9},{9,8},{10,11... | collective-permute-start | bytes 24584 | tf_op jit(solution)/shard_map/ppermute | solution.py:352
  33.1 3.7 %collective-permute-start.8 = (f32[16,128]{1,0:T(8,128)S(1)}, f32[16,128]{1,0:T(8,128)S(1)}, u32[]{:S(2)}, u32[]{:S(2)}) collective-permute-start(f32[16,128]{1,0:T(8,128)S(1)} %get-tuple-element.78), channel_id=1, source_target_pairs={{0,2},{1,3},{2,0},{3,1},{4,6},{5,7},{6,4},{7,5},{8,10},{9,11},{10,... | collective-permute-start | bytes 24584 | tf_op jit(solution)/shard_map/ppermute | solution.py:352
  34.6 3.1 %collective-permute-start.9 = (f32[16,128]{1,0:T(8,128)S(1)}, f32[16,128]{1,0:T(8,128)S(1)}, u32[]{:S(2)}, u32[]{:S(2)}) collective-permute-start(f32[16,128]{1,0:T(8,128)S(1)} %get-tuple-element.78), channel_id=1, source_target_pairs={{0,3},{1,2},{2,1},{3,0},{4,7},{5,6},{6,5},{7,4},{8,11},{9,10},{10,... | collective-permute-start | bytes 24584 | tf_op jit(solution)/shard_map/ppermute | solution.py:352
  39.0 10.4 %collective-permute-start.10 = (bf16[128,1024]{1,0:T(8,128)(2,1)S(1)}, bf16[128,1024]{1,0:T(8,128)(2,1)S(1)}, u32[]{:S(2)}, u32[]{:S(2)}) collective-permute-start(bf16[128,1024]{1,0:T(8,128)(2,1)S(1)} %collective-permute-done.6.refs_3_), channel_id=1, source_target_pairs={{4,0},{8,4},{12,8},{5,1},{9,5},{13,9},{6,2},{10,6},{14,10},{7,3},{... | collective-permute-start | bytes 786440 | tf_op jit(solution)/shard_map/ppermute | solution.py:19
  42.8 8.1 %collective-permute-start.11 = (f32[16,128]{1,0:T(8,128)S(1)}, f32[16,128]{1,0:T(8,128)S(1)}, u32[]{:S(2)}, u32[]{:S(2)}) collective-permute-start(f32[16,128]{1,0:T(8,128)S(1)} %add_add_fusion.refs_0_), channel_id=1, source_target_pairs={{0,4},{4,0},{8,12},{12,8},{1,5},{5,1},{9,13},{13,9},{2,6},{6,2},{1... | collective-permute-start | bytes 24584 | tf_op jit(solution)/shard_map/ppermute | solution.py:352
  45.6 5.4 %collective-permute-start.12 = (f32[16,128]{1,0:T(8,128)S(1)}, f32[16,128]{1,0:T(8,128)S(1)}, u32[]{:S(2)}, u32[]{:S(2)}) collective-permute-start(f32[16,128]{1,0:T(8,128)S(1)} %add_add_fusion.refs_0_), channel_id=1, source_target_pairs={{0,8},{4,12},{8,0},{12,4},{1,9},{5,13},{9,1},{13,5},{2,10},{6,14},... | collective-permute-start | bytes 24584 | tf_op jit(solution)/shard_map/ppermute | solution.py:352
  48.7 5.4 %collective-permute-start.13 = (f32[16,128]{1,0:T(8,128)S(1)}, f32[16,128]{1,0:T(8,128)S(1)}, u32[]{:S(2)}, u32[]{:S(2)}) collective-permute-start(f32[16,128]{1,0:T(8,128)S(1)} %add_add_fusion.refs_0_), channel_id=1, source_target_pairs={{0,12},{4,8},{8,4},{12,0},{1,13},{5,9},{9,5},{13,1},{2,14},{6,10},... | collective-permute-start | bytes 24584 | tf_op jit(solution)/shard_map/ppermute | solution.py:352
  54.2 1.0 %copy-start = (bf16[128,1024]{1,0:T(8,128)(2,1)S(1)}, bf16[128,1024]{1,0:T(8,128)(2,1)}, u32[]{:S(2)}) copy-start(bf16[128,1024]{1,0:T(8,128)(2,1)} %get-tuple-element.75.refs_4_) | copy-start | bytes 786436

commit v10 on v9

--- a/solution.py
+++ b/solution.py
@@ -348,10 +348,11 @@
 
 def exchanged(array, axis, distances):
     size = lax.axis_size(axis)
-    return [array] + [
+    found = [
         lax.ppermute(array, axis, [(i, i ^ distance) for i in range(size)])
-        for distance in distances
+        for distance in reversed(distances)
     ]
+    return [array] + found[::-1]
 
 
 def added_up(pieces):
@@ -456,11 +457,11 @@
         far_outs=2,
         scratch=[pltpu.VMEM((rows, features), BF16)] * 2 + [pltpu.SemaphoreType.DMA((heads,))],
     )
+    key_grad, value_grad, pieces[0] = lax.optimization_barrier((key_grad, value_grad, pieces[0]))
     gain_grad, bias_grad = on_device(
         sum_kernel,
         [jax.ShapeDtypeStruct((8, lanes), F32), jax.ShapeDtypeStruct((levels, heads), F32)],
-        pieces,
-        ahead=[key_grad],
+        pieces[::-1],
     )
     return (
         query_grad[None],

time: 56.1 us -> 53.7 us (0.957)
  waiting for transfers between devices: 12.4 us -> 10.8 us
  local copies, waits for them, and re-layouts: 1.6 us -> 0.65 us
    ppermute x6, waiting for transfers between devices: 5.95 us -> 4.59 us  [exchanged(): lax.ppermute(array, axis, [(i, i ^ distance) for i in range(size)])]
    unnamed x8 -> x6, local copies, waits for them, and re-layouts: 1.6 us -> 0.65 us
  transfers between devices with their start and end apart: 14 -> 14, of which waited for: 10 -> 10; matrix products, arithmetic and copies ran while one was open for 0% -> 0% of each run, Pallas kernels for 19% -> 20%
where the time goes in v10:
time: 53.7 us; the launch traced here: 53.3 us
  starting transfers between devices  30 us (56%)
  Pallas kernels  11 us (20%)
  waiting for transfers between devices  10.8 us (20%)
  between operations  0.8 us (1%)
  local copies, waits for them, and re-layouts  0.65 us (1%)
    ppermute x8, starting transfers between devices, passed_along(): return lax.ppermute(array, axis, pairs)  22.2 us
    pallas_call x8, Pallas kernels, on_device(): pl.pallas_call(body, out_shape=outs, in_specs=[pl.BlockSpec(memory_space=...  11 us
    ppermute x6, starting transfers between devices, exchanged(): lax.ppermute(array, axis, [(i, i ^ distance) for i in range(size)])  7.82 us
    ppermute x8, waiting for transfers between devices, passed_along(): return lax.ppermute(array, axis, pairs)  6.26 us
    ppermute x6, waiting for transfers between devices, exchanged(): lax.ppermute(array, axis, [(i, i ^ distance) for i in range(size)])  4.59 us
  transfers between devices with their start and end apart: 14, of which 10 were waited for; matrix products, arithmetic and copies ran while one was open for 0% of the time, Pallas kernels for 20%

profile of v10, /device:TPU:0, one launch (start us, length us, event | category | flops | bytes accessed | tf_op | source)
XLA Modules:
  0.0 53.3 jit_solution(4356974505708380170)
XLA Ops:
  0.6 0.0 copy-start.1
  0.6 4.9 %collective-permute-start = (bf16[128,1024]{1,0:T(8,128)(2,1)}, bf16[128,1024]{1,0:T(8,128)(2,1)S(1)}, u32[]{:S(2)}, u32[]{:S(2)}) collective-permute-start(bf16[128,1024]{1,0:T(8,128)(2,1)} %bitcast.15), channel_id=1, source_target_pairs={{0,4},{4,8},{8,12},{1,5},{5,9},{9,13},{2,6},{6,10},{10,14},{3,7},{... | collective-permute-start | bytes 786440 | tf_op jit(solution)/shard_map/ppermute | solution.py:19
  5.6 3.5 %collective-permute-start.2 = (bf16[128,1024]{1,0:T(8,128)(2,1)}, bf16[128,1024]{1,0:T(8,128)(2,1)S(1)}, u32[]{:S(2)}, u32[]{:S(2)}) collective-permute-start(bf16[128,1024]{1,0:T(8,128)(2,1)} %bitcast.17), channel_id=1, source_target_pairs={{0,4},{4,8},{8,12},{1,5},{5,9},{9,13},{2,6},{6,10},{10,14},{3,7},{... | collective-permute-start | bytes 786440 | tf_op jit(solution)/shard_map/ppermute | solution.py:19
  9.1 1.3 %collective-permute-start.4 = (bf16[128,1024]{1,0:T(8,128)(2,1)}, bf16[128,1024]{1,0:T(8,128)(2,1)S(1)}, u32[]{:S(2)}, u32[]{:S(2)}) collective-permute-start(bf16[128,1024]{1,0:T(8,128)(2,1)} %bitcast.13), channel_id=1, source_target_pairs={{4,0},{8,4},{12,8},{5,1},{9,5},{13,9},{6,2},{10,6},{14,10},{7,3},{... | collective-permute-start | bytes 786440 | tf_op jit(solution)/shard_map/ppermute | solution.py:19
  10.4 2.2 %collective-permute-done.refs_4_.refs_8_ = bf16[128,1024]{1,0:T(8,128)(2,1)S(1)} collective-permute-done((bf16[128,1024]{1,0:T(8,128)(2,1)}, bf16[128,1024]{1,0:T(8,128)(2,1)S(1)}, u32[]{:S(2)}, u32[]{:S(2)}) %collective-permute-start) | collective-permute-done | bytes 262176 | tf_op jit(solution)/shard_map/ppermute | solution.py:19
  12.6 4.3 %collective-permute-start.1 = (bf16[128,1024]{1,0:T(8,128)(2,1)S(1)}, bf16[128,1024]{1,0:T(8,128)(2,1)S(1)}, u32[]{:S(2)}, u32[]{:S(2)}) collective-permute-start(bf16[128,1024]{1,0:T(8,128)(2,1)S(1)} %collective-permute-done.refs_4_.refs_8_), channel_id=1, source_target_pairs={{0,4},{4,8},{8,12},{1,5},{5,9},{9,13},{2,6},{6,10},{10,14},{3,7},{... | collective-permute-start | bytes 786440 | tf_op jit(solution)/shard_map/ppermute | solution.py:19
  16.9 1.3 %collective-permute-done.2.refs_5_.refs_11_ = bf16[128,1024]{1,0:T(8,128)(2,1)S(1)} collective-permute-done((bf16[128,1024]{1,0:T(8,128)(2,1)}, bf16[128,1024]{1,0:T(8,128)(2,1)S(1)}, u32[]{:S(2)}, u32[]{:S(2)}) %collective-permute-start.2) | collective-permute-done | bytes 262176 | tf_op jit(solution)/shard_map/ppermute | solution.py:19
  18.2 4.3 %collective-permute-start.3 = (bf16[128,1024]{1,0:T(8,128)(2,1)S(1)}, bf16[128,1024]{1,0:T(8,128)(2,1)S(1)}, u32[]{:S(2)}, u32[]{:S(2)}) collective-permute-start(bf16[128,1024]{1,0:T(8,128)(2,1)S(1)} %collective-permute-done.2.refs_5_.refs_11_), channel_id=1, source_target_pairs={{0,4},{4,8},{8,12},{1,5},{5,9},{9,13},{2,6},{6,10},{10,14},{3,7},{... | collective-permute-start | bytes 786440 | tf_op jit(solution)/shard_map/ppermute | solution.py:19
  22.5 0.0 collective-permute-done.4.refs_7_.refs_2_
  22.5 1.3 %collective-permute-start.5 = (bf16[128,1024]{1,0:T(8,128)(2,1)S(1)}, bf16[128,1024]{1,0:T(8,128)(2,1)S(1)}, u32[]{:S(2)}, u32[]{:S(2)}) collective-permute-start(bf16[128,1024]{1,0:T(8,128)(2,1)S(1)} %collective-permute-done.4.refs_7_.refs_2_), channel_id=1, source_target_pairs={{4,0},{8,4},{12,8},{5,1},{9,5},{13,9},{6,2},{10,6},{14,10},{7,3},{... | collective-permute-start | bytes 786440 | tf_op jit(solution)/shard_map/ppermute | solution.py:19
  23.8 0.0 copy-start.2
  23.8 0.0 copy-done.1
  23.8 0.6 %copy-done.2 = s32[1,4]{1,0:T(1,128)S(1)} copy-done((s32[1,4]{1,0:T(1,128)S(1)}, s32[1,4]{1,0:T(1,128)}, u32[]{:S(2)}) %copy-start.2) | copy-done | bytes 40
  24.5 2.5 %shard_map.127 = (f32[64,128]{1,0:T(8,128)S(1)}, f32[1024,128]{1,0:T(8,128)S(1)}, f32[128,128]{1,0:T(8,128)S(1)}, f32[128,128]{1,0:T(8,128)S(1)}, f32[128,128]{1...) custom-call(s32[1,4]{1,0:T(1,128)S(1)} %copy-done.2, ...), custom_call_target="tpu_custom_call" | custom-call | flops 1000000 | bytes 100000 | tf_op jit(solution)/shard_map/pallas_call | solution.py:323
  26.9 0.6 %shard_map.128.refs_6_ = f32[128,1024]{1,0:T(8,128)S(1)} custom-call(f32[64,128]{1,0:T(8,128)S(1)} %get-tuple-element.48.refs_0_, f32[1024,128]{1,0:T(8,128)S(1)} %get-tuple-element.49.refs_1_, f32[128,128]{1,0:T(8,128)S(1)} %get-tuple-element.51.refs_2_.refs_3_, bf16[128,1024]{1,0:T(8,128)(2,1)S(1)} %get-tuple-element.53.refs_3_.refs_5_.refs_2_, ...), custom_call_target="tpu_custom_call" | custom-call | flops 1000000 | bytes 100000 | tf_op jit(solution)/shard_map/pallas_call | solution.py:323
  27.5 0.0 copy-start
  27.5 0.0 collective-permute-done.1.refs_4_.refs_9_
  27.5 0.7 %collective-permute-done.3.refs_5_.refs_12_ = bf16[128,1024]{1,0:T(8,128)(2,1)S(1)} collective-permute-done((bf16[128,1024]{1,0:T(8,128)(2,1)S(1)}, bf16[128,1024]{1,0:T(8,128)(2,1)S(1)}, u32[]{:S(2)}, u32[]{:S(2)}) %collective-permute-start.3) | collective-permute-done | bytes 262176 | tf_op jit(solution)/shard_map/ppermute | solution.py:19
  28.2 0.0 copy-done
  28.2 1.0 %shard_map.129 = (f32[128,1024]{1,0:T(8,128)S(1)}, bf16[128,1024]{1,0:T(8,128)(2,1)S(1)}, f32[1,1024]{1,0:T(1,128)S(1)}) custom-call(f32[64,128]{1,0:T(8,128)S(1)} %get-tuple-element.48.refs_0_, f32[1024,128]{1,0:T(8,128)S(1)} %get-tuple-element.49.refs_1_, f32[128,128]{1,0:T(8,128)S(1)} %get-tuple-element.52.refs_2_.refs_4_, ...), custom_call_target="tpu_custom_call" | custom-call | flops 1000000 | bytes 100000 | tf_op jit(solution)/shard_map/pallas_call | solution.py:323
  29.2 1.3 %collective-permute-start.6 = (bf16[128,1024]{1,0:T(8,128)(2,1)S(1)}, bf16[128,1024]{1,0:T(8,128)(2,1)S(1)}, u32[]{:S(2)}, u32[]{:S(2)}) collective-permute-start(bf16[128,1024]{1,0:T(8,128)(2,1)S(1)} %get-tuple-element.57.refs_6_.refs_3_), channel_id=1, source_target_pairs={{4,0},{8,4},{12,8},{5,1},{9,5},{13,9},{6,2},{10,6},{14,10},{7,3},{... | collective-permute-start | bytes 786440 | tf_op jit(solution)/shard_map/ppermute | solution.py:19
  30.5 0.3 collective-permute-done.5.refs_14_.refs_2_
  30.8 2.4 %shard_map.130 = (bf16[128,1024]{1,0:T(8,128)(2,1)}, f32[16,128]{1,0:T(8,128)S(1)}) custom-call(f32[64,128]{1,0:T(8,128)S(1)} %get-tuple-element.48.refs_0_, f32[1024,128]{1,0:T(8,128)S(1)} %get-tuple-element.49.refs_1_, f32[128,128]{1,0:T(8,128)S(1)} %get-tuple-element.50.refs_2_, f32[128,128]{1,0:T(8,128)S(1)} %get-tuple-element.51.refs_2_.refs_3_, ...), custom_call_target="tpu_custom_call" | custom-call | flops 1000000 | bytes 100000 | tf_op jit(solution)/shard_map/pallas_call | solution.py:323
  33.1 0.0 collective-permute-start.7
  33.1 1.5 %collective-permute-start.8 = (f32[16,128]{1,0:T(8,128)S(1)}, f32[16,128]{1,0:T(8,128)S(1)}, u32[]{:S(2)}, u32[]{:S(2)}) collective-permute-start(f32[16,128]{1,0:T(8,128)S(1)} %get-tuple-element.80), channel_id=1, source_target_pairs={{0,2},{1,3},{2,0},{3,1},{4,6},{5,7},{6,4},{7,5},{8,10},{9,11},{10,... | collective-permute-start | bytes 24584 | tf_op jit(solution)/shard_map/ppermute | solution.py:352
  34.6 0.4 collective-permute-start.9
  35.0 0.0 collective-permute-done.7.refs_6_
  35.0 1.8 %collective-permute-done.8 = f32[16,128]{1,0:T(8,128)S(1)} collective-permute-done((f32[16,128]{1,0:T(8,128)S(1)}, f32[16,128]{1,0:T(8,128)S(1)}, u32[]{:S(2)}, u32[]{:S(2)}) %collective-permute-start.8) | collective-permute-done | bytes 8224 | tf_op jit(solution)/shard_map/ppermute | solution.py:352
  36.8 0.9 %collective-permute-done.9 = f32[16,128]{1,0:T(8,128)S(1)} collective-permute-done((f32[16,128]{1,0:T(8,128)S(1)}, f32[16,128]{1,0:T(8,128)S(1)}, u32[]{:S(2)}, u32[]{:S(2)}) %collective-permute-start.9) | collective-permute-done | bytes 8224 | tf_op jit(solution)/shard_map/ppermute | solution.py:352
  37.7 1.3 %collective-permute-done.6.refs_3_ = bf16[128,1024]{1,0:T(8,128)(2,1)S(1)} collective-permute-done((bf16[128,1024]{1,0:T(8,128)(2,1)S(1)}, bf16[128,1024]{1,0:T(8,128)(2,1)S(1)}, u32[]{:S(2)}, u32[]{:S(2)}) %collective-permute-start.6) | collective-permute-done | bytes 262176 | tf_op jit(solution)/shard_map/ppermute | solution.py:19
  39.0 1.3 %collective-permute-start.10 = (bf16[128,1024]{1,0:T(8,128)(2,1)S(1)}, bf16[128,1024]{1,0:T(8,128)(2,1)S(1)}, u32[]{:S(2)}, u32[]{:S(2)}) collective-permute-start(bf16[128,1024]{1,0:T(8,128)(2,1)S(1)} %collective-permute-done.6.refs_3_), channel_id=1, source_target_pairs={{4,0},{8,4},{12,8},{5,1},{9,5},{13,9},{6,2},{10,6},{14,10},{7,3},{... | collective-permute-start | bytes 786440 | tf_op jit(solution)/shard_map/ppermute | solution.py:19
  40.3 0.9 %shard_map.131 = (f32[128,1024]{1,0:T(8,128)S(1)}, f32[128,1024]{1,0:T(8,128)S(1)}) custom-call(f32[64,128]{1,0:T(8,128)S(1)} %get-tuple-element.48.refs_0_, f32[128,128]{1,0:T(8,128)S(1)} %get-tuple-element.66.refs_1_, bf16[128,1024]{1,0:T(8,128)(2,1)S(1)} %get-tuple-element.53.refs_3_.refs_5_.refs_2_, ...), custom_call_target="tpu_custom_call" | custom-call | flops 1000000 | bytes 100000 | tf_op jit(solution)/shard_map/pallas_call | solution.py:323
  41.2 1.6 %shard_map.132 = (bf16[128,1024]{1,0:T(8,128)(2,1)}, f32[128,1024]{1,0:T(8,128)S(1)}, f32[128,1024]{1,0:T(8,128)S(1)}) custom-call(f32[64,128]{1,0:T(8,128)S(1)} %get-tuple-element.48.refs_0_, f32[128,128]{1,0:T(8,128)S(1)} %get-tuple-element.65.refs_1_, bf16[128,1024]{1,0:T(8,128)(2,1)S(1)} %collective-permute-done.4.refs_7_.refs_2_, ...), custom_call_target="tpu_custom_call" | custom-call | flops 1000000 | bytes 100000 | tf_op jit(solution)/shard_map/pallas_call | solution.py:323
  42.8 5.3 %collective-permute-start.11 = (f32[16,128]{1,0:T(8,128)S(1)}, f32[16,128]{1,0:T(8,128)S(1)}, u32[]{:S(2)}, u32[]{:S(2)}) collective-permute-start(f32[16,128]{1,0:T(8,128)S(1)} %add_add_fusion.refs_3_), channel_id=1, source_target_pairs={{0,12},{4,8},{8,4},{12,0},{1,13},{5,9},{9,5},{13,1},{2,14},{6,10},... | collective-permute-start | bytes 24584 | tf_op jit(solution)/shard_map/ppermute | solution.py:352
  48.2 0.0 collective-permute-start.12
  48.2 0.6 %collective-permute-start.13 = (f32[16,128]{1,0:T(8,128)S(1)}, f32[16,128]{1,0:T(8,128)S(1)}, u32[]{:S(2)}, u32[]{:S(2)}) collective-permute-start(f32[16,128]{1,0:T(8,128)S(1)} %add_add_fusion.refs_3_), channel_id=1, source_target_pairs={{0,4},{4,0},{8,12},{12,8},{1,5},{5,1},{9,13},{13,9},{2,6},{6,2},{1... | collective-permute-start | bytes 24584 | tf_op jit(solution)/shard_map/ppermute | solution.py:352
  48.8 0.5 collective-permute-done.10.refs_3_
  49.3 1.5 %shard_map.133 = (bf16[128,1024]{1,0:T(8,128)(2,1)}, bf16[128,1024]{1,0:T(8,128)(2,1)}) custom-call(f32[64,128]{1,0:T(8,128)S(1)} %get-tuple-element.48.refs_0_, f32[128,128]{1,0:T(8,128)S(1)} %get-tuple-element.62.refs_1_, bf16[128,1024]{1,0:T(8,128)(2,1)S(1)} %collective-permute-done.5.refs_14_.refs_2_, ...), custom_call_target="tpu_custom_call" | custom-call | flops 1000000 | bytes 100000 | tf_op jit(solution)/shard_map/pallas_call | solution.py:323
  50.8 1.3 %collective-permute-done.11.refs_0_ = f32[16,128]{1,0:T(8,128)S(1)} collective-permute-done((f32[16,128]{1,0:T(8,128)S(1)}, f32[16,128]{1,0:T(8,128)S(1)}, u32[]{:S(2)}, u32[]{:S(2)}) %collective-permute-start.11) | collective-permute-done | bytes 8224 | tf_op jit(solution)/shard_map/ppermute | solution.py:352
  52.2 0.5 %collective-permute-done.12.refs_1_ = f32[16,128]{1,0:T(8,128)S(1)} collective-permute-done((f32[16,128]{1,0:T(8,128)S(1)}, f32[16,128]{1,0:T(8,128)S(1)}, u32[]{:S(2)}, u32[]{:S(2)}) %collective-permute-start.12) | collective-permute-done | bytes 8224 | tf_op jit(solution)/shard_map/ppermute | solution.py:352
  52.7 0.0 collective-permute-done.13.refs_2_
  52.7 0.6 %shard_map.134 = (f32[8,128]{1,0:T(8,128)}, f32[8,8]{1,0:T(8,128)}) custom-call(f32[16,128]{1,0:T(8,128)S(1)} %collective-permute-done.11.refs_0_, f32[16,128]{1,0:T(8,128)S(1)} %collective-permute-done.12.refs_1_, f32[16,128]{1,0:T(8,128)S(1)} %collective-permute-done.13.refs_2_, f32[16,128]{1,0:T(8,128)S(1)} %add_add_fusion.refs_3_), custom_call_target="tpu_custom_call" | custom-call | flops 1000000 | bytes 100000 | tf_op jit(solution)/shard_map/pallas_call | solution.py:323
  (1 shorter events, 0.0 us)
Async XLA Ops:
  0.6 23.2 %copy-start.1 = (f32[8,8]{1,0:T(8,128)S(1)}, f32[8,8]{1,0:T(8,128)}, u32[]{:S(2)}) copy-start(f32[8,8]{1,0:T(8,128)} %refs_1_.1) | copy-start | bytes 772
  0.6 11.9 %collective-permute-start = (bf16[128,1024]{1,0:T(8,128)(2,1)}, bf16[128,1024]{1,0:T(8,128)(2,1)S(1)}, u32[]{:S(2)}, u32[]{:S(2)}) collective-permute-start(bf16[128,1024]{1,0:T(8,128)(2,1)} %bitcast.15), channel_id=1, source_target_pairs={{0,4},{4,8},{8,12},{1,5},{5,9},{9,13},{2,6},{6,10},{10,14},{3,7},{... | collective-permute-start | bytes 786440 | tf_op jit(solution)/shard_map/ppermute | solution.py:19
  5.6 12.6 %collective-permute-start.2 = (bf16[128,1024]{1,0:T(8,128)(2,1)}, bf16[128,1024]{1,0:T(8,128)(2,1)S(1)}, u32[]{:S(2)}, u32[]{:S(2)}) collective-permute-start(bf16[128,1024]{1,0:T(8,128)(2,1)} %bitcast.17), channel_id=1, source_target_pairs={{0,4},{4,8},{8,12},{1,5},{5,9},{9,13},{2,6},{6,10},{10,14},{3,7},{... | collective-permute-start | bytes 786440 | tf_op jit(solution)/shard_map/ppermute | solution.py:19
  9.1 13.4 %collective-permute-start.4 = (bf16[128,1024]{1,0:T(8,128)(2,1)}, bf16[128,1024]{1,0:T(8,128)(2,1)S(1)}, u32[]{:S(2)}, u32[]{:S(2)}) collective-permute-start(bf16[128,1024]{1,0:T(8,128)(2,1)} %bitcast.13), channel_id=1, source_target_pairs={{4,0},{8,4},{12,8},{5,1},{9,5},{13,9},{6,2},{10,6},{14,10},{7,3},{... | collective-permute-start | bytes 786440 | tf_op jit(solution)/shard_map/ppermute | solution.py:19
  12.6 14.9 %collective-permute-start.1 = (bf16[128,1024]{1,0:T(8,128)(2,1)S(1)}, bf16[128,1024]{1,0:T(8,128)(2,1)S(1)}, u32[]{:S(2)}, u32[]{:S(2)}) collective-permute-start(bf16[128,1024]{1,0:T(8,128)(2,1)S(1)} %collective-permute-done.refs_4_.refs_8_), channel_id=1, source_target_pairs={{0,4},{4,8},{8,12},{1,5},{5,9},{9,13},{2,6},{6,10},{10,14},{3,7},{... | collective-permute-start | bytes 786440 | tf_op jit(solution)/shard_map/ppermute | solution.py:19
  18.2 10.0 %collective-permute-start.3 = (bf16[128,1024]{1,0:T(8,128)(2,1)S(1)}, bf16[128,1024]{1,0:T(8,128)(2,1)S(1)}, u32[]{:S(2)}, u32[]{:S(2)}) collective-permute-start(bf16[128,1024]{1,0:T(8,128)(2,1)S(1)} %collective-permute-done.2.refs_5_.refs_11_), channel_id=1, source_target_pairs={{0,4},{4,8},{8,12},{1,5},{5,9},{9,13},{2,6},{6,10},{10,14},{3,7},{... | collective-permute-start | bytes 786440 | tf_op jit(solution)/shard_map/ppermute | solution.py:19
  22.5 8.3 %collective-permute-start.5 = (bf16[128,1024]{1,0:T(8,128)(2,1)S(1)}, bf16[128,1024]{1,0:T(8,128)(2,1)S(1)}, u32[]{:S(2)}, u32[]{:S(2)}) collective-permute-start(bf16[128,1024]{1,0:T(8,128)(2,1)S(1)} %collective-permute-done.4.refs_7_.refs_2_), channel_id=1, source_target_pairs={{4,0},{8,4},{12,8},{5,1},{9,5},{13,9},{6,2},{10,6},{14,10},{7,3},{... | collective-permute-start | bytes 786440 | tf_op jit(solution)/shard_map/ppermute | solution.py:19
  23.8 0.7 %copy-start.2 = (s32[1,4]{1,0:T(1,128)S(1)}, s32[1,4]{1,0:T(1,128)}, u32[]{:S(2)}) copy-start(s32[1,4]{1,0:T(1,128)} %refs_0_.1) | copy-start | bytes 52
  27.5 0.7 %copy-start = (f32[1024]{0:T(1024)S(1)}, f32[1024]{0:T(1024)}, u32[]{:S(2)}) copy-start(f32[1024]{0:T(1024)} %param.15) | copy-start | bytes 12292
  29.2 9.8 %collective-permute-start.6 = (bf16[128,1024]{1,0:T(8,128)(2,1)S(1)}, bf16[128,1024]{1,0:T(8,128)(2,1)S(1)}, u32[]{:S(2)}, u32[]{:S(2)}) collective-permute-start(bf16[128,1024]{1,0:T(8,128)(2,1)S(1)} %get-tuple-element.57.refs_6_.refs_3_), channel_id=1, source_target_pairs={{4,0},{8,4},{12,8},{5,1},{9,5},{13,9},{6,2},{10,6},{14,10},{7,3},{... | collective-permute-start | bytes 786440 | tf_op jit(solution)/shard_map/ppermute | solution.py:19
  33.1 1.9 %collective-permute-start.7 = (f32[16,128]{1,0:T(8,128)S(1)}, f32[16,128]{1,0:T(8,128)S(1)}, u32[]{:S(2)}, u32[]{:S(2)}) collective-permute-start(f32[16,128]{1,0:T(8,128)S(1)} %get-tuple-element.80), channel_id=1, source_target_pairs={{0,1},{1,0},{2,3},{3,2},{4,5},{5,4},{6,7},{7,6},{8,9},{9,8},{10,11... | collective-permute-start | bytes 24584 | tf_op jit(solution)/shard_map/ppermute | solution.py:352
  33.1 3.7 %collective-permute-start.8 = (f32[16,128]{1,0:T(8,128)S(1)}, f32[16,128]{1,0:T(8,128)S(1)}, u32[]{:S(2)}, u32[]{:S(2)}) collective-permute-start(f32[16,128]{1,0:T(8,128)S(1)} %get-tuple-element.80), channel_id=1, source_target_pairs={{0,2},{1,3},{2,0},{3,1},{4,6},{5,7},{6,4},{7,5},{8,10},{9,11},{10,... | collective-permute-start | bytes 24584 | tf_op jit(solution)/shard_map/ppermute | solution.py:352
  34.6 3.1 %collective-permute-start.9 = (f32[16,128]{1,0:T(8,128)S(1)}, f32[16,128]{1,0:T(8,128)S(1)}, u32[]{:S(2)}, u32[]{:S(2)}) collective-permute-start(f32[16,128]{1,0:T(8,128)S(1)} %get-tuple-element.80), channel_id=1, source_target_pairs={{0,3},{1,2},{2,1},{3,0},{4,7},{5,6},{6,5},{7,4},{8,11},{9,10},{10,... | collective-permute-start | bytes 24584 | tf_op jit(solution)/shard_map/ppermute | solution.py:352
  39.0 10.3 %collective-permute-start.10 = (bf16[128,1024]{1,0:T(8,128)(2,1)S(1)}, bf16[128,1024]{1,0:T(8,128)(2,1)S(1)}, u32[]{:S(2)}, u32[]{:S(2)}) collective-permute-start(bf16[128,1024]{1,0:T(8,128)(2,1)S(1)} %collective-permute-done.6.refs_3_), channel_id=1, source_target_pairs={{4,0},{8,4},{12,8},{5,1},{9,5},{13,9},{6,2},{10,6},{14,10},{7,3},{... | collective-permute-start | bytes 786440 | tf_op jit(solution)/shard_map/ppermute | solution.py:19
  42.8 9.3 %collective-permute-start.11 = (f32[16,128]{1,0:T(8,128)S(1)}, f32[16,128]{1,0:T(8,128)S(1)}, u32[]{:S(2)}, u32[]{:S(2)}) collective-permute-start(f32[16,128]{1,0:T(8,128)S(1)} %add_add_fusion.refs_3_), channel_id=1, source_target_pairs={{0,12},{4,8},{8,4},{12,0},{1,13},{5,9},{9,5},{13,1},{2,14},{6,10},... | collective-permute-start | bytes 24584 | tf_op jit(solution)/shard_map/ppermute | solution.py:352
  48.2 4.5 %collective-permute-start.12 = (f32[16,128]{1,0:T(8,128)S(1)}, f32[16,128]{1,0:T(8,128)S(1)}, u32[]{:S(2)}, u32[]{:S(2)}) collective-permute-start(f32[16,128]{1,0:T(8,128)S(1)} %add_add_fusion.refs_3_), channel_id=1, source_target_pairs={{0,8},{4,12},{8,0},{12,4},{1,9},{5,13},{9,1},{13,5},{2,10},{6,14},... | collective-permute-start | bytes 24584 | tf_op jit(solution)/shard_map/ppermute | solution.py:352
  48.2 4.5 %collective-permute-start.13 = (f32[16,128]{1,0:T(8,128)S(1)}, f32[16,128]{1,0:T(8,128)S(1)}, u32[]{:S(2)}, u32[]{:S(2)}) collective-permute-start(f32[16,128]{1,0:T(8,128)S(1)} %add_add_fusion.refs_3_), channel_id=1, source_target_pairs={{0,4},{4,0},{8,12},{12,8},{1,5},{5,1},{9,13},{13,9},{2,6},{6,2},{1... | collective-permute-start | bytes 24584 | tf_op jit(solution)/shard_map/ppermute | solution.py:352

commit v11 on v10

--- a/solution.py
+++ b/solution.py
@@ -13,10 +13,10 @@
 BF16 = jnp.bfloat16
 
 
-def passed_along(array, axis, by):
+def passed_along(array, axis, by, hop=1):
     size = lax.axis_size(axis)
-    pairs = [(i, i + by) for i in range(size) if 0 <= i + by < size]
-    return lax.ppermute(array, axis, pairs)
+    first, last = (hop - 1, size - 2) if by > 0 else (1, size - hop)
+    return lax.ppermute(array, axis, [(i, i + by) for i in range(first, last + 1)])
 
 
 def contract(left, right, left_dim, right_dim):
@@ -392,9 +392,9 @@
     later_queries = [query, arrived[2]]
     keys, values = [key, arrived[0]], [value, arrived[1]]
     for hops in range(1, reach):
-        keys.append(passed_along(keys[-1], "ctx", 1))
-        values.append(passed_along(values[-1], "ctx", 1))
-        later_queries.append(passed_along(later_queries[-1], "ctx", -1))
+        keys.append(passed_along(keys[-1], "ctx", 1, hops + 1))
+        values.append(passed_along(values[-1], "ctx", 1, hops + 1))
+        later_queries.append(passed_along(later_queries[-1], "ctx", -1, hops + 1))
     for hops in range(1, reach):
         (attention,) = on_device(
             partial(forward_kernel, hops, heads, scaling),
@@ -432,7 +432,7 @@
     )
     for hops in range(1, reach):
         arrived, *pieces = lax.optimization_barrier((later_grads[hops], *pieces))
-        later_grads.append(passed_along(arrived, "ctx", -1))
+        later_grads.append(passed_along(arrived, "ctx", -1, hops + 1))
         if hops == 1:
             gate_grad, *key_grads = on_device(
                 partial(gate_and_key_kernel, hops, heads, scaling),

time: 53.7 us -> 52 us (0.968)
  starting transfers between devices: 30 us -> 22 us
  waiting for transfers between devices: 10.8 us -> 16.5 us
  local copies, waits for them, and re-layouts: 0.65 us -> 1.3 us
    ppermute x8, waiting for transfers between devices: 6.26 us -> 13.6 us  [passed_along(): lax.ppermute(array, axis, [(i, i + by) for i in range(first, last + 1)])]
    ppermute x8, starting transfers between devices: 22.2 us -> 14.9 us  [passed_along(): lax.ppermute(array, axis, [(i, i + by) for i in range(first, last + 1)])]
    ppermute x6, waiting for transfers between devices: 4.59 us -> 2.88 us  [exchanged(): lax.ppermute(array, axis, [(i, i ^ distance) for i in range(size)])]
    ppermute x6, starting transfers between devices: 7.82 us -> 7.06 us  [exchanged(): lax.ppermute(array, axis, [(i, i ^ distance) for i in range(size)])]
    unnamed x6, local copies, waits for them, and re-layouts: 0.65 us -> 1.3 us
  transfers between devices with their start and end apart: 14 -> 14, of which waited for: 10 -> 9; matrix products, arithmetic and copies ran while one was open for 0% -> 0% of each run, Pallas kernels for 20% -> 20%
where the time goes in v11:
time: 52 us; the launch traced here: 51.6 us
  starting transfers between devices  22 us (42%)
  waiting for transfers between devices  16.5 us (32%)
  Pallas kernels  11 us (21%)
  local copies, waits for them, and re-layouts  1.3 us (2%)
  between operations  0.81 us (2%)
    ppermute x8, starting transfers between devices, passed_along(): lax.ppermute(array, axis, [(i, i + by) for i in range(first, last + 1)])  14.9 us
    ppermute x8, waiting for transfers between devices, passed_along(): lax.ppermute(array, axis, [(i, i + by) for i in range(first, last + 1)])  13.6 us
    pallas_call x8, Pallas kernels, on_device(): pl.pallas_call(body, out_shape=outs, in_specs=[pl.BlockSpec(memory_space=...  11 us
    ppermute x6, starting transfers between devices, exchanged(): lax.ppermute(array, axis, [(i, i ^ distance) for i in range(size)])  7.06 us
    ppermute x6, waiting for transfers between devices, exchanged(): lax.ppermute(array, axis, [(i, i ^ distance) for i in range(size)])  2.88 us
    unnamed x6, local copies, waits for them, and re-layouts  1.3 us
  transfers between devices with their start and end apart: 14, of which 9 were waited for; matrix products, arithmetic and copies ran while one was open for 0% of the time, Pallas kernels for 20%

profile of v11, /device:TPU:0, one launch (start us, length us, event | category | flops | bytes accessed | tf_op | source)
XLA Modules:
  0.0 51.6 jit_solution(18154250363255857522)
XLA Ops:
  0.6 0.0 copy-start.1
  0.6 4.9 %collective-permute-start = (bf16[128,1024]{1,0:T(8,128)(2,1)}, bf16[128,1024]{1,0:T(8,128)(2,1)S(1)}, u32[]{:S(2)}, u32[]{:S(2)}) collective-permute-start(bf16[128,1024]{1,0:T(8,128)(2,1)} %bitcast.15), channel_id=1, source_target_pairs={{0,4},{4,8},{8,12},{1,5},{5,9},{9,13},{2,6},{6,10},{10,14},{3,7},{... | collective-permute-start | bytes 786440 | tf_op jit(solution)/shard_map/ppermute | solution.py:19
  5.6 3.5 %collective-permute-start.2 = (bf16[128,1024]{1,0:T(8,128)(2,1)}, bf16[128,1024]{1,0:T(8,128)(2,1)S(1)}, u32[]{:S(2)}, u32[]{:S(2)}) collective-permute-start(bf16[128,1024]{1,0:T(8,128)(2,1)} %bitcast.17), channel_id=1, source_target_pairs={{0,4},{4,8},{8,12},{1,5},{5,9},{9,13},{2,6},{6,10},{10,14},{3,7},{... | collective-permute-start | bytes 786440 | tf_op jit(solution)/shard_map/ppermute | solution.py:19
  9.1 1.3 %collective-permute-start.4 = (bf16[128,1024]{1,0:T(8,128)(2,1)}, bf16[128,1024]{1,0:T(8,128)(2,1)S(1)}, u32[]{:S(2)}, u32[]{:S(2)}) collective-permute-start(bf16[128,1024]{1,0:T(8,128)(2,1)} %bitcast.13), channel_id=1, source_target_pairs={{4,0},{8,4},{12,8},{5,1},{9,5},{13,9},{6,2},{10,6},{14,10},{7,3},{... | collective-permute-start | bytes 786440 | tf_op jit(solution)/shard_map/ppermute | solution.py:19
  10.4 2.2 %collective-permute-done.refs_4_.refs_8_ = bf16[128,1024]{1,0:T(8,128)(2,1)S(1)} collective-permute-done((bf16[128,1024]{1,0:T(8,128)(2,1)}, bf16[128,1024]{1,0:T(8,128)(2,1)S(1)}, u32[]{:S(2)}, u32[]{:S(2)}) %collective-permute-start) | collective-permute-done | bytes 262176 | tf_op jit(solution)/shard_map/ppermute | solution.py:19
  12.6 0.7 %collective-permute-start.1 = (bf16[128,1024]{1,0:T(8,128)(2,1)S(1)}, bf16[128,1024]{1,0:T(8,128)(2,1)S(1)}, u32[]{:S(2)}, u32[]{:S(2)}) collective-permute-start(bf16[128,1024]{1,0:T(8,128)(2,1)S(1)} %collective-permute-done.refs_4_.refs_8_), channel_id=1, source_target_pairs={{4,8},{8,12},{5,9},{9,13},{6,10},{10,14},{7,11},{11,15},{20,24},{2... | collective-permute-start | bytes 786440 | tf_op jit(solution)/shard_map/ppermute | solution.py:19
  13.3 3.8 %collective-permute-done.2.refs_5_.refs_11_ = bf16[128,1024]{1,0:T(8,128)(2,1)S(1)} collective-permute-done((bf16[128,1024]{1,0:T(8,128)(2,1)}, bf16[128,1024]{1,0:T(8,128)(2,1)S(1)}, u32[]{:S(2)}, u32[]{:S(2)}) %collective-permute-start.2) | collective-permute-done | bytes 262176 | tf_op jit(solution)/shard_map/ppermute | solution.py:19
  17.1 0.7 %collective-permute-start.3 = (bf16[128,1024]{1,0:T(8,128)(2,1)S(1)}, bf16[128,1024]{1,0:T(8,128)(2,1)S(1)}, u32[]{:S(2)}, u32[]{:S(2)}) collective-permute-start(bf16[128,1024]{1,0:T(8,128)(2,1)S(1)} %collective-permute-done.2.refs_5_.refs_11_), channel_id=1, source_target_pairs={{4,8},{8,12},{5,9},{9,13},{6,10},{10,14},{7,11},{11,15},{20,24},{2... | collective-permute-start | bytes 786440 | tf_op jit(solution)/shard_map/ppermute | solution.py:19
  17.7 0.9 %collective-permute-done.4.refs_7_.refs_2_ = bf16[128,1024]{1,0:T(8,128)(2,1)S(1)} collective-permute-done((bf16[128,1024]{1,0:T(8,128)(2,1)}, bf16[128,1024]{1,0:T(8,128)(2,1)S(1)}, u32[]{:S(2)}, u32[]{:S(2)}) %collective-permute-start.4) | collective-permute-done | bytes 262176 | tf_op jit(solution)/shard_map/ppermute | solution.py:19
  18.7 1.3 %collective-permute-start.5 = (bf16[128,1024]{1,0:T(8,128)(2,1)S(1)}, bf16[128,1024]{1,0:T(8,128)(2,1)S(1)}, u32[]{:S(2)}, u32[]{:S(2)}) collective-permute-start(bf16[128,1024]{1,0:T(8,128)(2,1)S(1)} %collective-permute-done.4.refs_7_.refs_2_), channel_id=1, source_target_pairs={{4,0},{8,4},{5,1},{9,5},{6,2},{10,6},{7,3},{11,7},{20,16},{24,20},... | collective-permute-start | bytes 786440 | tf_op jit(solution)/shard_map/ppermute | solution.py:19
  20.0 0.0 copy-start.2
  20.0 0.0 copy-done.1
  20.0 0.6 %copy-done.2 = s32[1,4]{1,0:T(1,128)S(1)} copy-done((s32[1,4]{1,0:T(1,128)S(1)}, s32[1,4]{1,0:T(1,128)}, u32[]{:S(2)}) %copy-start.2) | copy-done | bytes 40
  20.6 2.5 %shard_map.127 = (f32[64,128]{1,0:T(8,128)S(1)}, f32[1024,128]{1,0:T(8,128)S(1)}, f32[128,128]{1,0:T(8,128)S(1)}, f32[128,128]{1,0:T(8,128)S(1)}, f32[128,128]{1...) custom-call(s32[1,4]{1,0:T(1,128)S(1)} %copy-done.2, ...), custom_call_target="tpu_custom_call" | custom-call | flops 1000000 | bytes 100000 | tf_op jit(solution)/shard_map/pallas_call | solution.py:323
  23.1 0.6 %shard_map.128.refs_6_ = f32[128,1024]{1,0:T(8,128)S(1)} custom-call(f32[64,128]{1,0:T(8,128)S(1)} %get-tuple-element.48.refs_0_, f32[1024,128]{1,0:T(8,128)S(1)} %get-tuple-element.49.refs_1_, f32[128,128]{1,0:T(8,128)S(1)} %get-tuple-element.51.refs_2_.refs_3_, bf16[128,1024]{1,0:T(8,128)(2,1)S(1)} %get-tuple-element.53.refs_3_.refs_5_.refs_2_, ...), custom_call_target="tpu_custom_call" | custom-call | flops 1000000 | bytes 100000 | tf_op jit(solution)/shard_map/pallas_call | solution.py:323
  23.7 0.0 copy-start
  23.7 0.0 collective-permute-done.1.refs_4_.refs_9_
  23.7 0.0 collective-permute-done.3.refs_5_.refs_12_
  23.7 0.7 %copy-done = f32[1024]{0:T(1024)S(1)} copy-done((f32[1024]{0:T(1024)S(1)}, f32[1024]{0:T(1024)}, u32[]{:S(2)}) %copy-start) | copy-done | bytes 4120
  24.3 1.0 %shard_map.129 = (f32[128,1024]{1,0:T(8,128)S(1)}, bf16[128,1024]{1,0:T(8,128)(2,1)S(1)}, f32[1,1024]{1,0:T(1,128)S(1)}) custom-call(f32[64,128]{1,0:T(8,128)S(1)} %get-tuple-element.48.refs_0_, f32[1024,128]{1,0:T(8,128)S(1)} %get-tuple-element.49.refs_1_, f32[128,128]{1,0:T(8,128)S(1)} %get-tuple-element.52.refs_2_.refs_4_, ...), custom_call_target="tpu_custom_call" | custom-call | flops 1000000 | bytes 100000 | tf_op jit(solution)/shard_map/pallas_call | solution.py:323
  25.3 1.3 %collective-permute-start.6 = (bf16[128,1024]{1,0:T(8,128)(2,1)S(1)}, bf16[128,1024]{1,0:T(8,128)(2,1)S(1)}, u32[]{:S(2)}, u32[]{:S(2)}) collective-permute-start(bf16[128,1024]{1,0:T(8,128)(2,1)S(1)} %get-tuple-element.57.refs_6_.refs_3_), channel_id=1, source_target_pairs={{4,0},{8,4},{12,8},{5,1},{9,5},{13,9},{6,2},{10,6},{14,10},{7,3},{... | collective-permute-start | bytes 786440 | tf_op jit(solution)/shard_map/ppermute | solution.py:19
  26.6 3.7 %collective-permute-done.5.refs_14_.refs_2_ = bf16[128,1024]{1,0:T(8,128)(2,1)S(1)} collective-permute-done((bf16[128,1024]{1,0:T(8,128)(2,1)S(1)}, bf16[128,1024]{1,0:T(8,128)(2,1)S(1)}, u32[]{:S(2)}, u32[]{:S(2)}) %collective-permute-start.5) | collective-permute-done | bytes 262176 | tf_op jit(solution)/shard_map/ppermute | solution.py:19
  30.3 2.4 %shard_map.130 = (bf16[128,1024]{1,0:T(8,128)(2,1)}, f32[16,128]{1,0:T(8,128)S(1)}) custom-call(f32[64,128]{1,0:T(8,128)S(1)} %get-tuple-element.48.refs_0_, f32[1024,128]{1,0:T(8,128)S(1)} %get-tuple-element.49.refs_1_, f32[128,128]{1,0:T(8,128)S(1)} %get-tuple-element.50.refs_2_, f32[128,128]{1,0:T(8,128)S(1)} %get-tuple-element.51.refs_2_.refs_3_, ...), custom_call_target="tpu_custom_call" | custom-call | flops 1000000 | bytes 100000 | tf_op jit(solution)/shard_map/pallas_call | solution.py:323
  32.7 0.0 collective-permute-start.7
  32.7 1.5 %collective-permute-start.8 = (f32[16,128]{1,0:T(8,128)S(1)}, f32[16,128]{1,0:T(8,128)S(1)}, u32[]{:S(2)}, u32[]{:S(2)}) collective-permute-start(f32[16,128]{1,0:T(8,128)S(1)} %get-tuple-element.80), channel_id=1, source_target_pairs={{0,2},{1,3},{2,0},{3,1},{4,6},{5,7},{6,4},{7,5},{8,10},{9,11},{10,... | collective-permute-start | bytes 24584 | tf_op jit(solution)/shard_map/ppermute | solution.py:352
  34.2 0.4 collective-permute-start.9
  34.6 0.0 collective-permute-done.7.refs_6_
  34.6 1.8 %collective-permute-done.8 = f32[16,128]{1,0:T(8,128)S(1)} collective-permute-done((f32[16,128]{1,0:T(8,128)S(1)}, f32[16,128]{1,0:T(8,128)S(1)}, u32[]{:S(2)}, u32[]{:S(2)}) %collective-permute-start.8) | collective-permute-done | bytes 8224 | tf_op jit(solution)/shard_map/ppermute | solution.py:352
  36.4 0.9 %collective-permute-done.9 = f32[16,128]{1,0:T(8,128)S(1)} collective-permute-done((f32[16,128]{1,0:T(8,128)S(1)}, f32[16,128]{1,0:T(8,128)S(1)}, u32[]{:S(2)}, u32[]{:S(2)}) %collective-permute-start.9) | collective-permute-done | bytes 8224 | tf_op jit(solution)/shard_map/ppermute | solution.py:352
  37.3 0.8 %collective-permute-done.6.refs_3_ = bf16[128,1024]{1,0:T(8,128)(2,1)S(1)} collective-permute-done((bf16[128,1024]{1,0:T(8,128)(2,1)S(1)}, bf16[128,1024]{1,0:T(8,128)(2,1)S(1)}, u32[]{:S(2)}, u32[]{:S(2)}) %collective-permute-start.6) | collective-permute-done | bytes 262176 | tf_op jit(solution)/shard_map/ppermute | solution.py:19
  38.1 1.3 %collective-permute-start.10 = (bf16[128,1024]{1,0:T(8,128)(2,1)S(1)}, bf16[128,1024]{1,0:T(8,128)(2,1)S(1)}, u32[]{:S(2)}, u32[]{:S(2)}) collective-permute-start(bf16[128,1024]{1,0:T(8,128)(2,1)S(1)} %collective-permute-done.6.refs_3_), channel_id=1, source_target_pairs={{4,0},{8,4},{5,1},{9,5},{6,2},{10,6},{7,3},{11,7},{20,16},{24,20},... | collective-permute-start | bytes 786440 | tf_op jit(solution)/shard_map/ppermute | solution.py:19
  39.4 0.9 %shard_map.131 = (f32[128,1024]{1,0:T(8,128)S(1)}, f32[128,1024]{1,0:T(8,128)S(1)}) custom-call(f32[64,128]{1,0:T(8,128)S(1)} %get-tuple-element.48.refs_0_, f32[128,128]{1,0:T(8,128)S(1)} %get-tuple-element.66.refs_1_, bf16[128,1024]{1,0:T(8,128)(2,1)S(1)} %get-tuple-element.53.refs_3_.refs_5_.refs_2_, ...), custom_call_target="tpu_custom_call" | custom-call | flops 1000000 | bytes 100000 | tf_op jit(solution)/shard_map/pallas_call | solution.py:323
  40.3 1.6 %shard_map.132 = (bf16[128,1024]{1,0:T(8,128)(2,1)}, f32[128,1024]{1,0:T(8,128)S(1)}, f32[128,1024]{1,0:T(8,128)S(1)}) custom-call(f32[64,128]{1,0:T(8,128)S(1)} %get-tuple-element.48.refs_0_, f32[128,128]{1,0:T(8,128)S(1)} %get-tuple-element.65.refs_1_, bf16[128,1024]{1,0:T(8,128)(2,1)S(1)} %collective-permute-done.4.refs_7_.refs_2_, ...), custom_call_target="tpu_custom_call" | custom-call | flops 1000000 | bytes 100000 | tf_op jit(solution)/shard_map/pallas_call | solution.py:323
  41.9 4.5 %collective-permute-start.11 = (f32[16,128]{1,0:T(8,128)S(1)}, f32[16,128]{1,0:T(8,128)S(1)}, u32[]{:S(2)}, u32[]{:S(2)}) collective-permute-start(f32[16,128]{1,0:T(8,128)S(1)} %add_add_fusion.refs_3_), channel_id=1, source_target_pairs={{0,12},{4,8},{8,4},{12,0},{1,13},{5,9},{9,5},{13,1},{2,14},{6,10},... | collective-permute-start | bytes 24584 | tf_op jit(solution)/shard_map/ppermute | solution.py:352
  46.5 0.2 collective-permute-start.12
  46.7 0.5 collective-permute-start.13
  47.1 2.2 %collective-permute-done.10.refs_3_ = bf16[128,1024]{1,0:T(8,128)(2,1)S(1)} collective-permute-done((bf16[128,1024]{1,0:T(8,128)(2,1)S(1)}, bf16[128,1024]{1,0:T(8,128)(2,1)S(1)}, u32[]{:S(2)}, u32[]{:S(2)}) %collective-permute-start.10) | collective-permute-done | bytes 262176 | tf_op jit(solution)/shard_map/ppermute | solution.py:19
  49.3 1.5 %shard_map.133 = (bf16[128,1024]{1,0:T(8,128)(2,1)}, bf16[128,1024]{1,0:T(8,128)(2,1)}) custom-call(f32[64,128]{1,0:T(8,128)S(1)} %get-tuple-element.48.refs_0_, f32[128,128]{1,0:T(8,128)S(1)} %get-tuple-element.62.refs_1_, bf16[128,1024]{1,0:T(8,128)(2,1)S(1)} %collective-permute-done.5.refs_14_.refs_2_, ...), custom_call_target="tpu_custom_call" | custom-call | flops 1000000 | bytes 100000 | tf_op jit(solution)/shard_map/pallas_call | solution.py:323
  50.9 0.0 collective-permute-done.11.refs_0_
  50.9 0.2 collective-permute-done.12.refs_1_
  51.0 0.0 collective-permute-done.13.refs_2_
  51.0 0.6 %shard_map.134 = (f32[8,128]{1,0:T(8,128)}, f32[8,8]{1,0:T(8,128)}) custom-call(f32[16,128]{1,0:T(8,128)S(1)} %collective-permute-done.11.refs_0_, f32[16,128]{1,0:T(8,128)S(1)} %collective-permute-done.12.refs_1_, f32[16,128]{1,0:T(8,128)S(1)} %collective-permute-done.13.refs_2_, f32[16,128]{1,0:T(8,128)S(1)} %add_add_fusion.refs_3_), custom_call_target="tpu_custom_call" | custom-call | flops 1000000 | bytes 100000 | tf_op jit(solution)/shard_map/pallas_call | solution.py:323
  (1 shorter events, 0.0 us)
Async XLA Ops:
  0.6 19.3 %copy-start.1 = (f32[8,8]{1,0:T(8,128)S(1)}, f32[8,8]{1,0:T(8,128)}, u32[]{:S(2)}) copy-start(f32[8,8]{1,0:T(8,128)} %refs_1_.1) | copy-start | bytes 772
  0.6 11.9 %collective-permute-start = (bf16[128,1024]{1,0:T(8,128)(2,1)}, bf16[128,1024]{1,0:T(8,128)(2,1)S(1)}, u32[]{:S(2)}, u32[]{:S(2)}) collective-permute-start(bf16[128,1024]{1,0:T(8,128)(2,1)} %bitcast.15), channel_id=1, source_target_pairs={{0,4},{4,8},{8,12},{1,5},{5,9},{9,13},{2,6},{6,10},{10,14},{3,7},{... | collective-permute-start | bytes 786440 | tf_op jit(solution)/shard_map/ppermute | solution.py:19
  5.6 11.5 %collective-permute-start.2 = (bf16[128,1024]{1,0:T(8,128)(2,1)}, bf16[128,1024]{1,0:T(8,128)(2,1)S(1)}, u32[]{:S(2)}, u32[]{:S(2)}) collective-permute-start(bf16[128,1024]{1,0:T(8,128)(2,1)} %bitcast.17), channel_id=1, source_target_pairs={{0,4},{4,8},{8,12},{1,5},{5,9},{9,13},{2,6},{6,10},{10,14},{3,7},{... | collective-permute-start | bytes 786440 | tf_op jit(solution)/shard_map/ppermute | solution.py:19
  9.1 9.6 %collective-permute-start.4 = (bf16[128,1024]{1,0:T(8,128)(2,1)}, bf16[128,1024]{1,0:T(8,128)(2,1)S(1)}, u32[]{:S(2)}, u32[]{:S(2)}) collective-permute-start(bf16[128,1024]{1,0:T(8,128)(2,1)} %bitcast.13), channel_id=1, source_target_pairs={{4,0},{8,4},{12,8},{5,1},{9,5},{13,9},{6,2},{10,6},{14,10},{7,3},{... | collective-permute-start | bytes 786440 | tf_op jit(solution)/shard_map/ppermute | solution.py:19
  12.6 11.1 %collective-permute-start.1 = (bf16[128,1024]{1,0:T(8,128)(2,1)S(1)}, bf16[128,1024]{1,0:T(8,128)(2,1)S(1)}, u32[]{:S(2)}, u32[]{:S(2)}) collective-permute-start(bf16[128,1024]{1,0:T(8,128)(2,1)S(1)} %collective-permute-done.refs_4_.refs_8_), channel_id=1, source_target_pairs={{4,8},{8,12},{5,9},{9,13},{6,10},{10,14},{7,11},{11,15},{20,24},{2... | collective-permute-start | bytes 786440 | tf_op jit(solution)/shard_map/ppermute | solution.py:19
  17.1 6.6 %collective-permute-start.3 = (bf16[128,1024]{1,0:T(8,128)(2,1)S(1)}, bf16[128,1024]{1,0:T(8,128)(2,1)S(1)}, u32[]{:S(2)}, u32[]{:S(2)}) collective-permute-start(bf16[128,1024]{1,0:T(8,128)(2,1)S(1)} %collective-permute-done.2.refs_5_.refs_11_), channel_id=1, source_target_pairs={{4,8},{8,12},{5,9},{9,13},{6,10},{10,14},{7,11},{11,15},{20,24},{2... | collective-permute-start | bytes 786440 | tf_op jit(solution)/shard_map/ppermute | solution.py:19
  18.7 11.7 %collective-permute-start.5 = (bf16[128,1024]{1,0:T(8,128)(2,1)S(1)}, bf16[128,1024]{1,0:T(8,128)(2,1)S(1)}, u32[]{:S(2)}, u32[]{:S(2)}) collective-permute-start(bf16[128,1024]{1,0:T(8,128)(2,1)S(1)} %collective-permute-done.4.refs_7_.refs_2_), channel_id=1, source_target_pairs={{4,0},{8,4},{5,1},{9,5},{6,2},{10,6},{7,3},{11,7},{20,16},{24,20},... | collective-permute-start | bytes 786440 | tf_op jit(solution)/shard_map/ppermute | solution.py:19
  20.0 0.7 %copy-start.2 = (s32[1,4]{1,0:T(1,128)S(1)}, s32[1,4]{1,0:T(1,128)}, u32[]{:S(2)}) copy-start(s32[1,4]{1,0:T(1,128)} %refs_0_.1) | copy-start | bytes 52
  23.7 0.7 %copy-start = (f32[1024]{0:T(1024)S(1)}, f32[1024]{0:T(1024)}, u32[]{:S(2)}) copy-start(f32[1024]{0:T(1024)} %param.15) | copy-start | bytes 12292
  25.3 12.8 %collective-permute-start.6 = (bf16[128,1024]{1,0:T(8,128)(2,1)S(1)}, bf16[128,1024]{1,0:T(8,128)(2,1)S(1)}, u32[]{:S(2)}, u32[]{:S(2)}) collective-permute-start(bf16[128,1024]{1,0:T(8,128)(2,1)S(1)} %get-tuple-element.57.refs_6_.refs_3_), channel_id=1, source_target_pairs={{4,0},{8,4},{12,8},{5,1},{9,5},{13,9},{6,2},{10,6},{14,10},{7,3},{... | collective-permute-start | bytes 786440 | tf_op jit(solution)/shard_map/ppermute | solution.py:19
  32.7 1.9 %collective-permute-start.7 = (f32[16,128]{1,0:T(8,128)S(1)}, f32[16,128]{1,0:T(8,128)S(1)}, u32[]{:S(2)}, u32[]{:S(2)}) collective-permute-start(f32[16,128]{1,0:T(8,128)S(1)} %get-tuple-element.80), channel_id=1, source_target_pairs={{0,1},{1,0},{2,3},{3,2},{4,5},{5,4},{6,7},{7,6},{8,9},{9,8},{10,11... | collective-permute-start | bytes 24584 | tf_op jit(solution)/shard_map/ppermute | solution.py:352
  32.7 3.7 %collective-permute-start.8 = (f32[16,128]{1,0:T(8,128)S(1)}, f32[16,128]{1,0:T(8,128)S(1)}, u32[]{:S(2)}, u32[]{:S(2)}) collective-permute-start(f32[16,128]{1,0:T(8,128)S(1)} %get-tuple-element.80), channel_id=1, source_target_pairs={{0,2},{1,3},{2,0},{3,1},{4,6},{5,7},{6,4},{7,5},{8,10},{9,11},{10,... | collective-permute-start | bytes 24584 | tf_op jit(solution)/shard_map/ppermute | solution.py:352
  34.2 3.1 %collective-permute-start.9 = (f32[16,128]{1,0:T(8,128)S(1)}, f32[16,128]{1,0:T(8,128)S(1)}, u32[]{:S(2)}, u32[]{:S(2)}) collective-permute-start(f32[16,128]{1,0:T(8,128)S(1)} %get-tuple-element.80), channel_id=1, source_target_pairs={{0,3},{1,2},{2,1},{3,0},{4,7},{5,6},{6,5},{7,4},{8,11},{9,10},{10,... | collective-permute-start | bytes 24584 | tf_op jit(solution)/shard_map/ppermute | solution.py:352
  38.1 11.2 %collective-permute-start.10 = (bf16[128,1024]{1,0:T(8,128)(2,1)S(1)}, bf16[128,1024]{1,0:T(8,128)(2,1)S(1)}, u32[]{:S(2)}, u32[]{:S(2)}) collective-permute-start(bf16[128,1024]{1,0:T(8,128)(2,1)S(1)} %collective-permute-done.6.refs_3_), channel_id=1, source_target_pairs={{4,0},{8,4},{5,1},{9,5},{6,2},{10,6},{7,3},{11,7},{20,16},{24,20},... | collective-permute-start | bytes 786440 | tf_op jit(solution)/shard_map/ppermute | solution.py:19
  41.9 8.9 %collective-permute-start.11 = (f32[16,128]{1,0:T(8,128)S(1)}, f32[16,128]{1,0:T(8,128)S(1)}, u32[]{:S(2)}, u32[]{:S(2)}) collective-permute-start(f32[16,128]{1,0:T(8,128)S(1)} %add_add_fusion.refs_3_), channel_id=1, source_target_pairs={{0,12},{4,8},{8,4},{12,0},{1,13},{5,9},{9,5},{13,1},{2,14},{6,10},... | collective-permute-start | bytes 24584 | tf_op jit(solution)/shard_map/ppermute | solution.py:352
  46.5 4.5 %collective-permute-start.12 = (f32[16,128]{1,0:T(8,128)S(1)}, f32[16,128]{1,0:T(8,128)S(1)}, u32[]{:S(2)}, u32[]{:S(2)}) collective-permute-start(f32[16,128]{1,0:T(8,128)S(1)} %add_add_fusion.refs_3_), channel_id=1, source_target_pairs={{0,8},{4,12},{8,0},{12,4},{1,9},{5,13},{9,1},{13,5},{2,10},{6,14},... | collective-permute-start | bytes 24584 | tf_op jit(solution)/shard_map/ppermute | solution.py:352
  46.7 4.4 %collective-permute-start.13 = (f32[16,128]{1,0:T(8,128)S(1)}, f32[16,128]{1,0:T(8,128)S(1)}, u32[]{:S(2)}, u32[]{:S(2)}) collective-permute-start(f32[16,128]{1,0:T(8,128)S(1)} %add_add_fusion.refs_3_), channel_id=1, source_target_pairs={{0,4},{4,0},{8,12},{12,8},{1,5},{5,1},{9,13},{13,9},{2,6},{6,2},{1... | collective-permute-start | bytes 24584 | tf_op jit(solution)/shard_map/ppermute | solution.py:352

commit v12 on v11

--- a/solution.py
+++ b/solution.py
@@ -152,9 +152,29 @@
     return center * inverse, inverse
 
 
-def norm_kernel(hops, heads, scaling, *refs):
-    out_grad, update_gate, gain, attention, attn_grad, gain_grad = refs[-6:]
-    forward_kernel(hops, heads, scaling, *refs[:-6], attention)
+def weights_kernel(hops, heads, scaling, table, near, mask, query, key, weights):
+    pair = Pair(mask, table, heads, hops, near=near)
+    rows, width = query.shape[0], query.shape[1] // heads
+
+    def scores(head):
+        cols = columns(head, width)
+        return contract(query[:, cols], key[:, cols], 1, 1)
+
+    def weigh(head, found):
+        half = pair.half_logits(found, head, scaling)
+        lines = columns(head, rows)
+        weights[lines, :] = ((half + half * jnp.tanh(half)) * pair.mask).astype(BF16)
+
+    in_stages(heads, scores, weigh)
+
+
+def norm_kernel(heads, *refs):
+    weights, value, total, out_grad, update_gate, gain = refs[:6]
+    attention, attn_grad, gain_grad = refs[6:]
+    width = total.shape[1] // heads
+    for head in range(heads):
+        cols, lines = columns(head, width), columns(head, total.shape[0])
+        attention[:, cols] = total[:, cols] + contract(weights[lines, :], value[:, cols], 1, 0)
     rows, features = attention.shape
     step = 16
     gain_row = gain[...]
@@ -284,32 +304,62 @@
     copy.wait()
 
 
-def last_kernel(hops, heads, scaling, *refs):
-    outs, held, written = refs[-5:-3], refs[-3:-1], refs[-1]
+def slopes_kernel(hops, heads, scaling, table, mask, query, key, weights, slopes):
+    pair = Pair(mask, table, heads, hops, True)
+    rows, width = query.shape[0], query.shape[1] // heads
+
+    def scores(head):
+        cols = columns(head, width)
+        return contract(key[:, cols], query[:, cols], 1, 1)
+
+    def derive(head, found):
+        half = pair.half_logits(found, head, scaling)
+        tanh = jnp.tanh(half)
+        lines = columns(head, rows)
+        weights[lines, :] = ((half + half * tanh) * pair.mask).astype(BF16)
+        slopes[lines, :] = slope_of(half, tanh) * pair.mask
+
+    in_stages(heads, scores, derive)
+
+
+def last_kernel(heads, scaling, *refs):
+    weights, slopes, query, grad, value, key_in, value_in = refs[:7]
+    pieces, outs, held, written = refs[7:-9], refs[-9:-5], refs[-5:-1], refs[-1]
+    rows, width = query.shape[0], query.shape[1] // heads
     copies = []
-    group = 2
-
-    def store(head, cols, key_part, value_part):
+    ends = [*range(1, heads - 1, 2), heads - 2, heads - 1]
+
+    def write(at, cols):
+        source, target = held[at].at[:, cols], outs[at].at[:, cols]
+        copies.append(pltpu.make_async_copy(source, target, written.at[len(copies)]))
+        copies[-1].start()
+
+    total = added_up([piece[...] for piece in pieces])
+    lines = held[2].shape[0]
+    held[2][...] = total[:lines]
+    held[3][...] = total[lines:, :heads]
+    for at in (2, 3):
+        write(at, slice(0, held[at].shape[1]))
+
+    def scores(head):
+        cols = columns(head, width)
+        return contract(value[:, cols], grad[:, cols], 1, 1)
+
+    def differentiate(head, found):
+        cols, lines = columns(head, width), columns(head, rows)
+        rounded = (found * slopes[lines, :]).astype(BF16)
+        key_part = key_in[:, cols] + contract(rounded, query[:, cols], 1, 0)
+        value_part = value_in[:, cols] + contract(weights[lines, :], grad[:, cols], 1, 0)
         held[0][:, cols] = (key_part * scaling).astype(BF16)
         held[1][:, cols] = value_part.astype(BF16)
-        if (head + 1) % group == 0:
-            done = slice(cols.stop - group * (cols.stop - cols.start), cols.stop)
-            for source, target in zip(held, outs):
-                at = written.at[len(copies)]
-                copies.append(pltpu.make_async_copy(source.at[:, done], target.at[:, done], at))
-                copies[-1].start()
-
-    add_key_grads(hops, heads, scaling, *refs[:6], refs[6:-5], store)
+        if head in ends:
+            before = ends[ends.index(head) - 1] + 1 if head != ends[0] else 0
+            for at in (0, 1):
+                write(at, slice(before * width, cols.stop))
+
+    in_stages(heads, scores, differentiate)
     for copy in copies:
         copy.wait()
-
-
-def sum_kernel(*refs):
-    gain_out, bias_out = refs[-2:]
-    total = added_up([piece[...] for piece in refs[:-2]])
-    lines = gain_out.shape[0]
-    gain_out[...] = total[:lines]
-    bias_out[...] = total[lines:, : bias_out.shape[1]]
 
 
 def on_device(kernel, outs, args, smem=(), ahead=(), far=(), far_outs=0, scratch=()):
@@ -402,10 +452,17 @@
             (table, near, masks[hops], query, keys[hops], values[hops], attention),
             ahead=later_queries[hops : hops + 1],
         )
+    stacked = (heads * rows, rows)
+    (far_weights,) = on_device(
+        partial(weights_kernel, reach, heads, scaling),
+        [jax.ShapeDtypeStruct(stacked, BF16)],
+        (table, near, masks[-1], query, keys[-1]),
+        ahead=[attention],
+    )
     attention, attn_grad, gain_part = on_device(
-        partial(norm_kernel, reach, heads, scaling),
+        partial(norm_kernel, heads),
         [wide, narrow, jax.ShapeDtypeStruct((1, features), F32)],
-        (table, near, masks[-1], query, keys[-1], values[-1], attention, grad, gate, gain),
+        (far_weights, values[-1], attention, grad, gate, gain),
     )
 
     lanes = features // 8
@@ -447,21 +504,31 @@
                 [wide] * 2,
                 (*key_operands(hops), *key_grads),
             )
-    key_grads, *pieces = lax.optimization_barrier((key_grads, *pieces))
+    far_tables = on_device(
+        partial(slopes_kernel, reach, heads, scaling),
+        [jax.ShapeDtypeStruct(stacked, BF16), jax.ShapeDtypeStruct(stacked, F32)],
+        (table, flipped[reach], later_queries[reach], key),
+        ahead=key_grads[:1],
+    )
+    key_grads, far_tables, *pieces = lax.optimization_barrier((key_grads, far_tables, *pieces))
     for axis, distances in rounds_of(("ctx",)):
         pieces = exchanged(added_up(pieces), axis, distances)
-    key_grad, value_grad = on_device(
-        partial(last_kernel, reach, heads, scaling),
-        [narrow, narrow],
-        (*key_operands(reach), *key_grads),
-        far_outs=2,
-        scratch=[pltpu.VMEM((rows, features), BF16)] * 2 + [pltpu.SemaphoreType.DMA((heads,))],
-    )
-    key_grad, value_grad, pieces[0] = lax.optimization_barrier((key_grad, value_grad, pieces[0]))
-    gain_grad, bias_grad = on_device(
-        sum_kernel,
-        [jax.ShapeDtypeStruct((8, lanes), F32), jax.ShapeDtypeStruct((levels, heads), F32)],
-        pieces[::-1],
+    small = [(8, lanes), (levels, heads)]
+    key_grad, value_grad, gain_grad, bias_grad = on_device(
+        partial(last_kernel, heads, scaling),
+        [narrow, narrow, *[jax.ShapeDtypeStruct(shape, F32) for shape in small]],
+        (
+            *far_tables,
+            later_queries[reach],
+            later_grads[reach],
+            value,
+            *key_grads,
+            *pieces[::-1],
+        ),
+        far_outs=4,
+        scratch=[pltpu.VMEM((rows, features), BF16)] * 2
+        + [pltpu.VMEM(shape, F32) for shape in small]
+        + [pltpu.SemaphoreType.DMA((2 * heads + 2,))],
     )
     return (
         query_grad[None],

time: 52 us -> 53.2 us (1.023)
  waiting for transfers between devices: 16.5 us -> 17.7 us
    ppermute x6, waiting for transfers between devices: 2.88 us -> 6.61 us  [exchanged(): lax.ppermute(array, axis, [(i, i ^ distance) for i in range(size)])]
    ppermute x8, waiting for transfers between devices: 13.6 us -> 11.1 us  [passed_along(): lax.ppermute(array, axis, [(i, i + by) for i in range(first, last + 1)])]
    pallas_call x8 -> x9, Pallas kernels: 11 us -> 10.6 us  [on_device(): pl.pallas_call(body, out_shape=outs, in_specs=[pl.BlockSpec(memory_space=...]
  transfers between devices with their start and end apart: 14 -> 14, of which waited for: 9 -> 9; matrix products, arithmetic and copies ran while one was open for 0% -> 0% of each run, Pallas kernels for 20% -> 18%
where the time goes in v12:
time: 53.2 us; the launch traced here: 52.8 us
  starting transfers between devices  22.3 us (42%)
  waiting for transfers between devices  17.7 us (33%)
  Pallas kernels  10.6 us (20%)
  local copies, waits for them, and re-layouts  1.31 us (2%)
  between operations  0.81 us (2%)
    ppermute x8, starting transfers between devices, passed_along(): lax.ppermute(array, axis, [(i, i + by) for i in range(first, last + 1)])  14.9 us
    ppermute x8, waiting for transfers between devices, passed_along(): lax.ppermute(array, axis, [(i, i + by) for i in range(first, last + 1)])  11.1 us
    pallas_call x9, Pallas kernels, on_device(): pl.pallas_call(body, out_shape=outs, in_specs=[pl.BlockSpec(memory_space=...  10.6 us
    ppermute x6, starting transfers between devices, exchanged(): lax.ppermute(array, axis, [(i, i ^ distance) for i in range(size)])  7.41 us
    ppermute x6, waiting for transfers between devices, exchanged(): lax.ppermute(array, axis, [(i, i ^ distance) for i in range(size)])  6.61 us
    unnamed x6, local copies, waits for them, and re-layouts  1.31 us
  transfers between devices with their start and end apart: 14, of which 9 were waited for; matrix products, arithmetic and copies ran while one was open for 0% of the time, Pallas kernels for 18%

profile of v12, /device:TPU:0, one launch (start us, length us, event | category | flops | bytes accessed | tf_op | source)
XLA Modules:
  0.0 52.8 jit_solution(9621938683597449113)
XLA Ops:
  0.6 0.0 copy-start.1
  0.6 4.9 %collective-permute-start = (bf16[128,1024]{1,0:T(8,128)(2,1)}, bf16[128,1024]{1,0:T(8,128)(2,1)S(1)}, u32[]{:S(2)}, u32[]{:S(2)}) collective-permute-start(bf16[128,1024]{1,0:T(8,128)(2,1)} %bitcast.15), channel_id=1, source_target_pairs={{0,4},{4,8},{8,12},{1,5},{5,9},{9,13},{2,6},{6,10},{10,14},{3,7},{... | collective-permute-start | bytes 786440 | tf_op jit(solution)/shard_map/ppermute | solution.py:19
  5.6 3.5 %collective-permute-start.2 = (bf16[128,1024]{1,0:T(8,128)(2,1)}, bf16[128,1024]{1,0:T(8,128)(2,1)S(1)}, u32[]{:S(2)}, u32[]{:S(2)}) collective-permute-start(bf16[128,1024]{1,0:T(8,128)(2,1)} %bitcast.17), channel_id=1, source_target_pairs={{0,4},{4,8},{8,12},{1,5},{5,9},{9,13},{2,6},{6,10},{10,14},{3,7},{... | collective-permute-start | bytes 786440 | tf_op jit(solution)/shard_map/ppermute | solution.py:19
  9.1 1.3 %collective-permute-start.3 = (bf16[128,1024]{1,0:T(8,128)(2,1)}, bf16[128,1024]{1,0:T(8,128)(2,1)S(1)}, u32[]{:S(2)}, u32[]{:S(2)}) collective-permute-start(bf16[128,1024]{1,0:T(8,128)(2,1)} %bitcast.13), channel_id=1, source_target_pairs={{4,0},{8,4},{12,8},{5,1},{9,5},{13,9},{6,2},{10,6},{14,10},{7,3},{... | collective-permute-start | bytes 786440 | tf_op jit(solution)/shard_map/ppermute | solution.py:19
  10.4 2.2 %collective-permute-done.refs_4_.refs_8_ = bf16[128,1024]{1,0:T(8,128)(2,1)S(1)} collective-permute-done((bf16[128,1024]{1,0:T(8,128)(2,1)}, bf16[128,1024]{1,0:T(8,128)(2,1)S(1)}, u32[]{:S(2)}, u32[]{:S(2)}) %collective-permute-start) | collective-permute-done | bytes 262176 | tf_op jit(solution)/shard_map/ppermute | solution.py:19
  12.6 0.7 %collective-permute-start.1 = (bf16[128,1024]{1,0:T(8,128)(2,1)S(1)}, bf16[128,1024]{1,0:T(8,128)(2,1)S(1)}, u32[]{:S(2)}, u32[]{:S(2)}) collective-permute-start(bf16[128,1024]{1,0:T(8,128)(2,1)S(1)} %collective-permute-done.refs_4_.refs_8_), channel_id=1, source_target_pairs={{4,8},{8,12},{5,9},{9,13},{6,10},{10,14},{7,11},{11,15},{20,24},{2... | collective-permute-start | bytes 786440 | tf_op jit(solution)/shard_map/ppermute | solution.py:19
  13.3 3.8 %collective-permute-done.2.refs_5_.refs_11_ = bf16[128,1024]{1,0:T(8,128)(2,1)S(1)} collective-permute-done((bf16[128,1024]{1,0:T(8,128)(2,1)}, bf16[128,1024]{1,0:T(8,128)(2,1)S(1)}, u32[]{:S(2)}, u32[]{:S(2)}) %collective-permute-start.2) | collective-permute-done | bytes 262176 | tf_op jit(solution)/shard_map/ppermute | solution.py:19
  17.1 0.7 %collective-permute-start.4 = (bf16[128,1024]{1,0:T(8,128)(2,1)S(1)}, bf16[128,1024]{1,0:T(8,128)(2,1)S(1)}, u32[]{:S(2)}, u32[]{:S(2)}) collective-permute-start(bf16[128,1024]{1,0:T(8,128)(2,1)S(1)} %collective-permute-done.2.refs_5_.refs_11_), channel_id=1, source_target_pairs={{4,8},{8,12},{5,9},{9,13},{6,10},{10,14},{7,11},{11,15},{20,24},{2... | collective-permute-start | bytes 786440 | tf_op jit(solution)/shard_map/ppermute | solution.py:19
  17.7 0.9 %collective-permute-done.3.refs_7_.refs_2_ = bf16[128,1024]{1,0:T(8,128)(2,1)S(1)} collective-permute-done((bf16[128,1024]{1,0:T(8,128)(2,1)}, bf16[128,1024]{1,0:T(8,128)(2,1)S(1)}, u32[]{:S(2)}, u32[]{:S(2)}) %collective-permute-start.3) | collective-permute-done | bytes 262176 | tf_op jit(solution)/shard_map/ppermute | solution.py:19
  18.7 1.3 %collective-permute-start.5 = (bf16[128,1024]{1,0:T(8,128)(2,1)S(1)}, bf16[128,1024]{1,0:T(8,128)(2,1)S(1)}, u32[]{:S(2)}, u32[]{:S(2)}) collective-permute-start(bf16[128,1024]{1,0:T(8,128)(2,1)S(1)} %collective-permute-done.3.refs_7_.refs_2_), channel_id=1, source_target_pairs={{4,0},{8,4},{5,1},{9,5},{6,2},{10,6},{7,3},{11,7},{20,16},{24,20},... | collective-permute-start | bytes 786440 | tf_op jit(solution)/shard_map/ppermute | solution.py:19
  20.0 0.0 copy-start.2
  20.0 0.0 copy-done.1
  20.0 0.6 %copy-done.2 = s32[1,4]{1,0:T(1,128)S(1)} copy-done((s32[1,4]{1,0:T(1,128)S(1)}, s32[1,4]{1,0:T(1,128)}, u32[]{:S(2)}) %copy-start.2) | copy-done | bytes 40
  20.6 2.5 %shard_map.127 = (f32[64,128]{1,0:T(8,128)S(1)}, f32[1024,128]{1,0:T(8,128)S(1)}, f32[128,128]{1,0:T(8,128)S(1)}, f32[128,128]{1,0:T(8,128)S(1)}, f32[128,128]{1...) custom-call(s32[1,4]{1,0:T(1,128)S(1)} %copy-done.2, ...), custom_call_target="tpu_custom_call" | custom-call | flops 1000000 | bytes 100000 | tf_op jit(solution)/shard_map/pallas_call | solution.py:373
  23.1 0.6 %shard_map.128.refs_5_.refs_2_ = f32[128,1024]{1,0:T(8,128)S(1)} custom-call(f32[64,128]{1,0:T(8,128)S(1)} %get-tuple-element.49.refs_0_, f32[1024,128]{1,0:T(8,128)S(1)} %get-tuple-element.50.refs_1_, f32[128,128]{1,0:T(8,128)S(1)} %get-tuple-element.52.refs_2_.refs_3_, bf16[128,1024]{1,0:T(8,128)(2,1)S(1)} %get-tuple-element.54.refs_3_.refs_5_.refs_2_, ...), custom_call_target="tpu_custom_call" | custom-call | flops 1000000 | bytes 100000 | tf_op jit(solution)/shard_map/pallas_call | solution.py:373
  23.7 0.0 collective-permute-done.1.refs_4_.refs_9_
  23.7 0.3 shard_map.129.refs_0_
  24.0 0.0 copy-start
  24.0 0.0 collective-permute-done.4.refs_1_.refs_12_
  24.0 0.7 %copy-done = f32[1024]{0:T(1024)S(1)} copy-done((f32[1024]{0:T(1024)S(1)}, f32[1024]{0:T(1024)}, u32[]{:S(2)}) %copy-start) | copy-done | bytes 4120
  24.7 0.6 %shard_map.130 = (f32[128,1024]{1,0:T(8,128)S(1)}, bf16[128,1024]{1,0:T(8,128)(2,1)S(1)}, f32[1,1024]{1,0:T(1,128)S(1)}) custom-call(bf16[1024,128]{1,0:T(8,128)(2,1)S(1)} %shard_map.129.refs_0_, bf16[128,1024]{1,0:T(8,128)(2,1)S(1)} %collective-permute-done.4.refs_1_.refs_12_, f32[128,1024]{1,0:T(8,128)S(1)} %shard_map.128.refs_5_.refs_2_, ...), custom_call_target="tpu_custom_call" | custom-call | flops 1000000 | bytes 100000 | tf_op jit(solution)/shard_map/pallas_call | solution.py:373
  25.3 1.3 %collective-permute-start.6 = (bf16[128,1024]{1,0:T(8,128)(2,1)S(1)}, bf16[128,1024]{1,0:T(8,128)(2,1)S(1)}, u32[]{:S(2)}, u32[]{:S(2)}) collective-permute-start(bf16[128,1024]{1,0:T(8,128)(2,1)S(1)} %get-tuple-element.58.refs_6_.refs_3_), channel_id=1, source_target_pairs={{4,0},{8,4},{12,8},{5,1},{9,5},{13,9},{6,2},{10,6},{14,10},{7,3},{... | collective-permute-start | bytes 786440 | tf_op jit(solution)/shard_map/ppermute | solution.py:19
  26.6 3.7 %collective-permute-done.5.refs_14_.refs_2_ = bf16[128,1024]{1,0:T(8,128)(2,1)S(1)} collective-permute-done((bf16[128,1024]{1,0:T(8,128)(2,1)S(1)}, bf16[128,1024]{1,0:T(8,128)(2,1)S(1)}, u32[]{:S(2)}, u32[]{:S(2)}) %collective-permute-start.5) | collective-permute-done | bytes 262176 | tf_op jit(solution)/shard_map/ppermute | solution.py:19
  30.3 2.4 %shard_map.131 = (bf16[128,1024]{1,0:T(8,128)(2,1)}, f32[16,128]{1,0:T(8,128)S(1)}) custom-call(f32[64,128]{1,0:T(8,128)S(1)} %get-tuple-element.49.refs_0_, f32[1024,128]{1,0:T(8,128)S(1)} %get-tuple-element.50.refs_1_, f32[128,128]{1,0:T(8,128)S(1)} %get-tuple-element.51.refs_2_, f32[128,128]{1,0:T(8,128)S(1)} %get-tuple-element.52.refs_2_.refs_3_, ...), custom_call_target="tpu_custom_call" | custom-call | flops 1000000 | bytes 100000 | tf_op jit(solution)/shard_map/pallas_call | solution.py:373
  32.7 0.0 collective-permute-start.7
  32.7 1.5 %collective-permute-start.8 = (f32[16,128]{1,0:T(8,128)S(1)}, f32[16,128]{1,0:T(8,128)S(1)}, u32[]{:S(2)}, u32[]{:S(2)}) collective-permute-start(f32[16,128]{1,0:T(8,128)S(1)} %get-tuple-element.83), channel_id=1, source_target_pairs={{0,2},{1,3},{2,0},{3,1},{4,6},{5,7},{6,4},{7,5},{8,10},{9,11},{10,... | collective-permute-start | bytes 24584 | tf_op jit(solution)/shard_map/ppermute | solution.py:402
  34.2 0.4 collective-permute-start.9
  34.6 0.0 collective-permute-done.7.refs_6_
  34.6 1.8 %collective-permute-done.8 = f32[16,128]{1,0:T(8,128)S(1)} collective-permute-done((f32[16,128]{1,0:T(8,128)S(1)}, f32[16,128]{1,0:T(8,128)S(1)}, u32[]{:S(2)}, u32[]{:S(2)}) %collective-permute-start.8) | collective-permute-done | bytes 8224 | tf_op jit(solution)/shard_map/ppermute | solution.py:402
  36.4 0.9 %collective-permute-done.9 = f32[16,128]{1,0:T(8,128)S(1)} collective-permute-done((f32[16,128]{1,0:T(8,128)S(1)}, f32[16,128]{1,0:T(8,128)S(1)}, u32[]{:S(2)}, u32[]{:S(2)}) %collective-permute-start.9) | collective-permute-done | bytes 8224 | tf_op jit(solution)/shard_map/ppermute | solution.py:402
  37.3 0.5 collective-permute-done.6.refs_3_
  37.7 1.3 %collective-permute-start.10 = (bf16[128,1024]{1,0:T(8,128)(2,1)S(1)}, bf16[128,1024]{1,0:T(8,128)(2,1)S(1)}, u32[]{:S(2)}, u32[]{:S(2)}) collective-permute-start(bf16[128,1024]{1,0:T(8,128)(2,1)S(1)} %collective-permute-done.6.refs_3_), channel_id=1, source_target_pairs={{4,0},{8,4},{5,1},{9,5},{6,2},{10,6},{7,3},{11,7},{20,16},{24,20},... | collective-permute-start | bytes 786440 | tf_op jit(solution)/shard_map/ppermute | solution.py:19
  39.0 0.9 %shard_map.132 = (f32[128,1024]{1,0:T(8,128)S(1)}, f32[128,1024]{1,0:T(8,128)S(1)}) custom-call(f32[64,128]{1,0:T(8,128)S(1)} %get-tuple-element.49.refs_0_, f32[128,128]{1,0:T(8,128)S(1)} %get-tuple-element.64.refs_1_, bf16[128,1024]{1,0:T(8,128)(2,1)S(1)} %get-tuple-element.54.refs_3_.refs_5_.refs_2_, ...), custom_call_target="tpu_custom_call" | custom-call | flops 1000000 | bytes 100000 | tf_op jit(solution)/shard_map/pallas_call | solution.py:373
  39.9 1.6 %shard_map.133 = (bf16[128,1024]{1,0:T(8,128)(2,1)}, f32[128,1024]{1,0:T(8,128)S(1)}, f32[128,1024]{1,0:T(8,128)S(1)}) custom-call(f32[64,128]{1,0:T(8,128)S(1)} %get-tuple-element.49.refs_0_, f32[128,128]{1,0:T(8,128)S(1)} %get-tuple-element.63.refs_1_, bf16[128,1024]{1,0:T(8,128)(2,1)S(1)} %collective-permute-done.3.refs_7_.refs_2_, ...), custom_call_target="tpu_custom_call" | custom-call | flops 1000000 | bytes 100000 | tf_op jit(solution)/shard_map/pallas_call | solution.py:373
  41.5 0.4 shard_map.134
  42.0 4.9 %collective-permute-start.11 = (f32[16,128]{1,0:T(8,128)S(1)}, f32[16,128]{1,0:T(8,128)S(1)}, u32[]{:S(2)}, u32[]{:S(2)}) collective-permute-start(f32[16,128]{1,0:T(8,128)S(1)} %add_add_fusion.refs_10_), channel_id=1, source_target_pairs={{0,12},{4,8},{8,4},{12,0},{1,13},{5,9},{9,5},{13,1},{2,14},{6,10},... | collective-permute-start | bytes 24584 | tf_op jit(solution)/shard_map/ppermute | solution.py:402
  46.9 0.0 collective-permute-start.12
  46.9 0.6 %collective-permute-start.13 = (f32[16,128]{1,0:T(8,128)S(1)}, f32[16,128]{1,0:T(8,128)S(1)}, u32[]{:S(2)}, u32[]{:S(2)}) collective-permute-start(f32[16,128]{1,0:T(8,128)S(1)} %add_add_fusion.refs_10_), channel_id=1, source_target_pairs={{0,4},{4,0},{8,12},{12,8},{1,5},{5,1},{9,13},{13,9},{2,6},{6,2},{1... | collective-permute-start | bytes 24584 | tf_op jit(solution)/shard_map/ppermute | solution.py:402
  47.5 1.0 %collective-permute-done.11.refs_7_ = f32[16,128]{1,0:T(8,128)S(1)} collective-permute-done((f32[16,128]{1,0:T(8,128)S(1)}, f32[16,128]{1,0:T(8,128)S(1)}, u32[]{:S(2)}, u32[]{:S(2)}) %collective-permute-start.11) | collective-permute-done | bytes 8224 | tf_op jit(solution)/shard_map/ppermute | solution.py:402
  48.5 2.9 %collective-permute-done.12.refs_8_ = f32[16,128]{1,0:T(8,128)S(1)} collective-permute-done((f32[16,128]{1,0:T(8,128)S(1)}, f32[16,128]{1,0:T(8,128)S(1)}, u32[]{:S(2)}, u32[]{:S(2)}) %collective-permute-start.12) | collective-permute-done | bytes 8224 | tf_op jit(solution)/shard_map/ppermute | solution.py:402
  51.5 0.0 collective-permute-done.13.refs_9_
  51.5 0.0 collective-permute-done.10.refs_3_
  51.5 1.4 %shard_map.135 = (bf16[128,1024]{1,0:T(8,128)(2,1)}, bf16[128,1024]{1,0:T(8,128)(2,1)}, f32[8,128]{1,0:T(8,128)}, f32[8,8]{1,0:T(8,128)}) custom-call(bf16[1024,128]{1,0:T(8,128)(2,1)S(1)} %get-tuple-element.78.refs_0_, f32[1024,128]{1,0:T(8,128)S(1)} %get-tuple-element.79.refs_1_, bf16[128,1024]{1,0:T(8,128)(2,1)S(1)} %collective-permute-done.5.refs_14_.refs_2_, ...), custom_call_target="tpu_custom_call" | custom-call | flops 1000000 | bytes 100000 | tf_op jit(solution)/shard_map/pallas_call | solution.py:373
  (1 shorter events, 0.0 us)
Async XLA Ops:
  0.6 19.3 %copy-start.1 = (f32[8,8]{1,0:T(8,128)S(1)}, f32[8,8]{1,0:T(8,128)}, u32[]{:S(2)}) copy-start(f32[8,8]{1,0:T(8,128)} %refs_1_.1) | copy-start | bytes 772
  0.6 11.9 %collective-permute-start = (bf16[128,1024]{1,0:T(8,128)(2,1)}, bf16[128,1024]{1,0:T(8,128)(2,1)S(1)}, u32[]{:S(2)}, u32[]{:S(2)}) collective-permute-start(bf16[128,1024]{1,0:T(8,128)(2,1)} %bitcast.15), channel_id=1, source_target_pairs={{0,4},{4,8},{8,12},{1,5},{5,9},{9,13},{2,6},{6,10},{10,14},{3,7},{... | collective-permute-start | bytes 786440 | tf_op jit(solution)/shard_map/ppermute | solution.py:19
  5.6 11.5 %collective-permute-start.2 = (bf16[128,1024]{1,0:T(8,128)(2,1)}, bf16[128,1024]{1,0:T(8,128)(2,1)S(1)}, u32[]{:S(2)}, u32[]{:S(2)}) collective-permute-start(bf16[128,1024]{1,0:T(8,128)(2,1)} %bitcast.17), channel_id=1, source_target_pairs={{0,4},{4,8},{8,12},{1,5},{5,9},{9,13},{2,6},{6,10},{10,14},{3,7},{... | collective-permute-start | bytes 786440 | tf_op jit(solution)/shard_map/ppermute | solution.py:19
  9.1 9.6 %collective-permute-start.3 = (bf16[128,1024]{1,0:T(8,128)(2,1)}, bf16[128,1024]{1,0:T(8,128)(2,1)S(1)}, u32[]{:S(2)}, u32[]{:S(2)}) collective-permute-start(bf16[128,1024]{1,0:T(8,128)(2,1)} %bitcast.13), channel_id=1, source_target_pairs={{4,0},{8,4},{12,8},{5,1},{9,5},{13,9},{6,2},{10,6},{14,10},{7,3},{... | collective-permute-start | bytes 786440 | tf_op jit(solution)/shard_map/ppermute | solution.py:19
  12.6 11.1 %collective-permute-start.1 = (bf16[128,1024]{1,0:T(8,128)(2,1)S(1)}, bf16[128,1024]{1,0:T(8,128)(2,1)S(1)}, u32[]{:S(2)}, u32[]{:S(2)}) collective-permute-start(bf16[128,1024]{1,0:T(8,128)(2,1)S(1)} %collective-permute-done.refs_4_.refs_8_), channel_id=1, source_target_pairs={{4,8},{8,12},{5,9},{9,13},{6,10},{10,14},{7,11},{11,15},{20,24},{2... | collective-permute-start | bytes 786440 | tf_op jit(solution)/shard_map/ppermute | solution.py:19
  17.1 7.0 %collective-permute-start.4 = (bf16[128,1024]{1,0:T(8,128)(2,1)S(1)}, bf16[128,1024]{1,0:T(8,128)(2,1)S(1)}, u32[]{:S(2)}, u32[]{:S(2)}) collective-permute-start(bf16[128,1024]{1,0:T(8,128)(2,1)S(1)} %collective-permute-done.2.refs_5_.refs_11_), channel_id=1, source_target_pairs={{4,8},{8,12},{5,9},{9,13},{6,10},{10,14},{7,11},{11,15},{20,24},{2... | collective-permute-start | bytes 786440 | tf_op jit(solution)/shard_map/ppermute | solution.py:19
  18.7 11.7 %collective-permute-start.5 = (bf16[128,1024]{1,0:T(8,128)(2,1)S(1)}, bf16[128,1024]{1,0:T(8,128)(2,1)S(1)}, u32[]{:S(2)}, u32[]{:S(2)}) collective-permute-start(bf16[128,1024]{1,0:T(8,128)(2,1)S(1)} %collective-permute-done.3.refs_7_.refs_2_), channel_id=1, source_target_pairs={{4,0},{8,4},{5,1},{9,5},{6,2},{10,6},{7,3},{11,7},{20,16},{24,20},... | collective-permute-start | bytes 786440 | tf_op jit(solution)/shard_map/ppermute | solution.py:19
  20.0 0.7 %copy-start.2 = (s32[1,4]{1,0:T(1,128)S(1)}, s32[1,4]{1,0:T(1,128)}, u32[]{:S(2)}) copy-start(s32[1,4]{1,0:T(1,128)} %refs_0_.1) | copy-start | bytes 52
  24.0 0.7 %copy-start = (f32[1024]{0:T(1024)S(1)}, f32[1024]{0:T(1024)}, u32[]{:S(2)}) copy-start(f32[1024]{0:T(1024)} %param.15) | copy-start | bytes 12292
  25.3 12.4 %collective-permute-start.6 = (bf16[128,1024]{1,0:T(8,128)(2,1)S(1)}, bf16[128,1024]{1,0:T(8,128)(2,1)S(1)}, u32[]{:S(2)}, u32[]{:S(2)}) collective-permute-start(bf16[128,1024]{1,0:T(8,128)(2,1)S(1)} %get-tuple-element.58.refs_6_.refs_3_), channel_id=1, source_target_pairs={{4,0},{8,4},{12,8},{5,1},{9,5},{13,9},{6,2},{10,6},{14,10},{7,3},{... | collective-permute-start | bytes 786440 | tf_op jit(solution)/shard_map/ppermute | solution.py:19
  32.7 1.9 %collective-permute-start.7 = (f32[16,128]{1,0:T(8,128)S(1)}, f32[16,128]{1,0:T(8,128)S(1)}, u32[]{:S(2)}, u32[]{:S(2)}) collective-permute-start(f32[16,128]{1,0:T(8,128)S(1)} %get-tuple-element.83), channel_id=1, source_target_pairs={{0,1},{1,0},{2,3},{3,2},{4,5},{5,4},{6,7},{7,6},{8,9},{9,8},{10,11... | collective-permute-start | bytes 24584 | tf_op jit(solution)/shard_map/ppermute | solution.py:402
  32.7 3.7 %collective-permute-start.8 = (f32[16,128]{1,0:T(8,128)S(1)}, f32[16,128]{1,0:T(8,128)S(1)}, u32[]{:S(2)}, u32[]{:S(2)}) collective-permute-start(f32[16,128]{1,0:T(8,128)S(1)} %get-tuple-element.83), channel_id=1, source_target_pairs={{0,2},{1,3},{2,0},{3,1},{4,6},{5,7},{6,4},{7,5},{8,10},{9,11},{10,... | collective-permute-start | bytes 24584 | tf_op jit(solution)/shard_map/ppermute | solution.py:402
  34.2 3.1 %collective-permute-start.9 = (f32[16,128]{1,0:T(8,128)S(1)}, f32[16,128]{1,0:T(8,128)S(1)}, u32[]{:S(2)}, u32[]{:S(2)}) collective-permute-start(f32[16,128]{1,0:T(8,128)S(1)} %get-tuple-element.83), channel_id=1, source_target_pairs={{0,3},{1,2},{2,1},{3,0},{4,7},{5,6},{6,5},{7,4},{8,11},{9,10},{10,... | collective-permute-start | bytes 24584 | tf_op jit(solution)/shard_map/ppermute | solution.py:402
  37.7 13.7 %collective-permute-start.10 = (bf16[128,1024]{1,0:T(8,128)(2,1)S(1)}, bf16[128,1024]{1,0:T(8,128)(2,1)S(1)}, u32[]{:S(2)}, u32[]{:S(2)}) collective-permute-start(bf16[128,1024]{1,0:T(8,128)(2,1)S(1)} %collective-permute-done.6.refs_3_), channel_id=1, source_target_pairs={{4,0},{8,4},{5,1},{9,5},{6,2},{10,6},{7,3},{11,7},{20,16},{24,20},... | collective-permute-start | bytes 786440 | tf_op jit(solution)/shard_map/ppermute | solution.py:19
  42.0 6.5 %collective-permute-start.11 = (f32[16,128]{1,0:T(8,128)S(1)}, f32[16,128]{1,0:T(8,128)S(1)}, u32[]{:S(2)}, u32[]{:S(2)}) collective-permute-start(f32[16,128]{1,0:T(8,128)S(1)} %add_add_fusion.refs_10_), channel_id=1, source_target_pairs={{0,12},{4,8},{8,4},{12,0},{1,13},{5,9},{9,5},{13,1},{2,14},{6,10},... | collective-permute-start | bytes 24584 | tf_op jit(solution)/shard_map/ppermute | solution.py:402
  46.9 4.5 %collective-permute-start.12 = (f32[16,128]{1,0:T(8,128)S(1)}, f32[16,128]{1,0:T(8,128)S(1)}, u32[]{:S(2)}, u32[]{:S(2)}) collective-permute-start(f32[16,128]{1,0:T(8,128)S(1)} %add_add_fusion.refs_10_), channel_id=1, source_target_pairs={{0,8},{4,12},{8,0},{12,4},{1,9},{5,13},{9,1},{13,5},{2,10},{6,14},... | collective-permute-start | bytes 24584 | tf_op jit(solution)/shard_map/ppermute | solution.py:402
  46.9 4.5 %collective-permute-start.13 = (f32[16,128]{1,0:T(8,128)S(1)}, f32[16,128]{1,0:T(8,128)S(1)}, u32[]{:S(2)}, u32[]{:S(2)}) collective-permute-start(f32[16,128]{1,0:T(8,128)S(1)} %add_add_fusion.refs_10_), channel_id=1, source_target_pairs={{0,4},{4,0},{8,12},{12,8},{1,5},{5,1},{9,13},{13,9},{2,6},{6,2},{1... | collective-permute-start | bytes 24584 | tf_op jit(solution)/shard_map/ppermute | solution.py:402

commit v13 on v12

--- a/solution.py
+++ b/solution.py
@@ -324,7 +324,7 @@
 
 def last_kernel(heads, scaling, *refs):
     weights, slopes, query, grad, value, key_in, value_in = refs[:7]
-    pieces, outs, held, written = refs[7:-9], refs[-9:-5], refs[-5:-1], refs[-1]
+    outs, held, written = refs[7:9], refs[9:11], refs[11]
     rows, width = query.shape[0], query.shape[1] // heads
     copies = []
     ends = [*range(1, heads - 1, 2), heads - 2, heads - 1]
@@ -333,13 +333,6 @@
         source, target = held[at].at[:, cols], outs[at].at[:, cols]
         copies.append(pltpu.make_async_copy(source, target, written.at[len(copies)]))
         copies[-1].start()
-
-    total = added_up([piece[...] for piece in pieces])
-    lines = held[2].shape[0]
-    held[2][...] = total[:lines]
-    held[3][...] = total[lines:, :heads]
-    for at in (2, 3):
-        write(at, slice(0, held[at].shape[1]))
 
     def scores(head):
         cols = columns(head, width)
@@ -360,6 +353,14 @@
     in_stages(heads, scores, differentiate)
     for copy in copies:
         copy.wait()
+
+
+def sum_kernel(*refs):
+    gain_out, bias_out = refs[-2:]
+    total = added_up([piece[...] for piece in refs[:-2]])
+    lines = gain_out.shape[0]
+    gain_out[...] = total[:lines]
+    bias_out[...] = total[lines:, : bias_out.shape[1]]
 
 
 def on_device(kernel, outs, args, smem=(), ahead=(), far=(), far_outs=0, scratch=()):
@@ -513,22 +514,18 @@
     key_grads, far_tables, *pieces = lax.optimization_barrier((key_grads, far_tables, *pieces))
     for axis, distances in rounds_of(("ctx",)):
         pieces = exchanged(added_up(pieces), axis, distances)
-    small = [(8, lanes), (levels, heads)]
-    key_grad, value_grad, gain_grad, bias_grad = on_device(
+    key_grad, value_grad = on_device(
         partial(last_kernel, heads, scaling),
-        [narrow, narrow, *[jax.ShapeDtypeStruct(shape, F32) for shape in small]],
-        (
-            *far_tables,
-            later_queries[reach],
-            later_grads[reach],
-            value,
-            *key_grads,
-            *pieces[::-1],
-        ),
-        far_outs=4,
-        scratch=[pltpu.VMEM((rows, features), BF16)] * 2
-        + [pltpu.VMEM(shape, F32) for shape in small]
-        + [pltpu.SemaphoreType.DMA((2 * heads + 2,))],
+        [narrow, narrow],
+        (*far_tables, later_queries[reach], later_grads[reach], value, *key_grads),
+        far_outs=2,
+        scratch=[pltpu.VMEM((rows, features), BF16)] * 2 + [pltpu.SemaphoreType.DMA((2 * heads,))],
+    )
+    key_grad, value_grad, pieces[0] = lax.optimization_barrier((key_grad, value_grad, pieces[0]))
+    gain_grad, bias_grad = on_device(
+        sum_kernel,
+        [jax.ShapeDtypeStruct((8, lanes), F32), jax.ShapeDtypeStruct((levels, heads), F32)],
+        pieces[::-1],
     )
     return (
         query_grad[None],

time: 53.2 us -> 52.4 us (0.985)
  waiting for transfers between devices: 17.7 us -> 16.4 us
  Pallas kernels: 10.6 us -> 11.2 us
    ppermute x6, waiting for transfers between devices: 6.61 us -> 3.77 us  [exchanged(): lax.ppermute(array, axis, [(i, i ^ distance) for i in range(size)])]
    ppermute x8, waiting for transfers between devices: 11.1 us -> 12.6 us  [passed_along(): lax.ppermute(array, axis, [(i, i + by) for i in range(first, last + 1)])]
    pallas_call x9 -> x10, Pallas kernels: 10.6 us -> 11.2 us  [on_device(): pl.pallas_call(body, out_shape=outs, in_specs=[pl.BlockSpec(memory_space=...]
  transfers between devices with their start and end apart: 14 -> 14, of which waited for: 9 -> 9; matrix products, arithmetic and copies ran while one was open for 0% -> 0% of each run, Pallas kernels for 18% -> 20%
where the time goes in v13:
time: 52.4 us; the launch traced here: 52.1 us
  starting transfers between devices  22.3 us (43%)
  waiting for transfers between devices  16.4 us (31%)
  Pallas kernels  11.2 us (21%)
  local copies, waits for them, and re-layouts  1.31 us (2%)
  between operations  0.82 us (2%)
    ppermute x8, starting transfers between devices, passed_along(): lax.ppermute(array, axis, [(i, i + by) for i in range(first, last + 1)])  14.9 us
    ppermute x8, waiting for transfers between devices, passed_along(): lax.ppermute(array, axis, [(i, i + by) for i in range(first, last + 1)])  12.6 us
    pallas_call x10, Pallas kernels, on_device(): pl.pallas_call(body, out_shape=outs, in_specs=[pl.BlockSpec(memory_space=...  11.2 us
    ppermute x6, starting transfers between devices, exchanged(): lax.ppermute(array, axis, [(i, i ^ distance) for i in range(size)])  7.41 us
    ppermute x6, waiting for transfers between devices, exchanged(): lax.ppermute(array, axis, [(i, i ^ distance) for i in range(size)])  3.77 us
    unnamed x6, local copies, waits for them, and re-layouts  1.31 us
  transfers between devices with their start and end apart: 14, of which 9 were waited for; matrix products, arithmetic and copies ran while one was open for 0% of the time, Pallas kernels for 20%

profile of v13, /device:TPU:0, one launch (start us, length us, event | category | flops | bytes accessed | tf_op | source)
XLA Modules:
  0.0 52.1 jit_solution(8847515182562779882)
XLA Ops:
  0.6 0.0 copy-start.1
  0.6 4.9 %collective-permute-start = (bf16[128,1024]{1,0:T(8,128)(2,1)}, bf16[128,1024]{1,0:T(8,128)(2,1)S(1)}, u32[]{:S(2)}, u32[]{:S(2)}) collective-permute-start(bf16[128,1024]{1,0:T(8,128)(2,1)} %bitcast.15), channel_id=1, source_target_pairs={{0,4},{4,8},{8,12},{1,5},{5,9},{9,13},{2,6},{6,10},{10,14},{3,7},{... | collective-permute-start | bytes 786440 | tf_op jit(solution)/shard_map/ppermute | solution.py:19
  5.6 3.5 %collective-permute-start.2 = (bf16[128,1024]{1,0:T(8,128)(2,1)}, bf16[128,1024]{1,0:T(8,128)(2,1)S(1)}, u32[]{:S(2)}, u32[]{:S(2)}) collective-permute-start(bf16[128,1024]{1,0:T(8,128)(2,1)} %bitcast.17), channel_id=1, source_target_pairs={{0,4},{4,8},{8,12},{1,5},{5,9},{9,13},{2,6},{6,10},{10,14},{3,7},{... | collective-permute-start | bytes 786440 | tf_op jit(solution)/shard_map/ppermute | solution.py:19
  9.1 1.3 %collective-permute-start.3 = (bf16[128,1024]{1,0:T(8,128)(2,1)}, bf16[128,1024]{1,0:T(8,128)(2,1)S(1)}, u32[]{:S(2)}, u32[]{:S(2)}) collective-permute-start(bf16[128,1024]{1,0:T(8,128)(2,1)} %bitcast.13), channel_id=1, source_target_pairs={{4,0},{8,4},{12,8},{5,1},{9,5},{13,9},{6,2},{10,6},{14,10},{7,3},{... | collective-permute-start | bytes 786440 | tf_op jit(solution)/shard_map/ppermute | solution.py:19
  10.4 2.2 %collective-permute-done.refs_4_.refs_8_ = bf16[128,1024]{1,0:T(8,128)(2,1)S(1)} collective-permute-done((bf16[128,1024]{1,0:T(8,128)(2,1)}, bf16[128,1024]{1,0:T(8,128)(2,1)S(1)}, u32[]{:S(2)}, u32[]{:S(2)}) %collective-permute-start) | collective-permute-done | bytes 262176 | tf_op jit(solution)/shard_map/ppermute | solution.py:19
  12.6 0.7 %collective-permute-start.1 = (bf16[128,1024]{1,0:T(8,128)(2,1)S(1)}, bf16[128,1024]{1,0:T(8,128)(2,1)S(1)}, u32[]{:S(2)}, u32[]{:S(2)}) collective-permute-start(bf16[128,1024]{1,0:T(8,128)(2,1)S(1)} %collective-permute-done.refs_4_.refs_8_), channel_id=1, source_target_pairs={{4,8},{8,12},{5,9},{9,13},{6,10},{10,14},{7,11},{11,15},{20,24},{2... | collective-permute-start | bytes 786440 | tf_op jit(solution)/shard_map/ppermute | solution.py:19
  13.3 3.8 %collective-permute-done.2.refs_5_.refs_11_ = bf16[128,1024]{1,0:T(8,128)(2,1)S(1)} collective-permute-done((bf16[128,1024]{1,0:T(8,128)(2,1)}, bf16[128,1024]{1,0:T(8,128)(2,1)S(1)}, u32[]{:S(2)}, u32[]{:S(2)}) %collective-permute-start.2) | collective-permute-done | bytes 262176 | tf_op jit(solution)/shard_map/ppermute | solution.py:19
  17.1 0.7 %collective-permute-start.4 = (bf16[128,1024]{1,0:T(8,128)(2,1)S(1)}, bf16[128,1024]{1,0:T(8,128)(2,1)S(1)}, u32[]{:S(2)}, u32[]{:S(2)}) collective-permute-start(bf16[128,1024]{1,0:T(8,128)(2,1)S(1)} %collective-permute-done.2.refs_5_.refs_11_), channel_id=1, source_target_pairs={{4,8},{8,12},{5,9},{9,13},{6,10},{10,14},{7,11},{11,15},{20,24},{2... | collective-permute-start | bytes 786440 | tf_op jit(solution)/shard_map/ppermute | solution.py:19
  17.7 0.9 %collective-permute-done.3.refs_7_.refs_2_ = bf16[128,1024]{1,0:T(8,128)(2,1)S(1)} collective-permute-done((bf16[128,1024]{1,0:T(8,128)(2,1)}, bf16[128,1024]{1,0:T(8,128)(2,1)S(1)}, u32[]{:S(2)}, u32[]{:S(2)}) %collective-permute-start.3) | collective-permute-done | bytes 262176 | tf_op jit(solution)/shard_map/ppermute | solution.py:19
  18.7 1.3 %collective-permute-start.5 = (bf16[128,1024]{1,0:T(8,128)(2,1)S(1)}, bf16[128,1024]{1,0:T(8,128)(2,1)S(1)}, u32[]{:S(2)}, u32[]{:S(2)}) collective-permute-start(bf16[128,1024]{1,0:T(8,128)(2,1)S(1)} %collective-permute-done.3.refs_7_.refs_2_), channel_id=1, source_target_pairs={{4,0},{8,4},{5,1},{9,5},{6,2},{10,6},{7,3},{11,7},{20,16},{24,20},... | collective-permute-start | bytes 786440 | tf_op jit(solution)/shard_map/ppermute | solution.py:19
  20.0 0.0 copy-start.2
  20.0 0.0 copy-done.1
  20.0 0.6 %copy-done.2 = s32[1,4]{1,0:T(1,128)S(1)} copy-done((s32[1,4]{1,0:T(1,128)S(1)}, s32[1,4]{1,0:T(1,128)}, u32[]{:S(2)}) %copy-start.2) | copy-done | bytes 40
  20.6 2.5 %shard_map.127 = (f32[64,128]{1,0:T(8,128)S(1)}, f32[1024,128]{1,0:T(8,128)S(1)}, f32[128,128]{1,0:T(8,128)S(1)}, f32[128,128]{1,0:T(8,128)S(1)}, f32[128,128]{1...) custom-call(s32[1,4]{1,0:T(1,128)S(1)} %copy-done.2, ...), custom_call_target="tpu_custom_call" | custom-call | flops 1000000 | bytes 100000 | tf_op jit(solution)/shard_map/pallas_call | solution.py:374
  23.1 0.6 %shard_map.128.refs_5_.refs_2_ = f32[128,1024]{1,0:T(8,128)S(1)} custom-call(f32[64,128]{1,0:T(8,128)S(1)} %get-tuple-element.52.refs_0_, f32[1024,128]{1,0:T(8,128)S(1)} %get-tuple-element.53.refs_1_, f32[128,128]{1,0:T(8,128)S(1)} %get-tuple-element.55.refs_2_.refs_3_, bf16[128,1024]{1,0:T(8,128)(2,1)S(1)} %get-tuple-element.57.refs_3_.refs_5_.refs_2_, ...), custom_call_target="tpu_custom_call" | custom-call | flops 1000000 | bytes 100000 | tf_op jit(solution)/shard_map/pallas_call | solution.py:374
  23.7 0.0 collective-permute-done.1.refs_4_.refs_9_
  23.7 0.3 shard_map.129.refs_0_
  24.0 0.0 copy-start
  24.0 0.0 collective-permute-done.4.refs_1_.refs_12_
  24.0 0.7 %copy-done = f32[1024]{0:T(1024)S(1)} copy-done((f32[1024]{0:T(1024)S(1)}, f32[1024]{0:T(1024)}, u32[]{:S(2)}) %copy-start) | copy-done | bytes 4120
  24.7 0.6 %shard_map.130 = (f32[128,1024]{1,0:T(8,128)S(1)}, bf16[128,1024]{1,0:T(8,128)(2,1)S(1)}, f32[1,1024]{1,0:T(1,128)S(1)}) custom-call(bf16[1024,128]{1,0:T(8,128)(2,1)S(1)} %shard_map.129.refs_0_, bf16[128,1024]{1,0:T(8,128)(2,1)S(1)} %collective-permute-done.4.refs_1_.refs_12_, f32[128,1024]{1,0:T(8,128)S(1)} %shard_map.128.refs_5_.refs_2_, ...), custom_call_target="tpu_custom_call" | custom-call | flops 1000000 | bytes 100000 | tf_op jit(solution)/shard_map/pallas_call | solution.py:374
  25.3 1.3 %collective-permute-start.6 = (bf16[128,1024]{1,0:T(8,128)(2,1)S(1)}, bf16[128,1024]{1,0:T(8,128)(2,1)S(1)}, u32[]{:S(2)}, u32[]{:S(2)}) collective-permute-start(bf16[128,1024]{1,0:T(8,128)(2,1)S(1)} %get-tuple-element.61.refs_6_.refs_3_), channel_id=1, source_target_pairs={{4,0},{8,4},{12,8},{5,1},{9,5},{13,9},{6,2},{10,6},{14,10},{7,3},{... | collective-permute-start | bytes 786440 | tf_op jit(solution)/shard_map/ppermute | solution.py:19
  26.6 3.7 %collective-permute-done.5.refs_14_.refs_2_ = bf16[128,1024]{1,0:T(8,128)(2,1)S(1)} collective-permute-done((bf16[128,1024]{1,0:T(8,128)(2,1)S(1)}, bf16[128,1024]{1,0:T(8,128)(2,1)S(1)}, u32[]{:S(2)}, u32[]{:S(2)}) %collective-permute-start.5) | collective-permute-done | bytes 262176 | tf_op jit(solution)/shard_map/ppermute | solution.py:19
  30.3 2.4 %shard_map.131 = (bf16[128,1024]{1,0:T(8,128)(2,1)}, f32[16,128]{1,0:T(8,128)S(1)}) custom-call(f32[64,128]{1,0:T(8,128)S(1)} %get-tuple-element.52.refs_0_, f32[1024,128]{1,0:T(8,128)S(1)} %get-tuple-element.53.refs_1_, f32[128,128]{1,0:T(8,128)S(1)} %get-tuple-element.54.refs_2_, f32[128,128]{1,0:T(8,128)S(1)} %get-tuple-element.55.refs_2_.refs_3_, ...), custom_call_target="tpu_custom_call" | custom-call | flops 1000000 | bytes 100000 | tf_op jit(solution)/shard_map/pallas_call | solution.py:374
  32.7 0.0 collective-permute-start.7
  32.7 1.5 %collective-permute-start.8 = (f32[16,128]{1,0:T(8,128)S(1)}, f32[16,128]{1,0:T(8,128)S(1)}, u32[]{:S(2)}, u32[]{:S(2)}) collective-permute-start(f32[16,128]{1,0:T(8,128)S(1)} %get-tuple-element.88), channel_id=1, source_target_pairs={{0,2},{1,3},{2,0},{3,1},{4,6},{5,7},{6,4},{7,5},{8,10},{9,11},{10,... | collective-permute-start | bytes 24584 | tf_op jit(solution)/shard_map/ppermute | solution.py:403
  34.2 0.4 collective-permute-start.9
  34.6 0.0 collective-permute-done.7.refs_6_
  34.6 1.8 %collective-permute-done.8 = f32[16,128]{1,0:T(8,128)S(1)} collective-permute-done((f32[16,128]{1,0:T(8,128)S(1)}, f32[16,128]{1,0:T(8,128)S(1)}, u32[]{:S(2)}, u32[]{:S(2)}) %collective-permute-start.8) | collective-permute-done | bytes 8224 | tf_op jit(solution)/shard_map/ppermute | solution.py:403
  36.4 0.9 %collective-permute-done.9 = f32[16,128]{1,0:T(8,128)S(1)} collective-permute-done((f32[16,128]{1,0:T(8,128)S(1)}, f32[16,128]{1,0:T(8,128)S(1)}, u32[]{:S(2)}, u32[]{:S(2)}) %collective-permute-start.9) | collective-permute-done | bytes 8224 | tf_op jit(solution)/shard_map/ppermute | solution.py:403
  37.3 0.5 collective-permute-done.6.refs_3_
  37.7 1.3 %collective-permute-start.10 = (bf16[128,1024]{1,0:T(8,128)(2,1)S(1)}, bf16[128,1024]{1,0:T(8,128)(2,1)S(1)}, u32[]{:S(2)}, u32[]{:S(2)}) collective-permute-start(bf16[128,1024]{1,0:T(8,128)(2,1)S(1)} %collective-permute-done.6.refs_3_), channel_id=1, source_target_pairs={{4,0},{8,4},{5,1},{9,5},{6,2},{10,6},{7,3},{11,7},{20,16},{24,20},... | collective-permute-start | bytes 786440 | tf_op jit(solution)/shard_map/ppermute | solution.py:19
  39.0 0.9 %shard_map.132 = (f32[128,1024]{1,0:T(8,128)S(1)}, f32[128,1024]{1,0:T(8,128)S(1)}) custom-call(f32[64,128]{1,0:T(8,128)S(1)} %get-tuple-element.52.refs_0_, f32[128,128]{1,0:T(8,128)S(1)} %get-tuple-element.67.refs_1_, bf16[128,1024]{1,0:T(8,128)(2,1)S(1)} %get-tuple-element.57.refs_3_.refs_5_.refs_2_, ...), custom_call_target="tpu_custom_call" | custom-call | flops 1000000 | bytes 100000 | tf_op jit(solution)/shard_map/pallas_call | solution.py:374
  39.9 1.6 %shard_map.133 = (bf16[128,1024]{1,0:T(8,128)(2,1)}, f32[128,1024]{1,0:T(8,128)S(1)}, f32[128,1024]{1,0:T(8,128)S(1)}) custom-call(f32[64,128]{1,0:T(8,128)S(1)} %get-tuple-element.52.refs_0_, f32[128,128]{1,0:T(8,128)S(1)} %get-tuple-element.66.refs_1_, bf16[128,1024]{1,0:T(8,128)(2,1)S(1)} %collective-permute-done.3.refs_7_.refs_2_, ...), custom_call_target="tpu_custom_call" | custom-call | flops 1000000 | bytes 100000 | tf_op jit(solution)/shard_map/pallas_call | solution.py:374
  41.5 0.4 shard_map.134
  42.0 4.9 %collective-permute-start.11 = (f32[16,128]{1,0:T(8,128)S(1)}, f32[16,128]{1,0:T(8,128)S(1)}, u32[]{:S(2)}, u32[]{:S(2)}) collective-permute-start(f32[16,128]{1,0:T(8,128)S(1)} %add_add_fusion.refs_3_), channel_id=1, source_target_pairs={{0,12},{4,8},{8,4},{12,0},{1,13},{5,9},{9,5},{13,1},{2,14},{6,10},... | collective-permute-start | bytes 24584 | tf_op jit(solution)/shard_map/ppermute | solution.py:403
  46.9 0.0 collective-permute-start.12
  46.9 0.6 %collective-permute-start.13 = (f32[16,128]{1,0:T(8,128)S(1)}, f32[16,128]{1,0:T(8,128)S(1)}, u32[]{:S(2)}, u32[]{:S(2)}) collective-permute-start(f32[16,128]{1,0:T(8,128)S(1)} %add_add_fusion.refs_3_), channel_id=1, source_target_pairs={{0,4},{4,0},{8,12},{12,8},{1,5},{5,1},{9,13},{13,9},{2,6},{6,2},{1... | collective-permute-start | bytes 24584 | tf_op jit(solution)/shard_map/ppermute | solution.py:403
  47.5 1.5 %collective-permute-done.10.refs_3_ = bf16[128,1024]{1,0:T(8,128)(2,1)S(1)} collective-permute-done((bf16[128,1024]{1,0:T(8,128)(2,1)S(1)}, bf16[128,1024]{1,0:T(8,128)(2,1)S(1)}, u32[]{:S(2)}, u32[]{:S(2)}) %collective-permute-start.10) | collective-permute-done | bytes 262176 | tf_op jit(solution)/shard_map/ppermute | solution.py:19
  49.0 1.3 %shard_map.135 = (bf16[128,1024]{1,0:T(8,128)(2,1)}, bf16[128,1024]{1,0:T(8,128)(2,1)}) custom-call(bf16[1024,128]{1,0:T(8,128)(2,1)S(1)} %get-tuple-element.81.refs_0_, f32[1024,128]{1,0:T(8,128)S(1)} %get-tuple-element.82.refs_1_, bf16[128,1024]{1,0:T(8,128)(2,1)S(1)} %collective-permute-done.5.refs_14_.refs_2_, ...), custom_call_target="tpu_custom_call" | custom-call | flops 1000000 | bytes 100000 | tf_op jit(solution)/shard_map/pallas_call | solution.py:374
  50.4 0.0 collective-permute-done.11.refs_0_
  50.4 1.1 %collective-permute-done.12.refs_1_ = f32[16,128]{1,0:T(8,128)S(1)} collective-permute-done((f32[16,128]{1,0:T(8,128)S(1)}, f32[16,128]{1,0:T(8,128)S(1)}, u32[]{:S(2)}, u32[]{:S(2)}) %collective-permute-start.12) | collective-permute-done | bytes 8224 | tf_op jit(solution)/shard_map/ppermute | solution.py:403
  51.5 0.0 collective-permute-done.13.refs_2_
  51.5 0.6 %shard_map.136 = (f32[8,128]{1,0:T(8,128)}, f32[8,8]{1,0:T(8,128)}) custom-call(f32[16,128]{1,0:T(8,128)S(1)} %collective-permute-done.11.refs_0_, f32[16,128]{1,0:T(8,128)S(1)} %collective-permute-done.12.refs_1_, f32[16,128]{1,0:T(8,128)S(1)} %collective-permute-done.13.refs_2_, f32[16,128]{1,0:T(8,128)S(1)} %add_add_fusion.refs_3_), custom_call_target="tpu_custom_call" | custom-call | flops 1000000 | bytes 100000 | tf_op jit(solution)/shard_map/pallas_call | solution.py:374
  (1 shorter events, 0.0 us)
Async XLA Ops:
  0.6 19.3 %copy-start.1 = (f32[8,8]{1,0:T(8,128)S(1)}, f32[8,8]{1,0:T(8,128)}, u32[]{:S(2)}) copy-start(f32[8,8]{1,0:T(8,128)} %refs_1_.1) | copy-start | bytes 772
  0.6 11.9 %collective-permute-start = (bf16[128,1024]{1,0:T(8,128)(2,1)}, bf16[128,1024]{1,0:T(8,128)(2,1)S(1)}, u32[]{:S(2)}, u32[]{:S(2)}) collective-permute-start(bf16[128,1024]{1,0:T(8,128)(2,1)} %bitcast.15), channel_id=1, source_target_pairs={{0,4},{4,8},{8,12},{1,5},{5,9},{9,13},{2,6},{6,10},{10,14},{3,7},{... | collective-permute-start | bytes 786440 | tf_op jit(solution)/shard_map/ppermute | solution.py:19
  5.6 11.5 %collective-permute-start.2 = (bf16[128,1024]{1,0:T(8,128)(2,1)}, bf16[128,1024]{1,0:T(8,128)(2,1)S(1)}, u32[]{:S(2)}, u32[]{:S(2)}) collective-permute-start(bf16[128,1024]{1,0:T(8,128)(2,1)} %bitcast.17), channel_id=1, source_target_pairs={{0,4},{4,8},{8,12},{1,5},{5,9},{9,13},{2,6},{6,10},{10,14},{3,7},{... | collective-permute-start | bytes 786440 | tf_op jit(solution)/shard_map/ppermute | solution.py:19
  9.1 9.6 %collective-permute-start.3 = (bf16[128,1024]{1,0:T(8,128)(2,1)}, bf16[128,1024]{1,0:T(8,128)(2,1)S(1)}, u32[]{:S(2)}, u32[]{:S(2)}) collective-permute-start(bf16[128,1024]{1,0:T(8,128)(2,1)} %bitcast.13), channel_id=1, source_target_pairs={{4,0},{8,4},{12,8},{5,1},{9,5},{13,9},{6,2},{10,6},{14,10},{7,3},{... | collective-permute-start | bytes 786440 | tf_op jit(solution)/shard_map/ppermute | solution.py:19
  12.6 11.1 %collective-permute-start.1 = (bf16[128,1024]{1,0:T(8,128)(2,1)S(1)}, bf16[128,1024]{1,0:T(8,128)(2,1)S(1)}, u32[]{:S(2)}, u32[]{:S(2)}) collective-permute-start(bf16[128,1024]{1,0:T(8,128)(2,1)S(1)} %collective-permute-done.refs_4_.refs_8_), channel_id=1, source_target_pairs={{4,8},{8,12},{5,9},{9,13},{6,10},{10,14},{7,11},{11,15},{20,24},{2... | collective-permute-start | bytes 786440 | tf_op jit(solution)/shard_map/ppermute | solution.py:19
  17.1 7.0 %collective-permute-start.4 = (bf16[128,1024]{1,0:T(8,128)(2,1)S(1)}, bf16[128,1024]{1,0:T(8,128)(2,1)S(1)}, u32[]{:S(2)}, u32[]{:S(2)}) collective-permute-start(bf16[128,1024]{1,0:T(8,128)(2,1)S(1)} %collective-permute-done.2.refs_5_.refs_11_), channel_id=1, source_target_pairs={{4,8},{8,12},{5,9},{9,13},{6,10},{10,14},{7,11},{11,15},{20,24},{2... | collective-permute-start | bytes 786440 | tf_op jit(solution)/shard_map/ppermute | solution.py:19
  18.7 11.7 %collective-permute-start.5 = (bf16[128,1024]{1,0:T(8,128)(2,1)S(1)}, bf16[128,1024]{1,0:T(8,128)(2,1)S(1)}, u32[]{:S(2)}, u32[]{:S(2)}) collective-permute-start(bf16[128,1024]{1,0:T(8,128)(2,1)S(1)} %collective-permute-done.3.refs_7_.refs_2_), channel_id=1, source_target_pairs={{4,0},{8,4},{5,1},{9,5},{6,2},{10,6},{7,3},{11,7},{20,16},{24,20},... | collective-permute-start | bytes 786440 | tf_op jit(solution)/shard_map/ppermute | solution.py:19
  20.0 0.7 %copy-start.2 = (s32[1,4]{1,0:T(1,128)S(1)}, s32[1,4]{1,0:T(1,128)}, u32[]{:S(2)}) copy-start(s32[1,4]{1,0:T(1,128)} %refs_0_.1) | copy-start | bytes 52
  24.0 0.7 %copy-start = (f32[1024]{0:T(1024)S(1)}, f32[1024]{0:T(1024)}, u32[]{:S(2)}) copy-start(f32[1024]{0:T(1024)} %param.15) | copy-start | bytes 12292
  25.3 12.4 %collective-permute-start.6 = (bf16[128,1024]{1,0:T(8,128)(2,1)S(1)}, bf16[128,1024]{1,0:T(8,128)(2,1)S(1)}, u32[]{:S(2)}, u32[]{:S(2)}) collective-permute-start(bf16[128,1024]{1,0:T(8,128)(2,1)S(1)} %get-tuple-element.61.refs_6_.refs_3_), channel_id=1, source_target_pairs={{4,0},{8,4},{12,8},{5,1},{9,5},{13,9},{6,2},{10,6},{14,10},{7,3},{... | collective-permute-start | bytes 786440 | tf_op jit(solution)/shard_map/ppermute | solution.py:19
  32.7 1.9 %collective-permute-start.7 = (f32[16,128]{1,0:T(8,128)S(1)}, f32[16,128]{1,0:T(8,128)S(1)}, u32[]{:S(2)}, u32[]{:S(2)}) collective-permute-start(f32[16,128]{1,0:T(8,128)S(1)} %get-tuple-element.88), channel_id=1, source_target_pairs={{0,1},{1,0},{2,3},{3,2},{4,5},{5,4},{6,7},{7,6},{8,9},{9,8},{10,11... | collective-permute-start | bytes 24584 | tf_op jit(solution)/shard_map/ppermute | solution.py:403
  32.7 3.7 %collective-permute-start.8 = (f32[16,128]{1,0:T(8,128)S(1)}, f32[16,128]{1,0:T(8,128)S(1)}, u32[]{:S(2)}, u32[]{:S(2)}) collective-permute-start(f32[16,128]{1,0:T(8,128)S(1)} %get-tuple-element.88), channel_id=1, source_target_pairs={{0,2},{1,3},{2,0},{3,1},{4,6},{5,7},{6,4},{7,5},{8,10},{9,11},{10,... | collective-permute-start | bytes 24584 | tf_op jit(solution)/shard_map/ppermute | solution.py:403
  34.2 3.1 %collective-permute-start.9 = (f32[16,128]{1,0:T(8,128)S(1)}, f32[16,128]{1,0:T(8,128)S(1)}, u32[]{:S(2)}, u32[]{:S(2)}) collective-permute-start(f32[16,128]{1,0:T(8,128)S(1)} %get-tuple-element.88), channel_id=1, source_target_pairs={{0,3},{1,2},{2,1},{3,0},{4,7},{5,6},{6,5},{7,4},{8,11},{9,10},{10,... | collective-permute-start | bytes 24584 | tf_op jit(solution)/shard_map/ppermute | solution.py:403
  37.7 11.3 %collective-permute-start.10 = (bf16[128,1024]{1,0:T(8,128)(2,1)S(1)}, bf16[128,1024]{1,0:T(8,128)(2,1)S(1)}, u32[]{:S(2)}, u32[]{:S(2)}) collective-permute-start(bf16[128,1024]{1,0:T(8,128)(2,1)S(1)} %collective-permute-done.6.refs_3_), channel_id=1, source_target_pairs={{4,0},{8,4},{5,1},{9,5},{6,2},{10,6},{7,3},{11,7},{20,16},{24,20},... | collective-permute-start | bytes 786440 | tf_op jit(solution)/shard_map/ppermute | solution.py:19
  42.0 8.4 %collective-permute-start.11 = (f32[16,128]{1,0:T(8,128)S(1)}, f32[16,128]{1,0:T(8,128)S(1)}, u32[]{:S(2)}, u32[]{:S(2)}) collective-permute-start(f32[16,128]{1,0:T(8,128)S(1)} %add_add_fusion.refs_3_), channel_id=1, source_target_pairs={{0,12},{4,8},{8,4},{12,0},{1,13},{5,9},{9,5},{13,1},{2,14},{6,10},... | collective-permute-start | bytes 24584 | tf_op jit(solution)/shard_map/ppermute | solution.py:403
  46.9 4.5 %collective-permute-start.12 = (f32[16,128]{1,0:T(8,128)S(1)}, f32[16,128]{1,0:T(8,128)S(1)}, u32[]{:S(2)}, u32[]{:S(2)}) collective-permute-start(f32[16,128]{1,0:T(8,128)S(1)} %add_add_fusion.refs_3_), channel_id=1, source_target_pairs={{0,8},{4,12},{8,0},{12,4},{1,9},{5,13},{9,1},{13,5},{2,10},{6,14},... | collective-permute-start | bytes 24584 | tf_op jit(solution)/shard_map/ppermute | solution.py:403
  46.9 4.5 %collective-permute-start.13 = (f32[16,128]{1,0:T(8,128)S(1)}, f32[16,128]{1,0:T(8,128)S(1)}, u32[]{:S(2)}, u32[]{:S(2)}) collective-permute-start(f32[16,128]{1,0:T(8,128)S(1)} %add_add_fusion.refs_3_), channel_id=1, source_target_pairs={{0,4},{4,0},{8,12},{12,8},{1,5},{5,1},{9,13},{13,9},{2,6},{6,2},{1... | collective-permute-start | bytes 24584 | tf_op jit(solution)/shard_map/ppermute | solution.py:403

commit v14 on v13

--- a/solution.py
+++ b/solution.py
@@ -36,7 +36,7 @@
 
 class Pair:
     def __init__(self, mask, table, heads, hops, flipped=False, near=None):
-        rows = mask.shape[0]
+        rows = table.shape[1]
         self.table, self.heads, self.levels = table, heads, table.shape[0] // heads
         self.mask, self.hops, self.near = mask[...], hops, near
         self.far = (hops - 1) * rows + 1 >= 2 ** (self.levels - 2)
@@ -49,7 +49,7 @@
     def half_bias(self, head):
         def level_row(level):
             at = level * self.heads + head
-            return self.table[at : at + 1, :]
+            return self.table[at : at + 1, : self.mask.shape[1]]
 
         value = level_row(self.levels - 1)
         if self.far:
@@ -102,9 +102,19 @@
     in_stages(heads, scores, weigh)
 
 
-def first_kernel(plan, heads, scaling, lengths, bias, *refs):
+def far_start(lengths, block, reach, rows):
+    first = (lax.axis_index("ctx") + block) * rows
+    end, start = jnp.int32(0), jnp.int32(0)
+    for user in range(lengths.shape[1]):
+        end = end + lengths[0, user]
+        start = jnp.where(first >= end, end, start)
+    return start - (first - reach * rows)
+
+
+def first_kernel(plan, cut, heads, scaling, lengths, bias, *refs):
     inputs, refs = refs[:5], refs[5:]
     table, near, masks, refs = refs[0], refs[1], refs[2 : 2 + len(plan)], refs[2 + len(plan) :]
+    late, refs = refs[0], refs[1:]
     held, out, arrived = refs[:5], refs[5], refs[6]
     copies = [
         pltpu.make_async_copy(source, target, arrived.at[at])
@@ -128,12 +138,20 @@
         near[head * rows : (head + 1) * rows, :] = value
     for (block, hops, flipped), mask in zip(plan, masks):
         query_dim, key_dim = (1, 0) if flipped else (0, 1)
-        line = (1, rows) if flipped else (rows, 1)
+        line = (1, mask.shape[1]) if flipped else (mask.shape[0], 1)
         first = (lax.axis_index("ctx") + block) * rows
         query_pos = first + lax.broadcasted_iota(jnp.int32, line, query_dim)
-        key_pos = first - hops * rows + lax.broadcasted_iota(jnp.int32, mask.shape, key_dim)
+        key_first = first - hops * rows + rows - mask.shape[key_dim]
+        key_pos = key_first + lax.broadcasted_iota(jnp.int32, mask.shape, key_dim)
         seen = (key_pos >= user_starts(lengths, query_pos)) & (key_pos <= query_pos)
-        mask[...] = jnp.where(seen, 1.0, 0.0).astype(F32)
+        value = jnp.where(seen, 1.0, 0.0).astype(F32)
+        if mask.shape == (rows, rows):
+            mask[...] = value
+            continue
+        at = 0 if mask.shape[0] == rows else 1
+        is_late = jnp.where(far_start(lengths, block, hops, rows) > cut, 1.0, 0.0).astype(F32)
+        late[8 * at : 8 * at + 8, :] = jnp.full((8, rows), is_late, F32)
+        mask[...] = value * (is_late if at else 1.0 - is_late)
     for copy in copies:
         copy.wait()
     query, key, value = held[:3]
@@ -304,13 +322,39 @@
     copy.wait()
 
 
+def message_kernel(hops, heads, scaling, *refs):
+    table, mask, late, query, grad, key, value, out = refs
+    tail, cut, width = mask.shape[0], out.shape[0], query.shape[1] // heads
+    pair = Pair(mask, table, heads, hops, True)
+    is_late = late[8:9, :width] > 0.5
+
+    def scores(head):
+        cols = columns(head, width)
+        score = contract(key[cut:, cols], query[:, cols], 1, 1)
+        return score, contract(value[cut:, cols], grad[:, cols], 1, 1)
+
+    def choose(head, found):
+        cols = columns(head, width)
+        half = pair.half_logits(found[0], head, scaling)
+        tanh = jnp.tanh(half)
+        rounded = (found[1] * (slope_of(half, tanh) * pair.mask)).astype(BF16)
+        weights = ((half + half * tanh) * pair.mask).astype(BF16)
+        parts = [contract(rounded, query[:, cols], 1, 0), contract(weights, grad[:, cols], 1, 0)]
+        for at, part in enumerate(parts):
+            lines = slice(at * tail, (at + 1) * tail)
+            out[lines, cols] = jnp.where(is_late, part, grad[lines, cols].astype(F32)).astype(BF16)
+        out[2 * tail :, cols] = grad[2 * tail : cut, cols]
+
+    in_stages(heads, scores, choose)
+
+
 def slopes_kernel(hops, heads, scaling, table, mask, query, key, weights, slopes):
     pair = Pair(mask, table, heads, hops, True)
-    rows, width = query.shape[0], query.shape[1] // heads
+    rows, cut, width = mask.shape[0], mask.shape[1], query.shape[1] // heads
 
     def scores(head):
         cols = columns(head, width)
-        return contract(key[:, cols], query[:, cols], 1, 1)
+        return contract(key[:, cols], query[:cut, cols], 1, 1)
 
     def derive(head, found):
         half = pair.half_logits(found, head, scaling)
@@ -323,9 +367,11 @@
 
 
 def last_kernel(heads, scaling, *refs):
-    weights, slopes, query, grad, value, key_in, value_in = refs[:7]
-    outs, held, written = refs[7:9], refs[9:11], refs[11]
-    rows, width = query.shape[0], query.shape[1] // heads
+    weights, slopes, late, query, message, value, key_in, value_in = refs[:8]
+    outs, held, written = refs[8:10], refs[10:12], refs[12]
+    rows, cut, width = query.shape[0], message.shape[0], query.shape[1] // heads
+    tail = rows - cut
+    is_late = late[0:1, :width]
     copies = []
     ends = [*range(1, heads - 1, 2), heads - 2, heads - 1]
 
@@ -336,15 +382,20 @@
 
     def scores(head):
         cols = columns(head, width)
-        return contract(value[:, cols], grad[:, cols], 1, 1)
+        return contract(value[:, cols], message[:, cols], 1, 1)
 
     def differentiate(head, found):
         cols, lines = columns(head, width), columns(head, rows)
         rounded = (found * slopes[lines, :]).astype(BF16)
-        key_part = key_in[:, cols] + contract(rounded, query[:, cols], 1, 0)
-        value_part = value_in[:, cols] + contract(weights[lines, :], grad[:, cols], 1, 0)
-        held[0][:, cols] = (key_part * scaling).astype(BF16)
-        held[1][:, cols] = value_part.astype(BF16)
+        parts = [
+            contract(rounded, query[:cut, cols], 1, 0),
+            contract(weights[lines, :], message[:, cols], 1, 0),
+        ]
+        for at, (part, before) in enumerate(zip(parts, (key_in, value_in))):
+            factor = 1.0 if at else scaling
+            held[at][:cut, cols] = ((before[:cut, cols] + part[:cut]) * factor).astype(BF16)
+            sent = message[at * tail : (at + 1) * tail, cols].astype(F32) * is_late
+            held[at][cut:, cols] = ((before[cut:, cols] + part[cut:] + sent) * factor).astype(BF16)
         if head in ends:
             before = ends[ends.index(head) - 1] + 1 if head != ends[0] else 0
             for at in (0, 1):
@@ -426,11 +477,14 @@
 
     hop_list = tuple(range(reach + 1))
     plan = [(0, hops, False) for hops in hop_list] + [(hops, hops, True) for hops in hop_list]
+    plan += [(reach - 1, reach, True)]
+    cut = rows - rows // 4
+    shapes = [(rows, rows)] * (len(plan) - 2) + [(rows, cut), (rows - cut, rows), (16, rows)]
     outs = [jax.ShapeDtypeStruct((count * heads, rows), F32) for count in (levels, rows)]
-    outs += [jax.ShapeDtypeStruct((rows, rows), F32)] * len(plan)
+    outs += [jax.ShapeDtypeStruct(shape, F32) for shape in shapes]
     outs += [narrow] * len(inputs) + [wide]
     table, near, *found = on_device(
-        partial(first_kernel, plan, heads, scaling),
+        partial(first_kernel, plan, cut, heads, scaling),
         outs,
         (),
         (user_lengths, rel_bias),
@@ -438,7 +492,7 @@
         scratch=[pltpu.SemaphoreType.DMA((len(inputs),))],
     )
     masks, flipped = found[: reach + 1], found[reach + 1 : 2 * reach + 2]
-    query, key, value, gate, grad, attention = found[2 * reach + 2 :]
+    sender_mask, late, query, key, value, gate, grad, attention = found[2 * reach + 2 :]
 
     later_queries = [query, arrived[2]]
     keys, values = [key, arrived[0]], [value, arrived[1]]
@@ -490,6 +544,12 @@
     )
     for hops in range(1, reach):
         arrived, *pieces = lax.optimization_barrier((later_grads[hops], *pieces))
+        if hops + 1 == reach:
+            (arrived,) = on_device(
+                partial(message_kernel, reach, heads, scaling),
+                [jax.ShapeDtypeStruct((cut, features), BF16)],
+                (table, sender_mask, late, later_queries[hops], arrived, keys[1], values[1]),
+            )
         later_grads.append(passed_along(arrived, "ctx", -1, hops + 1))
         if hops == 1:
             gate_grad, *key_grads = on_device(
@@ -507,7 +567,7 @@
             )
     far_tables = on_device(
         partial(slopes_kernel, reach, heads, scaling),
-        [jax.ShapeDtypeStruct(stacked, BF16), jax.ShapeDtypeStruct(stacked, F32)],
+        [jax.ShapeDtypeStruct((heads * rows, cut), kind) for kind in (BF16, F32)],
         (table, flipped[reach], later_queries[reach], key),
         ahead=key_grads[:1],
     )
@@ -517,7 +577,7 @@
     key_grad, value_grad = on_device(
         partial(last_kernel, heads, scaling),
         [narrow, narrow],
-        (*far_tables, later_queries[reach], later_grads[reach], value, *key_grads),
+        (*far_tables, late, later_queries[reach], later_grads[reach], value, *key_grads),
         far_outs=2,
         scratch=[pltpu.VMEM((rows, features), BF16)] * 2 + [pltpu.SemaphoreType.DMA((2 * heads,))],
     )
@@ -525,7 +585,7 @@
     gain_grad, bias_grad = on_device(
         sum_kernel,
         [jax.ShapeDtypeStruct((8, lanes), F32), jax.ShapeDtypeStruct((levels, heads), F32)],
-        pieces[::-1],
+        pieces,
     )
     return (
         query_grad[None],

time: 52.4 us -> 52.8 us (level)
  waiting for transfers between devices: 16.4 us -> 15.4 us
  starting transfers between devices: 22.3 us -> 23.1 us
  Pallas kernels: 11.2 us -> 11.8 us
    ppermute x8, waiting for transfers between devices: 12.6 us -> 10.7 us  [passed_along(): lax.ppermute(array, axis, [(i, i + by) for i in range(first, last + 1)])]
    ppermute x6, waiting for transfers between devices: 3.77 us -> 4.8 us  [exchanged(): lax.ppermute(array, axis, [(i, i ^ distance) for i in range(size)])]
    ppermute x6, starting transfers between devices: 7.41 us -> 8.15 us  [exchanged(): lax.ppermute(array, axis, [(i, i ^ distance) for i in range(size)])]
    pallas_call x10 -> x11, Pallas kernels: 11.2 us -> 11.8 us  [on_device(): pl.pallas_call(body, out_shape=outs, in_specs=[pl.BlockSpec(memory_space=...]
  transfers between devices with their start and end apart: 14 -> 14, of which waited for: 9 -> 6; matrix products, arithmetic and copies ran while one was open for 0% -> 0% of each run, Pallas kernels for 20% -> 20%
where the time goes in v14:
time: 52.8 us; the launch traced here: 52.5 us
  starting transfers between devices  23.1 us (44%)
  waiting for transfers between devices  15.4 us (29%)
  Pallas kernels  11.8 us (22%)
  local copies, waits for them, and re-layouts  1.31 us (2%)
  between operations  0.82 us (2%)
    ppermute x8, starting transfers between devices, passed_along(): lax.ppermute(array, axis, [(i, i + by) for i in range(first, last + 1)])  14.9 us
    pallas_call x11, Pallas kernels, on_device(): pl.pallas_call(body, out_shape=outs, in_specs=[pl.BlockSpec(memory_space=...  11.8 us
    ppermute x8, waiting for transfers between devices, passed_along(): lax.ppermute(array, axis, [(i, i + by) for i in range(first, last + 1)])  10.7 us
    ppermute x6, starting transfers between devices, exchanged(): lax.ppermute(array, axis, [(i, i ^ distance) for i in range(size)])  8.15 us
    ppermute x6, waiting for transfers between devices, exchanged(): lax.ppermute(array, axis, [(i, i ^ distance) for i in range(size)])  4.8 us
    unnamed x6, local copies, waits for them, and re-layouts  1.31 us
  transfers between devices with their start and end apart: 14, of which 6 were waited for; matrix products, arithmetic and copies ran while one was open for 0% of the time, Pallas kernels for 20%

profile of v14, /device:TPU:0, one launch (start us, length us, event | category | flops | bytes accessed | tf_op | source)
XLA Modules:
  0.0 52.5 jit_solution(3669956994892184204)
XLA Ops:
  0.6 0.0 copy-start.1
  0.6 4.9 %collective-permute-start = (bf16[128,1024]{1,0:T(8,128)(2,1)}, bf16[128,1024]{1,0:T(8,128)(2,1)S(1)}, u32[]{:S(2)}, u32[]{:S(2)}) collective-permute-start(bf16[128,1024]{1,0:T(8,128)(2,1)} %bitcast.15), channel_id=1, source_target_pairs={{0,4},{4,8},{8,12},{1,5},{5,9},{9,13},{2,6},{6,10},{10,14},{3,7},{... | collective-permute-start | bytes 786440 | tf_op jit(solution)/shard_map/ppermute | solution.py:19
  5.6 3.5 %collective-permute-start.2 = (bf16[128,1024]{1,0:T(8,128)(2,1)}, bf16[128,1024]{1,0:T(8,128)(2,1)S(1)}, u32[]{:S(2)}, u32[]{:S(2)}) collective-permute-start(bf16[128,1024]{1,0:T(8,128)(2,1)} %bitcast.17), channel_id=1, source_target_pairs={{0,4},{4,8},{8,12},{1,5},{5,9},{9,13},{2,6},{6,10},{10,14},{3,7},{... | collective-permute-start | bytes 786440 | tf_op jit(solution)/shard_map/ppermute | solution.py:19
  9.1 1.3 %collective-permute-start.3 = (bf16[128,1024]{1,0:T(8,128)(2,1)}, bf16[128,1024]{1,0:T(8,128)(2,1)S(1)}, u32[]{:S(2)}, u32[]{:S(2)}) collective-permute-start(bf16[128,1024]{1,0:T(8,128)(2,1)} %bitcast.13), channel_id=1, source_target_pairs={{4,0},{8,4},{12,8},{5,1},{9,5},{13,9},{6,2},{10,6},{14,10},{7,3},{... | collective-permute-start | bytes 786440 | tf_op jit(solution)/shard_map/ppermute | solution.py:19
  10.4 2.2 %collective-permute-done.refs_4_.refs_8_.refs_5_ = bf16[128,1024]{1,0:T(8,128)(2,1)S(1)} collective-permute-done((bf16[128,1024]{1,0:T(8,128)(2,1)}, bf16[128,1024]{1,0:T(8,128)(2,1)S(1)}, u32[]{:S(2)}, u32[]{:S(2)}) %collective-permute-start) | collective-permute-done | bytes 262176 | tf_op jit(solution)/shard_map/ppermute | solution.py:19
  12.6 0.7 %collective-permute-start.1 = (bf16[128,1024]{1,0:T(8,128)(2,1)S(1)}, bf16[128,1024]{1,0:T(8,128)(2,1)S(1)}, u32[]{:S(2)}, u32[]{:S(2)}) collective-permute-start(bf16[128,1024]{1,0:T(8,128)(2,1)S(1)} %collective-permute-done.refs_4_.refs_8_.refs_5_), channel_id=1, source_target_pairs={{4,8},{8,12},{5,9},{9,13},{6,10},{10,14},{7,11},{11,15},{20,24},{2... | collective-permute-start | bytes 786440 | tf_op jit(solution)/shard_map/ppermute | solution.py:19
  13.3 3.8 %collective-permute-done.2.refs_5_.refs_11_.refs_6_ = bf16[128,1024]{1,0:T(8,128)(2,1)S(1)} collective-permute-done((bf16[128,1024]{1,0:T(8,128)(2,1)}, bf16[128,1024]{1,0:T(8,128)(2,1)S(1)}, u32[]{:S(2)}, u32[]{:S(2)}) %collective-permute-start.2) | collective-permute-done | bytes 262176 | tf_op jit(solution)/shard_map/ppermute | solution.py:19
  17.1 0.7 %collective-permute-start.4 = (bf16[128,1024]{1,0:T(8,128)(2,1)S(1)}, bf16[128,1024]{1,0:T(8,128)(2,1)S(1)}, u32[]{:S(2)}, u32[]{:S(2)}) collective-permute-start(bf16[128,1024]{1,0:T(8,128)(2,1)S(1)} %collective-permute-done.2.refs_5_.refs_11_.refs_6_), channel_id=1, source_target_pairs={{4,8},{8,12},{5,9},{9,13},{6,10},{10,14},{7,11},{11,15},{20,24},{2... | collective-permute-start | bytes 786440 | tf_op jit(solution)/shard_map/ppermute | solution.py:19
  17.7 0.9 %collective-permute-done.3.refs_7_.refs_2_.refs_3_ = bf16[128,1024]{1,0:T(8,128)(2,1)S(1)} collective-permute-done((bf16[128,1024]{1,0:T(8,128)(2,1)}, bf16[128,1024]{1,0:T(8,128)(2,1)S(1)}, u32[]{:S(2)}, u32[]{:S(2)}) %collective-permute-start.3) | collective-permute-done | bytes 262176 | tf_op jit(solution)/shard_map/ppermute | solution.py:19
  18.7 1.3 %collective-permute-start.5 = (bf16[128,1024]{1,0:T(8,128)(2,1)S(1)}, bf16[128,1024]{1,0:T(8,128)(2,1)S(1)}, u32[]{:S(2)}, u32[]{:S(2)}) collective-permute-start(bf16[128,1024]{1,0:T(8,128)(2,1)S(1)} %collective-permute-done.3.refs_7_.refs_2_.refs_3_), channel_id=1, source_target_pairs={{4,0},{8,4},{5,1},{9,5},{6,2},{10,6},{7,3},{11,7},{20,16},{24,20},... | collective-permute-start | bytes 786440 | tf_op jit(solution)/shard_map/ppermute | solution.py:19
  20.0 0.0 copy-start.2
  20.0 0.0 copy-done.1
  20.0 0.6 %copy-done.2 = s32[1,4]{1,0:T(1,128)S(1)} copy-done((s32[1,4]{1,0:T(1,128)S(1)}, s32[1,4]{1,0:T(1,128)}, u32[]{:S(2)}) %copy-start.2) | copy-done | bytes 40
  20.6 2.5 %shard_map.127 = (f32[64,128]{1,0:T(8,128)S(1)}, f32[1024,128]{1,0:T(8,128)S(1)}, f32[128,128]{1,0:T(8,128)S(1)}, f32[128,128]{1,0:T(8,128)S(1)}, f32[128,128]{1...) custom-call(s32[1,4]{1,0:T(1,128)S(1)} %copy-done.2, ...), custom_call_target="tpu_custom_call" | custom-call | flops 1000000 | bytes 100000 | tf_op jit(solution)/shard_map/pallas_call | solution.py:425
  23.1 0.6 %shard_map.128.refs_5_.refs_2_ = f32[128,1024]{1,0:T(8,128)S(1)} custom-call(f32[64,128]{1,0:T(8,128)S(1)} %get-tuple-element.54.refs_0_, f32[1024,128]{1,0:T(8,128)S(1)} %get-tuple-element.55.refs_1_, f32[128,128]{1,0:T(8,128)S(1)} %get-tuple-element.57.refs_2_.refs_3_, bf16[128,1024]{1,0:T(8,128)(2,1)S(1)} %get-tuple-element.59.refs_3_.refs_5_.refs_2_, ...), custom_call_target="tpu_custom_call" | custom-call | flops 1000000 | bytes 100000 | tf_op jit(solution)/shard_map/pallas_call | solution.py:425
  23.7 0.0 collective-permute-done.1.refs_4_.refs_9_
  23.7 0.3 shard_map.129.refs_0_
  24.0 0.0 copy-start
  24.0 0.0 collective-permute-done.4.refs_1_.refs_12_
  24.0 0.7 %copy-done = f32[1024]{0:T(1024)S(1)} copy-done((f32[1024]{0:T(1024)S(1)}, f32[1024]{0:T(1024)}, u32[]{:S(2)}) %copy-start) | copy-done | bytes 4120
  24.7 0.6 %shard_map.130 = (f32[128,1024]{1,0:T(8,128)S(1)}, bf16[128,1024]{1,0:T(8,128)(2,1)S(1)}, f32[1,1024]{1,0:T(1,128)S(1)}) custom-call(bf16[1024,128]{1,0:T(8,128)(2,1)S(1)} %shard_map.129.refs_0_, bf16[128,1024]{1,0:T(8,128)(2,1)S(1)} %collective-permute-done.4.refs_1_.refs_12_, f32[128,1024]{1,0:T(8,128)S(1)} %shard_map.128.refs_5_.refs_2_, ...), custom_call_target="tpu_custom_call" | custom-call | flops 1000000 | bytes 100000 | tf_op jit(solution)/shard_map/pallas_call | solution.py:425
  25.3 1.3 %collective-permute-start.6 = (bf16[128,1024]{1,0:T(8,128)(2,1)S(1)}, bf16[128,1024]{1,0:T(8,128)(2,1)S(1)}, u32[]{:S(2)}, u32[]{:S(2)}) collective-permute-start(bf16[128,1024]{1,0:T(8,128)(2,1)S(1)} %get-tuple-element.63.refs_6_.refs_3_), channel_id=1, source_target_pairs={{4,0},{8,4},{12,8},{5,1},{9,5},{13,9},{6,2},{10,6},{14,10},{7,3},{... | collective-permute-start | bytes 786440 | tf_op jit(solution)/shard_map/ppermute | solution.py:19
  26.6 3.7 %collective-permute-done.5.refs_14_.refs_2_.refs_3_ = bf16[128,1024]{1,0:T(8,128)(2,1)S(1)} collective-permute-done((bf16[128,1024]{1,0:T(8,128)(2,1)S(1)}, bf16[128,1024]{1,0:T(8,128)(2,1)S(1)}, u32[]{:S(2)}, u32[]{:S(2)}) %collective-permute-start.5) | collective-permute-done | bytes 262176 | tf_op jit(solution)/shard_map/ppermute | solution.py:19
  30.3 2.4 %shard_map.131 = (bf16[128,1024]{1,0:T(8,128)(2,1)}, f32[16,128]{1,0:T(8,128)S(1)}) custom-call(f32[64,128]{1,0:T(8,128)S(1)} %get-tuple-element.54.refs_0_, f32[1024,128]{1,0:T(8,128)S(1)} %get-tuple-element.55.refs_1_, f32[128,128]{1,0:T(8,128)S(1)} %get-tuple-element.56.refs_2_, f32[128,128]{1,0:T(8,128)S(1)} %get-tuple-element.57.refs_2_.refs_3_, ...), custom_call_target="tpu_custom_call" | custom-call | flops 1000000 | bytes 100000 | tf_op jit(solution)/shard_map/pallas_call | solution.py:425
  32.7 0.0 collective-permute-start.7
  32.7 1.6 %collective-permute-start.9 = (f32[16,128]{1,0:T(8,128)S(1)}, f32[16,128]{1,0:T(8,128)S(1)}, u32[]{:S(2)}, u32[]{:S(2)}) collective-permute-start(f32[16,128]{1,0:T(8,128)S(1)} %get-tuple-element.92), channel_id=1, source_target_pairs={{0,3},{1,2},{2,1},{3,0},{4,7},{5,6},{6,5},{7,4},{8,11},{9,10},{10,... | collective-permute-start | bytes 24584 | tf_op jit(solution)/shard_map/ppermute | solution.py:454
  34.3 0.5 %collective-permute-start.8 = (f32[16,128]{1,0:T(8,128)S(1)}, f32[16,128]{1,0:T(8,128)S(1)}, u32[]{:S(2)}, u32[]{:S(2)}) collective-permute-start(f32[16,128]{1,0:T(8,128)S(1)} %get-tuple-element.92), channel_id=1, source_target_pairs={{0,2},{1,3},{2,0},{3,1},{4,6},{5,7},{6,4},{7,5},{8,10},{9,11},{10,... | collective-permute-start | bytes 24584 | tf_op jit(solution)/shard_map/ppermute | solution.py:454
  34.8 0.0 collective-permute-done.7.refs_6_
  34.9 0.9 %shard_map.132 = (f32[128,1024]{1,0:T(8,128)S(1)}, f32[128,1024]{1,0:T(8,128)S(1)}) custom-call(f32[64,128]{1,0:T(8,128)S(1)} %get-tuple-element.54.refs_0_, f32[128,128]{1,0:T(8,128)S(1)} %get-tuple-element.69.refs_1_, bf16[128,1024]{1,0:T(8,128)(2,1)S(1)} %get-tuple-element.59.refs_3_.refs_5_.refs_2_, ...), custom_call_target="tpu_custom_call" | custom-call | flops 1000000 | bytes 100000 | tf_op jit(solution)/shard_map/pallas_call | solution.py:425
  35.7 0.0 collective-permute-done.9
  35.8 2.2 %collective-permute-done.8 = f32[16,128]{1,0:T(8,128)S(1)} collective-permute-done((f32[16,128]{1,0:T(8,128)S(1)}, f32[16,128]{1,0:T(8,128)S(1)}, u32[]{:S(2)}, u32[]{:S(2)}) %collective-permute-start.8) | collective-permute-done | bytes 8224 | tf_op jit(solution)/shard_map/ppermute | solution.py:454
  38.0 0.0 collective-permute-done.6.refs_3_.refs_4_
  38.0 0.6 %shard_map.135 = bf16[96,1024]{1,0:T(8,128)(2,1)S(1)} custom-call(f32[64,128]{1,0:T(8,128)S(1)} %get-tuple-element.54.refs_0_, f32[32,128]{1,0:T(8,128)S(1)} %get-tuple-element.86.refs_1_, f32[16,128]{1,0:T(8,128)S(1)} %get-tuple-element.85.refs_2_, bf16[128,1024]{1,0:T(8,128)(2,1)S(1)} %collective-permute-done.3.refs_7_.refs_2_.refs_3_, ...), custom_call_target="tpu_custom_call" | custom-call | flops 1000000 | bytes 100000 | tf_op jit(solution)/shard_map/pallas_call | solution.py:425
  38.6 1.3 %collective-permute-start.10 = (bf16[96,1024]{1,0:T(8,128)(2,1)S(1)}, bf16[96,1024]{1,0:T(8,128)(2,1)S(1)}, u32[]{:S(2)}, u32[]{:S(2)}) collective-permute-start(bf16[96,1024]{1,0:T(8,128)(2,1)S(1)} %shard_map.135), channel_id=1, source_target_pairs={{4,0},{8,4},{5,1},{9,5},{6,2},{10,6},{7,3},{11,7},{20,16},{24,20},... | collective-permute-start | bytes 589832 | tf_op jit(solution)/shard_map/ppermute | solution.py:19
  39.9 1.6 %shard_map.133 = (bf16[128,1024]{1,0:T(8,128)(2,1)}, f32[128,1024]{1,0:T(8,128)S(1)}, f32[128,1024]{1,0:T(8,128)S(1)}) custom-call(f32[64,128]{1,0:T(8,128)S(1)} %get-tuple-element.54.refs_0_, f32[128,128]{1,0:T(8,128)S(1)} %get-tuple-element.68.refs_1_, bf16[128,1024]{1,0:T(8,128)(2,1)S(1)} %collective-permute-done.3.refs_7_.refs_2_.refs_3_, ...), custom_call_target="tpu_custom_call" | custom-call | flops 1000000 | bytes 100000 | tf_op jit(solution)/shard_map/pallas_call | solution.py:425
  41.5 0.4 shard_map.134
  41.9 5.4 %collective-permute-start.13 = (f32[16,128]{1,0:T(8,128)S(1)}, f32[16,128]{1,0:T(8,128)S(1)}, u32[]{:S(2)}, u32[]{:S(2)}) collective-permute-start(f32[16,128]{1,0:T(8,128)S(1)} %add_add_fusion.refs_0_), channel_id=1, source_target_pairs={{0,12},{4,8},{8,4},{12,0},{1,13},{5,9},{9,5},{13,1},{2,14},{6,10},... | collective-permute-start | bytes 24584 | tf_op jit(solution)/shard_map/ppermute | solution.py:454
  47.3 0.0 collective-permute-start.12
  47.3 0.6 %collective-permute-start.11 = (f32[16,128]{1,0:T(8,128)S(1)}, f32[16,128]{1,0:T(8,128)S(1)}, u32[]{:S(2)}, u32[]{:S(2)}) collective-permute-start(f32[16,128]{1,0:T(8,128)S(1)} %add_add_fusion.refs_0_), channel_id=1, source_target_pairs={{0,4},{4,0},{8,12},{12,8},{1,5},{5,1},{9,13},{13,9},{2,6},{6,2},{1... | collective-permute-start | bytes 24584 | tf_op jit(solution)/shard_map/ppermute | solution.py:454
  47.9 0.0 collective-permute-done.10.refs_4_
  47.9 1.3 %shard_map.136 = (bf16[128,1024]{1,0:T(8,128)(2,1)}, bf16[128,1024]{1,0:T(8,128)(2,1)}) custom-call(bf16[1024,96]{1,0:T(8,128)(2,1)S(1)} %get-tuple-element.83.refs_0_, f32[1024,96]{1,0:T(8,128)S(1)} %get-tuple-element.84.refs_1_, f32[16,128]{1,0:T(8,128)S(1)} %get-tuple-element.85.refs_2_, ...), custom_call_target="tpu_custom_call" | custom-call | flops 1000000 | bytes 100000 | tf_op jit(solution)/shard_map/pallas_call | solution.py:425
  49.3 0.0 collective-permute-done.13.refs_3_
  49.3 2.6 %collective-permute-done.12.refs_2_ = f32[16,128]{1,0:T(8,128)S(1)} collective-permute-done((f32[16,128]{1,0:T(8,128)S(1)}, f32[16,128]{1,0:T(8,128)S(1)}, u32[]{:S(2)}, u32[]{:S(2)}) %collective-permute-start.12) | collective-permute-done | bytes 8224 | tf_op jit(solution)/shard_map/ppermute | solution.py:454
  51.8 0.0 collective-permute-done.11.refs_1_
  51.8 0.6 %shard_map.137 = (f32[8,128]{1,0:T(8,128)}, f32[8,8]{1,0:T(8,128)}) custom-call(f32[16,128]{1,0:T(8,128)S(1)} %add_add_fusion.refs_0_, f32[16,128]{1,0:T(8,128)S(1)} %collective-permute-done.11.refs_1_, f32[16,128]{1,0:T(8,128)S(1)} %collective-permute-done.12.refs_2_, f32[16,128]{1,0:T(8,128)S(1)} %collective-permute-done.13.refs_3_), custom_call_target="tpu_custom_call" | custom-call | flops 1000000 | bytes 100000 | tf_op jit(solution)/shard_map/pallas_call | solution.py:425
  (1 shorter events, 0.0 us)
Async XLA Ops:
  0.6 19.3 %copy-start.1 = (f32[8,8]{1,0:T(8,128)S(1)}, f32[8,8]{1,0:T(8,128)}, u32[]{:S(2)}) copy-start(f32[8,8]{1,0:T(8,128)} %refs_1_.1) | copy-start | bytes 772
  0.6 11.9 %collective-permute-start = (bf16[128,1024]{1,0:T(8,128)(2,1)}, bf16[128,1024]{1,0:T(8,128)(2,1)S(1)}, u32[]{:S(2)}, u32[]{:S(2)}) collective-permute-start(bf16[128,1024]{1,0:T(8,128)(2,1)} %bitcast.15), channel_id=1, source_target_pairs={{0,4},{4,8},{8,12},{1,5},{5,9},{9,13},{2,6},{6,10},{10,14},{3,7},{... | collective-permute-start | bytes 786440 | tf_op jit(solution)/shard_map/ppermute | solution.py:19
  5.6 11.5 %collective-permute-start.2 = (bf16[128,1024]{1,0:T(8,128)(2,1)}, bf16[128,1024]{1,0:T(8,128)(2,1)S(1)}, u32[]{:S(2)}, u32[]{:S(2)}) collective-permute-start(bf16[128,1024]{1,0:T(8,128)(2,1)} %bitcast.17), channel_id=1, source_target_pairs={{0,4},{4,8},{8,12},{1,5},{5,9},{9,13},{2,6},{6,10},{10,14},{3,7},{... | collective-permute-start | bytes 786440 | tf_op jit(solution)/shard_map/ppermute | solution.py:19
  9.1 9.6 %collective-permute-start.3 = (bf16[128,1024]{1,0:T(8,128)(2,1)}, bf16[128,1024]{1,0:T(8,128)(2,1)S(1)}, u32[]{:S(2)}, u32[]{:S(2)}) collective-permute-start(bf16[128,1024]{1,0:T(8,128)(2,1)} %bitcast.13), channel_id=1, source_target_pairs={{4,0},{8,4},{12,8},{5,1},{9,5},{13,9},{6,2},{10,6},{14,10},{7,3},{... | collective-permute-start | bytes 786440 | tf_op jit(solution)/shard_map/ppermute | solution.py:19
  12.6 11.1 %collective-permute-start.1 = (bf16[128,1024]{1,0:T(8,128)(2,1)S(1)}, bf16[128,1024]{1,0:T(8,128)(2,1)S(1)}, u32[]{:S(2)}, u32[]{:S(2)}) collective-permute-start(bf16[128,1024]{1,0:T(8,128)(2,1)S(1)} %collective-permute-done.refs_4_.refs_8_.refs_5_), channel_id=1, source_target_pairs={{4,8},{8,12},{5,9},{9,13},{6,10},{10,14},{7,11},{11,15},{20,24},{2... | collective-permute-start | bytes 786440 | tf_op jit(solution)/shard_map/ppermute | solution.py:19
  17.1 7.0 %collective-permute-start.4 = (bf16[128,1024]{1,0:T(8,128)(2,1)S(1)}, bf16[128,1024]{1,0:T(8,128)(2,1)S(1)}, u32[]{:S(2)}, u32[]{:S(2)}) collective-permute-start(bf16[128,1024]{1,0:T(8,128)(2,1)S(1)} %collective-permute-done.2.refs_5_.refs_11_.refs_6_), channel_id=1, source_target_pairs={{4,8},{8,12},{5,9},{9,13},{6,10},{10,14},{7,11},{11,15},{20,24},{2... | collective-permute-start | bytes 786440 | tf_op jit(solution)/shard_map/ppermute | solution.py:19
  18.7 11.7 %collective-permute-start.5 = (bf16[128,1024]{1,0:T(8,128)(2,1)S(1)}, bf16[128,1024]{1,0:T(8,128)(2,1)S(1)}, u32[]{:S(2)}, u32[]{:S(2)}) collective-permute-start(bf16[128,1024]{1,0:T(8,128)(2,1)S(1)} %collective-permute-done.3.refs_7_.refs_2_.refs_3_), channel_id=1, source_target_pairs={{4,0},{8,4},{5,1},{9,5},{6,2},{10,6},{7,3},{11,7},{20,16},{24,20},... | collective-permute-start | bytes 786440 | tf_op jit(solution)/shard_map/ppermute | solution.py:19
  20.0 0.7 %copy-start.2 = (s32[1,4]{1,0:T(1,128)S(1)}, s32[1,4]{1,0:T(1,128)}, u32[]{:S(2)}) copy-start(s32[1,4]{1,0:T(1,128)} %refs_0_.1) | copy-start | bytes 52
  24.0 0.7 %copy-start = (f32[1024]{0:T(1024)S(1)}, f32[1024]{0:T(1024)}, u32[]{:S(2)}) copy-start(f32[1024]{0:T(1024)} %param.15) | copy-start | bytes 12292
  25.3 12.6 %collective-permute-start.6 = (bf16[128,1024]{1,0:T(8,128)(2,1)S(1)}, bf16[128,1024]{1,0:T(8,128)(2,1)S(1)}, u32[]{:S(2)}, u32[]{:S(2)}) collective-permute-start(bf16[128,1024]{1,0:T(8,128)(2,1)S(1)} %get-tuple-element.63.refs_6_.refs_3_), channel_id=1, source_target_pairs={{4,0},{8,4},{12,8},{5,1},{9,5},{13,9},{6,2},{10,6},{14,10},{7,3},{... | collective-permute-start | bytes 786440 | tf_op jit(solution)/shard_map/ppermute | solution.py:19
  32.7 2.1 %collective-permute-start.7 = (f32[16,128]{1,0:T(8,128)S(1)}, f32[16,128]{1,0:T(8,128)S(1)}, u32[]{:S(2)}, u32[]{:S(2)}) collective-permute-start(f32[16,128]{1,0:T(8,128)S(1)} %get-tuple-element.92), channel_id=1, source_target_pairs={{0,1},{1,0},{2,3},{3,2},{4,5},{5,4},{6,7},{7,6},{8,9},{9,8},{10,11... | collective-permute-start | bytes 24584 | tf_op jit(solution)/shard_map/ppermute | solution.py:454
  32.7 3.1 %collective-permute-start.9 = (f32[16,128]{1,0:T(8,128)S(1)}, f32[16,128]{1,0:T(8,128)S(1)}, u32[]{:S(2)}, u32[]{:S(2)}) collective-permute-start(f32[16,128]{1,0:T(8,128)S(1)} %get-tuple-element.92), channel_id=1, source_target_pairs={{0,3},{1,2},{2,1},{3,0},{4,7},{5,6},{6,5},{7,4},{8,11},{9,10},{10,... | collective-permute-start | bytes 24584 | tf_op jit(solution)/shard_map/ppermute | solution.py:454
  34.3 3.7 %collective-permute-start.8 = (f32[16,128]{1,0:T(8,128)S(1)}, f32[16,128]{1,0:T(8,128)S(1)}, u32[]{:S(2)}, u32[]{:S(2)}) collective-permute-start(f32[16,128]{1,0:T(8,128)S(1)} %get-tuple-element.92), channel_id=1, source_target_pairs={{0,2},{1,3},{2,0},{3,1},{4,6},{5,7},{6,4},{7,5},{8,10},{9,11},{10,... | collective-permute-start | bytes 24584 | tf_op jit(solution)/shard_map/ppermute | solution.py:454
  38.6 9.4 %collective-permute-start.10 = (bf16[96,1024]{1,0:T(8,128)(2,1)S(1)}, bf16[96,1024]{1,0:T(8,128)(2,1)S(1)}, u32[]{:S(2)}, u32[]{:S(2)}) collective-permute-start(bf16[96,1024]{1,0:T(8,128)(2,1)S(1)} %shard_map.135), channel_id=1, source_target_pairs={{4,0},{8,4},{5,1},{9,5},{6,2},{10,6},{7,3},{11,7},{20,16},{24,20},... | collective-permute-start | bytes 589832 | tf_op jit(solution)/shard_map/ppermute | solution.py:19
  41.9 7.3 %collective-permute-start.13 = (f32[16,128]{1,0:T(8,128)S(1)}, f32[16,128]{1,0:T(8,128)S(1)}, u32[]{:S(2)}, u32[]{:S(2)}) collective-permute-start(f32[16,128]{1,0:T(8,128)S(1)} %add_add_fusion.refs_0_), channel_id=1, source_target_pairs={{0,12},{4,8},{8,4},{12,0},{1,13},{5,9},{9,5},{13,1},{2,14},{6,10},... | collective-permute-start | bytes 24584 | tf_op jit(solution)/shard_map/ppermute | solution.py:454
  47.3 4.5 %collective-permute-start.12 = (f32[16,128]{1,0:T(8,128)S(1)}, f32[16,128]{1,0:T(8,128)S(1)}, u32[]{:S(2)}, u32[]{:S(2)}) collective-permute-start(f32[16,128]{1,0:T(8,128)S(1)} %add_add_fusion.refs_0_), channel_id=1, source_target_pairs={{0,8},{4,12},{8,0},{12,4},{1,9},{5,13},{9,1},{13,5},{2,10},{6,14},... | collective-permute-start | bytes 24584 | tf_op jit(solution)/shard_map/ppermute | solution.py:454
  47.3 4.5 %collective-permute-start.11 = (f32[16,128]{1,0:T(8,128)S(1)}, f32[16,128]{1,0:T(8,128)S(1)}, u32[]{:S(2)}, u32[]{:S(2)}) collective-permute-start(f32[16,128]{1,0:T(8,128)S(1)} %add_add_fusion.refs_0_), channel_id=1, source_target_pairs={{0,4},{4,0},{8,12},{12,8},{1,5},{5,1},{9,13},{13,9},{2,6},{6,2},{1... | collective-permute-start | bytes 24584 | tf_op jit(solution)/shard_map/ppermute | solution.py:454

commit v15 on v14

--- a/solution.py
+++ b/solution.py
@@ -571,7 +571,6 @@
         (table, flipped[reach], later_queries[reach], key),
         ahead=key_grads[:1],
     )
-    key_grads, far_tables, *pieces = lax.optimization_barrier((key_grads, far_tables, *pieces))
     for axis, distances in rounds_of(("ctx",)):
         pieces = exchanged(added_up(pieces), axis, distances)
     key_grad, value_grad = on_device(
@@ -585,7 +584,7 @@
     gain_grad, bias_grad = on_device(
         sum_kernel,
         [jax.ShapeDtypeStruct((8, lanes), F32), jax.ShapeDtypeStruct((levels, heads), F32)],
-        pieces,
+        pieces[::-1],
     )
     return (
         query_grad[None],

time: 52.8 us -> 50.9 us (0.964)
  waiting for transfers between devices: 15.4 us -> 14.3 us
  starting transfers between devices: 23.1 us -> 22.3 us
    ppermute x6, waiting for transfers between devices: 4.8 us -> 2.99 us  [exchanged(): lax.ppermute(array, axis, [(i, i ^ distance) for i in range(size)])]
    ppermute x6, starting transfers between devices: 8.15 us -> 7.41 us  [exchanged(): lax.ppermute(array, axis, [(i, i ^ distance) for i in range(size)])]
    ppermute x8, waiting for transfers between devices: 10.7 us -> 11.3 us  [passed_along(): lax.ppermute(array, axis, [(i, i + by) for i in range(first, last + 1)])]
  transfers between devices with their start and end apart: 14 -> 14, of which waited for: 6 -> 9; matrix products, arithmetic and copies ran while one was open for 0% -> 0% of each run, Pallas kernels for 20% -> 21%
where the time goes in v15:
time: 50.9 us; the launch traced here: 50.6 us
  starting transfers between devices  22.3 us (44%)
  waiting for transfers between devices  14.3 us (28%)
  Pallas kernels  11.8 us (23%)
  local copies, waits for them, and re-layouts  1.31 us (3%)
  between operations  0.82 us (2%)
    ppermute x8, starting transfers between devices, passed_along(): lax.ppermute(array, axis, [(i, i + by) for i in range(first, last + 1)])  14.9 us
    pallas_call x11, Pallas kernels, on_device(): pl.pallas_call(body, out_shape=outs, in_specs=[pl.BlockSpec(memory_space=...  11.8 us
    ppermute x8, waiting for transfers between devices, passed_along(): lax.ppermute(array, axis, [(i, i + by) for i in range(first, last + 1)])  11.3 us
    ppermute x6, starting transfers between devices, exchanged(): lax.ppermute(array, axis, [(i, i ^ distance) for i in range(size)])  7.41 us
    ppermute x6, waiting for transfers between devices, exchanged(): lax.ppermute(array, axis, [(i, i ^ distance) for i in range(size)])  2.99 us
    unnamed x6, local copies, waits for them, and re-layouts  1.31 us
  transfers between devices with their start and end apart: 14, of which 9 were waited for; matrix products, arithmetic and copies ran while one was open for 0% of the time, Pallas kernels for 21%

profile of v15, /device:TPU:0, one launch (start us, length us, event | category | flops | bytes accessed | tf_op | source)
XLA Modules:
  0.0 50.6 jit_solution(17483614777355862965)
XLA Ops:
  0.6 0.0 copy-start.1
  0.6 4.9 %collective-permute-start = (bf16[128,1024]{1,0:T(8,128)(2,1)}, bf16[128,1024]{1,0:T(8,128)(2,1)S(1)}, u32[]{:S(2)}, u32[]{:S(2)}) collective-permute-start(bf16[128,1024]{1,0:T(8,128)(2,1)} %bitcast.15), channel_id=1, source_target_pairs={{0,4},{4,8},{8,12},{1,5},{5,9},{9,13},{2,6},{6,10},{10,14},{3,7},{... | collective-permute-start | bytes 786440 | tf_op jit(solution)/shard_map/ppermute | solution.py:19
  5.6 3.5 %collective-permute-start.2 = (bf16[128,1024]{1,0:T(8,128)(2,1)}, bf16[128,1024]{1,0:T(8,128)(2,1)S(1)}, u32[]{:S(2)}, u32[]{:S(2)}) collective-permute-start(bf16[128,1024]{1,0:T(8,128)(2,1)} %bitcast.17), channel_id=1, source_target_pairs={{0,4},{4,8},{8,12},{1,5},{5,9},{9,13},{2,6},{6,10},{10,14},{3,7},{... | collective-permute-start | bytes 786440 | tf_op jit(solution)/shard_map/ppermute | solution.py:19
  9.1 1.3 %collective-permute-start.3 = (bf16[128,1024]{1,0:T(8,128)(2,1)}, bf16[128,1024]{1,0:T(8,128)(2,1)S(1)}, u32[]{:S(2)}, u32[]{:S(2)}) collective-permute-start(bf16[128,1024]{1,0:T(8,128)(2,1)} %bitcast.13), channel_id=1, source_target_pairs={{4,0},{8,4},{12,8},{5,1},{9,5},{13,9},{6,2},{10,6},{14,10},{7,3},{... | collective-permute-start | bytes 786440 | tf_op jit(solution)/shard_map/ppermute | solution.py:19
  10.4 2.2 %collective-permute-done.refs_4_.refs_8_.refs_5_ = bf16[128,1024]{1,0:T(8,128)(2,1)S(1)} collective-permute-done((bf16[128,1024]{1,0:T(8,128)(2,1)}, bf16[128,1024]{1,0:T(8,128)(2,1)S(1)}, u32[]{:S(2)}, u32[]{:S(2)}) %collective-permute-start) | collective-permute-done | bytes 262176 | tf_op jit(solution)/shard_map/ppermute | solution.py:19
  12.6 0.7 %collective-permute-start.1 = (bf16[128,1024]{1,0:T(8,128)(2,1)S(1)}, bf16[128,1024]{1,0:T(8,128)(2,1)S(1)}, u32[]{:S(2)}, u32[]{:S(2)}) collective-permute-start(bf16[128,1024]{1,0:T(8,128)(2,1)S(1)} %collective-permute-done.refs_4_.refs_8_.refs_5_), channel_id=1, source_target_pairs={{4,8},{8,12},{5,9},{9,13},{6,10},{10,14},{7,11},{11,15},{20,24},{2... | collective-permute-start | bytes 786440 | tf_op jit(solution)/shard_map/ppermute | solution.py:19
  13.3 3.8 %collective-permute-done.2.refs_5_.refs_11_.refs_6_ = bf16[128,1024]{1,0:T(8,128)(2,1)S(1)} collective-permute-done((bf16[128,1024]{1,0:T(8,128)(2,1)}, bf16[128,1024]{1,0:T(8,128)(2,1)S(1)}, u32[]{:S(2)}, u32[]{:S(2)}) %collective-permute-start.2) | collective-permute-done | bytes 262176 | tf_op jit(solution)/shard_map/ppermute | solution.py:19
  17.1 0.7 %collective-permute-start.4 = (bf16[128,1024]{1,0:T(8,128)(2,1)S(1)}, bf16[128,1024]{1,0:T(8,128)(2,1)S(1)}, u32[]{:S(2)}, u32[]{:S(2)}) collective-permute-start(bf16[128,1024]{1,0:T(8,128)(2,1)S(1)} %collective-permute-done.2.refs_5_.refs_11_.refs_6_), channel_id=1, source_target_pairs={{4,8},{8,12},{5,9},{9,13},{6,10},{10,14},{7,11},{11,15},{20,24},{2... | collective-permute-start | bytes 786440 | tf_op jit(solution)/shard_map/ppermute | solution.py:19
  17.7 0.9 %collective-permute-done.3.refs_7_.refs_2_.refs_3_ = bf16[128,1024]{1,0:T(8,128)(2,1)S(1)} collective-permute-done((bf16[128,1024]{1,0:T(8,128)(2,1)}, bf16[128,1024]{1,0:T(8,128)(2,1)S(1)}, u32[]{:S(2)}, u32[]{:S(2)}) %collective-permute-start.3) | collective-permute-done | bytes 262176 | tf_op jit(solution)/shard_map/ppermute | solution.py:19
  18.7 1.3 %collective-permute-start.5 = (bf16[128,1024]{1,0:T(8,128)(2,1)S(1)}, bf16[128,1024]{1,0:T(8,128)(2,1)S(1)}, u32[]{:S(2)}, u32[]{:S(2)}) collective-permute-start(bf16[128,1024]{1,0:T(8,128)(2,1)S(1)} %collective-permute-done.3.refs_7_.refs_2_.refs_3_), channel_id=1, source_target_pairs={{4,0},{8,4},{5,1},{9,5},{6,2},{10,6},{7,3},{11,7},{20,16},{24,20},... | collective-permute-start | bytes 786440 | tf_op jit(solution)/shard_map/ppermute | solution.py:19
  20.0 0.0 copy-start.2
  20.0 0.0 copy-done.1
  20.0 0.6 %copy-done.2 = s32[1,4]{1,0:T(1,128)S(1)} copy-done((s32[1,4]{1,0:T(1,128)S(1)}, s32[1,4]{1,0:T(1,128)}, u32[]{:S(2)}) %copy-start.2) | copy-done | bytes 40
  20.6 2.5 %shard_map.127 = (f32[64,128]{1,0:T(8,128)S(1)}, f32[1024,128]{1,0:T(8,128)S(1)}, f32[128,128]{1,0:T(8,128)S(1)}, f32[128,128]{1,0:T(8,128)S(1)}, f32[128,128]{1...) custom-call(s32[1,4]{1,0:T(1,128)S(1)} %copy-done.2, ...), custom_call_target="tpu_custom_call" | custom-call | flops 1000000 | bytes 100000 | tf_op jit(solution)/shard_map/pallas_call | solution.py:425
  23.1 0.6 %shard_map.128.refs_5_.refs_2_ = f32[128,1024]{1,0:T(8,128)S(1)} custom-call(f32[64,128]{1,0:T(8,128)S(1)} %get-tuple-element.46.refs_0_, f32[1024,128]{1,0:T(8,128)S(1)} %get-tuple-element.47.refs_1_, f32[128,128]{1,0:T(8,128)S(1)} %get-tuple-element.49.refs_2_.refs_3_, bf16[128,1024]{1,0:T(8,128)(2,1)S(1)} %get-tuple-element.51.refs_3_.refs_5_.refs_2_, ...), custom_call_target="tpu_custom_call" | custom-call | flops 1000000 | bytes 100000 | tf_op jit(solution)/shard_map/pallas_call | solution.py:425
  23.7 0.0 collective-permute-done.1.refs_4_.refs_9_
  23.7 0.3 shard_map.129.refs_0_
  24.0 0.0 copy-start
  24.0 0.0 collective-permute-done.4.refs_1_.refs_12_
  24.0 0.7 %copy-done = f32[1024]{0:T(1024)S(1)} copy-done((f32[1024]{0:T(1024)S(1)}, f32[1024]{0:T(1024)}, u32[]{:S(2)}) %copy-start) | copy-done | bytes 4120
  24.7 0.6 %shard_map.130 = (f32[128,1024]{1,0:T(8,128)S(1)}, bf16[128,1024]{1,0:T(8,128)(2,1)S(1)}, f32[1,1024]{1,0:T(1,128)S(1)}) custom-call(bf16[1024,128]{1,0:T(8,128)(2,1)S(1)} %shard_map.129.refs_0_, bf16[128,1024]{1,0:T(8,128)(2,1)S(1)} %collective-permute-done.4.refs_1_.refs_12_, f32[128,1024]{1,0:T(8,128)S(1)} %shard_map.128.refs_5_.refs_2_, ...), custom_call_target="tpu_custom_call" | custom-call | flops 1000000 | bytes 100000 | tf_op jit(solution)/shard_map/pallas_call | solution.py:425
  25.3 1.3 %collective-permute-start.6 = (bf16[128,1024]{1,0:T(8,128)(2,1)S(1)}, bf16[128,1024]{1,0:T(8,128)(2,1)S(1)}, u32[]{:S(2)}, u32[]{:S(2)}) collective-permute-start(bf16[128,1024]{1,0:T(8,128)(2,1)S(1)} %get-tuple-element.55.refs_6_.refs_3_), channel_id=1, source_target_pairs={{4,0},{8,4},{12,8},{5,1},{9,5},{13,9},{6,2},{10,6},{14,10},{7,3},{... | collective-permute-start | bytes 786440 | tf_op jit(solution)/shard_map/ppermute | solution.py:19
  26.6 3.7 %collective-permute-done.5.refs_14_.refs_2_.refs_3_ = bf16[128,1024]{1,0:T(8,128)(2,1)S(1)} collective-permute-done((bf16[128,1024]{1,0:T(8,128)(2,1)S(1)}, bf16[128,1024]{1,0:T(8,128)(2,1)S(1)}, u32[]{:S(2)}, u32[]{:S(2)}) %collective-permute-start.5) | collective-permute-done | bytes 262176 | tf_op jit(solution)/shard_map/ppermute | solution.py:19
  30.3 2.4 %shard_map.131 = (bf16[128,1024]{1,0:T(8,128)(2,1)}, f32[16,128]{1,0:T(8,128)S(1)}) custom-call(f32[64,128]{1,0:T(8,128)S(1)} %get-tuple-element.46.refs_0_, f32[1024,128]{1,0:T(8,128)S(1)} %get-tuple-element.47.refs_1_, f32[128,128]{1,0:T(8,128)S(1)} %get-tuple-element.48.refs_2_, f32[128,128]{1,0:T(8,128)S(1)} %get-tuple-element.49.refs_2_.refs_3_, ...), custom_call_target="tpu_custom_call" | custom-call | flops 1000000 | bytes 100000 | tf_op jit(solution)/shard_map/pallas_call | solution.py:425
  32.7 0.0 collective-permute-start.7
  32.7 1.5 %collective-permute-start.8 = (f32[16,128]{1,0:T(8,128)S(1)}, f32[16,128]{1,0:T(8,128)S(1)}, u32[]{:S(2)}, u32[]{:S(2)}) collective-permute-start(f32[16,128]{1,0:T(8,128)S(1)} %get-tuple-element.76), channel_id=1, source_target_pairs={{0,2},{1,3},{2,0},{3,1},{4,6},{5,7},{6,4},{7,5},{8,10},{9,11},{10,... | collective-permute-start | bytes 24584 | tf_op jit(solution)/shard_map/ppermute | solution.py:454
  34.2 0.4 collective-permute-start.9
  34.6 0.0 collective-permute-done.7.refs_6_
  34.6 1.8 %collective-permute-done.8 = f32[16,128]{1,0:T(8,128)S(1)} collective-permute-done((f32[16,128]{1,0:T(8,128)S(1)}, f32[16,128]{1,0:T(8,128)S(1)}, u32[]{:S(2)}, u32[]{:S(2)}) %collective-permute-start.8) | collective-permute-done | bytes 8224 | tf_op jit(solution)/shard_map/ppermute | solution.py:454
  36.4 0.9 %collective-permute-done.9 = f32[16,128]{1,0:T(8,128)S(1)} collective-permute-done((f32[16,128]{1,0:T(8,128)S(1)}, f32[16,128]{1,0:T(8,128)S(1)}, u32[]{:S(2)}, u32[]{:S(2)}) %collective-permute-start.9) | collective-permute-done | bytes 8224 | tf_op jit(solution)/shard_map/ppermute | solution.py:454
  37.3 0.5 collective-permute-done.6.refs_3_.refs_4_
  37.7 0.6 %shard_map.135 = bf16[96,1024]{1,0:T(8,128)(2,1)S(1)} custom-call(f32[64,128]{1,0:T(8,128)S(1)} %get-tuple-element.46.refs_0_, f32[32,128]{1,0:T(8,128)S(1)} %get-tuple-element.71.refs_1_, f32[16,128]{1,0:T(8,128)S(1)} %get-tuple-element.70.refs_2_, bf16[128,1024]{1,0:T(8,128)(2,1)S(1)} %collective-permute-done.3.refs_7_.refs_2_.refs_3_, ...), custom_call_target="tpu_custom_call" | custom-call | flops 1000000 | bytes 100000 | tf_op jit(solution)/shard_map/pallas_call | solution.py:425
  38.4 1.3 %collective-permute-start.10 = (bf16[96,1024]{1,0:T(8,128)(2,1)S(1)}, bf16[96,1024]{1,0:T(8,128)(2,1)S(1)}, u32[]{:S(2)}, u32[]{:S(2)}) collective-permute-start(bf16[96,1024]{1,0:T(8,128)(2,1)S(1)} %shard_map.135), channel_id=1, source_target_pairs={{4,0},{8,4},{5,1},{9,5},{6,2},{10,6},{7,3},{11,7},{20,16},{24,20},... | collective-permute-start | bytes 589832 | tf_op jit(solution)/shard_map/ppermute | solution.py:19
  39.7 4.9 %collective-permute-start.11 = (f32[16,128]{1,0:T(8,128)S(1)}, f32[16,128]{1,0:T(8,128)S(1)}, u32[]{:S(2)}, u32[]{:S(2)}) collective-permute-start(f32[16,128]{1,0:T(8,128)S(1)} %add_add_fusion.refs_3_), channel_id=1, source_target_pairs={{0,12},{4,8},{8,4},{12,0},{1,13},{5,9},{9,5},{13,1},{2,14},{6,10},... | collective-permute-start | bytes 24584 | tf_op jit(solution)/shard_map/ppermute | solution.py:454
  44.6 0.0 collective-permute-start.12
  44.6 0.6 %collective-permute-start.13 = (f32[16,128]{1,0:T(8,128)S(1)}, f32[16,128]{1,0:T(8,128)S(1)}, u32[]{:S(2)}, u32[]{:S(2)}) collective-permute-start(f32[16,128]{1,0:T(8,128)S(1)} %add_add_fusion.refs_3_), channel_id=1, source_target_pairs={{0,4},{4,0},{8,12},{12,8},{1,5},{5,1},{9,13},{13,9},{2,6},{6,2},{1... | collective-permute-start | bytes 24584 | tf_op jit(solution)/shard_map/ppermute | solution.py:454
  45.2 0.9 %shard_map.132 = (f32[128,1024]{1,0:T(8,128)S(1)}, f32[128,1024]{1,0:T(8,128)S(1)}) custom-call(f32[64,128]{1,0:T(8,128)S(1)} %get-tuple-element.46.refs_0_, f32[128,128]{1,0:T(8,128)S(1)} %get-tuple-element.62.refs_1_, bf16[128,1024]{1,0:T(8,128)(2,1)S(1)} %get-tuple-element.51.refs_3_.refs_5_.refs_2_, ...), custom_call_target="tpu_custom_call" | custom-call | flops 1000000 | bytes 100000 | tf_op jit(solution)/shard_map/pallas_call | solution.py:425
  46.1 1.6 %shard_map.133 = (bf16[128,1024]{1,0:T(8,128)(2,1)}, f32[128,1024]{1,0:T(8,128)S(1)}, f32[128,1024]{1,0:T(8,128)S(1)}) custom-call(f32[64,128]{1,0:T(8,128)S(1)} %get-tuple-element.46.refs_0_, f32[128,128]{1,0:T(8,128)S(1)} %get-tuple-element.61.refs_1_, bf16[128,1024]{1,0:T(8,128)(2,1)S(1)} %collective-permute-done.3.refs_7_.refs_2_.refs_3_, ...), custom_call_target="tpu_custom_call" | custom-call | flops 1000000 | bytes 100000 | tf_op jit(solution)/shard_map/pallas_call | solution.py:425
  47.7 0.4 shard_map.134
  48.1 0.2 collective-permute-done.10.refs_4_
  48.3 1.3 %shard_map.136 = (bf16[128,1024]{1,0:T(8,128)(2,1)}, bf16[128,1024]{1,0:T(8,128)(2,1)}) custom-call(bf16[1024,96]{1,0:T(8,128)(2,1)S(1)} %get-tuple-element.68.refs_0_, f32[1024,96]{1,0:T(8,128)S(1)} %get-tuple-element.69.refs_1_, f32[16,128]{1,0:T(8,128)S(1)} %get-tuple-element.70.refs_2_, ...), custom_call_target="tpu_custom_call" | custom-call | flops 1000000 | bytes 100000 | tf_op jit(solution)/shard_map/pallas_call | solution.py:425
  49.7 0.0 collective-permute-done.11.refs_0_
  49.7 0.3 collective-permute-done.12.refs_1_
  50.0 0.0 collective-permute-done.13.refs_2_
  50.0 0.6 %shard_map.137 = (f32[8,128]{1,0:T(8,128)}, f32[8,8]{1,0:T(8,128)}) custom-call(f32[16,128]{1,0:T(8,128)S(1)} %collective-permute-done.11.refs_0_, f32[16,128]{1,0:T(8,128)S(1)} %collective-permute-done.12.refs_1_, f32[16,128]{1,0:T(8,128)S(1)} %collective-permute-done.13.refs_2_, f32[16,128]{1,0:T(8,128)S(1)} %add_add_fusion.refs_3_), custom_call_target="tpu_custom_call" | custom-call | flops 1000000 | bytes 100000 | tf_op jit(solution)/shard_map/pallas_call | solution.py:425
  (1 shorter events, 0.0 us)
Async XLA Ops:
  0.6 19.3 %copy-start.1 = (f32[8,8]{1,0:T(8,128)S(1)}, f32[8,8]{1,0:T(8,128)}, u32[]{:S(2)}) copy-start(f32[8,8]{1,0:T(8,128)} %refs_1_.1) | copy-start | bytes 772
  0.6 11.9 %collective-permute-start = (bf16[128,1024]{1,0:T(8,128)(2,1)}, bf16[128,1024]{1,0:T(8,128)(2,1)S(1)}, u32[]{:S(2)}, u32[]{:S(2)}) collective-permute-start(bf16[128,1024]{1,0:T(8,128)(2,1)} %bitcast.15), channel_id=1, source_target_pairs={{0,4},{4,8},{8,12},{1,5},{5,9},{9,13},{2,6},{6,10},{10,14},{3,7},{... | collective-permute-start | bytes 786440 | tf_op jit(solution)/shard_map/ppermute | solution.py:19
  5.6 11.5 %collective-permute-start.2 = (bf16[128,1024]{1,0:T(8,128)(2,1)}, bf16[128,1024]{1,0:T(8,128)(2,1)S(1)}, u32[]{:S(2)}, u32[]{:S(2)}) collective-permute-start(bf16[128,1024]{1,0:T(8,128)(2,1)} %bitcast.17), channel_id=1, source_target_pairs={{0,4},{4,8},{8,12},{1,5},{5,9},{9,13},{2,6},{6,10},{10,14},{3,7},{... | collective-permute-start | bytes 786440 | tf_op jit(solution)/shard_map/ppermute | solution.py:19
  9.1 9.6 %collective-permute-start.3 = (bf16[128,1024]{1,0:T(8,128)(2,1)}, bf16[128,1024]{1,0:T(8,128)(2,1)S(1)}, u32[]{:S(2)}, u32[]{:S(2)}) collective-permute-start(bf16[128,1024]{1,0:T(8,128)(2,1)} %bitcast.13), channel_id=1, source_target_pairs={{4,0},{8,4},{12,8},{5,1},{9,5},{13,9},{6,2},{10,6},{14,10},{7,3},{... | collective-permute-start | bytes 786440 | tf_op jit(solution)/shard_map/ppermute | solution.py:19
  12.6 11.1 %collective-permute-start.1 = (bf16[128,1024]{1,0:T(8,128)(2,1)S(1)}, bf16[128,1024]{1,0:T(8,128)(2,1)S(1)}, u32[]{:S(2)}, u32[]{:S(2)}) collective-permute-start(bf16[128,1024]{1,0:T(8,128)(2,1)S(1)} %collective-permute-done.refs_4_.refs_8_.refs_5_), channel_id=1, source_target_pairs={{4,8},{8,12},{5,9},{9,13},{6,10},{10,14},{7,11},{11,15},{20,24},{2... | collective-permute-start | bytes 786440 | tf_op jit(solution)/shard_map/ppermute | solution.py:19
  17.1 7.0 %collective-permute-start.4 = (bf16[128,1024]{1,0:T(8,128)(2,1)S(1)}, bf16[128,1024]{1,0:T(8,128)(2,1)S(1)}, u32[]{:S(2)}, u32[]{:S(2)}) collective-permute-start(bf16[128,1024]{1,0:T(8,128)(2,1)S(1)} %collective-permute-done.2.refs_5_.refs_11_.refs_6_), channel_id=1, source_target_pairs={{4,8},{8,12},{5,9},{9,13},{6,10},{10,14},{7,11},{11,15},{20,24},{2... | collective-permute-start | bytes 786440 | tf_op jit(solution)/shard_map/ppermute | solution.py:19
  18.7 11.7 %collective-permute-start.5 = (bf16[128,1024]{1,0:T(8,128)(2,1)S(1)}, bf16[128,1024]{1,0:T(8,128)(2,1)S(1)}, u32[]{:S(2)}, u32[]{:S(2)}) collective-permute-start(bf16[128,1024]{1,0:T(8,128)(2,1)S(1)} %collective-permute-done.3.refs_7_.refs_2_.refs_3_), channel_id=1, source_target_pairs={{4,0},{8,4},{5,1},{9,5},{6,2},{10,6},{7,3},{11,7},{20,16},{24,20},... | collective-permute-start | bytes 786440 | tf_op jit(solution)/shard_map/ppermute | solution.py:19
  20.0 0.7 %copy-start.2 = (s32[1,4]{1,0:T(1,128)S(1)}, s32[1,4]{1,0:T(1,128)}, u32[]{:S(2)}) copy-start(s32[1,4]{1,0:T(1,128)} %refs_0_.1) | copy-start | bytes 52
  24.0 0.7 %copy-start = (f32[1024]{0:T(1024)S(1)}, f32[1024]{0:T(1024)}, u32[]{:S(2)}) copy-start(f32[1024]{0:T(1024)} %param.15) | copy-start | bytes 12292
  25.3 12.4 %collective-permute-start.6 = (bf16[128,1024]{1,0:T(8,128)(2,1)S(1)}, bf16[128,1024]{1,0:T(8,128)(2,1)S(1)}, u32[]{:S(2)}, u32[]{:S(2)}) collective-permute-start(bf16[128,1024]{1,0:T(8,128)(2,1)S(1)} %get-tuple-element.55.refs_6_.refs_3_), channel_id=1, source_target_pairs={{4,0},{8,4},{12,8},{5,1},{9,5},{13,9},{6,2},{10,6},{14,10},{7,3},{... | collective-permute-start | bytes 786440 | tf_op jit(solution)/shard_map/ppermute | solution.py:19
  32.7 1.9 %collective-permute-start.7 = (f32[16,128]{1,0:T(8,128)S(1)}, f32[16,128]{1,0:T(8,128)S(1)}, u32[]{:S(2)}, u32[]{:S(2)}) collective-permute-start(f32[16,128]{1,0:T(8,128)S(1)} %get-tuple-element.76), channel_id=1, source_target_pairs={{0,1},{1,0},{2,3},{3,2},{4,5},{5,4},{6,7},{7,6},{8,9},{9,8},{10,11... | collective-permute-start | bytes 24584 | tf_op jit(solution)/shard_map/ppermute | solution.py:454
  32.7 3.7 %collective-permute-start.8 = (f32[16,128]{1,0:T(8,128)S(1)}, f32[16,128]{1,0:T(8,128)S(1)}, u32[]{:S(2)}, u32[]{:S(2)}) collective-permute-start(f32[16,128]{1,0:T(8,128)S(1)} %get-tuple-element.76), channel_id=1, source_target_pairs={{0,2},{1,3},{2,0},{3,1},{4,6},{5,7},{6,4},{7,5},{8,10},{9,11},{10,... | collective-permute-start | bytes 24584 | tf_op jit(solution)/shard_map/ppermute | solution.py:454
  34.2 3.1 %collective-permute-start.9 = (f32[16,128]{1,0:T(8,128)S(1)}, f32[16,128]{1,0:T(8,128)S(1)}, u32[]{:S(2)}, u32[]{:S(2)}) collective-permute-start(f32[16,128]{1,0:T(8,128)S(1)} %get-tuple-element.76), channel_id=1, source_target_pairs={{0,3},{1,2},{2,1},{3,0},{4,7},{5,6},{6,5},{7,4},{8,11},{9,10},{10,... | collective-permute-start | bytes 24584 | tf_op jit(solution)/shard_map/ppermute | solution.py:454
  38.4 10.0 %collective-permute-start.10 = (bf16[96,1024]{1,0:T(8,128)(2,1)S(1)}, bf16[96,1024]{1,0:T(8,128)(2,1)S(1)}, u32[]{:S(2)}, u32[]{:S(2)}) collective-permute-start(bf16[96,1024]{1,0:T(8,128)(2,1)S(1)} %shard_map.135), channel_id=1, source_target_pairs={{4,0},{8,4},{5,1},{9,5},{6,2},{10,6},{7,3},{11,7},{20,16},{24,20},... | collective-permute-start | bytes 589832 | tf_op jit(solution)/shard_map/ppermute | solution.py:19
  39.7 10.0 %collective-permute-start.11 = (f32[16,128]{1,0:T(8,128)S(1)}, f32[16,128]{1,0:T(8,128)S(1)}, u32[]{:S(2)}, u32[]{:S(2)}) collective-permute-start(f32[16,128]{1,0:T(8,128)S(1)} %add_add_fusion.refs_3_), channel_id=1, source_target_pairs={{0,12},{4,8},{8,4},{12,0},{1,13},{5,9},{9,5},{13,1},{2,14},{6,10},... | collective-permute-start | bytes 24584 | tf_op jit(solution)/shard_map/ppermute | solution.py:454
  44.6 5.4 %collective-permute-start.12 = (f32[16,128]{1,0:T(8,128)S(1)}, f32[16,128]{1,0:T(8,128)S(1)}, u32[]{:S(2)}, u32[]{:S(2)}) collective-permute-start(f32[16,128]{1,0:T(8,128)S(1)} %add_add_fusion.refs_3_), channel_id=1, source_target_pairs={{0,8},{4,12},{8,0},{12,4},{1,9},{5,13},{9,1},{13,5},{2,10},{6,14},... | collective-permute-start | bytes 24584 | tf_op jit(solution)/shard_map/ppermute | solution.py:454
  44.6 5.4 %collective-permute-start.13 = (f32[16,128]{1,0:T(8,128)S(1)}, f32[16,128]{1,0:T(8,128)S(1)}, u32[]{:S(2)}, u32[]{:S(2)}) collective-permute-start(f32[16,128]{1,0:T(8,128)S(1)} %add_add_fusion.refs_3_), channel_id=1, source_target_pairs={{0,4},{4,0},{8,12},{12,8},{1,5},{5,1},{9,13},{13,9},{2,6},{6,2},{1... | collective-permute-start | bytes 24584 | tf_op jit(solution)/shard_map/ppermute | solution.py:454

commit v16 on v15

--- a/solution.py
+++ b/solution.py
@@ -188,18 +188,19 @@
 
 def norm_kernel(heads, *refs):
     weights, value, total, out_grad, update_gate, gain = refs[:6]
-    attention, attn_grad, gain_grad = refs[6:]
+    kept, attn_grad, gain_grad = refs[6:]
     width = total.shape[1] // heads
     for head in range(heads):
         cols, lines = columns(head, width), columns(head, total.shape[0])
-        attention[:, cols] = total[:, cols] + contract(weights[lines, :], value[:, cols], 1, 0)
-    rows, features = attention.shape
+        kept[:, cols] = total[:, cols] + contract(weights[lines, :], value[:, cols], 1, 0)
+    rows, features = kept.shape
     step = 16
     gain_row = gain[...]
     gain_sum = jnp.zeros((8, features), F32)
     for low in range(0, rows, step):
         span = slice(low, low + step)
-        normed, inverse = normed_rows(attention[span, :])
+        normed, inverse = normed_rows(kept[span, :])
+        kept[span, :] = normed
         gated = out_grad[span, :].astype(F32) * update_gate[span, :].astype(F32)
         product = gated * normed
         for part in range(0, step, 8):
@@ -308,38 +309,36 @@
 
 
 def gate_and_key_kernel(hops, heads, scaling, *refs):
-    attention, out_grad, gain = refs[8:11]
+    normed, out_grad, gain = refs[8:11]
     gate_out, key_out, value_out, held, written = refs[11:]
     step = 16
     gain_row = gain[...]
-    for low in range(0, attention.shape[0], step):
+    for low in range(0, normed.shape[0], step):
         span = slice(low, low + step)
-        normed, _ = normed_rows(attention[span, :])
-        held[span, :] = (out_grad[span, :].astype(F32) * normed * gain_row).astype(BF16)
+        held[span, :] = (out_grad[span, :].astype(F32) * normed[span, :] * gain_row).astype(BF16)
     copy = pltpu.make_async_copy(held, gate_out, written)
     copy.start()
     add_key_grads(hops, heads, scaling, *refs[:6], refs[6:8], into(key_out, value_out))
     copy.wait()
 
 
-def message_kernel(hops, heads, scaling, *refs):
-    table, mask, late, query, grad, key, value, out = refs
-    tail, cut, width = mask.shape[0], out.shape[0], query.shape[1] // heads
-    pair = Pair(mask, table, heads, hops, True)
+def message_kernel(heads, *refs):
+    weights, slopes, late, query, grad, value, out = refs
+    cut, width = out.shape[0], query.shape[1] // heads
+    tail = query.shape[0] - cut
     is_late = late[8:9, :width] > 0.5
 
     def scores(head):
         cols = columns(head, width)
-        score = contract(key[cut:, cols], query[:, cols], 1, 1)
-        return score, contract(value[cut:, cols], grad[:, cols], 1, 1)
+        return contract(value[cut:, cols], grad[:, cols], 1, 1)
 
     def choose(head, found):
-        cols = columns(head, width)
-        half = pair.half_logits(found[0], head, scaling)
-        tanh = jnp.tanh(half)
-        rounded = (found[1] * (slope_of(half, tanh) * pair.mask)).astype(BF16)
-        weights = ((half + half * tanh) * pair.mask).astype(BF16)
-        parts = [contract(rounded, query[:, cols], 1, 0), contract(weights, grad[:, cols], 1, 0)]
+        cols, lines = columns(head, width), columns(head, tail)
+        rounded = (found * slopes[lines, :]).astype(BF16)
+        parts = [
+            contract(rounded, query[:, cols], 1, 0),
+            contract(weights[lines, :], grad[:, cols], 1, 0),
+        ]
         for at, part in enumerate(parts):
             lines = slice(at * tail, (at + 1) * tail)
             out[lines, cols] = jnp.where(is_late, part, grad[lines, cols].astype(F32)).astype(BF16)
@@ -351,10 +350,11 @@
 def slopes_kernel(hops, heads, scaling, table, mask, query, key, weights, slopes):
     pair = Pair(mask, table, heads, hops, True)
     rows, cut, width = mask.shape[0], mask.shape[1], query.shape[1] // heads
+    first = key.shape[0] - rows
 
     def scores(head):
         cols = columns(head, width)
-        return contract(key[:, cols], query[:cut, cols], 1, 1)
+        return contract(key[first:, cols], query[:cut, cols], 1, 1)
 
     def derive(head, found):
         half = pair.half_logits(found, head, scaling)
@@ -514,18 +514,23 @@
         (table, near, masks[-1], query, keys[-1]),
         ahead=[attention],
     )
-    attention, attn_grad, gain_part = on_device(
+    normed, attn_grad, gain_part = on_device(
         partial(norm_kernel, heads),
         [wide, narrow, jax.ShapeDtypeStruct((1, features), F32)],
         (far_weights, values[-1], attention, grad, gate, gain),
     )
 
+    sent_tables = on_device(
+        partial(slopes_kernel, reach, heads, scaling),
+        [jax.ShapeDtypeStruct((heads * (rows - cut), rows), kind) for kind in (BF16, F32)],
+        (table, sender_mask, later_queries[reach - 1], keys[1]),
+    )
     lanes = features // 8
     query_grad, sums = on_device(
         partial(backward_query_kernel, hop_list, heads, scaling),
         [narrow, jax.ShapeDtypeStruct((8 + levels, lanes), F32)],
         (table, near, *masks, query, attn_grad, *keys, *values, gain_part),
-        ahead=later_queries[reach:],
+        ahead=[later_queries[reach], sent_tables[0]],
     )
     later_grads = [attn_grad, passed_along(attn_grad, "ctx", -1)]
     pieces = [sums]
@@ -546,16 +551,16 @@
         arrived, *pieces = lax.optimization_barrier((later_grads[hops], *pieces))
         if hops + 1 == reach:
             (arrived,) = on_device(
-                partial(message_kernel, reach, heads, scaling),
+                partial(message_kernel, heads),
                 [jax.ShapeDtypeStruct((cut, features), BF16)],
-                (table, sender_mask, late, later_queries[hops], arrived, keys[1], values[1]),
+                (*sent_tables, late, later_queries[hops], arrived, values[1]),
             )
         later_grads.append(passed_along(arrived, "ctx", -1, hops + 1))
         if hops == 1:
             gate_grad, *key_grads = on_device(
                 partial(gate_and_key_kernel, hops, heads, scaling),
                 [narrow, wide, wide],
-                (*key_operands(hops), *key_grads, attention, grad, gain),
+                (*key_operands(hops), *key_grads, normed, grad, gain),
                 far_outs=1,
                 scratch=[pltpu.VMEM((rows, features), BF16), pltpu.SemaphoreType.DMA(())],
             )
@@ -584,7 +589,7 @@
     gain_grad, bias_grad = on_device(
         sum_kernel,
         [jax.ShapeDtypeStruct((8, lanes), F32), jax.ShapeDtypeStruct((levels, heads), F32)],
-        pieces[::-1],
+        [*pieces[2:], *pieces[1::-1]],
     )
     return (
         query_grad[None],

time: 50.9 us -> 51.1 us (level)
    pallas_call x11 -> x12, Pallas kernels: 11.8 us -> 11.9 us  [on_device(): pl.pallas_call(body, out_shape=outs, in_specs=[pl.BlockSpec(memory_space=...]
  transfers between devices with their start and end apart: 14 -> 14, of which waited for: 9 -> 10; matrix products, arithmetic and copies ran while one was open for 0% -> 0% of each run, Pallas kernels for 21% -> 21%
where the time goes in v16:
time: 51.1 us; the launch traced here: 50.7 us
  starting transfers between devices  22.6 us (44%)
  waiting for transfers between devices  14 us (27%)
  Pallas kernels  11.9 us (23%)
  local copies, waits for them, and re-layouts  1.31 us (3%)
  between operations  0.82 us (2%)
    ppermute x8, starting transfers between devices, passed_along(): lax.ppermute(array, axis, [(i, i + by) for i in range(first, last + 1)])  14.9 us
    pallas_call x12, Pallas kernels, on_device(): pl.pallas_call(body, out_shape=outs, in_specs=[pl.BlockSpec(memory_space=...  11.9 us
    ppermute x8, waiting for transfers between devices, passed_along(): lax.ppermute(array, axis, [(i, i + by) for i in range(first, last + 1)])  10.9 us
    ppermute x6, starting transfers between devices, exchanged(): lax.ppermute(array, axis, [(i, i ^ distance) for i in range(size)])  7.72 us
    ppermute x6, waiting for transfers between devices, exchanged(): lax.ppermute(array, axis, [(i, i ^ distance) for i in range(size)])  3.13 us
    unnamed x6, local copies, waits for them, and re-layouts  1.31 us
  transfers between devices with their start and end apart: 14, of which 10 were waited for; matrix products, arithmetic and copies ran while one was open for 0% of the time, Pallas kernels for 21%

profile of v16, /device:TPU:0, one launch (start us, length us, event | category | flops | bytes accessed | tf_op | source)
XLA Modules:
  0.0 50.7 jit_solution(16456438814804038948)
XLA Ops:
  0.6 0.0 copy-start.1
  0.6 4.9 %collective-permute-start = (bf16[128,1024]{1,0:T(8,128)(2,1)}, bf16[128,1024]{1,0:T(8,128)(2,1)S(1)}, u32[]{:S(2)}, u32[]{:S(2)}) collective-permute-start(bf16[128,1024]{1,0:T(8,128)(2,1)} %bitcast.15), channel_id=1, source_target_pairs={{0,4},{4,8},{8,12},{1,5},{5,9},{9,13},{2,6},{6,10},{10,14},{3,7},{... | collective-permute-start | bytes 786440 | tf_op jit(solution)/shard_map/ppermute | solution.py:19
  5.6 3.5 %collective-permute-start.2 = (bf16[128,1024]{1,0:T(8,128)(2,1)}, bf16[128,1024]{1,0:T(8,128)(2,1)S(1)}, u32[]{:S(2)}, u32[]{:S(2)}) collective-permute-start(bf16[128,1024]{1,0:T(8,128)(2,1)} %bitcast.17), channel_id=1, source_target_pairs={{0,4},{4,8},{8,12},{1,5},{5,9},{9,13},{2,6},{6,10},{10,14},{3,7},{... | collective-permute-start | bytes 786440 | tf_op jit(solution)/shard_map/ppermute | solution.py:19
  9.1 1.3 %collective-permute-start.3 = (bf16[128,1024]{1,0:T(8,128)(2,1)}, bf16[128,1024]{1,0:T(8,128)(2,1)S(1)}, u32[]{:S(2)}, u32[]{:S(2)}) collective-permute-start(bf16[128,1024]{1,0:T(8,128)(2,1)} %bitcast.13), channel_id=1, source_target_pairs={{4,0},{8,4},{12,8},{5,1},{9,5},{13,9},{6,2},{10,6},{14,10},{7,3},{... | collective-permute-start | bytes 786440 | tf_op jit(solution)/shard_map/ppermute | solution.py:19
  10.4 2.2 %collective-permute-done.refs_4_.refs_3_.refs_8_ = bf16[128,1024]{1,0:T(8,128)(2,1)S(1)} collective-permute-done((bf16[128,1024]{1,0:T(8,128)(2,1)}, bf16[128,1024]{1,0:T(8,128)(2,1)S(1)}, u32[]{:S(2)}, u32[]{:S(2)}) %collective-permute-start) | collective-permute-done | bytes 262176 | tf_op jit(solution)/shard_map/ppermute | solution.py:19
  12.6 0.7 %collective-permute-start.1 = (bf16[128,1024]{1,0:T(8,128)(2,1)S(1)}, bf16[128,1024]{1,0:T(8,128)(2,1)S(1)}, u32[]{:S(2)}, u32[]{:S(2)}) collective-permute-start(bf16[128,1024]{1,0:T(8,128)(2,1)S(1)} %collective-permute-done.refs_4_.refs_3_.refs_8_), channel_id=1, source_target_pairs={{4,8},{8,12},{5,9},{9,13},{6,10},{10,14},{7,11},{11,15},{20,24},{2... | collective-permute-start | bytes 786440 | tf_op jit(solution)/shard_map/ppermute | solution.py:19
  13.3 3.8 %collective-permute-done.2.refs_5_.refs_11_ = bf16[128,1024]{1,0:T(8,128)(2,1)S(1)} collective-permute-done((bf16[128,1024]{1,0:T(8,128)(2,1)}, bf16[128,1024]{1,0:T(8,128)(2,1)S(1)}, u32[]{:S(2)}, u32[]{:S(2)}) %collective-permute-start.2) | collective-permute-done | bytes 262176 | tf_op jit(solution)/shard_map/ppermute | solution.py:19
  17.1 0.7 %collective-permute-start.4 = (bf16[128,1024]{1,0:T(8,128)(2,1)S(1)}, bf16[128,1024]{1,0:T(8,128)(2,1)S(1)}, u32[]{:S(2)}, u32[]{:S(2)}) collective-permute-start(bf16[128,1024]{1,0:T(8,128)(2,1)S(1)} %collective-permute-done.2.refs_5_.refs_11_), channel_id=1, source_target_pairs={{4,8},{8,12},{5,9},{9,13},{6,10},{10,14},{7,11},{11,15},{20,24},{2... | collective-permute-start | bytes 786440 | tf_op jit(solution)/shard_map/ppermute | solution.py:19
  17.7 0.9 %collective-permute-done.3.refs_7_.refs_2_.refs_3_ = bf16[128,1024]{1,0:T(8,128)(2,1)S(1)} collective-permute-done((bf16[128,1024]{1,0:T(8,128)(2,1)}, bf16[128,1024]{1,0:T(8,128)(2,1)S(1)}, u32[]{:S(2)}, u32[]{:S(2)}) %collective-permute-start.3) | collective-permute-done | bytes 262176 | tf_op jit(solution)/shard_map/ppermute | solution.py:19
  18.7 1.3 %collective-permute-start.5 = (bf16[128,1024]{1,0:T(8,128)(2,1)S(1)}, bf16[128,1024]{1,0:T(8,128)(2,1)S(1)}, u32[]{:S(2)}, u32[]{:S(2)}) collective-permute-start(bf16[128,1024]{1,0:T(8,128)(2,1)S(1)} %collective-permute-done.3.refs_7_.refs_2_.refs_3_), channel_id=1, source_target_pairs={{4,0},{8,4},{5,1},{9,5},{6,2},{10,6},{7,3},{11,7},{20,16},{24,20},... | collective-permute-start | bytes 786440 | tf_op jit(solution)/shard_map/ppermute | solution.py:19
  20.0 0.0 copy-start.2
  20.0 0.0 copy-done.1
  20.0 0.6 %copy-done.2 = s32[1,4]{1,0:T(1,128)S(1)} copy-done((s32[1,4]{1,0:T(1,128)S(1)}, s32[1,4]{1,0:T(1,128)}, u32[]{:S(2)}) %copy-start.2) | copy-done | bytes 40
  20.6 2.5 %shard_map.127 = (f32[64,128]{1,0:T(8,128)S(1)}, f32[1024,128]{1,0:T(8,128)S(1)}, f32[128,128]{1,0:T(8,128)S(1)}, f32[128,128]{1,0:T(8,128)S(1)}, f32[128,128]{1...) custom-call(s32[1,4]{1,0:T(1,128)S(1)} %copy-done.2, ...), custom_call_target="tpu_custom_call" | custom-call | flops 1000000 | bytes 100000 | tf_op jit(solution)/shard_map/pallas_call | solution.py:425
  23.1 0.6 %shard_map.128.refs_5_.refs_2_ = f32[128,1024]{1,0:T(8,128)S(1)} custom-call(f32[64,128]{1,0:T(8,128)S(1)} %get-tuple-element.48.refs_0_, f32[1024,128]{1,0:T(8,128)S(1)} %get-tuple-element.49.refs_1_, f32[128,128]{1,0:T(8,128)S(1)} %get-tuple-element.51.refs_2_.refs_3_, bf16[128,1024]{1,0:T(8,128)(2,1)S(1)} %get-tuple-element.53.refs_3_.refs_5_.refs_2_, ...), custom_call_target="tpu_custom_call" | custom-call | flops 1000000 | bytes 100000 | tf_op jit(solution)/shard_map/pallas_call | solution.py:425
  23.7 0.0 collective-permute-done.1.refs_4_.refs_9_
  23.7 0.3 shard_map.129.refs_0_
  24.0 0.0 copy-start
  24.0 0.0 collective-permute-done.4.refs_1_.refs_12_
  24.0 0.7 %copy-done = f32[1024]{0:T(1024)S(1)} copy-done((f32[1024]{0:T(1024)S(1)}, f32[1024]{0:T(1024)}, u32[]{:S(2)}) %copy-start) | copy-done | bytes 4120
  24.7 0.7 %shard_map.130 = (f32[128,1024]{1,0:T(8,128)S(1)}, bf16[128,1024]{1,0:T(8,128)(2,1)S(1)}, f32[1,1024]{1,0:T(1,128)S(1)}) custom-call(bf16[1024,128]{1,0:T(8,128)(2,1)S(1)} %shard_map.129.refs_0_, bf16[128,1024]{1,0:T(8,128)(2,1)S(1)} %collective-permute-done.4.refs_1_.refs_12_, f32[128,1024]{1,0:T(8,128)S(1)} %shard_map.128.refs_5_.refs_2_, ...), custom_call_target="tpu_custom_call" | custom-call | flops 1000000 | bytes 100000 | tf_op jit(solution)/shard_map/pallas_call | solution.py:425
  25.4 1.3 %collective-permute-start.6 = (bf16[128,1024]{1,0:T(8,128)(2,1)S(1)}, bf16[128,1024]{1,0:T(8,128)(2,1)S(1)}, u32[]{:S(2)}, u32[]{:S(2)}) collective-permute-start(bf16[128,1024]{1,0:T(8,128)(2,1)S(1)} %get-tuple-element.57.refs_6_.refs_3_), channel_id=1, source_target_pairs={{4,0},{8,4},{12,8},{5,1},{9,5},{13,9},{6,2},{10,6},{14,10},{7,3},{... | collective-permute-start | bytes 786440 | tf_op jit(solution)/shard_map/ppermute | solution.py:19
  26.7 0.3 shard_map.131
  26.9 3.4 %collective-permute-done.5.refs_14_.refs_2_.refs_3_ = bf16[128,1024]{1,0:T(8,128)(2,1)S(1)} collective-permute-done((bf16[128,1024]{1,0:T(8,128)(2,1)S(1)}, bf16[128,1024]{1,0:T(8,128)(2,1)S(1)}, u32[]{:S(2)}, u32[]{:S(2)}) %collective-permute-start.5) | collective-permute-done | bytes 262176 | tf_op jit(solution)/shard_map/ppermute | solution.py:19
  30.3 2.4 %shard_map.132 = (bf16[128,1024]{1,0:T(8,128)(2,1)}, f32[16,128]{1,0:T(8,128)S(1)}) custom-call(f32[64,128]{1,0:T(8,128)S(1)} %get-tuple-element.48.refs_0_, f32[1024,128]{1,0:T(8,128)S(1)} %get-tuple-element.49.refs_1_, f32[128,128]{1,0:T(8,128)S(1)} %get-tuple-element.50.refs_2_, f32[128,128]{1,0:T(8,128)S(1)} %get-tuple-element.51.refs_2_.refs_3_, ...), custom_call_target="tpu_custom_call" | custom-call | flops 1000000 | bytes 100000 | tf_op jit(solution)/shard_map/pallas_call | solution.py:425
  32.7 0.0 collective-permute-start.7
  32.7 1.5 %collective-permute-start.8 = (f32[16,128]{1,0:T(8,128)S(1)}, f32[16,128]{1,0:T(8,128)S(1)}, u32[]{:S(2)}, u32[]{:S(2)}) collective-permute-start(f32[16,128]{1,0:T(8,128)S(1)} %get-tuple-element.80), channel_id=1, source_target_pairs={{0,2},{1,3},{2,0},{3,1},{4,6},{5,7},{6,4},{7,5},{8,10},{9,11},{10,... | collective-permute-start | bytes 24584 | tf_op jit(solution)/shard_map/ppermute | solution.py:454
  34.2 0.4 collective-permute-start.9
  34.6 0.0 collective-permute-done.7.refs_6_
  34.6 1.8 %collective-permute-done.8 = f32[16,128]{1,0:T(8,128)S(1)} collective-permute-done((f32[16,128]{1,0:T(8,128)S(1)}, f32[16,128]{1,0:T(8,128)S(1)}, u32[]{:S(2)}, u32[]{:S(2)}) %collective-permute-start.8) | collective-permute-done | bytes 8224 | tf_op jit(solution)/shard_map/ppermute | solution.py:454
  36.4 0.9 %collective-permute-done.9 = f32[16,128]{1,0:T(8,128)S(1)} collective-permute-done((f32[16,128]{1,0:T(8,128)S(1)}, f32[16,128]{1,0:T(8,128)S(1)}, u32[]{:S(2)}, u32[]{:S(2)}) %collective-permute-start.9) | collective-permute-done | bytes 8224 | tf_op jit(solution)/shard_map/ppermute | solution.py:454
  37.3 0.5 collective-permute-done.6.refs_3_.refs_4_
  37.8 0.5 %shard_map.136 = bf16[96,1024]{1,0:T(8,128)(2,1)S(1)} custom-call(bf16[256,128]{1,0:T(8,128)(2,1)S(1)} %get-tuple-element.62.refs_15_.refs_0_, f32[256,128]{1,0:T(8,128)S(1)} %get-tuple-element.75.refs_1_, f32[16,128]{1,0:T(8,128)S(1)} %get-tuple-element.74.refs_2_, bf16[128,1024]{1,0:T(8,128)(2,1)S(1)} %collective-permute-done.3.refs_7_.refs_2_.refs_3_, ...), custom_call_target="tpu_custom_call" | custom-call | flops 1000000 | bytes 100000 | tf_op jit(solution)/shard_map/pallas_call | solution.py:425
  38.3 1.3 %collective-permute-start.10 = (bf16[96,1024]{1,0:T(8,128)(2,1)S(1)}, bf16[96,1024]{1,0:T(8,128)(2,1)S(1)}, u32[]{:S(2)}, u32[]{:S(2)}) collective-permute-start(bf16[96,1024]{1,0:T(8,128)(2,1)S(1)} %shard_map.136), channel_id=1, source_target_pairs={{4,0},{8,4},{5,1},{9,5},{6,2},{10,6},{7,3},{11,7},{20,16},{24,20},... | collective-permute-start | bytes 589832 | tf_op jit(solution)/shard_map/ppermute | solution.py:19
  39.6 5.0 %collective-permute-start.11 = (f32[16,128]{1,0:T(8,128)S(1)}, f32[16,128]{1,0:T(8,128)S(1)}, u32[]{:S(2)}, u32[]{:S(2)}) collective-permute-start(f32[16,128]{1,0:T(8,128)S(1)} %add_add_fusion.refs_3_), channel_id=1, source_target_pairs={{0,8},{4,12},{8,0},{12,4},{1,9},{5,13},{9,1},{13,5},{2,10},{6,14},... | collective-permute-start | bytes 24584 | tf_op jit(solution)/shard_map/ppermute | solution.py:454
  44.6 0.9 %collective-permute-start.12 = (f32[16,128]{1,0:T(8,128)S(1)}, f32[16,128]{1,0:T(8,128)S(1)}, u32[]{:S(2)}, u32[]{:S(2)}) collective-permute-start(f32[16,128]{1,0:T(8,128)S(1)} %add_add_fusion.refs_3_), channel_id=1, source_target_pairs={{0,12},{4,8},{8,4},{12,0},{1,13},{5,9},{9,5},{13,1},{2,14},{6,10},... | collective-permute-start | bytes 24584 | tf_op jit(solution)/shard_map/ppermute | solution.py:454
  45.5 0.0 collective-permute-start.13
  45.5 0.9 %shard_map.133 = (f32[128,1024]{1,0:T(8,128)S(1)}, f32[128,1024]{1,0:T(8,128)S(1)}) custom-call(f32[64,128]{1,0:T(8,128)S(1)} %get-tuple-element.48.refs_0_, f32[128,128]{1,0:T(8,128)S(1)} %get-tuple-element.66.refs_1_, bf16[128,1024]{1,0:T(8,128)(2,1)S(1)} %get-tuple-element.53.refs_3_.refs_5_.refs_2_, ...), custom_call_target="tpu_custom_call" | custom-call | flops 1000000 | bytes 100000 | tf_op jit(solution)/shard_map/pallas_call | solution.py:425
  46.3 1.5 %shard_map.134 = (bf16[128,1024]{1,0:T(8,128)(2,1)}, f32[128,1024]{1,0:T(8,128)S(1)}, f32[128,1024]{1,0:T(8,128)S(1)}) custom-call(f32[64,128]{1,0:T(8,128)S(1)} %get-tuple-element.48.refs_0_, f32[128,128]{1,0:T(8,128)S(1)} %get-tuple-element.65.refs_1_, bf16[128,1024]{1,0:T(8,128)(2,1)S(1)} %collective-permute-done.3.refs_7_.refs_2_.refs_3_, ...), custom_call_target="tpu_custom_call" | custom-call | flops 1000000 | bytes 100000 | tf_op jit(solution)/shard_map/pallas_call | solution.py:425
  47.9 0.4 shard_map.135
  48.3 0.1 collective-permute-done.10.refs_4_
  48.4 1.3 %shard_map.137 = (bf16[128,1024]{1,0:T(8,128)(2,1)}, bf16[128,1024]{1,0:T(8,128)(2,1)}) custom-call(bf16[1024,96]{1,0:T(8,128)(2,1)S(1)} %get-tuple-element.72.refs_0_, f32[1024,96]{1,0:T(8,128)S(1)} %get-tuple-element.73.refs_1_, f32[16,128]{1,0:T(8,128)S(1)} %get-tuple-element.74.refs_2_, ...), custom_call_target="tpu_custom_call" | custom-call | flops 1000000 | bytes 100000 | tf_op jit(solution)/shard_map/pallas_call | solution.py:425
  49.7 0.3 collective-permute-done.11.refs_0_
  50.0 0.1 collective-permute-done.12.refs_1_
  50.1 0.0 collective-permute-done.13.refs_2_
  50.1 0.6 %shard_map.138 = (f32[8,128]{1,0:T(8,128)}, f32[8,8]{1,0:T(8,128)}) custom-call(f32[16,128]{1,0:T(8,128)S(1)} %collective-permute-done.11.refs_0_, f32[16,128]{1,0:T(8,128)S(1)} %collective-permute-done.12.refs_1_, f32[16,128]{1,0:T(8,128)S(1)} %collective-permute-done.13.refs_2_, f32[16,128]{1,0:T(8,128)S(1)} %add_add_fusion.refs_3_), custom_call_target="tpu_custom_call" | custom-call | flops 1000000 | bytes 100000 | tf_op jit(solution)/shard_map/pallas_call | solution.py:425
  (1 shorter events, 0.0 us)
Async XLA Ops:
  0.6 19.3 %copy-start.1 = (f32[8,8]{1,0:T(8,128)S(1)}, f32[8,8]{1,0:T(8,128)}, u32[]{:S(2)}) copy-start(f32[8,8]{1,0:T(8,128)} %refs_1_.1) | copy-start | bytes 772
  0.6 11.9 %collective-permute-start = (bf16[128,1024]{1,0:T(8,128)(2,1)}, bf16[128,1024]{1,0:T(8,128)(2,1)S(1)}, u32[]{:S(2)}, u32[]{:S(2)}) collective-permute-start(bf16[128,1024]{1,0:T(8,128)(2,1)} %bitcast.15), channel_id=1, source_target_pairs={{0,4},{4,8},{8,12},{1,5},{5,9},{9,13},{2,6},{6,10},{10,14},{3,7},{... | collective-permute-start | bytes 786440 | tf_op jit(solution)/shard_map/ppermute | solution.py:19
  5.6 11.5 %collective-permute-start.2 = (bf16[128,1024]{1,0:T(8,128)(2,1)}, bf16[128,1024]{1,0:T(8,128)(2,1)S(1)}, u32[]{:S(2)}, u32[]{:S(2)}) collective-permute-start(bf16[128,1024]{1,0:T(8,128)(2,1)} %bitcast.17), channel_id=1, source_target_pairs={{0,4},{4,8},{8,12},{1,5},{5,9},{9,13},{2,6},{6,10},{10,14},{3,7},{... | collective-permute-start | bytes 786440 | tf_op jit(solution)/shard_map/ppermute | solution.py:19
  9.1 9.6 %collective-permute-start.3 = (bf16[128,1024]{1,0:T(8,128)(2,1)}, bf16[128,1024]{1,0:T(8,128)(2,1)S(1)}, u32[]{:S(2)}, u32[]{:S(2)}) collective-permute-start(bf16[128,1024]{1,0:T(8,128)(2,1)} %bitcast.13), channel_id=1, source_target_pairs={{4,0},{8,4},{12,8},{5,1},{9,5},{13,9},{6,2},{10,6},{14,10},{7,3},{... | collective-permute-start | bytes 786440 | tf_op jit(solution)/shard_map/ppermute | solution.py:19
  12.6 11.1 %collective-permute-start.1 = (bf16[128,1024]{1,0:T(8,128)(2,1)S(1)}, bf16[128,1024]{1,0:T(8,128)(2,1)S(1)}, u32[]{:S(2)}, u32[]{:S(2)}) collective-permute-start(bf16[128,1024]{1,0:T(8,128)(2,1)S(1)} %collective-permute-done.refs_4_.refs_3_.refs_8_), channel_id=1, source_target_pairs={{4,8},{8,12},{5,9},{9,13},{6,10},{10,14},{7,11},{11,15},{20,24},{2... | collective-permute-start | bytes 786440 | tf_op jit(solution)/shard_map/ppermute | solution.py:19
  17.1 7.0 %collective-permute-start.4 = (bf16[128,1024]{1,0:T(8,128)(2,1)S(1)}, bf16[128,1024]{1,0:T(8,128)(2,1)S(1)}, u32[]{:S(2)}, u32[]{:S(2)}) collective-permute-start(bf16[128,1024]{1,0:T(8,128)(2,1)S(1)} %collective-permute-done.2.refs_5_.refs_11_), channel_id=1, source_target_pairs={{4,8},{8,12},{5,9},{9,13},{6,10},{10,14},{7,11},{11,15},{20,24},{2... | collective-permute-start | bytes 786440 | tf_op jit(solution)/shard_map/ppermute | solution.py:19
  18.7 11.7 %collective-permute-start.5 = (bf16[128,1024]{1,0:T(8,128)(2,1)S(1)}, bf16[128,1024]{1,0:T(8,128)(2,1)S(1)}, u32[]{:S(2)}, u32[]{:S(2)}) collective-permute-start(bf16[128,1024]{1,0:T(8,128)(2,1)S(1)} %collective-permute-done.3.refs_7_.refs_2_.refs_3_), channel_id=1, source_target_pairs={{4,0},{8,4},{5,1},{9,5},{6,2},{10,6},{7,3},{11,7},{20,16},{24,20},... | collective-permute-start | bytes 786440 | tf_op jit(solution)/shard_map/ppermute | solution.py:19
  20.0 0.7 %copy-start.2 = (s32[1,4]{1,0:T(1,128)S(1)}, s32[1,4]{1,0:T(1,128)}, u32[]{:S(2)}) copy-start(s32[1,4]{1,0:T(1,128)} %refs_0_.1) | copy-start | bytes 52
  24.0 0.7 %copy-start = (f32[1024]{0:T(1024)S(1)}, f32[1024]{0:T(1024)}, u32[]{:S(2)}) copy-start(f32[1024]{0:T(1024)} %param.15) | copy-start | bytes 12292
  25.4 12.4 %collective-permute-start.6 = (bf16[128,1024]{1,0:T(8,128)(2,1)S(1)}, bf16[128,1024]{1,0:T(8,128)(2,1)S(1)}, u32[]{:S(2)}, u32[]{:S(2)}) collective-permute-start(bf16[128,1024]{1,0:T(8,128)(2,1)S(1)} %get-tuple-element.57.refs_6_.refs_3_), channel_id=1, source_target_pairs={{4,0},{8,4},{12,8},{5,1},{9,5},{13,9},{6,2},{10,6},{14,10},{7,3},{... | collective-permute-start | bytes 786440 | tf_op jit(solution)/shard_map/ppermute | solution.py:19
  32.7 1.9 %collective-permute-start.7 = (f32[16,128]{1,0:T(8,128)S(1)}, f32[16,128]{1,0:T(8,128)S(1)}, u32[]{:S(2)}, u32[]{:S(2)}) collective-permute-start(f32[16,128]{1,0:T(8,128)S(1)} %get-tuple-element.80), channel_id=1, source_target_pairs={{0,1},{1,0},{2,3},{3,2},{4,5},{5,4},{6,7},{7,6},{8,9},{9,8},{10,11... | collective-permute-start | bytes 24584 | tf_op jit(solution)/shard_map/ppermute | solution.py:454
  32.7 3.7 %collective-permute-start.8 = (f32[16,128]{1,0:T(8,128)S(1)}, f32[16,128]{1,0:T(8,128)S(1)}, u32[]{:S(2)}, u32[]{:S(2)}) collective-permute-start(f32[16,128]{1,0:T(8,128)S(1)} %get-tuple-element.80), channel_id=1, source_target_pairs={{0,2},{1,3},{2,0},{3,1},{4,6},{5,7},{6,4},{7,5},{8,10},{9,11},{10,... | collective-permute-start | bytes 24584 | tf_op jit(solution)/shard_map/ppermute | solution.py:454
  34.2 3.1 %collective-permute-start.9 = (f32[16,128]{1,0:T(8,128)S(1)}, f32[16,128]{1,0:T(8,128)S(1)}, u32[]{:S(2)}, u32[]{:S(2)}) collective-permute-start(f32[16,128]{1,0:T(8,128)S(1)} %get-tuple-element.80), channel_id=1, source_target_pairs={{0,3},{1,2},{2,1},{3,0},{4,7},{5,6},{6,5},{7,4},{8,11},{9,10},{10,... | collective-permute-start | bytes 24584 | tf_op jit(solution)/shard_map/ppermute | solution.py:454
  38.3 10.1 %collective-permute-start.10 = (bf16[96,1024]{1,0:T(8,128)(2,1)S(1)}, bf16[96,1024]{1,0:T(8,128)(2,1)S(1)}, u32[]{:S(2)}, u32[]{:S(2)}) collective-permute-start(bf16[96,1024]{1,0:T(8,128)(2,1)S(1)} %shard_map.136), channel_id=1, source_target_pairs={{4,0},{8,4},{5,1},{9,5},{6,2},{10,6},{7,3},{11,7},{20,16},{24,20},... | collective-permute-start | bytes 589832 | tf_op jit(solution)/shard_map/ppermute | solution.py:19
  39.6 10.4 %collective-permute-start.11 = (f32[16,128]{1,0:T(8,128)S(1)}, f32[16,128]{1,0:T(8,128)S(1)}, u32[]{:S(2)}, u32[]{:S(2)}) collective-permute-start(f32[16,128]{1,0:T(8,128)S(1)} %add_add_fusion.refs_3_), channel_id=1, source_target_pairs={{0,8},{4,12},{8,0},{12,4},{1,9},{5,13},{9,1},{13,5},{2,10},{6,14},... | collective-permute-start | bytes 24584 | tf_op jit(solution)/shard_map/ppermute | solution.py:454
  44.6 5.6 %collective-permute-start.12 = (f32[16,128]{1,0:T(8,128)S(1)}, f32[16,128]{1,0:T(8,128)S(1)}, u32[]{:S(2)}, u32[]{:S(2)}) collective-permute-start(f32[16,128]{1,0:T(8,128)S(1)} %add_add_fusion.refs_3_), channel_id=1, source_target_pairs={{0,12},{4,8},{8,4},{12,0},{1,13},{5,9},{9,5},{13,1},{2,14},{6,10},... | collective-permute-start | bytes 24584 | tf_op jit(solution)/shard_map/ppermute | solution.py:454
  45.5 4.7 %collective-permute-start.13 = (f32[16,128]{1,0:T(8,128)S(1)}, f32[16,128]{1,0:T(8,128)S(1)}, u32[]{:S(2)}, u32[]{:S(2)}) collective-permute-start(f32[16,128]{1,0:T(8,128)S(1)} %add_add_fusion.refs_3_), channel_id=1, source_target_pairs={{0,4},{4,0},{8,12},{12,8},{1,5},{5,1},{9,13},{13,9},{2,6},{6,2},{1... | collective-permute-start | bytes 24584 | tf_op jit(solution)/shard_map/ppermute | solution.py:454

commit v17 on v15

--- a/solution.py
+++ b/solution.py
@@ -308,18 +308,31 @@
 
 
 def gate_and_key_kernel(hops, heads, scaling, *refs):
-    attention, out_grad, gain = refs[8:11]
-    gate_out, key_out, value_out, held, written = refs[11:]
-    step = 16
+    attention, out_grad, gain, query_grad = refs[8:12]
+    gate_out, query_out, key_out, value_out, held, written = refs[12:]
+    rows, step = attention.shape[0], 16
+    part = rows // 4
+    copies = []
+
+    def write(source, target, low):
+        lines = slice(low, low + part)
+        copies.append(
+            pltpu.make_async_copy(source.at[lines], target.at[lines], written.at[len(copies)])
+        )
+        copies[-1].start()
+
+    for low in range(0, rows, part):
+        write(query_grad, query_out, low)
     gain_row = gain[...]
-    for low in range(0, attention.shape[0], step):
+    for low in range(0, rows, step):
         span = slice(low, low + step)
         normed, _ = normed_rows(attention[span, :])
         held[span, :] = (out_grad[span, :].astype(F32) * normed * gain_row).astype(BF16)
-    copy = pltpu.make_async_copy(held, gate_out, written)
-    copy.start()
+        if (low + step) % part == 0:
+            write(held, gate_out, low + step - part)
     add_key_grads(hops, heads, scaling, *refs[:6], refs[6:8], into(key_out, value_out))
-    copy.wait()
+    for copy in copies:
+        copy.wait()
 
 
 def message_kernel(hops, heads, scaling, *refs):
@@ -373,7 +386,6 @@
     tail = rows - cut
     is_late = late[0:1, :width]
     copies = []
-    ends = [*range(1, heads - 1, 2), heads - 2, heads - 1]
 
     def write(at, cols):
         source, target = held[at].at[:, cols], outs[at].at[:, cols]
@@ -396,10 +408,8 @@
             held[at][:cut, cols] = ((before[:cut, cols] + part[:cut]) * factor).astype(BF16)
             sent = message[at * tail : (at + 1) * tail, cols].astype(F32) * is_late
             held[at][cut:, cols] = ((before[cut:, cols] + part[cut:] + sent) * factor).astype(BF16)
-        if head in ends:
-            before = ends[ends.index(head) - 1] + 1 if head != ends[0] else 0
-            for at in (0, 1):
-                write(at, slice(before * width, cols.stop))
+        for at in (0, 1):
+            write(at, cols)
 
     in_stages(heads, scores, differentiate)
     for copy in copies:
@@ -552,12 +562,12 @@
             )
         later_grads.append(passed_along(arrived, "ctx", -1, hops + 1))
         if hops == 1:
-            gate_grad, *key_grads = on_device(
+            gate_grad, query_grad, *key_grads = on_device(
                 partial(gate_and_key_kernel, hops, heads, scaling),
-                [narrow, wide, wide],
-                (*key_operands(hops), *key_grads, attention, grad, gain),
-                far_outs=1,
-                scratch=[pltpu.VMEM((rows, features), BF16), pltpu.SemaphoreType.DMA(())],
+                [narrow, narrow, wide, wide],
+                (*key_operands(hops), *key_grads, attention, grad, gain, query_grad),
+                far_outs=2,
+                scratch=[pltpu.VMEM((rows, features), BF16), pltpu.SemaphoreType.DMA((8,))],
             )
         else:
             key_grads = on_device(

time: 50.9 us -> 50.6 us (level)
  Pallas kernels: 11.8 us -> 11.2 us
  waiting for transfers between devices: 14.3 us -> 14.9 us
    pallas_call x11, Pallas kernels: 11.8 us -> 11.2 us  [on_device(): pl.pallas_call(body, out_shape=outs, in_specs=[pl.BlockSpec(memory_space=...]
    ppermute x8, waiting for transfers between devices: 11.3 us -> 11.9 us  [passed_along(): lax.ppermute(array, axis, [(i, i + by) for i in range(first, last + 1)])]
  transfers between devices with their start and end apart: 14 -> 14, of which waited for: 9 -> 9; matrix products, arithmetic and copies ran while one was open for 0% -> 0% of each run, Pallas kernels for 21% -> 20%
where the time goes in v17:
time: 50.6 us; the launch traced here: 50.2 us
  starting transfers between devices  22 us (43%)
  waiting for transfers between devices  14.9 us (29%)
  Pallas kernels  11.2 us (22%)
  local copies, waits for them, and re-layouts  1.31 us (3%)
  between operations  0.83 us (2%)
    ppermute x8, starting transfers between devices, passed_along(): lax.ppermute(array, axis, [(i, i + by) for i in range(first, last + 1)])  14.9 us
    ppermute x8, waiting for transfers between devices, passed_along(): lax.ppermute(array, axis, [(i, i + by) for i in range(first, last + 1)])  11.9 us
    pallas_call x11, Pallas kernels, on_device(): pl.pallas_call(body, out_shape=outs, in_specs=[pl.BlockSpec(memory_space=...  11.2 us
    ppermute x6, starting transfers between devices, exchanged(): lax.ppermute(array, axis, [(i, i ^ distance) for i in range(size)])  7.11 us
    ppermute x6, waiting for transfers between devices, exchanged(): lax.ppermute(array, axis, [(i, i ^ distance) for i in range(size)])  3.03 us
    unnamed x6, local copies, waits for them, and re-layouts  1.31 us
  transfers between devices with their start and end apart: 14, of which 9 were waited for; matrix products, arithmetic and copies ran while one was open for 0% of the time, Pallas kernels for 20%

profile of v17, /device:TPU:0, one launch (start us, length us, event | category | flops | bytes accessed | tf_op | source)
XLA Modules:
  0.0 50.2 jit_solution(10828236038888270114)
XLA Ops:
  0.6 0.0 copy-start.1
  0.6 4.9 %collective-permute-start.1 = (bf16[128,1024]{1,0:T(8,128)(2,1)}, bf16[128,1024]{1,0:T(8,128)(2,1)S(1)}, u32[]{:S(2)}, u32[]{:S(2)}) collective-permute-start(bf16[128,1024]{1,0:T(8,128)(2,1)} %bitcast.15), channel_id=1, source_target_pairs={{0,4},{4,8},{8,12},{1,5},{5,9},{9,13},{2,6},{6,10},{10,14},{3,7},{... | collective-permute-start | bytes 786440 | tf_op jit(solution)/shard_map/ppermute | solution.py:19
  5.6 3.5 %collective-permute-start.3 = (bf16[128,1024]{1,0:T(8,128)(2,1)}, bf16[128,1024]{1,0:T(8,128)(2,1)S(1)}, u32[]{:S(2)}, u32[]{:S(2)}) collective-permute-start(bf16[128,1024]{1,0:T(8,128)(2,1)} %bitcast.17), channel_id=1, source_target_pairs={{0,4},{4,8},{8,12},{1,5},{5,9},{9,13},{2,6},{6,10},{10,14},{3,7},{... | collective-permute-start | bytes 786440 | tf_op jit(solution)/shard_map/ppermute | solution.py:19
  9.1 1.3 %collective-permute-start = (bf16[128,1024]{1,0:T(8,128)(2,1)}, bf16[128,1024]{1,0:T(8,128)(2,1)S(1)}, u32[]{:S(2)}, u32[]{:S(2)}) collective-permute-start(bf16[128,1024]{1,0:T(8,128)(2,1)} %bitcast.13), channel_id=1, source_target_pairs={{4,0},{8,4},{12,8},{5,1},{9,5},{13,9},{6,2},{10,6},{14,10},{7,3},{... | collective-permute-start | bytes 786440 | tf_op jit(solution)/shard_map/ppermute | solution.py:19
  10.4 2.2 %collective-permute-done.1.refs_4_.refs_8_.refs_5_ = bf16[128,1024]{1,0:T(8,128)(2,1)S(1)} collective-permute-done((bf16[128,1024]{1,0:T(8,128)(2,1)}, bf16[128,1024]{1,0:T(8,128)(2,1)S(1)}, u32[]{:S(2)}, u32[]{:S(2)}) %collective-permute-start.1) | collective-permute-done | bytes 262176 | tf_op jit(solution)/shard_map/ppermute | solution.py:19
  12.6 0.7 %collective-permute-start.2 = (bf16[128,1024]{1,0:T(8,128)(2,1)S(1)}, bf16[128,1024]{1,0:T(8,128)(2,1)S(1)}, u32[]{:S(2)}, u32[]{:S(2)}) collective-permute-start(bf16[128,1024]{1,0:T(8,128)(2,1)S(1)} %collective-permute-done.1.refs_4_.refs_8_.refs_5_), channel_id=1, source_target_pairs={{4,8},{8,12},{5,9},{9,13},{6,10},{10,14},{7,11},{11,15},{20,24},{2... | collective-permute-start | bytes 786440 | tf_op jit(solution)/shard_map/ppermute | solution.py:19
  13.3 3.8 %collective-permute-done.3.refs_5_.refs_11_.refs_6_ = bf16[128,1024]{1,0:T(8,128)(2,1)S(1)} collective-permute-done((bf16[128,1024]{1,0:T(8,128)(2,1)}, bf16[128,1024]{1,0:T(8,128)(2,1)S(1)}, u32[]{:S(2)}, u32[]{:S(2)}) %collective-permute-start.3) | collective-permute-done | bytes 262176 | tf_op jit(solution)/shard_map/ppermute | solution.py:19
  17.1 0.7 %collective-permute-start.4 = (bf16[128,1024]{1,0:T(8,128)(2,1)S(1)}, bf16[128,1024]{1,0:T(8,128)(2,1)S(1)}, u32[]{:S(2)}, u32[]{:S(2)}) collective-permute-start(bf16[128,1024]{1,0:T(8,128)(2,1)S(1)} %collective-permute-done.3.refs_5_.refs_11_.refs_6_), channel_id=1, source_target_pairs={{4,8},{8,12},{5,9},{9,13},{6,10},{10,14},{7,11},{11,15},{20,24},{2... | collective-permute-start | bytes 786440 | tf_op jit(solution)/shard_map/ppermute | solution.py:19
  17.7 0.9 %collective-permute-done.refs_7_.refs_2_.refs_3_ = bf16[128,1024]{1,0:T(8,128)(2,1)S(1)} collective-permute-done((bf16[128,1024]{1,0:T(8,128)(2,1)}, bf16[128,1024]{1,0:T(8,128)(2,1)S(1)}, u32[]{:S(2)}, u32[]{:S(2)}) %collective-permute-start) | collective-permute-done | bytes 262176 | tf_op jit(solution)/shard_map/ppermute | solution.py:19
  18.7 1.3 %collective-permute-start.6 = (bf16[128,1024]{1,0:T(8,128)(2,1)S(1)}, bf16[128,1024]{1,0:T(8,128)(2,1)S(1)}, u32[]{:S(2)}, u32[]{:S(2)}) collective-permute-start(bf16[128,1024]{1,0:T(8,128)(2,1)S(1)} %collective-permute-done.refs_7_.refs_2_.refs_3_), channel_id=1, source_target_pairs={{4,0},{8,4},{5,1},{9,5},{6,2},{10,6},{7,3},{11,7},{20,16},{24,20},... | collective-permute-start | bytes 786440 | tf_op jit(solution)/shard_map/ppermute | solution.py:19
  20.0 0.0 copy-start.2
  20.0 0.0 copy-done.1
  20.0 0.6 %copy-done.2 = s32[1,4]{1,0:T(1,128)S(1)} copy-done((s32[1,4]{1,0:T(1,128)S(1)}, s32[1,4]{1,0:T(1,128)}, u32[]{:S(2)}) %copy-start.2) | copy-done | bytes 40
  20.6 2.5 %shard_map.127 = (f32[64,128]{1,0:T(8,128)S(1)}, f32[1024,128]{1,0:T(8,128)S(1)}, f32[128,128]{1,0:T(8,128)S(1)}, f32[128,128]{1,0:T(8,128)S(1)}, f32[128,128]{1...) custom-call(s32[1,4]{1,0:T(1,128)S(1)} %copy-done.2, ...), custom_call_target="tpu_custom_call" | custom-call | flops 1000000 | bytes 100000 | tf_op jit(solution)/shard_map/pallas_call | solution.py:435
  23.1 0.6 %shard_map.128.refs_5_.refs_2_ = f32[128,1024]{1,0:T(8,128)S(1)} custom-call(f32[64,128]{1,0:T(8,128)S(1)} %get-tuple-element.47.refs_0_, f32[1024,128]{1,0:T(8,128)S(1)} %get-tuple-element.49.refs_1_, f32[128,128]{1,0:T(8,128)S(1)} %get-tuple-element.52.refs_2_.refs_3_, bf16[128,1024]{1,0:T(8,128)(2,1)S(1)} %get-tuple-element.51.refs_3_.refs_5_.refs_2_, ...), custom_call_target="tpu_custom_call" | custom-call | flops 1000000 | bytes 100000 | tf_op jit(solution)/shard_map/pallas_call | solution.py:435
  23.7 0.0 collective-permute-done.2.refs_4_.refs_9_
  23.7 0.3 shard_map.129.refs_0_
  24.0 0.0 copy-start
  24.0 0.0 collective-permute-done.4.refs_1_.refs_12_
  24.0 0.7 %copy-done = f32[1024]{0:T(1024)S(1)} copy-done((f32[1024]{0:T(1024)S(1)}, f32[1024]{0:T(1024)}, u32[]{:S(2)}) %copy-start) | copy-done | bytes 4120
  24.7 0.6 %shard_map.130 = (f32[128,1024]{1,0:T(8,128)S(1)}, bf16[128,1024]{1,0:T(8,128)(2,1)S(1)}, f32[1,1024]{1,0:T(1,128)S(1)}) custom-call(bf16[1024,128]{1,0:T(8,128)(2,1)S(1)} %shard_map.129.refs_0_, bf16[128,1024]{1,0:T(8,128)(2,1)S(1)} %collective-permute-done.4.refs_1_.refs_12_, f32[128,1024]{1,0:T(8,128)S(1)} %shard_map.128.refs_5_.refs_2_, ...), custom_call_target="tpu_custom_call" | custom-call | flops 1000000 | bytes 100000 | tf_op jit(solution)/shard_map/pallas_call | solution.py:435
  25.3 1.3 %collective-permute-start.5 = (bf16[128,1024]{1,0:T(8,128)(2,1)S(1)}, bf16[128,1024]{1,0:T(8,128)(2,1)S(1)}, u32[]{:S(2)}, u32[]{:S(2)}) collective-permute-start(bf16[128,1024]{1,0:T(8,128)(2,1)S(1)} %get-tuple-element.56.refs_6_.refs_3_), channel_id=1, source_target_pairs={{4,0},{8,4},{12,8},{5,1},{9,5},{13,9},{6,2},{10,6},{14,10},{7,3},{... | collective-permute-start | bytes 786440 | tf_op jit(solution)/shard_map/ppermute | solution.py:19
  26.6 3.7 %collective-permute-done.6.refs_14_.refs_2_.refs_3_ = bf16[128,1024]{1,0:T(8,128)(2,1)S(1)} collective-permute-done((bf16[128,1024]{1,0:T(8,128)(2,1)S(1)}, bf16[128,1024]{1,0:T(8,128)(2,1)S(1)}, u32[]{:S(2)}, u32[]{:S(2)}) %collective-permute-start.6) | collective-permute-done | bytes 262176 | tf_op jit(solution)/shard_map/ppermute | solution.py:19
  30.3 1.7 %shard_map.131 = (bf16[128,1024]{1,0:T(8,128)(2,1)S(1)}, f32[16,128]{1,0:T(8,128)S(1)}) custom-call(f32[64,128]{1,0:T(8,128)S(1)} %get-tuple-element.47.refs_0_, f32[1024,128]{1,0:T(8,128)S(1)} %get-tuple-element.49.refs_1_, f32[128,128]{1,0:T(8,128)S(1)} %get-tuple-element.60.refs_2_, f32[128,128]{1,0:T(8,128)S(1)} %get-tuple-element.52.refs_2_.refs_3_, ...), custom_call_target="tpu_custom_call" | custom-call | flops 1000000 | bytes 100000 | tf_op jit(solution)/shard_map/pallas_call | solution.py:435
  32.0 0.1 collective-permute-start.7
  32.1 1.6 %collective-permute-start.8 = (f32[16,128]{1,0:T(8,128)S(1)}, f32[16,128]{1,0:T(8,128)S(1)}, u32[]{:S(2)}, u32[]{:S(2)}) collective-permute-start(f32[16,128]{1,0:T(8,128)S(1)} %get-tuple-element.78), channel_id=1, source_target_pairs={{0,2},{1,3},{2,0},{3,1},{4,6},{5,7},{6,4},{7,5},{8,10},{9,11},{10,... | collective-permute-start | bytes 24584 | tf_op jit(solution)/shard_map/ppermute | solution.py:464
  33.7 0.3 collective-permute-start.9
  34.0 0.0 collective-permute-done.7.refs_6_
  34.0 1.9 %collective-permute-done.8 = f32[16,128]{1,0:T(8,128)S(1)} collective-permute-done((f32[16,128]{1,0:T(8,128)S(1)}, f32[16,128]{1,0:T(8,128)S(1)}, u32[]{:S(2)}, u32[]{:S(2)}) %collective-permute-start.8) | collective-permute-done | bytes 8224 | tf_op jit(solution)/shard_map/ppermute | solution.py:464
  35.8 0.9 %collective-permute-done.9 = f32[16,128]{1,0:T(8,128)S(1)} collective-permute-done((f32[16,128]{1,0:T(8,128)S(1)}, f32[16,128]{1,0:T(8,128)S(1)}, u32[]{:S(2)}, u32[]{:S(2)}) %collective-permute-start.9) | collective-permute-done | bytes 8224 | tf_op jit(solution)/shard_map/ppermute | solution.py:464
  36.7 1.0 %collective-permute-done.5.refs_3_.refs_4_ = bf16[128,1024]{1,0:T(8,128)(2,1)S(1)} collective-permute-done((bf16[128,1024]{1,0:T(8,128)(2,1)S(1)}, bf16[128,1024]{1,0:T(8,128)(2,1)S(1)}, u32[]{:S(2)}, u32[]{:S(2)}) %collective-permute-start.5) | collective-permute-done | bytes 262176 | tf_op jit(solution)/shard_map/ppermute | solution.py:19
  37.7 0.6 %shard_map.135 = bf16[96,1024]{1,0:T(8,128)(2,1)S(1)} custom-call(f32[64,128]{1,0:T(8,128)S(1)} %get-tuple-element.47.refs_0_, f32[32,128]{1,0:T(8,128)S(1)} %get-tuple-element.73.refs_1_, f32[16,128]{1,0:T(8,128)S(1)} %get-tuple-element.72.refs_2_, bf16[128,1024]{1,0:T(8,128)(2,1)S(1)} %collective-permute-done.refs_7_.refs_2_.refs_3_, ...), custom_call_target="tpu_custom_call" | custom-call | flops 1000000 | bytes 100000 | tf_op jit(solution)/shard_map/pallas_call | solution.py:435
  38.4 1.3 %collective-permute-start.10 = (bf16[96,1024]{1,0:T(8,128)(2,1)S(1)}, bf16[96,1024]{1,0:T(8,128)(2,1)S(1)}, u32[]{:S(2)}, u32[]{:S(2)}) collective-permute-start(bf16[96,1024]{1,0:T(8,128)(2,1)S(1)} %shard_map.135), channel_id=1, source_target_pairs={{4,0},{8,4},{5,1},{9,5},{6,2},{10,6},{7,3},{11,7},{20,16},{24,20},... | collective-permute-start | bytes 589832 | tf_op jit(solution)/shard_map/ppermute | solution.py:19
  39.7 4.4 %collective-permute-start.11 = (f32[16,128]{1,0:T(8,128)S(1)}, f32[16,128]{1,0:T(8,128)S(1)}, u32[]{:S(2)}, u32[]{:S(2)}) collective-permute-start(f32[16,128]{1,0:T(8,128)S(1)} %add_add_fusion.refs_3_), channel_id=1, source_target_pairs={{0,12},{4,8},{8,4},{12,0},{1,13},{5,9},{9,5},{13,1},{2,14},{6,10},... | collective-permute-start | bytes 24584 | tf_op jit(solution)/shard_map/ppermute | solution.py:464
  44.0 0.4 collective-permute-start.12
  44.4 0.5 collective-permute-start.13
  44.9 0.9 %shard_map.132 = (f32[128,1024]{1,0:T(8,128)S(1)}, f32[128,1024]{1,0:T(8,128)S(1)}) custom-call(f32[64,128]{1,0:T(8,128)S(1)} %get-tuple-element.47.refs_0_, f32[128,128]{1,0:T(8,128)S(1)} %get-tuple-element.59.refs_1_, bf16[128,1024]{1,0:T(8,128)(2,1)S(1)} %get-tuple-element.51.refs_3_.refs_5_.refs_2_, ...), custom_call_target="tpu_custom_call" | custom-call | flops 1000000 | bytes 100000 | tf_op jit(solution)/shard_map/pallas_call | solution.py:435
  45.8 1.6 %shard_map.133 = (bf16[128,1024]{1,0:T(8,128)(2,1)}, bf16[128,1024]{1,0:T(8,128)(2,1)}, f32[128,1024]{1,0:T(8,128)S(1)}, f32[128,1024]{1,0:T(8,128)S(1)}) custom-call(f32[64,128]{1,0:T(8,128)S(1)} %get-tuple-element.47.refs_0_, f32[128,128]{1,0:T(8,128)S(1)} %get-tuple-element.48.refs_1_, bf16[128,1024]{1,0:T(8,128)(2,1)S(1)} %collective-permute-done.refs_7_.refs_2_.refs_3_, ...), custom_call_target="tpu_custom_call" | custom-call | flops 1000000 | bytes 100000 | tf_op jit(solution)/shard_map/pallas_call | solution.py:435
  47.4 0.4 shard_map.134
  47.8 0.2 collective-permute-done.10.refs_4_
  48.0 1.3 %shard_map.136 = (bf16[128,1024]{1,0:T(8,128)(2,1)}, bf16[128,1024]{1,0:T(8,128)(2,1)}) custom-call(bf16[1024,96]{1,0:T(8,128)(2,1)S(1)} %get-tuple-element.70.refs_0_, f32[1024,96]{1,0:T(8,128)S(1)} %get-tuple-element.71.refs_1_, f32[16,128]{1,0:T(8,128)S(1)} %get-tuple-element.72.refs_2_, ...), custom_call_target="tpu_custom_call" | custom-call | flops 1000000 | bytes 100000 | tf_op jit(solution)/shard_map/pallas_call | solution.py:435
  49.4 0.0 collective-permute-done.11.refs_0_
  49.4 0.3 collective-permute-done.12.refs_1_
  49.6 0.0 collective-permute-done.13.refs_2_
  49.6 0.6 %shard_map.137 = (f32[8,128]{1,0:T(8,128)}, f32[8,8]{1,0:T(8,128)}) custom-call(f32[16,128]{1,0:T(8,128)S(1)} %collective-permute-done.11.refs_0_, f32[16,128]{1,0:T(8,128)S(1)} %collective-permute-done.12.refs_1_, f32[16,128]{1,0:T(8,128)S(1)} %collective-permute-done.13.refs_2_, f32[16,128]{1,0:T(8,128)S(1)} %add_add_fusion.refs_3_), custom_call_target="tpu_custom_call" | custom-call | flops 1000000 | bytes 100000 | tf_op jit(solution)/shard_map/pallas_call | solution.py:435
  (1 shorter events, 0.0 us)
Async XLA Ops:
  0.6 19.3 %copy-start.1 = (f32[8,8]{1,0:T(8,128)S(1)}, f32[8,8]{1,0:T(8,128)}, u32[]{:S(2)}) copy-start(f32[8,8]{1,0:T(8,128)} %refs_1_.1) | copy-start | bytes 772
  0.6 11.9 %collective-permute-start.1 = (bf16[128,1024]{1,0:T(8,128)(2,1)}, bf16[128,1024]{1,0:T(8,128)(2,1)S(1)}, u32[]{:S(2)}, u32[]{:S(2)}) collective-permute-start(bf16[128,1024]{1,0:T(8,128)(2,1)} %bitcast.15), channel_id=1, source_target_pairs={{0,4},{4,8},{8,12},{1,5},{5,9},{9,13},{2,6},{6,10},{10,14},{3,7},{... | collective-permute-start | bytes 786440 | tf_op jit(solution)/shard_map/ppermute | solution.py:19
  5.6 11.5 %collective-permute-start.3 = (bf16[128,1024]{1,0:T(8,128)(2,1)}, bf16[128,1024]{1,0:T(8,128)(2,1)S(1)}, u32[]{:S(2)}, u32[]{:S(2)}) collective-permute-start(bf16[128,1024]{1,0:T(8,128)(2,1)} %bitcast.17), channel_id=1, source_target_pairs={{0,4},{4,8},{8,12},{1,5},{5,9},{9,13},{2,6},{6,10},{10,14},{3,7},{... | collective-permute-start | bytes 786440 | tf_op jit(solution)/shard_map/ppermute | solution.py:19
  9.1 9.6 %collective-permute-start = (bf16[128,1024]{1,0:T(8,128)(2,1)}, bf16[128,1024]{1,0:T(8,128)(2,1)S(1)}, u32[]{:S(2)}, u32[]{:S(2)}) collective-permute-start(bf16[128,1024]{1,0:T(8,128)(2,1)} %bitcast.13), channel_id=1, source_target_pairs={{4,0},{8,4},{12,8},{5,1},{9,5},{13,9},{6,2},{10,6},{14,10},{7,3},{... | collective-permute-start | bytes 786440 | tf_op jit(solution)/shard_map/ppermute | solution.py:19
  12.6 11.1 %collective-permute-start.2 = (bf16[128,1024]{1,0:T(8,128)(2,1)S(1)}, bf16[128,1024]{1,0:T(8,128)(2,1)S(1)}, u32[]{:S(2)}, u32[]{:S(2)}) collective-permute-start(bf16[128,1024]{1,0:T(8,128)(2,1)S(1)} %collective-permute-done.1.refs_4_.refs_8_.refs_5_), channel_id=1, source_target_pairs={{4,8},{8,12},{5,9},{9,13},{6,10},{10,14},{7,11},{11,15},{20,24},{2... | collective-permute-start | bytes 786440 | tf_op jit(solution)/shard_map/ppermute | solution.py:19
  17.1 7.0 %collective-permute-start.4 = (bf16[128,1024]{1,0:T(8,128)(2,1)S(1)}, bf16[128,1024]{1,0:T(8,128)(2,1)S(1)}, u32[]{:S(2)}, u32[]{:S(2)}) collective-permute-start(bf16[128,1024]{1,0:T(8,128)(2,1)S(1)} %collective-permute-done.3.refs_5_.refs_11_.refs_6_), channel_id=1, source_target_pairs={{4,8},{8,12},{5,9},{9,13},{6,10},{10,14},{7,11},{11,15},{20,24},{2... | collective-permute-start | bytes 786440 | tf_op jit(solution)/shard_map/ppermute | solution.py:19
  18.7 11.7 %collective-permute-start.6 = (bf16[128,1024]{1,0:T(8,128)(2,1)S(1)}, bf16[128,1024]{1,0:T(8,128)(2,1)S(1)}, u32[]{:S(2)}, u32[]{:S(2)}) collective-permute-start(bf16[128,1024]{1,0:T(8,128)(2,1)S(1)} %collective-permute-done.refs_7_.refs_2_.refs_3_), channel_id=1, source_target_pairs={{4,0},{8,4},{5,1},{9,5},{6,2},{10,6},{7,3},{11,7},{20,16},{24,20},... | collective-permute-start | bytes 786440 | tf_op jit(solution)/shard_map/ppermute | solution.py:19
  20.0 0.7 %copy-start.2 = (s32[1,4]{1,0:T(1,128)S(1)}, s32[1,4]{1,0:T(1,128)}, u32[]{:S(2)}) copy-start(s32[1,4]{1,0:T(1,128)} %refs_0_.1) | copy-start | bytes 52
  24.0 0.7 %copy-start = (f32[1024]{0:T(1024)S(1)}, f32[1024]{0:T(1024)}, u32[]{:S(2)}) copy-start(f32[1024]{0:T(1024)} %param.15) | copy-start | bytes 12292
  25.3 12.4 %collective-permute-start.5 = (bf16[128,1024]{1,0:T(8,128)(2,1)S(1)}, bf16[128,1024]{1,0:T(8,128)(2,1)S(1)}, u32[]{:S(2)}, u32[]{:S(2)}) collective-permute-start(bf16[128,1024]{1,0:T(8,128)(2,1)S(1)} %get-tuple-element.56.refs_6_.refs_3_), channel_id=1, source_target_pairs={{4,0},{8,4},{12,8},{5,1},{9,5},{13,9},{6,2},{10,6},{14,10},{7,3},{... | collective-permute-start | bytes 786440 | tf_op jit(solution)/shard_map/ppermute | solution.py:19
  32.0 1.9 %collective-permute-start.7 = (f32[16,128]{1,0:T(8,128)S(1)}, f32[16,128]{1,0:T(8,128)S(1)}, u32[]{:S(2)}, u32[]{:S(2)}) collective-permute-start(f32[16,128]{1,0:T(8,128)S(1)} %get-tuple-element.78), channel_id=1, source_target_pairs={{0,1},{1,0},{2,3},{3,2},{4,5},{5,4},{6,7},{7,6},{8,9},{9,8},{10,11... | collective-permute-start | bytes 24584 | tf_op jit(solution)/shard_map/ppermute | solution.py:464
  32.1 3.7 %collective-permute-start.8 = (f32[16,128]{1,0:T(8,128)S(1)}, f32[16,128]{1,0:T(8,128)S(1)}, u32[]{:S(2)}, u32[]{:S(2)}) collective-permute-start(f32[16,128]{1,0:T(8,128)S(1)} %get-tuple-element.78), channel_id=1, source_target_pairs={{0,2},{1,3},{2,0},{3,1},{4,6},{5,7},{6,4},{7,5},{8,10},{9,11},{10,... | collective-permute-start | bytes 24584 | tf_op jit(solution)/shard_map/ppermute | solution.py:464
  33.7 3.1 %collective-permute-start.9 = (f32[16,128]{1,0:T(8,128)S(1)}, f32[16,128]{1,0:T(8,128)S(1)}, u32[]{:S(2)}, u32[]{:S(2)}) collective-permute-start(f32[16,128]{1,0:T(8,128)S(1)} %get-tuple-element.78), channel_id=1, source_target_pairs={{0,3},{1,2},{2,1},{3,0},{4,7},{5,6},{6,5},{7,4},{8,11},{9,10},{10,... | collective-permute-start | bytes 24584 | tf_op jit(solution)/shard_map/ppermute | solution.py:464
  38.4 9.7 %collective-permute-start.10 = (bf16[96,1024]{1,0:T(8,128)(2,1)S(1)}, bf16[96,1024]{1,0:T(8,128)(2,1)S(1)}, u32[]{:S(2)}, u32[]{:S(2)}) collective-permute-start(bf16[96,1024]{1,0:T(8,128)(2,1)S(1)} %shard_map.135), channel_id=1, source_target_pairs={{4,0},{8,4},{5,1},{9,5},{6,2},{10,6},{7,3},{11,7},{20,16},{24,20},... | collective-permute-start | bytes 589832 | tf_op jit(solution)/shard_map/ppermute | solution.py:19
  39.7 9.7 %collective-permute-start.11 = (f32[16,128]{1,0:T(8,128)S(1)}, f32[16,128]{1,0:T(8,128)S(1)}, u32[]{:S(2)}, u32[]{:S(2)}) collective-permute-start(f32[16,128]{1,0:T(8,128)S(1)} %add_add_fusion.refs_3_), channel_id=1, source_target_pairs={{0,12},{4,8},{8,4},{12,0},{1,13},{5,9},{9,5},{13,1},{2,14},{6,10},... | collective-permute-start | bytes 24584 | tf_op jit(solution)/shard_map/ppermute | solution.py:464
  44.0 5.6 %collective-permute-start.12 = (f32[16,128]{1,0:T(8,128)S(1)}, f32[16,128]{1,0:T(8,128)S(1)}, u32[]{:S(2)}, u32[]{:S(2)}) collective-permute-start(f32[16,128]{1,0:T(8,128)S(1)} %add_add_fusion.refs_3_), channel_id=1, source_target_pairs={{0,8},{4,12},{8,0},{12,4},{1,9},{5,13},{9,1},{13,5},{2,10},{6,14},... | collective-permute-start | bytes 24584 | tf_op jit(solution)/shard_map/ppermute | solution.py:464
  44.4 5.3 %collective-permute-start.13 = (f32[16,128]{1,0:T(8,128)S(1)}, f32[16,128]{1,0:T(8,128)S(1)}, u32[]{:S(2)}, u32[]{:S(2)}) collective-permute-start(f32[16,128]{1,0:T(8,128)S(1)} %add_add_fusion.refs_3_), channel_id=1, source_target_pairs={{0,4},{4,0},{8,12},{12,8},{1,5},{5,1},{9,13},{13,9},{2,6},{6,2},{1... | collective-permute-start | bytes 24584 | tf_op jit(solution)/shard_map/ppermute | solution.py:464

commit v18 on v17

--- a/solution.py
+++ b/solution.py
@@ -112,10 +112,10 @@
 
 
 def first_kernel(plan, cut, heads, scaling, lengths, bias, *refs):
-    inputs, refs = refs[:5], refs[5:]
+    inputs, refs = refs[:6], refs[6:]
     table, near, masks, refs = refs[0], refs[1], refs[2 : 2 + len(plan)], refs[2 + len(plan) :]
     late, refs = refs[0], refs[1:]
-    held, out, arrived = refs[:5], refs[5], refs[6]
+    held, out, arrived = refs[:6], refs[6], refs[7]
     copies = [
         pltpu.make_async_copy(source, target, arrived.at[at])
         for at, (source, target) in enumerate(zip(inputs, held))
@@ -480,8 +480,7 @@
     reach = min(3, lax.axis_size("ctx") // 2)
     wide = jax.ShapeDtypeStruct((rows, features), F32)
     narrow = jax.ShapeDtypeStruct((rows, features), BF16)
-    inputs = (queries[0], key_rows[0], value_rows[0], update_gate[0], out_grad[0])
-    gain = norm_gain[None]
+    inputs = (queries[0], key_rows[0], value_rows[0], update_gate[0], out_grad[0], norm_gain[None])
 
     arrived = [passed_along(inputs[at], "ctx", by) for at, by in ((1, 1), (2, 1), (0, -1))]
 
@@ -492,7 +491,7 @@
     shapes = [(rows, rows)] * (len(plan) - 2) + [(rows, cut), (rows - cut, rows), (16, rows)]
     outs = [jax.ShapeDtypeStruct((count * heads, rows), F32) for count in (levels, rows)]
     outs += [jax.ShapeDtypeStruct(shape, F32) for shape in shapes]
-    outs += [narrow] * len(inputs) + [wide]
+    outs += [jax.ShapeDtypeStruct(array.shape, array.dtype) for array in inputs] + [wide]
     table, near, *found = on_device(
         partial(first_kernel, plan, cut, heads, scaling),
         outs,
@@ -502,7 +501,7 @@
         scratch=[pltpu.SemaphoreType.DMA((len(inputs),))],
     )
     masks, flipped = found[: reach + 1], found[reach + 1 : 2 * reach + 2]
-    sender_mask, late, query, key, value, gate, grad, attention = found[2 * reach + 2 :]
+    sender_mask, late, query, key, value, gate, grad, gain, attention = found[2 * reach + 2 :]
 
     later_queries = [query, arrived[2]]
     keys, values = [key, arrived[0]], [value, arrived[1]]

time: 50.6 us -> 50.1 us (level)
  local copies, waits for them, and re-layouts: 1.31 us -> 0.64 us
    unnamed x6 -> x4, local copies, waits for them, and re-layouts: 1.31 us -> 0.64 us
  transfers between devices with their start and end apart: 14 -> 14, of which waited for: 9 -> 7; matrix products, arithmetic and copies ran while one was open for 0% -> 0% of each run, Pallas kernels for 20% -> 20%
where the time goes in v18:
time: 50.1 us; the launch traced here: 49.8 us
  starting transfers between devices  22 us (44%)
  waiting for transfers between devices  15.1 us (30%)
  Pallas kernels  11.2 us (22%)
  between operations  0.84 us (2%)
  local copies, waits for them, and re-layouts  0.64 us (1%)
    ppermute x8, starting transfers between devices, passed_along(): lax.ppermute(array, axis, [(i, i + by) for i in range(first, last + 1)])  14.9 us
    ppermute x8, waiting for transfers between devices, passed_along(): lax.ppermute(array, axis, [(i, i + by) for i in range(first, last + 1)])  12.3 us
    pallas_call x11, Pallas kernels, on_device(): pl.pallas_call(body, out_shape=outs, in_specs=[pl.BlockSpec(memory_space=...  11.2 us
    ppermute x6, starting transfers between devices, exchanged(): lax.ppermute(array, axis, [(i, i ^ distance) for i in range(size)])  7.12 us
    ppermute x6, waiting for transfers between devices, exchanged(): lax.ppermute(array, axis, [(i, i ^ distance) for i in range(size)])  2.78 us
  transfers between devices with their start and end apart: 14, of which 7 were waited for; matrix products, arithmetic and copies ran while one was open for 0% of the time, Pallas kernels for 20%

profile of v18, /device:TPU:0, one launch (start us, length us, event | category | flops | bytes accessed | tf_op | source)
XLA Modules:
  0.0 49.8 jit_solution(17985753967397517397)
XLA Ops:
  0.6 4.9 %collective-permute-start.1 = (bf16[128,1024]{1,0:T(8,128)(2,1)}, bf16[128,1024]{1,0:T(8,128)(2,1)S(1)}, u32[]{:S(2)}, u32[]{:S(2)}) collective-permute-start(bf16[128,1024]{1,0:T(8,128)(2,1)} %bitcast.13), channel_id=1, source_target_pairs={{0,4},{4,8},{8,12},{1,5},{5,9},{9,13},{2,6},{6,10},{10,14},{3,7},{... | collective-permute-start | bytes 786440 | tf_op jit(solution)/shard_map/ppermute | solution.py:19
  5.6 0.0 copy-start
  5.6 3.5 %collective-permute-start.3 = (bf16[128,1024]{1,0:T(8,128)(2,1)}, bf16[128,1024]{1,0:T(8,128)(2,1)S(1)}, u32[]{:S(2)}, u32[]{:S(2)}) collective-permute-start(bf16[128,1024]{1,0:T(8,128)(2,1)} %bitcast.15), channel_id=1, source_target_pairs={{0,4},{4,8},{8,12},{1,5},{5,9},{9,13},{2,6},{6,10},{10,14},{3,7},{... | collective-permute-start | bytes 786440 | tf_op jit(solution)/shard_map/ppermute | solution.py:19
  9.1 1.3 %collective-permute-start = (bf16[128,1024]{1,0:T(8,128)(2,1)}, bf16[128,1024]{1,0:T(8,128)(2,1)S(1)}, u32[]{:S(2)}, u32[]{:S(2)}) collective-permute-start(bf16[128,1024]{1,0:T(8,128)(2,1)} %bitcast.11), channel_id=1, source_target_pairs={{4,0},{8,4},{12,8},{5,1},{9,5},{13,9},{6,2},{10,6},{14,10},{7,3},{... | collective-permute-start | bytes 786440 | tf_op jit(solution)/shard_map/ppermute | solution.py:19
  10.4 2.2 %collective-permute-done.1.refs_4_.refs_8_.refs_5_ = bf16[128,1024]{1,0:T(8,128)(2,1)S(1)} collective-permute-done((bf16[128,1024]{1,0:T(8,128)(2,1)}, bf16[128,1024]{1,0:T(8,128)(2,1)S(1)}, u32[]{:S(2)}, u32[]{:S(2)}) %collective-permute-start.1) | collective-permute-done | bytes 262176 | tf_op jit(solution)/shard_map/ppermute | solution.py:19
  12.6 0.7 %collective-permute-start.2 = (bf16[128,1024]{1,0:T(8,128)(2,1)S(1)}, bf16[128,1024]{1,0:T(8,128)(2,1)S(1)}, u32[]{:S(2)}, u32[]{:S(2)}) collective-permute-start(bf16[128,1024]{1,0:T(8,128)(2,1)S(1)} %collective-permute-done.1.refs_4_.refs_8_.refs_5_), channel_id=1, source_target_pairs={{4,8},{8,12},{5,9},{9,13},{6,10},{10,14},{7,11},{11,15},{20,24},{2... | collective-permute-start | bytes 786440 | tf_op jit(solution)/shard_map/ppermute | solution.py:19
  13.3 3.8 %collective-permute-done.3.refs_5_.refs_11_.refs_6_ = bf16[128,1024]{1,0:T(8,128)(2,1)S(1)} collective-permute-done((bf16[128,1024]{1,0:T(8,128)(2,1)}, bf16[128,1024]{1,0:T(8,128)(2,1)S(1)}, u32[]{:S(2)}, u32[]{:S(2)}) %collective-permute-start.3) | collective-permute-done | bytes 262176 | tf_op jit(solution)/shard_map/ppermute | solution.py:19
  17.1 0.7 %collective-permute-start.4 = (bf16[128,1024]{1,0:T(8,128)(2,1)S(1)}, bf16[128,1024]{1,0:T(8,128)(2,1)S(1)}, u32[]{:S(2)}, u32[]{:S(2)}) collective-permute-start(bf16[128,1024]{1,0:T(8,128)(2,1)S(1)} %collective-permute-done.3.refs_5_.refs_11_.refs_6_), channel_id=1, source_target_pairs={{4,8},{8,12},{5,9},{9,13},{6,10},{10,14},{7,11},{11,15},{20,24},{2... | collective-permute-start | bytes 786440 | tf_op jit(solution)/shard_map/ppermute | solution.py:19
  17.7 1.0 %collective-permute-done.refs_7_.refs_2_.refs_3_ = bf16[128,1024]{1,0:T(8,128)(2,1)S(1)} collective-permute-done((bf16[128,1024]{1,0:T(8,128)(2,1)}, bf16[128,1024]{1,0:T(8,128)(2,1)S(1)}, u32[]{:S(2)}, u32[]{:S(2)}) %collective-permute-start) | collective-permute-done | bytes 262176 | tf_op jit(solution)/shard_map/ppermute | solution.py:19
  18.7 1.3 %collective-permute-start.6 = (bf16[128,1024]{1,0:T(8,128)(2,1)S(1)}, bf16[128,1024]{1,0:T(8,128)(2,1)S(1)}, u32[]{:S(2)}, u32[]{:S(2)}) collective-permute-start(bf16[128,1024]{1,0:T(8,128)(2,1)S(1)} %collective-permute-done.refs_7_.refs_2_.refs_3_), channel_id=1, source_target_pairs={{4,0},{8,4},{5,1},{9,5},{6,2},{10,6},{7,3},{11,7},{20,16},{24,20},... | collective-permute-start | bytes 786440 | tf_op jit(solution)/shard_map/ppermute | solution.py:19
  20.0 0.0 copy-start.1
  20.0 0.0 copy-done
  20.0 0.6 %copy-done.1 = s32[1,4]{1,0:T(1,128)S(1)} copy-done((s32[1,4]{1,0:T(1,128)S(1)}, s32[1,4]{1,0:T(1,128)}, u32[]{:S(2)}) %copy-start.1) | copy-done | bytes 40
  20.6 2.5 %shard_map.127 = (f32[64,128]{1,0:T(8,128)S(1)}, f32[1024,128]{1,0:T(8,128)S(1)}, f32[128,128]{1,0:T(8,128)S(1)}, f32[128,128]{1,0:T(8,128)S(1)}, f32[128,128]{1...) custom-call(s32[1,4]{1,0:T(1,128)S(1)} %copy-done.1, ...), custom_call_target="tpu_custom_call" | custom-call | flops 1000000 | bytes 100000 | tf_op jit(solution)/shard_map/pallas_call | solution.py:435
  23.1 0.6 %shard_map.128.refs_5_.refs_2_ = f32[128,1024]{1,0:T(8,128)S(1)} custom-call(f32[64,128]{1,0:T(8,128)S(1)} %get-tuple-element.48.refs_0_, f32[1024,128]{1,0:T(8,128)S(1)} %get-tuple-element.50.refs_1_, f32[128,128]{1,0:T(8,128)S(1)} %get-tuple-element.53.refs_2_.refs_3_, bf16[128,1024]{1,0:T(8,128)(2,1)S(1)} %get-tuple-element.52.refs_3_.refs_5_.refs_2_, ...), custom_call_target="tpu_custom_call" | custom-call | flops 1000000 | bytes 100000 | tf_op jit(solution)/shard_map/pallas_call | solution.py:435
  23.7 0.0 collective-permute-done.2.refs_4_.refs_9_
  23.7 0.3 shard_map.129.refs_0_
  24.0 0.0 collective-permute-done.4.refs_1_.refs_12_
  24.0 0.6 %shard_map.130 = (f32[128,1024]{1,0:T(8,128)S(1)}, bf16[128,1024]{1,0:T(8,128)(2,1)S(1)}, f32[1,1024]{1,0:T(1,128)S(1)}) custom-call(bf16[1024,128]{1,0:T(8,128)(2,1)S(1)} %shard_map.129.refs_0_, bf16[128,1024]{1,0:T(8,128)(2,1)S(1)} %collective-permute-done.4.refs_1_.refs_12_, f32[128,1024]{1,0:T(8,128)S(1)} %shard_map.128.refs_5_.refs_2_, ...), custom_call_target="tpu_custom_call" | custom-call | flops 1000000 | bytes 100000 | tf_op jit(solution)/shard_map/pallas_call | solution.py:435
  24.7 1.3 %collective-permute-start.5 = (bf16[128,1024]{1,0:T(8,128)(2,1)S(1)}, bf16[128,1024]{1,0:T(8,128)(2,1)S(1)}, u32[]{:S(2)}, u32[]{:S(2)}) collective-permute-start(bf16[128,1024]{1,0:T(8,128)(2,1)S(1)} %get-tuple-element.58.refs_6_.refs_3_), channel_id=1, source_target_pairs={{4,0},{8,4},{12,8},{5,1},{9,5},{13,9},{6,2},{10,6},{14,10},{7,3},{... | collective-permute-start | bytes 786440 | tf_op jit(solution)/shard_map/ppermute | solution.py:19
  26.0 4.3 %collective-permute-done.6.refs_14_.refs_2_.refs_3_ = bf16[128,1024]{1,0:T(8,128)(2,1)S(1)} collective-permute-done((bf16[128,1024]{1,0:T(8,128)(2,1)S(1)}, bf16[128,1024]{1,0:T(8,128)(2,1)S(1)}, u32[]{:S(2)}, u32[]{:S(2)}) %collective-permute-start.6) | collective-permute-done | bytes 262176 | tf_op jit(solution)/shard_map/ppermute | solution.py:19
  30.3 1.7 %shard_map.131 = (bf16[128,1024]{1,0:T(8,128)(2,1)S(1)}, f32[16,128]{1,0:T(8,128)S(1)}) custom-call(f32[64,128]{1,0:T(8,128)S(1)} %get-tuple-element.48.refs_0_, f32[1024,128]{1,0:T(8,128)S(1)} %get-tuple-element.50.refs_1_, f32[128,128]{1,0:T(8,128)S(1)} %get-tuple-element.62.refs_2_, f32[128,128]{1,0:T(8,128)S(1)} %get-tuple-element.53.refs_2_.refs_3_, ...), custom_call_target="tpu_custom_call" | custom-call | flops 1000000 | bytes 100000 | tf_op jit(solution)/shard_map/pallas_call | solution.py:435
  32.0 0.1 collective-permute-start.7
  32.1 1.6 %collective-permute-start.8 = (f32[16,128]{1,0:T(8,128)S(1)}, f32[16,128]{1,0:T(8,128)S(1)}, u32[]{:S(2)}, u32[]{:S(2)}) collective-permute-start(f32[16,128]{1,0:T(8,128)S(1)} %get-tuple-element.80), channel_id=1, source_target_pairs={{0,2},{1,3},{2,0},{3,1},{4,6},{5,7},{6,4},{7,5},{8,10},{9,11},{10,... | collective-permute-start | bytes 24584 | tf_op jit(solution)/shard_map/ppermute | solution.py:464
  33.6 0.3 collective-permute-start.9
  34.0 0.0 collective-permute-done.7.refs_6_
  34.0 1.9 %collective-permute-done.8 = f32[16,128]{1,0:T(8,128)S(1)} collective-permute-done((f32[16,128]{1,0:T(8,128)S(1)}, f32[16,128]{1,0:T(8,128)S(1)}, u32[]{:S(2)}, u32[]{:S(2)}) %collective-permute-start.8) | collective-permute-done | bytes 8224 | tf_op jit(solution)/shard_map/ppermute | solution.py:464
  35.8 0.9 %collective-permute-done.9 = f32[16,128]{1,0:T(8,128)S(1)} collective-permute-done((f32[16,128]{1,0:T(8,128)S(1)}, f32[16,128]{1,0:T(8,128)S(1)}, u32[]{:S(2)}, u32[]{:S(2)}) %collective-permute-start.9) | collective-permute-done | bytes 8224 | tf_op jit(solution)/shard_map/ppermute | solution.py:464
  36.7 1.0 %collective-permute-done.5.refs_3_.refs_4_ = bf16[128,1024]{1,0:T(8,128)(2,1)S(1)} collective-permute-done((bf16[128,1024]{1,0:T(8,128)(2,1)S(1)}, bf16[128,1024]{1,0:T(8,128)(2,1)S(1)}, u32[]{:S(2)}, u32[]{:S(2)}) %collective-permute-start.5) | collective-permute-done | bytes 262176 | tf_op jit(solution)/shard_map/ppermute | solution.py:19
  37.7 0.6 %shard_map.135 = bf16[96,1024]{1,0:T(8,128)(2,1)S(1)} custom-call(f32[64,128]{1,0:T(8,128)S(1)} %get-tuple-element.48.refs_0_, f32[32,128]{1,0:T(8,128)S(1)} %get-tuple-element.75.refs_1_, f32[16,128]{1,0:T(8,128)S(1)} %get-tuple-element.74.refs_2_, bf16[128,1024]{1,0:T(8,128)(2,1)S(1)} %collective-permute-done.refs_7_.refs_2_.refs_3_, ...), custom_call_target="tpu_custom_call" | custom-call | flops 1000000 | bytes 100000 | tf_op jit(solution)/shard_map/pallas_call | solution.py:435
  38.3 1.3 %collective-permute-start.10 = (bf16[96,1024]{1,0:T(8,128)(2,1)S(1)}, bf16[96,1024]{1,0:T(8,128)(2,1)S(1)}, u32[]{:S(2)}, u32[]{:S(2)}) collective-permute-start(bf16[96,1024]{1,0:T(8,128)(2,1)S(1)} %shard_map.135), channel_id=1, source_target_pairs={{4,0},{8,4},{5,1},{9,5},{6,2},{10,6},{7,3},{11,7},{20,16},{24,20},... | collective-permute-start | bytes 589832 | tf_op jit(solution)/shard_map/ppermute | solution.py:19
  39.7 3.8 %collective-permute-start.11 = (f32[16,128]{1,0:T(8,128)S(1)}, f32[16,128]{1,0:T(8,128)S(1)}, u32[]{:S(2)}, u32[]{:S(2)}) collective-permute-start(f32[16,128]{1,0:T(8,128)S(1)} %add_add_fusion.refs_3_), channel_id=1, source_target_pairs={{0,12},{4,8},{8,4},{12,0},{1,13},{5,9},{9,5},{13,1},{2,14},{6,10},... | collective-permute-start | bytes 24584 | tf_op jit(solution)/shard_map/ppermute | solution.py:464
  43.5 0.9 %collective-permute-start.12 = (f32[16,128]{1,0:T(8,128)S(1)}, f32[16,128]{1,0:T(8,128)S(1)}, u32[]{:S(2)}, u32[]{:S(2)}) collective-permute-start(f32[16,128]{1,0:T(8,128)S(1)} %add_add_fusion.refs_3_), channel_id=1, source_target_pairs={{0,8},{4,12},{8,0},{12,4},{1,9},{5,13},{9,1},{13,5},{2,10},{6,14},... | collective-permute-start | bytes 24584 | tf_op jit(solution)/shard_map/ppermute | solution.py:464
  44.4 0.5 collective-permute-start.13
  44.9 0.9 %shard_map.132 = (f32[128,1024]{1,0:T(8,128)S(1)}, f32[128,1024]{1,0:T(8,128)S(1)}) custom-call(f32[64,128]{1,0:T(8,128)S(1)} %get-tuple-element.48.refs_0_, f32[128,128]{1,0:T(8,128)S(1)} %get-tuple-element.61.refs_1_, bf16[128,1024]{1,0:T(8,128)(2,1)S(1)} %get-tuple-element.52.refs_3_.refs_5_.refs_2_, ...), custom_call_target="tpu_custom_call" | custom-call | flops 1000000 | bytes 100000 | tf_op jit(solution)/shard_map/pallas_call | solution.py:435
  45.7 1.6 %shard_map.133 = (bf16[128,1024]{1,0:T(8,128)(2,1)}, bf16[128,1024]{1,0:T(8,128)(2,1)}, f32[128,1024]{1,0:T(8,128)S(1)}, f32[128,1024]{1,0:T(8,128)S(1)}) custom-call(f32[64,128]{1,0:T(8,128)S(1)} %get-tuple-element.48.refs_0_, f32[128,128]{1,0:T(8,128)S(1)} %get-tuple-element.49.refs_1_, bf16[128,1024]{1,0:T(8,128)(2,1)S(1)} %collective-permute-done.refs_7_.refs_2_.refs_3_, ...), custom_call_target="tpu_custom_call" | custom-call | flops 1000000 | bytes 100000 | tf_op jit(solution)/shard_map/pallas_call | solution.py:435
  47.4 0.4 shard_map.134
  47.8 0.0 collective-permute-done.10.refs_4_
  47.8 1.3 %shard_map.136 = (bf16[128,1024]{1,0:T(8,128)(2,1)}, bf16[128,1024]{1,0:T(8,128)(2,1)}) custom-call(bf16[1024,96]{1,0:T(8,128)(2,1)S(1)} %get-tuple-element.72.refs_0_, f32[1024,96]{1,0:T(8,128)S(1)} %get-tuple-element.73.refs_1_, f32[16,128]{1,0:T(8,128)S(1)} %get-tuple-element.74.refs_2_, ...), custom_call_target="tpu_custom_call" | custom-call | flops 1000000 | bytes 100000 | tf_op jit(solution)/shard_map/pallas_call | solution.py:435
  49.1 0.0 collective-permute-done.11.refs_0_
  49.1 0.0 collective-permute-done.12.refs_1_
  49.2 0.0 collective-permute-done.13.refs_2_
  49.2 0.6 %shard_map.137 = (f32[8,128]{1,0:T(8,128)}, f32[8,8]{1,0:T(8,128)}) custom-call(f32[16,128]{1,0:T(8,128)S(1)} %collective-permute-done.11.refs_0_, f32[16,128]{1,0:T(8,128)S(1)} %collective-permute-done.12.refs_1_, f32[16,128]{1,0:T(8,128)S(1)} %collective-permute-done.13.refs_2_, f32[16,128]{1,0:T(8,128)S(1)} %add_add_fusion.refs_3_), custom_call_target="tpu_custom_call" | custom-call | flops 1000000 | bytes 100000 | tf_op jit(solution)/shard_map/pallas_call | solution.py:435
  (1 shorter events, 0.0 us)
Async XLA Ops:
  0.6 11.9 %collective-permute-start.1 = (bf16[128,1024]{1,0:T(8,128)(2,1)}, bf16[128,1024]{1,0:T(8,128)(2,1)S(1)}, u32[]{:S(2)}, u32[]{:S(2)}) collective-permute-start(bf16[128,1024]{1,0:T(8,128)(2,1)} %bitcast.13), channel_id=1, source_target_pairs={{0,4},{4,8},{8,12},{1,5},{5,9},{9,13},{2,6},{6,10},{10,14},{3,7},{... | collective-permute-start | bytes 786440 | tf_op jit(solution)/shard_map/ppermute | solution.py:19
  5.6 14.4 %copy-start = (f32[8,8]{1,0:T(8,128)S(1)}, f32[8,8]{1,0:T(8,128)}, u32[]{:S(2)}) copy-start(f32[8,8]{1,0:T(8,128)} %refs_1_.1) | copy-start | bytes 772
  5.6 11.5 %collective-permute-start.3 = (bf16[128,1024]{1,0:T(8,128)(2,1)}, bf16[128,1024]{1,0:T(8,128)(2,1)S(1)}, u32[]{:S(2)}, u32[]{:S(2)}) collective-permute-start(bf16[128,1024]{1,0:T(8,128)(2,1)} %bitcast.15), channel_id=1, source_target_pairs={{0,4},{4,8},{8,12},{1,5},{5,9},{9,13},{2,6},{6,10},{10,14},{3,7},{... | collective-permute-start | bytes 786440 | tf_op jit(solution)/shard_map/ppermute | solution.py:19
  9.1 9.6 %collective-permute-start = (bf16[128,1024]{1,0:T(8,128)(2,1)}, bf16[128,1024]{1,0:T(8,128)(2,1)S(1)}, u32[]{:S(2)}, u32[]{:S(2)}) collective-permute-start(bf16[128,1024]{1,0:T(8,128)(2,1)} %bitcast.11), channel_id=1, source_target_pairs={{4,0},{8,4},{12,8},{5,1},{9,5},{13,9},{6,2},{10,6},{14,10},{7,3},{... | collective-permute-start | bytes 786440 | tf_op jit(solution)/shard_map/ppermute | solution.py:19
  12.6 11.1 %collective-permute-start.2 = (bf16[128,1024]{1,0:T(8,128)(2,1)S(1)}, bf16[128,1024]{1,0:T(8,128)(2,1)S(1)}, u32[]{:S(2)}, u32[]{:S(2)}) collective-permute-start(bf16[128,1024]{1,0:T(8,128)(2,1)S(1)} %collective-permute-done.1.refs_4_.refs_8_.refs_5_), channel_id=1, source_target_pairs={{4,8},{8,12},{5,9},{9,13},{6,10},{10,14},{7,11},{11,15},{20,24},{2... | collective-permute-start | bytes 786440 | tf_op jit(solution)/shard_map/ppermute | solution.py:19
  17.1 7.0 %collective-permute-start.4 = (bf16[128,1024]{1,0:T(8,128)(2,1)S(1)}, bf16[128,1024]{1,0:T(8,128)(2,1)S(1)}, u32[]{:S(2)}, u32[]{:S(2)}) collective-permute-start(bf16[128,1024]{1,0:T(8,128)(2,1)S(1)} %collective-permute-done.3.refs_5_.refs_11_.refs_6_), channel_id=1, source_target_pairs={{4,8},{8,12},{5,9},{9,13},{6,10},{10,14},{7,11},{11,15},{20,24},{2... | collective-permute-start | bytes 786440 | tf_op jit(solution)/shard_map/ppermute | solution.py:19
  18.7 11.7 %collective-permute-start.6 = (bf16[128,1024]{1,0:T(8,128)(2,1)S(1)}, bf16[128,1024]{1,0:T(8,128)(2,1)S(1)}, u32[]{:S(2)}, u32[]{:S(2)}) collective-permute-start(bf16[128,1024]{1,0:T(8,128)(2,1)S(1)} %collective-permute-done.refs_7_.refs_2_.refs_3_), channel_id=1, source_target_pairs={{4,0},{8,4},{5,1},{9,5},{6,2},{10,6},{7,3},{11,7},{20,16},{24,20},... | collective-permute-start | bytes 786440 | tf_op jit(solution)/shard_map/ppermute | solution.py:19
  20.0 0.7 %copy-start.1 = (s32[1,4]{1,0:T(1,128)S(1)}, s32[1,4]{1,0:T(1,128)}, u32[]{:S(2)}) copy-start(s32[1,4]{1,0:T(1,128)} %refs_0_.1) | copy-start | bytes 52
  24.7 13.1 %collective-permute-start.5 = (bf16[128,1024]{1,0:T(8,128)(2,1)S(1)}, bf16[128,1024]{1,0:T(8,128)(2,1)S(1)}, u32[]{:S(2)}, u32[]{:S(2)}) collective-permute-start(bf16[128,1024]{1,0:T(8,128)(2,1)S(1)} %get-tuple-element.58.refs_6_.refs_3_), channel_id=1, source_target_pairs={{4,0},{8,4},{12,8},{5,1},{9,5},{13,9},{6,2},{10,6},{14,10},{7,3},{... | collective-permute-start | bytes 786440 | tf_op jit(solution)/shard_map/ppermute | solution.py:19
  32.0 1.9 %collective-permute-start.7 = (f32[16,128]{1,0:T(8,128)S(1)}, f32[16,128]{1,0:T(8,128)S(1)}, u32[]{:S(2)}, u32[]{:S(2)}) collective-permute-start(f32[16,128]{1,0:T(8,128)S(1)} %get-tuple-element.80), channel_id=1, source_target_pairs={{0,1},{1,0},{2,3},{3,2},{4,5},{5,4},{6,7},{7,6},{8,9},{9,8},{10,11... | collective-permute-start | bytes 24584 | tf_op jit(solution)/shard_map/ppermute | solution.py:464
  32.1 3.7 %collective-permute-start.8 = (f32[16,128]{1,0:T(8,128)S(1)}, f32[16,128]{1,0:T(8,128)S(1)}, u32[]{:S(2)}, u32[]{:S(2)}) collective-permute-start(f32[16,128]{1,0:T(8,128)S(1)} %get-tuple-element.80), channel_id=1, source_target_pairs={{0,2},{1,3},{2,0},{3,1},{4,6},{5,7},{6,4},{7,5},{8,10},{9,11},{10,... | collective-permute-start | bytes 24584 | tf_op jit(solution)/shard_map/ppermute | solution.py:464
  33.6 3.1 %collective-permute-start.9 = (f32[16,128]{1,0:T(8,128)S(1)}, f32[16,128]{1,0:T(8,128)S(1)}, u32[]{:S(2)}, u32[]{:S(2)}) collective-permute-start(f32[16,128]{1,0:T(8,128)S(1)} %get-tuple-element.80), channel_id=1, source_target_pairs={{0,3},{1,2},{2,1},{3,0},{4,7},{5,6},{6,5},{7,4},{8,11},{9,10},{10,... | collective-permute-start | bytes 24584 | tf_op jit(solution)/shard_map/ppermute | solution.py:464
  38.3 9.5 %collective-permute-start.10 = (bf16[96,1024]{1,0:T(8,128)(2,1)S(1)}, bf16[96,1024]{1,0:T(8,128)(2,1)S(1)}, u32[]{:S(2)}, u32[]{:S(2)}) collective-permute-start(bf16[96,1024]{1,0:T(8,128)(2,1)S(1)} %shard_map.135), channel_id=1, source_target_pairs={{4,0},{8,4},{5,1},{9,5},{6,2},{10,6},{7,3},{11,7},{20,16},{24,20},... | collective-permute-start | bytes 589832 | tf_op jit(solution)/shard_map/ppermute | solution.py:19
  39.7 9.5 %collective-permute-start.11 = (f32[16,128]{1,0:T(8,128)S(1)}, f32[16,128]{1,0:T(8,128)S(1)}, u32[]{:S(2)}, u32[]{:S(2)}) collective-permute-start(f32[16,128]{1,0:T(8,128)S(1)} %add_add_fusion.refs_3_), channel_id=1, source_target_pairs={{0,12},{4,8},{8,4},{12,0},{1,13},{5,9},{9,5},{13,1},{2,14},{6,10},... | collective-permute-start | bytes 24584 | tf_op jit(solution)/shard_map/ppermute | solution.py:464
  43.5 5.7 %collective-permute-start.12 = (f32[16,128]{1,0:T(8,128)S(1)}, f32[16,128]{1,0:T(8,128)S(1)}, u32[]{:S(2)}, u32[]{:S(2)}) collective-permute-start(f32[16,128]{1,0:T(8,128)S(1)} %add_add_fusion.refs_3_), channel_id=1, source_target_pairs={{0,8},{4,12},{8,0},{12,4},{1,9},{5,13},{9,1},{13,5},{2,10},{6,14},... | collective-permute-start | bytes 24584 | tf_op jit(solution)/shard_map/ppermute | solution.py:464
  44.4 4.8 %collective-permute-start.13 = (f32[16,128]{1,0:T(8,128)S(1)}, f32[16,128]{1,0:T(8,128)S(1)}, u32[]{:S(2)}, u32[]{:S(2)}) collective-permute-start(f32[16,128]{1,0:T(8,128)S(1)} %add_add_fusion.refs_3_), channel_id=1, source_target_pairs={{0,4},{4,0},{8,12},{12,8},{1,5},{5,1},{9,13},{13,9},{2,6},{6,2},{1... | collective-permute-start | bytes 24584 | tf_op jit(solution)/shard_map/ppermute | solution.py:464

commit v19 on v18

--- a/solution.py
+++ b/solution.py
@@ -549,7 +549,11 @@
         partial(next_key_kernel, 0, heads, scaling),
         [wide] * 2,
         key_operands(0),
-        ahead=pieces[1:2],
+    )
+    far_tables = on_device(
+        partial(slopes_kernel, reach, heads, scaling),
+        [jax.ShapeDtypeStruct((heads * rows, cut), kind) for kind in (BF16, F32)],
+        (table, flipped[reach], later_queries[reach], key),
     )
     for hops in range(1, reach):
         arrived, *pieces = lax.optimization_barrier((later_grads[hops], *pieces))
@@ -558,6 +562,7 @@
                 partial(message_kernel, reach, heads, scaling),
                 [jax.ShapeDtypeStruct((cut, features), BF16)],
                 (table, sender_mask, late, later_queries[hops], arrived, keys[1], values[1]),
+                ahead=[key_grads[0], far_tables[0]],
             )
         later_grads.append(passed_along(arrived, "ctx", -1, hops + 1))
         if hops == 1:
@@ -574,12 +579,6 @@
                 [wide] * 2,
                 (*key_operands(hops), *key_grads),
             )
-    far_tables = on_device(
-        partial(slopes_kernel, reach, heads, scaling),
-        [jax.ShapeDtypeStruct((heads * rows, cut), kind) for kind in (BF16, F32)],
-        (table, flipped[reach], later_queries[reach], key),
-        ahead=key_grads[:1],
-    )
     for axis, distances in rounds_of(("ctx",)):
         pieces = exchanged(added_up(pieces), axis, distances)
     key_grad, value_grad = on_device(
@@ -593,7 +592,7 @@
     gain_grad, bias_grad = on_device(
         sum_kernel,
         [jax.ShapeDtypeStruct((8, lanes), F32), jax.ShapeDtypeStruct((levels, heads), F32)],
-        pieces[::-1],
+        pieces,
     )
     return (
         query_grad[None],

time: 50.1 us -> 49.1 us (0.980)
  waiting for transfers between devices: 15.1 us -> 14.1 us
    ppermute x6, waiting for transfers between devices: 2.78 us -> 0.67 us  [exchanged(): lax.ppermute(array, axis, [(i, i ^ distance) for i in range(size)])]
    ppermute x8, waiting for transfers between devices: 12.3 us -> 13.5 us  [passed_along(): lax.ppermute(array, axis, [(i, i + by) for i in range(first, last + 1)])]
  transfers between devices with their start and end apart: 14 -> 14, of which waited for: 7 -> 8; matrix products, arithmetic and copies ran while one was open for 0% -> 0% of each run, Pallas kernels for 20% -> 20%
where the time goes in v19:
time: 49.1 us; the launch traced here: 48.8 us
  starting transfers between devices  22 us (45%)
  waiting for transfers between devices  14.1 us (29%)
  Pallas kernels  11.1 us (23%)
  between operations  0.83 us (2%)
  local copies, waits for them, and re-layouts  0.64 us (1%)
    ppermute x8, starting transfers between devices, passed_along(): lax.ppermute(array, axis, [(i, i + by) for i in range(first, last + 1)])  14.9 us
    ppermute x8, waiting for transfers between devices, passed_along(): lax.ppermute(array, axis, [(i, i + by) for i in range(first, last + 1)])  13.5 us
    pallas_call x11, Pallas kernels, on_device(): pl.pallas_call(body, out_shape=outs, in_specs=[pl.BlockSpec(memory_space=...  11.1 us
    ppermute x6, starting transfers between devices, exchanged(): lax.ppermute(array, axis, [(i, i ^ distance) for i in range(size)])  7.1 us
  transfers between devices with their start and end apart: 14, of which 8 were waited for; matrix products, arithmetic and copies ran while one was open for 0% of the time, Pallas kernels for 20%

profile of v19, /device:TPU:0, one launch (start us, length us, event | category | flops | bytes accessed | tf_op | source)
XLA Modules:
  0.0 48.8 jit_solution(9382930424230437039)
XLA Ops:
  0.6 4.9 %collective-permute-start.1 = (bf16[128,1024]{1,0:T(8,128)(2,1)}, bf16[128,1024]{1,0:T(8,128)(2,1)S(1)}, u32[]{:S(2)}, u32[]{:S(2)}) collective-permute-start(bf16[128,1024]{1,0:T(8,128)(2,1)} %bitcast.13), channel_id=1, source_target_pairs={{0,4},{4,8},{8,12},{1,5},{5,9},{9,13},{2,6},{6,10},{10,14},{3,7},{... | collective-permute-start | bytes 786440 | tf_op jit(solution)/shard_map/ppermute | solution.py:19
  5.6 0.0 copy-start
  5.6 3.5 %collective-permute-start.3 = (bf16[128,1024]{1,0:T(8,128)(2,1)}, bf16[128,1024]{1,0:T(8,128)(2,1)S(1)}, u32[]{:S(2)}, u32[]{:S(2)}) collective-permute-start(bf16[128,1024]{1,0:T(8,128)(2,1)} %bitcast.15), channel_id=1, source_target_pairs={{0,4},{4,8},{8,12},{1,5},{5,9},{9,13},{2,6},{6,10},{10,14},{3,7},{... | collective-permute-start | bytes 786440 | tf_op jit(solution)/shard_map/ppermute | solution.py:19
  9.1 1.3 %collective-permute-start = (bf16[128,1024]{1,0:T(8,128)(2,1)}, bf16[128,1024]{1,0:T(8,128)(2,1)S(1)}, u32[]{:S(2)}, u32[]{:S(2)}) collective-permute-start(bf16[128,1024]{1,0:T(8,128)(2,1)} %bitcast.11), channel_id=1, source_target_pairs={{4,0},{8,4},{12,8},{5,1},{9,5},{13,9},{6,2},{10,6},{14,10},{7,3},{... | collective-permute-start | bytes 786440 | tf_op jit(solution)/shard_map/ppermute | solution.py:19
  10.4 2.2 %collective-permute-done.1.refs_4_.refs_8_.refs_5_ = bf16[128,1024]{1,0:T(8,128)(2,1)S(1)} collective-permute-done((bf16[128,1024]{1,0:T(8,128)(2,1)}, bf16[128,1024]{1,0:T(8,128)(2,1)S(1)}, u32[]{:S(2)}, u32[]{:S(2)}) %collective-permute-start.1) | collective-permute-done | bytes 262176 | tf_op jit(solution)/shard_map/ppermute | solution.py:19
  12.6 0.7 %collective-permute-start.2 = (bf16[128,1024]{1,0:T(8,128)(2,1)S(1)}, bf16[128,1024]{1,0:T(8,128)(2,1)S(1)}, u32[]{:S(2)}, u32[]{:S(2)}) collective-permute-start(bf16[128,1024]{1,0:T(8,128)(2,1)S(1)} %collective-permute-done.1.refs_4_.refs_8_.refs_5_), channel_id=1, source_target_pairs={{4,8},{8,12},{5,9},{9,13},{6,10},{10,14},{7,11},{11,15},{20,24},{2... | collective-permute-start | bytes 786440 | tf_op jit(solution)/shard_map/ppermute | solution.py:19
  13.3 3.8 %collective-permute-done.3.refs_5_.refs_11_.refs_6_ = bf16[128,1024]{1,0:T(8,128)(2,1)S(1)} collective-permute-done((bf16[128,1024]{1,0:T(8,128)(2,1)}, bf16[128,1024]{1,0:T(8,128)(2,1)S(1)}, u32[]{:S(2)}, u32[]{:S(2)}) %collective-permute-start.3) | collective-permute-done | bytes 262176 | tf_op jit(solution)/shard_map/ppermute | solution.py:19
  17.1 0.7 %collective-permute-start.4 = (bf16[128,1024]{1,0:T(8,128)(2,1)S(1)}, bf16[128,1024]{1,0:T(8,128)(2,1)S(1)}, u32[]{:S(2)}, u32[]{:S(2)}) collective-permute-start(bf16[128,1024]{1,0:T(8,128)(2,1)S(1)} %collective-permute-done.3.refs_5_.refs_11_.refs_6_), channel_id=1, source_target_pairs={{4,8},{8,12},{5,9},{9,13},{6,10},{10,14},{7,11},{11,15},{20,24},{2... | collective-permute-start | bytes 786440 | tf_op jit(solution)/shard_map/ppermute | solution.py:19
  17.7 1.0 %collective-permute-done.refs_7_.refs_2_.refs_3_ = bf16[128,1024]{1,0:T(8,128)(2,1)S(1)} collective-permute-done((bf16[128,1024]{1,0:T(8,128)(2,1)}, bf16[128,1024]{1,0:T(8,128)(2,1)S(1)}, u32[]{:S(2)}, u32[]{:S(2)}) %collective-permute-start) | collective-permute-done | bytes 262176 | tf_op jit(solution)/shard_map/ppermute | solution.py:19
  18.7 1.3 %collective-permute-start.6 = (bf16[128,1024]{1,0:T(8,128)(2,1)S(1)}, bf16[128,1024]{1,0:T(8,128)(2,1)S(1)}, u32[]{:S(2)}, u32[]{:S(2)}) collective-permute-start(bf16[128,1024]{1,0:T(8,128)(2,1)S(1)} %collective-permute-done.refs_7_.refs_2_.refs_3_), channel_id=1, source_target_pairs={{4,0},{8,4},{5,1},{9,5},{6,2},{10,6},{7,3},{11,7},{20,16},{24,20},... | collective-permute-start | bytes 786440 | tf_op jit(solution)/shard_map/ppermute | solution.py:19
  20.0 0.0 copy-start.1
  20.0 0.0 copy-done
  20.0 0.6 %copy-done.1 = s32[1,4]{1,0:T(1,128)S(1)} copy-done((s32[1,4]{1,0:T(1,128)S(1)}, s32[1,4]{1,0:T(1,128)}, u32[]{:S(2)}) %copy-start.1) | copy-done | bytes 40
  20.6 2.5 %shard_map.127 = (f32[64,128]{1,0:T(8,128)S(1)}, f32[1024,128]{1,0:T(8,128)S(1)}, f32[128,128]{1,0:T(8,128)S(1)}, f32[128,128]{1,0:T(8,128)S(1)}, f32[128,128]{1...) custom-call(s32[1,4]{1,0:T(1,128)S(1)} %copy-done.1, ...), custom_call_target="tpu_custom_call" | custom-call | flops 1000000 | bytes 100000 | tf_op jit(solution)/shard_map/pallas_call | solution.py:435
  23.1 0.6 %shard_map.128.refs_5_.refs_2_ = f32[128,1024]{1,0:T(8,128)S(1)} custom-call(f32[64,128]{1,0:T(8,128)S(1)} %get-tuple-element.48.refs_0_, f32[1024,128]{1,0:T(8,128)S(1)} %get-tuple-element.50.refs_1_, f32[128,128]{1,0:T(8,128)S(1)} %get-tuple-element.53.refs_2_.refs_3_, bf16[128,1024]{1,0:T(8,128)(2,1)S(1)} %get-tuple-element.52.refs_3_.refs_2_.refs_5_, ...), custom_call_target="tpu_custom_call" | custom-call | flops 1000000 | bytes 100000 | tf_op jit(solution)/shard_map/pallas_call | solution.py:435
  23.7 0.0 collective-permute-done.2.refs_4_.refs_9_
  23.7 0.3 shard_map.129.refs_0_
  24.0 0.0 collective-permute-done.4.refs_1_.refs_12_
  24.0 0.6 %shard_map.130 = (f32[128,1024]{1,0:T(8,128)S(1)}, bf16[128,1024]{1,0:T(8,128)(2,1)S(1)}, f32[1,1024]{1,0:T(1,128)S(1)}) custom-call(bf16[1024,128]{1,0:T(8,128)(2,1)S(1)} %shard_map.129.refs_0_, bf16[128,1024]{1,0:T(8,128)(2,1)S(1)} %collective-permute-done.4.refs_1_.refs_12_, f32[128,1024]{1,0:T(8,128)S(1)} %shard_map.128.refs_5_.refs_2_, ...), custom_call_target="tpu_custom_call" | custom-call | flops 1000000 | bytes 100000 | tf_op jit(solution)/shard_map/pallas_call | solution.py:435
  24.7 1.3 %collective-permute-start.5 = (bf16[128,1024]{1,0:T(8,128)(2,1)S(1)}, bf16[128,1024]{1,0:T(8,128)(2,1)S(1)}, u32[]{:S(2)}, u32[]{:S(2)}) collective-permute-start(bf16[128,1024]{1,0:T(8,128)(2,1)S(1)} %get-tuple-element.58.refs_3_.refs_6_), channel_id=1, source_target_pairs={{4,0},{8,4},{12,8},{5,1},{9,5},{13,9},{6,2},{10,6},{14,10},{7,3},{... | collective-permute-start | bytes 786440 | tf_op jit(solution)/shard_map/ppermute | solution.py:19
  26.0 4.4 %collective-permute-done.6.refs_14_.refs_2_.refs_3_ = bf16[128,1024]{1,0:T(8,128)(2,1)S(1)} collective-permute-done((bf16[128,1024]{1,0:T(8,128)(2,1)S(1)}, bf16[128,1024]{1,0:T(8,128)(2,1)S(1)}, u32[]{:S(2)}, u32[]{:S(2)}) %collective-permute-start.6) | collective-permute-done | bytes 262176 | tf_op jit(solution)/shard_map/ppermute | solution.py:19
  30.3 1.7 %shard_map.132 = (bf16[128,1024]{1,0:T(8,128)(2,1)S(1)}, f32[16,128]{1,0:T(8,128)S(1)}) custom-call(f32[64,128]{1,0:T(8,128)S(1)} %get-tuple-element.48.refs_0_, f32[1024,128]{1,0:T(8,128)S(1)} %get-tuple-element.50.refs_1_, f32[128,128]{1,0:T(8,128)S(1)} %get-tuple-element.65.refs_2_, f32[128,128]{1,0:T(8,128)S(1)} %get-tuple-element.53.refs_2_.refs_3_, ...), custom_call_target="tpu_custom_call" | custom-call | flops 1000000 | bytes 100000 | tf_op jit(solution)/shard_map/pallas_call | solution.py:435
  32.0 0.1 collective-permute-start.9
  32.1 1.6 %collective-permute-start.8 = (f32[16,128]{1,0:T(8,128)S(1)}, f32[16,128]{1,0:T(8,128)S(1)}, u32[]{:S(2)}, u32[]{:S(2)}) collective-permute-start(f32[16,128]{1,0:T(8,128)S(1)} %get-tuple-element.80), channel_id=1, source_target_pairs={{0,2},{1,3},{2,0},{3,1},{4,6},{5,7},{6,4},{7,5},{8,10},{9,11},{10,... | collective-permute-start | bytes 24584 | tf_op jit(solution)/shard_map/ppermute | solution.py:464
  33.6 0.3 collective-permute-start.7
  33.9 0.9 %shard_map.131 = (f32[128,1024]{1,0:T(8,128)S(1)}, f32[128,1024]{1,0:T(8,128)S(1)}) custom-call(f32[64,128]{1,0:T(8,128)S(1)} %get-tuple-element.48.refs_0_, f32[128,128]{1,0:T(8,128)S(1)} %get-tuple-element.61.refs_1_, bf16[128,1024]{1,0:T(8,128)(2,1)S(1)} %get-tuple-element.52.refs_3_.refs_2_.refs_5_, ...), custom_call_target="tpu_custom_call" | custom-call | flops 1000000 | bytes 100000 | tf_op jit(solution)/shard_map/pallas_call | solution.py:435
  34.8 0.4 shard_map.134
  35.2 0.0 collective-permute-done.9
  35.2 0.5 %collective-permute-done.8 = f32[16,128]{1,0:T(8,128)S(1)} collective-permute-done((f32[16,128]{1,0:T(8,128)S(1)}, f32[16,128]{1,0:T(8,128)S(1)}, u32[]{:S(2)}, u32[]{:S(2)}) %collective-permute-start.8) | collective-permute-done | bytes 8224 | tf_op jit(solution)/shard_map/ppermute | solution.py:464
  35.8 0.0 collective-permute-done.7
  35.8 1.9 %collective-permute-done.5.refs_3_.refs_4_ = bf16[128,1024]{1,0:T(8,128)(2,1)S(1)} collective-permute-done((bf16[128,1024]{1,0:T(8,128)(2,1)S(1)}, bf16[128,1024]{1,0:T(8,128)(2,1)S(1)}, u32[]{:S(2)}, u32[]{:S(2)}) %collective-permute-start.5) | collective-permute-done | bytes 262176 | tf_op jit(solution)/shard_map/ppermute | solution.py:19
  37.7 0.6 %shard_map.135 = bf16[96,1024]{1,0:T(8,128)(2,1)S(1)} custom-call(f32[64,128]{1,0:T(8,128)S(1)} %get-tuple-element.48.refs_0_, f32[32,128]{1,0:T(8,128)S(1)} %get-tuple-element.73.refs_1_, f32[16,128]{1,0:T(8,128)S(1)} %get-tuple-element.72.refs_2_, bf16[128,1024]{1,0:T(8,128)(2,1)S(1)} %collective-permute-done.refs_7_.refs_2_.refs_3_, ...), custom_call_target="tpu_custom_call" | custom-call | flops 1000000 | bytes 100000 | tf_op jit(solution)/shard_map/pallas_call | solution.py:435
  38.3 1.3 %collective-permute-start.10 = (bf16[96,1024]{1,0:T(8,128)(2,1)S(1)}, bf16[96,1024]{1,0:T(8,128)(2,1)S(1)}, u32[]{:S(2)}, u32[]{:S(2)}) collective-permute-start(bf16[96,1024]{1,0:T(8,128)(2,1)S(1)} %shard_map.135), channel_id=1, source_target_pairs={{4,0},{8,4},{5,1},{9,5},{6,2},{10,6},{7,3},{11,7},{20,16},{24,20},... | collective-permute-start | bytes 589832 | tf_op jit(solution)/shard_map/ppermute | solution.py:19
  39.6 2.9 %collective-permute-start.13 = (f32[16,128]{1,0:T(8,128)S(1)}, f32[16,128]{1,0:T(8,128)S(1)}, u32[]{:S(2)}, u32[]{:S(2)}) collective-permute-start(f32[16,128]{1,0:T(8,128)S(1)} %add_add_fusion.refs_0_), channel_id=1, source_target_pairs={{0,12},{4,8},{8,4},{12,0},{1,13},{5,9},{9,5},{13,1},{2,14},{6,10},... | collective-permute-start | bytes 24584 | tf_op jit(solution)/shard_map/ppermute | solution.py:464
  42.6 1.8 %collective-permute-start.12 = (f32[16,128]{1,0:T(8,128)S(1)}, f32[16,128]{1,0:T(8,128)S(1)}, u32[]{:S(2)}, u32[]{:S(2)}) collective-permute-start(f32[16,128]{1,0:T(8,128)S(1)} %add_add_fusion.refs_0_), channel_id=1, source_target_pairs={{0,8},{4,12},{8,0},{12,4},{1,9},{5,13},{9,1},{13,5},{2,10},{6,14},... | collective-permute-start | bytes 24584 | tf_op jit(solution)/shard_map/ppermute | solution.py:464
  44.4 0.5 %collective-permute-start.11 = (f32[16,128]{1,0:T(8,128)S(1)}, f32[16,128]{1,0:T(8,128)S(1)}, u32[]{:S(2)}, u32[]{:S(2)}) collective-permute-start(f32[16,128]{1,0:T(8,128)S(1)} %add_add_fusion.refs_0_), channel_id=1, source_target_pairs={{0,4},{4,0},{8,12},{12,8},{1,5},{5,1},{9,13},{13,9},{2,6},{6,2},{1... | collective-permute-start | bytes 24584 | tf_op jit(solution)/shard_map/ppermute | solution.py:464
  44.8 1.6 %shard_map.133 = (bf16[128,1024]{1,0:T(8,128)(2,1)}, bf16[128,1024]{1,0:T(8,128)(2,1)}, f32[128,1024]{1,0:T(8,128)S(1)}, f32[128,1024]{1,0:T(8,128)S(1)}) custom-call(f32[64,128]{1,0:T(8,128)S(1)} %get-tuple-element.48.refs_0_, f32[128,128]{1,0:T(8,128)S(1)} %get-tuple-element.49.refs_1_, bf16[128,1024]{1,0:T(8,128)(2,1)S(1)} %collective-permute-done.refs_7_.refs_2_.refs_3_, ...), custom_call_target="tpu_custom_call" | custom-call | flops 1000000 | bytes 100000 | tf_op jit(solution)/shard_map/pallas_call | solution.py:435
  46.5 0.2 collective-permute-done.10.refs_4_
  46.7 1.3 %shard_map.136 = (bf16[128,1024]{1,0:T(8,128)(2,1)}, bf16[128,1024]{1,0:T(8,128)(2,1)}) custom-call(bf16[1024,96]{1,0:T(8,128)(2,1)S(1)} %get-tuple-element.70.refs_8_.refs_0_, f32[1024,96]{1,0:T(8,128)S(1)} %get-tuple-element.71.refs_1_, f32[16,128]{1,0:T(8,128)S(1)} %get-tuple-element.72.refs_2_, ...), custom_call_target="tpu_custom_call" | custom-call | flops 1000000 | bytes 100000 | tf_op jit(solution)/shard_map/pallas_call | solution.py:435
  48.0 0.0 collective-permute-done.13.refs_3_
  48.1 0.1 collective-permute-done.12.refs_2_
  48.2 0.0 collective-permute-done.11.refs_1_
  48.2 0.6 %shard_map.137 = (f32[8,128]{1,0:T(8,128)}, f32[8,8]{1,0:T(8,128)}) custom-call(f32[16,128]{1,0:T(8,128)S(1)} %add_add_fusion.refs_0_, f32[16,128]{1,0:T(8,128)S(1)} %collective-permute-done.11.refs_1_, f32[16,128]{1,0:T(8,128)S(1)} %collective-permute-done.12.refs_2_, f32[16,128]{1,0:T(8,128)S(1)} %collective-permute-done.13.refs_3_), custom_call_target="tpu_custom_call" | custom-call | flops 1000000 | bytes 100000 | tf_op jit(solution)/shard_map/pallas_call | solution.py:435
  (1 shorter events, 0.0 us)
Async XLA Ops:
  0.6 11.9 %collective-permute-start.1 = (bf16[128,1024]{1,0:T(8,128)(2,1)}, bf16[128,1024]{1,0:T(8,128)(2,1)S(1)}, u32[]{:S(2)}, u32[]{:S(2)}) collective-permute-start(bf16[128,1024]{1,0:T(8,128)(2,1)} %bitcast.13), channel_id=1, source_target_pairs={{0,4},{4,8},{8,12},{1,5},{5,9},{9,13},{2,6},{6,10},{10,14},{3,7},{... | collective-permute-start | bytes 786440 | tf_op jit(solution)/shard_map/ppermute | solution.py:19
  5.6 14.4 %copy-start = (f32[8,8]{1,0:T(8,128)S(1)}, f32[8,8]{1,0:T(8,128)}, u32[]{:S(2)}) copy-start(f32[8,8]{1,0:T(8,128)} %refs_1_.1) | copy-start | bytes 772
  5.6 11.5 %collective-permute-start.3 = (bf16[128,1024]{1,0:T(8,128)(2,1)}, bf16[128,1024]{1,0:T(8,128)(2,1)S(1)}, u32[]{:S(2)}, u32[]{:S(2)}) collective-permute-start(bf16[128,1024]{1,0:T(8,128)(2,1)} %bitcast.15), channel_id=1, source_target_pairs={{0,4},{4,8},{8,12},{1,5},{5,9},{9,13},{2,6},{6,10},{10,14},{3,7},{... | collective-permute-start | bytes 786440 | tf_op jit(solution)/shard_map/ppermute | solution.py:19
  9.1 9.6 %collective-permute-start = (bf16[128,1024]{1,0:T(8,128)(2,1)}, bf16[128,1024]{1,0:T(8,128)(2,1)S(1)}, u32[]{:S(2)}, u32[]{:S(2)}) collective-permute-start(bf16[128,1024]{1,0:T(8,128)(2,1)} %bitcast.11), channel_id=1, source_target_pairs={{4,0},{8,4},{12,8},{5,1},{9,5},{13,9},{6,2},{10,6},{14,10},{7,3},{... | collective-permute-start | bytes 786440 | tf_op jit(solution)/shard_map/ppermute | solution.py:19
  12.6 11.1 %collective-permute-start.2 = (bf16[128,1024]{1,0:T(8,128)(2,1)S(1)}, bf16[128,1024]{1,0:T(8,128)(2,1)S(1)}, u32[]{:S(2)}, u32[]{:S(2)}) collective-permute-start(bf16[128,1024]{1,0:T(8,128)(2,1)S(1)} %collective-permute-done.1.refs_4_.refs_8_.refs_5_), channel_id=1, source_target_pairs={{4,8},{8,12},{5,9},{9,13},{6,10},{10,14},{7,11},{11,15},{20,24},{2... | collective-permute-start | bytes 786440 | tf_op jit(solution)/shard_map/ppermute | solution.py:19
  17.1 7.0 %collective-permute-start.4 = (bf16[128,1024]{1,0:T(8,128)(2,1)S(1)}, bf16[128,1024]{1,0:T(8,128)(2,1)S(1)}, u32[]{:S(2)}, u32[]{:S(2)}) collective-permute-start(bf16[128,1024]{1,0:T(8,128)(2,1)S(1)} %collective-permute-done.3.refs_5_.refs_11_.refs_6_), channel_id=1, source_target_pairs={{4,8},{8,12},{5,9},{9,13},{6,10},{10,14},{7,11},{11,15},{20,24},{2... | collective-permute-start | bytes 786440 | tf_op jit(solution)/shard_map/ppermute | solution.py:19
  18.7 11.7 %collective-permute-start.6 = (bf16[128,1024]{1,0:T(8,128)(2,1)S(1)}, bf16[128,1024]{1,0:T(8,128)(2,1)S(1)}, u32[]{:S(2)}, u32[]{:S(2)}) collective-permute-start(bf16[128,1024]{1,0:T(8,128)(2,1)S(1)} %collective-permute-done.refs_7_.refs_2_.refs_3_), channel_id=1, source_target_pairs={{4,0},{8,4},{5,1},{9,5},{6,2},{10,6},{7,3},{11,7},{20,16},{24,20},... | collective-permute-start | bytes 786440 | tf_op jit(solution)/shard_map/ppermute | solution.py:19
  20.0 0.7 %copy-start.1 = (s32[1,4]{1,0:T(1,128)S(1)}, s32[1,4]{1,0:T(1,128)}, u32[]{:S(2)}) copy-start(s32[1,4]{1,0:T(1,128)} %refs_0_.1) | copy-start | bytes 52
  24.7 13.1 %collective-permute-start.5 = (bf16[128,1024]{1,0:T(8,128)(2,1)S(1)}, bf16[128,1024]{1,0:T(8,128)(2,1)S(1)}, u32[]{:S(2)}, u32[]{:S(2)}) collective-permute-start(bf16[128,1024]{1,0:T(8,128)(2,1)S(1)} %get-tuple-element.58.refs_3_.refs_6_), channel_id=1, source_target_pairs={{4,0},{8,4},{12,8},{5,1},{9,5},{13,9},{6,2},{10,6},{14,10},{7,3},{... | collective-permute-start | bytes 786440 | tf_op jit(solution)/shard_map/ppermute | solution.py:19
  32.0 3.2 %collective-permute-start.9 = (f32[16,128]{1,0:T(8,128)S(1)}, f32[16,128]{1,0:T(8,128)S(1)}, u32[]{:S(2)}, u32[]{:S(2)}) collective-permute-start(f32[16,128]{1,0:T(8,128)S(1)} %get-tuple-element.80), channel_id=1, source_target_pairs={{0,3},{1,2},{2,1},{3,0},{4,7},{5,6},{6,5},{7,4},{8,11},{9,10},{10,... | collective-permute-start | bytes 24584 | tf_op jit(solution)/shard_map/ppermute | solution.py:464
  32.1 3.7 %collective-permute-start.8 = (f32[16,128]{1,0:T(8,128)S(1)}, f32[16,128]{1,0:T(8,128)S(1)}, u32[]{:S(2)}, u32[]{:S(2)}) collective-permute-start(f32[16,128]{1,0:T(8,128)S(1)} %get-tuple-element.80), channel_id=1, source_target_pairs={{0,2},{1,3},{2,0},{3,1},{4,6},{5,7},{6,4},{7,5},{8,10},{9,11},{10,... | collective-permute-start | bytes 24584 | tf_op jit(solution)/shard_map/ppermute | solution.py:464
  33.6 2.2 %collective-permute-start.7 = (f32[16,128]{1,0:T(8,128)S(1)}, f32[16,128]{1,0:T(8,128)S(1)}, u32[]{:S(2)}, u32[]{:S(2)}) collective-permute-start(f32[16,128]{1,0:T(8,128)S(1)} %get-tuple-element.80), channel_id=1, source_target_pairs={{0,1},{1,0},{2,3},{3,2},{4,5},{5,4},{6,7},{7,6},{8,9},{9,8},{10,11... | collective-permute-start | bytes 24584 | tf_op jit(solution)/shard_map/ppermute | solution.py:464
  38.3 8.4 %collective-permute-start.10 = (bf16[96,1024]{1,0:T(8,128)(2,1)S(1)}, bf16[96,1024]{1,0:T(8,128)(2,1)S(1)}, u32[]{:S(2)}, u32[]{:S(2)}) collective-permute-start(bf16[96,1024]{1,0:T(8,128)(2,1)S(1)} %shard_map.135), channel_id=1, source_target_pairs={{4,0},{8,4},{5,1},{9,5},{6,2},{10,6},{7,3},{11,7},{20,16},{24,20},... | collective-permute-start | bytes 589832 | tf_op jit(solution)/shard_map/ppermute | solution.py:19
  39.6 8.4 %collective-permute-start.13 = (f32[16,128]{1,0:T(8,128)S(1)}, f32[16,128]{1,0:T(8,128)S(1)}, u32[]{:S(2)}, u32[]{:S(2)}) collective-permute-start(f32[16,128]{1,0:T(8,128)S(1)} %add_add_fusion.refs_0_), channel_id=1, source_target_pairs={{0,12},{4,8},{8,4},{12,0},{1,13},{5,9},{9,5},{13,1},{2,14},{6,10},... | collective-permute-start | bytes 24584 | tf_op jit(solution)/shard_map/ppermute | solution.py:464
  42.6 5.6 %collective-permute-start.12 = (f32[16,128]{1,0:T(8,128)S(1)}, f32[16,128]{1,0:T(8,128)S(1)}, u32[]{:S(2)}, u32[]{:S(2)}) collective-permute-start(f32[16,128]{1,0:T(8,128)S(1)} %add_add_fusion.refs_0_), channel_id=1, source_target_pairs={{0,8},{4,12},{8,0},{12,4},{1,9},{5,13},{9,1},{13,5},{2,10},{6,14},... | collective-permute-start | bytes 24584 | tf_op jit(solution)/shard_map/ppermute | solution.py:464
  44.4 3.8 %collective-permute-start.11 = (f32[16,128]{1,0:T(8,128)S(1)}, f32[16,128]{1,0:T(8,128)S(1)}, u32[]{:S(2)}, u32[]{:S(2)}) collective-permute-start(f32[16,128]{1,0:T(8,128)S(1)} %add_add_fusion.refs_0_), channel_id=1, source_target_pairs={{0,4},{4,0},{8,12},{12,8},{1,5},{5,1},{9,13},{13,9},{2,6},{6,2},{1... | collective-permute-start | bytes 24584 | tf_op jit(solution)/shard_map/ppermute | solution.py:464

commit v20 on v19

--- a/solution.py
+++ b/solution.py
@@ -9,6 +9,7 @@
 
 EPSILON = 1e-05
 VMEM_LIMIT = 24 * 1024 * 1024
+LONG = 4 * 10**9
 F32 = jnp.float32
 BF16 = jnp.bfloat16
 
@@ -416,6 +417,10 @@
         copy.wait()
 
 
+def pair_kernel(left, right, out):
+    out[...] = left[...] + right[...]
+
+
 def sum_kernel(*refs):
     gain_out, bias_out = refs[-2:]
     total = added_up([piece[...] for piece in refs[:-2]])
@@ -424,7 +429,7 @@
     bias_out[...] = total[lines:, : bias_out.shape[1]]
 
 
-def on_device(kernel, outs, args, smem=(), ahead=(), far=(), far_outs=0, scratch=()):
+def on_device(kernel, outs, args, smem=(), ahead=(), far=(), far_outs=0, scratch=(), flops=1000000):
     count = len(smem) + len(far) + len(args)
     far = [pltpu.with_memory_space_constraint(array, pltpu.HBM) for array in far]
 
@@ -442,15 +447,15 @@
         out_specs=[anywhere] * far_outs + [vmem] * (len(outs) - far_outs),
         scratch_shapes=scratch,
         compiler_params=pltpu.CompilerParams(vmem_limit_bytes=VMEM_LIMIT),
-        cost_estimate=pl.CostEstimate(flops=1000000, bytes_accessed=100000, transcendentals=0),
+        cost_estimate=pl.CostEstimate(flops=flops, bytes_accessed=100000, transcendentals=0),
     )(*smem, *far, *args, *ahead)
 
 
-def rounds_of(axes):
+def rounds_of(axes, first=1):
     rounds = []
     for axis in axes:
         size = lax.axis_size(axis)
-        step = 1
+        step = first
         while step < size:
             radix = 4 if size // step >= 4 else 2
             rounds.append((axis, [step * at for at in range(1, radix)]))
@@ -555,8 +560,17 @@
         [jax.ShapeDtypeStruct((heads * rows, cut), kind) for kind in (BF16, F32)],
         (table, flipped[reach], later_queries[reach], key),
     )
+    key_grads, far_tables, *pieces = lax.optimization_barrier((key_grads, far_tables, *pieces))
+    sums = added_up(pieces)
+    [(axis, distances), *rest] = [("ctx", [1]), *rounds_of(("ctx",), 2)]
+    (paired,) = on_device(
+        pair_kernel,
+        [jax.ShapeDtypeStruct(sums.shape, F32)],
+        exchanged(sums, axis, distances),
+        flops=LONG,
+    )
     for hops in range(1, reach):
-        arrived, *pieces = lax.optimization_barrier((later_grads[hops], *pieces))
+        arrived, sums = lax.optimization_barrier((later_grads[hops], sums))
         if hops + 1 == reach:
             (arrived,) = on_device(
                 partial(message_kernel, reach, heads, scaling),
@@ -579,7 +593,8 @@
                 [wide] * 2,
                 (*key_operands(hops), *key_grads),
             )
-    for axis, distances in rounds_of(("ctx",)):
+    pieces = [paired]
+    for axis, distances in rest:
         pieces = exchanged(added_up(pieces), axis, distances)
     key_grad, value_grad = on_device(
         partial(last_kernel, heads, scaling),

time: 49.1 us -> 50.8 us (1.035)
  waiting for transfers between devices: 14.1 us -> 15 us
  starting transfers between devices: 22 us -> 22.9 us
    ppermute x6 -> x5, starting transfers between devices: 7.1 us -> 7.95 us  [exchanged(): lax.ppermute(array, axis, [(i, i ^ distance) for i in range(size)])]
    ppermute x6 -> x5, waiting for transfers between devices: 0.67 us -> 1.45 us  [exchanged(): lax.ppermute(array, axis, [(i, i ^ distance) for i in range(size)])]
    pallas_call x11 -> x12, Pallas kernels: 11.1 us -> 11.1 us  [on_device(): pl.pallas_call(body, out_shape=outs, in_specs=[pl.BlockSpec(memory_space=...]
  transfers between devices with their start and end apart: 14 -> 13, of which waited for: 8 -> 7; matrix products, arithmetic and copies ran while one was open for 0% -> 0% of each run, Pallas kernels for 20% -> 21%
where the time goes in v20:
time: 50.8 us; the launch traced here: 50.5 us
  starting transfers between devices  22.9 us (45%)
  waiting for transfers between devices  15 us (30%)
  Pallas kernels  11.1 us (22%)
  between operations  0.84 us (2%)
  local copies, waits for them, and re-layouts  0.64 us (1%)
    ppermute x8, starting transfers between devices, passed_along(): lax.ppermute(array, axis, [(i, i + by) for i in range(first, last + 1)])  14.9 us
    ppermute x8, waiting for transfers between devices, passed_along(): lax.ppermute(array, axis, [(i, i + by) for i in range(first, last + 1)])  13.5 us
    pallas_call x12, Pallas kernels, on_device(): pl.pallas_call(body, out_shape=outs, in_specs=[pl.BlockSpec(memory_space=...  11.1 us
    ppermute x5, starting transfers between devices, exchanged(): lax.ppermute(array, axis, [(i, i ^ distance) for i in range(size)])  7.95 us
    ppermute x5, waiting for transfers between devices, exchanged(): lax.ppermute(array, axis, [(i, i ^ distance) for i in range(size)])  1.45 us
  transfers between devices with their start and end apart: 13, of which 7 were waited for; matrix products, arithmetic and copies ran while one was open for 0% of the time, Pallas kernels for 21%

profile of v20, /device:TPU:0, one launch (start us, length us, event | category | flops | bytes accessed | tf_op | source)
XLA Modules:
  0.0 50.5 jit_solution(16412365893156248985)
XLA Ops:
  0.6 4.9 %collective-permute-start.1 = (bf16[128,1024]{1,0:T(8,128)(2,1)}, bf16[128,1024]{1,0:T(8,128)(2,1)S(1)}, u32[]{:S(2)}, u32[]{:S(2)}) collective-permute-start(bf16[128,1024]{1,0:T(8,128)(2,1)} %bitcast.13), channel_id=1, source_target_pairs={{0,4},{4,8},{8,12},{1,5},{5,9},{9,13},{2,6},{6,10},{10,14},{3,7},{... | collective-permute-start | bytes 786440 | tf_op jit(solution)/shard_map/ppermute | solution.py:20
  5.6 0.0 copy-start
  5.6 3.5 %collective-permute-start.3 = (bf16[128,1024]{1,0:T(8,128)(2,1)}, bf16[128,1024]{1,0:T(8,128)(2,1)S(1)}, u32[]{:S(2)}, u32[]{:S(2)}) collective-permute-start(bf16[128,1024]{1,0:T(8,128)(2,1)} %bitcast.15), channel_id=1, source_target_pairs={{0,4},{4,8},{8,12},{1,5},{5,9},{9,13},{2,6},{6,10},{10,14},{3,7},{... | collective-permute-start | bytes 786440 | tf_op jit(solution)/shard_map/ppermute | solution.py:20
  9.1 1.3 %collective-permute-start = (bf16[128,1024]{1,0:T(8,128)(2,1)}, bf16[128,1024]{1,0:T(8,128)(2,1)S(1)}, u32[]{:S(2)}, u32[]{:S(2)}) collective-permute-start(bf16[128,1024]{1,0:T(8,128)(2,1)} %bitcast.11), channel_id=1, source_target_pairs={{4,0},{8,4},{12,8},{5,1},{9,5},{13,9},{6,2},{10,6},{14,10},{7,3},{... | collective-permute-start | bytes 786440 | tf_op jit(solution)/shard_map/ppermute | solution.py:20
  10.4 2.2 %collective-permute-done.1.refs_4_.refs_8_.refs_5_ = bf16[128,1024]{1,0:T(8,128)(2,1)S(1)} collective-permute-done((bf16[128,1024]{1,0:T(8,128)(2,1)}, bf16[128,1024]{1,0:T(8,128)(2,1)S(1)}, u32[]{:S(2)}, u32[]{:S(2)}) %collective-permute-start.1) | collective-permute-done | bytes 262176 | tf_op jit(solution)/shard_map/ppermute | solution.py:20
  12.6 0.7 %collective-permute-start.2 = (bf16[128,1024]{1,0:T(8,128)(2,1)S(1)}, bf16[128,1024]{1,0:T(8,128)(2,1)S(1)}, u32[]{:S(2)}, u32[]{:S(2)}) collective-permute-start(bf16[128,1024]{1,0:T(8,128)(2,1)S(1)} %collective-permute-done.1.refs_4_.refs_8_.refs_5_), channel_id=1, source_target_pairs={{4,8},{8,12},{5,9},{9,13},{6,10},{10,14},{7,11},{11,15},{20,24},{2... | collective-permute-start | bytes 786440 | tf_op jit(solution)/shard_map/ppermute | solution.py:20
  13.3 3.8 %collective-permute-done.3.refs_5_.refs_11_.refs_6_ = bf16[128,1024]{1,0:T(8,128)(2,1)S(1)} collective-permute-done((bf16[128,1024]{1,0:T(8,128)(2,1)}, bf16[128,1024]{1,0:T(8,128)(2,1)S(1)}, u32[]{:S(2)}, u32[]{:S(2)}) %collective-permute-start.3) | collective-permute-done | bytes 262176 | tf_op jit(solution)/shard_map/ppermute | solution.py:20
  17.1 0.7 %collective-permute-start.4 = (bf16[128,1024]{1,0:T(8,128)(2,1)S(1)}, bf16[128,1024]{1,0:T(8,128)(2,1)S(1)}, u32[]{:S(2)}, u32[]{:S(2)}) collective-permute-start(bf16[128,1024]{1,0:T(8,128)(2,1)S(1)} %collective-permute-done.3.refs_5_.refs_11_.refs_6_), channel_id=1, source_target_pairs={{4,8},{8,12},{5,9},{9,13},{6,10},{10,14},{7,11},{11,15},{20,24},{2... | collective-permute-start | bytes 786440 | tf_op jit(solution)/shard_map/ppermute | solution.py:20
  17.7 1.0 %collective-permute-done.refs_7_.refs_2_.refs_3_ = bf16[128,1024]{1,0:T(8,128)(2,1)S(1)} collective-permute-done((bf16[128,1024]{1,0:T(8,128)(2,1)}, bf16[128,1024]{1,0:T(8,128)(2,1)S(1)}, u32[]{:S(2)}, u32[]{:S(2)}) %collective-permute-start) | collective-permute-done | bytes 262176 | tf_op jit(solution)/shard_map/ppermute | solution.py:20
  18.7 1.3 %collective-permute-start.6 = (bf16[128,1024]{1,0:T(8,128)(2,1)S(1)}, bf16[128,1024]{1,0:T(8,128)(2,1)S(1)}, u32[]{:S(2)}, u32[]{:S(2)}) collective-permute-start(bf16[128,1024]{1,0:T(8,128)(2,1)S(1)} %collective-permute-done.refs_7_.refs_2_.refs_3_), channel_id=1, source_target_pairs={{4,0},{8,4},{5,1},{9,5},{6,2},{10,6},{7,3},{11,7},{20,16},{24,20},... | collective-permute-start | bytes 786440 | tf_op jit(solution)/shard_map/ppermute | solution.py:20
  20.0 0.0 copy-start.1
  20.0 0.0 copy-done
  20.0 0.6 %copy-done.1 = s32[1,4]{1,0:T(1,128)S(1)} copy-done((s32[1,4]{1,0:T(1,128)S(1)}, s32[1,4]{1,0:T(1,128)}, u32[]{:S(2)}) %copy-start.1) | copy-done | bytes 40
  20.6 2.5 %shard_map.127 = (f32[64,128]{1,0:T(8,128)S(1)}, f32[1024,128]{1,0:T(8,128)S(1)}, f32[128,128]{1,0:T(8,128)S(1)}, f32[128,128]{1,0:T(8,128)S(1)}, f32[128,128]{1...) custom-call(s32[1,4]{1,0:T(1,128)S(1)} %copy-done.1, ...), custom_call_target="tpu_custom_call" | custom-call | flops 1000000 | bytes 100000 | tf_op jit(solution)/shard_map/pallas_call | solution.py:440
  23.1 0.6 %shard_map.128.refs_5_.refs_2_ = f32[128,1024]{1,0:T(8,128)S(1)} custom-call(f32[64,128]{1,0:T(8,128)S(1)} %get-tuple-element.52.refs_0_, f32[1024,128]{1,0:T(8,128)S(1)} %get-tuple-element.54.refs_1_, f32[128,128]{1,0:T(8,128)S(1)} %get-tuple-element.57.refs_2_.refs_3_, bf16[128,1024]{1,0:T(8,128)(2,1)S(1)} %get-tuple-element.56.refs_3_.refs_2_.refs_5_, ...), custom_call_target="tpu_custom_call" | custom-call | flops 1000000 | bytes 100000 | tf_op jit(solution)/shard_map/pallas_call | solution.py:440
  23.7 0.0 collective-permute-done.2.refs_4_.refs_9_
  23.7 0.3 shard_map.129.refs_0_
  24.0 0.0 collective-permute-done.4.refs_1_.refs_12_
  24.0 0.6 %shard_map.130 = (f32[128,1024]{1,0:T(8,128)S(1)}, bf16[128,1024]{1,0:T(8,128)(2,1)S(1)}, f32[1,1024]{1,0:T(1,128)S(1)}) custom-call(bf16[1024,128]{1,0:T(8,128)(2,1)S(1)} %shard_map.129.refs_0_, bf16[128,1024]{1,0:T(8,128)(2,1)S(1)} %collective-permute-done.4.refs_1_.refs_12_, f32[128,1024]{1,0:T(8,128)S(1)} %shard_map.128.refs_5_.refs_2_, ...), custom_call_target="tpu_custom_call" | custom-call | flops 1000000 | bytes 100000 | tf_op jit(solution)/shard_map/pallas_call | solution.py:440
  24.7 1.3 %collective-permute-start.5 = (bf16[128,1024]{1,0:T(8,128)(2,1)S(1)}, bf16[128,1024]{1,0:T(8,128)(2,1)S(1)}, u32[]{:S(2)}, u32[]{:S(2)}) collective-permute-start(bf16[128,1024]{1,0:T(8,128)(2,1)S(1)} %get-tuple-element.62.refs_3_.refs_6_), channel_id=1, source_target_pairs={{4,0},{8,4},{12,8},{5,1},{9,5},{13,9},{6,2},{10,6},{14,10},{7,3},{... | collective-permute-start | bytes 786440 | tf_op jit(solution)/shard_map/ppermute | solution.py:20
  26.0 4.4 %collective-permute-done.6.refs_2_.refs_14_.refs_3_ = bf16[128,1024]{1,0:T(8,128)(2,1)S(1)} collective-permute-done((bf16[128,1024]{1,0:T(8,128)(2,1)S(1)}, bf16[128,1024]{1,0:T(8,128)(2,1)S(1)}, u32[]{:S(2)}, u32[]{:S(2)}) %collective-permute-start.6) | collective-permute-done | bytes 262176 | tf_op jit(solution)/shard_map/ppermute | solution.py:20
  30.3 1.7 %shard_map.133 = (bf16[128,1024]{1,0:T(8,128)(2,1)S(1)}, f32[16,128]{1,0:T(8,128)S(1)}) custom-call(f32[64,128]{1,0:T(8,128)S(1)} %get-tuple-element.52.refs_0_, f32[1024,128]{1,0:T(8,128)S(1)} %get-tuple-element.54.refs_1_, f32[128,128]{1,0:T(8,128)S(1)} %get-tuple-element.71.refs_2_, f32[128,128]{1,0:T(8,128)S(1)} %get-tuple-element.57.refs_2_.refs_3_, ...), custom_call_target="tpu_custom_call" | custom-call | flops 1000000 | bytes 100000 | tf_op jit(solution)/shard_map/pallas_call | solution.py:440
  32.0 0.1 collective-permute-start.7
  32.1 1.5 %collective-permute-start.8 = (f32[16,128]{1,0:T(8,128)S(1)}, f32[16,128]{1,0:T(8,128)S(1)}, u32[]{:S(2)}, u32[]{:S(2)}) collective-permute-start(f32[16,128]{1,0:T(8,128)S(1)} %get-tuple-element.83), channel_id=1, source_target_pairs={{0,2},{1,3},{2,0},{3,1},{4,6},{5,7},{6,4},{7,5},{8,10},{9,11},{10,... | collective-permute-start | bytes 24584 | tf_op jit(solution)/shard_map/ppermute | solution.py:469
  33.6 0.3 collective-permute-start.9
  33.9 0.9 %shard_map.131 = (f32[128,1024]{1,0:T(8,128)S(1)}, f32[128,1024]{1,0:T(8,128)S(1)}) custom-call(f32[64,128]{1,0:T(8,128)S(1)} %get-tuple-element.52.refs_0_, f32[128,128]{1,0:T(8,128)S(1)} %get-tuple-element.65.refs_1_, bf16[128,1024]{1,0:T(8,128)(2,1)S(1)} %get-tuple-element.56.refs_3_.refs_2_.refs_5_, ...), custom_call_target="tpu_custom_call" | custom-call | flops 1000000 | bytes 100000 | tf_op jit(solution)/shard_map/pallas_call | solution.py:440
  34.8 0.4 shard_map.132
  35.2 0.0 collective-permute-done.7
  35.2 0.5 %collective-permute-done.8 = f32[16,128]{1,0:T(8,128)S(1)} collective-permute-done((f32[16,128]{1,0:T(8,128)S(1)}, f32[16,128]{1,0:T(8,128)S(1)}, u32[]{:S(2)}, u32[]{:S(2)}) %collective-permute-start.8) | collective-permute-done | bytes 8224 | tf_op jit(solution)/shard_map/ppermute | solution.py:469
  35.8 0.9 %collective-permute-done.9 = f32[16,128]{1,0:T(8,128)S(1)} collective-permute-done((f32[16,128]{1,0:T(8,128)S(1)}, f32[16,128]{1,0:T(8,128)S(1)}, u32[]{:S(2)}, u32[]{:S(2)}) %collective-permute-start.9) | collective-permute-done | bytes 8224 | tf_op jit(solution)/shard_map/ppermute | solution.py:469
  36.7 2.3 %collective-permute-start.11 = (f32[16,128]{1,0:T(8,128)S(1)}, f32[16,128]{1,0:T(8,128)S(1)}, u32[]{:S(2)}, u32[]{:S(2)}) collective-permute-start(f32[16,128]{1,0:T(8,128)S(1)} %add_add_fusion.refs_0_), channel_id=1, source_target_pairs={{0,4},{4,0},{8,12},{12,8},{1,5},{5,1},{9,13},{13,9},{2,6},{6,2},{1... | collective-permute-start | bytes 24584 | tf_op jit(solution)/shard_map/ppermute | solution.py:469
  39.0 0.0 collective-permute-done.5.refs_3_.refs_4_
  39.0 0.6 %shard_map.135 = bf16[96,1024]{1,0:T(8,128)(2,1)S(1)} custom-call(f32[64,128]{1,0:T(8,128)S(1)} %get-tuple-element.52.refs_0_, f32[32,128]{1,0:T(8,128)S(1)} %get-tuple-element.82.refs_1_, f32[16,128]{1,0:T(8,128)S(1)} %get-tuple-element.81.refs_2_, bf16[128,1024]{1,0:T(8,128)(2,1)S(1)} %collective-permute-done.refs_7_.refs_2_.refs_3_, ...), custom_call_target="tpu_custom_call" | custom-call | flops 1000000 | bytes 100000 | tf_op jit(solution)/shard_map/pallas_call | solution.py:440
  39.6 1.3 %collective-permute-start.10 = (bf16[96,1024]{1,0:T(8,128)(2,1)S(1)}, bf16[96,1024]{1,0:T(8,128)(2,1)S(1)}, u32[]{:S(2)}, u32[]{:S(2)}) collective-permute-start(bf16[96,1024]{1,0:T(8,128)(2,1)S(1)} %shard_map.135), channel_id=1, source_target_pairs={{4,0},{8,4},{5,1},{9,5},{6,2},{10,6},{7,3},{11,7},{20,16},{24,20},... | collective-permute-start | bytes 589832 | tf_op jit(solution)/shard_map/ppermute | solution.py:20
  40.9 0.0 collective-permute-done.11.refs_1_
  41.0 3.7 %collective-permute-start.12 = (f32[16,128]{1,0:T(8,128)S(1)}, f32[16,128]{1,0:T(8,128)S(1)}, u32[]{:S(2)}, u32[]{:S(2)}) collective-permute-start(f32[16,128]{1,0:T(8,128)S(1)} %shard_map.137.refs_0_), channel_id=1, source_target_pairs={{0,8},{4,12},{8,0},{12,4},{1,9},{5,13},{9,1},{13,5},{2,10},{6,14},... | collective-permute-start | bytes 24584 | tf_op jit(solution)/shard_map/ppermute | solution.py:469
  44.7 1.6 %shard_map.134 = (bf16[128,1024]{1,0:T(8,128)(2,1)}, bf16[128,1024]{1,0:T(8,128)(2,1)}, f32[128,1024]{1,0:T(8,128)S(1)}, f32[128,1024]{1,0:T(8,128)S(1)}) custom-call(f32[64,128]{1,0:T(8,128)S(1)} %get-tuple-element.52.refs_0_, f32[128,128]{1,0:T(8,128)S(1)} %get-tuple-element.53.refs_1_, bf16[128,1024]{1,0:T(8,128)(2,1)S(1)} %collective-permute-done.refs_7_.refs_2_.refs_3_, ...), custom_call_target="tpu_custom_call" | custom-call | flops 1000000 | bytes 100000 | tf_op jit(solution)/shard_map/pallas_call | solution.py:440
  46.3 2.2 %collective-permute-done.10.refs_4_ = bf16[96,1024]{1,0:T(8,128)(2,1)S(1)} collective-permute-done((bf16[96,1024]{1,0:T(8,128)(2,1)S(1)}, bf16[96,1024]{1,0:T(8,128)(2,1)S(1)}, u32[]{:S(2)}, u32[]{:S(2)}) %collective-permute-start.10) | collective-permute-done | bytes 196640 | tf_op jit(solution)/shard_map/ppermute | solution.py:20
  48.5 1.3 %shard_map.136 = (bf16[128,1024]{1,0:T(8,128)(2,1)}, bf16[128,1024]{1,0:T(8,128)(2,1)}) custom-call(bf16[1024,96]{1,0:T(8,128)(2,1)S(1)} %get-tuple-element.79.refs_8_.refs_0_, f32[1024,96]{1,0:T(8,128)S(1)} %get-tuple-element.80.refs_1_, f32[16,128]{1,0:T(8,128)S(1)} %get-tuple-element.81.refs_2_, ...), custom_call_target="tpu_custom_call" | custom-call | flops 1000000 | bytes 100000 | tf_op jit(solution)/shard_map/pallas_call | solution.py:440
  49.9 0.0 collective-permute-done.12.refs_1_
  49.9 0.6 %shard_map.138 = (f32[8,128]{1,0:T(8,128)}, f32[8,8]{1,0:T(8,128)}) custom-call(f32[16,128]{1,0:T(8,128)S(1)} %shard_map.137.refs_0_, f32[16,128]{1,0:T(8,128)S(1)} %collective-permute-done.12.refs_1_), custom_call_target="tpu_custom_call" | custom-call | flops 1000000 | bytes 100000 | tf_op jit(solution)/shard_map/pallas_call | solution.py:440
  (2 shorter events, 0.0 us)
Async XLA Ops:
  0.6 11.9 %collective-permute-start.1 = (bf16[128,1024]{1,0:T(8,128)(2,1)}, bf16[128,1024]{1,0:T(8,128)(2,1)S(1)}, u32[]{:S(2)}, u32[]{:S(2)}) collective-permute-start(bf16[128,1024]{1,0:T(8,128)(2,1)} %bitcast.13), channel_id=1, source_target_pairs={{0,4},{4,8},{8,12},{1,5},{5,9},{9,13},{2,6},{6,10},{10,14},{3,7},{... | collective-permute-start | bytes 786440 | tf_op jit(solution)/shard_map/ppermute | solution.py:20
  5.6 14.4 %copy-start = (f32[8,8]{1,0:T(8,128)S(1)}, f32[8,8]{1,0:T(8,128)}, u32[]{:S(2)}) copy-start(f32[8,8]{1,0:T(8,128)} %refs_1_.1) | copy-start | bytes 772
  5.6 11.5 %collective-permute-start.3 = (bf16[128,1024]{1,0:T(8,128)(2,1)}, bf16[128,1024]{1,0:T(8,128)(2,1)S(1)}, u32[]{:S(2)}, u32[]{:S(2)}) collective-permute-start(bf16[128,1024]{1,0:T(8,128)(2,1)} %bitcast.15), channel_id=1, source_target_pairs={{0,4},{4,8},{8,12},{1,5},{5,9},{9,13},{2,6},{6,10},{10,14},{3,7},{... | collective-permute-start | bytes 786440 | tf_op jit(solution)/shard_map/ppermute | solution.py:20
  9.1 9.6 %collective-permute-start = (bf16[128,1024]{1,0:T(8,128)(2,1)}, bf16[128,1024]{1,0:T(8,128)(2,1)S(1)}, u32[]{:S(2)}, u32[]{:S(2)}) collective-permute-start(bf16[128,1024]{1,0:T(8,128)(2,1)} %bitcast.11), channel_id=1, source_target_pairs={{4,0},{8,4},{12,8},{5,1},{9,5},{13,9},{6,2},{10,6},{14,10},{7,3},{... | collective-permute-start | bytes 786440 | tf_op jit(solution)/shard_map/ppermute | solution.py:20
  12.6 11.1 %collective-permute-start.2 = (bf16[128,1024]{1,0:T(8,128)(2,1)S(1)}, bf16[128,1024]{1,0:T(8,128)(2,1)S(1)}, u32[]{:S(2)}, u32[]{:S(2)}) collective-permute-start(bf16[128,1024]{1,0:T(8,128)(2,1)S(1)} %collective-permute-done.1.refs_4_.refs_8_.refs_5_), channel_id=1, source_target_pairs={{4,8},{8,12},{5,9},{9,13},{6,10},{10,14},{7,11},{11,15},{20,24},{2... | collective-permute-start | bytes 786440 | tf_op jit(solution)/shard_map/ppermute | solution.py:20
  17.1 7.0 %collective-permute-start.4 = (bf16[128,1024]{1,0:T(8,128)(2,1)S(1)}, bf16[128,1024]{1,0:T(8,128)(2,1)S(1)}, u32[]{:S(2)}, u32[]{:S(2)}) collective-permute-start(bf16[128,1024]{1,0:T(8,128)(2,1)S(1)} %collective-permute-done.3.refs_5_.refs_11_.refs_6_), channel_id=1, source_target_pairs={{4,8},{8,12},{5,9},{9,13},{6,10},{10,14},{7,11},{11,15},{20,24},{2... | collective-permute-start | bytes 786440 | tf_op jit(solution)/shard_map/ppermute | solution.py:20
  18.7 11.7 %collective-permute-start.6 = (bf16[128,1024]{1,0:T(8,128)(2,1)S(1)}, bf16[128,1024]{1,0:T(8,128)(2,1)S(1)}, u32[]{:S(2)}, u32[]{:S(2)}) collective-permute-start(bf16[128,1024]{1,0:T(8,128)(2,1)S(1)} %collective-permute-done.refs_7_.refs_2_.refs_3_), channel_id=1, source_target_pairs={{4,0},{8,4},{5,1},{9,5},{6,2},{10,6},{7,3},{11,7},{20,16},{24,20},... | collective-permute-start | bytes 786440 | tf_op jit(solution)/shard_map/ppermute | solution.py:20
  20.0 0.7 %copy-start.1 = (s32[1,4]{1,0:T(1,128)S(1)}, s32[1,4]{1,0:T(1,128)}, u32[]{:S(2)}) copy-start(s32[1,4]{1,0:T(1,128)} %refs_0_.1) | copy-start | bytes 52
  24.7 14.4 %collective-permute-start.5 = (bf16[128,1024]{1,0:T(8,128)(2,1)S(1)}, bf16[128,1024]{1,0:T(8,128)(2,1)S(1)}, u32[]{:S(2)}, u32[]{:S(2)}) collective-permute-start(bf16[128,1024]{1,0:T(8,128)(2,1)S(1)} %get-tuple-element.62.refs_3_.refs_6_), channel_id=1, source_target_pairs={{4,0},{8,4},{12,8},{5,1},{9,5},{13,9},{6,2},{10,6},{14,10},{7,3},{... | collective-permute-start | bytes 786440 | tf_op jit(solution)/shard_map/ppermute | solution.py:20
  32.0 3.2 %collective-permute-start.7 = (f32[16,128]{1,0:T(8,128)S(1)}, f32[16,128]{1,0:T(8,128)S(1)}, u32[]{:S(2)}, u32[]{:S(2)}) collective-permute-start(f32[16,128]{1,0:T(8,128)S(1)} %get-tuple-element.83), channel_id=1, source_target_pairs={{0,1},{1,0},{2,3},{3,2},{4,5},{5,4},{6,7},{7,6},{8,9},{9,8},{10,11... | collective-permute-start | bytes 24584 | tf_op jit(solution)/shard_map/ppermute | solution.py:469
  32.1 3.7 %collective-permute-start.8 = (f32[16,128]{1,0:T(8,128)S(1)}, f32[16,128]{1,0:T(8,128)S(1)}, u32[]{:S(2)}, u32[]{:S(2)}) collective-permute-start(f32[16,128]{1,0:T(8,128)S(1)} %get-tuple-element.83), channel_id=1, source_target_pairs={{0,2},{1,3},{2,0},{3,1},{4,6},{5,7},{6,4},{7,5},{8,10},{9,11},{10,... | collective-permute-start | bytes 24584 | tf_op jit(solution)/shard_map/ppermute | solution.py:469
  33.6 3.1 %collective-permute-start.9 = (f32[16,128]{1,0:T(8,128)S(1)}, f32[16,128]{1,0:T(8,128)S(1)}, u32[]{:S(2)}, u32[]{:S(2)}) collective-permute-start(f32[16,128]{1,0:T(8,128)S(1)} %get-tuple-element.83), channel_id=1, source_target_pairs={{0,3},{1,2},{2,1},{3,0},{4,7},{5,6},{6,5},{7,4},{8,11},{9,10},{10,... | collective-permute-start | bytes 24584 | tf_op jit(solution)/shard_map/ppermute | solution.py:469
  36.7 4.2 %collective-permute-start.11 = (f32[16,128]{1,0:T(8,128)S(1)}, f32[16,128]{1,0:T(8,128)S(1)}, u32[]{:S(2)}, u32[]{:S(2)}) collective-permute-start(f32[16,128]{1,0:T(8,128)S(1)} %add_add_fusion.refs_0_), channel_id=1, source_target_pairs={{0,4},{4,0},{8,12},{12,8},{1,5},{5,1},{9,13},{13,9},{2,6},{6,2},{1... | collective-permute-start | bytes 24584 | tf_op jit(solution)/shard_map/ppermute | solution.py:469
  39.6 8.9 %collective-permute-start.10 = (bf16[96,1024]{1,0:T(8,128)(2,1)S(1)}, bf16[96,1024]{1,0:T(8,128)(2,1)S(1)}, u32[]{:S(2)}, u32[]{:S(2)}) collective-permute-start(bf16[96,1024]{1,0:T(8,128)(2,1)S(1)} %shard_map.135), channel_id=1, source_target_pairs={{4,0},{8,4},{5,1},{9,5},{6,2},{10,6},{7,3},{11,7},{20,16},{24,20},... | collective-permute-start | bytes 589832 | tf_op jit(solution)/shard_map/ppermute | solution.py:20
  41.0 8.9 %collective-permute-start.12 = (f32[16,128]{1,0:T(8,128)S(1)}, f32[16,128]{1,0:T(8,128)S(1)}, u32[]{:S(2)}, u32[]{:S(2)}) collective-permute-start(f32[16,128]{1,0:T(8,128)S(1)} %shard_map.137.refs_0_), channel_id=1, source_target_pairs={{0,8},{4,12},{8,0},{12,4},{1,9},{5,13},{9,1},{13,5},{2,10},{6,14},... | collective-permute-start | bytes 24584 | tf_op jit(solution)/shard_map/ppermute | solution.py:469

commit v21 on v20

--- a/solution.py
+++ b/solution.py
@@ -560,8 +560,8 @@
         [jax.ShapeDtypeStruct((heads * rows, cut), kind) for kind in (BF16, F32)],
         (table, flipped[reach], later_queries[reach], key),
     )
-    key_grads, far_tables, *pieces = lax.optimization_barrier((key_grads, far_tables, *pieces))
-    sums = added_up(pieces)
+    key_grads, far_tables, *pieces = lax.optimization_barrier((key_grads, far_tables, *pieces[::-1]))
+    sums = added_up(pieces[::-1])
     [(axis, distances), *rest] = [("ctx", [1]), *rounds_of(("ctx",), 2)]
     (paired,) = on_device(
         pair_kernel,
@@ -596,18 +596,21 @@
     pieces = [paired]
     for axis, distances in rest:
         pieces = exchanged(added_up(pieces), axis, distances)
+    key_grads, pieces[0] = lax.optimization_barrier((key_grads, pieces[0]))
+    gain_grad, bias_grad = on_device(
+        sum_kernel,
+        [jax.ShapeDtypeStruct((8, lanes), F32), jax.ShapeDtypeStruct((levels, heads), F32)],
+        pieces,
+    )
+    later_grads[reach], gain_grad, bias_grad = lax.optimization_barrier(
+        (later_grads[reach], gain_grad, bias_grad)
+    )
     key_grad, value_grad = on_device(
         partial(last_kernel, heads, scaling),
         [narrow, narrow],
         (*far_tables, late, later_queries[reach], later_grads[reach], value, *key_grads),
         far_outs=2,
         scratch=[pltpu.VMEM((rows, features), BF16)] * 2 + [pltpu.SemaphoreType.DMA((2 * heads,))],
-    )
-    key_grad, value_grad, pieces[0] = lax.optimization_barrier((key_grad, value_grad, pieces[0]))
-    gain_grad, bias_grad = on_device(
-        sum_kernel,
-        [jax.ShapeDtypeStruct((8, lanes), F32), jax.ShapeDtypeStruct((levels, heads), F32)],
-        pieces,
     )
     return (
         query_grad[None],

time: 50.8 us -> 51.5 us (1.014)
    ppermute x5, waiting for transfers between devices: 1.45 us -> 3.86 us  [exchanged(): lax.ppermute(array, axis, [(i, i ^ distance) for i in range(size)])]
    ppermute x8, waiting for transfers between devices: 13.5 us -> 11.3 us  [passed_along(): lax.ppermute(array, axis, [(i, i + by) for i in range(first, last + 1)])]
  transfers between devices with their start and end apart: 13 -> 13, of which waited for: 7 -> 6; matrix products, arithmetic and copies ran while one was open for 0% -> 0% of each run, Pallas kernels for 21% -> 19%
where the time goes in v21:
time: 51.5 us; the launch traced here: 51.1 us
  starting transfers between devices  23.4 us (45%)
  waiting for transfers between devices  15.2 us (30%)
  Pallas kernels  11.1 us (22%)
  between operations  0.82 us (2%)
  local copies, waits for them, and re-layouts  0.64 us (1%)
    ppermute x8, starting transfers between devices, passed_along(): lax.ppermute(array, axis, [(i, i + by) for i in range(first, last + 1)])  14.9 us
    ppermute x8, waiting for transfers between devices, passed_along(): lax.ppermute(array, axis, [(i, i + by) for i in range(first, last + 1)])  11.3 us
    pallas_call x12, Pallas kernels, on_device(): pl.pallas_call(body, out_shape=outs, in_specs=[pl.BlockSpec(memory_space=...  11.1 us
    ppermute x5, starting transfers between devices, exchanged(): lax.ppermute(array, axis, [(i, i ^ distance) for i in range(size)])  8.46 us
    ppermute x5, waiting for transfers between devices, exchanged(): lax.ppermute(array, axis, [(i, i ^ distance) for i in range(size)])  3.86 us
  transfers between devices with their start and end apart: 13, of which 6 were waited for; matrix products, arithmetic and copies ran while one was open for 0% of the time, Pallas kernels for 19%

profile of v21, /device:TPU:0, one launch (start us, length us, event | category | flops | bytes accessed | tf_op | source)
XLA Modules:
  0.0 51.1 jit_solution(14813327755785027781)
XLA Ops:
  0.6 4.9 %collective-permute-start.1 = (bf16[128,1024]{1,0:T(8,128)(2,1)}, bf16[128,1024]{1,0:T(8,128)(2,1)S(1)}, u32[]{:S(2)}, u32[]{:S(2)}) collective-permute-start(bf16[128,1024]{1,0:T(8,128)(2,1)} %bitcast.13), channel_id=1, source_target_pairs={{0,4},{4,8},{8,12},{1,5},{5,9},{9,13},{2,6},{6,10},{10,14},{3,7},{... | collective-permute-start | bytes 786440 | tf_op jit(solution)/shard_map/ppermute | solution.py:20
  5.6 0.0 copy-start
  5.6 3.5 %collective-permute-start.3 = (bf16[128,1024]{1,0:T(8,128)(2,1)}, bf16[128,1024]{1,0:T(8,128)(2,1)S(1)}, u32[]{:S(2)}, u32[]{:S(2)}) collective-permute-start(bf16[128,1024]{1,0:T(8,128)(2,1)} %bitcast.15), channel_id=1, source_target_pairs={{0,4},{4,8},{8,12},{1,5},{5,9},{9,13},{2,6},{6,10},{10,14},{3,7},{... | collective-permute-start | bytes 786440 | tf_op jit(solution)/shard_map/ppermute | solution.py:20
  9.1 1.3 %collective-permute-start = (bf16[128,1024]{1,0:T(8,128)(2,1)}, bf16[128,1024]{1,0:T(8,128)(2,1)S(1)}, u32[]{:S(2)}, u32[]{:S(2)}) collective-permute-start(bf16[128,1024]{1,0:T(8,128)(2,1)} %bitcast.11), channel_id=1, source_target_pairs={{4,0},{8,4},{12,8},{5,1},{9,5},{13,9},{6,2},{10,6},{14,10},{7,3},{... | collective-permute-start | bytes 786440 | tf_op jit(solution)/shard_map/ppermute | solution.py:20
  10.4 2.2 %collective-permute-done.1.refs_4_.refs_8_.refs_5_ = bf16[128,1024]{1,0:T(8,128)(2,1)S(1)} collective-permute-done((bf16[128,1024]{1,0:T(8,128)(2,1)}, bf16[128,1024]{1,0:T(8,128)(2,1)S(1)}, u32[]{:S(2)}, u32[]{:S(2)}) %collective-permute-start.1) | collective-permute-done | bytes 262176 | tf_op jit(solution)/shard_map/ppermute | solution.py:20
  12.6 0.7 %collective-permute-start.2 = (bf16[128,1024]{1,0:T(8,128)(2,1)S(1)}, bf16[128,1024]{1,0:T(8,128)(2,1)S(1)}, u32[]{:S(2)}, u32[]{:S(2)}) collective-permute-start(bf16[128,1024]{1,0:T(8,128)(2,1)S(1)} %collective-permute-done.1.refs_4_.refs_8_.refs_5_), channel_id=1, source_target_pairs={{4,8},{8,12},{5,9},{9,13},{6,10},{10,14},{7,11},{11,15},{20,24},{2... | collective-permute-start | bytes 786440 | tf_op jit(solution)/shard_map/ppermute | solution.py:20
  13.3 3.8 %collective-permute-done.3.refs_5_.refs_11_.refs_6_ = bf16[128,1024]{1,0:T(8,128)(2,1)S(1)} collective-permute-done((bf16[128,1024]{1,0:T(8,128)(2,1)}, bf16[128,1024]{1,0:T(8,128)(2,1)S(1)}, u32[]{:S(2)}, u32[]{:S(2)}) %collective-permute-start.3) | collective-permute-done | bytes 262176 | tf_op jit(solution)/shard_map/ppermute | solution.py:20
  17.1 0.7 %collective-permute-start.4 = (bf16[128,1024]{1,0:T(8,128)(2,1)S(1)}, bf16[128,1024]{1,0:T(8,128)(2,1)S(1)}, u32[]{:S(2)}, u32[]{:S(2)}) collective-permute-start(bf16[128,1024]{1,0:T(8,128)(2,1)S(1)} %collective-permute-done.3.refs_5_.refs_11_.refs_6_), channel_id=1, source_target_pairs={{4,8},{8,12},{5,9},{9,13},{6,10},{10,14},{7,11},{11,15},{20,24},{2... | collective-permute-start | bytes 786440 | tf_op jit(solution)/shard_map/ppermute | solution.py:20
  17.7 1.0 %collective-permute-done.refs_7_.refs_2_.refs_3_ = bf16[128,1024]{1,0:T(8,128)(2,1)S(1)} collective-permute-done((bf16[128,1024]{1,0:T(8,128)(2,1)}, bf16[128,1024]{1,0:T(8,128)(2,1)S(1)}, u32[]{:S(2)}, u32[]{:S(2)}) %collective-permute-start) | collective-permute-done | bytes 262176 | tf_op jit(solution)/shard_map/ppermute | solution.py:20
  18.7 1.3 %collective-permute-start.6 = (bf16[128,1024]{1,0:T(8,128)(2,1)S(1)}, bf16[128,1024]{1,0:T(8,128)(2,1)S(1)}, u32[]{:S(2)}, u32[]{:S(2)}) collective-permute-start(bf16[128,1024]{1,0:T(8,128)(2,1)S(1)} %collective-permute-done.refs_7_.refs_2_.refs_3_), channel_id=1, source_target_pairs={{4,0},{8,4},{5,1},{9,5},{6,2},{10,6},{7,3},{11,7},{20,16},{24,20},... | collective-permute-start | bytes 786440 | tf_op jit(solution)/shard_map/ppermute | solution.py:20
  20.0 0.0 copy-start.1
  20.0 0.0 copy-done
  20.0 0.6 %copy-done.1 = s32[1,4]{1,0:T(1,128)S(1)} copy-done((s32[1,4]{1,0:T(1,128)S(1)}, s32[1,4]{1,0:T(1,128)}, u32[]{:S(2)}) %copy-start.1) | copy-done | bytes 40
  20.6 2.5 %shard_map.127 = (f32[64,128]{1,0:T(8,128)S(1)}, f32[1024,128]{1,0:T(8,128)S(1)}, f32[128,128]{1,0:T(8,128)S(1)}, f32[128,128]{1,0:T(8,128)S(1)}, f32[128,128]{1...) custom-call(s32[1,4]{1,0:T(1,128)S(1)} %copy-done.1, ...), custom_call_target="tpu_custom_call" | custom-call | flops 1000000 | bytes 100000 | tf_op jit(solution)/shard_map/pallas_call | solution.py:440
  23.1 0.6 %shard_map.128.refs_5_.refs_2_ = f32[128,1024]{1,0:T(8,128)S(1)} custom-call(f32[64,128]{1,0:T(8,128)S(1)} %get-tuple-element.55.refs_0_, f32[1024,128]{1,0:T(8,128)S(1)} %get-tuple-element.57.refs_1_, f32[128,128]{1,0:T(8,128)S(1)} %get-tuple-element.60.refs_2_.refs_3_, bf16[128,1024]{1,0:T(8,128)(2,1)S(1)} %get-tuple-element.59.refs_3_.refs_2_.refs_5_, ...), custom_call_target="tpu_custom_call" | custom-call | flops 1000000 | bytes 100000 | tf_op jit(solution)/shard_map/pallas_call | solution.py:440
  23.7 0.0 collective-permute-done.2.refs_4_.refs_9_
  23.7 0.3 shard_map.129.refs_0_
  24.0 0.0 collective-permute-done.4.refs_1_.refs_12_
  24.0 0.6 %shard_map.130 = (f32[128,1024]{1,0:T(8,128)S(1)}, bf16[128,1024]{1,0:T(8,128)(2,1)S(1)}, f32[1,1024]{1,0:T(1,128)S(1)}) custom-call(bf16[1024,128]{1,0:T(8,128)(2,1)S(1)} %shard_map.129.refs_0_, bf16[128,1024]{1,0:T(8,128)(2,1)S(1)} %collective-permute-done.4.refs_1_.refs_12_, f32[128,1024]{1,0:T(8,128)S(1)} %shard_map.128.refs_5_.refs_2_, ...), custom_call_target="tpu_custom_call" | custom-call | flops 1000000 | bytes 100000 | tf_op jit(solution)/shard_map/pallas_call | solution.py:440
  24.7 1.3 %collective-permute-start.5 = (bf16[128,1024]{1,0:T(8,128)(2,1)S(1)}, bf16[128,1024]{1,0:T(8,128)(2,1)S(1)}, u32[]{:S(2)}, u32[]{:S(2)}) collective-permute-start(bf16[128,1024]{1,0:T(8,128)(2,1)S(1)} %get-tuple-element.65.refs_3_.refs_6_), channel_id=1, source_target_pairs={{4,0},{8,4},{12,8},{5,1},{9,5},{13,9},{6,2},{10,6},{14,10},{7,3},{... | collective-permute-start | bytes 786440 | tf_op jit(solution)/shard_map/ppermute | solution.py:20
  26.0 4.4 %collective-permute-done.6.refs_2_.refs_14_.refs_3_ = bf16[128,1024]{1,0:T(8,128)(2,1)S(1)} collective-permute-done((bf16[128,1024]{1,0:T(8,128)(2,1)S(1)}, bf16[128,1024]{1,0:T(8,128)(2,1)S(1)}, u32[]{:S(2)}, u32[]{:S(2)}) %collective-permute-start.6) | collective-permute-done | bytes 262176 | tf_op jit(solution)/shard_map/ppermute | solution.py:20
  30.3 1.7 %shard_map.133 = (bf16[128,1024]{1,0:T(8,128)(2,1)S(1)}, f32[16,128]{1,0:T(8,128)S(1)}) custom-call(f32[64,128]{1,0:T(8,128)S(1)} %get-tuple-element.55.refs_0_, f32[1024,128]{1,0:T(8,128)S(1)} %get-tuple-element.57.refs_1_, f32[128,128]{1,0:T(8,128)S(1)} %get-tuple-element.74.refs_2_, f32[128,128]{1,0:T(8,128)S(1)} %get-tuple-element.60.refs_2_.refs_3_, ...), custom_call_target="tpu_custom_call" | custom-call | flops 1000000 | bytes 100000 | tf_op jit(solution)/shard_map/pallas_call | solution.py:440
  32.0 0.1 collective-permute-start.7
  32.1 1.5 %collective-permute-start.8 = (f32[16,128]{1,0:T(8,128)S(1)}, f32[16,128]{1,0:T(8,128)S(1)}, u32[]{:S(2)}, u32[]{:S(2)}) collective-permute-start(f32[16,128]{1,0:T(8,128)S(1)} %get-tuple-element.86), channel_id=1, source_target_pairs={{0,2},{1,3},{2,0},{3,1},{4,6},{5,7},{6,4},{7,5},{8,10},{9,11},{10,... | collective-permute-start | bytes 24584 | tf_op jit(solution)/shard_map/ppermute | solution.py:469
  33.6 0.3 collective-permute-start.9
  33.9 0.9 %shard_map.131 = (f32[128,1024]{1,0:T(8,128)S(1)}, f32[128,1024]{1,0:T(8,128)S(1)}) custom-call(f32[64,128]{1,0:T(8,128)S(1)} %get-tuple-element.55.refs_0_, f32[128,128]{1,0:T(8,128)S(1)} %get-tuple-element.68.refs_1_, bf16[128,1024]{1,0:T(8,128)(2,1)S(1)} %get-tuple-element.59.refs_3_.refs_2_.refs_5_, ...), custom_call_target="tpu_custom_call" | custom-call | flops 1000000 | bytes 100000 | tf_op jit(solution)/shard_map/pallas_call | solution.py:440
  34.8 0.4 shard_map.132
  35.2 0.0 collective-permute-done.7
  35.2 0.6 %collective-permute-done.8 = f32[16,128]{1,0:T(8,128)S(1)} collective-permute-done((f32[16,128]{1,0:T(8,128)S(1)}, f32[16,128]{1,0:T(8,128)S(1)}, u32[]{:S(2)}, u32[]{:S(2)}) %collective-permute-start.8) | collective-permute-done | bytes 8224 | tf_op jit(solution)/shard_map/ppermute | solution.py:469
  35.8 0.0 collective-permute-done.9
  35.8 2.4 %collective-permute-start.11 = (f32[16,128]{1,0:T(8,128)S(1)}, f32[16,128]{1,0:T(8,128)S(1)}, u32[]{:S(2)}, u32[]{:S(2)}) collective-permute-start(f32[16,128]{1,0:T(8,128)S(1)} %add_add_fusion.refs_0_), channel_id=1, source_target_pairs={{0,4},{4,0},{8,12},{12,8},{1,5},{5,1},{9,13},{13,9},{2,6},{6,2},{1... | collective-permute-start | bytes 24584 | tf_op jit(solution)/shard_map/ppermute | solution.py:469
  38.2 0.0 collective-permute-done.5.refs_3_.refs_4_
  38.2 0.6 %shard_map.135 = bf16[96,1024]{1,0:T(8,128)(2,1)S(1)} custom-call(f32[64,128]{1,0:T(8,128)S(1)} %get-tuple-element.55.refs_0_, f32[32,128]{1,0:T(8,128)S(1)} %get-tuple-element.85.refs_1_, f32[16,128]{1,0:T(8,128)S(1)} %get-tuple-element.84.refs_2_, bf16[128,1024]{1,0:T(8,128)(2,1)S(1)} %collective-permute-done.refs_7_.refs_2_.refs_3_, ...), custom_call_target="tpu_custom_call" | custom-call | flops 1000000 | bytes 100000 | tf_op jit(solution)/shard_map/pallas_call | solution.py:440
  38.8 1.3 %collective-permute-start.10 = (bf16[96,1024]{1,0:T(8,128)(2,1)S(1)}, bf16[96,1024]{1,0:T(8,128)(2,1)S(1)}, u32[]{:S(2)}, u32[]{:S(2)}) collective-permute-start(bf16[96,1024]{1,0:T(8,128)(2,1)S(1)} %shard_map.135), channel_id=1, source_target_pairs={{4,0},{8,4},{5,1},{9,5},{6,2},{10,6},{7,3},{11,7},{20,16},{24,20},... | collective-permute-start | bytes 589832 | tf_op jit(solution)/shard_map/ppermute | solution.py:20
  40.1 0.0 collective-permute-done.11.refs_1_
  40.1 4.2 %collective-permute-start.12 = (f32[16,128]{1,0:T(8,128)S(1)}, f32[16,128]{1,0:T(8,128)S(1)}, u32[]{:S(2)}, u32[]{:S(2)}) collective-permute-start(f32[16,128]{1,0:T(8,128)S(1)} %shard_map.136.refs_0_), channel_id=1, source_target_pairs={{0,8},{4,12},{8,0},{12,4},{1,9},{5,13},{9,1},{13,5},{2,10},{6,14},... | collective-permute-start | bytes 24584 | tf_op jit(solution)/shard_map/ppermute | solution.py:469
  44.3 1.6 %shard_map.134 = (bf16[128,1024]{1,0:T(8,128)(2,1)}, bf16[128,1024]{1,0:T(8,128)(2,1)}, f32[128,1024]{1,0:T(8,128)S(1)}, f32[128,1024]{1,0:T(8,128)S(1)}) custom-call(f32[64,128]{1,0:T(8,128)S(1)} %get-tuple-element.55.refs_0_, f32[128,128]{1,0:T(8,128)S(1)} %get-tuple-element.56.refs_1_, bf16[128,1024]{1,0:T(8,128)(2,1)S(1)} %collective-permute-done.refs_7_.refs_2_.refs_3_, ...), custom_call_target="tpu_custom_call" | custom-call | flops 1000000 | bytes 100000 | tf_op jit(solution)/shard_map/pallas_call | solution.py:440
  45.9 3.3 %collective-permute-done.12.refs_1_ = f32[16,128]{1,0:T(8,128)S(1)} collective-permute-done((f32[16,128]{1,0:T(8,128)S(1)}, f32[16,128]{1,0:T(8,128)S(1)}, u32[]{:S(2)}, u32[]{:S(2)}) %collective-permute-start.12) | collective-permute-done | bytes 8224 | tf_op jit(solution)/shard_map/ppermute | solution.py:469
  49.2 0.6 %shard_map.137 = (f32[8,128]{1,0:T(8,128)}, f32[8,8]{1,0:T(8,128)}) custom-call(f32[16,128]{1,0:T(8,128)S(1)} %shard_map.136.refs_0_, f32[16,128]{1,0:T(8,128)S(1)} %collective-permute-done.12.refs_1_), custom_call_target="tpu_custom_call" | custom-call | flops 1000000 | bytes 100000 | tf_op jit(solution)/shard_map/pallas_call | solution.py:440
  49.8 0.0 collective-permute-done.10.refs_4_
  49.8 1.3 %shard_map.138 = (bf16[128,1024]{1,0:T(8,128)(2,1)}, bf16[128,1024]{1,0:T(8,128)(2,1)}) custom-call(bf16[1024,96]{1,0:T(8,128)(2,1)S(1)} %get-tuple-element.82.refs_8_.refs_0_, f32[1024,96]{1,0:T(8,128)S(1)} %get-tuple-element.83.refs_1_, f32[16,128]{1,0:T(8,128)S(1)} %get-tuple-element.84.refs_2_, ...), custom_call_target="tpu_custom_call" | custom-call | flops 1000000 | bytes 100000 | tf_op jit(solution)/shard_map/pallas_call | solution.py:440
  (2 shorter events, 0.0 us)
Async XLA Ops:
  0.6 11.9 %collective-permute-start.1 = (bf16[128,1024]{1,0:T(8,128)(2,1)}, bf16[128,1024]{1,0:T(8,128)(2,1)S(1)}, u32[]{:S(2)}, u32[]{:S(2)}) collective-permute-start(bf16[128,1024]{1,0:T(8,128)(2,1)} %bitcast.13), channel_id=1, source_target_pairs={{0,4},{4,8},{8,12},{1,5},{5,9},{9,13},{2,6},{6,10},{10,14},{3,7},{... | collective-permute-start | bytes 786440 | tf_op jit(solution)/shard_map/ppermute | solution.py:20
  5.6 14.4 %copy-start = (f32[8,8]{1,0:T(8,128)S(1)}, f32[8,8]{1,0:T(8,128)}, u32[]{:S(2)}) copy-start(f32[8,8]{1,0:T(8,128)} %refs_1_.1) | copy-start | bytes 772
  5.6 11.5 %collective-permute-start.3 = (bf16[128,1024]{1,0:T(8,128)(2,1)}, bf16[128,1024]{1,0:T(8,128)(2,1)S(1)}, u32[]{:S(2)}, u32[]{:S(2)}) collective-permute-start(bf16[128,1024]{1,0:T(8,128)(2,1)} %bitcast.15), channel_id=1, source_target_pairs={{0,4},{4,8},{8,12},{1,5},{5,9},{9,13},{2,6},{6,10},{10,14},{3,7},{... | collective-permute-start | bytes 786440 | tf_op jit(solution)/shard_map/ppermute | solution.py:20
  9.1 9.6 %collective-permute-start = (bf16[128,1024]{1,0:T(8,128)(2,1)}, bf16[128,1024]{1,0:T(8,128)(2,1)S(1)}, u32[]{:S(2)}, u32[]{:S(2)}) collective-permute-start(bf16[128,1024]{1,0:T(8,128)(2,1)} %bitcast.11), channel_id=1, source_target_pairs={{4,0},{8,4},{12,8},{5,1},{9,5},{13,9},{6,2},{10,6},{14,10},{7,3},{... | collective-permute-start | bytes 786440 | tf_op jit(solution)/shard_map/ppermute | solution.py:20
  12.6 11.1 %collective-permute-start.2 = (bf16[128,1024]{1,0:T(8,128)(2,1)S(1)}, bf16[128,1024]{1,0:T(8,128)(2,1)S(1)}, u32[]{:S(2)}, u32[]{:S(2)}) collective-permute-start(bf16[128,1024]{1,0:T(8,128)(2,1)S(1)} %collective-permute-done.1.refs_4_.refs_8_.refs_5_), channel_id=1, source_target_pairs={{4,8},{8,12},{5,9},{9,13},{6,10},{10,14},{7,11},{11,15},{20,24},{2... | collective-permute-start | bytes 786440 | tf_op jit(solution)/shard_map/ppermute | solution.py:20
  17.1 7.0 %collective-permute-start.4 = (bf16[128,1024]{1,0:T(8,128)(2,1)S(1)}, bf16[128,1024]{1,0:T(8,128)(2,1)S(1)}, u32[]{:S(2)}, u32[]{:S(2)}) collective-permute-start(bf16[128,1024]{1,0:T(8,128)(2,1)S(1)} %collective-permute-done.3.refs_5_.refs_11_.refs_6_), channel_id=1, source_target_pairs={{4,8},{8,12},{5,9},{9,13},{6,10},{10,14},{7,11},{11,15},{20,24},{2... | collective-permute-start | bytes 786440 | tf_op jit(solution)/shard_map/ppermute | solution.py:20
  18.7 11.7 %collective-permute-start.6 = (bf16[128,1024]{1,0:T(8,128)(2,1)S(1)}, bf16[128,1024]{1,0:T(8,128)(2,1)S(1)}, u32[]{:S(2)}, u32[]{:S(2)}) collective-permute-start(bf16[128,1024]{1,0:T(8,128)(2,1)S(1)} %collective-permute-done.refs_7_.refs_2_.refs_3_), channel_id=1, source_target_pairs={{4,0},{8,4},{5,1},{9,5},{6,2},{10,6},{7,3},{11,7},{20,16},{24,20},... | collective-permute-start | bytes 786440 | tf_op jit(solution)/shard_map/ppermute | solution.py:20
  20.0 0.7 %copy-start.1 = (s32[1,4]{1,0:T(1,128)S(1)}, s32[1,4]{1,0:T(1,128)}, u32[]{:S(2)}) copy-start(s32[1,4]{1,0:T(1,128)} %refs_0_.1) | copy-start | bytes 52
  24.7 13.5 %collective-permute-start.5 = (bf16[128,1024]{1,0:T(8,128)(2,1)S(1)}, bf16[128,1024]{1,0:T(8,128)(2,1)S(1)}, u32[]{:S(2)}, u32[]{:S(2)}) collective-permute-start(bf16[128,1024]{1,0:T(8,128)(2,1)S(1)} %get-tuple-element.65.refs_3_.refs_6_), channel_id=1, source_target_pairs={{4,0},{8,4},{12,8},{5,1},{9,5},{13,9},{6,2},{10,6},{14,10},{7,3},{... | collective-permute-start | bytes 786440 | tf_op jit(solution)/shard_map/ppermute | solution.py:20
  32.0 3.2 %collective-permute-start.7 = (f32[16,128]{1,0:T(8,128)S(1)}, f32[16,128]{1,0:T(8,128)S(1)}, u32[]{:S(2)}, u32[]{:S(2)}) collective-permute-start(f32[16,128]{1,0:T(8,128)S(1)} %get-tuple-element.86), channel_id=1, source_target_pairs={{0,3},{1,2},{2,1},{3,0},{4,7},{5,6},{6,5},{7,4},{8,11},{9,10},{10,... | collective-permute-start | bytes 24584 | tf_op jit(solution)/shard_map/ppermute | solution.py:469
  32.1 3.7 %collective-permute-start.8 = (f32[16,128]{1,0:T(8,128)S(1)}, f32[16,128]{1,0:T(8,128)S(1)}, u32[]{:S(2)}, u32[]{:S(2)}) collective-permute-start(f32[16,128]{1,0:T(8,128)S(1)} %get-tuple-element.86), channel_id=1, source_target_pairs={{0,2},{1,3},{2,0},{3,1},{4,6},{5,7},{6,4},{7,5},{8,10},{9,11},{10,... | collective-permute-start | bytes 24584 | tf_op jit(solution)/shard_map/ppermute | solution.py:469
  33.6 2.2 %collective-permute-start.9 = (f32[16,128]{1,0:T(8,128)S(1)}, f32[16,128]{1,0:T(8,128)S(1)}, u32[]{:S(2)}, u32[]{:S(2)}) collective-permute-start(f32[16,128]{1,0:T(8,128)S(1)} %get-tuple-element.86), channel_id=1, source_target_pairs={{0,1},{1,0},{2,3},{3,2},{4,5},{5,4},{6,7},{7,6},{8,9},{9,8},{10,11... | collective-permute-start | bytes 24584 | tf_op jit(solution)/shard_map/ppermute | solution.py:469
  35.8 4.3 %collective-permute-start.11 = (f32[16,128]{1,0:T(8,128)S(1)}, f32[16,128]{1,0:T(8,128)S(1)}, u32[]{:S(2)}, u32[]{:S(2)}) collective-permute-start(f32[16,128]{1,0:T(8,128)S(1)} %add_add_fusion.refs_0_), channel_id=1, source_target_pairs={{0,4},{4,0},{8,12},{12,8},{1,5},{5,1},{9,13},{13,9},{2,6},{6,2},{1... | collective-permute-start | bytes 24584 | tf_op jit(solution)/shard_map/ppermute | solution.py:469
  38.8 11.0 %collective-permute-start.10 = (bf16[96,1024]{1,0:T(8,128)(2,1)S(1)}, bf16[96,1024]{1,0:T(8,128)(2,1)S(1)}, u32[]{:S(2)}, u32[]{:S(2)}) collective-permute-start(bf16[96,1024]{1,0:T(8,128)(2,1)S(1)} %shard_map.135), channel_id=1, source_target_pairs={{4,0},{8,4},{5,1},{9,5},{6,2},{10,6},{7,3},{11,7},{20,16},{24,20},... | collective-permute-start | bytes 589832 | tf_op jit(solution)/shard_map/ppermute | solution.py:20
  40.1 9.1 %collective-permute-start.12 = (f32[16,128]{1,0:T(8,128)S(1)}, f32[16,128]{1,0:T(8,128)S(1)}, u32[]{:S(2)}, u32[]{:S(2)}) collective-permute-start(f32[16,128]{1,0:T(8,128)S(1)} %shard_map.136.refs_0_), channel_id=1, source_target_pairs={{0,8},{4,12},{8,0},{12,4},{1,9},{5,13},{9,1},{13,5},{2,10},{6,14},... | collective-permute-start | bytes 24584 | tf_op jit(solution)/shard_map/ppermute | solution.py:469

commit v22 on v19

--- a/solution.py
+++ b/solution.py
@@ -335,24 +335,23 @@
         copy.wait()
 
 
-def message_kernel(hops, heads, scaling, *refs):
-    table, mask, late, query, grad, key, value, out = refs
-    tail, cut, width = mask.shape[0], out.shape[0], query.shape[1] // heads
-    pair = Pair(mask, table, heads, hops, True)
+def message_kernel(heads, *refs):
+    weights, slopes, late, query, grad, value, out = refs
+    cut, width = out.shape[0], query.shape[1] // heads
+    tail = query.shape[0] - cut
     is_late = late[8:9, :width] > 0.5
 
     def scores(head):
         cols = columns(head, width)
-        score = contract(key[cut:, cols], query[:, cols], 1, 1)
-        return score, contract(value[cut:, cols], grad[:, cols], 1, 1)
+        return contract(value[cut:, cols], grad[:, cols], 1, 1)
 
     def choose(head, found):
-        cols = columns(head, width)
-        half = pair.half_logits(found[0], head, scaling)
-        tanh = jnp.tanh(half)
-        rounded = (found[1] * (slope_of(half, tanh) * pair.mask)).astype(BF16)
-        weights = ((half + half * tanh) * pair.mask).astype(BF16)
-        parts = [contract(rounded, query[:, cols], 1, 0), contract(weights, grad[:, cols], 1, 0)]
+        cols, lines = columns(head, width), columns(head, tail)
+        rounded = (found * slopes[lines, :]).astype(BF16)
+        parts = [
+            contract(rounded, query[:, cols], 1, 0),
+            contract(weights[lines, :], grad[:, cols], 1, 0),
+        ]
         for at, part in enumerate(parts):
             lines = slice(at * tail, (at + 1) * tail)
             out[lines, cols] = jnp.where(is_late, part, grad[lines, cols].astype(F32)).astype(BF16)
@@ -364,10 +363,11 @@
 def slopes_kernel(hops, heads, scaling, table, mask, query, key, weights, slopes):
     pair = Pair(mask, table, heads, hops, True)
     rows, cut, width = mask.shape[0], mask.shape[1], query.shape[1] // heads
+    first = key.shape[0] - rows
 
     def scores(head):
         cols = columns(head, width)
-        return contract(key[:, cols], query[:cut, cols], 1, 1)
+        return contract(key[first:, cols], query[:cut, cols], 1, 1)
 
     def derive(head, found):
         half = pair.half_logits(found, head, scaling)
@@ -550,6 +550,11 @@
         [wide] * 2,
         key_operands(0),
     )
+    sent_tables = on_device(
+        partial(slopes_kernel, reach, heads, scaling),
+        [jax.ShapeDtypeStruct((heads * (rows - cut), rows), kind) for kind in (BF16, F32)],
+        (table, sender_mask, later_queries[reach - 1], keys[1]),
+    )
     far_tables = on_device(
         partial(slopes_kernel, reach, heads, scaling),
         [jax.ShapeDtypeStruct((heads * rows, cut), kind) for kind in (BF16, F32)],
@@ -559,9 +564,9 @@
         arrived, *pieces = lax.optimization_barrier((later_grads[hops], *pieces))
         if hops + 1 == reach:
             (arrived,) = on_device(
-                partial(message_kernel, reach, heads, scaling),
+                partial(message_kernel, heads),
                 [jax.ShapeDtypeStruct((cut, features), BF16)],
-                (table, sender_mask, late, later_queries[hops], arrived, keys[1], values[1]),
+                (*sent_tables, late, later_queries[hops], arrived, values[1]),
                 ahead=[key_grads[0], far_tables[0]],
             )
         later_grads.append(passed_along(arrived, "ctx", -1, hops + 1))

time: 49.1 us -> 49 us (level)
    pallas_call x11 -> x12, Pallas kernels: 11.1 us -> 11.3 us  [on_device(): pl.pallas_call(body, out_shape=outs, in_specs=[pl.BlockSpec(memory_space=...]
  transfers between devices with their start and end apart: 14 -> 14, of which waited for: 8 -> 8; matrix products, arithmetic and copies ran while one was open for 0% -> 0% of each run, Pallas kernels for 20% -> 21%
where the time goes in v22:
time: 49 us; the launch traced here: 48.7 us
  starting transfers between devices  22 us (45%)
  waiting for transfers between devices  13.8 us (28%)
  Pallas kernels  11.3 us (23%)
  between operations  0.84 us (2%)
  local copies, waits for them, and re-layouts  0.64 us (1%)
    ppermute x8, starting transfers between devices, passed_along(): lax.ppermute(array, axis, [(i, i + by) for i in range(first, last + 1)])  14.9 us
    ppermute x8, waiting for transfers between devices, passed_along(): lax.ppermute(array, axis, [(i, i + by) for i in range(first, last + 1)])  13.5 us
    pallas_call x12, Pallas kernels, on_device(): pl.pallas_call(body, out_shape=outs, in_specs=[pl.BlockSpec(memory_space=...  11.3 us
    ppermute x6, starting transfers between devices, exchanged(): lax.ppermute(array, axis, [(i, i ^ distance) for i in range(size)])  7.1 us
  transfers between devices with their start and end apart: 14, of which 8 were waited for; matrix products, arithmetic and copies ran while one was open for 0% of the time, Pallas kernels for 21%

profile of v22, /device:TPU:0, one launch (start us, length us, event | category | flops | bytes accessed | tf_op | source)
XLA Modules:
  0.0 48.7 jit_solution(2153567002925462872)
XLA Ops:
  0.6 4.9 %collective-permute-start.1 = (bf16[128,1024]{1,0:T(8,128)(2,1)}, bf16[128,1024]{1,0:T(8,128)(2,1)S(1)}, u32[]{:S(2)}, u32[]{:S(2)}) collective-permute-start(bf16[128,1024]{1,0:T(8,128)(2,1)} %bitcast.13), channel_id=1, source_target_pairs={{0,4},{4,8},{8,12},{1,5},{5,9},{9,13},{2,6},{6,10},{10,14},{3,7},{... | collective-permute-start | bytes 786440 | tf_op jit(solution)/shard_map/ppermute | solution.py:19
  5.6 0.0 copy-start
  5.6 3.5 %collective-permute-start.3 = (bf16[128,1024]{1,0:T(8,128)(2,1)}, bf16[128,1024]{1,0:T(8,128)(2,1)S(1)}, u32[]{:S(2)}, u32[]{:S(2)}) collective-permute-start(bf16[128,1024]{1,0:T(8,128)(2,1)} %bitcast.15), channel_id=1, source_target_pairs={{0,4},{4,8},{8,12},{1,5},{5,9},{9,13},{2,6},{6,10},{10,14},{3,7},{... | collective-permute-start | bytes 786440 | tf_op jit(solution)/shard_map/ppermute | solution.py:19
  9.1 1.3 %collective-permute-start = (bf16[128,1024]{1,0:T(8,128)(2,1)}, bf16[128,1024]{1,0:T(8,128)(2,1)S(1)}, u32[]{:S(2)}, u32[]{:S(2)}) collective-permute-start(bf16[128,1024]{1,0:T(8,128)(2,1)} %bitcast.11), channel_id=1, source_target_pairs={{4,0},{8,4},{12,8},{5,1},{9,5},{13,9},{6,2},{10,6},{14,10},{7,3},{... | collective-permute-start | bytes 786440 | tf_op jit(solution)/shard_map/ppermute | solution.py:19
  10.4 2.2 %collective-permute-done.1.refs_4_.refs_8_.refs_3_ = bf16[128,1024]{1,0:T(8,128)(2,1)S(1)} collective-permute-done((bf16[128,1024]{1,0:T(8,128)(2,1)}, bf16[128,1024]{1,0:T(8,128)(2,1)S(1)}, u32[]{:S(2)}, u32[]{:S(2)}) %collective-permute-start.1) | collective-permute-done | bytes 262176 | tf_op jit(solution)/shard_map/ppermute | solution.py:19
  12.6 0.7 %collective-permute-start.2 = (bf16[128,1024]{1,0:T(8,128)(2,1)S(1)}, bf16[128,1024]{1,0:T(8,128)(2,1)S(1)}, u32[]{:S(2)}, u32[]{:S(2)}) collective-permute-start(bf16[128,1024]{1,0:T(8,128)(2,1)S(1)} %collective-permute-done.1.refs_4_.refs_8_.refs_3_), channel_id=1, source_target_pairs={{4,8},{8,12},{5,9},{9,13},{6,10},{10,14},{7,11},{11,15},{20,24},{2... | collective-permute-start | bytes 786440 | tf_op jit(solution)/shard_map/ppermute | solution.py:19
  13.3 3.8 %collective-permute-done.3.refs_5_.refs_11_ = bf16[128,1024]{1,0:T(8,128)(2,1)S(1)} collective-permute-done((bf16[128,1024]{1,0:T(8,128)(2,1)}, bf16[128,1024]{1,0:T(8,128)(2,1)S(1)}, u32[]{:S(2)}, u32[]{:S(2)}) %collective-permute-start.3) | collective-permute-done | bytes 262176 | tf_op jit(solution)/shard_map/ppermute | solution.py:19
  17.1 0.7 %collective-permute-start.4 = (bf16[128,1024]{1,0:T(8,128)(2,1)S(1)}, bf16[128,1024]{1,0:T(8,128)(2,1)S(1)}, u32[]{:S(2)}, u32[]{:S(2)}) collective-permute-start(bf16[128,1024]{1,0:T(8,128)(2,1)S(1)} %collective-permute-done.3.refs_5_.refs_11_), channel_id=1, source_target_pairs={{4,8},{8,12},{5,9},{9,13},{6,10},{10,14},{7,11},{11,15},{20,24},{2... | collective-permute-start | bytes 786440 | tf_op jit(solution)/shard_map/ppermute | solution.py:19
  17.7 1.0 %collective-permute-done.refs_7_.refs_2_.refs_3_ = bf16[128,1024]{1,0:T(8,128)(2,1)S(1)} collective-permute-done((bf16[128,1024]{1,0:T(8,128)(2,1)}, bf16[128,1024]{1,0:T(8,128)(2,1)S(1)}, u32[]{:S(2)}, u32[]{:S(2)}) %collective-permute-start) | collective-permute-done | bytes 262176 | tf_op jit(solution)/shard_map/ppermute | solution.py:19
  18.7 1.3 %collective-permute-start.6 = (bf16[128,1024]{1,0:T(8,128)(2,1)S(1)}, bf16[128,1024]{1,0:T(8,128)(2,1)S(1)}, u32[]{:S(2)}, u32[]{:S(2)}) collective-permute-start(bf16[128,1024]{1,0:T(8,128)(2,1)S(1)} %collective-permute-done.refs_7_.refs_2_.refs_3_), channel_id=1, source_target_pairs={{4,0},{8,4},{5,1},{9,5},{6,2},{10,6},{7,3},{11,7},{20,16},{24,20},... | collective-permute-start | bytes 786440 | tf_op jit(solution)/shard_map/ppermute | solution.py:19
  20.0 0.0 copy-start.1
  20.0 0.0 copy-done
  20.0 0.6 %copy-done.1 = s32[1,4]{1,0:T(1,128)S(1)} copy-done((s32[1,4]{1,0:T(1,128)S(1)}, s32[1,4]{1,0:T(1,128)}, u32[]{:S(2)}) %copy-start.1) | copy-done | bytes 40
  20.6 2.5 %shard_map.127 = (f32[64,128]{1,0:T(8,128)S(1)}, f32[1024,128]{1,0:T(8,128)S(1)}, f32[128,128]{1,0:T(8,128)S(1)}, f32[128,128]{1,0:T(8,128)S(1)}, f32[128,128]{1...) custom-call(s32[1,4]{1,0:T(1,128)S(1)} %copy-done.1, ...), custom_call_target="tpu_custom_call" | custom-call | flops 1000000 | bytes 100000 | tf_op jit(solution)/shard_map/pallas_call | solution.py:435
  23.1 0.6 %shard_map.128.refs_5_.refs_2_ = f32[128,1024]{1,0:T(8,128)S(1)} custom-call(f32[64,128]{1,0:T(8,128)S(1)} %get-tuple-element.50.refs_0_, f32[1024,128]{1,0:T(8,128)S(1)} %get-tuple-element.52.refs_1_, f32[128,128]{1,0:T(8,128)S(1)} %get-tuple-element.55.refs_2_.refs_3_, bf16[128,1024]{1,0:T(8,128)(2,1)S(1)} %get-tuple-element.54.refs_3_.refs_2_.refs_5_, ...), custom_call_target="tpu_custom_call" | custom-call | flops 1000000 | bytes 100000 | tf_op jit(solution)/shard_map/pallas_call | solution.py:435
  23.7 0.0 collective-permute-done.2.refs_4_.refs_9_
  23.7 0.3 shard_map.129.refs_0_
  24.0 0.0 collective-permute-done.4.refs_1_.refs_12_
  24.0 0.6 %shard_map.130 = (f32[128,1024]{1,0:T(8,128)S(1)}, bf16[128,1024]{1,0:T(8,128)(2,1)S(1)}, f32[1,1024]{1,0:T(1,128)S(1)}) custom-call(bf16[1024,128]{1,0:T(8,128)(2,1)S(1)} %shard_map.129.refs_0_, bf16[128,1024]{1,0:T(8,128)(2,1)S(1)} %collective-permute-done.4.refs_1_.refs_12_, f32[128,1024]{1,0:T(8,128)S(1)} %shard_map.128.refs_5_.refs_2_, ...), custom_call_target="tpu_custom_call" | custom-call | flops 1000000 | bytes 100000 | tf_op jit(solution)/shard_map/pallas_call | solution.py:435
  24.7 1.3 %collective-permute-start.5 = (bf16[128,1024]{1,0:T(8,128)(2,1)S(1)}, bf16[128,1024]{1,0:T(8,128)(2,1)S(1)}, u32[]{:S(2)}, u32[]{:S(2)}) collective-permute-start(bf16[128,1024]{1,0:T(8,128)(2,1)S(1)} %get-tuple-element.60.refs_3_.refs_6_), channel_id=1, source_target_pairs={{4,0},{8,4},{12,8},{5,1},{9,5},{13,9},{6,2},{10,6},{14,10},{7,3},{... | collective-permute-start | bytes 786440 | tf_op jit(solution)/shard_map/ppermute | solution.py:19
  26.0 4.4 %collective-permute-done.6.refs_14_.refs_2_.refs_3_ = bf16[128,1024]{1,0:T(8,128)(2,1)S(1)} collective-permute-done((bf16[128,1024]{1,0:T(8,128)(2,1)S(1)}, bf16[128,1024]{1,0:T(8,128)(2,1)S(1)}, u32[]{:S(2)}, u32[]{:S(2)}) %collective-permute-start.6) | collective-permute-done | bytes 262176 | tf_op jit(solution)/shard_map/ppermute | solution.py:19
  30.3 1.7 %shard_map.132 = (bf16[128,1024]{1,0:T(8,128)(2,1)S(1)}, f32[16,128]{1,0:T(8,128)S(1)}) custom-call(f32[64,128]{1,0:T(8,128)S(1)} %get-tuple-element.50.refs_0_, f32[1024,128]{1,0:T(8,128)S(1)} %get-tuple-element.52.refs_1_, f32[128,128]{1,0:T(8,128)S(1)} %get-tuple-element.67.refs_2_, f32[128,128]{1,0:T(8,128)S(1)} %get-tuple-element.55.refs_2_.refs_3_, ...), custom_call_target="tpu_custom_call" | custom-call | flops 1000000 | bytes 100000 | tf_op jit(solution)/shard_map/pallas_call | solution.py:435
  32.0 0.1 collective-permute-start.9
  32.1 1.6 %collective-permute-start.8 = (f32[16,128]{1,0:T(8,128)S(1)}, f32[16,128]{1,0:T(8,128)S(1)}, u32[]{:S(2)}, u32[]{:S(2)}) collective-permute-start(f32[16,128]{1,0:T(8,128)S(1)} %get-tuple-element.84), channel_id=1, source_target_pairs={{0,2},{1,3},{2,0},{3,1},{4,6},{5,7},{6,4},{7,5},{8,10},{9,11},{10,... | collective-permute-start | bytes 24584 | tf_op jit(solution)/shard_map/ppermute | solution.py:464
  33.7 0.3 collective-permute-start.7
  33.9 0.3 shard_map.135
  34.2 0.9 %shard_map.131 = (f32[128,1024]{1,0:T(8,128)S(1)}, f32[128,1024]{1,0:T(8,128)S(1)}) custom-call(f32[64,128]{1,0:T(8,128)S(1)} %get-tuple-element.50.refs_0_, f32[128,128]{1,0:T(8,128)S(1)} %get-tuple-element.63.refs_1_, bf16[128,1024]{1,0:T(8,128)(2,1)S(1)} %get-tuple-element.54.refs_3_.refs_2_.refs_5_, ...), custom_call_target="tpu_custom_call" | custom-call | flops 1000000 | bytes 100000 | tf_op jit(solution)/shard_map/pallas_call | solution.py:435
  35.1 0.4 shard_map.134
  35.5 0.0 collective-permute-done.9
  35.5 0.3 collective-permute-done.8
  35.8 0.0 collective-permute-done.7
  35.8 1.9 %collective-permute-done.5.refs_3_.refs_4_ = bf16[128,1024]{1,0:T(8,128)(2,1)S(1)} collective-permute-done((bf16[128,1024]{1,0:T(8,128)(2,1)S(1)}, bf16[128,1024]{1,0:T(8,128)(2,1)S(1)}, u32[]{:S(2)}, u32[]{:S(2)}) %collective-permute-start.5) | collective-permute-done | bytes 262176 | tf_op jit(solution)/shard_map/ppermute | solution.py:19
  37.7 0.5 %shard_map.136 = bf16[96,1024]{1,0:T(8,128)(2,1)S(1)} custom-call(bf16[256,128]{1,0:T(8,128)(2,1)S(1)} %get-tuple-element.76.refs_0_, f32[256,128]{1,0:T(8,128)S(1)} %get-tuple-element.77.refs_1_, f32[16,128]{1,0:T(8,128)S(1)} %get-tuple-element.74.refs_2_, bf16[128,1024]{1,0:T(8,128)(2,1)S(1)} %collective-permute-done.refs_7_.refs_2_.refs_3_, ...), custom_call_target="tpu_custom_call" | custom-call | flops 1000000 | bytes 100000 | tf_op jit(solution)/shard_map/pallas_call | solution.py:435
  38.2 1.3 %collective-permute-start.10 = (bf16[96,1024]{1,0:T(8,128)(2,1)S(1)}, bf16[96,1024]{1,0:T(8,128)(2,1)S(1)}, u32[]{:S(2)}, u32[]{:S(2)}) collective-permute-start(bf16[96,1024]{1,0:T(8,128)(2,1)S(1)} %shard_map.136), channel_id=1, source_target_pairs={{4,0},{8,4},{5,1},{9,5},{6,2},{10,6},{7,3},{11,7},{20,16},{24,20},... | collective-permute-start | bytes 589832 | tf_op jit(solution)/shard_map/ppermute | solution.py:19
  39.6 2.9 %collective-permute-start.13 = (f32[16,128]{1,0:T(8,128)S(1)}, f32[16,128]{1,0:T(8,128)S(1)}, u32[]{:S(2)}, u32[]{:S(2)}) collective-permute-start(f32[16,128]{1,0:T(8,128)S(1)} %add_add_fusion.refs_0_), channel_id=1, source_target_pairs={{0,12},{4,8},{8,4},{12,0},{1,13},{5,9},{9,5},{13,1},{2,14},{6,10},... | collective-permute-start | bytes 24584 | tf_op jit(solution)/shard_map/ppermute | solution.py:464
  42.5 1.8 %collective-permute-start.12 = (f32[16,128]{1,0:T(8,128)S(1)}, f32[16,128]{1,0:T(8,128)S(1)}, u32[]{:S(2)}, u32[]{:S(2)}) collective-permute-start(f32[16,128]{1,0:T(8,128)S(1)} %add_add_fusion.refs_0_), channel_id=1, source_target_pairs={{0,8},{4,12},{8,0},{12,4},{1,9},{5,13},{9,1},{13,5},{2,10},{6,14},... | collective-permute-start | bytes 24584 | tf_op jit(solution)/shard_map/ppermute | solution.py:464
  44.3 0.5 %collective-permute-start.11 = (f32[16,128]{1,0:T(8,128)S(1)}, f32[16,128]{1,0:T(8,128)S(1)}, u32[]{:S(2)}, u32[]{:S(2)}) collective-permute-start(f32[16,128]{1,0:T(8,128)S(1)} %add_add_fusion.refs_0_), channel_id=1, source_target_pairs={{0,4},{4,0},{8,12},{12,8},{1,5},{5,1},{9,13},{13,9},{2,6},{6,2},{1... | collective-permute-start | bytes 24584 | tf_op jit(solution)/shard_map/ppermute | solution.py:464
  44.8 1.6 %shard_map.133 = (bf16[128,1024]{1,0:T(8,128)(2,1)}, bf16[128,1024]{1,0:T(8,128)(2,1)}, f32[128,1024]{1,0:T(8,128)S(1)}, f32[128,1024]{1,0:T(8,128)S(1)}) custom-call(f32[64,128]{1,0:T(8,128)S(1)} %get-tuple-element.50.refs_0_, f32[128,128]{1,0:T(8,128)S(1)} %get-tuple-element.51.refs_1_, bf16[128,1024]{1,0:T(8,128)(2,1)S(1)} %collective-permute-done.refs_7_.refs_2_.refs_3_, ...), custom_call_target="tpu_custom_call" | custom-call | flops 1000000 | bytes 100000 | tf_op jit(solution)/shard_map/pallas_call | solution.py:435
  46.4 0.3 collective-permute-done.10.refs_4_
  46.6 1.3 %shard_map.137 = (bf16[128,1024]{1,0:T(8,128)(2,1)}, bf16[128,1024]{1,0:T(8,128)(2,1)}) custom-call(bf16[1024,96]{1,0:T(8,128)(2,1)S(1)} %get-tuple-element.72.refs_7_.refs_0_, f32[1024,96]{1,0:T(8,128)S(1)} %get-tuple-element.73.refs_1_, f32[16,128]{1,0:T(8,128)S(1)} %get-tuple-element.74.refs_2_, ...), custom_call_target="tpu_custom_call" | custom-call | flops 1000000 | bytes 100000 | tf_op jit(solution)/shard_map/pallas_call | solution.py:435
  48.0 0.0 collective-permute-done.13.refs_3_
  48.0 0.1 collective-permute-done.12.refs_2_
  48.1 0.0 collective-permute-done.11.refs_1_
  48.1 0.6 %shard_map.138 = (f32[8,128]{1,0:T(8,128)}, f32[8,8]{1,0:T(8,128)}) custom-call(f32[16,128]{1,0:T(8,128)S(1)} %add_add_fusion.refs_0_, f32[16,128]{1,0:T(8,128)S(1)} %collective-permute-done.11.refs_1_, f32[16,128]{1,0:T(8,128)S(1)} %collective-permute-done.12.refs_2_, f32[16,128]{1,0:T(8,128)S(1)} %collective-permute-done.13.refs_3_), custom_call_target="tpu_custom_call" | custom-call | flops 1000000 | bytes 100000 | tf_op jit(solution)/shard_map/pallas_call | solution.py:435
  (1 shorter events, 0.0 us)
Async XLA Ops:
  0.6 11.9 %collective-permute-start.1 = (bf16[128,1024]{1,0:T(8,128)(2,1)}, bf16[128,1024]{1,0:T(8,128)(2,1)S(1)}, u32[]{:S(2)}, u32[]{:S(2)}) collective-permute-start(bf16[128,1024]{1,0:T(8,128)(2,1)} %bitcast.13), channel_id=1, source_target_pairs={{0,4},{4,8},{8,12},{1,5},{5,9},{9,13},{2,6},{6,10},{10,14},{3,7},{... | collective-permute-start | bytes 786440 | tf_op jit(solution)/shard_map/ppermute | solution.py:19
  5.6 14.4 %copy-start = (f32[8,8]{1,0:T(8,128)S(1)}, f32[8,8]{1,0:T(8,128)}, u32[]{:S(2)}) copy-start(f32[8,8]{1,0:T(8,128)} %refs_1_.1) | copy-start | bytes 772
  5.6 11.5 %collective-permute-start.3 = (bf16[128,1024]{1,0:T(8,128)(2,1)}, bf16[128,1024]{1,0:T(8,128)(2,1)S(1)}, u32[]{:S(2)}, u32[]{:S(2)}) collective-permute-start(bf16[128,1024]{1,0:T(8,128)(2,1)} %bitcast.15), channel_id=1, source_target_pairs={{0,4},{4,8},{8,12},{1,5},{5,9},{9,13},{2,6},{6,10},{10,14},{3,7},{... | collective-permute-start | bytes 786440 | tf_op jit(solution)/shard_map/ppermute | solution.py:19
  9.1 9.6 %collective-permute-start = (bf16[128,1024]{1,0:T(8,128)(2,1)}, bf16[128,1024]{1,0:T(8,128)(2,1)S(1)}, u32[]{:S(2)}, u32[]{:S(2)}) collective-permute-start(bf16[128,1024]{1,0:T(8,128)(2,1)} %bitcast.11), channel_id=1, source_target_pairs={{4,0},{8,4},{12,8},{5,1},{9,5},{13,9},{6,2},{10,6},{14,10},{7,3},{... | collective-permute-start | bytes 786440 | tf_op jit(solution)/shard_map/ppermute | solution.py:19
  12.6 11.1 %collective-permute-start.2 = (bf16[128,1024]{1,0:T(8,128)(2,1)S(1)}, bf16[128,1024]{1,0:T(8,128)(2,1)S(1)}, u32[]{:S(2)}, u32[]{:S(2)}) collective-permute-start(bf16[128,1024]{1,0:T(8,128)(2,1)S(1)} %collective-permute-done.1.refs_4_.refs_8_.refs_3_), channel_id=1, source_target_pairs={{4,8},{8,12},{5,9},{9,13},{6,10},{10,14},{7,11},{11,15},{20,24},{2... | collective-permute-start | bytes 786440 | tf_op jit(solution)/shard_map/ppermute | solution.py:19
  17.1 7.0 %collective-permute-start.4 = (bf16[128,1024]{1,0:T(8,128)(2,1)S(1)}, bf16[128,1024]{1,0:T(8,128)(2,1)S(1)}, u32[]{:S(2)}, u32[]{:S(2)}) collective-permute-start(bf16[128,1024]{1,0:T(8,128)(2,1)S(1)} %collective-permute-done.3.refs_5_.refs_11_), channel_id=1, source_target_pairs={{4,8},{8,12},{5,9},{9,13},{6,10},{10,14},{7,11},{11,15},{20,24},{2... | collective-permute-start | bytes 786440 | tf_op jit(solution)/shard_map/ppermute | solution.py:19
  18.7 11.7 %collective-permute-start.6 = (bf16[128,1024]{1,0:T(8,128)(2,1)S(1)}, bf16[128,1024]{1,0:T(8,128)(2,1)S(1)}, u32[]{:S(2)}, u32[]{:S(2)}) collective-permute-start(bf16[128,1024]{1,0:T(8,128)(2,1)S(1)} %collective-permute-done.refs_7_.refs_2_.refs_3_), channel_id=1, source_target_pairs={{4,0},{8,4},{5,1},{9,5},{6,2},{10,6},{7,3},{11,7},{20,16},{24,20},... | collective-permute-start | bytes 786440 | tf_op jit(solution)/shard_map/ppermute | solution.py:19
  20.0 0.7 %copy-start.1 = (s32[1,4]{1,0:T(1,128)S(1)}, s32[1,4]{1,0:T(1,128)}, u32[]{:S(2)}) copy-start(s32[1,4]{1,0:T(1,128)} %refs_0_.1) | copy-start | bytes 52
  24.7 13.1 %collective-permute-start.5 = (bf16[128,1024]{1,0:T(8,128)(2,1)S(1)}, bf16[128,1024]{1,0:T(8,128)(2,1)S(1)}, u32[]{:S(2)}, u32[]{:S(2)}) collective-permute-start(bf16[128,1024]{1,0:T(8,128)(2,1)S(1)} %get-tuple-element.60.refs_3_.refs_6_), channel_id=1, source_target_pairs={{4,0},{8,4},{12,8},{5,1},{9,5},{13,9},{6,2},{10,6},{14,10},{7,3},{... | collective-permute-start | bytes 786440 | tf_op jit(solution)/shard_map/ppermute | solution.py:19
  32.0 3.5 %collective-permute-start.9 = (f32[16,128]{1,0:T(8,128)S(1)}, f32[16,128]{1,0:T(8,128)S(1)}, u32[]{:S(2)}, u32[]{:S(2)}) collective-permute-start(f32[16,128]{1,0:T(8,128)S(1)} %get-tuple-element.84), channel_id=1, source_target_pairs={{0,3},{1,2},{2,1},{3,0},{4,7},{5,6},{6,5},{7,4},{8,11},{9,10},{10,... | collective-permute-start | bytes 24584 | tf_op jit(solution)/shard_map/ppermute | solution.py:464
  32.1 3.7 %collective-permute-start.8 = (f32[16,128]{1,0:T(8,128)S(1)}, f32[16,128]{1,0:T(8,128)S(1)}, u32[]{:S(2)}, u32[]{:S(2)}) collective-permute-start(f32[16,128]{1,0:T(8,128)S(1)} %get-tuple-element.84), channel_id=1, source_target_pairs={{0,2},{1,3},{2,0},{3,1},{4,6},{5,7},{6,4},{7,5},{8,10},{9,11},{10,... | collective-permute-start | bytes 24584 | tf_op jit(solution)/shard_map/ppermute | solution.py:464
  33.7 2.2 %collective-permute-start.7 = (f32[16,128]{1,0:T(8,128)S(1)}, f32[16,128]{1,0:T(8,128)S(1)}, u32[]{:S(2)}, u32[]{:S(2)}) collective-permute-start(f32[16,128]{1,0:T(8,128)S(1)} %get-tuple-element.84), channel_id=1, source_target_pairs={{0,1},{1,0},{2,3},{3,2},{4,5},{5,4},{6,7},{7,6},{8,9},{9,8},{10,11... | collective-permute-start | bytes 24584 | tf_op jit(solution)/shard_map/ppermute | solution.py:464
  38.2 8.4 %collective-permute-start.10 = (bf16[96,1024]{1,0:T(8,128)(2,1)S(1)}, bf16[96,1024]{1,0:T(8,128)(2,1)S(1)}, u32[]{:S(2)}, u32[]{:S(2)}) collective-permute-start(bf16[96,1024]{1,0:T(8,128)(2,1)S(1)} %shard_map.136), channel_id=1, source_target_pairs={{4,0},{8,4},{5,1},{9,5},{6,2},{10,6},{7,3},{11,7},{20,16},{24,20},... | collective-permute-start | bytes 589832 | tf_op jit(solution)/shard_map/ppermute | solution.py:19
  39.6 8.4 %collective-permute-start.13 = (f32[16,128]{1,0:T(8,128)S(1)}, f32[16,128]{1,0:T(8,128)S(1)}, u32[]{:S(2)}, u32[]{:S(2)}) collective-permute-start(f32[16,128]{1,0:T(8,128)S(1)} %add_add_fusion.refs_0_), channel_id=1, source_target_pairs={{0,12},{4,8},{8,4},{12,0},{1,13},{5,9},{9,5},{13,1},{2,14},{6,10},... | collective-permute-start | bytes 24584 | tf_op jit(solution)/shard_map/ppermute | solution.py:464
  42.5 5.6 %collective-permute-start.12 = (f32[16,128]{1,0:T(8,128)S(1)}, f32[16,128]{1,0:T(8,128)S(1)}, u32[]{:S(2)}, u32[]{:S(2)}) collective-permute-start(f32[16,128]{1,0:T(8,128)S(1)} %add_add_fusion.refs_0_), channel_id=1, source_target_pairs={{0,8},{4,12},{8,0},{12,4},{1,9},{5,13},{9,1},{13,5},{2,10},{6,14},... | collective-permute-start | bytes 24584 | tf_op jit(solution)/shard_map/ppermute | solution.py:464
  44.3 3.8 %collective-permute-start.11 = (f32[16,128]{1,0:T(8,128)S(1)}, f32[16,128]{1,0:T(8,128)S(1)}, u32[]{:S(2)}, u32[]{:S(2)}) collective-permute-start(f32[16,128]{1,0:T(8,128)S(1)} %add_add_fusion.refs_0_), channel_id=1, source_target_pairs={{0,4},{4,0},{8,12},{12,8},{1,5},{5,1},{9,13},{13,9},{2,6},{6,2},{1... | collective-permute-start | bytes 24584 | tf_op jit(solution)/shard_map/ppermute | solution.py:464

commit v23 on v22

--- a/solution.py
+++ b/solution.py
@@ -308,8 +308,8 @@
 
 
 def gate_and_key_kernel(hops, heads, scaling, *refs):
-    attention, out_grad, gain, query_grad = refs[8:12]
-    gate_out, query_out, key_out, value_out, held, written = refs[12:]
+    attention, out_grad, gain, query_grad = refs[6:10]
+    gate_out, query_out, key_out, value_out, held, written = refs[10:]
     rows, step = attention.shape[0], 16
     part = rows // 4
     copies = []
@@ -330,7 +330,7 @@
         held[span, :] = (out_grad[span, :].astype(F32) * normed * gain_row).astype(BF16)
         if (low + step) % part == 0:
             write(held, gate_out, low + step - part)
-    add_key_grads(hops, heads, scaling, *refs[:6], refs[6:8], into(key_out, value_out))
+    add_key_grads(hops, heads, scaling, *refs[:6], (), into(key_out, value_out))
     for copy in copies:
         copy.wait()
 
@@ -545,10 +545,12 @@
         later = (later_queries[hops], later_grads[hops])
         return (table, flipped[hops], *later, key, value)
 
-    key_grads = on_device(
-        partial(next_key_kernel, 0, heads, scaling),
-        [wide] * 2,
-        key_operands(0),
+    gate_grad, query_grad, *key_grads = on_device(
+        partial(gate_and_key_kernel, 0, heads, scaling),
+        [narrow, narrow, wide, wide],
+        (*key_operands(0), attention, grad, gain, query_grad),
+        far_outs=2,
+        scratch=[pltpu.VMEM((rows, features), BF16), pltpu.SemaphoreType.DMA((8,))],
     )
     sent_tables = on_device(
         partial(slopes_kernel, reach, heads, scaling),
@@ -570,20 +572,11 @@
                 ahead=[key_grads[0], far_tables[0]],
             )
         later_grads.append(passed_along(arrived, "ctx", -1, hops + 1))
-        if hops == 1:
-            gate_grad, query_grad, *key_grads = on_device(
-                partial(gate_and_key_kernel, hops, heads, scaling),
-                [narrow, narrow, wide, wide],
-                (*key_operands(hops), *key_grads, attention, grad, gain, query_grad),
-                far_outs=2,
-                scratch=[pltpu.VMEM((rows, features), BF16), pltpu.SemaphoreType.DMA((8,))],
-            )
-        else:
-            key_grads = on_device(
-                partial(next_key_kernel, hops, heads, scaling),
-                [wide] * 2,
-                (*key_operands(hops), *key_grads),
-            )
+        key_grads = on_device(
+            partial(next_key_kernel, hops, heads, scaling),
+            [wide] * 2,
+            (*key_operands(hops), *key_grads),
+        )
     for axis, distances in rounds_of(("ctx",)):
         pieces = exchanged(added_up(pieces), axis, distances)
     key_grad, value_grad = on_device(
@@ -597,7 +590,7 @@
     gain_grad, bias_grad = on_device(
         sum_kernel,
         [jax.ShapeDtypeStruct((8, lanes), F32), jax.ShapeDtypeStruct((levels, heads), F32)],
-        pieces,
+        pieces[::-1],
     )
     return (
         query_grad[None],

time: 49 us -> 49.7 us (1.014)
  waiting for transfers between devices: 13.8 us -> 14.6 us
    ppermute x8, waiting for transfers between devices: 13.5 us -> 14.1 us  [passed_along(): lax.ppermute(array, axis, [(i, i + by) for i in range(first, last + 1)])]
where the time goes in v23:
time: 49.7 us; the launch traced here: 49.4 us
  starting transfers between devices  22 us (44%)
  waiting for transfers between devices  14.6 us (29%)
  Pallas kernels  11.3 us (23%)
  between operations  0.85 us (2%)
  local copies, waits for them, and re-layouts  0.64 us (1%)
    ppermute x8, starting transfers between devices, passed_along(): lax.ppermute(array, axis, [(i, i + by) for i in range(first, last + 1)])  14.9 us
    ppermute x8, waiting for transfers between devices, passed_along(): lax.ppermute(array, axis, [(i, i + by) for i in range(first, last + 1)])  14.1 us
    pallas_call x12, Pallas kernels, on_device(): pl.pallas_call(body, out_shape=outs, in_specs=[pl.BlockSpec(memory_space=...  11.3 us
    ppermute x6, starting transfers between devices, exchanged(): lax.ppermute(array, axis, [(i, i ^ distance) for i in range(size)])  7.11 us
  transfers between devices with their start and end apart: 14, of which 8 were waited for; matrix products, arithmetic and copies ran while one was open for 0% of the time, Pallas kernels for 21%

profile of v23, /device:TPU:0, one launch (start us, length us, event | category | flops | bytes accessed | tf_op | source)
XLA Modules:
  0.0 49.4 jit_solution(7425643879625418431)
XLA Ops:
  0.6 4.9 %collective-permute-start = (bf16[128,1024]{1,0:T(8,128)(2,1)}, bf16[128,1024]{1,0:T(8,128)(2,1)S(1)}, u32[]{:S(2)}, u32[]{:S(2)}) collective-permute-start(bf16[128,1024]{1,0:T(8,128)(2,1)} %bitcast.13), channel_id=1, source_target_pairs={{0,4},{4,8},{8,12},{1,5},{5,9},{9,13},{2,6},{6,10},{10,14},{3,7},{... | collective-permute-start | bytes 786440 | tf_op jit(solution)/shard_map/ppermute | solution.py:19
  5.6 0.0 copy-start
  5.6 3.5 %collective-permute-start.2 = (bf16[128,1024]{1,0:T(8,128)(2,1)}, bf16[128,1024]{1,0:T(8,128)(2,1)S(1)}, u32[]{:S(2)}, u32[]{:S(2)}) collective-permute-start(bf16[128,1024]{1,0:T(8,128)(2,1)} %bitcast.15), channel_id=1, source_target_pairs={{0,4},{4,8},{8,12},{1,5},{5,9},{9,13},{2,6},{6,10},{10,14},{3,7},{... | collective-permute-start | bytes 786440 | tf_op jit(solution)/shard_map/ppermute | solution.py:19
  9.1 1.3 %collective-permute-start.3 = (bf16[128,1024]{1,0:T(8,128)(2,1)}, bf16[128,1024]{1,0:T(8,128)(2,1)S(1)}, u32[]{:S(2)}, u32[]{:S(2)}) collective-permute-start(bf16[128,1024]{1,0:T(8,128)(2,1)} %bitcast.11), channel_id=1, source_target_pairs={{4,0},{8,4},{12,8},{5,1},{9,5},{13,9},{6,2},{10,6},{14,10},{7,3},{... | collective-permute-start | bytes 786440 | tf_op jit(solution)/shard_map/ppermute | solution.py:19
  10.4 2.2 %collective-permute-done.refs_4_.refs_8_.refs_3_ = bf16[128,1024]{1,0:T(8,128)(2,1)S(1)} collective-permute-done((bf16[128,1024]{1,0:T(8,128)(2,1)}, bf16[128,1024]{1,0:T(8,128)(2,1)S(1)}, u32[]{:S(2)}, u32[]{:S(2)}) %collective-permute-start) | collective-permute-done | bytes 262176 | tf_op jit(solution)/shard_map/ppermute | solution.py:19
  12.6 0.7 %collective-permute-start.1 = (bf16[128,1024]{1,0:T(8,128)(2,1)S(1)}, bf16[128,1024]{1,0:T(8,128)(2,1)S(1)}, u32[]{:S(2)}, u32[]{:S(2)}) collective-permute-start(bf16[128,1024]{1,0:T(8,128)(2,1)S(1)} %collective-permute-done.refs_4_.refs_8_.refs_3_), channel_id=1, source_target_pairs={{4,8},{8,12},{5,9},{9,13},{6,10},{10,14},{7,11},{11,15},{20,24},{2... | collective-permute-start | bytes 786440 | tf_op jit(solution)/shard_map/ppermute | solution.py:19
  13.3 3.8 %collective-permute-done.2.refs_5_.refs_11_ = bf16[128,1024]{1,0:T(8,128)(2,1)S(1)} collective-permute-done((bf16[128,1024]{1,0:T(8,128)(2,1)}, bf16[128,1024]{1,0:T(8,128)(2,1)S(1)}, u32[]{:S(2)}, u32[]{:S(2)}) %collective-permute-start.2) | collective-permute-done | bytes 262176 | tf_op jit(solution)/shard_map/ppermute | solution.py:19
  17.1 0.7 %collective-permute-start.4 = (bf16[128,1024]{1,0:T(8,128)(2,1)S(1)}, bf16[128,1024]{1,0:T(8,128)(2,1)S(1)}, u32[]{:S(2)}, u32[]{:S(2)}) collective-permute-start(bf16[128,1024]{1,0:T(8,128)(2,1)S(1)} %collective-permute-done.2.refs_5_.refs_11_), channel_id=1, source_target_pairs={{4,8},{8,12},{5,9},{9,13},{6,10},{10,14},{7,11},{11,15},{20,24},{2... | collective-permute-start | bytes 786440 | tf_op jit(solution)/shard_map/ppermute | solution.py:19
  17.7 1.0 %collective-permute-done.3.refs_7_.refs_2_.refs_3_ = bf16[128,1024]{1,0:T(8,128)(2,1)S(1)} collective-permute-done((bf16[128,1024]{1,0:T(8,128)(2,1)}, bf16[128,1024]{1,0:T(8,128)(2,1)S(1)}, u32[]{:S(2)}, u32[]{:S(2)}) %collective-permute-start.3) | collective-permute-done | bytes 262176 | tf_op jit(solution)/shard_map/ppermute | solution.py:19
  18.7 1.3 %collective-permute-start.5 = (bf16[128,1024]{1,0:T(8,128)(2,1)S(1)}, bf16[128,1024]{1,0:T(8,128)(2,1)S(1)}, u32[]{:S(2)}, u32[]{:S(2)}) collective-permute-start(bf16[128,1024]{1,0:T(8,128)(2,1)S(1)} %collective-permute-done.3.refs_7_.refs_2_.refs_3_), channel_id=1, source_target_pairs={{4,0},{8,4},{5,1},{9,5},{6,2},{10,6},{7,3},{11,7},{20,16},{24,20},... | collective-permute-start | bytes 786440 | tf_op jit(solution)/shard_map/ppermute | solution.py:19
  20.0 0.0 copy-start.1
  20.0 0.0 copy-done
  20.0 0.6 %copy-done.1 = s32[1,4]{1,0:T(1,128)S(1)} copy-done((s32[1,4]{1,0:T(1,128)S(1)}, s32[1,4]{1,0:T(1,128)}, u32[]{:S(2)}) %copy-start.1) | copy-done | bytes 40
  20.6 2.5 %shard_map.127 = (f32[64,128]{1,0:T(8,128)S(1)}, f32[1024,128]{1,0:T(8,128)S(1)}, f32[128,128]{1,0:T(8,128)S(1)}, f32[128,128]{1,0:T(8,128)S(1)}, f32[128,128]{1...) custom-call(s32[1,4]{1,0:T(1,128)S(1)} %copy-done.1, ...), custom_call_target="tpu_custom_call" | custom-call | flops 1000000 | bytes 100000 | tf_op jit(solution)/shard_map/pallas_call | solution.py:435
  23.1 0.6 %shard_map.128.refs_5_.refs_2_ = f32[128,1024]{1,0:T(8,128)S(1)} custom-call(f32[64,128]{1,0:T(8,128)S(1)} %get-tuple-element.50.refs_0_, f32[1024,128]{1,0:T(8,128)S(1)} %get-tuple-element.53.refs_1_, f32[128,128]{1,0:T(8,128)S(1)} %get-tuple-element.55.refs_2_.refs_3_, bf16[128,1024]{1,0:T(8,128)(2,1)S(1)} %get-tuple-element.52.refs_3_.refs_5_.refs_2_, ...), custom_call_target="tpu_custom_call" | custom-call | flops 1000000 | bytes 100000 | tf_op jit(solution)/shard_map/pallas_call | solution.py:435
  23.7 0.0 collective-permute-done.1.refs_4_.refs_9_
  23.7 0.3 shard_map.129.refs_0_
  24.0 0.0 collective-permute-done.4.refs_1_.refs_12_
  24.0 0.6 %shard_map.130 = (f32[128,1024]{1,0:T(8,128)S(1)}, bf16[128,1024]{1,0:T(8,128)(2,1)S(1)}, f32[1,1024]{1,0:T(1,128)S(1)}) custom-call(bf16[1024,128]{1,0:T(8,128)(2,1)S(1)} %shard_map.129.refs_0_, bf16[128,1024]{1,0:T(8,128)(2,1)S(1)} %collective-permute-done.4.refs_1_.refs_12_, f32[128,1024]{1,0:T(8,128)S(1)} %shard_map.128.refs_5_.refs_2_, ...), custom_call_target="tpu_custom_call" | custom-call | flops 1000000 | bytes 100000 | tf_op jit(solution)/shard_map/pallas_call | solution.py:435
  24.7 1.3 %collective-permute-start.6 = (bf16[128,1024]{1,0:T(8,128)(2,1)S(1)}, bf16[128,1024]{1,0:T(8,128)(2,1)S(1)}, u32[]{:S(2)}, u32[]{:S(2)}) collective-permute-start(bf16[128,1024]{1,0:T(8,128)(2,1)S(1)} %get-tuple-element.60.refs_6_.refs_3_), channel_id=1, source_target_pairs={{4,0},{8,4},{12,8},{5,1},{9,5},{13,9},{6,2},{10,6},{14,10},{7,3},{... | collective-permute-start | bytes 786440 | tf_op jit(solution)/shard_map/ppermute | solution.py:19
  26.0 4.4 %collective-permute-done.5.refs_14_.refs_2_.refs_3_ = bf16[128,1024]{1,0:T(8,128)(2,1)S(1)} collective-permute-done((bf16[128,1024]{1,0:T(8,128)(2,1)S(1)}, bf16[128,1024]{1,0:T(8,128)(2,1)S(1)}, u32[]{:S(2)}, u32[]{:S(2)}) %collective-permute-start.5) | collective-permute-done | bytes 262176 | tf_op jit(solution)/shard_map/ppermute | solution.py:19
  30.3 1.7 %shard_map.131 = (bf16[128,1024]{1,0:T(8,128)(2,1)S(1)}, f32[16,128]{1,0:T(8,128)S(1)}) custom-call(f32[64,128]{1,0:T(8,128)S(1)} %get-tuple-element.50.refs_0_, f32[1024,128]{1,0:T(8,128)S(1)} %get-tuple-element.53.refs_1_, f32[128,128]{1,0:T(8,128)S(1)} %get-tuple-element.64.refs_2_, f32[128,128]{1,0:T(8,128)S(1)} %get-tuple-element.55.refs_2_.refs_3_, ...), custom_call_target="tpu_custom_call" | custom-call | flops 1000000 | bytes 100000 | tf_op jit(solution)/shard_map/pallas_call | solution.py:435
  32.0 0.1 collective-permute-start.7
  32.1 1.6 %collective-permute-start.8 = (f32[16,128]{1,0:T(8,128)S(1)}, f32[16,128]{1,0:T(8,128)S(1)}, u32[]{:S(2)}, u32[]{:S(2)}) collective-permute-start(f32[16,128]{1,0:T(8,128)S(1)} %get-tuple-element.84), channel_id=1, source_target_pairs={{0,2},{1,3},{2,0},{3,1},{4,6},{5,7},{6,4},{7,5},{8,10},{9,11},{10,... | collective-permute-start | bytes 24584 | tf_op jit(solution)/shard_map/ppermute | solution.py:464
  33.6 0.3 collective-permute-start.9
  33.9 0.3 shard_map.134
  34.2 1.7 %shard_map.132 = (bf16[128,1024]{1,0:T(8,128)(2,1)}, bf16[128,1024]{1,0:T(8,128)(2,1)}, f32[128,1024]{1,0:T(8,128)S(1)}, f32[128,1024]{1,0:T(8,128)S(1)}) custom-call(f32[64,128]{1,0:T(8,128)S(1)} %get-tuple-element.50.refs_0_, f32[128,128]{1,0:T(8,128)S(1)} %get-tuple-element.51.refs_1_, bf16[128,1024]{1,0:T(8,128)(2,1)S(1)} %get-tuple-element.52.refs_3_.refs_5_.refs_2_, ...), custom_call_target="tpu_custom_call" | custom-call | flops 1000000 | bytes 100000 | tf_op jit(solution)/shard_map/pallas_call | solution.py:435
  35.9 0.4 shard_map.133
  36.3 0.0 collective-permute-done.7
  36.3 0.0 collective-permute-done.8
  36.3 0.4 collective-permute-done.9
  36.7 1.0 %collective-permute-done.6.refs_4_.refs_3_ = bf16[128,1024]{1,0:T(8,128)(2,1)S(1)} collective-permute-done((bf16[128,1024]{1,0:T(8,128)(2,1)S(1)}, bf16[128,1024]{1,0:T(8,128)(2,1)S(1)}, u32[]{:S(2)}, u32[]{:S(2)}) %collective-permute-start.6) | collective-permute-done | bytes 262176 | tf_op jit(solution)/shard_map/ppermute | solution.py:19
  37.7 0.5 %shard_map.135 = bf16[96,1024]{1,0:T(8,128)(2,1)S(1)} custom-call(bf16[256,128]{1,0:T(8,128)(2,1)S(1)} %get-tuple-element.73.refs_0_, f32[256,128]{1,0:T(8,128)S(1)} %get-tuple-element.74.refs_1_, f32[16,128]{1,0:T(8,128)S(1)} %get-tuple-element.71.refs_2_, bf16[128,1024]{1,0:T(8,128)(2,1)S(1)} %collective-permute-done.3.refs_7_.refs_2_.refs_3_, ...), custom_call_target="tpu_custom_call" | custom-call | flops 1000000 | bytes 100000 | tf_op jit(solution)/shard_map/pallas_call | solution.py:435
  38.2 1.3 %collective-permute-start.10 = (bf16[96,1024]{1,0:T(8,128)(2,1)S(1)}, bf16[96,1024]{1,0:T(8,128)(2,1)S(1)}, u32[]{:S(2)}, u32[]{:S(2)}) collective-permute-start(bf16[96,1024]{1,0:T(8,128)(2,1)S(1)} %shard_map.135), channel_id=1, source_target_pairs={{4,0},{8,4},{5,1},{9,5},{6,2},{10,6},{7,3},{11,7},{20,16},{24,20},... | collective-permute-start | bytes 589832 | tf_op jit(solution)/shard_map/ppermute | solution.py:19
  39.6 3.8 %collective-permute-start.11 = (f32[16,128]{1,0:T(8,128)S(1)}, f32[16,128]{1,0:T(8,128)S(1)}, u32[]{:S(2)}, u32[]{:S(2)}) collective-permute-start(f32[16,128]{1,0:T(8,128)S(1)} %add_add_fusion.refs_3_), channel_id=1, source_target_pairs={{0,12},{4,8},{8,4},{12,0},{1,13},{5,9},{9,5},{13,1},{2,14},{6,10},... | collective-permute-start | bytes 24584 | tf_op jit(solution)/shard_map/ppermute | solution.py:464
  43.4 0.9 %collective-permute-start.12 = (f32[16,128]{1,0:T(8,128)S(1)}, f32[16,128]{1,0:T(8,128)S(1)}, u32[]{:S(2)}, u32[]{:S(2)}) collective-permute-start(f32[16,128]{1,0:T(8,128)S(1)} %add_add_fusion.refs_3_), channel_id=1, source_target_pairs={{0,8},{4,12},{8,0},{12,4},{1,9},{5,13},{9,1},{13,5},{2,10},{6,14},... | collective-permute-start | bytes 24584 | tf_op jit(solution)/shard_map/ppermute | solution.py:464
  44.3 0.5 collective-permute-start.13
  44.8 0.8 %shard_map.136 = (f32[128,1024]{1,0:T(8,128)S(1)}, f32[128,1024]{1,0:T(8,128)S(1)}) custom-call(f32[64,128]{1,0:T(8,128)S(1)} %get-tuple-element.50.refs_0_, f32[128,128]{1,0:T(8,128)S(1)} %get-tuple-element.78.refs_1_, bf16[128,1024]{1,0:T(8,128)(2,1)S(1)} %collective-permute-done.3.refs_7_.refs_2_.refs_3_, ...), custom_call_target="tpu_custom_call" | custom-call | flops 1000000 | bytes 100000 | tf_op jit(solution)/shard_map/pallas_call | solution.py:435
  45.6 1.7 %collective-permute-done.10.refs_4_ = bf16[96,1024]{1,0:T(8,128)(2,1)S(1)} collective-permute-done((bf16[96,1024]{1,0:T(8,128)(2,1)S(1)}, bf16[96,1024]{1,0:T(8,128)(2,1)S(1)}, u32[]{:S(2)}, u32[]{:S(2)}) %collective-permute-start.10) | collective-permute-done | bytes 196640 | tf_op jit(solution)/shard_map/ppermute | solution.py:19
  47.3 1.3 %shard_map.137 = (bf16[128,1024]{1,0:T(8,128)(2,1)}, bf16[128,1024]{1,0:T(8,128)(2,1)}) custom-call(bf16[1024,96]{1,0:T(8,128)(2,1)S(1)} %get-tuple-element.69.refs_7_.refs_0_, f32[1024,96]{1,0:T(8,128)S(1)} %get-tuple-element.70.refs_1_, f32[16,128]{1,0:T(8,128)S(1)} %get-tuple-element.71.refs_2_, ...), custom_call_target="tpu_custom_call" | custom-call | flops 1000000 | bytes 100000 | tf_op jit(solution)/shard_map/pallas_call | solution.py:435
  48.6 0.0 collective-permute-done.11.refs_0_
  48.7 0.1 collective-permute-done.12.refs_1_
  48.8 0.0 collective-permute-done.13.refs_2_
  48.8 0.6 %shard_map.138 = (f32[8,128]{1,0:T(8,128)}, f32[8,8]{1,0:T(8,128)}) custom-call(f32[16,128]{1,0:T(8,128)S(1)} %collective-permute-done.11.refs_0_, f32[16,128]{1,0:T(8,128)S(1)} %collective-permute-done.12.refs_1_, f32[16,128]{1,0:T(8,128)S(1)} %collective-permute-done.13.refs_2_, f32[16,128]{1,0:T(8,128)S(1)} %add_add_fusion.refs_3_), custom_call_target="tpu_custom_call" | custom-call | flops 1000000 | bytes 100000 | tf_op jit(solution)/shard_map/pallas_call | solution.py:435
  (1 shorter events, 0.0 us)
Async XLA Ops:
  0.6 11.9 %collective-permute-start = (bf16[128,1024]{1,0:T(8,128)(2,1)}, bf16[128,1024]{1,0:T(8,128)(2,1)S(1)}, u32[]{:S(2)}, u32[]{:S(2)}) collective-permute-start(bf16[128,1024]{1,0:T(8,128)(2,1)} %bitcast.13), channel_id=1, source_target_pairs={{0,4},{4,8},{8,12},{1,5},{5,9},{9,13},{2,6},{6,10},{10,14},{3,7},{... | collective-permute-start | bytes 786440 | tf_op jit(solution)/shard_map/ppermute | solution.py:19
  5.6 14.4 %copy-start = (f32[8,8]{1,0:T(8,128)S(1)}, f32[8,8]{1,0:T(8,128)}, u32[]{:S(2)}) copy-start(f32[8,8]{1,0:T(8,128)} %refs_1_.1) | copy-start | bytes 772
  5.6 11.5 %collective-permute-start.2 = (bf16[128,1024]{1,0:T(8,128)(2,1)}, bf16[128,1024]{1,0:T(8,128)(2,1)S(1)}, u32[]{:S(2)}, u32[]{:S(2)}) collective-permute-start(bf16[128,1024]{1,0:T(8,128)(2,1)} %bitcast.15), channel_id=1, source_target_pairs={{0,4},{4,8},{8,12},{1,5},{5,9},{9,13},{2,6},{6,10},{10,14},{3,7},{... | collective-permute-start | bytes 786440 | tf_op jit(solution)/shard_map/ppermute | solution.py:19
  9.1 9.6 %collective-permute-start.3 = (bf16[128,1024]{1,0:T(8,128)(2,1)}, bf16[128,1024]{1,0:T(8,128)(2,1)S(1)}, u32[]{:S(2)}, u32[]{:S(2)}) collective-permute-start(bf16[128,1024]{1,0:T(8,128)(2,1)} %bitcast.11), channel_id=1, source_target_pairs={{4,0},{8,4},{12,8},{5,1},{9,5},{13,9},{6,2},{10,6},{14,10},{7,3},{... | collective-permute-start | bytes 786440 | tf_op jit(solution)/shard_map/ppermute | solution.py:19
  12.6 11.1 %collective-permute-start.1 = (bf16[128,1024]{1,0:T(8,128)(2,1)S(1)}, bf16[128,1024]{1,0:T(8,128)(2,1)S(1)}, u32[]{:S(2)}, u32[]{:S(2)}) collective-permute-start(bf16[128,1024]{1,0:T(8,128)(2,1)S(1)} %collective-permute-done.refs_4_.refs_8_.refs_3_), channel_id=1, source_target_pairs={{4,8},{8,12},{5,9},{9,13},{6,10},{10,14},{7,11},{11,15},{20,24},{2... | collective-permute-start | bytes 786440 | tf_op jit(solution)/shard_map/ppermute | solution.py:19
  17.1 7.0 %collective-permute-start.4 = (bf16[128,1024]{1,0:T(8,128)(2,1)S(1)}, bf16[128,1024]{1,0:T(8,128)(2,1)S(1)}, u32[]{:S(2)}, u32[]{:S(2)}) collective-permute-start(bf16[128,1024]{1,0:T(8,128)(2,1)S(1)} %collective-permute-done.2.refs_5_.refs_11_), channel_id=1, source_target_pairs={{4,8},{8,12},{5,9},{9,13},{6,10},{10,14},{7,11},{11,15},{20,24},{2... | collective-permute-start | bytes 786440 | tf_op jit(solution)/shard_map/ppermute | solution.py:19
  18.7 11.7 %collective-permute-start.5 = (bf16[128,1024]{1,0:T(8,128)(2,1)S(1)}, bf16[128,1024]{1,0:T(8,128)(2,1)S(1)}, u32[]{:S(2)}, u32[]{:S(2)}) collective-permute-start(bf16[128,1024]{1,0:T(8,128)(2,1)S(1)} %collective-permute-done.3.refs_7_.refs_2_.refs_3_), channel_id=1, source_target_pairs={{4,0},{8,4},{5,1},{9,5},{6,2},{10,6},{7,3},{11,7},{20,16},{24,20},... | collective-permute-start | bytes 786440 | tf_op jit(solution)/shard_map/ppermute | solution.py:19
  20.0 0.7 %copy-start.1 = (s32[1,4]{1,0:T(1,128)S(1)}, s32[1,4]{1,0:T(1,128)}, u32[]{:S(2)}) copy-start(s32[1,4]{1,0:T(1,128)} %refs_0_.1) | copy-start | bytes 52
  24.7 13.1 %collective-permute-start.6 = (bf16[128,1024]{1,0:T(8,128)(2,1)S(1)}, bf16[128,1024]{1,0:T(8,128)(2,1)S(1)}, u32[]{:S(2)}, u32[]{:S(2)}) collective-permute-start(bf16[128,1024]{1,0:T(8,128)(2,1)S(1)} %get-tuple-element.60.refs_6_.refs_3_), channel_id=1, source_target_pairs={{4,0},{8,4},{12,8},{5,1},{9,5},{13,9},{6,2},{10,6},{14,10},{7,3},{... | collective-permute-start | bytes 786440 | tf_op jit(solution)/shard_map/ppermute | solution.py:19
  32.0 4.3 %collective-permute-start.7 = (f32[16,128]{1,0:T(8,128)S(1)}, f32[16,128]{1,0:T(8,128)S(1)}, u32[]{:S(2)}, u32[]{:S(2)}) collective-permute-start(f32[16,128]{1,0:T(8,128)S(1)} %get-tuple-element.84), channel_id=1, source_target_pairs={{0,1},{1,0},{2,3},{3,2},{4,5},{5,4},{6,7},{7,6},{8,9},{9,8},{10,11... | collective-permute-start | bytes 24584 | tf_op jit(solution)/shard_map/ppermute | solution.py:464
  32.1 4.3 %collective-permute-start.8 = (f32[16,128]{1,0:T(8,128)S(1)}, f32[16,128]{1,0:T(8,128)S(1)}, u32[]{:S(2)}, u32[]{:S(2)}) collective-permute-start(f32[16,128]{1,0:T(8,128)S(1)} %get-tuple-element.84), channel_id=1, source_target_pairs={{0,2},{1,3},{2,0},{3,1},{4,6},{5,7},{6,4},{7,5},{8,10},{9,11},{10,... | collective-permute-start | bytes 24584 | tf_op jit(solution)/shard_map/ppermute | solution.py:464
  33.6 3.1 %collective-permute-start.9 = (f32[16,128]{1,0:T(8,128)S(1)}, f32[16,128]{1,0:T(8,128)S(1)}, u32[]{:S(2)}, u32[]{:S(2)}) collective-permute-start(f32[16,128]{1,0:T(8,128)S(1)} %get-tuple-element.84), channel_id=1, source_target_pairs={{0,3},{1,2},{2,1},{3,0},{4,7},{5,6},{6,5},{7,4},{8,11},{9,10},{10,... | collective-permute-start | bytes 24584 | tf_op jit(solution)/shard_map/ppermute | solution.py:464
  38.2 9.1 %collective-permute-start.10 = (bf16[96,1024]{1,0:T(8,128)(2,1)S(1)}, bf16[96,1024]{1,0:T(8,128)(2,1)S(1)}, u32[]{:S(2)}, u32[]{:S(2)}) collective-permute-start(bf16[96,1024]{1,0:T(8,128)(2,1)S(1)} %shard_map.135), channel_id=1, source_target_pairs={{4,0},{8,4},{5,1},{9,5},{6,2},{10,6},{7,3},{11,7},{20,16},{24,20},... | collective-permute-start | bytes 589832 | tf_op jit(solution)/shard_map/ppermute | solution.py:19
  39.6 9.1 %collective-permute-start.11 = (f32[16,128]{1,0:T(8,128)S(1)}, f32[16,128]{1,0:T(8,128)S(1)}, u32[]{:S(2)}, u32[]{:S(2)}) collective-permute-start(f32[16,128]{1,0:T(8,128)S(1)} %add_add_fusion.refs_3_), channel_id=1, source_target_pairs={{0,12},{4,8},{8,4},{12,0},{1,13},{5,9},{9,5},{13,1},{2,14},{6,10},... | collective-permute-start | bytes 24584 | tf_op jit(solution)/shard_map/ppermute | solution.py:464
  43.4 5.4 %collective-permute-start.12 = (f32[16,128]{1,0:T(8,128)S(1)}, f32[16,128]{1,0:T(8,128)S(1)}, u32[]{:S(2)}, u32[]{:S(2)}) collective-permute-start(f32[16,128]{1,0:T(8,128)S(1)} %add_add_fusion.refs_3_), channel_id=1, source_target_pairs={{0,8},{4,12},{8,0},{12,4},{1,9},{5,13},{9,1},{13,5},{2,10},{6,14},... | collective-permute-start | bytes 24584 | tf_op jit(solution)/shard_map/ppermute | solution.py:464
  44.3 4.5 %collective-permute-start.13 = (f32[16,128]{1,0:T(8,128)S(1)}, f32[16,128]{1,0:T(8,128)S(1)}, u32[]{:S(2)}, u32[]{:S(2)}) collective-permute-start(f32[16,128]{1,0:T(8,128)S(1)} %add_add_fusion.refs_3_), channel_id=1, source_target_pairs={{0,4},{4,0},{8,12},{12,8},{1,5},{5,1},{9,13},{13,9},{2,6},{6,2},{1... | collective-permute-start | bytes 24584 | tf_op jit(solution)/shard_map/ppermute | solution.py:464
